TPU v7x, 32 devices: a whole 2x2x4 slice. The times are simulated.
32 devices in a mesh: seq: 8 (over z, x), mp: 4 (over y, core).
Axes of the slice: x: 2, y: 2, z: 4, core: 2. Of those that a mesh axis runs over, the one named last changes fastest.
Arguments:
- qkv: bfloat16 [4, 1024, 12288], P('mp', 'seq'), may hold values from -8 to 8
- readout: bfloat16 [2, 4096, 64], replicated, may hold values from -0.375 to 0.375
- step_weight: float32 [1000], replicated, may hold values from 0.3 to 3
- timestep: int32 [2], replicated, may hold values from 0 to 999
- span_frames: int32 [4], replicated, may hold values from 1 to 8, as said below
Outputs:
- grad: float32 [1024, 64], P('seq')
Inputs may be any that keep to these rules, and one draw needn't show every extreme that they name: `span_frames`: they sum to 16; one span has exactly 8 frames.
All inputs are finite; a program needn't handle non-finite values.
Results may differ from a plain program's by a relative error of at most 0.0037.
Values may be sent and summed in bfloat16 or wider, within the bound.
No kernel may reach another device: no remote copies, remote signals or barrier semaphores. Data moves between devices by JAX's collectives and lax.ppermute only.
A program may use at most 64 MiB of HBM per device.

v0:
```python
import math

import jax
import jax.numpy as jnp
from jax import lax
from jax.sharding import PartitionSpec as P

HEADS = 32
HD = 128
FRAME_TOK = 64


def span_limits(span_frames, token_count):
    span_ends = jnp.cumsum(span_frames) * FRAME_TOK
    places = jnp.arange(token_count, dtype=jnp.int32)
    owner_span = jnp.sum((places[:, None] >= span_ends[None, :]).astype(jnp.int32), axis=1)
    span_ids = jnp.arange(span_ends.shape[0], dtype=jnp.int32)
    picked = jnp.where(span_ids[None, :] == owner_span[:, None], span_ends[None, :], 0)
    return jnp.sum(picked, axis=1)


def attend_one(head_group, key_limits, block_size):
    token_count = head_group.shape[0]
    queries = head_group[:, :HD]
    keyset = head_group[:, HD : 2 * HD]
    valueset = head_group[:, 2 * HD :]
    score_scale = 1.0 / math.sqrt(HD)
    offsets = jnp.arange(block_size, dtype=jnp.int32)

    def query_block(block_index, output):
        row_start = block_index * block_size
        query_rows = lax.dynamic_slice_in_dim(queries, row_start, block_size, 0)
        bounds = lax.dynamic_slice_in_dim(key_limits, row_start, block_size, 0)
        key_blocks = (jnp.max(bounds) + block_size - 1) // block_size

        def key_block(key_index, carry_state):
            row_peak, row_total, accumulated = carry_state
            key_start = key_index * block_size
            keys_here = lax.dynamic_slice_in_dim(keyset, key_start, block_size, 0)
            values_here = lax.dynamic_slice_in_dim(valueset, key_start, block_size, 0)
            scores = (
                jnp.dot(query_rows, keys_here.T, preferred_element_type=jnp.float32) * score_scale
            )
            scores = jnp.where((key_start + offsets)[None, :] < bounds[:, None], scores, -jnp.inf)
            new_peak = jnp.maximum(row_peak, jnp.max(scores, axis=1))
            rescale = jnp.exp(row_peak - new_peak)
            raw_weights = jnp.exp(scores - new_peak[:, None])
            row_total = row_total * rescale + jnp.sum(raw_weights, axis=1)
            weights = raw_weights.astype(jnp.bfloat16)
            accumulated = accumulated * rescale[:, None] + jnp.dot(
                weights, values_here, preferred_element_type=jnp.float32
            )
            return (new_peak, row_total, accumulated)

        start_state = (
            jnp.full((block_size,), -jnp.inf, jnp.float32),
            jnp.zeros((block_size,), jnp.float32),
            jnp.zeros((block_size, HD), jnp.float32),
        )
        row_peak, row_total, accumulated = lax.fori_loop(0, key_blocks, key_block, start_state)
        result = (accumulated / row_total[:, None]).astype(jnp.bfloat16)
        return lax.dynamic_update_slice_in_dim(output, result, row_start, 0)

    return lax.fori_loop(
        0, token_count // block_size, query_block, jnp.zeros((token_count, HD), jnp.bfloat16)
    )


def body(qkv, readout, step_weight, timestep, span_frames):
    seq_count = lax.axis_size("seq")
    own_rows = qkv[0]
    row_count = own_rows.shape[0]
    token_count = row_count * seq_count
    heads_local = HEADS // seq_count
    block_size = min(512, token_count)
    key_limits = span_limits(span_frames, token_count)
    grouped = own_rows.reshape(row_count, seq_count, heads_local, 3 * HD)
    items = lax.all_to_all(grouped, "seq", split_axis=1, concat_axis=0, tiled=True)
    flat_items = items.reshape(items.shape[0], items.shape[2], 3 * HD)
    outputs = jax.vmap(
        lambda head_group: attend_one(head_group, key_limits, block_size), in_axes=1, out_axes=1
    )(flat_items)
    attended = outputs.reshape(items.shape[0], 1, items.shape[2], HD)
    mp_index = lax.axis_index("mp")
    sample_count = lax.axis_size("mp") // 2
    model_index = mp_index // sample_count
    sample_index = mp_index % sample_count
    signed = jnp.where(model_index == 1, 1.0, -1.0).astype(jnp.float32)
    factor = signed * step_weight[timestep[sample_index]]
    readout_rows = lax.dynamic_index_in_dim(readout, model_index, 0, keepdims=False)
    returned = lax.all_to_all(attended, "seq", split_axis=0, concat_axis=1, tiled=True)
    token_major = returned.reshape(row_count, HEADS * HD)
    partial_sum = factor * jnp.dot(token_major, readout_rows, preferred_element_type=jnp.float32)
    return lax.psum(partial_sum, "mp")


def solution(mesh):
    return jax.shard_map(
        body,
        mesh=mesh,
        in_specs=(P("mp", "seq", None), P(), P(), P(), P()),
        out_specs=P("seq", None),
        check_vma=False,
    )
```

profile of v0, /device:TPU:0, one launch (start us, length us, event | category | flops | bytes accessed | tf_op | source)
XLA Modules:
  0.0 173.8 jit_solution(14776579187252551757)
XLA Ops:
  0.0 4.8 %copy.25 = bf16[1,128,12288]{1,2,0:T(8,128)(2,1)} copy(bf16[1,128,12288]{2,1,0:T(8,128)(2,1)} %param.11) | data formatting | bytes 6291456 | tf_op args[0]
  4.8 4.6 %copy.26 = bf16[128,8,4,384]{3,0,2,1:T(8,128)(2,1)} copy(bf16[128,8,4,384]{0,3,2,1:T(8,128)(2,1)} %bitcast.82) | data formatting | bytes 6291456 | tf_op jit(solution)/shard_map/reshape;squeeze | solution.py:77
  9.4 7.4 %all-to-all-start = ((bf16[128,8,4,384]{3,0,2,1:T(8,128)(2,1)}), bf16[128,8,4,384]{3,0,2,1:T(8,128)(2,1)}, u32[]{:S(2)}, u32[]{:S(2)}) async-start(bf16[128,8,4,384]{3,0,2,1:T(8,128)(2,1)} %copy.26), calls=%async_computation | async-start | bytes 6291456 | tf_op jit(solution)/shard_map/all_to_all | solution.py:78
  17.2 70.4 %all-to-all-done = bf16[128,8,4,384]{3,0,2,1:T(8,128)(2,1)} async-done(((bf16[128,8,4,384]{3,0,2,1:T(8,128)(2,1)}), bf16[128,8,4,384]{3,0,2,1:T(8,128)(2,1)}, u32[]{:S(2)}, u32[]{:S(2)}) %all-to-all-start) | async-done | bytes 3145760 | tf_op jit(solution)/shard_map/all_to_all | solution.py:78
  87.6 2.4 %copy.27 = bf16[128,8,4,384]{3,0,1,2:T(8,128)(2,1)S(1)} copy(bf16[128,8,4,384]{3,0,2,1:T(8,128)(2,1)} %all-to-all-done) | data formatting | bytes 6291456 | tf_op jit(solution)/shard_map/all_to_all | solution.py:78
  90.0 2.1 %slice_bitcast_fusion = (bf16[4,1024,128]{2,1,0:T(8,128)(2,1)}, bf16[4,1024,128]{2,1,0:T(8,128)(2,1)S(1)}, bf16[4,1024,128]{2,1,0:T(8,128)(2,1)}) fusion(bf16[1024,4,384]{2,0,1:T(8,128)(2,1)S(1)} %bitcast.81), kind=kLoop, calls=%fused_computation.34 | loop fusion | bytes 6291456 | tf_op jit(solution)/shard_map/vmap()/transpose | solution.py:64
  92.1 1.3 broadcast_in_dim.52.clone
  93.4 38.8 %while.83 = (s32[]{:T(128)}, bf16[4,1024,128]{2,0,1:T(4,128)(2,1)}, s32[1024]{0:T(1024)S(1)}, bf16[4,1024,128]{2,1,0:T(8,128)(2,1)}, bf16[4,1024,128]{2,1,0:T(8,...) while((s32[]{:T(128)}, bf16[4,1024,128]{2,0,1:T(4,128)(2,1)}, ...), condition=%wide.region_10.11_spmd.clone, body=%wide.region_3.10_spmd.clone.sunk | while | flops 549983232 | bytes 36347808 | solution.py:64
  93.4 0.7 fusion.38
  94.9 1.2 constant_dynamic-slice_fusion.4
  96.1 1.1 broadcast.216
  97.2 10.2 %while.84 = (s32[]{:T(128)}, f32[4,512]{1,0:T(4,128)S(1)}, f32[4,512]{1,0:T(4,128)S(1)}, f32[4,512,128]{2,1,0:T(8,128)}, s32[]{:T(128)}, /*index=5*/s32[512]{0:T...) while((s32[]{:T(128)}, f32[4,512]{1,0:T(4,128)S(1)}, ...), condition=%wide.region_9.9_spmd, body=%wide.region_6.8_spmd.sunk | while | flops 549196288 | bytes 30024996 | solution.py:60
  97.2 0.2 broadcast_compare_fusion.2
  97.5 1.0 fusion.44
  98.5 0.9 fusion.45
  99.4 1.8 %fusion.46 = f32[4,512,128]{2,1,0:T(8,128)S(1)} fusion(f32[4,512,512]{2,1,0:T(8,128)S(1)} %get-tuple-element.556, f32[4,512]{1,0:T(4,128)S(1)} %max.4, pred[512,512]{0,1:T(8,128)(4,1)S(1)} %broadcast_compare_fusion.2, f32[4,512,128]{2,1,0:T(8,128)S(1)} %copy-done.1, bf16[4,1024,128]{2,1,0:T(8,128)(2,1)S(1)} %copy-done.3, s32[]{:T(128)S(1)} %bitcast.86, ...), kind=kOutput, calls=%fused_computation.11.clone.1 | convolution fusion | flops 273154048 | bytes 7094784 | tf_op jit(solution)/shard_map/vmap()/while/body/eval_jaxpr/while/body/dot_general | solution.py:50
  101.3 1.0 copy-done.2
  102.6 1.0 fusion.44
  103.6 0.9 fusion.45
  104.5 1.8 %fusion.46 = f32[4,512,128]{2,1,0:T(8,128)S(1)} fusion(f32[4,512,512]{2,1,0:T(8,128)S(1)} %get-tuple-element.556, f32[4,512]{1,0:T(4,128)S(1)} %max.4, pred[512,512]{0,1:T(8,128)(4,1)S(1)} %broadcast_compare_fusion.2, f32[4,512,128]{2,1,0:T(8,128)S(1)} %copy-done.1, bf16[4,1024,128]{2,1,0:T(8,128)(2,1)S(1)} %copy-done.3, s32[]{:T(128)S(1)} %bitcast.86, ...), kind=kOutput, calls=%fused_computation.11.clone.1 | convolution fusion | flops 273154048 | bytes 7094784 | tf_op jit(solution)/shard_map/vmap()/while/body/eval_jaxpr/while/body/dot_general | solution.py:50
  106.3 1.0 copy-done.2
  107.4 0.7 and_reduce_fusion.2
  108.1 1.3 constant_dynamic-slice_fusion.5
  109.4 2.2 %fusion.40 = bf16[4,512,128]{2,1,0:T(8,128)(2,1)S(1)} fusion(f32[4,512,128]{2,1,0:T(8,128)} %get-tuple-element.543, bf16[4,512,128]{2,0,1:T(4,128)(2,1)S(1)} %constant_dynamic-slice_fusion.5, f32[4,512]{1,0:T(4,128)S(1)} %get-tuple-element.542, pred[]{:T(512)} %and_reduce_fusion.2), kind=kLoop, calls=%fused_computation.25.clone.1 | loop fusion | flops 786432 | bytes 2105345 | tf_op jit(solution)/shard_map/select.52
  111.6 1.2 copy_dynamic-update-slice_fusion.2
  112.8 0.7 fusion.38
  114.2 1.2 constant_dynamic-slice_fusion.4
  115.5 1.1 broadcast.216
  116.5 10.1 %while.84 = (s32[]{:T(128)}, f32[4,512]{1,0:T(4,128)S(1)}, f32[4,512]{1,0:T(4,128)S(1)}, f32[4,512,128]{2,1,0:T(8,128)}, s32[]{:T(128)}, /*index=5*/s32[512]{0:T...) while((s32[]{:T(128)}, f32[4,512]{1,0:T(4,128)S(1)}, ...), condition=%wide.region_9.9_spmd, body=%wide.region_6.8_spmd.sunk | while | flops 549196288 | bytes 30024996 | solution.py:60
  116.9 1.0 fusion.44
  117.9 0.9 fusion.45
  118.8 1.8 %fusion.46 = f32[4,512,128]{2,1,0:T(8,128)S(1)} fusion(f32[4,512,512]{2,1,0:T(8,128)S(1)} %get-tuple-element.556, f32[4,512]{1,0:T(4,128)S(1)} %max.4, pred[512,512]{0,1:T(8,128)(4,1)S(1)} %broadcast_compare_fusion.2, f32[4,512,128]{2,1,0:T(8,128)S(1)} %copy-done.1, bf16[4,1024,128]{2,1,0:T(8,128)(2,1)S(1)} %copy-done.3, s32[]{:T(128)S(1)} %bitcast.86, ...), kind=kOutput, calls=%fused_computation.11.clone.1 | convolution fusion | flops 273154048 | bytes 7094784 | tf_op jit(solution)/shard_map/vmap()/while/body/eval_jaxpr/while/body/dot_general | solution.py:50
  120.6 1.0 copy-done.2
  121.9 1.0 fusion.44
  122.9 0.9 fusion.45
  123.9 1.8 %fusion.46 = f32[4,512,128]{2,1,0:T(8,128)S(1)} fusion(f32[4,512,512]{2,1,0:T(8,128)S(1)} %get-tuple-element.556, f32[4,512]{1,0:T(4,128)S(1)} %max.4, pred[512,512]{0,1:T(8,128)(4,1)S(1)} %broadcast_compare_fusion.2, f32[4,512,128]{2,1,0:T(8,128)S(1)} %copy-done.1, bf16[4,1024,128]{2,1,0:T(8,128)(2,1)S(1)} %copy-done.3, s32[]{:T(128)S(1)} %bitcast.86, ...), kind=kOutput, calls=%fused_computation.11.clone.1 | convolution fusion | flops 273154048 | bytes 7094784 | tf_op jit(solution)/shard_map/vmap()/while/body/eval_jaxpr/while/body/dot_general | solution.py:50
  125.7 1.0 copy-done.2
  126.8 0.7 and_reduce_fusion.2
  127.5 1.3 constant_dynamic-slice_fusion.5
  128.7 2.2 %fusion.40 = bf16[4,512,128]{2,1,0:T(8,128)(2,1)S(1)} fusion(f32[4,512,128]{2,1,0:T(8,128)} %get-tuple-element.543, bf16[4,512,128]{2,0,1:T(4,128)(2,1)S(1)} %constant_dynamic-slice_fusion.5, f32[4,512]{1,0:T(4,128)S(1)} %get-tuple-element.542, pred[]{:T(512)} %and_reduce_fusion.2), kind=kLoop, calls=%fused_computation.25.clone.1 | loop fusion | flops 786432 | bytes 2105345 | tf_op jit(solution)/shard_map/select.52
  130.9 1.3 copy_dynamic-update-slice_fusion.2
  132.2 3.6 %all-to-all-start.1 = ((bf16[1024,1,4,128]{3,2,1,0:T(4,128)(2,1)}), bf16[1024,1,4,128]{3,2,1,0:T(4,128)(2,1)S(1)}, u32[]{:S(2)}, u32[]{:S(2)}) async-start(bf16[1024,1,4,128]{3,2,1,0:T(4,128)(2,1)} %bitcast.80), calls=%async_computation.1 | async-start | bytes 2097152 | tf_op jit(solution)/shard_map/all_to_all | solution.py:91
  135.8 0.6 dynamic_slice.24
  138.4 1.3 dynamic_slice.25
  140.3 21.5 %all-to-all-done.1 = bf16[1024,1,4,128]{3,2,1,0:T(4,128)(2,1)S(1)} async-done(((bf16[1024,1,4,128]{3,2,1,0:T(4,128)(2,1)}), bf16[1024,1,4,128]{3,2,1,0:T(4,128)(2,1)S(1)}, u32[]{:S(2)}, u32[]{:S(2)}) %all-to-all-start.1) | async-done | bytes 1048608 | tf_op jit(solution)/shard_map/all_to_all | solution.py:91
  161.9 0.7 copy.30
  162.6 0.3 convolution_multiply_fusion
  162.9 10.9 %psum.7 = f32[128,64]{0,1:T(8,128)} all-reduce(f32[128,64]{0,1:T(8,128)S(1)} %convolution_multiply_fusion), channel_id=1, replica_groups=mesh['seq'=8,'mp'=4] {'mp'}, use_global_device_ids=true, to_apply=%region_11.12 | all-reduce | flops 8192 | bytes 65536 | tf_op jit(solution)/shard_map/psum | solution.py:94
  (68 shorter events, 1.9 us)
Async XLA Ops:
  0.0 162.6 %copy-start = (bf16[2,4096,64]{1,2,0:T(8,128)(2,1)S(1)}, bf16[2,4096,64]{1,2,0:T(8,128)(2,1)}, u32[]{:S(2)}) copy-start(bf16[2,4096,64]{1,2,0:T(8,128)(2,1)} %param.12) | copy-start | bytes 3145732
  9.4 7.4 %copy-start.6 = (s32[4]{0:T(128)S(1)}, s32[4]{0:T(128)}, u32[]{:S(2)}) copy-start(s32[4]{0:T(128)} %param.15) | copy-start | bytes 52
  9.4 78.2 %all-to-all-start = ((bf16[128,8,4,384]{3,0,2,1:T(8,128)(2,1)}), bf16[128,8,4,384]{3,0,2,1:T(8,128)(2,1)}, u32[]{:S(2)}, u32[]{:S(2)}) async-start(bf16[128,8,4,384]{3,0,2,1:T(8,128)(2,1)} %copy.26), calls=%async_computation | async-start | bytes 6291456 | tf_op jit(solution)/shard_map/all_to_all | solution.py:78
  90.0 3.4 %copy-start.4 = (s32[2]{0:T(128)S(1)}, s32[2]{0:T(128)}, u32[]{:S(2)}) copy-start(s32[2]{0:T(128)} %constant.272.clone.2) | copy-start | bytes 28
  90.0 3.4 %copy-start.5 = (s32[3]{0:T(128)S(1)}, s32[3]{0:T(128)}, u32[]{:S(2)}) copy-start(s32[3]{0:T(128)} %constant.273.clone.2) | copy-start | bytes 40
  93.4 42.4 %copy-start.7 = (s32[2]{0:T(128)S(1)}, s32[2]{0:T(128)}, u32[]{:S(2)}) copy-start(s32[2]{0:T(128)} %param.14) | copy-start | bytes 28
  97.5 2.0 %copy-start.1 = (f32[4,512,128]{2,1,0:T(8,128)S(1)}, f32[4,512,128]{2,1,0:T(8,128)}, u32[]{:S(2)}) copy-start(f32[4,512,128]{2,1,0:T(8,128)} %get-tuple-element.577) | copy-start | bytes 3145732 | tf_op jit(solution)/shard_map/vmap()/while/body/eval_jaxpr/while
  97.5 2.0 %copy-start.3 = (bf16[4,1024,128]{2,1,0:T(8,128)(2,1)S(1)}, bf16[4,1024,128]{2,1,0:T(8,128)(2,1)}, u32[]{:S(2)}) copy-start(bf16[4,1024,128]{2,1,0:T(8,128)(2,1)} %get-tuple-element.598) | copy-start | bytes 3145732 | tf_op jit(solution)/shard_map/vmap()/while/body/eval_jaxpr/while
  101.2 1.0 copy-start.2
  102.5 2.0 %copy-start.1 = (f32[4,512,128]{2,1,0:T(8,128)S(1)}, f32[4,512,128]{2,1,0:T(8,128)}, u32[]{:S(2)}) copy-start(f32[4,512,128]{2,1,0:T(8,128)} %get-tuple-element.577) | copy-start | bytes 3145732 | tf_op jit(solution)/shard_map/vmap()/while/body/eval_jaxpr/while
  102.5 2.0 %copy-start.3 = (bf16[4,1024,128]{2,1,0:T(8,128)(2,1)S(1)}, bf16[4,1024,128]{2,1,0:T(8,128)(2,1)}, u32[]{:S(2)}) copy-start(bf16[4,1024,128]{2,1,0:T(8,128)(2,1)} %get-tuple-element.598) | copy-start | bytes 3145732 | tf_op jit(solution)/shard_map/vmap()/while/body/eval_jaxpr/while
  106.3 1.0 copy-start.2
  116.8 2.0 %copy-start.1 = (f32[4,512,128]{2,1,0:T(8,128)S(1)}, f32[4,512,128]{2,1,0:T(8,128)}, u32[]{:S(2)}) copy-start(f32[4,512,128]{2,1,0:T(8,128)} %get-tuple-element.577) | copy-start | bytes 3145732 | tf_op jit(solution)/shard_map/vmap()/while/body/eval_jaxpr/while
  116.8 2.0 %copy-start.3 = (bf16[4,1024,128]{2,1,0:T(8,128)(2,1)S(1)}, bf16[4,1024,128]{2,1,0:T(8,128)(2,1)}, u32[]{:S(2)}) copy-start(bf16[4,1024,128]{2,1,0:T(8,128)(2,1)} %get-tuple-element.598) | copy-start | bytes 3145732 | tf_op jit(solution)/shard_map/vmap()/while/body/eval_jaxpr/while
  120.6 1.0 copy-start.2
  121.9 2.0 %copy-start.1 = (f32[4,512,128]{2,1,0:T(8,128)S(1)}, f32[4,512,128]{2,1,0:T(8,128)}, u32[]{:S(2)}) copy-start(f32[4,512,128]{2,1,0:T(8,128)} %get-tuple-element.577) | copy-start | bytes 3145732 | tf_op jit(solution)/shard_map/vmap()/while/body/eval_jaxpr/while
  121.9 2.0 %copy-start.3 = (bf16[4,1024,128]{2,1,0:T(8,128)(2,1)S(1)}, bf16[4,1024,128]{2,1,0:T(8,128)(2,1)}, u32[]{:S(2)}) copy-start(bf16[4,1024,128]{2,1,0:T(8,128)(2,1)} %get-tuple-element.598) | copy-start | bytes 3145732 | tf_op jit(solution)/shard_map/vmap()/while/body/eval_jaxpr/while
  125.7 1.0 copy-start.2
  132.2 29.6 %all-to-all-start.1 = ((bf16[1024,1,4,128]{3,2,1,0:T(4,128)(2,1)}), bf16[1024,1,4,128]{3,2,1,0:T(4,128)(2,1)S(1)}, u32[]{:S(2)}, u32[]{:S(2)}) async-start(bf16[1024,1,4,128]{3,2,1,0:T(4,128)(2,1)} %bitcast.80), calls=%async_computation.1 | async-start | bytes 2097152 | tf_op jit(solution)/shard_map/all_to_all | solution.py:91
where the time goes:
time: 172 us; the launch traced here: 174 us
  waiting for transfers between devices  91.9 us (53%)
  local copies, waits for them, and re-layouts  31.4 us (18%)
  other arithmetic  12.8 us (7%)
  matrix products  11.5 us (7%)
  starting transfers between devices  11 us (6%)
  blocking collectives  10.9 us (6%)
  between operations  2.68 us (2%)
    all_to_all x1, waiting for transfers between devices, body(): lax.all_to_all(grouped, 'seq', split_axis=1, concat_axis=0, tiled=True)  70.4 us
    all_to_all x1, waiting for transfers between devices, body(): lax.all_to_all(attended, 'seq', split_axis=0, concat_axis=1, tiled=True)  21.5 us
    psum x1, blocking collectives, body(): return lax.psum(partial_sum, 'mp')  10.9 us
    all_to_all x1, starting transfers between devices, body(): lax.all_to_all(grouped, 'seq', split_axis=1, concat_axis=0, tiled=True)  7.38 us
    dot_general x4, matrix products, key_block(): jnp.dot(weights, values_here, preferred_element_type=jnp.float32)  7.21 us
    another operation x5, other arithmetic  5.98 us
    unnamed x11, local copies, waits for them, and re-layouts  4.8 us
    another operation x1, local copies, waits for them, and re-layouts, body(): grouped = own_rows.reshape(row_count, seq_count, heads_local, 3 * HD)  4.64 us
  transfers between devices with their start and end apart: 2, of which 2 were waited for; matrix products, arithmetic and copies ran while one was open for 1% of the time, Pallas kernels for 0%

commit v1 on v0

v1 whole, which is shorter than its diff:
```python
import functools
import math

import jax
import jax.numpy as jnp
from jax import lax
from jax.experimental import pallas as pl
from jax.experimental.pallas import tpu as pltpu
from jax.sharding import PartitionSpec as P

HEADS = 32
HD = 128
FRAME_TOK = 64
NT = (((1,), (1,)), ((), ()))
VMEM_LIMIT = 48 * 1024 * 1024


def pack_kernel(chunks, qkv_ref, readout_ref, *out_refs):
    lat = readout_ref.shape[1]
    head = 0
    for out_ref, count in zip(out_refs, chunks):
        for i in range(count):
            base = (head + i) * 3 * HD
            out_ref[0, :, i * 2 * HD : (i + 1) * 2 * HD] = qkv_ref[0, :, base : base + 2 * HD]
            values = qkv_ref[0, :, base + 2 * HD : base + 3 * HD]
            rows = readout_ref[0, :, (head + i) * HD : (head + i + 1) * HD]
            folded = lax.dot_general(rows, values, NT, preferred_element_type=jnp.float32)
            column = count * 2 * HD + (i * lat // HD) * HD
            row = (i * lat) % HD
            out_ref[0, row : row + lat, column : column + HD] = folded.astype(jnp.bfloat16)
        head += count


def pack(qkv, readout_t, model_index, seq_count, chunks):
    _, rows, _ = qkv.shape
    lat = readout_t.shape[1]
    heads_local = HEADS // seq_count
    widths = [c * 2 * HD + -(-c * lat // HD) * HD for c in chunks]

    def kernel(index_ref, *refs):
        pack_kernel(chunks, *refs)

    return pl.pallas_call(
        kernel,
        grid_spec=pltpu.PrefetchScalarGridSpec(
            num_scalar_prefetch=1,
            grid=(seq_count,),
            in_specs=[
                pl.BlockSpec((1, rows, heads_local * 3 * HD), lambda d, m: (0, 0, d)),
                pl.BlockSpec((1, lat, heads_local * HD), lambda d, m: (m[0], 0, d)),
            ],
            out_specs=[pl.BlockSpec((1, rows, w), lambda d, m: (d, 0, 0)) for w in widths],
        ),
        out_shape=[jax.ShapeDtypeStruct((seq_count, rows, w), jnp.bfloat16) for w in widths],
        compiler_params=pltpu.CompilerParams(vmem_limit_bytes=VMEM_LIMIT),
        name="pack",
    )(model_index, qkv, readout_t)


def attend_kernel(count, lat, block, last, frames_ref, factor_ref, packed_ref, *refs):
    seq_count, rows, _ = packed_ref.shape
    tokens = seq_count * rows
    spans = frames_ref.shape[0]
    out_ref = refs[-1]
    log2_scale = math.log2(math.e) / math.sqrt(HD)
    per_block = block // rows

    def one_block(b, carry):
        places = b * block + lax.broadcasted_iota(jnp.int32, (1, block), 1)
        end = frames_ref[0] * FRAME_TOK
        bound = jnp.full((1, block), end, jnp.int32)
        for c in range(1, spans):
            later = end + frames_ref[c] * FRAME_TOK
            bound = jnp.where(places >= end, later, bound)
            end = later
        key_places = lax.broadcasted_iota(jnp.int32, (tokens, 1), 0)
        allowed = key_places < bound
        total = None
        for i in range(count):
            queries = packed_ref[pl.ds(b * per_block, per_block), :, i * 2 * HD : i * 2 * HD + HD]
            queries = queries.reshape(block, HD)
            keys = packed_ref[:, :, i * 2 * HD + HD : (i + 1) * 2 * HD].reshape(tokens, HD)
            scores = lax.dot_general(keys, queries, NT, preferred_element_type=jnp.float32)
            scores = jnp.where(allowed, scores, -jnp.inf)
            peak = jnp.max(scores, axis=0, keepdims=True)
            raw = jnp.exp2((scores - peak) * log2_scale)
            row_total = jnp.sum(raw, axis=0, keepdims=True)
            weights = raw.astype(jnp.bfloat16)
            column = count * 2 * HD + (i * lat // HD) * HD
            row = (i * lat) % HD
            folded = jnp.concatenate(
                [packed_ref[s, row : row + lat, column : column + HD] for s in range(seq_count)], axis=1
            )
            summed = jnp.dot(folded, weights, preferred_element_type=jnp.float32) / row_total
            total = summed if total is None else total + summed
        for j in range(per_block):
            part = total[:, j * rows : (j + 1) * rows]
            if len(refs) > 1:
                part = part + refs[0][b * per_block + j]
            if last:
                part = part * factor_ref[0]
            out_ref[b * per_block + j] = part.astype(out_ref.dtype)
        return carry

    lax.fori_loop(0, tokens // block, one_block, 0)


def attend(packed, earlier, span_frames, factor, count, lat, last):
    seq_count, rows, _ = packed.shape
    tokens = seq_count * rows
    block = 256
    smem = pl.BlockSpec(memory_space=pltpu.SMEM)
    vmem = pl.BlockSpec(memory_space=pltpu.VMEM)
    operands = [span_frames, factor, packed] + ([] if earlier is None else [earlier])
    return pl.pallas_call(
        functools.partial(attend_kernel, count, lat, block, last),
        in_specs=[smem, smem] + [vmem] * (len(operands) - 2),
        out_specs=vmem,
        out_shape=jax.ShapeDtypeStruct((seq_count, lat, rows), jnp.bfloat16 if last else jnp.float32),
        compiler_params=pltpu.CompilerParams(vmem_limit_bytes=VMEM_LIMIT),
        cost_estimate=pl.CostEstimate(
            flops=count * tokens * tokens * 2 * (HD + lat),
            bytes_accessed=packed.size * 2,
            transcendentals=count * tokens * tokens,
        ),
        name="attend",
    )(*operands)


def body(qkv, readout, step_weight, timestep, span_frames):
    seq_count = lax.axis_size("seq")
    heads_local = HEADS // seq_count
    lat = readout.shape[2]
    mp_index = lax.axis_index("mp")
    sample_count = lax.axis_size("mp") // 2
    model_index = mp_index // sample_count
    sample_index = mp_index % sample_count
    signed = jnp.where(model_index == 1, 1.0, -1.0).astype(jnp.float32)
    factor = (signed * step_weight[timestep[sample_index]]).reshape(1)
    chunks = [2] * (heads_local // 2) if heads_local % 2 == 0 else [heads_local]
    readout_t = jnp.swapaxes(readout, 1, 2)
    packed = pack(qkv, readout_t, model_index.astype(jnp.int32).reshape(1), seq_count, chunks)
    arrived = [lax.all_to_all(p, "seq", split_axis=0, concat_axis=0, tiled=True) for p in packed]
    result = None
    for n, (array, count) in enumerate(zip(arrived, chunks)):
        result = attend(array, result, span_frames, factor, count, lat, n == len(chunks) - 1)
    parts = lax.all_to_all(result, "seq", split_axis=0, concat_axis=0, tiled=True)
    own = jnp.sum(parts.astype(jnp.float32), axis=0)
    return lax.psum(own, "mp").T


def solution(mesh):
    return jax.shard_map(
        body,
        mesh=mesh,
        in_specs=(P("mp", "seq", None), P(), P(), P(), P()),
        out_specs=P("seq", None),
        check_vma=False,
    )
```

time: 172 us -> 110 us (0.64); the launches traced: 174 us -> 109 us
  waiting for transfers between devices: 91.9 us -> 19.7 us
  blocking collectives: 10.9 us -> 60 us
  local copies, waits for them, and re-layouts: 31.4 us -> 3.09 us
  Pallas kernels: 0 us -> 20 us
  other arithmetic: 12.8 us -> 0.02 us
  matrix products: 11.5 us -> 0 us
  starting transfers between devices: 11 us -> 3.72 us
    all_to_all x2 -> x1, waiting for transfers between devices: 91.9 us -> 19.7 us  [body(): lax.all_to_all(p, 'seq', split_axis=0, concat_axis=0, tiled=True)]
    all_to_all x0 -> x2, blocking collectives: none -> 49.2 us  [the longest x1 38.4 us: body(): lax.all_to_all(p, 'seq', split_axis=0, concat_axis=0, tiled=True)]
    pallas_call x0 -> x3, Pallas kernels: none -> 20 us  [the longest x2 13.7 us: attend(): pl.pallas_call(functools.partial(attend_kernel, count, lat, block, last),...]
    dot_general x9 -> x0, matrix products: 11.5 us -> none  [the longest x4 7.21 us: key_block(): jnp.dot(weights, values_here, preferred_element_type=jnp.float32)]
    another operation x9 -> x0, local copies, waits for them, and re-layouts: 9.28 us -> none  [the longest x1 4.64 us: body(): grouped = own_rows.reshape(row_count, seq_count, heads_local, 3 * HD)]
    all_to_all x2 -> x1, starting transfers between devices: 11 us -> 3.72 us  [body(): lax.all_to_all(p, 'seq', split_axis=0, concat_axis=0, tiled=True)]
    another operation x5 -> x0, other arithmetic: 5.98 us -> none
    while x28 -> x0, local copies, waits for them, and re-layouts: 3.95 us -> none
  transfers between devices with their start and end apart: 2 -> 1, of which waited for: 2 -> 1; matrix products, arithmetic and copies ran while one was open for 1% -> 2% of each run, Pallas kernels for 0% -> 6%
where the time goes in v1:
time: 110 us; the launch traced here: 109 us
  blocking collectives  60 us (55%)
  Pallas kernels  20 us (18%)
  waiting for transfers between devices  19.7 us (18%)
  starting transfers between devices  3.72 us (3%)
  local copies, waits for them, and re-layouts  3.09 us (3%)
  between operations  2.64 us (2%)
    all_to_all x1, blocking collectives, body(): lax.all_to_all(p, 'seq', split_axis=0, concat_axis=0, tiled=True)  38.4 us
    all_to_all x1, waiting for transfers between devices, body(): lax.all_to_all(p, 'seq', split_axis=0, concat_axis=0, tiled=True)  19.7 us
    pallas_call x2, Pallas kernels, attend(): pl.pallas_call(functools.partial(attend_kernel, count, lat, block, last),...  13.7 us
    psum x1, blocking collectives, body(): return lax.psum(own, 'mp').T  10.9 us
    all_to_all x1, blocking collectives, body(): lax.all_to_all(result, 'seq', split_axis=0, concat_axis=0, tiled=True)  10.7 us
    pallas_call x1, Pallas kernels, pack(): pl.pallas_call(kernel, grid_spec=pltpu.PrefetchScalarGridSpec(num_scalar_...  6.32 us
    all_to_all x1, starting transfers between devices, body(): lax.all_to_all(p, 'seq', split_axis=0, concat_axis=0, tiled=True)  3.72 us
  transfers between devices with their start and end apart: 1, of which 1 were waited for; matrix products, arithmetic and copies ran while one was open for 2% of the time, Pallas kernels for 6%

profile of v1, /device:TPU:0, one launch (start us, length us, event | category | flops | bytes accessed | tf_op | source)
XLA Modules:
  0.0 109.2 jit_solution(6949496476000698871)
XLA Ops:
  0.0 0.0 copy-start
  0.0 1.2 %copy-done = bf16[2,4096,64]{1,2,0:T(8,128)(2,1)S(1)} copy-done((bf16[2,4096,64]{1,2,0:T(8,128)(2,1)S(1)}, bf16[2,4096,64]{1,2,0:T(8,128)(2,1)}, u32[]{:S(2)}) %copy-start) | copy-done | bytes 1048600
  1.2 6.3 %pack.1 = (bf16[8,128,640]{2,1,0:T(8,128)(2,1)S(1)}, bf16[8,128,640]{2,1,0:T(8,128)(2,1)}) custom-call(s32[1]{0:T(128)} %bitcast.3.index_ref, bf16[1,128,12288]{2,1,0:T(8,128)(2,1)} %refs_0_.1, bf16[2,64,4096]{2,1,0:T(8,128)(2,1)S(1)} %bitcast.6), custom_call_target="tpu_custom_call" | custom-call | tf_op jit(solution)/shard_map/pack/pallas_call | solution.py:43
  7.5 38.4 %all_to_all.15.packed_ref = bf16[8,128,640]{2,1,0:T(8,128)(2,1)S(1)} all-to-all(bf16[8,128,640]{2,1,0:T(8,128)(2,1)S(1)} %get-tuple-element.8), channel_id=1, replica_groups=mesh['seq'=8,'mp'=4] {'seq'}, dimensions={0} | all-to-all | bytes 2621440 | tf_op jit(solution)/shard_map/all_to_all | solution.py:143
  46.0 0.0 copy-start.2
  46.0 0.0 copy-start.1
  46.0 3.7 %all-to-all-start = ((bf16[8,128,640]{2,1,0:T(8,128)(2,1)}), bf16[8,128,640]{2,1,0:T(8,128)(2,1)S(1)}, u32[]{:S(2)}, u32[]{:S(2)}) async-start(bf16[8,128,640]{2,1,0:T(8,128)(2,1)} %get-tuple-element.7), calls=%async_computation | async-start | bytes 2621440 | tf_op jit(solution)/shard_map/all_to_all | solution.py:143
  49.7 0.0 copy-done.2
  49.7 0.6 dynamic_slice.6
  52.2 1.3 %dynamic_slice.7 = f32[1]{0:T(128)} dynamic-slice(f32[1000]{0:T(1024)} %param.7, s32[]{:T(128)S(6)} %select_n.25), dynamic_slice_sizes={1} | dynamic-slice | bytes 12 | tf_op jit(solution)/shard_map/dynamic_slice | solution.py:139
  54.2 0.0 copy-done.1
  54.2 6.9 %attend.2.refs_0_ = f32[8,64,128]{2,1,0:T(8,128)S(1)} custom-call(s32[4]{0:T(128)S(1)} %copy-done.1, f32[1]{0:T(128)} %bitcast.2.factor_ref, bf16[8,128,640]{2,1,0:T(8,128)(2,1)S(1)} %all_to_all.15.packed_ref), custom_call_target="tpu_custom_call" | custom-call | flops 805306368 | bytes 1310720 | tf_op jit(solution)/shard_map/attend/pallas_call | solution.py:115
  61.0 19.7 %all-to-all-done.packed_ref = bf16[8,128,640]{2,1,0:T(8,128)(2,1)S(1)} async-done(((bf16[8,128,640]{2,1,0:T(8,128)(2,1)}), bf16[8,128,640]{2,1,0:T(8,128)(2,1)S(1)}, u32[]{:S(2)}, u32[]{:S(2)}) %all-to-all-start) | async-done | bytes 1310752 | tf_op jit(solution)/shard_map/all_to_all | solution.py:143
  80.7 6.9 %attend.3 = bf16[8,64,128]{2,1,0:T(8,128)(2,1)S(1)} custom-call(s32[4]{0:T(128)S(1)} %copy-done.1, f32[1]{0:T(128)} %bitcast.2.factor_ref, bf16[8,128,640]{2,1,0:T(8,128)(2,1)S(1)} %all-to-all-done.packed_ref, f32[8,64,128]{2,1,0:T(8,128)S(1)} %attend.2.refs_0_), custom_call_target="tpu_custom_call" | custom-call | flops 805306368 | bytes 1310720 | tf_op jit(solution)/shard_map/attend/pallas_call | solution.py:115
  87.6 10.7 %all_to_all.16 = bf16[8,64,128]{2,1,0:T(8,128)(2,1)S(1)} all-to-all(bf16[8,64,128]{2,1,0:T(8,128)(2,1)S(1)} %attend.3), channel_id=1, replica_groups=mesh['seq'=8,'mp'=4] {'seq'}, dimensions={0} | all-to-all | bytes 262144 | tf_op jit(solution)/shard_map/all_to_all | solution.py:147
  98.4 10.9 %psum.7 = f32[128,64]{0,1:T(8,128)} all-reduce(f32[128,64]{0,1:T(8,128)S(1)} %bitcast.7), channel_id=1, replica_groups=mesh['seq'=8,'mp'=4] {'mp'}, use_global_device_ids=true, to_apply=%region_1.2 | all-reduce | flops 8192 | bytes 65536 | tf_op jit(solution)/shard_map/psum | solution.py:149
  (1 shorter events, 0.0 us)
Async XLA Ops:
  0.0 1.2 %copy-start = (bf16[2,4096,64]{1,2,0:T(8,128)(2,1)S(1)}, bf16[2,4096,64]{1,2,0:T(8,128)(2,1)}, u32[]{:S(2)}) copy-start(bf16[2,4096,64]{1,2,0:T(8,128)(2,1)} %param.6) | copy-start | bytes 3145732
  46.0 3.7 %copy-start.2 = (s32[2]{0:T(128)S(1)}, s32[2]{0:T(128)}, u32[]{:S(2)}) copy-start(s32[2]{0:T(128)} %param.8) | copy-start | bytes 28
  46.0 8.2 %copy-start.1 = (s32[4]{0:T(128)S(1)}, s32[4]{0:T(128)}, u32[]{:S(2)}) copy-start(s32[4]{0:T(128)} %frames_ref.3) | copy-start | bytes 52
  46.0 34.8 %all-to-all-start = ((bf16[8,128,640]{2,1,0:T(8,128)(2,1)}), bf16[8,128,640]{2,1,0:T(8,128)(2,1)S(1)}, u32[]{:S(2)}, u32[]{:S(2)}) async-start(bf16[8,128,640]{2,1,0:T(8,128)(2,1)} %get-tuple-element.7), calls=%async_computation | async-start | bytes 2621440 | tf_op jit(solution)/shard_map/all_to_all | solution.py:143

commit v2 on v1

v2 whole, which is shorter than its diff:
```python
import functools
import math

import jax
import jax.numpy as jnp
from jax import lax
from jax.experimental import pallas as pl
from jax.experimental.pallas import tpu as pltpu
from jax.sharding import PartitionSpec as P

HEADS = 32
HD = 128
FRAME_TOK = 64
NT = (((1,), (1,)), ((), ()))
VMEM_LIMIT = 48 * 1024 * 1024


def pack_kernel(chunks, place_ref, qkv_ref, readout_ref, *out_refs):
    lat = readout_ref.shape[1]
    head = 0
    for out_ref, count in zip(out_refs, chunks):
        for i in range(count):
            base = (head + i) * 3 * HD
            out_ref[:, i * 2 * HD : (i + 1) * 2 * HD] = qkv_ref[0, :, base : base + 2 * HD]
        head += count
    for i in range(head):
        base = i * 3 * HD
        values = qkv_ref[0, :, base + 2 * HD : base + 3 * HD]
        rows = readout_ref[0, :, i * HD : (i + 1) * HD]
        folded = lax.dot_general(rows, values, NT, preferred_element_type=jnp.float32)
        column = chunks[0] * 2 * HD + (i * lat // HD) * HD
        row = (i * lat) % HD
        out_refs[0][row : row + lat, column : column + HD] = folded.astype(jnp.bfloat16)


def pack(place, qkv, readout_t, chunks, widths):
    rows = qkv.shape[1]
    lat = readout_t.shape[1]
    heads_local = sum(chunks)
    return pl.pallas_call(
        functools.partial(pack_kernel, chunks),
        grid_spec=pltpu.PrefetchScalarGridSpec(
            num_scalar_prefetch=1,
            grid=(1,),
            in_specs=[
                pl.BlockSpec((1, rows, heads_local * 3 * HD), lambda g, m: (0, 0, m[0])),
                pl.BlockSpec((1, lat, heads_local * HD), lambda g, m: (m[1], 0, m[0])),
            ],
            out_specs=[pl.BlockSpec((rows, w), lambda g, m: (0, 0)) for w in widths],
        ),
        out_shape=[jax.ShapeDtypeStruct((rows, w), jnp.bfloat16) for w in widths],
        compiler_params=pltpu.CompilerParams(vmem_limit_bytes=VMEM_LIMIT),
        cost_estimate=pl.CostEstimate(
            flops=2 * rows * lat * heads_local * HD,
            bytes_accessed=rows * heads_local * HD * 12,
            transcendentals=0,
        ),
        name="pack",
    )(place, qkv, readout_t)


def attend_kernel(seq_count, count, value_head, lat, block, last, frames_ref, factor_ref, me_ref, *refs):
    pieces = refs[:seq_count]
    others = refs[seq_count:-4]
    held, kept, total_ref, sems = refs[-4:]
    rows = pieces[0].shape[0]
    tokens = seq_count * rows
    spans = frames_ref.shape[0]
    log2_scale = math.log2(math.e) / math.sqrt(HD)
    per_block = block // rows
    own = value_head == 0
    if own:
        value_refs, earlier, outs = None, None, others
        value_column = count * 2 * HD
    else:
        value_refs, earlier, outs = others[:seq_count], others[seq_count], others[seq_count + 1 :]
        value_column = 0

    copies = [pltpu.make_async_copy(pieces[k], held.at[k], sems.at[k]) for k in range(seq_count)]
    if not own:
        width = kept.shape[2]
        start = value_refs[0].shape[1] - width
        copies += [
            pltpu.make_async_copy(value_refs[k].at[:, start:], kept.at[k], sems.at[seq_count + k])
            for k in range(seq_count)
        ]
    for copy in copies:
        copy.start()
    for copy in copies:
        copy.wait()
    value_source = held if own else kept

    def ends_of():
        end = frames_ref[0] * FRAME_TOK
        ends = [end]
        for c in range(1, spans):
            end = end + frames_ref[c] * FRAME_TOK
            ends.append(end)
        return ends

    ends = ends_of()
    me = me_ref[0]
    row_places = lax.broadcasted_iota(jnp.int32, (rows, 1), 0)
    key_places = jnp.concatenate([(me ^ k) * rows + row_places for k in range(seq_count)], axis=0)
    column_places = lax.broadcasted_iota(jnp.int32, (1, rows), 1)

    def one_block(b, carry):
        first = b * per_block
        places = jnp.concatenate(
            [(me ^ (first + j)) * rows + column_places for j in range(per_block)], axis=1
        )
        bound = jnp.full((1, block), ends[0], jnp.int32)
        for c in range(1, spans):
            bound = jnp.where(places >= ends[c - 1], ends[c], bound)
        allowed = key_places < bound
        total = None
        for i in range(count):
            queries = held[pl.ds(first, per_block), :, i * 2 * HD : i * 2 * HD + HD]
            queries = queries.reshape(block, HD)
            keys = held[:, :, i * 2 * HD + HD : (i + 1) * 2 * HD].reshape(tokens, HD)
            scores = lax.dot_general(keys, queries, NT, preferred_element_type=jnp.float32)
            scores = jnp.where(allowed, scores, -jnp.inf)
            peak = jnp.max(scores, axis=0, keepdims=True)
            raw = jnp.exp2((scores - peak) * log2_scale)
            row_total = jnp.sum(raw, axis=0, keepdims=True)
            weights = raw.astype(jnp.bfloat16)
            h = value_head + i
            column = value_column + (h * lat // HD) * HD
            row = (h * lat) % HD
            folded = jnp.concatenate(
                [value_source[s, row : row + lat, column : column + HD] for s in range(seq_count)], axis=1
            )
            summed = jnp.dot(folded, weights, preferred_element_type=jnp.float32) / row_total
            total = summed if total is None else total + summed
        for j in range(per_block):
            part = total[:, j * rows : (j + 1) * rows]
            if earlier is not None:
                part = part + earlier[first + j]
            total_ref[first + j] = part
        return carry

    lax.fori_loop(0, seq_count // per_block, one_block, 0)
    if last:
        for k in range(seq_count):
            outs[k][...] = (total_ref[k] * factor_ref[0]).astype(jnp.bfloat16)
    else:
        outs[0][...] = total_ref[...]


def attend(pieces, value_pieces, earlier, span_frames, factor, me, count, value_head, lat, last):
    seq_count = len(pieces)
    rows, width = pieces[0].shape
    tokens = seq_count * rows
    smem = pl.BlockSpec(memory_space=pltpu.SMEM)
    vmem = pl.BlockSpec(memory_space=pltpu.VMEM)
    anywhere = pl.BlockSpec(memory_space=pl.ANY)
    operands = [span_frames, factor, me] + list(pieces)
    in_specs = [smem] * 3 + [anywhere] * seq_count
    value_width = HD
    if value_head:
        operands += list(value_pieces) + [earlier]
        in_specs += [anywhere] * seq_count + [vmem]
        value_width = -(-(value_head + count) * lat // HD) * HD
    if last:
        out_shape = [jax.ShapeDtypeStruct((lat, rows), jnp.bfloat16)] * seq_count
    else:
        out_shape = [jax.ShapeDtypeStruct((seq_count, lat, rows), jnp.float32)]
    return pl.pallas_call(
        functools.partial(attend_kernel, seq_count, count, value_head, lat, 2 * rows, last),
        in_specs=in_specs,
        out_specs=[vmem] * len(out_shape),
        out_shape=out_shape,
        scratch_shapes=[
            pltpu.VMEM((seq_count, rows, width), jnp.bfloat16),
            pltpu.VMEM((seq_count, rows, value_width), jnp.bfloat16),
            pltpu.VMEM((seq_count, lat, rows), jnp.float32),
            pltpu.SemaphoreType.DMA((2 * seq_count,)),
        ],
        compiler_params=pltpu.CompilerParams(vmem_limit_bytes=VMEM_LIMIT),
        cost_estimate=pl.CostEstimate(
            flops=count * tokens * tokens * 2 * (HD + lat),
            bytes_accessed=tokens * width * 2,
            transcendentals=count * tokens * tokens,
        ),
        name="attend",
    )(*operands)


def swap(array, axis, offset):
    size = lax.axis_size(axis)
    return lax.ppermute(array, axis, [(i, i ^ offset) for i in range(size)])


def body(qkv, readout, step_weight, timestep, span_frames):
    seq_count = lax.axis_size("seq")
    mp_count = lax.axis_size("mp")
    heads_local = HEADS // seq_count
    lat = readout.shape[2]
    me = lax.axis_index("seq").astype(jnp.int32)
    mp_index = lax.axis_index("mp")
    sample_count = mp_count // 2
    model_index = (mp_index // sample_count).astype(jnp.int32)
    sample_index = mp_index % sample_count
    signed = jnp.where(model_index == 1, 1.0, -1.0).astype(jnp.float32)
    factor = (signed * step_weight[timestep[sample_index]]).reshape(1)
    chunks = [heads_local - 1, 1] if heads_local > 1 else [1]
    widths = [c * 2 * HD for c in chunks]
    widths[0] += -(-heads_local * lat // HD) * HD
    readout_t = jnp.swapaxes(readout, 1, 2)

    arrived = [[None] * seq_count for _ in chunks]
    for k in range(seq_count - 1, -1, -1):
        packed = pack(jnp.stack([me ^ k, model_index]), qkv, readout_t, chunks, widths)
        for c, array in enumerate(packed):
            arrived[c][k] = swap(array, "seq", k) if k else array

    result, head = None, 0
    for c, count in enumerate(chunks):
        result = attend(
            arrived[c], arrived[0], result, span_frames, factor, me.reshape(1), count, head, lat, c == len(chunks) - 1
        )
        head += count
        if c < len(chunks) - 1:
            result = result[0]
    own = result[0].astype(jnp.float32)
    for k in range(seq_count - 1, 0, -1):
        own = own + swap(result[k], "seq", k).astype(jnp.float32)
    whole = own
    for k in range(mp_count - 1, 0, -1):
        whole = whole + swap(own, "mp", k)
    return whole.T


def solution(mesh):
    return jax.shard_map(
        body,
        mesh=mesh,
        in_specs=(P("mp", "seq", None), P(), P(), P(), P()),
        out_specs=P("seq", None),
        check_vma=False,
    )
```

time: 110 us -> 107 us (0.973)
  blocking collectives: 60 us -> 0 us
  starting transfers between devices: 3.72 us -> 42.1 us
  local copies, waits for them, and re-layouts: 3.09 us -> 11.2 us
  Pallas kernels: 20 us -> 27.1 us
  waiting for transfers between devices: 19.7 us -> 22.9 us
    all_to_all x2 -> x0, blocking collectives: 49.2 us -> none  [the longest x1 38.4 us: body(): lax.all_to_all(p, 'seq', split_axis=0, concat_axis=0, tiled=True)]
    ppermute x0 -> x24, starting transfers between devices: none -> 42.1 us  [swap(): return lax.ppermute(array, axis, [(i, i ^ offset) for i in range(size)])]
    ppermute x0 -> x24, waiting for transfers between devices: none -> 22.9 us  [swap(): return lax.ppermute(array, axis, [(i, i ^ offset) for i in range(size)])]
    all_to_all x1 -> x0, waiting for transfers between devices: 19.7 us -> none  [body(): lax.all_to_all(p, 'seq', split_axis=0, concat_axis=0, tiled=True)]
    psum x1 -> x0, blocking collectives: 10.9 us -> none  [body(): return lax.psum(own, 'mp').T]
    unnamed x6 -> x38, local copies, waits for them, and re-layouts: 1.23 us -> 9.32 us
    pallas_call x3 -> x10, Pallas kernels: 20 us -> 27.1 us  [the longest x2 16.1 us: attend(): pl.pallas_call(functools.partial(attend_kernel, seq_count, count, value_h...]
    all_to_all x1 -> x0, starting transfers between devices: 3.72 us -> none  [body(): lax.all_to_all(p, 'seq', split_axis=0, concat_axis=0, tiled=True)]
  transfers between devices with their start and end apart: 1 -> 24, of which waited for: 1 -> 6; matrix products, arithmetic and copies ran while one was open for 2% -> 2% of each run, Pallas kernels for 6% -> 19%
where the time goes in v2:
time: 107 us
  starting transfers between devices  42.1 us (39%)
  Pallas kernels  27.1 us (25%)
  waiting for transfers between devices  22.9 us (21%)
  local copies, waits for them, and re-layouts  11.2 us (10%)
  between operations  2.76 us (3%)
    ppermute x24, starting transfers between devices, swap(): return lax.ppermute(array, axis, [(i, i ^ offset) for i in range(size)])  42.1 us
    ppermute x24, waiting for transfers between devices, swap(): return lax.ppermute(array, axis, [(i, i ^ offset) for i in range(size)])  22.9 us
    pallas_call x2, Pallas kernels, attend(): pl.pallas_call(functools.partial(attend_kernel, seq_count, count, value_h...  16.1 us
    pallas_call x8, Pallas kernels, pack(): pl.pallas_call(functools.partial(pack_kernel, chunks), grid_spec=pltpu.Pr...  11 us
    unnamed x38, local copies, waits for them, and re-layouts  9.32 us
  transfers between devices with their start and end apart: 24, of which 6 were waited for; matrix products, arithmetic and copies ran while one was open for 2% of the time, Pallas kernels for 19%

profile of v2, /device:TPU:0, one launch (start us, length us, event | category | flops | bytes accessed | tf_op | source)
XLA Modules:
  0.0 106.9 jit_solution(763817489419335082)
XLA Ops:
  0.0 0.1 pad_add_fusion.4
  0.1 1.9 %copy-done = bf16[1,128,12288]{2,1,0:T(8,128)(2,1)S(1)} copy-done((bf16[1,128,12288]{2,1,0:T(8,128)(2,1)S(1)}, bf16[1,128,12288]{2,1,0:T(8,128)(2,1)}, u32[]{:S(2)}) %copy-start) | copy-done | bytes 3145752
  2.0 1.2 %copy-done.2 = bf16[2,4096,64]{1,2,0:T(8,128)(2,1)S(1)} copy-done((bf16[2,4096,64]{1,2,0:T(8,128)(2,1)S(1)}, bf16[2,4096,64]{1,2,0:T(8,128)(2,1)}, u32[]{:S(2)}) %copy-start.2) | copy-done | bytes 1048600
  3.2 1.5 %pack.12 = (bf16[128,1024]{1,0:T(8,128)(2,1)}, bf16[128,256]{1,0:T(8,128)(2,1)}) custom-call(s32[2]{0:T(128)S(1)} %get-tuple-element.57.place_ref, bf16[1,128,12288]{2,1,0:T(8,128)(2,1)S(1)} %copy-done, bf16[2,64,4096]{2,1,0:T(8,128)(2,1)S(1)} %bitcast.15), custom_call_target="tpu_custom_call" | custom-call | flops 8388608 | bytes 786432 | tf_op jit(solution)/shard_map/pack/pallas_call | solution.py:40
  4.7 4.0 %collective-permute-start.10 = (bf16[128,1024]{1,0:T(8,128)(2,1)}, bf16[128,1024]{1,0:T(8,128)(2,1)S(1)}, u32[]{:S(2)}, u32[]{:S(2)}) collective-permute-start(bf16[128,1024]{1,0:T(8,128)(2,1)} %get-tuple-element.41), channel_id=1, source_target_pairs={{0,16},{4,20},{8,24},{12,28},{16,0},{20,4},{24,8},{28,12},{1,17},{... | collective-permute-start | bytes 786440 | tf_op jit(solution)/shard_map/ppermute | solution.py:191
  8.8 1.2 %copy-done.3 = bf16[2,4096,64]{1,2,0:T(8,128)(2,1)S(1)} copy-done((bf16[2,4096,64]{1,2,0:T(8,128)(2,1)S(1)}, bf16[2,4096,64]{1,2,0:T(8,128)(2,1)}, u32[]{:S(2)}) %copy-start.3) | copy-done | bytes 1048600
  10.0 1.5 %pack.14 = (bf16[128,1024]{1,0:T(8,128)(2,1)}, bf16[128,256]{1,0:T(8,128)(2,1)}) custom-call(s32[2]{0:T(128)S(1)} %get-tuple-element.59.place_ref, bf16[1,128,12288]{2,1,0:T(8,128)(2,1)S(1)} %copy-done.1, bf16[2,64,4096]{2,1,0:T(8,128)(2,1)S(1)} %bitcast.16), custom_call_target="tpu_custom_call" | custom-call | flops 8388608 | bytes 786432 | tf_op jit(solution)/shard_map/pack/pallas_call | solution.py:40
  11.4 1.5 %collective-permute-start.12 = (bf16[128,1024]{1,0:T(8,128)(2,1)}, bf16[128,1024]{1,0:T(8,128)(2,1)}, u32[]{:S(2)}, u32[]{:S(2)}) collective-permute-start(bf16[128,1024]{1,0:T(8,128)(2,1)} %get-tuple-element.43), channel_id=1, source_target_pairs={{0,24},{4,28},{8,16},{12,20},{16,8},{20,12},{24,0},{28,4},{1,25},{... | collective-permute-start | bytes 786440 | tf_op jit(solution)/shard_map/ppermute | solution.py:191
  12.9 1.6 %collective-permute-start.3 = (bf16[128,256]{1,0:T(8,128)(2,1)}, bf16[128,256]{1,0:T(8,128)(2,1)S(1)}, u32[]{:S(2)}, u32[]{:S(2)}) collective-permute-start(bf16[128,256]{1,0:T(8,128)(2,1)} %get-tuple-element.33), channel_id=1, source_target_pairs={{0,16},{4,20},{8,24},{12,28},{16,0},{20,4},{24,8},{28,12},{1,17},{... | collective-permute-start | bytes 196616 | tf_op jit(solution)/shard_map/ppermute | solution.py:191
  14.5 0.9 collective-permute-start.5
  15.5 1.2 %copy-done.4 = bf16[2,4096,64]{1,2,0:T(8,128)(2,1)S(1)} copy-done((bf16[2,4096,64]{1,2,0:T(8,128)(2,1)S(1)}, bf16[2,4096,64]{1,2,0:T(8,128)(2,1)}, u32[]{:S(2)}) %copy-start.4) | copy-done | bytes 1048600
  16.7 1.5 %pack.10 = (bf16[128,1024]{1,0:T(8,128)(2,1)}, bf16[128,256]{1,0:T(8,128)(2,1)S(1)}) custom-call(s32[2]{0:T(128)S(1)} %get-tuple-element.55.place_ref, bf16[1,128,12288]{2,1,0:T(8,128)(2,1)S(1)} %copy-done.1, bf16[2,64,4096]{2,1,0:T(8,128)(2,1)S(1)} %bitcast.17), custom_call_target="tpu_custom_call" | custom-call | flops 8388608 | bytes 786432 | tf_op jit(solution)/shard_map/pack/pallas_call | solution.py:40
  18.2 0.6 copy-done.8
  18.8 1.0 collective-permute-start.8
  19.9 1.2 %copy-done.5 = bf16[2,4096,64]{1,2,0:T(8,128)(2,1)S(1)} copy-done((bf16[2,4096,64]{1,2,0:T(8,128)(2,1)S(1)}, bf16[2,4096,64]{1,2,0:T(8,128)(2,1)}, u32[]{:S(2)}) %copy-start.5) | copy-done | bytes 1048600
  21.1 1.5 %pack.9 = (bf16[128,1024]{1,0:T(8,128)(2,1)}, bf16[128,256]{1,0:T(8,128)(2,1)S(1)}) custom-call(s32[2]{0:T(128)S(1)} %get-tuple-element.54.place_ref, bf16[1,128,12288]{2,1,0:T(8,128)(2,1)S(1)} %copy-done.1, bf16[2,64,4096]{2,1,0:T(8,128)(2,1)S(1)} %bitcast.18), custom_call_target="tpu_custom_call" | custom-call | flops 8388608 | bytes 786432 | tf_op jit(solution)/shard_map/pack/pallas_call | solution.py:40
  22.6 1.5 %pack.13 = (bf16[128,1024]{1,0:T(8,128)(2,1)}, bf16[128,256]{1,0:T(8,128)(2,1)S(1)}) custom-call(s32[2]{0:T(128)S(1)} %get-tuple-element.58.place_ref, bf16[1,128,12288]{2,1,0:T(8,128)(2,1)S(1)} %copy-done.1, bf16[2,64,4096]{2,1,0:T(8,128)(2,1)S(1)} %bitcast.19), custom_call_target="tpu_custom_call" | custom-call | flops 8388608 | bytes 786432 | tf_op jit(solution)/shard_map/pack/pallas_call | solution.py:40
  24.1 1.4 %pack.15 = (bf16[128,1024]{1,0:T(8,128)(2,1)}, bf16[128,256]{1,0:T(8,128)(2,1)S(1)}) custom-call(s32[2]{0:T(128)S(1)} %get-tuple-element.60.place_ref, bf16[1,128,12288]{2,1,0:T(8,128)(2,1)S(1)} %copy-done.1, bf16[2,64,4096]{2,1,0:T(8,128)(2,1)S(1)} %bitcast.20), custom_call_target="tpu_custom_call" | custom-call | flops 8388608 | bytes 786432 | tf_op jit(solution)/shard_map/pack/pallas_call | solution.py:40
  25.5 1.5 %pack.11 = (bf16[128,1024]{1,0:T(8,128)(2,1)}, bf16[128,256]{1,0:T(8,128)(2,1)S(1)}) custom-call(s32[2]{0:T(128)S(1)} %get-tuple-element.56.place_ref, bf16[1,128,12288]{2,1,0:T(8,128)(2,1)S(1)} %copy-done.1, bf16[2,64,4096]{2,1,0:T(8,128)(2,1)S(1)} %bitcast.21), custom_call_target="tpu_custom_call" | custom-call | flops 8388608 | bytes 786432 | tf_op jit(solution)/shard_map/pack/pallas_call | solution.py:40
  27.0 0.6 copy-done.16
  27.6 9.4 %collective-permute-done.3.refs_4_ = bf16[128,256]{1,0:T(8,128)(2,1)S(1)} collective-permute-done((bf16[128,256]{1,0:T(8,128)(2,1)}, bf16[128,256]{1,0:T(8,128)(2,1)S(1)}, u32[]{:S(2)}, u32[]{:S(2)}) %collective-permute-start.3) | collective-permute-done | bytes 65568 | tf_op jit(solution)/shard_map/ppermute | solution.py:191
  37.0 1.5 %collective-permute-start.7 = (bf16[128,1024]{1,0:T(8,128)(2,1)}, bf16[128,1024]{1,0:T(8,128)(2,1)}, u32[]{:S(2)}, u32[]{:S(2)}) collective-permute-start(bf16[128,1024]{1,0:T(8,128)(2,1)} %get-tuple-element.38), channel_id=1, source_target_pairs={{0,4},{4,0},{8,12},{12,8},{16,20},{20,16},{24,28},{28,24},{1,5},{5... | collective-permute-start | bytes 786440 | tf_op jit(solution)/shard_map/ppermute | solution.py:191
  38.5 2.7 %collective-permute-start.11 = (bf16[128,1024]{1,0:T(8,128)(2,1)}, bf16[128,1024]{1,0:T(8,128)(2,1)}, u32[]{:S(2)}, u32[]{:S(2)}) collective-permute-start(bf16[128,1024]{1,0:T(8,128)(2,1)} %get-tuple-element.42), channel_id=1, source_target_pairs={{0,20},{4,16},{8,28},{12,24},{16,4},{20,0},{24,12},{28,8},{1,21},{... | collective-permute-start | bytes 786440 | tf_op jit(solution)/shard_map/ppermute | solution.py:191
  41.2 0.7 collective-permute-start.13
  42.0 1.0 collective-permute-start.9
  43.0 0.6 dynamic_slice.6
  45.5 1.3 %dynamic_slice.7 = f32[1]{0:T(128)} dynamic-slice(f32[1000]{0:T(1024)} %param.7, s32[]{:T(128)S(6)} %select_n.25), dynamic_slice_sizes={1} | dynamic-slice | bytes 12 | tf_op jit(solution)/shard_map/dynamic_slice | solution.py:205
  47.4 1.2 %copy-done.6 = bf16[2,4096,64]{1,2,0:T(8,128)(2,1)S(1)} copy-done((bf16[2,4096,64]{1,2,0:T(8,128)(2,1)S(1)}, bf16[2,4096,64]{1,2,0:T(8,128)(2,1)}, u32[]{:S(2)}) %copy-start.6) | copy-done | bytes 1048600
  48.7 0.8 pack.8
  49.5 1.8 %collective-permute-start.1 = (bf16[128,256]{1,0:T(8,128)(2,1)S(1)}, bf16[128,256]{1,0:T(8,128)(2,1)S(1)}, u32[]{:S(2)}, u32[]{:S(2)}) collective-permute-start(bf16[128,256]{1,0:T(8,128)(2,1)S(1)} %copy-done.9), channel_id=1, source_target_pairs={{0,8},{4,12},{8,0},{12,4},{16,24},{20,28},{24,16},{28,20},{1,9},{5... | collective-permute-start | bytes 196616 | tf_op jit(solution)/shard_map/ppermute | solution.py:191
  51.3 0.7 collective-permute-start
  52.0 7.7 %collective-permute-done.11.refs_5_.refs_13_ = bf16[128,1024]{1,0:T(8,128)(2,1)} collective-permute-done((bf16[128,1024]{1,0:T(8,128)(2,1)}, bf16[128,1024]{1,0:T(8,128)(2,1)}, u32[]{:S(2)}, u32[]{:S(2)}) %collective-permute-start.11) | collective-permute-done | bytes 262176 | tf_op jit(solution)/shard_map/ppermute | solution.py:191
  59.8 6.5 %collective-permute-start.6 = (bf16[128,256]{1,0:T(8,128)(2,1)S(1)}, bf16[128,256]{1,0:T(8,128)(2,1)S(1)}, u32[]{:S(2)}, u32[]{:S(2)}) collective-permute-start(bf16[128,256]{1,0:T(8,128)(2,1)S(1)} %copy-done.15), channel_id=1, source_target_pairs={{0,28},{4,24},{8,20},{12,16},{16,12},{20,8},{24,4},{28,0},{1,29},{... | collective-permute-start | bytes 196616 | tf_op jit(solution)/shard_map/ppermute | solution.py:191
  66.3 4.9 %collective-permute-start.2 = (bf16[128,256]{1,0:T(8,128)(2,1)S(1)}, bf16[128,256]{1,0:T(8,128)(2,1)S(1)}, u32[]{:S(2)}, u32[]{:S(2)}) collective-permute-start(bf16[128,256]{1,0:T(8,128)(2,1)S(1)} %copy-done.17), channel_id=1, source_target_pairs={{0,12},{4,8},{8,4},{12,0},{16,28},{20,24},{24,20},{28,16},{1,13},{... | collective-permute-start | bytes 196616 | tf_op jit(solution)/shard_map/ppermute | solution.py:191
  71.2 10.6 %attend.2.refs_16_ = f32[8,64,128]{2,1,0:T(8,128)S(1)} custom-call(s32[4]{0:T(128)S(1)} %copy-done.7, f32[1]{0:T(128)} %bitcast.2.factor_ref, s32[1]{0:T(128)} %bitcast.3.me_ref, bf16[128,1024]{1,0:T(8,128)(2,1)S(1)} %get-tuple-element.37.refs_0_.refs_8_, bf16[128,1024]{1,0:T(8,128)(2,1)} %collective-permute-done.7.refs_1_.refs_9_, ...), custom_call_target="tpu_custom_call" | custom-call | flops 1207959552 | bytes 2097152 | tf_op jit(solution)/shard_map/attend/pallas_call | solution.py:168
  81.9 5.5 %attend.3 = (bf16[64,128]{1,0:T(8,128)(2,1)S(1)}, bf16[64,128]{1,0:T(8,128)(2,1)S(1)}, bf16[64,128]{1,0:T(8,128)(2,1)S(1)}, bf16[64,128]{1,0:T(8,128)(2,1)S(1)},...) custom-call(s32[4]{0:T(128)S(1)} %copy-done.7, ...), custom_call_target="tpu_custom_call" | custom-call | flops 402653184 | bytes 524288 | tf_op jit(solution)/shard_map/attend/pallas_call | solution.py:168
  87.4 2.4 %collective-permute-start.14 = (bf16[64,128]{1,0:T(8,128)(2,1)S(1)}, bf16[64,128]{1,0:T(8,128)(2,1)S(1)}, u32[]{:S(2)}, u32[]{:S(2)}) collective-permute-start(bf16[64,128]{1,0:T(8,128)(2,1)S(1)} %get-tuple-element.46), channel_id=1, source_target_pairs={{0,28},{4,24},{8,20},{12,16},{16,12},{20,8},{24,4},{28,0},{1,29},{... | collective-permute-start | bytes 49160 | tf_op jit(solution)/shard_map/ppermute | solution.py:191
  89.8 1.9 %collective-permute-start.15 = (bf16[64,128]{1,0:T(8,128)(2,1)S(1)}, bf16[64,128]{1,0:T(8,128)(2,1)S(1)}, u32[]{:S(2)}, u32[]{:S(2)}) collective-permute-start(bf16[64,128]{1,0:T(8,128)(2,1)S(1)} %get-tuple-element.47), channel_id=1, source_target_pairs={{0,24},{4,28},{8,16},{12,20},{16,8},{20,12},{24,0},{28,4},{1,25},{... | collective-permute-start | bytes 49160 | tf_op jit(solution)/shard_map/ppermute | solution.py:191
  91.7 3.4 %collective-permute-start.17 = (bf16[64,128]{1,0:T(8,128)(2,1)S(1)}, bf16[64,128]{1,0:T(8,128)(2,1)S(1)}, u32[]{:S(2)}, u32[]{:S(2)}) collective-permute-start(bf16[64,128]{1,0:T(8,128)(2,1)S(1)} %get-tuple-element.49), channel_id=1, source_target_pairs={{0,16},{4,20},{8,24},{12,28},{16,0},{20,4},{24,8},{28,12},{1,17},{... | collective-permute-start | bytes 49160 | tf_op jit(solution)/shard_map/ppermute | solution.py:191
  95.1 2.4 %collective-permute-start.19 = (bf16[64,128]{1,0:T(8,128)(2,1)S(1)}, bf16[64,128]{1,0:T(8,128)(2,1)S(1)}, u32[]{:S(2)}, u32[]{:S(2)}) collective-permute-start(bf16[64,128]{1,0:T(8,128)(2,1)S(1)} %get-tuple-element.51), channel_id=1, source_target_pairs={{0,8},{4,12},{8,0},{12,4},{16,24},{20,28},{24,16},{28,20},{1,9},{5... | collective-permute-start | bytes 49160 | tf_op jit(solution)/shard_map/ppermute | solution.py:191
  97.5 1.1 collective-permute-start.20
  98.6 1.1 %collective-permute-done.18 = bf16[64,128]{1,0:T(8,128)(2,1)S(1)} collective-permute-done((bf16[64,128]{1,0:T(8,128)(2,1)S(1)}, bf16[64,128]{1,0:T(8,128)(2,1)S(1)}, u32[]{:S(2)}, u32[]{:S(2)}) %collective-permute-start.18) | collective-permute-done | bytes 16416 | tf_op jit(solution)/shard_map/ppermute | solution.py:191
  99.7 1.5 %collective-permute-done.20 = bf16[64,128]{1,0:T(8,128)(2,1)S(1)} collective-permute-done((bf16[64,128]{1,0:T(8,128)(2,1)S(1)}, bf16[64,128]{1,0:T(8,128)(2,1)S(1)}, u32[]{:S(2)}, u32[]{:S(2)}) %collective-permute-start.20) | collective-permute-done | bytes 16416 | tf_op jit(solution)/shard_map/ppermute | solution.py:191
  101.4 1.6 %collective-permute-start.22 = (f32[64,128]{1,0:T(8,128)S(1)}, f32[64,128]{1,0:T(8,128)S(1)}, u32[]{:S(2)}, u32[]{:S(2)}) collective-permute-start(f32[64,128]{1,0:T(8,128)S(1)} %convert_add_fusion), channel_id=1, source_target_pairs={{0,2},{1,3},{2,0},{3,1},{4,6},{5,7},{6,4},{7,5},{8,10},{9,11},{10,... | collective-permute-start | bytes 98312 | tf_op jit(solution)/shard_map/ppermute | solution.py:191
  102.9 0.3 collective-permute-start.21
  103.2 2.1 %collective-permute-done.22 = f32[64,128]{1,0:T(8,128)S(1)} collective-permute-done((f32[64,128]{1,0:T(8,128)S(1)}, f32[64,128]{1,0:T(8,128)S(1)}, u32[]{:S(2)}, u32[]{:S(2)}) %collective-permute-start.22) | collective-permute-done | bytes 32800 | tf_op jit(solution)/shard_map/ppermute | solution.py:191
  105.3 0.9 collective-permute-done.21
  106.3 0.6 add_bitcast_fusion
  (56 shorter events, 0.5 us)
Async XLA Ops:
  0.1 1.9 %copy-start = (bf16[1,128,12288]{2,1,0:T(8,128)(2,1)S(1)}, bf16[1,128,12288]{2,1,0:T(8,128)(2,1)}, u32[]{:S(2)}) copy-start(bf16[1,128,12288]{2,1,0:T(8,128)(2,1)} %qkv_ref.15) | copy-start | bytes 9437188
  2.0 1.2 %copy-start.2 = (bf16[2,4096,64]{1,2,0:T(8,128)(2,1)S(1)}, bf16[2,4096,64]{1,2,0:T(8,128)(2,1)}, u32[]{:S(2)}) copy-start(bf16[2,4096,64]{1,2,0:T(8,128)(2,1)} %param.6) | copy-start | bytes 3145732
  3.2 5.6 %copy-start.1 = (bf16[1,128,12288]{2,1,0:T(8,128)(2,1)S(1)}, bf16[1,128,12288]{2,1,0:T(8,128)(2,1)}, u32[]{:S(2)}) copy-start(bf16[1,128,12288]{2,1,0:T(8,128)(2,1)} %qkv_ref.15) | copy-start | bytes 9437188
  4.7 36.6 %collective-permute-start.10 = (bf16[128,1024]{1,0:T(8,128)(2,1)}, bf16[128,1024]{1,0:T(8,128)(2,1)S(1)}, u32[]{:S(2)}, u32[]{:S(2)}) collective-permute-start(bf16[128,1024]{1,0:T(8,128)(2,1)} %get-tuple-element.41), channel_id=1, source_target_pairs={{0,16},{4,20},{8,24},{12,28},{16,0},{20,4},{24,8},{28,12},{1,17},{... | collective-permute-start | bytes 786440 | tf_op jit(solution)/shard_map/ppermute | solution.py:191
  8.8 1.2 %copy-start.3 = (bf16[2,4096,64]{1,2,0:T(8,128)(2,1)S(1)}, bf16[2,4096,64]{1,2,0:T(8,128)(2,1)}, u32[]{:S(2)}) copy-start(bf16[2,4096,64]{1,2,0:T(8,128)(2,1)} %param.6) | copy-start | bytes 3145732
  11.4 30.5 %collective-permute-start.12 = (bf16[128,1024]{1,0:T(8,128)(2,1)}, bf16[128,1024]{1,0:T(8,128)(2,1)}, u32[]{:S(2)}, u32[]{:S(2)}) collective-permute-start(bf16[128,1024]{1,0:T(8,128)(2,1)} %get-tuple-element.43), channel_id=1, source_target_pairs={{0,24},{4,28},{8,16},{12,20},{16,8},{20,12},{24,0},{28,4},{1,25},{... | collective-permute-start | bytes 786440 | tf_op jit(solution)/shard_map/ppermute | solution.py:191
  12.9 24.0 %collective-permute-start.3 = (bf16[128,256]{1,0:T(8,128)(2,1)}, bf16[128,256]{1,0:T(8,128)(2,1)S(1)}, u32[]{:S(2)}, u32[]{:S(2)}) collective-permute-start(bf16[128,256]{1,0:T(8,128)(2,1)} %get-tuple-element.33), channel_id=1, source_target_pairs={{0,16},{4,20},{8,24},{12,28},{16,0},{20,4},{24,8},{28,12},{1,17},{... | collective-permute-start | bytes 196616 | tf_op jit(solution)/shard_map/ppermute | solution.py:191
  14.5 24.0 %collective-permute-start.5 = (bf16[128,256]{1,0:T(8,128)(2,1)}, bf16[128,256]{1,0:T(8,128)(2,1)S(1)}, u32[]{:S(2)}, u32[]{:S(2)}) collective-permute-start(bf16[128,256]{1,0:T(8,128)(2,1)} %get-tuple-element.35), channel_id=1, source_target_pairs={{0,24},{4,28},{8,16},{12,20},{16,8},{20,12},{24,0},{28,4},{1,25},{... | collective-permute-start | bytes 196616 | tf_op jit(solution)/shard_map/ppermute | solution.py:191
  15.5 1.2 %copy-start.4 = (bf16[2,4096,64]{1,2,0:T(8,128)(2,1)S(1)}, bf16[2,4096,64]{1,2,0:T(8,128)(2,1)}, u32[]{:S(2)}) copy-start(bf16[2,4096,64]{1,2,0:T(8,128)(2,1)} %param.6) | copy-start | bytes 3145732
  18.2 0.6 copy-start.8
  18.8 30.7 %collective-permute-start.8 = (bf16[128,1024]{1,0:T(8,128)(2,1)}, bf16[128,1024]{1,0:T(8,128)(2,1)}, u32[]{:S(2)}, u32[]{:S(2)}) collective-permute-start(bf16[128,1024]{1,0:T(8,128)(2,1)} %get-tuple-element.39), channel_id=1, source_target_pairs={{0,8},{4,12},{8,0},{12,4},{16,24},{20,28},{24,16},{28,20},{1,9},{5... | collective-permute-start | bytes 786440 | tf_op jit(solution)/shard_map/ppermute | solution.py:191
  19.9 1.2 %copy-start.5 = (bf16[2,4096,64]{1,2,0:T(8,128)(2,1)S(1)}, bf16[2,4096,64]{1,2,0:T(8,128)(2,1)}, u32[]{:S(2)}) copy-start(bf16[2,4096,64]{1,2,0:T(8,128)(2,1)} %param.6) | copy-start | bytes 3145732
  22.6 2.9 %copy-start.10 = (bf16[128,256]{1,0:T(8,128)(2,1)}, bf16[128,256]{1,0:T(8,128)(2,1)S(1)}, u32[]{:S(2)}) copy-start(bf16[128,256]{1,0:T(8,128)(2,1)S(1)} %get-tuple-element.30) | copy-start | bytes 196612
  24.0 2.9 %copy-start.12 = (bf16[128,256]{1,0:T(8,128)(2,1)}, bf16[128,256]{1,0:T(8,128)(2,1)S(1)}, u32[]{:S(2)}) copy-start(bf16[128,256]{1,0:T(8,128)(2,1)S(1)} %get-tuple-element.34) | copy-start | bytes 196612
  25.5 15.7 %copy-start.14 = (bf16[128,256]{1,0:T(8,128)(2,1)}, bf16[128,256]{1,0:T(8,128)(2,1)S(1)}, u32[]{:S(2)}) copy-start(bf16[128,256]{1,0:T(8,128)(2,1)S(1)} %get-tuple-element.36) | copy-start | bytes 196612
  25.5 17.4 %copy-start.18 = (s32[2]{0:T(128)S(1)}, s32[2]{0:T(128)}, u32[]{:S(2)}) copy-start(s32[2]{0:T(128)} %param.8) | copy-start | bytes 28
  27.0 0.6 copy-start.16
  27.6 43.6 %copy-start.7 = (s32[4]{0:T(128)S(1)}, s32[4]{0:T(128)}, u32[]{:S(2)}) copy-start(s32[4]{0:T(128)} %frames_ref.3) | copy-start | bytes 52
  37.0 14.3 %collective-permute-start.7 = (bf16[128,1024]{1,0:T(8,128)(2,1)}, bf16[128,1024]{1,0:T(8,128)(2,1)}, u32[]{:S(2)}, u32[]{:S(2)}) collective-permute-start(bf16[128,1024]{1,0:T(8,128)(2,1)} %get-tuple-element.38), channel_id=1, source_target_pairs={{0,4},{4,0},{8,12},{12,8},{16,20},{20,16},{24,28},{28,24},{1,5},{5... | collective-permute-start | bytes 786440 | tf_op jit(solution)/shard_map/ppermute | solution.py:191
  38.5 21.2 %collective-permute-start.11 = (bf16[128,1024]{1,0:T(8,128)(2,1)}, bf16[128,1024]{1,0:T(8,128)(2,1)}, u32[]{:S(2)}, u32[]{:S(2)}) collective-permute-start(bf16[128,1024]{1,0:T(8,128)(2,1)} %get-tuple-element.42), channel_id=1, source_target_pairs={{0,20},{4,16},{8,28},{12,24},{16,4},{20,0},{24,12},{28,8},{1,21},{... | collective-permute-start | bytes 786440 | tf_op jit(solution)/shard_map/ppermute | solution.py:191
  41.2 18.5 %collective-permute-start.13 = (bf16[128,1024]{1,0:T(8,128)(2,1)}, bf16[128,1024]{1,0:T(8,128)(2,1)}, u32[]{:S(2)}, u32[]{:S(2)}) collective-permute-start(bf16[128,1024]{1,0:T(8,128)(2,1)} %get-tuple-element.44), channel_id=1, source_target_pairs={{0,28},{4,24},{8,20},{12,16},{16,12},{20,8},{24,4},{28,0},{1,29},{... | collective-permute-start | bytes 786440 | tf_op jit(solution)/shard_map/ppermute | solution.py:191
  42.0 24.4 %collective-permute-start.9 = (bf16[128,1024]{1,0:T(8,128)(2,1)}, bf16[128,1024]{1,0:T(8,128)(2,1)}, u32[]{:S(2)}, u32[]{:S(2)}) collective-permute-start(bf16[128,1024]{1,0:T(8,128)(2,1)} %get-tuple-element.40), channel_id=1, source_target_pairs={{0,12},{4,8},{8,4},{12,0},{16,28},{20,24},{24,20},{28,16},{1,13},{... | collective-permute-start | bytes 786440 | tf_op jit(solution)/shard_map/ppermute | solution.py:191
  47.4 1.2 %copy-start.6 = (bf16[2,4096,64]{1,2,0:T(8,128)(2,1)S(1)}, bf16[2,4096,64]{1,2,0:T(8,128)(2,1)}, u32[]{:S(2)}) copy-start(bf16[2,4096,64]{1,2,0:T(8,128)(2,1)} %param.6) | copy-start | bytes 3145732
  48.6 0.8 copy-start.9
  48.6 2.7 %copy-start.11 = (bf16[128,256]{1,0:T(8,128)(2,1)S(1)}, bf16[128,256]{1,0:T(8,128)(2,1)}, u32[]{:S(2)}) copy-start(bf16[128,256]{1,0:T(8,128)(2,1)} %copy-done.10) | copy-start | bytes 196612
  48.6 11.1 %copy-start.13 = (bf16[128,256]{1,0:T(8,128)(2,1)S(1)}, bf16[128,256]{1,0:T(8,128)(2,1)}, u32[]{:S(2)}) copy-start(bf16[128,256]{1,0:T(8,128)(2,1)} %copy-done.12) | copy-start | bytes 196612
  48.6 11.1 %copy-start.15 = (bf16[128,256]{1,0:T(8,128)(2,1)S(1)}, bf16[128,256]{1,0:T(8,128)(2,1)}, u32[]{:S(2)}) copy-start(bf16[128,256]{1,0:T(8,128)(2,1)} %copy-done.14) | copy-start | bytes 196612
  48.6 17.7 %copy-start.17 = (bf16[128,256]{1,0:T(8,128)(2,1)S(1)}, bf16[128,256]{1,0:T(8,128)(2,1)}, u32[]{:S(2)}) copy-start(bf16[128,256]{1,0:T(8,128)(2,1)} %copy-done.16) | copy-start | bytes 196612
  49.5 32.3 %collective-permute-start.1 = (bf16[128,256]{1,0:T(8,128)(2,1)S(1)}, bf16[128,256]{1,0:T(8,128)(2,1)S(1)}, u32[]{:S(2)}, u32[]{:S(2)}) collective-permute-start(bf16[128,256]{1,0:T(8,128)(2,1)S(1)} %copy-done.9), channel_id=1, source_target_pairs={{0,8},{4,12},{8,0},{12,4},{16,24},{20,28},{24,16},{28,20},{1,9},{5... | collective-permute-start | bytes 196616 | tf_op jit(solution)/shard_map/ppermute | solution.py:191
  51.3 30.5 %collective-permute-start = (bf16[128,256]{1,0:T(8,128)(2,1)S(1)}, bf16[128,256]{1,0:T(8,128)(2,1)S(1)}, u32[]{:S(2)}, u32[]{:S(2)}) collective-permute-start(bf16[128,256]{1,0:T(8,128)(2,1)S(1)} %copy-done.11), channel_id=1, source_target_pairs={{0,4},{4,0},{8,12},{12,8},{16,20},{20,16},{24,28},{28,24},{1,5},{5... | collective-permute-start | bytes 196616 | tf_op jit(solution)/shard_map/ppermute | solution.py:191
  59.8 22.1 %collective-permute-start.4 = (bf16[128,256]{1,0:T(8,128)(2,1)S(1)}, bf16[128,256]{1,0:T(8,128)(2,1)S(1)}, u32[]{:S(2)}, u32[]{:S(2)}) collective-permute-start(bf16[128,256]{1,0:T(8,128)(2,1)S(1)} %copy-done.13), channel_id=1, source_target_pairs={{0,20},{4,16},{8,28},{12,24},{16,4},{20,0},{24,12},{28,8},{1,21},{... | collective-permute-start | bytes 196616 | tf_op jit(solution)/shard_map/ppermute | solution.py:191
  59.8 22.1 %collective-permute-start.6 = (bf16[128,256]{1,0:T(8,128)(2,1)S(1)}, bf16[128,256]{1,0:T(8,128)(2,1)S(1)}, u32[]{:S(2)}, u32[]{:S(2)}) collective-permute-start(bf16[128,256]{1,0:T(8,128)(2,1)S(1)} %copy-done.15), channel_id=1, source_target_pairs={{0,28},{4,24},{8,20},{12,16},{16,12},{20,8},{24,4},{28,0},{1,29},{... | collective-permute-start | bytes 196616 | tf_op jit(solution)/shard_map/ppermute | solution.py:191
  66.3 15.5 %collective-permute-start.2 = (bf16[128,256]{1,0:T(8,128)(2,1)S(1)}, bf16[128,256]{1,0:T(8,128)(2,1)S(1)}, u32[]{:S(2)}, u32[]{:S(2)}) collective-permute-start(bf16[128,256]{1,0:T(8,128)(2,1)S(1)} %copy-done.17), channel_id=1, source_target_pairs={{0,12},{4,8},{8,4},{12,0},{16,28},{20,24},{24,20},{28,16},{1,13},{... | collective-permute-start | bytes 196616 | tf_op jit(solution)/shard_map/ppermute | solution.py:191
  87.4 7.7 %collective-permute-start.14 = (bf16[64,128]{1,0:T(8,128)(2,1)S(1)}, bf16[64,128]{1,0:T(8,128)(2,1)S(1)}, u32[]{:S(2)}, u32[]{:S(2)}) collective-permute-start(bf16[64,128]{1,0:T(8,128)(2,1)S(1)} %get-tuple-element.46), channel_id=1, source_target_pairs={{0,28},{4,24},{8,20},{12,16},{16,12},{20,8},{24,4},{28,0},{1,29},{... | collective-permute-start | bytes 49160 | tf_op jit(solution)/shard_map/ppermute | solution.py:191
  89.8 7.7 %collective-permute-start.15 = (bf16[64,128]{1,0:T(8,128)(2,1)S(1)}, bf16[64,128]{1,0:T(8,128)(2,1)S(1)}, u32[]{:S(2)}, u32[]{:S(2)}) collective-permute-start(bf16[64,128]{1,0:T(8,128)(2,1)S(1)} %get-tuple-element.47), channel_id=1, source_target_pairs={{0,24},{4,28},{8,16},{12,20},{16,8},{20,12},{24,0},{28,4},{1,25},{... | collective-permute-start | bytes 49160 | tf_op jit(solution)/shard_map/ppermute | solution.py:191
  91.7 6.9 %collective-permute-start.16 = (bf16[64,128]{1,0:T(8,128)(2,1)S(1)}, bf16[64,128]{1,0:T(8,128)(2,1)S(1)}, u32[]{:S(2)}, u32[]{:S(2)}) collective-permute-start(bf16[64,128]{1,0:T(8,128)(2,1)S(1)} %get-tuple-element.48), channel_id=1, source_target_pairs={{0,20},{4,16},{8,28},{12,24},{16,4},{20,0},{24,12},{28,8},{1,21},{... | collective-permute-start | bytes 49160 | tf_op jit(solution)/shard_map/ppermute | solution.py:191
  91.7 6.9 %collective-permute-start.17 = (bf16[64,128]{1,0:T(8,128)(2,1)S(1)}, bf16[64,128]{1,0:T(8,128)(2,1)S(1)}, u32[]{:S(2)}, u32[]{:S(2)}) collective-permute-start(bf16[64,128]{1,0:T(8,128)(2,1)S(1)} %get-tuple-element.49), channel_id=1, source_target_pairs={{0,16},{4,20},{8,24},{12,28},{16,0},{20,4},{24,8},{28,12},{1,17},{... | collective-permute-start | bytes 49160 | tf_op jit(solution)/shard_map/ppermute | solution.py:191
  95.1 4.6 %collective-permute-start.18 = (bf16[64,128]{1,0:T(8,128)(2,1)S(1)}, bf16[64,128]{1,0:T(8,128)(2,1)S(1)}, u32[]{:S(2)}, u32[]{:S(2)}) collective-permute-start(bf16[64,128]{1,0:T(8,128)(2,1)S(1)} %get-tuple-element.50), channel_id=1, source_target_pairs={{0,12},{4,8},{8,4},{12,0},{16,28},{20,24},{24,20},{28,16},{1,13},{... | collective-permute-start | bytes 49160 | tf_op jit(solution)/shard_map/ppermute | solution.py:191
  95.1 4.6 %collective-permute-start.19 = (bf16[64,128]{1,0:T(8,128)(2,1)S(1)}, bf16[64,128]{1,0:T(8,128)(2,1)S(1)}, u32[]{:S(2)}, u32[]{:S(2)}) collective-permute-start(bf16[64,128]{1,0:T(8,128)(2,1)S(1)} %get-tuple-element.51), channel_id=1, source_target_pairs={{0,8},{4,12},{8,0},{12,4},{16,24},{20,28},{24,16},{28,20},{1,9},{5... | collective-permute-start | bytes 49160 | tf_op jit(solution)/shard_map/ppermute | solution.py:191
  97.5 3.7 %collective-permute-start.20 = (bf16[64,128]{1,0:T(8,128)(2,1)S(1)}, bf16[64,128]{1,0:T(8,128)(2,1)S(1)}, u32[]{:S(2)}, u32[]{:S(2)}) collective-permute-start(bf16[64,128]{1,0:T(8,128)(2,1)S(1)} %get-tuple-element.52), channel_id=1, source_target_pairs={{0,4},{4,0},{8,12},{12,8},{16,20},{20,16},{24,28},{28,24},{1,5},{5... | collective-permute-start | bytes 49160 | tf_op jit(solution)/shard_map/ppermute | solution.py:191
  101.3 1.9 %collective-permute-start.23 = (f32[64,128]{1,0:T(8,128)S(1)}, f32[64,128]{1,0:T(8,128)S(1)}, u32[]{:S(2)}, u32[]{:S(2)}) collective-permute-start(f32[64,128]{1,0:T(8,128)S(1)} %convert_add_fusion), channel_id=1, source_target_pairs={{0,1},{1,0},{2,3},{3,2},{4,5},{5,4},{6,7},{7,6},{8,9},{9,8},{10,11... | collective-permute-start | bytes 98312 | tf_op jit(solution)/shard_map/ppermute | solution.py:191
  101.4 4.0 %collective-permute-start.22 = (f32[64,128]{1,0:T(8,128)S(1)}, f32[64,128]{1,0:T(8,128)S(1)}, u32[]{:S(2)}, u32[]{:S(2)}) collective-permute-start(f32[64,128]{1,0:T(8,128)S(1)} %convert_add_fusion), channel_id=1, source_target_pairs={{0,2},{1,3},{2,0},{3,1},{4,6},{5,7},{6,4},{7,5},{8,10},{9,11},{10,... | collective-permute-start | bytes 98312 | tf_op jit(solution)/shard_map/ppermute | solution.py:191
  102.9 3.3 %collective-permute-start.21 = (f32[64,128]{1,0:T(8,128)S(1)}, f32[64,128]{1,0:T(8,128)S(1)}, u32[]{:S(2)}, u32[]{:S(2)}) collective-permute-start(f32[64,128]{1,0:T(8,128)S(1)} %convert_add_fusion), channel_id=1, source_target_pairs={{0,3},{1,2},{2,1},{3,0},{4,7},{5,6},{6,5},{7,4},{8,11},{9,10},{10,... | collective-permute-start | bytes 98312 | tf_op jit(solution)/shard_map/ppermute | solution.py:191

commit v3 on v2

v3 whole, which is shorter than its diff:
```python
import functools
import math

import jax
import jax.numpy as jnp
from jax import lax
from jax.experimental import pallas as pl
from jax.experimental.pallas import tpu as pltpu
from jax.sharding import PartitionSpec as P

HEADS = 32
HD = 128
FRAME_TOK = 64
NT = (((1,), (1,)), ((), ()))
VMEM_LIMIT = 32 * 1024 * 1024


def pack_first_kernel(count, place_ref, qkv_ref, readout_ref, *refs):
    out_ref = refs[-1]
    lat = readout_ref.shape[1]
    heads_local = readout_ref.shape[2] // HD
    for i in range(heads_local):
        base = i * 3 * HD
        if i < count:
            out_ref[:, i * 2 * HD : (i + 1) * 2 * HD] = qkv_ref[0, :, base : base + 2 * HD]
        values = qkv_ref[0, :, base + 2 * HD : base + 3 * HD]
        rows = readout_ref[0, :, i * HD : (i + 1) * HD]
        folded = lax.dot_general(rows, values, NT, preferred_element_type=jnp.float32)
        column = count * 2 * HD + (i * lat // HD) * HD
        row = (i * lat) % HD
        out_ref[row : row + lat, column : column + HD] = folded.astype(jnp.bfloat16)


def pack_last_kernel(place_ref, queries_ref, keys_ref, *refs):
    refs[-1][:, :HD] = queries_ref[0]
    refs[-1][:, HD:] = keys_ref[0]


def pack(place, qkv, readout_t, k, heads_local, chunk, count, width, after):
    rows = qkv.shape[1]
    lat = readout_t.shape[1]
    operands = [place, qkv]
    if chunk == 0:
        kernel = functools.partial(pack_first_kernel, count)
        in_specs = [
            pl.BlockSpec((1, rows, heads_local * 3 * HD), lambda g, m: (0, 0, m[0] ^ k)),
            pl.BlockSpec((1, lat, heads_local * HD), lambda g, m: (m[1], 0, m[0] ^ k)),
        ]
        operands += [readout_t]
    else:
        kernel = pack_last_kernel
        in_specs = [
            pl.BlockSpec((1, rows, HD), lambda g, m: (0, 0, ((m[0] ^ k) * heads_local + heads_local - 1) * 3)),
            pl.BlockSpec((1, rows, HD), lambda g, m: (0, 0, ((m[0] ^ k) * heads_local + heads_local - 1) * 3 + 1)),
        ]
        operands += [qkv]
    if after is not None:
        operands += [after]
        in_specs += [pl.BlockSpec(memory_space=pl.ANY)]
    return pl.pallas_call(
        kernel,
        grid_spec=pltpu.PrefetchScalarGridSpec(
            num_scalar_prefetch=1,
            grid=(1,),
            in_specs=in_specs,
            out_specs=pl.BlockSpec((rows, width), lambda g, m: (0, 0)),
        ),
        out_shape=jax.ShapeDtypeStruct((rows, width), jnp.bfloat16),
        compiler_params=pltpu.CompilerParams(vmem_limit_bytes=VMEM_LIMIT),
        cost_estimate=pl.CostEstimate(
            flops=2 * rows * lat * heads_local * HD if chunk == 0 else 0,
            bytes_accessed=rows * width * 4,
            transcendentals=0,
        ),
        name="pack",
    )(*operands)


def attend_kernel(seq_count, count, value_head, value_column, lat, order, last, frames_ref, factor_ref, me_ref, *refs):
    pieces = refs[:seq_count]
    refs = refs[seq_count:]
    value_refs, earlier = pieces, None
    if value_head:
        value_refs, earlier = refs[:seq_count], refs[seq_count]
        refs = refs[seq_count + 1 :]
    out_refs = refs[-3:-1] if last else refs[-2:-1]
    asked = refs[-1]
    rows = pieces[0].shape[0]
    tokens = seq_count * rows
    spans = frames_ref.shape[0]
    log2_scale = math.log2(math.e) / math.sqrt(HD)
    half = seq_count // 2

    end = frames_ref[0] * FRAME_TOK
    ends = [end]
    for c in range(1, spans):
        end = end + frames_ref[c] * FRAME_TOK
        ends.append(end)
    me = me_ref[0]
    row_places = lax.broadcasted_iota(jnp.int32, (rows, 1), 0)
    key_places = jnp.concatenate([(me ^ k) * rows + row_places for k in range(seq_count)], axis=0)
    column_places = lax.broadcasted_iota(jnp.int32, (1, rows), 1)
    for n, k in enumerate(order):
        for i in range(count):
            asked[n, i] = pieces[k][:, i * 2 * HD : i * 2 * HD + HD]
    reversed_bits = seq_count.bit_length() - 1

    def place_of(n):
        k = jnp.int32(0)
        for bit in range(reversed_bits):
            k = k | (((n >> bit) & 1) << (reversed_bits - 1 - bit))
        return me ^ k

    def one_block(b, carry):
        first = b * 2
        places = jnp.concatenate([place_of(first + j) * rows + column_places for j in range(2)], axis=1)
        bound = jnp.full((1, 2 * rows), ends[0], jnp.int32)
        for c in range(1, spans):
            bound = jnp.where(places >= ends[c - 1], ends[c], bound)
        allowed = key_places < bound
        total = None
        for i in range(count):
            queries = asked[pl.ds(first, 2), i].reshape(2 * rows, HD)
            keys = jnp.concatenate([p[:, i * 2 * HD + HD : (i + 1) * 2 * HD] for p in pieces], axis=0)
            scores = lax.dot_general(keys, queries, NT, preferred_element_type=jnp.float32)
            scores = jnp.where(allowed, scores, -jnp.inf)
            peak = jnp.max(scores, axis=0, keepdims=True)
            raw = jnp.exp2((scores - peak) * log2_scale)
            row_total = jnp.sum(raw, axis=0, keepdims=True)
            weights = raw.astype(jnp.bfloat16)
            h = value_head + i
            column = value_column + (h * lat // HD) * HD
            row = (h * lat) % HD
            folded = jnp.concatenate([v[row : row + lat, column : column + HD] for v in value_refs], axis=1)
            summed = jnp.dot(folded, weights, preferred_element_type=jnp.float32) / row_total
            total = summed if total is None else total + summed
        for j in range(2):
            part = total[:, j * rows : (j + 1) * rows]
            n = first + j
            if earlier is not None:
                part = part + earlier[n]
            if last:
                part = part * factor_ref[0]

                @pl.when(n < half)
                def _():
                    out_refs[0][n] = part

                @pl.when(n >= half)
                def _():
                    out_refs[1][n - half] = part.astype(jnp.bfloat16)
            else:
                out_refs[0][n] = part
        return carry

    lax.fori_loop(0, half, one_block, 0)


def attend(pieces, value_pieces, earlier, after, span_frames, factor, me, count, value_head, value_column, lat, order, last):
    seq_count = len(pieces)
    rows, width = pieces[0].shape
    tokens = seq_count * rows
    smem = pl.BlockSpec(memory_space=pltpu.SMEM)
    vmem = pl.BlockSpec(memory_space=pltpu.VMEM)
    operands = [span_frames, factor, me] + list(pieces)
    in_specs = [smem] * 3 + [vmem] * seq_count
    if value_head:
        operands += list(value_pieces) + [earlier]
        in_specs += [vmem] * (seq_count + 1)
    if after is not None:
        operands += [after]
        in_specs += [pl.BlockSpec(memory_space=pl.ANY)]
    if last:
        out_shape = [
            jax.ShapeDtypeStruct((seq_count // 2, lat, rows), jnp.float32),
            jax.ShapeDtypeStruct((seq_count // 2, lat, rows), jnp.bfloat16),
        ]
    else:
        out_shape = [jax.ShapeDtypeStruct((seq_count, lat, rows), jnp.float32)]
    return pl.pallas_call(
        functools.partial(attend_kernel, seq_count, count, value_head, value_column, lat, order, last),
        in_specs=in_specs,
        out_specs=[vmem] * len(out_shape),
        out_shape=out_shape,
        scratch_shapes=[pltpu.VMEM((seq_count, count, rows, HD), jnp.bfloat16)],
        compiler_params=pltpu.CompilerParams(vmem_limit_bytes=VMEM_LIMIT),
        cost_estimate=pl.CostEstimate(
            flops=count * tokens * tokens * 2 * (HD + lat),
            bytes_accessed=tokens * width * 2,
            transcendentals=count * tokens * tokens,
        ),
        name="attend",
    )(*operands)


def swap(array, axis, offset):
    size = lax.axis_size(axis)
    return lax.ppermute(array, axis, [(i, i ^ offset) for i in range(size)])


def body(qkv, readout, step_weight, timestep, span_frames):
    seq_count = lax.axis_size("seq")
    mp_count = lax.axis_size("mp")
    heads_local = HEADS // seq_count
    lat = readout.shape[2]
    me = lax.axis_index("seq").astype(jnp.int32)
    mp_index = lax.axis_index("mp")
    sample_count = mp_count // 2
    model_index = (mp_index // sample_count).astype(jnp.int32)
    sample_index = mp_index % sample_count
    signed = jnp.where(model_index == 1, 1.0, -1.0).astype(jnp.float32)
    factor = (signed * step_weight[timestep[sample_index]]).reshape(1)
    chunks = [heads_local - 1, 1] if heads_local > 1 else [1]
    value_column = chunks[0] * 2 * HD
    widths = [value_column + -(-heads_local * lat // HD) * HD, 2 * HD]
    readout_t = jnp.swapaxes(readout, 1, 2)
    place = jnp.stack([me, model_index])
    bits = seq_count.bit_length() - 1
    order = [sum(((n >> b) & 1) << (bits - 1 - b) for b in range(bits)) for n in range(seq_count)]

    half = seq_count // 2
    far = list(range(seq_count - 1, half - 1, -1))
    near = list(range(half - 1, 0, -1))
    arrived = [[None] * seq_count for _ in chunks]

    def send(c, k, after):
        packed = pack(place, qkv, readout_t, k, heads_local, c, chunks[c], widths[c], after)
        arrived[c][k] = swap(packed, "seq", k) if k else packed
        return packed

    before = None
    for k in far:
        before = send(0, k, before)
    for k in near:
        send(0, k, before)
        before = arrived[0][k]
    send(0, 0, before)
    hold = None
    if len(chunks) > 1:
        for k in near:
            send(1, k, before)
            before = arrived[1][k]
        send(1, 0, before)
        for k in far:
            hold = send(1, k, before)
            before = arrived[0][k]

    result, head = None, 0
    for c, count in enumerate(chunks):
        last = c == len(chunks) - 1
        result = attend(
            arrived[c], arrived[0], result, None if last else hold, span_frames, factor, me.reshape(1),
            count, head, value_column, lat, order, last,
        )
        head += count
        if not last:
            result = result[0]
    keep, give = result
    offset = 1
    while True:
        keep = keep + swap(give, "seq", offset).astype(jnp.float32)
        offset *= 2
        if offset == seq_count:
            break
        size = keep.shape[0] // 2
        keep, give = keep[:size], keep[size:]
    whole = keep[0]
    offset = 1
    while offset < mp_count:
        whole = whole + swap(whole, "mp", offset)
        offset *= 2
    return whole.T


def solution(mesh):
    return jax.shard_map(
        body,
        mesh=mesh,
        in_specs=(P("mp", "seq", None), P(), P(), P(), P()),
        out_specs=P("seq", None),
        check_vma=False,
    )
```

time: 107 us -> 118 us (1.10)
  waiting for transfers between devices: 22.9 us -> 43.3 us
  starting transfers between devices: 42.1 us -> 36.7 us
  local copies, waits for them, and re-layouts: 11.2 us -> 5.85 us
  Pallas kernels: 27.1 us -> 28.3 us
    ppermute x24 -> x19, waiting for transfers between devices: 22.9 us -> 43.3 us  [swap(): return lax.ppermute(array, axis, [(i, i ^ offset) for i in range(size)])]
    ppermute x24 -> x19, starting transfers between devices: 42.1 us -> 36.7 us  [swap(): return lax.ppermute(array, axis, [(i, i ^ offset) for i in range(size)])]
    unnamed x38 -> x24, local copies, waits for them, and re-layouts: 9.32 us -> 3.99 us
    pallas_call x8 -> x16, Pallas kernels: 11 us -> 14.1 us  [pack(): pl.pallas_call(kernel, grid_spec=pltpu.PrefetchScalarGridSpec(num_scalar_...]
    pallas_call x2, Pallas kernels: 16.1 us -> 14.1 us  [attend(): pl.pallas_call(functools.partial(attend_kernel, seq_count, count, value_h...]
  transfers between devices with their start and end apart: 24 -> 19, of which waited for: 6 -> 10; matrix products, arithmetic and copies ran while one was open for 2% -> 2% of each run, Pallas kernels for 19% -> 13%
where the time goes in v3:
time: 118 us
  waiting for transfers between devices  43.3 us (37%)
  starting transfers between devices  36.7 us (31%)
  Pallas kernels  28.3 us (24%)
  local copies, waits for them, and re-layouts  5.85 us (5%)
  between operations  2.89 us (2%)
    ppermute x19, waiting for transfers between devices, swap(): return lax.ppermute(array, axis, [(i, i ^ offset) for i in range(size)])  43.3 us
    ppermute x19, starting transfers between devices, swap(): return lax.ppermute(array, axis, [(i, i ^ offset) for i in range(size)])  36.7 us
    pallas_call x16, Pallas kernels, pack(): pl.pallas_call(kernel, grid_spec=pltpu.PrefetchScalarGridSpec(num_scalar_...  14.1 us
    pallas_call x2, Pallas kernels, attend(): pl.pallas_call(functools.partial(attend_kernel, seq_count, count, value_h...  14.1 us
    unnamed x24, local copies, waits for them, and re-layouts  3.99 us
  transfers between devices with their start and end apart: 19, of which 10 were waited for; matrix products, arithmetic and copies ran while one was open for 2% of the time, Pallas kernels for 13%

profile of v3, /device:TPU:0, one launch (start us, length us, event | category | flops | bytes accessed | tf_op | source)
XLA Modules:
  0.0 117.8 jit_solution(10752835618078845522)
XLA Ops:
  0.1 1.9 %copy-done = bf16[1,128,12288]{2,1,0:T(8,128)(2,1)S(1)} copy-done((bf16[1,128,12288]{2,1,0:T(8,128)(2,1)S(1)}, bf16[1,128,12288]{2,1,0:T(8,128)(2,1)}, u32[]{:S(2)}) %copy-start) | copy-done | bytes 3145752
  2.0 1.2 %copy-done.2 = bf16[2,4096,64]{1,2,0:T(8,128)(2,1)S(1)} copy-done((bf16[2,4096,64]{1,2,0:T(8,128)(2,1)S(1)}, bf16[2,4096,64]{1,2,0:T(8,128)(2,1)}, u32[]{:S(2)}) %copy-start.2) | copy-done | bytes 1048600
  3.2 1.5 %pack.16.refs_0_ = bf16[128,1024]{1,0:T(8,128)(2,1)} custom-call(s32[2]{0:T(128)S(1)} %pad_add_fusion.place_ref, bf16[1,128,12288]{2,1,0:T(8,128)(2,1)S(1)} %copy-done, bf16[2,64,4096]{2,1,0:T(8,128)(2,1)S(1)} %bitcast.10), custom_call_target="tpu_custom_call" | custom-call | flops 8388608 | bytes 524288 | tf_op jit(solution)/shard_map/pack/pallas_call | solution.py:60
  4.7 1.5 %pack.17.refs_0_ = bf16[128,1024]{1,0:T(8,128)(2,1)} custom-call(s32[2]{0:T(128)S(1)} %pad_add_fusion.place_ref, bf16[1,128,12288]{2,1,0:T(8,128)(2,1)S(1)} %copy-done, bf16[2,64,4096]{2,1,0:T(8,128)(2,1)S(1)} %bitcast.11, bf16[128,1024]{1,0:T(8,128)(2,1)} %pack.16.refs_0_), custom_call_target="tpu_custom_call" | custom-call | flops 8388608 | bytes 524288 | tf_op jit(solution)/shard_map/pack/pallas_call | solution.py:60
  6.1 1.5 %pack.18.refs_0_ = bf16[128,1024]{1,0:T(8,128)(2,1)} custom-call(s32[2]{0:T(128)S(1)} %pad_add_fusion.place_ref, bf16[1,128,12288]{2,1,0:T(8,128)(2,1)S(1)} %copy-done, bf16[2,64,4096]{2,1,0:T(8,128)(2,1)S(1)} %bitcast.12, bf16[128,1024]{1,0:T(8,128)(2,1)} %pack.17.refs_0_), custom_call_target="tpu_custom_call" | custom-call | flops 8388608 | bytes 524288 | tf_op jit(solution)/shard_map/pack/pallas_call | solution.py:60
  7.6 1.5 %pack.19.refs_0_ = bf16[128,1024]{1,0:T(8,128)(2,1)} custom-call(s32[2]{0:T(128)S(1)} %pad_add_fusion.place_ref, bf16[1,128,12288]{2,1,0:T(8,128)(2,1)S(1)} %copy-done, bf16[2,64,4096]{2,1,0:T(8,128)(2,1)S(1)} %bitcast.13, bf16[128,1024]{1,0:T(8,128)(2,1)} %pack.18.refs_0_), custom_call_target="tpu_custom_call" | custom-call | flops 8388608 | bytes 524288 | tf_op jit(solution)/shard_map/pack/pallas_call | solution.py:60
  9.1 0.8 pack.20
  9.9 4.0 %collective-permute-start = (bf16[128,1024]{1,0:T(8,128)(2,1)S(1)}, bf16[128,1024]{1,0:T(8,128)(2,1)S(1)}, u32[]{:S(2)}, u32[]{:S(2)}) collective-permute-start(bf16[128,1024]{1,0:T(8,128)(2,1)S(1)} %pack.20), channel_id=1, source_target_pairs={{0,12},{4,8},{8,4},{12,0},{16,28},{20,24},{24,20},{28,16},{1,13},{... | collective-permute-start | bytes 786440 | tf_op jit(solution)/shard_map/ppermute | solution.py:198
  13.9 6.3 %collective-permute-done.refs_0_.refs_3_.refs_11_ = bf16[128,1024]{1,0:T(8,128)(2,1)S(1)} collective-permute-done((bf16[128,1024]{1,0:T(8,128)(2,1)S(1)}, bf16[128,1024]{1,0:T(8,128)(2,1)S(1)}, u32[]{:S(2)}, u32[]{:S(2)}) %collective-permute-start) | collective-permute-done | bytes 262176 | tf_op jit(solution)/shard_map/ppermute | solution.py:198
  20.2 0.8 pack.21
  21.0 1.8 %collective-permute-start.1 = (bf16[128,1024]{1,0:T(8,128)(2,1)S(1)}, bf16[128,1024]{1,0:T(8,128)(2,1)S(1)}, u32[]{:S(2)}, u32[]{:S(2)}) collective-permute-start(bf16[128,1024]{1,0:T(8,128)(2,1)S(1)} %pack.21), channel_id=1, source_target_pairs={{0,8},{4,12},{8,0},{12,4},{16,24},{20,28},{24,16},{28,20},{1,9},{5... | collective-permute-start | bytes 786440 | tf_op jit(solution)/shard_map/ppermute | solution.py:198
  22.7 5.8 %collective-permute-done.1.refs_0_.refs_2_.refs_10_ = bf16[128,1024]{1,0:T(8,128)(2,1)S(1)} collective-permute-done((bf16[128,1024]{1,0:T(8,128)(2,1)S(1)}, bf16[128,1024]{1,0:T(8,128)(2,1)S(1)}, u32[]{:S(2)}, u32[]{:S(2)}) %collective-permute-start.1) | collective-permute-done | bytes 262176 | tf_op jit(solution)/shard_map/ppermute | solution.py:198
  28.5 0.8 pack.22
  29.3 1.4 %collective-permute-start.2 = (bf16[128,1024]{1,0:T(8,128)(2,1)S(1)}, bf16[128,1024]{1,0:T(8,128)(2,1)S(1)}, u32[]{:S(2)}, u32[]{:S(2)}) collective-permute-start(bf16[128,1024]{1,0:T(8,128)(2,1)S(1)} %pack.22), channel_id=1, source_target_pairs={{0,4},{4,0},{8,12},{12,8},{16,20},{20,16},{24,28},{28,24},{1,5},{5... | collective-permute-start | bytes 786440 | tf_op jit(solution)/shard_map/ppermute | solution.py:198
  30.7 2.6 %collective-permute-start.6 = (bf16[128,1024]{1,0:T(8,128)(2,1)}, bf16[128,1024]{1,0:T(8,128)(2,1)}, u32[]{:S(2)}, u32[]{:S(2)}) collective-permute-start(bf16[128,1024]{1,0:T(8,128)(2,1)} %pack.18.refs_0_), channel_id=1, source_target_pairs={{0,20},{4,16},{8,28},{12,24},{16,4},{20,0},{24,12},{28,8},{1,21},{... | collective-permute-start | bytes 786440 | tf_op jit(solution)/shard_map/ppermute | solution.py:198
  33.2 1.3 %collective-permute-start.8 = (bf16[128,1024]{1,0:T(8,128)(2,1)}, bf16[128,1024]{1,0:T(8,128)(2,1)}, u32[]{:S(2)}, u32[]{:S(2)}) collective-permute-start(bf16[128,1024]{1,0:T(8,128)(2,1)} %pack.17.refs_0_), channel_id=1, source_target_pairs={{0,24},{4,28},{8,16},{12,20},{16,8},{20,12},{24,0},{28,4},{1,25},{... | collective-permute-start | bytes 786440 | tf_op jit(solution)/shard_map/ppermute | solution.py:198
  34.6 3.4 %collective-permute-start.10 = (bf16[128,1024]{1,0:T(8,128)(2,1)}, bf16[128,1024]{1,0:T(8,128)(2,1)}, u32[]{:S(2)}, u32[]{:S(2)}) collective-permute-start(bf16[128,1024]{1,0:T(8,128)(2,1)} %pack.16.refs_0_), channel_id=1, source_target_pairs={{0,28},{4,24},{8,20},{12,16},{16,12},{20,8},{24,4},{28,0},{1,29},{... | collective-permute-start | bytes 786440 | tf_op jit(solution)/shard_map/ppermute | solution.py:198
  38.0 0.6 pack.23
  38.6 5.6 %collective-permute-start.3 = (bf16[128,256]{1,0:T(8,128)(2,1)S(1)}, bf16[128,256]{1,0:T(8,128)(2,1)S(1)}, u32[]{:S(2)}, u32[]{:S(2)}) collective-permute-start(bf16[128,256]{1,0:T(8,128)(2,1)S(1)} %pack.23), channel_id=1, source_target_pairs={{0,12},{4,8},{8,4},{12,0},{16,28},{20,24},{24,20},{28,16},{1,13},{... | collective-permute-start | bytes 196616 | tf_op jit(solution)/shard_map/ppermute | solution.py:198
  44.2 11.1 %collective-permute-done.3.refs_0_.refs_3_ = bf16[128,256]{1,0:T(8,128)(2,1)S(1)} collective-permute-done((bf16[128,256]{1,0:T(8,128)(2,1)S(1)}, bf16[128,256]{1,0:T(8,128)(2,1)S(1)}, u32[]{:S(2)}, u32[]{:S(2)}) %collective-permute-start.3) | collective-permute-done | bytes 65568 | tf_op jit(solution)/shard_map/ppermute | solution.py:198
  55.9 3.5 %collective-permute-start.4 = (bf16[128,256]{1,0:T(8,128)(2,1)S(1)}, bf16[128,256]{1,0:T(8,128)(2,1)S(1)}, u32[]{:S(2)}, u32[]{:S(2)}) collective-permute-start(bf16[128,256]{1,0:T(8,128)(2,1)S(1)} %pack.24), channel_id=1, source_target_pairs={{0,8},{4,12},{8,0},{12,4},{16,24},{20,28},{24,16},{28,20},{1,9},{5... | collective-permute-start | bytes 196616 | tf_op jit(solution)/shard_map/ppermute | solution.py:198
  59.4 2.8 %collective-permute-done.4.refs_0_.refs_2_ = bf16[128,256]{1,0:T(8,128)(2,1)S(1)} collective-permute-done((bf16[128,256]{1,0:T(8,128)(2,1)S(1)}, bf16[128,256]{1,0:T(8,128)(2,1)S(1)}, u32[]{:S(2)}, u32[]{:S(2)}) %collective-permute-start.4) | collective-permute-done | bytes 65568 | tf_op jit(solution)/shard_map/ppermute | solution.py:198
  62.2 1.2 %pack.25 = bf16[128,256]{1,0:T(8,128)(2,1)} custom-call(s32[2]{0:T(128)S(1)} %pad_add_fusion.place_ref, bf16[1,128,12288]{2,1,0:T(8,128)(2,1)S(1)} %copy-done, bf16[1,128,12288]{2,1,0:T(8,128)(2,1)S(1)} %copy-done, bf16[128,256]{1,0:T(8,128)(2,1)S(1)} %collective-permute-done.4.refs_0_.refs_2_), custom_call_target="tpu_custom_call" | custom-call | bytes 131072 | tf_op jit(solution)/shard_map/pack/pallas_call | solution.py:60
  63.4 0.6 copy-done.8
  64.0 0.8 collective-permute-start.5
  64.8 0.6 dynamic_slice.6
  67.3 1.3 %dynamic_slice.7 = f32[1]{0:T(128)} dynamic-slice(f32[1000]{0:T(1024)} %param.7, s32[]{:T(128)S(6)} %select_n.25), dynamic_slice_sizes={1} | dynamic-slice | bytes 12 | tf_op jit(solution)/shard_map/dynamic_slice | solution.py:212
  69.2 0.6 pack.27.refs_8_
  69.8 1.2 collective-permute-start.7
  71.0 0.6 pack.28
  71.6 2.6 %collective-permute-start.9 = (bf16[128,256]{1,0:T(8,128)(2,1)S(1)}, bf16[128,256]{1,0:T(8,128)(2,1)S(1)}, u32[]{:S(2)}, u32[]{:S(2)}) collective-permute-start(bf16[128,256]{1,0:T(8,128)(2,1)S(1)} %pack.28), channel_id=1, source_target_pairs={{0,20},{4,16},{8,28},{12,24},{16,4},{20,0},{24,12},{28,8},{1,21},{... | collective-permute-start | bytes 196616 | tf_op jit(solution)/shard_map/ppermute | solution.py:198
  74.7 2.7 %collective-permute-start.11 = (bf16[128,256]{1,0:T(8,128)(2,1)S(1)}, bf16[128,256]{1,0:T(8,128)(2,1)S(1)}, u32[]{:S(2)}, u32[]{:S(2)}) collective-permute-start(bf16[128,256]{1,0:T(8,128)(2,1)S(1)} %pack.29), channel_id=1, source_target_pairs={{0,24},{4,28},{8,16},{12,20},{16,8},{20,12},{24,0},{28,4},{1,25},{... | collective-permute-start | bytes 196616 | tf_op jit(solution)/shard_map/ppermute | solution.py:198
  77.5 0.8 pack.31.refs_0_.refs_8_
  78.3 0.6 pack.30
  78.9 1.5 %collective-permute-start.12 = (bf16[128,256]{1,0:T(8,128)(2,1)S(1)}, bf16[128,256]{1,0:T(8,128)(2,1)S(1)}, u32[]{:S(2)}, u32[]{:S(2)}) collective-permute-start(bf16[128,256]{1,0:T(8,128)(2,1)S(1)} %pack.30), channel_id=1, source_target_pairs={{0,28},{4,24},{8,20},{12,16},{16,12},{20,8},{24,4},{28,0},{1,29},{... | collective-permute-start | bytes 196616 | tf_op jit(solution)/shard_map/ppermute | solution.py:198
  80.3 3.1 %collective-permute-done.13.refs_4_.refs_12_ = bf16[128,1024]{1,0:T(8,128)(2,1)} collective-permute-done((bf16[128,1024]{1,0:T(8,128)(2,1)}, bf16[128,1024]{1,0:T(8,128)(2,1)}, u32[]{:S(2)}, u32[]{:S(2)}) %collective-permute-start.13) | collective-permute-done | bytes 262176 | tf_op jit(solution)/shard_map/ppermute | solution.py:198
  83.4 9.9 %attend.2.refs_16_ = f32[8,64,128]{2,1,0:T(8,128)S(1)} custom-call(s32[4]{0:T(128)S(1)} %copy-done.10, f32[1]{0:T(128)} %bitcast.2.factor_ref, s32[1]{0:T(128)} %bitcast.3.me_ref, bf16[128,1024]{1,0:T(8,128)(2,1)S(1)} %pack.31.refs_0_.refs_8_, bf16[128,1024]{1,0:T(8,128)(2,1)S(1)} %collective-permute-done.2.refs_0_.refs_1_.refs_9_, ...), custom_call_target="tpu_custom_call" | custom-call | flops 1207959552 | bytes 2097152 | tf_op jit(solution)/shard_map/attend/pallas_call | solution.py:180
  93.3 0.6 pack.26.refs_0_
  94.1 4.3 %attend.3 = (f32[4,64,128]{2,1,0:T(8,128)S(1)}, bf16[4,64,128]{2,1,0:T(8,128)(2,1)S(1)}) custom-call(s32[4]{0:T(128)S(1)} %copy-done.10, f32[1]{0:T(128)} %bitcast.2.factor_ref, s32[1]{0:T(128)} %bitcast.3.me_ref, bf16[128,256]{1,0:T(8,128)(2,1)S(1)} %pack.26.refs_0_, bf16[128,256]{1,0:T(8,128)(2,1)S(1)} %collective-permute-done.5.refs_0_.refs_1_, ...), custom_call_target="tpu_custom_call" | custom-call | flops 402653184 | bytes 524288 | tf_op jit(solution)/shard_map/attend/pallas_call | solution.py:180
  98.4 1.6 %collective-permute-start.14 = (bf16[4,64,128]{2,1,0:T(8,128)(2,1)S(1)}, bf16[4,64,128]{2,1,0:T(8,128)(2,1)S(1)}, u32[]{:S(2)}, u32[]{:S(2)}) collective-permute-start(bf16[4,64,128]{2,1,0:T(8,128)(2,1)S(1)} %get-tuple-element.8), channel_id=1, source_target_pairs={{0,4},{4,0},{8,12},{12,8},{16,20},{20,16},{24,28},{28,24},{1,5},{5... | collective-permute-start | bytes 196616 | tf_op jit(solution)/shard_map/ppermute | solution.py:198
  99.9 2.8 %collective-permute-done.14 = bf16[4,64,128]{2,1,0:T(8,128)(2,1)S(1)} collective-permute-done((bf16[4,64,128]{2,1,0:T(8,128)(2,1)S(1)}, bf16[4,64,128]{2,1,0:T(8,128)(2,1)S(1)}, u32[]{:S(2)}, u32[]{:S(2)}) %collective-permute-start.14) | collective-permute-done | bytes 65568 | tf_op jit(solution)/shard_map/ppermute | solution.py:198
  102.8 4.3 %collective-permute-done.15 = f32[2,64,128]{2,1,0:T(8,128)S(1)} collective-permute-done((f32[2,64,128]{2,1,0:T(8,128)S(1)}, f32[2,64,128]{2,1,0:T(8,128)S(1)}, u32[]{:S(2)}, u32[]{:S(2)}) %collective-permute-start.15) | collective-permute-done | bytes 65568 | tf_op jit(solution)/shard_map/ppermute | solution.py:198
  107.1 1.2 %collective-permute-start.16 = (f32[1,64,128]{2,1,0:T(8,128)S(1)}, f32[1,64,128]{2,1,0:T(8,128)S(1)}, u32[]{:S(2)}, u32[]{:S(2)}) collective-permute-start(f32[1,64,128]{2,1,0:T(8,128)S(1)} %slice.19), channel_id=1, source_target_pairs={{0,16},{4,20},{8,24},{12,28},{16,0},{20,4},{24,8},{28,12},{1,17},{... | collective-permute-start | bytes 98312 | tf_op jit(solution)/shard_map/ppermute | solution.py:198
  108.3 3.7 %collective-permute-done.16 = f32[1,64,128]{2,1,0:T(8,128)S(1)} collective-permute-done((f32[1,64,128]{2,1,0:T(8,128)S(1)}, f32[1,64,128]{2,1,0:T(8,128)S(1)}, u32[]{:S(2)}, u32[]{:S(2)}) %collective-permute-start.16) | collective-permute-done | bytes 32800 | tf_op jit(solution)/shard_map/ppermute | solution.py:198
  112.0 1.2 %collective-permute-done.17 = f32[64,128]{1,0:T(8,128)S(1)} collective-permute-done((f32[64,128]{1,0:T(8,128)S(1)}, f32[64,128]{1,0:T(8,128)S(1)}, u32[]{:S(2)}, u32[]{:S(2)}) %collective-permute-start.17) | collective-permute-done | bytes 32800 | tf_op jit(solution)/shard_map/ppermute | solution.py:198
  113.2 1.5 %collective-permute-start.18 = (f32[64,128]{1,0:T(8,128)S(1)}, f32[64,128]{1,0:T(8,128)S(1)}, u32[]{:S(2)}, u32[]{:S(2)}) collective-permute-start(f32[64,128]{1,0:T(8,128)S(1)} %add.32), channel_id=1, source_target_pairs={{0,2},{1,3},{2,0},{3,1},{4,6},{5,7},{6,4},{7,5},{8,10},{9,11},{10,... | collective-permute-start | bytes 98312 | tf_op jit(solution)/shard_map/ppermute | solution.py:198
  114.7 2.4 %collective-permute-done.18 = f32[64,128]{1,0:T(8,128)S(1)} collective-permute-done((f32[64,128]{1,0:T(8,128)S(1)}, f32[64,128]{1,0:T(8,128)S(1)}, u32[]{:S(2)}, u32[]{:S(2)}) %collective-permute-start.18) | collective-permute-done | bytes 32800 | tf_op jit(solution)/shard_map/ppermute | solution.py:198
  117.1 0.6 add_bitcast_fusion
  (42 shorter events, 1.6 us)
Async XLA Ops:
  0.1 1.9 %copy-start = (bf16[1,128,12288]{2,1,0:T(8,128)(2,1)S(1)}, bf16[1,128,12288]{2,1,0:T(8,128)(2,1)}, u32[]{:S(2)}) copy-start(bf16[1,128,12288]{2,1,0:T(8,128)(2,1)} %qkv_ref.15) | copy-start | bytes 9437188
  2.0 1.2 %copy-start.2 = (bf16[2,4096,64]{1,2,0:T(8,128)(2,1)S(1)}, bf16[2,4096,64]{1,2,0:T(8,128)(2,1)}, u32[]{:S(2)}) copy-start(bf16[2,4096,64]{1,2,0:T(8,128)(2,1)} %param.6) | copy-start | bytes 3145732
  9.9 10.3 %collective-permute-start = (bf16[128,1024]{1,0:T(8,128)(2,1)S(1)}, bf16[128,1024]{1,0:T(8,128)(2,1)S(1)}, u32[]{:S(2)}, u32[]{:S(2)}) collective-permute-start(bf16[128,1024]{1,0:T(8,128)(2,1)S(1)} %pack.20), channel_id=1, source_target_pairs={{0,12},{4,8},{8,4},{12,0},{16,28},{20,24},{24,20},{28,16},{1,13},{... | collective-permute-start | bytes 786440 | tf_op jit(solution)/shard_map/ppermute | solution.py:198
  20.2 9.1 %copy-start.4 = (bf16[128,1024]{1,0:T(8,128)(2,1)}, bf16[128,1024]{1,0:T(8,128)(2,1)S(1)}, u32[]{:S(2)}) copy-start(bf16[128,1024]{1,0:T(8,128)(2,1)S(1)} %collective-permute-done.refs_0_.refs_3_.refs_11_) | copy-start | bytes 786436
  21.0 7.6 %collective-permute-start.1 = (bf16[128,1024]{1,0:T(8,128)(2,1)S(1)}, bf16[128,1024]{1,0:T(8,128)(2,1)S(1)}, u32[]{:S(2)}, u32[]{:S(2)}) collective-permute-start(bf16[128,1024]{1,0:T(8,128)(2,1)S(1)} %pack.21), channel_id=1, source_target_pairs={{0,8},{4,12},{8,0},{12,4},{16,24},{20,28},{24,16},{28,20},{1,9},{5... | collective-permute-start | bytes 786440 | tf_op jit(solution)/shard_map/ppermute | solution.py:198
  28.5 10.1 %copy-start.6 = (bf16[128,1024]{1,0:T(8,128)(2,1)}, bf16[128,1024]{1,0:T(8,128)(2,1)S(1)}, u32[]{:S(2)}) copy-start(bf16[128,1024]{1,0:T(8,128)(2,1)S(1)} %collective-permute-done.1.refs_0_.refs_2_.refs_10_) | copy-start | bytes 786436
  29.3 8.7 %collective-permute-start.2 = (bf16[128,1024]{1,0:T(8,128)(2,1)S(1)}, bf16[128,1024]{1,0:T(8,128)(2,1)S(1)}, u32[]{:S(2)}, u32[]{:S(2)}) collective-permute-start(bf16[128,1024]{1,0:T(8,128)(2,1)S(1)} %pack.22), channel_id=1, source_target_pairs={{0,4},{4,0},{8,12},{12,8},{16,20},{20,16},{24,28},{28,24},{1,5},{5... | collective-permute-start | bytes 786440 | tf_op jit(solution)/shard_map/ppermute | solution.py:198
  30.7 38.5 %collective-permute-start.6 = (bf16[128,1024]{1,0:T(8,128)(2,1)}, bf16[128,1024]{1,0:T(8,128)(2,1)}, u32[]{:S(2)}, u32[]{:S(2)}) collective-permute-start(bf16[128,1024]{1,0:T(8,128)(2,1)} %pack.18.refs_0_), channel_id=1, source_target_pairs={{0,20},{4,16},{8,28},{12,24},{16,4},{20,0},{24,12},{28,8},{1,21},{... | collective-permute-start | bytes 786440 | tf_op jit(solution)/shard_map/ppermute | solution.py:198
  33.2 37.7 %collective-permute-start.8 = (bf16[128,1024]{1,0:T(8,128)(2,1)}, bf16[128,1024]{1,0:T(8,128)(2,1)}, u32[]{:S(2)}, u32[]{:S(2)}) collective-permute-start(bf16[128,1024]{1,0:T(8,128)(2,1)} %pack.17.refs_0_), channel_id=1, source_target_pairs={{0,24},{4,28},{8,16},{12,20},{16,8},{20,12},{24,0},{28,4},{1,25},{... | collective-permute-start | bytes 786440 | tf_op jit(solution)/shard_map/ppermute | solution.py:198
  34.6 39.5 %collective-permute-start.10 = (bf16[128,1024]{1,0:T(8,128)(2,1)}, bf16[128,1024]{1,0:T(8,128)(2,1)}, u32[]{:S(2)}, u32[]{:S(2)}) collective-permute-start(bf16[128,1024]{1,0:T(8,128)(2,1)} %pack.16.refs_0_), channel_id=1, source_target_pairs={{0,28},{4,24},{8,20},{12,16},{16,12},{20,8},{24,4},{28,0},{1,29},{... | collective-permute-start | bytes 786440 | tf_op jit(solution)/shard_map/ppermute | solution.py:198
  38.0 45.4 %collective-permute-start.13 = (bf16[128,1024]{1,0:T(8,128)(2,1)}, bf16[128,1024]{1,0:T(8,128)(2,1)}, u32[]{:S(2)}, u32[]{:S(2)}) collective-permute-start(bf16[128,1024]{1,0:T(8,128)(2,1)} %pack.19.refs_0_), channel_id=1, source_target_pairs={{0,16},{4,20},{8,24},{12,28},{16,0},{20,4},{24,8},{28,12},{1,17},{... | collective-permute-start | bytes 786440 | tf_op jit(solution)/shard_map/ppermute | solution.py:198
  38.6 16.7 %collective-permute-start.3 = (bf16[128,256]{1,0:T(8,128)(2,1)S(1)}, bf16[128,256]{1,0:T(8,128)(2,1)S(1)}, u32[]{:S(2)}, u32[]{:S(2)}) collective-permute-start(bf16[128,256]{1,0:T(8,128)(2,1)S(1)} %pack.23), channel_id=1, source_target_pairs={{0,12},{4,8},{8,4},{12,0},{16,28},{20,24},{24,20},{28,16},{1,13},{... | collective-permute-start | bytes 196616 | tf_op jit(solution)/shard_map/ppermute | solution.py:198
  55.9 8.9 %copy-start.11 = (s32[2]{0:T(128)S(1)}, s32[2]{0:T(128)}, u32[]{:S(2)}) copy-start(s32[2]{0:T(128)} %param.8) | copy-start | bytes 28
  55.9 13.4 %copy-start.1 = (bf16[1,128,12288]{2,1,0:T(8,128)(2,1)S(1)}, bf16[1,128,12288]{2,1,0:T(8,128)(2,1)}, u32[]{:S(2)}) copy-start(bf16[1,128,12288]{2,1,0:T(8,128)(2,1)} %qkv_ref.15) | copy-start | bytes 9437188
  55.9 6.3 %collective-permute-start.4 = (bf16[128,256]{1,0:T(8,128)(2,1)S(1)}, bf16[128,256]{1,0:T(8,128)(2,1)S(1)}, u32[]{:S(2)}, u32[]{:S(2)}) collective-permute-start(bf16[128,256]{1,0:T(8,128)(2,1)S(1)} %pack.24), channel_id=1, source_target_pairs={{0,8},{4,12},{8,0},{12,4},{16,24},{20,28},{24,16},{28,20},{1,9},{5... | collective-permute-start | bytes 196616 | tf_op jit(solution)/shard_map/ppermute | solution.py:198
  63.4 0.6 copy-start.8
  64.0 14.3 %collective-permute-start.5 = (bf16[128,256]{1,0:T(8,128)(2,1)}, bf16[128,256]{1,0:T(8,128)(2,1)S(1)}, u32[]{:S(2)}, u32[]{:S(2)}) collective-permute-start(bf16[128,256]{1,0:T(8,128)(2,1)} %pack.25), channel_id=1, source_target_pairs={{0,4},{4,0},{8,12},{12,8},{16,20},{20,16},{24,28},{28,24},{1,5},{5... | collective-permute-start | bytes 196616 | tf_op jit(solution)/shard_map/ppermute | solution.py:198
  69.8 24.0 %collective-permute-start.7 = (bf16[128,256]{1,0:T(8,128)(2,1)S(1)}, bf16[128,256]{1,0:T(8,128)(2,1)S(1)}, u32[]{:S(2)}, u32[]{:S(2)}) collective-permute-start(bf16[128,256]{1,0:T(8,128)(2,1)S(1)} %pack.27.refs_8_), channel_id=1, source_target_pairs={{0,16},{4,20},{8,24},{12,28},{16,0},{20,4},{24,8},{28,12},{1,17},{... | collective-permute-start | bytes 196616 | tf_op jit(solution)/shard_map/ppermute | solution.py:198
  71.6 5.9 %copy-start.3 = (bf16[2,4096,64]{1,2,0:T(8,128)(2,1)S(1)}, bf16[2,4096,64]{1,2,0:T(8,128)(2,1)}, u32[]{:S(2)}) copy-start(bf16[2,4096,64]{1,2,0:T(8,128)(2,1)} %param.6) | copy-start | bytes 3145732
  71.6 22.3 %collective-permute-start.9 = (bf16[128,256]{1,0:T(8,128)(2,1)S(1)}, bf16[128,256]{1,0:T(8,128)(2,1)S(1)}, u32[]{:S(2)}, u32[]{:S(2)}) collective-permute-start(bf16[128,256]{1,0:T(8,128)(2,1)S(1)} %pack.28), channel_id=1, source_target_pairs={{0,20},{4,16},{8,28},{12,24},{16,4},{20,0},{24,12},{28,8},{1,21},{... | collective-permute-start | bytes 196616 | tf_op jit(solution)/shard_map/ppermute | solution.py:198
  74.7 19.2 %collective-permute-start.11 = (bf16[128,256]{1,0:T(8,128)(2,1)S(1)}, bf16[128,256]{1,0:T(8,128)(2,1)S(1)}, u32[]{:S(2)}, u32[]{:S(2)}) collective-permute-start(bf16[128,256]{1,0:T(8,128)(2,1)S(1)} %pack.29), channel_id=1, source_target_pairs={{0,24},{4,28},{8,16},{12,20},{16,8},{20,12},{24,0},{28,4},{1,25},{... | collective-permute-start | bytes 196616 | tf_op jit(solution)/shard_map/ppermute | solution.py:198
  78.2 5.2 %copy-start.5 = (bf16[128,1024]{1,0:T(8,128)(2,1)S(1)}, bf16[128,1024]{1,0:T(8,128)(2,1)}, u32[]{:S(2)}) copy-start(bf16[128,1024]{1,0:T(8,128)(2,1)} %copy-done.4) | copy-start | bytes 786436
  78.2 5.1 %copy-start.7 = (bf16[128,1024]{1,0:T(8,128)(2,1)S(1)}, bf16[128,1024]{1,0:T(8,128)(2,1)}, u32[]{:S(2)}) copy-start(bf16[128,1024]{1,0:T(8,128)(2,1)} %copy-done.6) | copy-start | bytes 786436
  78.3 5.1 %copy-start.10 = (s32[4]{0:T(128)S(1)}, s32[4]{0:T(128)}, u32[]{:S(2)}) copy-start(s32[4]{0:T(128)} %frames_ref.3) | copy-start | bytes 52
  78.9 15.0 %collective-permute-start.12 = (bf16[128,256]{1,0:T(8,128)(2,1)S(1)}, bf16[128,256]{1,0:T(8,128)(2,1)S(1)}, u32[]{:S(2)}, u32[]{:S(2)}) collective-permute-start(bf16[128,256]{1,0:T(8,128)(2,1)S(1)} %pack.30), channel_id=1, source_target_pairs={{0,28},{4,24},{8,20},{12,16},{16,12},{20,8},{24,4},{28,0},{1,29},{... | collective-permute-start | bytes 196616 | tf_op jit(solution)/shard_map/ppermute | solution.py:198
  93.3 0.8 copy-start.9
  98.4 4.3 %collective-permute-start.14 = (bf16[4,64,128]{2,1,0:T(8,128)(2,1)S(1)}, bf16[4,64,128]{2,1,0:T(8,128)(2,1)S(1)}, u32[]{:S(2)}, u32[]{:S(2)}) collective-permute-start(bf16[4,64,128]{2,1,0:T(8,128)(2,1)S(1)} %get-tuple-element.8), channel_id=1, source_target_pairs={{0,4},{4,0},{8,12},{12,8},{16,20},{20,16},{24,28},{28,24},{1,5},{5... | collective-permute-start | bytes 196616 | tf_op jit(solution)/shard_map/ppermute | solution.py:198
  102.7 4.3 %collective-permute-start.15 = (f32[2,64,128]{2,1,0:T(8,128)S(1)}, f32[2,64,128]{2,1,0:T(8,128)S(1)}, u32[]{:S(2)}, u32[]{:S(2)}) collective-permute-start(f32[2,64,128]{2,1,0:T(8,128)S(1)} %slice.17), channel_id=1, source_target_pairs={{0,8},{4,12},{8,0},{12,4},{16,24},{20,28},{24,16},{28,20},{1,9},{5... | collective-permute-start | bytes 196616 | tf_op jit(solution)/shard_map/ppermute | solution.py:198
  107.1 4.9 %collective-permute-start.16 = (f32[1,64,128]{2,1,0:T(8,128)S(1)}, f32[1,64,128]{2,1,0:T(8,128)S(1)}, u32[]{:S(2)}, u32[]{:S(2)}) collective-permute-start(f32[1,64,128]{2,1,0:T(8,128)S(1)} %slice.19), channel_id=1, source_target_pairs={{0,16},{4,20},{8,24},{12,28},{16,0},{20,4},{24,8},{28,12},{1,17},{... | collective-permute-start | bytes 98312 | tf_op jit(solution)/shard_map/ppermute | solution.py:198
  112.0 1.2 %collective-permute-start.17 = (f32[64,128]{1,0:T(8,128)S(1)}, f32[64,128]{1,0:T(8,128)S(1)}, u32[]{:S(2)}, u32[]{:S(2)}) collective-permute-start(f32[64,128]{1,0:T(8,128)S(1)} %fusion), channel_id=1, source_target_pairs={{0,1},{1,0},{2,3},{3,2},{4,5},{5,4},{6,7},{7,6},{8,9},{9,8},{10,11... | collective-permute-start | bytes 98312 | tf_op jit(solution)/shard_map/ppermute | solution.py:198
  113.2 3.9 %collective-permute-start.18 = (f32[64,128]{1,0:T(8,128)S(1)}, f32[64,128]{1,0:T(8,128)S(1)}, u32[]{:S(2)}, u32[]{:S(2)}) collective-permute-start(f32[64,128]{1,0:T(8,128)S(1)} %add.32), channel_id=1, source_target_pairs={{0,2},{1,3},{2,0},{3,1},{4,6},{5,7},{6,4},{7,5},{8,10},{9,11},{10,... | collective-permute-start | bytes 98312 | tf_op jit(solution)/shard_map/ppermute | solution.py:198

commit v4 on v3

v4 whole, which is shorter than its diff:
```python
import functools
import math

import jax
import jax.numpy as jnp
from jax import lax
from jax.experimental import pallas as pl
from jax.experimental.pallas import tpu as pltpu
from jax.sharding import PartitionSpec as P

HEADS = 32
HD = 128
FRAME_TOK = 64
NT = (((1,), (1,)), ((), ()))
VMEM_LIMIT = 32 * 1024 * 1024


def fold(out_ref, column, lat, heads, qkv_ref, readout_ref):
    for i in range(heads):
        base = i * 3 * HD + 2 * HD
        values = qkv_ref[0, :, base : base + HD]
        rows = readout_ref[0, :, i * HD : (i + 1) * HD]
        folded = lax.dot_general(rows, values, NT, preferred_element_type=jnp.float32)
        row, c = (i * lat) % HD, column + (i * lat // HD) * HD
        out_ref[row : row + lat, c : c + HD] = folded.astype(jnp.bfloat16)


def pack_first_kernel(count, place_ref, qkv_ref, readout_ref, *refs):
    out_ref = refs[-1].at[0]
    for i in range(count):
        out_ref[:, i * 2 * HD : (i + 1) * 2 * HD] = qkv_ref[0, :, i * 3 * HD : i * 3 * HD + 2 * HD]
    heads = readout_ref.shape[2] // HD
    fold(out_ref, count * 2 * HD, readout_ref.shape[1], heads, qkv_ref, readout_ref)


def pack_last_kernel(place_ref, queries_ref, keys_ref, *refs):
    refs[-1][0, :, :HD] = queries_ref[0]
    refs[-1][0, :, HD:] = keys_ref[0]


def pack(place, qkv, readout_t, steps, target, heads_local, first, count, width, after):
    rows = qkv.shape[1]
    lat = readout_t.shape[1]
    operands = [place, qkv]
    if first:
        kernel = functools.partial(pack_first_kernel, count)
        in_specs = [
            pl.BlockSpec((1, rows, heads_local * 3 * HD), lambda g, m: (0, 0, target(g, m[0]))),
            pl.BlockSpec((1, lat, heads_local * HD), lambda g, m: (m[1], 0, target(g, m[0]))),
        ]
        operands += [readout_t]
    else:
        kernel = pack_last_kernel
        in_specs = [
            pl.BlockSpec((1, rows, HD), lambda g, m: (0, 0, (target(g, m[0]) * heads_local + heads_local - 1) * 3)),
            pl.BlockSpec((1, rows, HD), lambda g, m: (0, 0, (target(g, m[0]) * heads_local + heads_local - 1) * 3 + 1)),
        ]
        operands += [qkv]
    if after is not None:
        operands += [after]
        in_specs += [pl.BlockSpec(memory_space=pl.ANY)]
    return pl.pallas_call(
        kernel,
        grid_spec=pltpu.PrefetchScalarGridSpec(
            num_scalar_prefetch=1,
            grid=(steps,),
            in_specs=in_specs,
            out_specs=pl.BlockSpec((1, rows, width), lambda g, m: (g, 0, 0)),
        ),
        out_shape=jax.ShapeDtypeStruct((steps, rows, width), jnp.bfloat16),
        compiler_params=pltpu.CompilerParams(vmem_limit_bytes=VMEM_LIMIT),
        cost_estimate=pl.CostEstimate(
            flops=2 * steps * rows * lat * heads_local * HD if first else 0,
            bytes_accessed=steps * rows * width * 4,
            transcendentals=0,
        ),
        name="pack",
    )(*operands)


def attend_kernel(
    seq_count, head, count, near_value_column, far_value_column, lat, order, last, frames_ref, factor_ref, me_ref, near_ref, *refs
):
    half = seq_count // 2
    far_refs, refs = refs[:half], refs[half:]
    far_values, earlier = far_refs, None
    if head:
        far_values, earlier, refs = refs[:half], refs[half], refs[half + 1 :]
    out_refs = refs[-3:-1] if last else refs[-2:-1]
    asked = refs[-1]
    me = me_ref[0]
    rows = near_ref.shape[1]

    def near(k, i):
        return near_ref[(me & (half - 1)) ^ k, :, i * HD : (i + 1) * HD]

    def far(k, i):
        return far_refs[k - half][0, :, i * HD : (i + 1) * HD]

    def cell(k, i, what):
        return near(k, 2 * (head + i) + what) if k < half else far(k, 2 * i + what)

    def value(k, h):
        row, column = (h * lat) % HD, (h * lat // HD) * HD
        if k < half:
            column += near_value_column
            return near_ref[(me & (half - 1)) ^ k, row : row + lat, column : column + HD]
        column += far_value_column
        return far_values[k - half][0, row : row + lat, column : column + HD]

    tokens = seq_count * rows
    spans = frames_ref.shape[0]
    log2_scale = math.log2(math.e) / math.sqrt(HD)

    end = frames_ref[0] * FRAME_TOK
    ends = [end]
    for c in range(1, spans):
        end = end + frames_ref[c] * FRAME_TOK
        ends.append(end)
    row_places = lax.broadcasted_iota(jnp.int32, (rows, 1), 0)
    key_places = jnp.concatenate([(me ^ k) * rows + row_places for k in range(seq_count)], axis=0)
    column_places = lax.broadcasted_iota(jnp.int32, (1, rows), 1)
    for n, k in enumerate(order):
        for i in range(count):
            asked[n, i] = cell(k, i, 0)
    reversed_bits = seq_count.bit_length() - 1

    def place_of(n):
        k = jnp.int32(0)
        for bit in range(reversed_bits):
            k = k | (((n >> bit) & 1) << (reversed_bits - 1 - bit))
        return me ^ k

    def one_block(b, carry):
        first = b * 2
        places = jnp.concatenate([place_of(first + j) * rows + column_places for j in range(2)], axis=1)
        bound = jnp.full((1, 2 * rows), ends[0], jnp.int32)
        for c in range(1, spans):
            bound = jnp.where(places >= ends[c - 1], ends[c], bound)
        allowed = key_places < bound
        total = None
        for i in range(count):
            queries = asked[pl.ds(first, 2), i].reshape(2 * rows, HD)
            keys = jnp.concatenate([cell(k, i, 1) for k in range(seq_count)], axis=0)
            scores = lax.dot_general(keys, queries, NT, preferred_element_type=jnp.float32)
            scores = jnp.where(allowed, scores, -jnp.inf)
            peak = jnp.max(scores, axis=0, keepdims=True)
            raw = jnp.exp2((scores - peak) * log2_scale)
            row_total = jnp.sum(raw, axis=0, keepdims=True)
            weights = raw.astype(jnp.bfloat16)
            folded = jnp.concatenate([value(k, head + i) for k in range(seq_count)], axis=1)
            summed = jnp.dot(folded, weights, preferred_element_type=jnp.float32) / row_total
            total = summed if total is None else total + summed
        for j in range(2):
            part = total[:, j * rows : (j + 1) * rows]
            n = first + j
            if earlier is not None:
                part = part + earlier[n]
            if last:
                part = part * factor_ref[0]

                @pl.when(n < half)
                def _():
                    out_refs[0][n] = part

                @pl.when(n >= half)
                def _():
                    out_refs[1][n - half] = part.astype(jnp.bfloat16)
            else:
                out_refs[0][n] = part
        return carry

    lax.fori_loop(0, half, one_block, 0)


def attend(
    near, far, far_values, earlier, after, span_frames, factor, me, head, count, columns, lat, order, last
):
    half, rows, _ = near.shape
    seq_count = 2 * half
    tokens = seq_count * rows
    smem = pl.BlockSpec(memory_space=pltpu.SMEM)
    vmem = pl.BlockSpec(memory_space=pltpu.VMEM)
    operands = [span_frames, factor, me, near] + list(far)
    if head:
        operands += list(far_values) + [earlier]
    in_specs = [smem] * 3 + [vmem] * (len(operands) - 3)
    if after is not None:
        operands += [after]
        in_specs += [pl.BlockSpec(memory_space=pl.ANY)]
    if last:
        out_shape = [
            jax.ShapeDtypeStruct((seq_count // 2, lat, rows), jnp.float32),
            jax.ShapeDtypeStruct((seq_count // 2, lat, rows), jnp.bfloat16),
        ]
    else:
        out_shape = [jax.ShapeDtypeStruct((seq_count, lat, rows), jnp.float32)]
    return pl.pallas_call(
        functools.partial(attend_kernel, seq_count, head, count, *columns, lat, order, last),
        in_specs=in_specs,
        out_specs=[vmem] * len(out_shape),
        out_shape=out_shape,
        scratch_shapes=[pltpu.VMEM((seq_count, count, rows, HD), jnp.bfloat16)],
        compiler_params=pltpu.CompilerParams(vmem_limit_bytes=VMEM_LIMIT),
        cost_estimate=pl.CostEstimate(
            flops=count * tokens * tokens * 2 * (HD + lat),
            bytes_accessed=tokens * count * 3 * HD * 2,
            transcendentals=count * tokens * tokens,
        ),
        name="attend",
    )(*operands)


def swap(array, axis, offset):
    size = lax.axis_size(axis)
    return lax.ppermute(array, axis, [(i, i ^ offset) for i in range(size)])


def body(qkv, readout, step_weight, timestep, span_frames):
    seq_count = lax.axis_size("seq")
    mp_count = lax.axis_size("mp")
    heads_local = HEADS // seq_count
    lat = readout.shape[2]
    me = lax.axis_index("seq").astype(jnp.int32)
    mp_index = lax.axis_index("mp")
    sample_count = mp_count // 2
    model_index = (mp_index // sample_count).astype(jnp.int32)
    sample_index = mp_index % sample_count
    signed = jnp.where(model_index == 1, 1.0, -1.0).astype(jnp.float32)
    factor = (signed * step_weight[timestep[sample_index]]).reshape(1)
    chunks = [heads_local - 1, 1] if heads_local > 1 else [1]
    value_width = -(-heads_local * lat // HD) * HD
    columns = (heads_local * 2 * HD, chunks[0] * 2 * HD)
    widths = [columns[1] + value_width, 2 * HD]
    readout_t = jnp.swapaxes(readout, 1, 2)
    place = jnp.stack([me, model_index])
    bits = seq_count.bit_length() - 1
    order = [sum(((n >> b) & 1) << (bits - 1 - b) for b in range(bits)) for n in range(seq_count)]
    half = seq_count // 2

    def send(c, k, after):
        packed = pack(
            place, qkv, readout_t, 1, lambda g, m: m ^ k, heads_local, c == 0, chunks[c], widths[c], after
        )
        return packed, swap(packed, "seq", k)

    far = [[None] * half for _ in chunks]
    before = None
    for k in range(seq_count - 1, half - 1, -1):
        before, far[0][k - half] = send(0, k, before)
    near = pack(
        place, qkv, readout_t, half, lambda g, m: (m & -half) | g, heads_local, True, heads_local,
        columns[0] + value_width, before,
    )
    groups = [list(range(half)), list(range(half, seq_count))]
    near = lax.all_to_all(near, "seq", split_axis=0, concat_axis=0, axis_index_groups=groups, tiled=True)
    hold = None
    if len(chunks) > 1:
        for k in range(seq_count - 1, half - 1, -1):
            hold, far[1][k - half] = send(1, k, far[0][k - half])

    result, head = None, 0
    for c, count in enumerate(chunks):
        last = c == len(chunks) - 1
        result = attend(
            near, far[c], far[0], result, None if last else hold, span_frames, factor, me.reshape(1),
            head, count, columns, lat, order, last,
        )
        head += count
        if not last:
            result = result[0]
    keep, give = result
    offset = 1
    while True:
        keep = keep + swap(give, "seq", offset).astype(jnp.float32)
        offset *= 2
        if offset == seq_count:
            break
        size = keep.shape[0] // 2
        keep, give = keep[:size], keep[size:]
    whole = keep[0]
    offset = 1
    while offset < mp_count:
        whole = whole + swap(whole, "mp", offset)
        offset *= 2
    return whole.T


def solution(mesh):
    return jax.shard_map(
        body,
        mesh=mesh,
        in_specs=(P("mp", "seq", None), P(), P(), P(), P()),
        out_specs=P("seq", None),
        check_vma=False,
    )
```

time: 118 us -> 110 us (0.932)
  waiting for transfers between devices: 43.3 us -> 27.5 us
  starting transfers between devices: 36.7 us -> 48.2 us
  Pallas kernels: 28.3 us -> 22.4 us
  local copies, waits for them, and re-layouts: 5.85 us -> 7.48 us
    ppermute x19 -> x13, waiting for transfers between devices: 43.3 us -> 27.5 us  [swap(): return lax.ppermute(array, axis, [(i, i ^ offset) for i in range(size)])]
    pallas_call x16 -> x9, Pallas kernels: 14.1 us -> 7.47 us  [pack(): pl.pallas_call(kernel, grid_spec=pltpu.PrefetchScalarGridSpec(num_scalar_...]
    ppermute x19 -> x13, starting transfers between devices: 36.7 us -> 42.9 us  [swap(): return lax.ppermute(array, axis, [(i, i ^ offset) for i in range(size)])]
    all_to_all x0 -> x1, starting transfers between devices: none -> 5.35 us  [body(): lax.all_to_all(near, 'seq', split_axis=0, concat_axis=0, axis_index_group...]
    unnamed x24 -> x18, local copies, waits for them, and re-layouts: 3.99 us -> 5.61 us
  transfers between devices with their start and end apart: 19 -> 14, of which waited for: 10 -> 8; matrix products, arithmetic and copies ran while one was open for 2% -> 2% of each run, Pallas kernels for 13% -> 12%
where the time goes in v4:
time: 110 us; the launch traced here: 109 us
  starting transfers between devices  48.2 us (44%)
  waiting for transfers between devices  27.5 us (25%)
  Pallas kernels  22.4 us (20%)
  local copies, waits for them, and re-layouts  7.48 us (7%)
  between operations  2.81 us (3%)
    ppermute x13, starting transfers between devices, swap(): return lax.ppermute(array, axis, [(i, i ^ offset) for i in range(size)])  42.9 us
    ppermute x13, waiting for transfers between devices, swap(): return lax.ppermute(array, axis, [(i, i ^ offset) for i in range(size)])  27.5 us
    pallas_call x2, Pallas kernels, attend(): pl.pallas_call(functools.partial(attend_kernel, seq_count, head, count, *...  14.9 us
    pallas_call x9, Pallas kernels, pack(): pl.pallas_call(kernel, grid_spec=pltpu.PrefetchScalarGridSpec(num_scalar_...  7.47 us
    unnamed x18, local copies, waits for them, and re-layouts  5.61 us
    all_to_all x1, starting transfers between devices, body(): lax.all_to_all(near, 'seq', split_axis=0, concat_axis=0, axis_index_group...  5.35 us
  transfers between devices with their start and end apart: 14, of which 8 were waited for; matrix products, arithmetic and copies ran while one was open for 2% of the time, Pallas kernels for 12%

profile of v4, /device:TPU:0, one launch (start us, length us, event | category | flops | bytes accessed | tf_op | source)
XLA Modules:
  0.0 109.2 jit_solution(17498174826300576445)
XLA Ops:
  0.0 0.1 pad_add_fusion.place_ref
  0.1 1.9 %copy-done = bf16[1,128,12288]{2,1,0:T(8,128)(2,1)S(1)} copy-done((bf16[1,128,12288]{2,1,0:T(8,128)(2,1)S(1)}, bf16[1,128,12288]{2,1,0:T(8,128)(2,1)}, u32[]{:S(2)}) %copy-start) | copy-done | bytes 3145752
  2.0 1.2 %copy-done.2 = bf16[2,4096,64]{1,2,0:T(8,128)(2,1)S(1)} copy-done((bf16[2,4096,64]{1,2,0:T(8,128)(2,1)S(1)}, bf16[2,4096,64]{1,2,0:T(8,128)(2,1)}, u32[]{:S(2)}) %copy-start.2) | copy-done | bytes 1048600
  3.2 0.8 pack.9.refs_0_
  4.0 0.8 pack.10.refs_0_
  4.7 0.8 pack.11.refs_0_
  5.5 0.8 pack.12.refs_0_
  6.3 0.7 copy-done.5
  7.0 1.5 %pack.13 = bf16[4,128,1280]{2,1,0:T(8,128)(2,1)S(1)} custom-call(s32[2]{0:T(128)S(1)} %pad_add_fusion.place_ref, bf16[1,128,12288]{2,1,0:T(8,128)(2,1)S(1)} %copy-done, bf16[2,64,4096]{2,1,0:T(8,128)(2,1)S(1)} %bitcast.14, bf16[1,128,1024]{2,1,0:T(8,128)(2,1)S(1)} %pack.12.refs_0_), custom_call_target="tpu_custom_call" | custom-call | flops 33554432 | bytes 2621440 | tf_op jit(solution)/shard_map/pack/pallas_call | solution.py:62
  8.5 1.1 copy-done.3
  9.6 0.7 copy-done.6
  10.3 5.4 %all-to-all-start = ((bf16[4,128,1280]{2,1,0:T(8,128)(2,1)}), bf16[4,128,1280]{2,1,0:T(8,128)(2,1)}, u32[]{:S(2)}, u32[]{:S(2)}) async-start(bf16[4,128,1280]{2,1,0:T(8,128)(2,1)} %copy-done.3), calls=%async_computation | async-start | bytes 2621440 | tf_op jit(solution)/shard_map/all_to_all | solution.py:256
  15.7 3.2 %collective-permute-start = (bf16[1,128,1024]{2,1,0:T(8,128)(2,1)}, bf16[1,128,1024]{2,1,0:T(8,128)(2,1)}, u32[]{:S(2)}, u32[]{:S(2)}) collective-permute-start(bf16[1,128,1024]{2,1,0:T(8,128)(2,1)} %copy-done.6), channel_id=1, source_target_pairs={{0,16},{4,20},{8,24},{12,28},{16,0},{20,4},{24,8},{28,12},{1,17},{... | collective-permute-start | bytes 786440 | tf_op jit(solution)/shard_map/ppermute | solution.py:216
  18.9 1.3 %collective-permute-start.2 = (bf16[1,128,1024]{2,1,0:T(8,128)(2,1)}, bf16[1,128,1024]{2,1,0:T(8,128)(2,1)}, u32[]{:S(2)}, u32[]{:S(2)}) collective-permute-start(bf16[1,128,1024]{2,1,0:T(8,128)(2,1)} %copy-done.5), channel_id=1, source_target_pairs={{0,20},{4,16},{8,28},{12,24},{16,4},{20,0},{24,12},{28,8},{1,21},{... | collective-permute-start | bytes 786440 | tf_op jit(solution)/shard_map/ppermute | solution.py:216
  20.2 3.8 %collective-permute-start.4 = (bf16[1,128,1024]{2,1,0:T(8,128)(2,1)}, bf16[1,128,1024]{2,1,0:T(8,128)(2,1)}, u32[]{:S(2)}, u32[]{:S(2)}) collective-permute-start(bf16[1,128,1024]{2,1,0:T(8,128)(2,1)} %copy-done.4), channel_id=1, source_target_pairs={{0,24},{4,28},{8,16},{12,20},{16,8},{20,12},{24,0},{28,4},{1,25},{... | collective-permute-start | bytes 786440 | tf_op jit(solution)/shard_map/ppermute | solution.py:216
  24.0 0.0 collective-permute-start.6
  24.1 0.6 dynamic_slice.6
  26.6 1.3 %dynamic_slice.7 = f32[1]{0:T(128)} dynamic-slice(f32[1000]{0:T(1024)} %param.7, s32[]{:T(128)S(6)} %select_n.25), dynamic_slice_sizes={1} | dynamic-slice | bytes 12 | tf_op jit(solution)/shard_map/dynamic_slice | solution.py:230
  28.5 8.3 %collective-permute-done.refs_0_.refs_4_ = bf16[1,128,1024]{2,1,0:T(8,128)(2,1)} collective-permute-done((bf16[1,128,1024]{2,1,0:T(8,128)(2,1)}, bf16[1,128,1024]{2,1,0:T(8,128)(2,1)}, u32[]{:S(2)}, u32[]{:S(2)}) %collective-permute-start) | collective-permute-done | bytes 262176 | tf_op jit(solution)/shard_map/ppermute | solution.py:216
  36.8 0.6 pack.14.refs_4_
  37.4 3.5 %collective-permute-start.1 = (bf16[1,128,256]{2,1,0:T(8,128)(2,1)S(1)}, bf16[1,128,256]{2,1,0:T(8,128)(2,1)}, u32[]{:S(2)}, u32[]{:S(2)}) collective-permute-start(bf16[1,128,256]{2,1,0:T(8,128)(2,1)S(1)} %pack.14.refs_4_), channel_id=1, source_target_pairs={{0,16},{4,20},{8,24},{12,28},{16,0},{20,4},{24,8},{28,12},{1,17},{... | collective-permute-start | bytes 196616 | tf_op jit(solution)/shard_map/ppermute | solution.py:216
  40.9 1.5 %collective-permute-done.2.refs_0_.refs_1_.refs_5_ = bf16[1,128,1024]{2,1,0:T(8,128)(2,1)} collective-permute-done((bf16[1,128,1024]{2,1,0:T(8,128)(2,1)}, bf16[1,128,1024]{2,1,0:T(8,128)(2,1)}, u32[]{:S(2)}, u32[]{:S(2)}) %collective-permute-start.2) | collective-permute-done | bytes 262176 | tf_op jit(solution)/shard_map/ppermute | solution.py:216
  42.5 0.6 pack.15
  43.0 4.4 %collective-permute-start.3 = (bf16[1,128,256]{2,1,0:T(8,128)(2,1)S(1)}, bf16[1,128,256]{2,1,0:T(8,128)(2,1)}, u32[]{:S(2)}, u32[]{:S(2)}) collective-permute-start(bf16[1,128,256]{2,1,0:T(8,128)(2,1)S(1)} %pack.15), channel_id=1, source_target_pairs={{0,20},{4,16},{8,28},{12,24},{16,4},{20,0},{24,12},{28,8},{1,21},{... | collective-permute-start | bytes 196616 | tf_op jit(solution)/shard_map/ppermute | solution.py:216
  47.4 5.6 %collective-permute-done.4.refs_0_.refs_2_.refs_6_ = bf16[1,128,1024]{2,1,0:T(8,128)(2,1)} collective-permute-done((bf16[1,128,1024]{2,1,0:T(8,128)(2,1)}, bf16[1,128,1024]{2,1,0:T(8,128)(2,1)}, u32[]{:S(2)}, u32[]{:S(2)}) %collective-permute-start.4) | collective-permute-done | bytes 262176 | tf_op jit(solution)/shard_map/ppermute | solution.py:216
  53.1 1.2 %pack.16 = bf16[1,128,256]{2,1,0:T(8,128)(2,1)} custom-call(s32[2]{0:T(128)S(1)} %pad_add_fusion.place_ref, bf16[1,128,12288]{2,1,0:T(8,128)(2,1)S(1)} %copy-done.1, bf16[1,128,12288]{2,1,0:T(8,128)(2,1)S(1)} %copy-done.1, bf16[1,128,1024]{2,1,0:T(8,128)(2,1)} %collective-permute-done.4.refs_0_.refs_2_.refs_6_), custom_call_target="tpu_custom_call" | custom-call | bytes 131072 | tf_op jit(solution)/shard_map/pack/pallas_call | solution.py:62
  54.3 10.8 %collective-permute-start.5 = (bf16[1,128,256]{2,1,0:T(8,128)(2,1)}, bf16[1,128,256]{2,1,0:T(8,128)(2,1)}, u32[]{:S(2)}, u32[]{:S(2)}) collective-permute-start(bf16[1,128,256]{2,1,0:T(8,128)(2,1)} %pack.16), channel_id=1, source_target_pairs={{0,24},{4,28},{8,16},{12,20},{16,8},{20,12},{24,0},{28,4},{1,25},{... | collective-permute-start | bytes 196616 | tf_op jit(solution)/shard_map/ppermute | solution.py:216
  65.1 0.0 collective-permute-done.6.refs_0_.refs_3_.refs_7_
  65.1 0.6 pack.17
  65.7 0.1 collective-permute-start.7
  65.7 0.0 all-to-all-done.near_ref
  65.8 10.2 %attend.2.refs_8_ = f32[8,64,128]{2,1,0:T(8,128)S(1)} custom-call(s32[4]{0:T(128)S(1)} %copy-done.7, f32[1]{0:T(128)} %bitcast.2.factor_ref, s32[1]{0:T(128)} %bitcast.3.me_ref, bf16[4,128,1280]{2,1,0:T(8,128)(2,1)} %all-to-all-done.near_ref, bf16[1,128,1024]{2,1,0:T(8,128)(2,1)} %collective-permute-done.refs_0_.refs_4_, ...), custom_call_target="tpu_custom_call" | custom-call | flops 1207959552 | bytes 2359296 | tf_op jit(solution)/shard_map/attend/pallas_call | solution.py:198
  76.0 0.0 collective-permute-done.1.refs_0_
  76.0 0.0 collective-permute-done.3.refs_1_
  76.0 0.0 collective-permute-done.5.refs_2_
  76.0 0.0 collective-permute-done.7.refs_3_
  76.0 4.7 %attend.3 = (f32[4,64,128]{2,1,0:T(8,128)S(1)}, bf16[4,64,128]{2,1,0:T(8,128)(2,1)S(1)}) custom-call(s32[4]{0:T(128)S(1)} %copy-done.7, f32[1]{0:T(128)} %bitcast.2.factor_ref, s32[1]{0:T(128)} %bitcast.3.me_ref, bf16[4,128,1280]{2,1,0:T(8,128)(2,1)} %all-to-all-done.near_ref, bf16[1,128,256]{2,1,0:T(8,128)(2,1)} %collective-permute-done.1.refs_0_, ...), custom_call_target="tpu_custom_call" | custom-call | flops 402653184 | bytes 786432 | tf_op jit(solution)/shard_map/attend/pallas_call | solution.py:198
  80.8 1.5 %collective-permute-start.8 = (bf16[4,64,128]{2,1,0:T(8,128)(2,1)S(1)}, bf16[4,64,128]{2,1,0:T(8,128)(2,1)S(1)}, u32[]{:S(2)}, u32[]{:S(2)}) collective-permute-start(bf16[4,64,128]{2,1,0:T(8,128)(2,1)S(1)} %get-tuple-element.8), channel_id=1, source_target_pairs={{0,4},{4,0},{8,12},{12,8},{16,20},{20,16},{24,28},{28,24},{1,5},{5... | collective-permute-start | bytes 196616 | tf_op jit(solution)/shard_map/ppermute | solution.py:216
  82.3 2.8 %collective-permute-done.8 = bf16[4,64,128]{2,1,0:T(8,128)(2,1)S(1)} collective-permute-done((bf16[4,64,128]{2,1,0:T(8,128)(2,1)S(1)}, bf16[4,64,128]{2,1,0:T(8,128)(2,1)S(1)}, u32[]{:S(2)}, u32[]{:S(2)}) %collective-permute-start.8) | collective-permute-done | bytes 65568 | tf_op jit(solution)/shard_map/ppermute | solution.py:216
  85.1 11.2 %collective-permute-start.9 = (f32[2,64,128]{2,1,0:T(8,128)S(1)}, f32[2,64,128]{2,1,0:T(8,128)S(1)}, u32[]{:S(2)}, u32[]{:S(2)}) collective-permute-start(f32[2,64,128]{2,1,0:T(8,128)S(1)} %slice.17), channel_id=1, source_target_pairs={{0,8},{4,12},{8,0},{12,4},{16,24},{20,28},{24,16},{28,20},{1,9},{5... | collective-permute-start | bytes 196616 | tf_op jit(solution)/shard_map/ppermute | solution.py:216
  96.3 2.2 %collective-permute-done.9 = f32[2,64,128]{2,1,0:T(8,128)S(1)} collective-permute-done((f32[2,64,128]{2,1,0:T(8,128)S(1)}, f32[2,64,128]{2,1,0:T(8,128)S(1)}, u32[]{:S(2)}, u32[]{:S(2)}) %collective-permute-start.9) | collective-permute-done | bytes 65568 | tf_op jit(solution)/shard_map/ppermute | solution.py:216
  98.6 1.6 %collective-permute-start.10 = (f32[1,64,128]{2,1,0:T(8,128)S(1)}, f32[1,64,128]{2,1,0:T(8,128)S(1)}, u32[]{:S(2)}, u32[]{:S(2)}) collective-permute-start(f32[1,64,128]{2,1,0:T(8,128)S(1)} %slice.19), channel_id=1, source_target_pairs={{0,16},{4,20},{8,24},{12,28},{16,0},{20,4},{24,8},{28,12},{1,17},{... | collective-permute-start | bytes 98312 | tf_op jit(solution)/shard_map/ppermute | solution.py:216
  100.1 3.3 %collective-permute-done.10 = f32[1,64,128]{2,1,0:T(8,128)S(1)} collective-permute-done((f32[1,64,128]{2,1,0:T(8,128)S(1)}, f32[1,64,128]{2,1,0:T(8,128)S(1)}, u32[]{:S(2)}, u32[]{:S(2)}) %collective-permute-start.10) | collective-permute-done | bytes 32800 | tf_op jit(solution)/shard_map/ppermute | solution.py:216
  103.4 0.0 collective-permute-start.11
  103.5 1.2 %collective-permute-done.11 = f32[64,128]{1,0:T(8,128)S(1)} collective-permute-done((f32[64,128]{1,0:T(8,128)S(1)}, f32[64,128]{1,0:T(8,128)S(1)}, u32[]{:S(2)}, u32[]{:S(2)}) %collective-permute-start.11) | collective-permute-done | bytes 32800 | tf_op jit(solution)/shard_map/ppermute | solution.py:216
  104.7 1.5 %collective-permute-start.12 = (f32[64,128]{1,0:T(8,128)S(1)}, f32[64,128]{1,0:T(8,128)S(1)}, u32[]{:S(2)}, u32[]{:S(2)}) collective-permute-start(f32[64,128]{1,0:T(8,128)S(1)} %add.32), channel_id=1, source_target_pairs={{0,2},{1,3},{2,0},{3,1},{4,6},{5,7},{6,4},{7,5},{8,10},{9,11},{10,... | collective-permute-start | bytes 98312 | tf_op jit(solution)/shard_map/ppermute | solution.py:216
  106.2 2.4 %collective-permute-done.12 = f32[64,128]{1,0:T(8,128)S(1)} collective-permute-done((f32[64,128]{1,0:T(8,128)S(1)}, f32[64,128]{1,0:T(8,128)S(1)}, u32[]{:S(2)}, u32[]{:S(2)}) %collective-permute-start.12) | collective-permute-done | bytes 32800 | tf_op jit(solution)/shard_map/ppermute | solution.py:216
  108.6 0.6 add_bitcast_fusion
  (19 shorter events, 0.1 us)
Async XLA Ops:
  0.1 1.9 %copy-start = (bf16[1,128,12288]{2,1,0:T(8,128)(2,1)S(1)}, bf16[1,128,12288]{2,1,0:T(8,128)(2,1)}, u32[]{:S(2)}) copy-start(bf16[1,128,12288]{2,1,0:T(8,128)(2,1)} %keys_ref.7) | copy-start | bytes 9437188
  2.0 1.2 %copy-start.2 = (bf16[2,4096,64]{1,2,0:T(8,128)(2,1)S(1)}, bf16[2,4096,64]{1,2,0:T(8,128)(2,1)}, u32[]{:S(2)}) copy-start(bf16[2,4096,64]{1,2,0:T(8,128)(2,1)} %param.6) | copy-start | bytes 3145732
  4.7 0.8 copy-start.4
  6.3 0.7 copy-start.5
  7.0 29.8 %copy-start.1 = (bf16[1,128,12288]{2,1,0:T(8,128)(2,1)S(1)}, bf16[1,128,12288]{2,1,0:T(8,128)(2,1)}, u32[]{:S(2)}) copy-start(bf16[1,128,12288]{2,1,0:T(8,128)(2,1)} %keys_ref.7) | copy-start | bytes 9437188
  8.5 1.1 copy-start.3
  9.6 0.7 copy-start.6
  10.3 13.7 %copy-start.8 = (s32[2]{0:T(128)S(1)}, s32[2]{0:T(128)}, u32[]{:S(2)}) copy-start(s32[2]{0:T(128)} %param.8) | copy-start | bytes 28
  10.3 55.4 %all-to-all-start = ((bf16[4,128,1280]{2,1,0:T(8,128)(2,1)}), bf16[4,128,1280]{2,1,0:T(8,128)(2,1)}, u32[]{:S(2)}, u32[]{:S(2)}) async-start(bf16[4,128,1280]{2,1,0:T(8,128)(2,1)} %copy-done.3), calls=%async_computation | async-start | bytes 2621440 | tf_op jit(solution)/shard_map/all_to_all | solution.py:256
  15.7 21.2 %collective-permute-start = (bf16[1,128,1024]{2,1,0:T(8,128)(2,1)}, bf16[1,128,1024]{2,1,0:T(8,128)(2,1)}, u32[]{:S(2)}, u32[]{:S(2)}) collective-permute-start(bf16[1,128,1024]{2,1,0:T(8,128)(2,1)} %copy-done.6), channel_id=1, source_target_pairs={{0,16},{4,20},{8,24},{12,28},{16,0},{20,4},{24,8},{28,12},{1,17},{... | collective-permute-start | bytes 786440 | tf_op jit(solution)/shard_map/ppermute | solution.py:216
  18.9 23.6 %collective-permute-start.2 = (bf16[1,128,1024]{2,1,0:T(8,128)(2,1)}, bf16[1,128,1024]{2,1,0:T(8,128)(2,1)}, u32[]{:S(2)}, u32[]{:S(2)}) collective-permute-start(bf16[1,128,1024]{2,1,0:T(8,128)(2,1)} %copy-done.5), channel_id=1, source_target_pairs={{0,20},{4,16},{8,28},{12,24},{16,4},{20,0},{24,12},{28,8},{1,21},{... | collective-permute-start | bytes 786440 | tf_op jit(solution)/shard_map/ppermute | solution.py:216
  20.2 32.9 %collective-permute-start.4 = (bf16[1,128,1024]{2,1,0:T(8,128)(2,1)}, bf16[1,128,1024]{2,1,0:T(8,128)(2,1)}, u32[]{:S(2)}, u32[]{:S(2)}) collective-permute-start(bf16[1,128,1024]{2,1,0:T(8,128)(2,1)} %copy-done.4), channel_id=1, source_target_pairs={{0,24},{4,28},{8,16},{12,20},{16,8},{20,12},{24,0},{28,4},{1,25},{... | collective-permute-start | bytes 786440 | tf_op jit(solution)/shard_map/ppermute | solution.py:216
  24.0 41.0 %collective-permute-start.6 = (bf16[1,128,1024]{2,1,0:T(8,128)(2,1)S(1)}, bf16[1,128,1024]{2,1,0:T(8,128)(2,1)}, u32[]{:S(2)}, u32[]{:S(2)}) collective-permute-start(bf16[1,128,1024]{2,1,0:T(8,128)(2,1)S(1)} %pack.9.refs_0_), channel_id=1, source_target_pairs={{0,28},{4,24},{8,20},{12,16},{16,12},{20,8},{24,4},{28,0},{1,29},{... | collective-permute-start | bytes 786440 | tf_op jit(solution)/shard_map/ppermute | solution.py:216
  37.4 38.6 %collective-permute-start.1 = (bf16[1,128,256]{2,1,0:T(8,128)(2,1)S(1)}, bf16[1,128,256]{2,1,0:T(8,128)(2,1)}, u32[]{:S(2)}, u32[]{:S(2)}) collective-permute-start(bf16[1,128,256]{2,1,0:T(8,128)(2,1)S(1)} %pack.14.refs_4_), channel_id=1, source_target_pairs={{0,16},{4,20},{8,24},{12,28},{16,0},{20,4},{24,8},{28,12},{1,17},{... | collective-permute-start | bytes 196616 | tf_op jit(solution)/shard_map/ppermute | solution.py:216
  43.0 32.9 %collective-permute-start.3 = (bf16[1,128,256]{2,1,0:T(8,128)(2,1)S(1)}, bf16[1,128,256]{2,1,0:T(8,128)(2,1)}, u32[]{:S(2)}, u32[]{:S(2)}) collective-permute-start(bf16[1,128,256]{2,1,0:T(8,128)(2,1)S(1)} %pack.15), channel_id=1, source_target_pairs={{0,20},{4,16},{8,28},{12,24},{16,4},{20,0},{24,12},{28,8},{1,21},{... | collective-permute-start | bytes 196616 | tf_op jit(solution)/shard_map/ppermute | solution.py:216
  54.3 11.5 %copy-start.7 = (s32[4]{0:T(128)S(1)}, s32[4]{0:T(128)}, u32[]{:S(2)}) copy-start(s32[4]{0:T(128)} %frames_ref.3) | copy-start | bytes 52
  54.3 21.7 %collective-permute-start.5 = (bf16[1,128,256]{2,1,0:T(8,128)(2,1)}, bf16[1,128,256]{2,1,0:T(8,128)(2,1)}, u32[]{:S(2)}, u32[]{:S(2)}) collective-permute-start(bf16[1,128,256]{2,1,0:T(8,128)(2,1)} %pack.16), channel_id=1, source_target_pairs={{0,24},{4,28},{8,16},{12,20},{16,8},{20,12},{24,0},{28,4},{1,25},{... | collective-permute-start | bytes 196616 | tf_op jit(solution)/shard_map/ppermute | solution.py:216
  65.7 10.4 %collective-permute-start.7 = (bf16[1,128,256]{2,1,0:T(8,128)(2,1)S(1)}, bf16[1,128,256]{2,1,0:T(8,128)(2,1)S(1)}, u32[]{:S(2)}, u32[]{:S(2)}) collective-permute-start(bf16[1,128,256]{2,1,0:T(8,128)(2,1)S(1)} %pack.17), channel_id=1, source_target_pairs={{0,28},{4,24},{8,20},{12,16},{16,12},{20,8},{24,4},{28,0},{1,29},{... | collective-permute-start | bytes 196616 | tf_op jit(solution)/shard_map/ppermute | solution.py:216
  80.8 4.3 %collective-permute-start.8 = (bf16[4,64,128]{2,1,0:T(8,128)(2,1)S(1)}, bf16[4,64,128]{2,1,0:T(8,128)(2,1)S(1)}, u32[]{:S(2)}, u32[]{:S(2)}) collective-permute-start(bf16[4,64,128]{2,1,0:T(8,128)(2,1)S(1)} %get-tuple-element.8), channel_id=1, source_target_pairs={{0,4},{4,0},{8,12},{12,8},{16,20},{20,16},{24,28},{28,24},{1,5},{5... | collective-permute-start | bytes 196616 | tf_op jit(solution)/shard_map/ppermute | solution.py:216
  85.1 13.4 %collective-permute-start.9 = (f32[2,64,128]{2,1,0:T(8,128)S(1)}, f32[2,64,128]{2,1,0:T(8,128)S(1)}, u32[]{:S(2)}, u32[]{:S(2)}) collective-permute-start(f32[2,64,128]{2,1,0:T(8,128)S(1)} %slice.17), channel_id=1, source_target_pairs={{0,8},{4,12},{8,0},{12,4},{16,24},{20,28},{24,16},{28,20},{1,9},{5... | collective-permute-start | bytes 196616 | tf_op jit(solution)/shard_map/ppermute | solution.py:216
  98.6 4.9 %collective-permute-start.10 = (f32[1,64,128]{2,1,0:T(8,128)S(1)}, f32[1,64,128]{2,1,0:T(8,128)S(1)}, u32[]{:S(2)}, u32[]{:S(2)}) collective-permute-start(f32[1,64,128]{2,1,0:T(8,128)S(1)} %slice.19), channel_id=1, source_target_pairs={{0,16},{4,20},{8,24},{12,28},{16,0},{20,4},{24,8},{28,12},{1,17},{... | collective-permute-start | bytes 98312 | tf_op jit(solution)/shard_map/ppermute | solution.py:216
  103.4 1.2 %collective-permute-start.11 = (f32[64,128]{1,0:T(8,128)S(1)}, f32[64,128]{1,0:T(8,128)S(1)}, u32[]{:S(2)}, u32[]{:S(2)}) collective-permute-start(f32[64,128]{1,0:T(8,128)S(1)} %fusion), channel_id=1, source_target_pairs={{0,1},{1,0},{2,3},{3,2},{4,5},{5,4},{6,7},{7,6},{8,9},{9,8},{10,11... | collective-permute-start | bytes 98312 | tf_op jit(solution)/shard_map/ppermute | solution.py:216
  104.7 3.9 %collective-permute-start.12 = (f32[64,128]{1,0:T(8,128)S(1)}, f32[64,128]{1,0:T(8,128)S(1)}, u32[]{:S(2)}, u32[]{:S(2)}) collective-permute-start(f32[64,128]{1,0:T(8,128)S(1)} %add.32), channel_id=1, source_target_pairs={{0,2},{1,3},{2,0},{3,1},{4,6},{5,7},{6,4},{7,5},{8,10},{9,11},{10,... | collective-permute-start | bytes 98312 | tf_op jit(solution)/shard_map/ppermute | solution.py:216

commit v5 on v3

v5 whole, which is shorter than its diff:
```python
import functools
import math

import jax
import jax.numpy as jnp
from jax import lax
from jax.experimental import pallas as pl
from jax.experimental.pallas import tpu as pltpu
from jax.sharding import PartitionSpec as P

HEADS = 32
HD = 128
FRAME_TOK = 64
NT = (((1,), (1,)), ((), ()))
VMEM_LIMIT = 32 * 1024 * 1024


def layout(score_heads, value_heads, lat):
    scores = {h: n * 2 * HD for n, h in enumerate(score_heads)}
    start = len(score_heads) * 2 * HD
    values = {h: ((n * lat) % HD, start + (n * lat // HD) * HD) for n, h in enumerate(value_heads)}
    return scores, values, start + -(-len(value_heads) * lat // HD) * HD


def pack_kernel(scores, values, place_ref, qkv_ref, readout_ref, *refs):
    out_ref = refs[-1]
    lat = readout_ref.shape[1]
    for h, column in scores.items():
        out_ref[:, column : column + 2 * HD] = qkv_ref[0, :, h * 3 * HD : h * 3 * HD + 2 * HD]
    for h, (row, column) in values.items():
        own = qkv_ref[0, :, h * 3 * HD + 2 * HD : (h + 1) * 3 * HD]
        rows = readout_ref[0, :, h * HD : (h + 1) * HD]
        folded = lax.dot_general(rows, own, NT, preferred_element_type=jnp.float32)
        out_ref[row : row + lat, column : column + HD] = folded.astype(jnp.bfloat16)


def pack(place, qkv, readout_t, k, heads_local, piece, after):
    rows = qkv.shape[1]
    lat = readout_t.shape[1]
    scores, values, width = piece
    operands = [place, qkv, readout_t]
    in_specs = [
        pl.BlockSpec((1, rows, heads_local * 3 * HD), lambda g, m: (0, 0, m[0] ^ k)),
        pl.BlockSpec((1, lat, heads_local * HD), lambda g, m: (m[1], 0, m[0] ^ k)),
    ]
    if after is not None:
        operands += [after]
        in_specs += [pl.BlockSpec(memory_space=pl.ANY)]
    return pl.pallas_call(
        functools.partial(pack_kernel, scores, values),
        grid_spec=pltpu.PrefetchScalarGridSpec(
            num_scalar_prefetch=1,
            grid=(1,),
            in_specs=in_specs,
            out_specs=pl.BlockSpec((rows, width), lambda g, m: (0, 0)),
        ),
        out_shape=jax.ShapeDtypeStruct((rows, width), jnp.bfloat16),
        compiler_params=pltpu.CompilerParams(vmem_limit_bytes=VMEM_LIMIT),
        cost_estimate=pl.CostEstimate(
            flops=2 * rows * lat * len(values) * HD, bytes_accessed=rows * width * 4, transcendentals=0
        ),
        name="pack",
    )(*operands)


def attend_kernel(seq_count, heads, near_piece, far_pieces, lat, order, last, later, frames_ref, factor_ref, me_ref, *refs):
    half = seq_count // 2
    count = len(heads)
    near_refs, refs = refs[:half], refs[half:]
    far_refs, refs = refs[: half * len(far_pieces)], refs[half * len(far_pieces) :]
    earlier = refs[0] if later else None
    out_refs = refs[-3:-1] if last else refs[-2:-1]
    asked = refs[-1]
    me = me_ref[0]
    rows = near_refs[0].shape[0]

    def sources(k):
        if k < half:
            return [(near_refs[k], near_piece)]
        return [(far_refs[c * half + k - half], piece) for c, piece in enumerate(far_pieces)]

    def cell(k, h, what):
        for ref, (scores, _, _) in sources(k):
            if h in scores:
                column = scores[h] + what * HD
                return ref[:, column : column + HD]

    def value(k, h):
        for ref, (_, values, _) in sources(k):
            if h in values:
                row, column = values[h]
                return ref[row : row + lat, column : column + HD]

    tokens = seq_count * rows
    spans = frames_ref.shape[0]
    log2_scale = math.log2(math.e) / math.sqrt(HD)

    end = frames_ref[0] * FRAME_TOK
    ends = [end]
    for c in range(1, spans):
        end = end + frames_ref[c] * FRAME_TOK
        ends.append(end)
    row_places = lax.broadcasted_iota(jnp.int32, (rows, 1), 0)
    key_places = jnp.concatenate([(me ^ k) * rows + row_places for k in range(seq_count)], axis=0)
    column_places = lax.broadcasted_iota(jnp.int32, (1, rows), 1)
    for n, k in enumerate(order):
        for i in range(count):
            asked[n, i] = cell(k, heads[i], 0)
    reversed_bits = seq_count.bit_length() - 1

    def place_of(n):
        k = jnp.int32(0)
        for bit in range(reversed_bits):
            k = k | (((n >> bit) & 1) << (reversed_bits - 1 - bit))
        return me ^ k

    def one_block(b, carry):
        first = b * 2
        places = jnp.concatenate([place_of(first + j) * rows + column_places for j in range(2)], axis=1)
        bound = jnp.full((1, 2 * rows), ends[0], jnp.int32)
        for c in range(1, spans):
            bound = jnp.where(places >= ends[c - 1], ends[c], bound)
        allowed = key_places < bound
        total = None
        for i in range(count):
            queries = asked[pl.ds(first, 2), i].reshape(2 * rows, HD)
            keys = jnp.concatenate([cell(k, heads[i], 1) for k in range(seq_count)], axis=0)
            scores = lax.dot_general(keys, queries, NT, preferred_element_type=jnp.float32)
            scores = jnp.where(allowed, scores, -jnp.inf)
            peak = jnp.max(scores, axis=0, keepdims=True)
            raw = jnp.exp2((scores - peak) * log2_scale)
            row_total = jnp.sum(raw, axis=0, keepdims=True)
            weights = raw.astype(jnp.bfloat16)
            folded = jnp.concatenate([value(k, heads[i]) for k in range(seq_count)], axis=1)
            summed = jnp.dot(folded, weights, preferred_element_type=jnp.float32) / row_total
            total = summed if total is None else total + summed
        for j in range(2):
            part = total[:, j * rows : (j + 1) * rows]
            n = first + j
            if earlier is not None:
                part = part + earlier[n]
            if last:
                part = part * factor_ref[0]

                @pl.when(n < half)
                def _():
                    out_refs[0][n] = part

                @pl.when(n >= half)
                def _():
                    out_refs[1][n - half] = part.astype(jnp.bfloat16)
            else:
                out_refs[0][n] = part
        return carry

    lax.fori_loop(0, half, one_block, 0)


def attend(near, far, earlier, after, span_frames, factor, me, heads, near_piece, far_pieces, lat, order, last):
    half = len(near)
    rows = near[0].shape[0]
    seq_count = 2 * half
    tokens = seq_count * rows
    count = len(heads)
    smem = pl.BlockSpec(memory_space=pltpu.SMEM)
    vmem = pl.BlockSpec(memory_space=pltpu.VMEM)
    operands = [span_frames, factor, me] + list(near) + [p for pieces in far for p in pieces]
    if earlier is not None:
        operands += [earlier]
    in_specs = [smem] * 3 + [vmem] * (len(operands) - 3)
    for array in after:
        operands += [array]
        in_specs += [pl.BlockSpec(memory_space=pl.ANY)]
    if last:
        out_shape = [
            jax.ShapeDtypeStruct((seq_count // 2, lat, rows), jnp.float32),
            jax.ShapeDtypeStruct((seq_count // 2, lat, rows), jnp.bfloat16),
        ]
    else:
        out_shape = [jax.ShapeDtypeStruct((seq_count, lat, rows), jnp.float32)]
    return pl.pallas_call(
        functools.partial(
            attend_kernel, seq_count, heads, near_piece, far_pieces, lat, order, last, earlier is not None
        ),
        in_specs=in_specs,
        out_specs=[vmem] * len(out_shape),
        out_shape=out_shape,
        scratch_shapes=[pltpu.VMEM((seq_count, count, rows, HD), jnp.bfloat16)],
        compiler_params=pltpu.CompilerParams(vmem_limit_bytes=VMEM_LIMIT),
        cost_estimate=pl.CostEstimate(
            flops=count * tokens * tokens * 2 * (HD + lat),
            bytes_accessed=tokens * count * 3 * HD * 2,
            transcendentals=count * tokens * tokens,
        ),
        name="attend",
    )(*operands)


def swap(array, axis, offset):
    size = lax.axis_size(axis)
    return lax.ppermute(array, axis, [(i, i ^ offset) for i in range(size)])


def body(qkv, readout, step_weight, timestep, span_frames):
    seq_count = lax.axis_size("seq")
    mp_count = lax.axis_size("mp")
    heads_local = HEADS // seq_count
    lat = readout.shape[2]
    me = lax.axis_index("seq").astype(jnp.int32)
    mp_index = lax.axis_index("mp")
    sample_count = mp_count // 2
    model_index = (mp_index // sample_count).astype(jnp.int32)
    sample_index = mp_index % sample_count
    signed = jnp.where(model_index == 1, 1.0, -1.0).astype(jnp.float32)
    factor = (signed * step_weight[timestep[sample_index]]).reshape(1)
    readout_t = jnp.swapaxes(readout, 1, 2)
    place = jnp.stack([me, model_index])
    bits = seq_count.bit_length() - 1
    order = [sum(((n >> b) & 1) << (bits - 1 - b) for b in range(bits)) for n in range(seq_count)]
    half = seq_count // 2
    every = list(range(heads_local))
    chunks = [[0,1,2],[3]] if heads_local > 1 else [[0]]
    near_piece = layout(every, every, lat)
    far_pieces = [layout(heads, every if c == 0 else [], lat) for c, heads in enumerate(chunks)]

    def send(k, piece, after):
        packed = pack(place, qkv, readout_t, k, heads_local, piece, after)
        return packed, (swap(packed, "seq", k) if k else packed)

    far = [[None] * half for _ in chunks]
    near = [None] * half
    holds = [[] for _ in chunks]
    gates = [None, None]
    for c in range(len(chunks)):
        for n in range(half):
            k = seq_count - 1 - n
            packed, far[c][k - half] = send(k, far_pieces[c], gates[n % 2])
            if c:
                holds[c - 1].append(packed)
            else:
                gates[n % 2] = far[c][k - half]
        if c:
            gates = [far[c][1 % half], far[c][0]]
    for k in range(half):
        _, near[k] = send(k, near_piece, None)

    result = None
    for c, heads in enumerate(chunks):
        last = c == len(chunks) - 1
        result = attend(
            near, far[: c + 1], result, holds[c], span_frames, factor, me.reshape(1),
            heads, near_piece, far_pieces[: c + 1], lat, order, last,
        )
        if not last:
            result = result[0]
    keep, give = result
    keep = keep + swap(give, "seq", 1).astype(jnp.float32)
    offset = 2
    while offset < seq_count:
        radix = min(4, seq_count // offset)
        size = keep.shape[0] // radix
        parts = [keep[n * size : (n + 1) * size] for n in range(radix)]
        keep = parts[0]
        for n in range(radix - 1, 0, -1):
            bits_n = (n >> 1) | ((n & 1) << 1) if radix == 4 else n
            keep = keep + swap(parts[n], "seq", offset * bits_n)
        offset *= radix
    whole = keep[0]
    offset = 1
    while offset < mp_count:
        radix = min(4, mp_count // offset)
        own = whole
        for n in range(radix - 1, 0, -1):
            whole = whole + swap(own, "mp", offset * n)
        offset *= radix
    return whole.T


def solution(mesh):
    return jax.shard_map(
        body,
        mesh=mesh,
        in_specs=(P("mp", "seq", None), P(), P(), P(), P()),
        out_specs=P("seq", None),
        check_vma=False,
    )
```

time: 118 us -> 93.7 us (0.79)
  waiting for transfers between devices: 43.3 us -> 16.4 us
  starting transfers between devices: 36.7 us -> 41 us
  Pallas kernels: 28.3 us -> 26.2 us
    ppermute x19 -> x18, waiting for transfers between devices: 43.3 us -> 16.4 us  [swap(): return lax.ppermute(array, axis, [(i, i ^ offset) for i in range(size)])]
    ppermute x19 -> x18, starting transfers between devices: 36.7 us -> 41 us  [swap(): return lax.ppermute(array, axis, [(i, i ^ offset) for i in range(size)])]
    pallas_call x18 -> x14, Pallas kernels: 28.3 us -> 26.2 us  [the longest x2 14.2 us: attend(): pl.pallas_call(functools.partial(attend_kernel, seq_count, heads, near_pi...]
    unnamed x24 -> x20, local copies, waits for them, and re-layouts: 3.99 us -> 4.36 us
  transfers between devices with their start and end apart: 19 -> 18, of which waited for: 10 -> 7; matrix products, arithmetic and copies ran while one was open for 2% -> 2% of each run, Pallas kernels for 13% -> 23%
where the time goes in v5:
time: 93.7 us; the launch traced here: 93.3 us
  starting transfers between devices  41 us (44%)
  Pallas kernels  26.2 us (28%)
  waiting for transfers between devices  16.4 us (18%)
  local copies, waits for them, and re-layouts  6.23 us (7%)
  between operations  2.81 us (3%)
    ppermute x18, starting transfers between devices, swap(): return lax.ppermute(array, axis, [(i, i ^ offset) for i in range(size)])  41 us
    ppermute x18, waiting for transfers between devices, swap(): return lax.ppermute(array, axis, [(i, i ^ offset) for i in range(size)])  16.4 us
    pallas_call x2, Pallas kernels, attend(): pl.pallas_call(functools.partial(attend_kernel, seq_count, heads, near_pi...  14.2 us
    pallas_call x12, Pallas kernels, pack(): pl.pallas_call(functools.partial(pack_kernel, scores, values), grid_spec=...  12 us
    unnamed x20, local copies, waits for them, and re-layouts  4.36 us
  transfers between devices with their start and end apart: 18, of which 7 were waited for; matrix products, arithmetic and copies ran while one was open for 2% of the time, Pallas kernels for 23%

profile of v5, /device:TPU:0, one launch (start us, length us, event | category | flops | bytes accessed | tf_op | source)
XLA Modules:
  0.0 93.3 jit_solution(9882105052596810627)
XLA Ops:
  0.0 0.1 pad_add_fusion.place_ref
  0.1 1.9 %copy-done = bf16[1,128,12288]{2,1,0:T(8,128)(2,1)S(1)} copy-done((bf16[1,128,12288]{2,1,0:T(8,128)(2,1)S(1)}, bf16[1,128,12288]{2,1,0:T(8,128)(2,1)}, u32[]{:S(2)}) %copy-start) | copy-done | bytes 3145752
  2.0 1.2 %copy-done.2 = bf16[2,4096,64]{1,2,0:T(8,128)(2,1)S(1)} copy-done((bf16[2,4096,64]{1,2,0:T(8,128)(2,1)S(1)}, bf16[2,4096,64]{1,2,0:T(8,128)(2,1)}, u32[]{:S(2)}) %copy-start.2) | copy-done | bytes 1048600
  3.2 0.8 pack.18
  4.0 6.0 %collective-permute-start.5 = (bf16[128,1024]{1,0:T(8,128)(2,1)S(1)}, bf16[128,1024]{1,0:T(8,128)(2,1)S(1)}, u32[]{:S(2)}, u32[]{:S(2)}) collective-permute-start(bf16[128,1024]{1,0:T(8,128)(2,1)S(1)} %pack.18), channel_id=1, source_target_pairs={{0,28},{4,24},{8,20},{12,16},{16,12},{20,8},{24,4},{28,0},{1,29},{... | collective-permute-start | bytes 786440 | tf_op jit(solution)/shard_map/ppermute | solution.py:201
  10.0 0.8 pack.16
  10.8 0.3 collective-permute-start.3
  11.1 1.5 %pack.13 = bf16[128,1280]{1,0:T(8,128)(2,1)} custom-call(s32[2]{0:T(128)S(1)} %pad_add_fusion.place_ref, bf16[1,128,12288]{2,1,0:T(8,128)(2,1)S(1)} %copy-done, bf16[2,64,4096]{2,1,0:T(8,128)(2,1)S(1)} %bitcast.12), custom_call_target="tpu_custom_call" | custom-call | flops 8388608 | bytes 655360 | tf_op jit(solution)/shard_map/pack/pallas_call | solution.py:49
  12.6 0.3 collective-permute-start
  12.9 1.5 %pack.14 = bf16[128,1280]{1,0:T(8,128)(2,1)} custom-call(s32[2]{0:T(128)S(1)} %pad_add_fusion.place_ref, bf16[1,128,12288]{2,1,0:T(8,128)(2,1)S(1)} %copy-done, bf16[2,64,4096]{2,1,0:T(8,128)(2,1)S(1)} %bitcast.13), custom_call_target="tpu_custom_call" | custom-call | flops 8388608 | bytes 655360 | tf_op jit(solution)/shard_map/pack/pallas_call | solution.py:49
  14.4 0.0 collective-permute-start.1
  14.4 1.5 %pack.15 = bf16[128,1280]{1,0:T(8,128)(2,1)} custom-call(s32[2]{0:T(128)S(1)} %pad_add_fusion.place_ref, bf16[1,128,12288]{2,1,0:T(8,128)(2,1)S(1)} %copy-done, bf16[2,64,4096]{2,1,0:T(8,128)(2,1)S(1)} %bitcast.14), custom_call_target="tpu_custom_call" | custom-call | flops 8388608 | bytes 655360 | tf_op jit(solution)/shard_map/pack/pallas_call | solution.py:49
  15.9 3.1 %collective-permute-start.2 = (bf16[128,1280]{1,0:T(8,128)(2,1)}, bf16[128,1280]{1,0:T(8,128)(2,1)}, u32[]{:S(2)}, u32[]{:S(2)}) collective-permute-start(bf16[128,1280]{1,0:T(8,128)(2,1)} %pack.15), channel_id=1, source_target_pairs={{0,12},{4,8},{8,4},{12,0},{16,28},{20,24},{24,20},{28,16},{1,13},{... | collective-permute-start | bytes 983048 | tf_op jit(solution)/shard_map/ppermute | solution.py:201
  19.1 0.0 collective-permute-done.5.refs_0_.refs_7_
  19.1 1.5 %pack.19 = bf16[128,1024]{1,0:T(8,128)(2,1)} custom-call(s32[2]{0:T(128)S(1)} %pad_add_fusion.place_ref, bf16[1,128,12288]{2,1,0:T(8,128)(2,1)S(1)} %copy-done, bf16[2,64,4096]{2,1,0:T(8,128)(2,1)S(1)} %bitcast.15, bf16[128,1024]{1,0:T(8,128)(2,1)S(1)} %collective-permute-done.5.refs_0_.refs_7_), custom_call_target="tpu_custom_call" | custom-call | flops 8388608 | bytes 524288 | tf_op jit(solution)/shard_map/pack/pallas_call | solution.py:49
  20.6 11.3 %collective-permute-start.6 = (bf16[128,1024]{1,0:T(8,128)(2,1)}, bf16[128,1024]{1,0:T(8,128)(2,1)S(1)}, u32[]{:S(2)}, u32[]{:S(2)}) collective-permute-start(bf16[128,1024]{1,0:T(8,128)(2,1)} %pack.19), channel_id=1, source_target_pairs={{0,20},{4,16},{8,28},{12,24},{16,4},{20,0},{24,12},{28,8},{1,21},{... | collective-permute-start | bytes 786440 | tf_op jit(solution)/shard_map/ppermute | solution.py:201
  31.8 1.5 %pack.17 = bf16[128,1024]{1,0:T(8,128)(2,1)} custom-call(s32[2]{0:T(128)S(1)} %pad_add_fusion.place_ref, bf16[1,128,12288]{2,1,0:T(8,128)(2,1)S(1)} %copy-done, bf16[2,64,4096]{2,1,0:T(8,128)(2,1)S(1)} %bitcast.16, bf16[128,1024]{1,0:T(8,128)(2,1)S(1)} %collective-permute-done.3.refs_0_.refs_6_), custom_call_target="tpu_custom_call" | custom-call | flops 8388608 | bytes 524288 | tf_op jit(solution)/shard_map/pack/pallas_call | solution.py:49
  33.3 3.2 %collective-permute-start.4 = (bf16[128,1024]{1,0:T(8,128)(2,1)}, bf16[128,1024]{1,0:T(8,128)(2,1)}, u32[]{:S(2)}, u32[]{:S(2)}) collective-permute-start(bf16[128,1024]{1,0:T(8,128)(2,1)} %pack.17), channel_id=1, source_target_pairs={{0,16},{4,20},{8,24},{12,28},{16,0},{20,4},{24,8},{28,12},{1,17},{... | collective-permute-start | bytes 786440 | tf_op jit(solution)/shard_map/ppermute | solution.py:201
  36.5 0.6 dynamic_slice.6
  39.0 1.3 %dynamic_slice.7 = f32[1]{0:T(128)} dynamic-slice(f32[1000]{0:T(1024)} %param.7, s32[]{:T(128)S(6)} %select_n.25), dynamic_slice_sizes={1} | dynamic-slice | bytes 12 | tf_op jit(solution)/shard_map/dynamic_slice | solution.py:215
  41.0 0.0 copy-start.3
  41.0 1.2 %copy-done.3 = bf16[2,4096,64]{1,2,0:T(8,128)(2,1)S(1)} copy-done((bf16[2,4096,64]{1,2,0:T(8,128)(2,1)S(1)}, bf16[2,4096,64]{1,2,0:T(8,128)(2,1)}, u32[]{:S(2)}) %copy-start.3) | copy-done | bytes 1048600
  42.2 0.8 pack.12.refs_0_
  43.0 8.2 %collective-permute-done.6.refs_0_.refs_5_ = bf16[128,1024]{1,0:T(8,128)(2,1)S(1)} collective-permute-done((bf16[128,1024]{1,0:T(8,128)(2,1)}, bf16[128,1024]{1,0:T(8,128)(2,1)S(1)}, u32[]{:S(2)}, u32[]{:S(2)}) %collective-permute-start.6) | collective-permute-done | bytes 262176 | tf_op jit(solution)/shard_map/ppermute | solution.py:201
  51.2 0.6 pack.23.refs_8_
  51.8 3.3 %collective-permute-start.10 = (bf16[128,256]{1,0:T(8,128)(2,1)S(1)}, bf16[128,256]{1,0:T(8,128)(2,1)S(1)}, u32[]{:S(2)}, u32[]{:S(2)}) collective-permute-start(bf16[128,256]{1,0:T(8,128)(2,1)S(1)} %pack.23.refs_8_), channel_id=1, source_target_pairs={{0,28},{4,24},{8,20},{12,16},{16,12},{20,8},{24,4},{28,0},{1,29},{... | collective-permute-start | bytes 196616 | tf_op jit(solution)/shard_map/ppermute | solution.py:201
  55.1 1.3 %collective-permute-done.4.refs_0_.refs_4_ = bf16[128,1024]{1,0:T(8,128)(2,1)} collective-permute-done((bf16[128,1024]{1,0:T(8,128)(2,1)}, bf16[128,1024]{1,0:T(8,128)(2,1)}, u32[]{:S(2)}, u32[]{:S(2)}) %collective-permute-start.4) | collective-permute-done | bytes 262176 | tf_op jit(solution)/shard_map/ppermute | solution.py:201
  56.3 0.6 pack.20.refs_11_
  56.9 0.1 collective-permute-start.7
  57.0 0.6 pack.21.refs_10_
  57.6 0.0 copy-start.8
  57.6 0.6 pack.22.refs_9_
  58.2 2.9 %collective-permute-start.8 = (bf16[128,256]{1,0:T(8,128)(2,1)S(1)}, bf16[128,256]{1,0:T(8,128)(2,1)S(1)}, u32[]{:S(2)}, u32[]{:S(2)}) collective-permute-start(bf16[128,256]{1,0:T(8,128)(2,1)S(1)} %pack.21.refs_10_), channel_id=1, source_target_pairs={{0,20},{4,16},{8,28},{12,24},{16,4},{20,0},{24,12},{28,8},{1,21},{... | collective-permute-start | bytes 196616 | tf_op jit(solution)/shard_map/ppermute | solution.py:201
  61.1 2.5 %collective-permute-start.9 = (bf16[128,256]{1,0:T(8,128)(2,1)S(1)}, bf16[128,256]{1,0:T(8,128)(2,1)S(1)}, u32[]{:S(2)}, u32[]{:S(2)}) collective-permute-start(bf16[128,256]{1,0:T(8,128)(2,1)S(1)} %pack.22.refs_9_), channel_id=1, source_target_pairs={{0,24},{4,28},{8,16},{12,20},{16,8},{20,12},{24,0},{28,4},{1,25},{... | collective-permute-start | bytes 196616 | tf_op jit(solution)/shard_map/ppermute | solution.py:201
  63.6 9.9 %attend.2.refs_12_ = f32[8,64,128]{2,1,0:T(8,128)S(1)} custom-call(s32[4]{0:T(128)S(1)} %copy-done.8, f32[1]{0:T(128)} %bitcast.2.factor_ref, s32[1]{0:T(128)} %bitcast.3.me_ref, bf16[128,1280]{1,0:T(8,128)(2,1)S(1)} %pack.12.refs_0_, bf16[128,1280]{1,0:T(8,128)(2,1)} %collective-permute-done.refs_1_, bf16[128,1280]{1,0:T(8,128)(2,1)} %collective-permute-done.1.refs_2_, ...), custom_call_target="tpu_custom_call" | custom-call | flops 1207959552 | bytes 2359296 | tf_op jit(solution)/shard_map/attend/pallas_call | solution.py:181
  73.5 4.3 %attend.3 = (f32[4,64,128]{2,1,0:T(8,128)S(1)}, bf16[4,64,128]{2,1,0:T(8,128)(2,1)S(1)}) custom-call(s32[4]{0:T(128)S(1)} %copy-done.8, f32[1]{0:T(128)} %bitcast.2.factor_ref, s32[1]{0:T(128)} %bitcast.3.me_ref, bf16[128,1280]{1,0:T(8,128)(2,1)S(1)} %pack.12.refs_0_, bf16[128,1280]{1,0:T(8,128)(2,1)} %collective-permute-done.refs_1_, ...), custom_call_target="tpu_custom_call" | custom-call | flops 402653184 | bytes 786432 | tf_op jit(solution)/shard_map/attend/pallas_call | solution.py:181
  77.9 1.6 %collective-permute-start.11 = (bf16[4,64,128]{2,1,0:T(8,128)(2,1)S(1)}, bf16[4,64,128]{2,1,0:T(8,128)(2,1)S(1)}, u32[]{:S(2)}, u32[]{:S(2)}) collective-permute-start(bf16[4,64,128]{2,1,0:T(8,128)(2,1)S(1)} %get-tuple-element.8), channel_id=1, source_target_pairs={{0,4},{4,0},{8,12},{12,8},{16,20},{20,16},{24,28},{28,24},{1,5},{5... | collective-permute-start | bytes 196616 | tf_op jit(solution)/shard_map/ppermute | solution.py:201
  79.4 2.8 %collective-permute-done.11 = bf16[4,64,128]{2,1,0:T(8,128)(2,1)S(1)} collective-permute-done((bf16[4,64,128]{2,1,0:T(8,128)(2,1)S(1)}, bf16[4,64,128]{2,1,0:T(8,128)(2,1)S(1)}, u32[]{:S(2)}, u32[]{:S(2)}) %collective-permute-start.11) | collective-permute-done | bytes 65568 | tf_op jit(solution)/shard_map/ppermute | solution.py:201
  82.2 1.4 %collective-permute-start.12 = (f32[1,64,128]{2,1,0:T(8,128)S(1)}, f32[1,64,128]{2,1,0:T(8,128)S(1)}, u32[]{:S(2)}, u32[]{:S(2)}) collective-permute-start(f32[1,64,128]{2,1,0:T(8,128)S(1)} %get-tuple-element.9), channel_id=1, source_target_pairs={{0,24},{4,28},{8,16},{12,20},{16,8},{20,12},{24,0},{28,4},{1,25},{... | collective-permute-start | bytes 98312 | tf_op jit(solution)/shard_map/ppermute | solution.py:201
  83.7 3.0 %collective-permute-start.14 = (f32[1,64,128]{2,1,0:T(8,128)S(1)}, f32[1,64,128]{2,1,0:T(8,128)S(1)}, u32[]{:S(2)}, u32[]{:S(2)}) collective-permute-start(f32[1,64,128]{2,1,0:T(8,128)S(1)} %get-tuple-element.10), channel_id=1, source_target_pairs={{0,16},{4,20},{8,24},{12,28},{16,0},{20,4},{24,8},{28,12},{1,17},{... | collective-permute-start | bytes 98312 | tf_op jit(solution)/shard_map/ppermute | solution.py:201
  86.7 1.3 %collective-permute-done.12 = f32[1,64,128]{2,1,0:T(8,128)S(1)} collective-permute-done((f32[1,64,128]{2,1,0:T(8,128)S(1)}, f32[1,64,128]{2,1,0:T(8,128)S(1)}, u32[]{:S(2)}, u32[]{:S(2)}) %collective-permute-start.12) | collective-permute-done | bytes 32800 | tf_op jit(solution)/shard_map/ppermute | solution.py:201
  88.0 0.6 collective-permute-done.14
  88.6 0.1 collective-permute-start.15
  88.7 1.6 %collective-permute-start.16 = (f32[64,128]{1,0:T(8,128)S(1)}, f32[64,128]{1,0:T(8,128)S(1)}, u32[]{:S(2)}, u32[]{:S(2)}) collective-permute-start(f32[64,128]{1,0:T(8,128)S(1)} %fusion.2), channel_id=1, source_target_pairs={{0,2},{1,3},{2,0},{3,1},{4,6},{5,7},{6,4},{7,5},{8,10},{9,11},{10,... | collective-permute-start | bytes 98312 | tf_op jit(solution)/shard_map/ppermute | solution.py:201
  90.3 0.3 collective-permute-start.17
  90.5 1.8 %collective-permute-done.15 = f32[64,128]{1,0:T(8,128)S(1)} collective-permute-done((f32[64,128]{1,0:T(8,128)S(1)}, f32[64,128]{1,0:T(8,128)S(1)}, u32[]{:S(2)}, u32[]{:S(2)}) %collective-permute-start.15) | collective-permute-done | bytes 32800 | tf_op jit(solution)/shard_map/ppermute | solution.py:201
  92.3 0.4 collective-permute-done.16
  92.7 0.6 add_bitcast_fusion
  (29 shorter events, 0.1 us)
Async XLA Ops:
  0.1 1.9 %copy-start = (bf16[1,128,12288]{2,1,0:T(8,128)(2,1)S(1)}, bf16[1,128,12288]{2,1,0:T(8,128)(2,1)}, u32[]{:S(2)}) copy-start(bf16[1,128,12288]{2,1,0:T(8,128)(2,1)} %qkv_ref.23) | copy-start | bytes 9437188
  2.0 1.2 %copy-start.2 = (bf16[2,4096,64]{1,2,0:T(8,128)(2,1)S(1)}, bf16[2,4096,64]{1,2,0:T(8,128)(2,1)}, u32[]{:S(2)}) copy-start(bf16[2,4096,64]{1,2,0:T(8,128)(2,1)} %param.6) | copy-start | bytes 3145732
  4.0 15.1 %collective-permute-start.5 = (bf16[128,1024]{1,0:T(8,128)(2,1)S(1)}, bf16[128,1024]{1,0:T(8,128)(2,1)S(1)}, u32[]{:S(2)}, u32[]{:S(2)}) collective-permute-start(bf16[128,1024]{1,0:T(8,128)(2,1)S(1)} %pack.18), channel_id=1, source_target_pairs={{0,28},{4,24},{8,20},{12,16},{16,12},{20,8},{24,4},{28,0},{1,29},{... | collective-permute-start | bytes 786440 | tf_op jit(solution)/shard_map/ppermute | solution.py:201
  10.8 21.0 %collective-permute-start.3 = (bf16[128,1024]{1,0:T(8,128)(2,1)S(1)}, bf16[128,1024]{1,0:T(8,128)(2,1)S(1)}, u32[]{:S(2)}, u32[]{:S(2)}) collective-permute-start(bf16[128,1024]{1,0:T(8,128)(2,1)S(1)} %pack.16), channel_id=1, source_target_pairs={{0,24},{4,28},{8,16},{12,20},{16,8},{20,12},{24,0},{28,4},{1,25},{... | collective-permute-start | bytes 786440 | tf_op jit(solution)/shard_map/ppermute | solution.py:201
  12.6 45.6 %collective-permute-start = (bf16[128,1280]{1,0:T(8,128)(2,1)}, bf16[128,1280]{1,0:T(8,128)(2,1)}, u32[]{:S(2)}, u32[]{:S(2)}) collective-permute-start(bf16[128,1280]{1,0:T(8,128)(2,1)} %pack.13), channel_id=1, source_target_pairs={{0,4},{4,0},{8,12},{12,8},{16,20},{20,16},{24,28},{28,24},{1,5},{5... | collective-permute-start | bytes 983048 | tf_op jit(solution)/shard_map/ppermute | solution.py:201
  14.4 46.7 %collective-permute-start.1 = (bf16[128,1280]{1,0:T(8,128)(2,1)}, bf16[128,1280]{1,0:T(8,128)(2,1)}, u32[]{:S(2)}, u32[]{:S(2)}) collective-permute-start(bf16[128,1280]{1,0:T(8,128)(2,1)} %pack.14), channel_id=1, source_target_pairs={{0,8},{4,12},{8,0},{12,4},{16,24},{20,28},{24,16},{28,20},{1,9},{5... | collective-permute-start | bytes 983048 | tf_op jit(solution)/shard_map/ppermute | solution.py:201
  15.9 47.6 %collective-permute-start.2 = (bf16[128,1280]{1,0:T(8,128)(2,1)}, bf16[128,1280]{1,0:T(8,128)(2,1)}, u32[]{:S(2)}, u32[]{:S(2)}) collective-permute-start(bf16[128,1280]{1,0:T(8,128)(2,1)} %pack.15), channel_id=1, source_target_pairs={{0,12},{4,8},{8,4},{12,0},{16,28},{20,24},{24,20},{28,16},{1,13},{... | collective-permute-start | bytes 983048 | tf_op jit(solution)/shard_map/ppermute | solution.py:201
  19.1 14.2 %copy-start.4 = (bf16[128,1024]{1,0:T(8,128)(2,1)}, bf16[128,1024]{1,0:T(8,128)(2,1)S(1)}, u32[]{:S(2)}) copy-start(bf16[128,1024]{1,0:T(8,128)(2,1)S(1)} %collective-permute-done.5.refs_0_.refs_7_) | copy-start | bytes 786436
  20.5 16.0 %copy-start.9 = (s32[2]{0:T(128)S(1)}, s32[2]{0:T(128)}, u32[]{:S(2)}) copy-start(s32[2]{0:T(128)} %param.8) | copy-start | bytes 28
  20.5 20.4 %copy-start.1 = (bf16[1,128,12288]{2,1,0:T(8,128)(2,1)S(1)}, bf16[1,128,12288]{2,1,0:T(8,128)(2,1)}, u32[]{:S(2)}) copy-start(bf16[1,128,12288]{2,1,0:T(8,128)(2,1)} %qkv_ref.23) | copy-start | bytes 9437188
  20.6 30.7 %collective-permute-start.6 = (bf16[128,1024]{1,0:T(8,128)(2,1)}, bf16[128,1024]{1,0:T(8,128)(2,1)S(1)}, u32[]{:S(2)}, u32[]{:S(2)}) collective-permute-start(bf16[128,1024]{1,0:T(8,128)(2,1)} %pack.19), channel_id=1, source_target_pairs={{0,20},{4,16},{8,28},{12,24},{16,4},{20,0},{24,12},{28,8},{1,21},{... | collective-permute-start | bytes 786440 | tf_op jit(solution)/shard_map/ppermute | solution.py:201
  31.8 1.5 %copy-start.6 = (bf16[128,1024]{1,0:T(8,128)(2,1)}, bf16[128,1024]{1,0:T(8,128)(2,1)S(1)}, u32[]{:S(2)}) copy-start(bf16[128,1024]{1,0:T(8,128)(2,1)S(1)} %collective-permute-done.3.refs_0_.refs_6_) | copy-start | bytes 786436
  33.3 23.1 %collective-permute-start.4 = (bf16[128,1024]{1,0:T(8,128)(2,1)}, bf16[128,1024]{1,0:T(8,128)(2,1)}, u32[]{:S(2)}, u32[]{:S(2)}) collective-permute-start(bf16[128,1024]{1,0:T(8,128)(2,1)} %pack.17), channel_id=1, source_target_pairs={{0,16},{4,20},{8,24},{12,28},{16,0},{20,4},{24,8},{28,12},{1,17},{... | collective-permute-start | bytes 786440 | tf_op jit(solution)/shard_map/ppermute | solution.py:201
  41.0 1.2 %copy-start.3 = (bf16[2,4096,64]{1,2,0:T(8,128)(2,1)S(1)}, bf16[2,4096,64]{1,2,0:T(8,128)(2,1)}, u32[]{:S(2)}) copy-start(bf16[2,4096,64]{1,2,0:T(8,128)(2,1)} %param.6) | copy-start | bytes 3145732
  51.8 21.7 %collective-permute-start.10 = (bf16[128,256]{1,0:T(8,128)(2,1)S(1)}, bf16[128,256]{1,0:T(8,128)(2,1)S(1)}, u32[]{:S(2)}, u32[]{:S(2)}) collective-permute-start(bf16[128,256]{1,0:T(8,128)(2,1)S(1)} %pack.23.refs_8_), channel_id=1, source_target_pairs={{0,28},{4,24},{8,20},{12,16},{16,12},{20,8},{24,4},{28,0},{1,29},{... | collective-permute-start | bytes 196616 | tf_op jit(solution)/shard_map/ppermute | solution.py:201
  56.9 16.6 %collective-permute-start.7 = (bf16[128,256]{1,0:T(8,128)(2,1)S(1)}, bf16[128,256]{1,0:T(8,128)(2,1)S(1)}, u32[]{:S(2)}, u32[]{:S(2)}) collective-permute-start(bf16[128,256]{1,0:T(8,128)(2,1)S(1)} %pack.20.refs_11_), channel_id=1, source_target_pairs={{0,16},{4,20},{8,24},{12,28},{16,0},{20,4},{24,8},{28,12},{1,17},{... | collective-permute-start | bytes 196616 | tf_op jit(solution)/shard_map/ppermute | solution.py:201
  57.6 6.0 %copy-start.5 = (bf16[128,1024]{1,0:T(8,128)(2,1)S(1)}, bf16[128,1024]{1,0:T(8,128)(2,1)}, u32[]{:S(2)}) copy-start(bf16[128,1024]{1,0:T(8,128)(2,1)} %copy-done.4) | copy-start | bytes 786436
  57.6 6.0 %copy-start.7 = (bf16[128,1024]{1,0:T(8,128)(2,1)S(1)}, bf16[128,1024]{1,0:T(8,128)(2,1)}, u32[]{:S(2)}) copy-start(bf16[128,1024]{1,0:T(8,128)(2,1)} %copy-done.6) | copy-start | bytes 786436
  57.6 6.0 %copy-start.8 = (s32[4]{0:T(128)S(1)}, s32[4]{0:T(128)}, u32[]{:S(2)}) copy-start(s32[4]{0:T(128)} %frames_ref.3) | copy-start | bytes 52
  58.2 15.4 %collective-permute-start.8 = (bf16[128,256]{1,0:T(8,128)(2,1)S(1)}, bf16[128,256]{1,0:T(8,128)(2,1)S(1)}, u32[]{:S(2)}, u32[]{:S(2)}) collective-permute-start(bf16[128,256]{1,0:T(8,128)(2,1)S(1)} %pack.21.refs_10_), channel_id=1, source_target_pairs={{0,20},{4,16},{8,28},{12,24},{16,4},{20,0},{24,12},{28,8},{1,21},{... | collective-permute-start | bytes 196616 | tf_op jit(solution)/shard_map/ppermute | solution.py:201
  61.1 12.4 %collective-permute-start.9 = (bf16[128,256]{1,0:T(8,128)(2,1)S(1)}, bf16[128,256]{1,0:T(8,128)(2,1)S(1)}, u32[]{:S(2)}, u32[]{:S(2)}) collective-permute-start(bf16[128,256]{1,0:T(8,128)(2,1)S(1)} %pack.22.refs_9_), channel_id=1, source_target_pairs={{0,24},{4,28},{8,16},{12,20},{16,8},{20,12},{24,0},{28,4},{1,25},{... | collective-permute-start | bytes 196616 | tf_op jit(solution)/shard_map/ppermute | solution.py:201
  77.9 4.3 %collective-permute-start.11 = (bf16[4,64,128]{2,1,0:T(8,128)(2,1)S(1)}, bf16[4,64,128]{2,1,0:T(8,128)(2,1)S(1)}, u32[]{:S(2)}, u32[]{:S(2)}) collective-permute-start(bf16[4,64,128]{2,1,0:T(8,128)(2,1)S(1)} %get-tuple-element.8), channel_id=1, source_target_pairs={{0,4},{4,0},{8,12},{12,8},{16,20},{20,16},{24,28},{28,24},{1,5},{5... | collective-permute-start | bytes 196616 | tf_op jit(solution)/shard_map/ppermute | solution.py:201
  82.2 5.8 %collective-permute-start.12 = (f32[1,64,128]{2,1,0:T(8,128)S(1)}, f32[1,64,128]{2,1,0:T(8,128)S(1)}, u32[]{:S(2)}, u32[]{:S(2)}) collective-permute-start(f32[1,64,128]{2,1,0:T(8,128)S(1)} %get-tuple-element.9), channel_id=1, source_target_pairs={{0,24},{4,28},{8,16},{12,20},{16,8},{20,12},{24,0},{28,4},{1,25},{... | collective-permute-start | bytes 98312 | tf_op jit(solution)/shard_map/ppermute | solution.py:201
  83.7 4.4 %collective-permute-start.13 = (f32[1,64,128]{2,1,0:T(8,128)S(1)}, f32[1,64,128]{2,1,0:T(8,128)S(1)}, u32[]{:S(2)}, u32[]{:S(2)}) collective-permute-start(f32[1,64,128]{2,1,0:T(8,128)S(1)} %get-tuple-element.11), channel_id=1, source_target_pairs={{0,8},{4,12},{8,0},{12,4},{16,24},{20,28},{24,16},{28,20},{1,9},{5... | collective-permute-start | bytes 98312 | tf_op jit(solution)/shard_map/ppermute | solution.py:201
  83.7 4.9 %collective-permute-start.14 = (f32[1,64,128]{2,1,0:T(8,128)S(1)}, f32[1,64,128]{2,1,0:T(8,128)S(1)}, u32[]{:S(2)}, u32[]{:S(2)}) collective-permute-start(f32[1,64,128]{2,1,0:T(8,128)S(1)} %get-tuple-element.10), channel_id=1, source_target_pairs={{0,16},{4,20},{8,24},{12,28},{16,0},{20,4},{24,8},{28,12},{1,17},{... | collective-permute-start | bytes 98312 | tf_op jit(solution)/shard_map/ppermute | solution.py:201
  88.6 3.7 %collective-permute-start.15 = (f32[64,128]{1,0:T(8,128)S(1)}, f32[64,128]{1,0:T(8,128)S(1)}, u32[]{:S(2)}, u32[]{:S(2)}) collective-permute-start(f32[64,128]{1,0:T(8,128)S(1)} %fusion.2), channel_id=1, source_target_pairs={{0,3},{1,2},{2,1},{3,0},{4,7},{5,6},{6,5},{7,4},{8,11},{9,10},{10,... | collective-permute-start | bytes 98312 | tf_op jit(solution)/shard_map/ppermute | solution.py:201
  88.7 4.0 %collective-permute-start.16 = (f32[64,128]{1,0:T(8,128)S(1)}, f32[64,128]{1,0:T(8,128)S(1)}, u32[]{:S(2)}, u32[]{:S(2)}) collective-permute-start(f32[64,128]{1,0:T(8,128)S(1)} %fusion.2), channel_id=1, source_target_pairs={{0,2},{1,3},{2,0},{3,1},{4,6},{5,7},{6,4},{7,5},{8,10},{9,11},{10,... | collective-permute-start | bytes 98312 | tf_op jit(solution)/shard_map/ppermute | solution.py:201
  90.3 2.4 %collective-permute-start.17 = (f32[64,128]{1,0:T(8,128)S(1)}, f32[64,128]{1,0:T(8,128)S(1)}, u32[]{:S(2)}, u32[]{:S(2)}) collective-permute-start(f32[64,128]{1,0:T(8,128)S(1)} %fusion.2), channel_id=1, source_target_pairs={{0,1},{1,0},{2,3},{3,2},{4,5},{5,4},{6,7},{7,6},{8,9},{9,8},{10,11... | collective-permute-start | bytes 98312 | tf_op jit(solution)/shard_map/ppermute | solution.py:201

commit v6 on v5

--- a/solution.py
+++ b/solution.py
@@ -13,6 +13,7 @@
 FRAME_TOK = 64
 NT = (((1,), (1,)), ((), ()))
 VMEM_LIMIT = 32 * 1024 * 1024
+WHOLE_VMEM = 60 * 1024 * 1024
 
 
 def layout(score_heads, value_heads, lat):
@@ -34,7 +35,7 @@
         out_ref[row : row + lat, column : column + HD] = folded.astype(jnp.bfloat16)
 
 
-def pack(place, qkv, readout_t, k, heads_local, piece, after):
+def pack(place, qkv, readout_t, k, heads_local, piece, after, limit=VMEM_LIMIT):
     rows = qkv.shape[1]
     lat = readout_t.shape[1]
     scores, values, width = piece
@@ -55,7 +56,7 @@
             out_specs=pl.BlockSpec((rows, width), lambda g, m: (0, 0)),
         ),
         out_shape=jax.ShapeDtypeStruct((rows, width), jnp.bfloat16),
-        compiler_params=pltpu.CompilerParams(vmem_limit_bytes=VMEM_LIMIT),
+        compiler_params=pltpu.CompilerParams(vmem_limit_bytes=limit),
         cost_estimate=pl.CostEstimate(
             flops=2 * rows * lat * len(values) * HD, bytes_accessed=rows * width * 4, transcendentals=0
         ),
@@ -69,8 +70,8 @@
     near_refs, refs = refs[:half], refs[half:]
     far_refs, refs = refs[: half * len(far_pieces)], refs[half * len(far_pieces) :]
     earlier = refs[0] if later else None
-    out_refs = refs[-3:-1] if last else refs[-2:-1]
-    asked = refs[-1]
+    out_refs = refs[-4:-2] if last else refs[-3:-2]
+    asked, folded = refs[-2:]
     me = me_ref[0]
     rows = near_refs[0].shape[0]
 
@@ -91,22 +92,24 @@
                 row, column = values[h]
                 return ref[row : row + lat, column : column + HD]
 
-    tokens = seq_count * rows
     spans = frames_ref.shape[0]
     log2_scale = math.log2(math.e) / math.sqrt(HD)
+    reversed_bits = seq_count.bit_length() - 1
+    block = 2 * rows
 
     end = frames_ref[0] * FRAME_TOK
     ends = [end]
     for c in range(1, spans):
         end = end + frames_ref[c] * FRAME_TOK
         ends.append(end)
-    row_places = lax.broadcasted_iota(jnp.int32, (rows, 1), 0)
-    key_places = jnp.concatenate([(me ^ k) * rows + row_places for k in range(seq_count)], axis=0)
     column_places = lax.broadcasted_iota(jnp.int32, (1, rows), 1)
     for n, k in enumerate(order):
-        for i in range(count):
-            asked[n, i] = cell(k, heads[i], 0)
-    reversed_bits = seq_count.bit_length() - 1
+        for i, h in enumerate(heads):
+            asked[n, i] = cell(k, h, 0)
+    for i, h in enumerate(heads):
+        for k in range(seq_count):
+            folded[i, :lat, k * rows : (k + 1) * rows] = value(k, h)
+        folded[i, lat:] = jnp.ones_like(folded[i, lat:])
 
     def place_of(n):
         k = jnp.int32(0)
@@ -114,26 +117,31 @@
             k = k | (((n >> bit) & 1) << (reversed_bits - 1 - bit))
         return me ^ k
 
-    def one_block(b, carry):
+    def one_block(b):
         first = b * 2
         places = jnp.concatenate([place_of(first + j) * rows + column_places for j in range(2)], axis=1)
-        bound = jnp.full((1, 2 * rows), ends[0], jnp.int32)
+        bound = jnp.full((1, block), ends[0], jnp.int32)
         for c in range(1, spans):
             bound = jnp.where(places >= ends[c - 1], ends[c], bound)
-        allowed = key_places < bound
+        bias = [
+            jnp.where((me ^ k) * rows + start < bound, 0.0, -jnp.inf)
+            for k in range(seq_count)
+            for start in range(0, rows, FRAME_TOK)
+        ]
         total = None
-        for i in range(count):
-            queries = asked[pl.ds(first, 2), i].reshape(2 * rows, HD)
-            keys = jnp.concatenate([cell(k, heads[i], 1) for k in range(seq_count)], axis=0)
+        for i, h in enumerate(heads):
+            queries = asked[pl.ds(first, 2), i].reshape(block, HD)
+            keys = jnp.concatenate([cell(k, h, 1) for k in range(seq_count)], axis=0)
             scores = lax.dot_general(keys, queries, NT, preferred_element_type=jnp.float32)
-            scores = jnp.where(allowed, scores, -jnp.inf)
-            peak = jnp.max(scores, axis=0, keepdims=True)
-            raw = jnp.exp2((scores - peak) * log2_scale)
-            row_total = jnp.sum(raw, axis=0, keepdims=True)
-            weights = raw.astype(jnp.bfloat16)
-            folded = jnp.concatenate([value(k, heads[i]) for k in range(seq_count)], axis=1)
-            summed = jnp.dot(folded, weights, preferred_element_type=jnp.float32) / row_total
-            total = summed if total is None else total + summed
+            frames = [scores[g * FRAME_TOK : (g + 1) * FRAME_TOK] for g in range(len(bias))]
+            peaks = [jnp.max(f, axis=0, keepdims=True) + shift for f, shift in zip(frames, bias)]
+            peak = functools.reduce(jnp.maximum, peaks)
+            weights = [
+                jnp.exp2((f + (shift - peak)) * log2_scale).astype(jnp.bfloat16) for f, shift in zip(frames, bias)
+            ]
+            summed = jnp.dot(folded[i], jnp.concatenate(weights, axis=0), preferred_element_type=jnp.float32)
+            part = summed[:lat] / summed[lat : lat + 1]
+            total = part if total is None else total + part
         for j in range(2):
             part = total[:, j * rows : (j + 1) * rows]
             n = first + j
@@ -151,9 +159,15 @@
                     out_refs[1][n - half] = part.astype(jnp.bfloat16)
             else:
                 out_refs[0][n] = part
+
+    together = 2 if count == 1 and half % 2 == 0 else 1
+
+    def some_blocks(b, carry):
+        for j in range(together):
+            one_block(b * together + j)
         return carry
 
-    lax.fori_loop(0, half, one_block, 0)
+    lax.fori_loop(0, half // together, some_blocks, 0)
 
 
 def attend(near, far, earlier, after, span_frames, factor, me, heads, near_piece, far_pieces, lat, order, last):
@@ -185,7 +199,10 @@
         in_specs=in_specs,
         out_specs=[vmem] * len(out_shape),
         out_shape=out_shape,
-        scratch_shapes=[pltpu.VMEM((seq_count, count, rows, HD), jnp.bfloat16)],
+        scratch_shapes=[
+            pltpu.VMEM((seq_count, count, rows, HD), jnp.bfloat16),
+            pltpu.VMEM((count, lat + 16, tokens), jnp.bfloat16),
+        ],
         compiler_params=pltpu.CompilerParams(vmem_limit_bytes=VMEM_LIMIT),
         cost_estimate=pl.CostEstimate(
             flops=count * tokens * tokens * 2 * (HD + lat),
@@ -223,8 +240,8 @@
     near_piece = layout(every, every, lat)
     far_pieces = [layout(heads, every if c == 0 else [], lat) for c, heads in enumerate(chunks)]
 
-    def send(k, piece, after):
-        packed = pack(place, qkv, readout_t, k, heads_local, piece, after)
+    def send(k, piece, after, limit=VMEM_LIMIT):
+        packed = pack(place, qkv, readout_t, k, heads_local, piece, after, limit)
         return packed, (swap(packed, "seq", k) if k else packed)
 
     far = [[None] * half for _ in chunks]
@@ -234,7 +251,7 @@
     for c in range(len(chunks)):
         for n in range(half):
             k = seq_count - 1 - n
-            packed, far[c][k - half] = send(k, far_pieces[c], gates[n % 2])
+            packed, far[c][k - half] = send(k, far_pieces[c], gates[n % 2], VMEM_LIMIT if c or n else WHOLE_VMEM)
             if c:
                 holds[c - 1].append(packed)
             else:

time: 93.7 us -> 92.2 us (0.984)
  local copies, waits for them, and re-layouts: 6.23 us -> 4.34 us
  starting transfers between devices: 41 us -> 40 us
    pallas_call x12, Pallas kernels: 12 us -> 13.9 us  [pack(): pl.pallas_call(functools.partial(pack_kernel, scores, values), grid_spec=...]
    unnamed x20, local copies, waits for them, and re-layouts: 4.36 us -> 2.48 us
    ppermute x18, starting transfers between devices: 41 us -> 40 us  [swap(): return lax.ppermute(array, axis, [(i, i ^ offset) for i in range(size)])]
    pallas_call x2, Pallas kernels: 14.2 us -> 13.2 us  [attend(): pl.pallas_call(functools.partial(attend_kernel, seq_count, heads, near_pi...]
  transfers between devices with their start and end apart: 18 -> 18, of which waited for: 7 -> 7; matrix products, arithmetic and copies ran while one was open for 2% -> 2% of each run, Pallas kernels for 23% -> 22%
where the time goes in v6:
time: 92.2 us; the launch traced here: 91.9 us
  starting transfers between devices  40 us (43%)
  Pallas kernels  27.1 us (29%)
  waiting for transfers between devices  16.4 us (18%)
  local copies, waits for them, and re-layouts  4.34 us (5%)
  between operations  2.79 us (3%)
  other arithmetic  1.3 us (1%)
    ppermute x18, starting transfers between devices, swap(): return lax.ppermute(array, axis, [(i, i ^ offset) for i in range(size)])  40 us
    ppermute x18, waiting for transfers between devices, swap(): return lax.ppermute(array, axis, [(i, i ^ offset) for i in range(size)])  16.4 us
    pallas_call x12, Pallas kernels, pack(): pl.pallas_call(functools.partial(pack_kernel, scores, values), grid_spec=...  13.9 us
    pallas_call x2, Pallas kernels, attend(): pl.pallas_call(functools.partial(attend_kernel, seq_count, heads, near_pi...  13.2 us
    unnamed x20, local copies, waits for them, and re-layouts  2.48 us
    dynamic_slice x2, local copies, waits for them, and re-layouts, body(): factor = (signed * step_weight[timestep[sample_index]]).reshape(1)  1.86 us
  transfers between devices with their start and end apart: 18, of which 7 were waited for; matrix products, arithmetic and copies ran while one was open for 2% of the time, Pallas kernels for 22%

profile of v6, /device:TPU:0, one launch (start us, length us, event | category | flops | bytes accessed | tf_op | source)
XLA Modules:
  0.0 91.9 jit_solution(7229621059190083072)
XLA Ops:
  0.0 0.6 pad_add_fusion.place_ref
  0.7 2.7 %pack.18 = bf16[128,1024]{1,0:T(8,128)(2,1)} custom-call(s32[2]{0:T(128)} %pad_add_fusion.place_ref, bf16[1,128,12288]{2,1,0:T(8,128)(2,1)} %qkv_ref.23, bf16[2,64,4096]{2,1,0:T(8,128)(2,1)} %bitcast.10), custom_call_target="tpu_custom_call" | custom-call | flops 8388608 | bytes 524288 | tf_op jit(solution)/shard_map/pack/pallas_call | solution.py:50
  3.3 6.0 %collective-permute-start.5 = (bf16[128,1024]{1,0:T(8,128)(2,1)}, bf16[128,1024]{1,0:T(8,128)(2,1)S(1)}, u32[]{:S(2)}, u32[]{:S(2)}) collective-permute-start(bf16[128,1024]{1,0:T(8,128)(2,1)} %pack.18), channel_id=1, source_target_pairs={{0,28},{4,24},{8,20},{12,16},{16,12},{20,8},{24,4},{28,0},{1,29},{... | collective-permute-start | bytes 786440 | tf_op jit(solution)/shard_map/ppermute | solution.py:218
  9.3 1.2 %copy-done.1 = bf16[2,4096,64]{1,2,0:T(8,128)(2,1)S(1)} copy-done((bf16[2,4096,64]{1,2,0:T(8,128)(2,1)S(1)}, bf16[2,4096,64]{1,2,0:T(8,128)(2,1)}, u32[]{:S(2)}) %copy-start.1) | copy-done | bytes 1048600
  10.6 0.8 pack.16
  11.3 0.3 collective-permute-start.3
  11.6 1.5 %pack.13 = bf16[128,1280]{1,0:T(8,128)(2,1)} custom-call(s32[2]{0:T(128)S(1)} %copy-done.7, bf16[1,128,12288]{2,1,0:T(8,128)(2,1)S(1)} %copy-done, bf16[2,64,4096]{2,1,0:T(8,128)(2,1)S(1)} %bitcast.12), custom_call_target="tpu_custom_call" | custom-call | flops 8388608 | bytes 655360 | tf_op jit(solution)/shard_map/pack/pallas_call | solution.py:50
  13.1 0.4 collective-permute-start
  13.5 1.5 %pack.14 = bf16[128,1280]{1,0:T(8,128)(2,1)} custom-call(s32[2]{0:T(128)S(1)} %copy-done.7, bf16[1,128,12288]{2,1,0:T(8,128)(2,1)S(1)} %copy-done, bf16[2,64,4096]{2,1,0:T(8,128)(2,1)S(1)} %bitcast.13), custom_call_target="tpu_custom_call" | custom-call | flops 8388608 | bytes 655360 | tf_op jit(solution)/shard_map/pack/pallas_call | solution.py:50
  15.0 0.0 collective-permute-start.1
  15.0 1.5 %pack.15 = bf16[128,1280]{1,0:T(8,128)(2,1)} custom-call(s32[2]{0:T(128)S(1)} %copy-done.7, bf16[1,128,12288]{2,1,0:T(8,128)(2,1)S(1)} %copy-done, bf16[2,64,4096]{2,1,0:T(8,128)(2,1)S(1)} %bitcast.14), custom_call_target="tpu_custom_call" | custom-call | flops 8388608 | bytes 655360 | tf_op jit(solution)/shard_map/pack/pallas_call | solution.py:50
  16.5 3.1 %collective-permute-start.2 = (bf16[128,1280]{1,0:T(8,128)(2,1)}, bf16[128,1280]{1,0:T(8,128)(2,1)}, u32[]{:S(2)}, u32[]{:S(2)}) collective-permute-start(bf16[128,1280]{1,0:T(8,128)(2,1)} %pack.15), channel_id=1, source_target_pairs={{0,12},{4,8},{8,4},{12,0},{16,28},{20,24},{24,20},{28,16},{1,13},{... | collective-permute-start | bytes 983048 | tf_op jit(solution)/shard_map/ppermute | solution.py:218
  19.6 0.0 collective-permute-done.5.refs_0_.refs_7_
  19.6 1.5 %pack.19 = bf16[128,1024]{1,0:T(8,128)(2,1)} custom-call(s32[2]{0:T(128)S(1)} %copy-done.7, bf16[1,128,12288]{2,1,0:T(8,128)(2,1)S(1)} %copy-done, bf16[2,64,4096]{2,1,0:T(8,128)(2,1)S(1)} %bitcast.15, bf16[128,1024]{1,0:T(8,128)(2,1)S(1)} %collective-permute-done.5.refs_0_.refs_7_), custom_call_target="tpu_custom_call" | custom-call | flops 8388608 | bytes 524288 | tf_op jit(solution)/shard_map/pack/pallas_call | solution.py:50
  21.1 10.3 %collective-permute-start.6 = (bf16[128,1024]{1,0:T(8,128)(2,1)}, bf16[128,1024]{1,0:T(8,128)(2,1)S(1)}, u32[]{:S(2)}, u32[]{:S(2)}) collective-permute-start(bf16[128,1024]{1,0:T(8,128)(2,1)} %pack.19), channel_id=1, source_target_pairs={{0,20},{4,16},{8,28},{12,24},{16,4},{20,0},{24,12},{28,8},{1,21},{... | collective-permute-start | bytes 786440 | tf_op jit(solution)/shard_map/ppermute | solution.py:218
  31.3 0.0 collective-permute-done.3.refs_0_.refs_6_
  31.3 1.5 %pack.17 = bf16[128,1024]{1,0:T(8,128)(2,1)} custom-call(s32[2]{0:T(128)S(1)} %copy-done.7, bf16[1,128,12288]{2,1,0:T(8,128)(2,1)S(1)} %copy-done, bf16[2,64,4096]{2,1,0:T(8,128)(2,1)S(1)} %bitcast.16, bf16[128,1024]{1,0:T(8,128)(2,1)S(1)} %collective-permute-done.3.refs_0_.refs_6_), custom_call_target="tpu_custom_call" | custom-call | flops 8388608 | bytes 524288 | tf_op jit(solution)/shard_map/pack/pallas_call | solution.py:50
  32.8 3.2 %collective-permute-start.4 = (bf16[128,1024]{1,0:T(8,128)(2,1)}, bf16[128,1024]{1,0:T(8,128)(2,1)}, u32[]{:S(2)}, u32[]{:S(2)}) collective-permute-start(bf16[128,1024]{1,0:T(8,128)(2,1)} %pack.17), channel_id=1, source_target_pairs={{0,16},{4,20},{8,24},{12,28},{16,0},{20,4},{24,8},{28,12},{1,17},{... | collective-permute-start | bytes 786440 | tf_op jit(solution)/shard_map/ppermute | solution.py:218
  36.0 0.6 dynamic_slice.6
  38.6 1.3 %dynamic_slice.7 = f32[1]{0:T(128)} dynamic-slice(f32[1000]{0:T(1024)} %param.7, s32[]{:T(128)S(6)} %select_n.25), dynamic_slice_sizes={1} | dynamic-slice | bytes 12 | tf_op jit(solution)/shard_map/dynamic_slice | solution.py:232
  40.5 0.0 copy-start.2
  40.5 1.2 %copy-done.2 = bf16[2,4096,64]{1,2,0:T(8,128)(2,1)S(1)} copy-done((bf16[2,4096,64]{1,2,0:T(8,128)(2,1)S(1)}, bf16[2,4096,64]{1,2,0:T(8,128)(2,1)}, u32[]{:S(2)}) %copy-start.2) | copy-done | bytes 1048600
  41.7 0.8 pack.12.refs_0_
  42.5 8.2 %collective-permute-done.6.refs_0_.refs_5_ = bf16[128,1024]{1,0:T(8,128)(2,1)S(1)} collective-permute-done((bf16[128,1024]{1,0:T(8,128)(2,1)}, bf16[128,1024]{1,0:T(8,128)(2,1)S(1)}, u32[]{:S(2)}, u32[]{:S(2)}) %collective-permute-start.6) | collective-permute-done | bytes 262176 | tf_op jit(solution)/shard_map/ppermute | solution.py:218
  50.7 0.6 pack.23.refs_8_
  51.3 3.3 %collective-permute-start.10 = (bf16[128,256]{1,0:T(8,128)(2,1)S(1)}, bf16[128,256]{1,0:T(8,128)(2,1)S(1)}, u32[]{:S(2)}, u32[]{:S(2)}) collective-permute-start(bf16[128,256]{1,0:T(8,128)(2,1)S(1)} %pack.23.refs_8_), channel_id=1, source_target_pairs={{0,28},{4,24},{8,20},{12,16},{16,12},{20,8},{24,4},{28,0},{1,29},{... | collective-permute-start | bytes 196616 | tf_op jit(solution)/shard_map/ppermute | solution.py:218
  54.6 1.3 %collective-permute-done.4.refs_0_.refs_4_ = bf16[128,1024]{1,0:T(8,128)(2,1)} collective-permute-done((bf16[128,1024]{1,0:T(8,128)(2,1)}, bf16[128,1024]{1,0:T(8,128)(2,1)}, u32[]{:S(2)}, u32[]{:S(2)}) %collective-permute-start.4) | collective-permute-done | bytes 262176 | tf_op jit(solution)/shard_map/ppermute | solution.py:218
  55.9 0.6 pack.20.refs_11_
  56.4 0.1 collective-permute-start.7
  56.5 0.6 pack.21.refs_10_
  57.1 0.0 copy-start.8
  57.1 0.6 pack.22.refs_9_
  57.7 2.9 %collective-permute-start.8 = (bf16[128,256]{1,0:T(8,128)(2,1)S(1)}, bf16[128,256]{1,0:T(8,128)(2,1)S(1)}, u32[]{:S(2)}, u32[]{:S(2)}) collective-permute-start(bf16[128,256]{1,0:T(8,128)(2,1)S(1)} %pack.21.refs_10_), channel_id=1, source_target_pairs={{0,20},{4,16},{8,28},{12,24},{16,4},{20,0},{24,12},{28,8},{1,21},{... | collective-permute-start | bytes 196616 | tf_op jit(solution)/shard_map/ppermute | solution.py:218
  60.6 2.5 %collective-permute-start.9 = (bf16[128,256]{1,0:T(8,128)(2,1)S(1)}, bf16[128,256]{1,0:T(8,128)(2,1)S(1)}, u32[]{:S(2)}, u32[]{:S(2)}) collective-permute-start(bf16[128,256]{1,0:T(8,128)(2,1)S(1)} %pack.22.refs_9_), channel_id=1, source_target_pairs={{0,24},{4,28},{8,16},{12,20},{16,8},{20,12},{24,0},{28,4},{1,25},{... | collective-permute-start | bytes 196616 | tf_op jit(solution)/shard_map/ppermute | solution.py:218
  63.1 8.9 %attend.2.refs_12_ = f32[8,64,128]{2,1,0:T(8,128)S(1)} custom-call(s32[4]{0:T(128)S(1)} %copy-done.8, f32[1]{0:T(128)} %bitcast.2.factor_ref, s32[1]{0:T(128)} %bitcast.3.me_ref, bf16[128,1280]{1,0:T(8,128)(2,1)S(1)} %pack.12.refs_0_, bf16[128,1280]{1,0:T(8,128)(2,1)} %collective-permute-done.refs_1_, bf16[128,1280]{1,0:T(8,128)(2,1)} %collective-permute-done.1.refs_2_, ...), custom_call_target="tpu_custom_call" | custom-call | flops 1207959552 | bytes 2359296 | tf_op jit(solution)/shard_map/attend/pallas_call | solution.py:195
  72.1 4.3 %attend.3 = (f32[4,64,128]{2,1,0:T(8,128)S(1)}, bf16[4,64,128]{2,1,0:T(8,128)(2,1)S(1)}) custom-call(s32[4]{0:T(128)S(1)} %copy-done.8, f32[1]{0:T(128)} %bitcast.2.factor_ref, s32[1]{0:T(128)} %bitcast.3.me_ref, bf16[128,1280]{1,0:T(8,128)(2,1)S(1)} %pack.12.refs_0_, bf16[128,1280]{1,0:T(8,128)(2,1)} %collective-permute-done.refs_1_, ...), custom_call_target="tpu_custom_call" | custom-call | flops 402653184 | bytes 786432 | tf_op jit(solution)/shard_map/attend/pallas_call | solution.py:195
  76.4 1.6 %collective-permute-start.11 = (bf16[4,64,128]{2,1,0:T(8,128)(2,1)S(1)}, bf16[4,64,128]{2,1,0:T(8,128)(2,1)S(1)}, u32[]{:S(2)}, u32[]{:S(2)}) collective-permute-start(bf16[4,64,128]{2,1,0:T(8,128)(2,1)S(1)} %get-tuple-element.8), channel_id=1, source_target_pairs={{0,4},{4,0},{8,12},{12,8},{16,20},{20,16},{24,28},{28,24},{1,5},{5... | collective-permute-start | bytes 196616 | tf_op jit(solution)/shard_map/ppermute | solution.py:218
  78.0 2.8 %collective-permute-done.11 = bf16[4,64,128]{2,1,0:T(8,128)(2,1)S(1)} collective-permute-done((bf16[4,64,128]{2,1,0:T(8,128)(2,1)S(1)}, bf16[4,64,128]{2,1,0:T(8,128)(2,1)S(1)}, u32[]{:S(2)}, u32[]{:S(2)}) %collective-permute-start.11) | collective-permute-done | bytes 65568 | tf_op jit(solution)/shard_map/ppermute | solution.py:218
  80.8 1.4 %collective-permute-start.12 = (f32[1,64,128]{2,1,0:T(8,128)S(1)}, f32[1,64,128]{2,1,0:T(8,128)S(1)}, u32[]{:S(2)}, u32[]{:S(2)}) collective-permute-start(f32[1,64,128]{2,1,0:T(8,128)S(1)} %get-tuple-element.9), channel_id=1, source_target_pairs={{0,24},{4,28},{8,16},{12,20},{16,8},{20,12},{24,0},{28,4},{1,25},{... | collective-permute-start | bytes 98312 | tf_op jit(solution)/shard_map/ppermute | solution.py:218
  82.2 3.0 %collective-permute-start.14 = (f32[1,64,128]{2,1,0:T(8,128)S(1)}, f32[1,64,128]{2,1,0:T(8,128)S(1)}, u32[]{:S(2)}, u32[]{:S(2)}) collective-permute-start(f32[1,64,128]{2,1,0:T(8,128)S(1)} %get-tuple-element.10), channel_id=1, source_target_pairs={{0,16},{4,20},{8,24},{12,28},{16,0},{20,4},{24,8},{28,12},{1,17},{... | collective-permute-start | bytes 98312 | tf_op jit(solution)/shard_map/ppermute | solution.py:218
  85.2 1.3 %collective-permute-done.12 = f32[1,64,128]{2,1,0:T(8,128)S(1)} collective-permute-done((f32[1,64,128]{2,1,0:T(8,128)S(1)}, f32[1,64,128]{2,1,0:T(8,128)S(1)}, u32[]{:S(2)}, u32[]{:S(2)}) %collective-permute-start.12) | collective-permute-done | bytes 32800 | tf_op jit(solution)/shard_map/ppermute | solution.py:218
  86.6 0.6 collective-permute-done.14
  87.1 0.1 collective-permute-start.15
  87.2 1.6 %collective-permute-start.16 = (f32[64,128]{1,0:T(8,128)S(1)}, f32[64,128]{1,0:T(8,128)S(1)}, u32[]{:S(2)}, u32[]{:S(2)}) collective-permute-start(f32[64,128]{1,0:T(8,128)S(1)} %fusion.2), channel_id=1, source_target_pairs={{0,2},{1,3},{2,0},{3,1},{4,6},{5,7},{6,4},{7,5},{8,10},{9,11},{10,... | collective-permute-start | bytes 98312 | tf_op jit(solution)/shard_map/ppermute | solution.py:218
  88.8 0.3 collective-permute-start.17
  89.1 1.8 %collective-permute-done.15 = f32[64,128]{1,0:T(8,128)S(1)} collective-permute-done((f32[64,128]{1,0:T(8,128)S(1)}, f32[64,128]{1,0:T(8,128)S(1)}, u32[]{:S(2)}, u32[]{:S(2)}) %collective-permute-start.15) | collective-permute-done | bytes 32800 | tf_op jit(solution)/shard_map/ppermute | solution.py:218
  90.8 0.4 collective-permute-done.16
  91.2 0.6 add_bitcast_fusion
  (29 shorter events, 0.1 us)
Async XLA Ops:
  0.0 9.3 %copy-start = (bf16[1,128,12288]{2,1,0:T(8,128)(2,1)S(1)}, bf16[1,128,12288]{2,1,0:T(8,128)(2,1)}, u32[]{:S(2)}) copy-start(bf16[1,128,12288]{2,1,0:T(8,128)(2,1)} %qkv_ref.23) | copy-start | bytes 9437188
  0.7 8.7 %copy-start.7 = (s32[2]{0:T(128)S(1)}, s32[2]{0:T(128)}, u32[]{:S(2)}) copy-start(s32[2]{0:T(128)} %pad_add_fusion.place_ref) | copy-start | bytes 28
  3.3 16.3 %collective-permute-start.5 = (bf16[128,1024]{1,0:T(8,128)(2,1)}, bf16[128,1024]{1,0:T(8,128)(2,1)S(1)}, u32[]{:S(2)}, u32[]{:S(2)}) collective-permute-start(bf16[128,1024]{1,0:T(8,128)(2,1)} %pack.18), channel_id=1, source_target_pairs={{0,28},{4,24},{8,20},{12,16},{16,12},{20,8},{24,4},{28,0},{1,29},{... | collective-permute-start | bytes 786440 | tf_op jit(solution)/shard_map/ppermute | solution.py:218
  9.3 1.2 %copy-start.1 = (bf16[2,4096,64]{1,2,0:T(8,128)(2,1)S(1)}, bf16[2,4096,64]{1,2,0:T(8,128)(2,1)}, u32[]{:S(2)}) copy-start(bf16[2,4096,64]{1,2,0:T(8,128)(2,1)} %param.6) | copy-start | bytes 3145732
  11.3 20.0 %collective-permute-start.3 = (bf16[128,1024]{1,0:T(8,128)(2,1)S(1)}, bf16[128,1024]{1,0:T(8,128)(2,1)S(1)}, u32[]{:S(2)}, u32[]{:S(2)}) collective-permute-start(bf16[128,1024]{1,0:T(8,128)(2,1)S(1)} %pack.16), channel_id=1, source_target_pairs={{0,24},{4,28},{8,16},{12,20},{16,8},{20,12},{24,0},{28,4},{1,25},{... | collective-permute-start | bytes 786440 | tf_op jit(solution)/shard_map/ppermute | solution.py:218
  13.1 44.6 %collective-permute-start = (bf16[128,1280]{1,0:T(8,128)(2,1)}, bf16[128,1280]{1,0:T(8,128)(2,1)}, u32[]{:S(2)}, u32[]{:S(2)}) collective-permute-start(bf16[128,1280]{1,0:T(8,128)(2,1)} %pack.13), channel_id=1, source_target_pairs={{0,4},{4,0},{8,12},{12,8},{16,20},{20,16},{24,28},{28,24},{1,5},{5... | collective-permute-start | bytes 983048 | tf_op jit(solution)/shard_map/ppermute | solution.py:218
  15.0 45.7 %collective-permute-start.1 = (bf16[128,1280]{1,0:T(8,128)(2,1)}, bf16[128,1280]{1,0:T(8,128)(2,1)}, u32[]{:S(2)}, u32[]{:S(2)}) collective-permute-start(bf16[128,1280]{1,0:T(8,128)(2,1)} %pack.14), channel_id=1, source_target_pairs={{0,8},{4,12},{8,0},{12,4},{16,24},{20,28},{24,16},{28,20},{1,9},{5... | collective-permute-start | bytes 983048 | tf_op jit(solution)/shard_map/ppermute | solution.py:218
  16.5 46.6 %collective-permute-start.2 = (bf16[128,1280]{1,0:T(8,128)(2,1)}, bf16[128,1280]{1,0:T(8,128)(2,1)}, u32[]{:S(2)}, u32[]{:S(2)}) collective-permute-start(bf16[128,1280]{1,0:T(8,128)(2,1)} %pack.15), channel_id=1, source_target_pairs={{0,12},{4,8},{8,4},{12,0},{16,28},{20,24},{24,20},{28,16},{1,13},{... | collective-permute-start | bytes 983048 | tf_op jit(solution)/shard_map/ppermute | solution.py:218
  19.6 13.2 %copy-start.3 = (bf16[128,1024]{1,0:T(8,128)(2,1)}, bf16[128,1024]{1,0:T(8,128)(2,1)S(1)}, u32[]{:S(2)}) copy-start(bf16[128,1024]{1,0:T(8,128)(2,1)S(1)} %collective-permute-done.5.refs_0_.refs_7_) | copy-start | bytes 786436
  21.1 15.0 %copy-start.9 = (s32[2]{0:T(128)S(1)}, s32[2]{0:T(128)}, u32[]{:S(2)}) copy-start(s32[2]{0:T(128)} %param.8) | copy-start | bytes 28
  21.1 29.7 %collective-permute-start.6 = (bf16[128,1024]{1,0:T(8,128)(2,1)}, bf16[128,1024]{1,0:T(8,128)(2,1)S(1)}, u32[]{:S(2)}, u32[]{:S(2)}) collective-permute-start(bf16[128,1024]{1,0:T(8,128)(2,1)} %pack.19), channel_id=1, source_target_pairs={{0,20},{4,16},{8,28},{12,24},{16,4},{20,0},{24,12},{28,8},{1,21},{... | collective-permute-start | bytes 786440 | tf_op jit(solution)/shard_map/ppermute | solution.py:218
  31.3 1.5 %copy-start.5 = (bf16[128,1024]{1,0:T(8,128)(2,1)}, bf16[128,1024]{1,0:T(8,128)(2,1)S(1)}, u32[]{:S(2)}) copy-start(bf16[128,1024]{1,0:T(8,128)(2,1)S(1)} %collective-permute-done.3.refs_0_.refs_6_) | copy-start | bytes 786436
  32.8 23.1 %collective-permute-start.4 = (bf16[128,1024]{1,0:T(8,128)(2,1)}, bf16[128,1024]{1,0:T(8,128)(2,1)}, u32[]{:S(2)}, u32[]{:S(2)}) collective-permute-start(bf16[128,1024]{1,0:T(8,128)(2,1)} %pack.17), channel_id=1, source_target_pairs={{0,16},{4,20},{8,24},{12,28},{16,0},{20,4},{24,8},{28,12},{1,17},{... | collective-permute-start | bytes 786440 | tf_op jit(solution)/shard_map/ppermute | solution.py:218
  40.5 1.2 %copy-start.2 = (bf16[2,4096,64]{1,2,0:T(8,128)(2,1)S(1)}, bf16[2,4096,64]{1,2,0:T(8,128)(2,1)}, u32[]{:S(2)}) copy-start(bf16[2,4096,64]{1,2,0:T(8,128)(2,1)} %param.6) | copy-start | bytes 3145732
  51.3 20.8 %collective-permute-start.10 = (bf16[128,256]{1,0:T(8,128)(2,1)S(1)}, bf16[128,256]{1,0:T(8,128)(2,1)S(1)}, u32[]{:S(2)}, u32[]{:S(2)}) collective-permute-start(bf16[128,256]{1,0:T(8,128)(2,1)S(1)} %pack.23.refs_8_), channel_id=1, source_target_pairs={{0,28},{4,24},{8,20},{12,16},{16,12},{20,8},{24,4},{28,0},{1,29},{... | collective-permute-start | bytes 196616 | tf_op jit(solution)/shard_map/ppermute | solution.py:218
  56.4 15.6 %collective-permute-start.7 = (bf16[128,256]{1,0:T(8,128)(2,1)S(1)}, bf16[128,256]{1,0:T(8,128)(2,1)S(1)}, u32[]{:S(2)}, u32[]{:S(2)}) collective-permute-start(bf16[128,256]{1,0:T(8,128)(2,1)S(1)} %pack.20.refs_11_), channel_id=1, source_target_pairs={{0,16},{4,20},{8,24},{12,28},{16,0},{20,4},{24,8},{28,12},{1,17},{... | collective-permute-start | bytes 196616 | tf_op jit(solution)/shard_map/ppermute | solution.py:218
  57.1 6.0 %copy-start.4 = (bf16[128,1024]{1,0:T(8,128)(2,1)S(1)}, bf16[128,1024]{1,0:T(8,128)(2,1)}, u32[]{:S(2)}) copy-start(bf16[128,1024]{1,0:T(8,128)(2,1)} %copy-done.3) | copy-start | bytes 786436
  57.1 6.0 %copy-start.6 = (bf16[128,1024]{1,0:T(8,128)(2,1)S(1)}, bf16[128,1024]{1,0:T(8,128)(2,1)}, u32[]{:S(2)}) copy-start(bf16[128,1024]{1,0:T(8,128)(2,1)} %copy-done.5) | copy-start | bytes 786436
  57.1 6.0 %copy-start.8 = (s32[4]{0:T(128)S(1)}, s32[4]{0:T(128)}, u32[]{:S(2)}) copy-start(s32[4]{0:T(128)} %frames_ref.3) | copy-start | bytes 52
  57.7 14.4 %collective-permute-start.8 = (bf16[128,256]{1,0:T(8,128)(2,1)S(1)}, bf16[128,256]{1,0:T(8,128)(2,1)S(1)}, u32[]{:S(2)}, u32[]{:S(2)}) collective-permute-start(bf16[128,256]{1,0:T(8,128)(2,1)S(1)} %pack.21.refs_10_), channel_id=1, source_target_pairs={{0,20},{4,16},{8,28},{12,24},{16,4},{20,0},{24,12},{28,8},{1,21},{... | collective-permute-start | bytes 196616 | tf_op jit(solution)/shard_map/ppermute | solution.py:218
  60.6 11.4 %collective-permute-start.9 = (bf16[128,256]{1,0:T(8,128)(2,1)S(1)}, bf16[128,256]{1,0:T(8,128)(2,1)S(1)}, u32[]{:S(2)}, u32[]{:S(2)}) collective-permute-start(bf16[128,256]{1,0:T(8,128)(2,1)S(1)} %pack.22.refs_9_), channel_id=1, source_target_pairs={{0,24},{4,28},{8,16},{12,20},{16,8},{20,12},{24,0},{28,4},{1,25},{... | collective-permute-start | bytes 196616 | tf_op jit(solution)/shard_map/ppermute | solution.py:218
  76.4 4.3 %collective-permute-start.11 = (bf16[4,64,128]{2,1,0:T(8,128)(2,1)S(1)}, bf16[4,64,128]{2,1,0:T(8,128)(2,1)S(1)}, u32[]{:S(2)}, u32[]{:S(2)}) collective-permute-start(bf16[4,64,128]{2,1,0:T(8,128)(2,1)S(1)} %get-tuple-element.8), channel_id=1, source_target_pairs={{0,4},{4,0},{8,12},{12,8},{16,20},{20,16},{24,28},{28,24},{1,5},{5... | collective-permute-start | bytes 196616 | tf_op jit(solution)/shard_map/ppermute | solution.py:218
  80.8 5.8 %collective-permute-start.12 = (f32[1,64,128]{2,1,0:T(8,128)S(1)}, f32[1,64,128]{2,1,0:T(8,128)S(1)}, u32[]{:S(2)}, u32[]{:S(2)}) collective-permute-start(f32[1,64,128]{2,1,0:T(8,128)S(1)} %get-tuple-element.9), channel_id=1, source_target_pairs={{0,24},{4,28},{8,16},{12,20},{16,8},{20,12},{24,0},{28,4},{1,25},{... | collective-permute-start | bytes 98312 | tf_op jit(solution)/shard_map/ppermute | solution.py:218
  82.2 4.4 %collective-permute-start.13 = (f32[1,64,128]{2,1,0:T(8,128)S(1)}, f32[1,64,128]{2,1,0:T(8,128)S(1)}, u32[]{:S(2)}, u32[]{:S(2)}) collective-permute-start(f32[1,64,128]{2,1,0:T(8,128)S(1)} %get-tuple-element.11), channel_id=1, source_target_pairs={{0,8},{4,12},{8,0},{12,4},{16,24},{20,28},{24,16},{28,20},{1,9},{5... | collective-permute-start | bytes 98312 | tf_op jit(solution)/shard_map/ppermute | solution.py:218
  82.2 4.9 %collective-permute-start.14 = (f32[1,64,128]{2,1,0:T(8,128)S(1)}, f32[1,64,128]{2,1,0:T(8,128)S(1)}, u32[]{:S(2)}, u32[]{:S(2)}) collective-permute-start(f32[1,64,128]{2,1,0:T(8,128)S(1)} %get-tuple-element.10), channel_id=1, source_target_pairs={{0,16},{4,20},{8,24},{12,28},{16,0},{20,4},{24,8},{28,12},{1,17},{... | collective-permute-start | bytes 98312 | tf_op jit(solution)/shard_map/ppermute | solution.py:218
  87.1 3.7 %collective-permute-start.15 = (f32[64,128]{1,0:T(8,128)S(1)}, f32[64,128]{1,0:T(8,128)S(1)}, u32[]{:S(2)}, u32[]{:S(2)}) collective-permute-start(f32[64,128]{1,0:T(8,128)S(1)} %fusion.2), channel_id=1, source_target_pairs={{0,3},{1,2},{2,1},{3,0},{4,7},{5,6},{6,5},{7,4},{8,11},{9,10},{10,... | collective-permute-start | bytes 98312 | tf_op jit(solution)/shard_map/ppermute | solution.py:218
  87.2 4.0 %collective-permute-start.16 = (f32[64,128]{1,0:T(8,128)S(1)}, f32[64,128]{1,0:T(8,128)S(1)}, u32[]{:S(2)}, u32[]{:S(2)}) collective-permute-start(f32[64,128]{1,0:T(8,128)S(1)} %fusion.2), channel_id=1, source_target_pairs={{0,2},{1,3},{2,0},{3,1},{4,6},{5,7},{6,4},{7,5},{8,10},{9,11},{10,... | collective-permute-start | bytes 98312 | tf_op jit(solution)/shard_map/ppermute | solution.py:218
  88.8 2.4 %collective-permute-start.17 = (f32[64,128]{1,0:T(8,128)S(1)}, f32[64,128]{1,0:T(8,128)S(1)}, u32[]{:S(2)}, u32[]{:S(2)}) collective-permute-start(f32[64,128]{1,0:T(8,128)S(1)} %fusion.2), channel_id=1, source_target_pairs={{0,1},{1,0},{2,3},{3,2},{4,5},{5,4},{6,7},{7,6},{8,9},{9,8},{10,11... | collective-permute-start | bytes 98312 | tf_op jit(solution)/shard_map/ppermute | solution.py:218

commit v7 on v6

--- a/solution.py
+++ b/solution.py
@@ -12,7 +12,8 @@
 HD = 128
 FRAME_TOK = 64
 NT = (((1,), (1,)), ((), ()))
-VMEM_LIMIT = 32 * 1024 * 1024
+VMEM_LIMIT = 8 * 1024 * 1024
+ATTEND_VMEM = 20 * 1024 * 1024
 WHOLE_VMEM = 60 * 1024 * 1024
 
 
@@ -35,7 +36,7 @@
         out_ref[row : row + lat, column : column + HD] = folded.astype(jnp.bfloat16)
 
 
-def pack(place, qkv, readout_t, k, heads_local, piece, after, limit=VMEM_LIMIT):
+def pack(place, qkv, readout_t, k, heads_local, piece, after):
     rows = qkv.shape[1]
     lat = readout_t.shape[1]
     scores, values, width = piece
@@ -56,7 +57,7 @@
             out_specs=pl.BlockSpec((rows, width), lambda g, m: (0, 0)),
         ),
         out_shape=jax.ShapeDtypeStruct((rows, width), jnp.bfloat16),
-        compiler_params=pltpu.CompilerParams(vmem_limit_bytes=limit),
+        compiler_params=pltpu.CompilerParams(vmem_limit_bytes=VMEM_LIMIT),
         cost_estimate=pl.CostEstimate(
             flops=2 * rows * lat * len(values) * HD, bytes_accessed=rows * width * 4, transcendentals=0
         ),
@@ -117,34 +118,30 @@
             k = k | (((n >> bit) & 1) << (reversed_bits - 1 - bit))
         return me ^ k
 
-    def one_block(b):
-        first = b * 2
-        places = jnp.concatenate([place_of(first + j) * rows + column_places for j in range(2)], axis=1)
+    tile = 2 * rows
+    tiles = seq_count // 2
+
+    def bounds_of(b):
+        places = jnp.concatenate([place_of(b * 2 + j) * rows + column_places for j in range(2)], axis=1)
         bound = jnp.full((1, block), ends[0], jnp.int32)
         for c in range(1, spans):
             bound = jnp.where(places >= ends[c - 1], ends[c], bound)
-        bias = [
+        return [
             jnp.where((me ^ k) * rows + start < bound, 0.0, -jnp.inf)
             for k in range(seq_count)
             for start in range(0, rows, FRAME_TOK)
         ]
-        total = None
-        for i, h in enumerate(heads):
-            queries = asked[pl.ds(first, 2), i].reshape(block, HD)
-            keys = jnp.concatenate([cell(k, h, 1) for k in range(seq_count)], axis=0)
-            scores = lax.dot_general(keys, queries, NT, preferred_element_type=jnp.float32)
-            frames = [scores[g * FRAME_TOK : (g + 1) * FRAME_TOK] for g in range(len(bias))]
-            peaks = [jnp.max(f, axis=0, keepdims=True) + shift for f, shift in zip(frames, bias)]
-            peak = functools.reduce(jnp.maximum, peaks)
-            weights = [
-                jnp.exp2((f + (shift - peak)) * log2_scale).astype(jnp.bfloat16) for f, shift in zip(frames, bias)
-            ]
-            summed = jnp.dot(folded[i], jnp.concatenate(weights, axis=0), preferred_element_type=jnp.float32)
-            part = summed[:lat] / summed[lat : lat + 1]
-            total = part if total is None else total + part
+
+    def score_tile(b, i, t):
+        queries = asked[pl.ds(b * 2, 2), i].reshape(block, HD)
+        keys = jnp.concatenate([cell(2 * t + j, heads[i], 1) for j in range(2)], axis=0)
+        scores = lax.dot_general(keys, queries, NT, preferred_element_type=jnp.float32)
+        return [scores[start : start + FRAME_TOK] for start in range(0, tile, FRAME_TOK)]
+
+    def finish(b, total):
         for j in range(2):
             part = total[:, j * rows : (j + 1) * rows]
-            n = first + j
+            n = b * 2 + j
             if earlier is not None:
                 part = part + earlier[n]
             if last:
@@ -160,11 +157,41 @@
             else:
                 out_refs[0][n] = part
 
-    together = 2 if count == 1 and half % 2 == 0 else 1
+    def units(work):
+        biases = {}
+        frames = [score_tile(*work[0], t) for t in range(tiles)]
+        total = None
+        for u, (b, i) in enumerate(work):
+            if i == 0:
+                biases = bounds_of(b)
+            each = len(frames[0])
+            flat = [f for t in frames for f in t]
+            peaks = [jnp.max(f, axis=0, keepdims=True) + shift for f, shift in zip(flat, biases)]
+            peak = functools.reduce(jnp.maximum, peaks)
+            following, summed = [], None
+            for t in range(tiles):
+                if u + 1 < len(work):
+                    following.append(score_tile(*work[u + 1], t))
+                weights = [
+                    jnp.exp2((f + (shift - peak)) * log2_scale).astype(jnp.bfloat16)
+                    for f, shift in zip(frames[t], biases[t * each : (t + 1) * each])
+                ]
+                part = jnp.dot(
+                    folded[i, :, t * tile : (t + 1) * tile],
+                    jnp.concatenate(weights, axis=0),
+                    preferred_element_type=jnp.float32,
+                )
+                summed = part if summed is None else summed + part
+            part = summed[:lat] / summed[lat : lat + 1]
+            total = part if i == 0 else total + part
+            if i == count - 1:
+                finish(b, total)
+            frames = following
+
+    together = min(half, 4 if count == 1 else 1)
 
     def some_blocks(b, carry):
-        for j in range(together):
-            one_block(b * together + j)
+        units([(b * together + j, i) for j in range(together) for i in range(count)])
         return carry
 
     lax.fori_loop(0, half // together, some_blocks, 0)
@@ -203,7 +230,7 @@
             pltpu.VMEM((seq_count, count, rows, HD), jnp.bfloat16),
             pltpu.VMEM((count, lat + 16, tokens), jnp.bfloat16),
         ],
-        compiler_params=pltpu.CompilerParams(vmem_limit_bytes=VMEM_LIMIT),
+        compiler_params=pltpu.CompilerParams(vmem_limit_bytes=ATTEND_VMEM if seq_count <= 8 else WHOLE_VMEM),
         cost_estimate=pl.CostEstimate(
             flops=count * tokens * tokens * 2 * (HD + lat),
             bytes_accessed=tokens * count * 3 * HD * 2,
@@ -240,26 +267,26 @@
     near_piece = layout(every, every, lat)
     far_pieces = [layout(heads, every if c == 0 else [], lat) for c, heads in enumerate(chunks)]
 
-    def send(k, piece, after, limit=VMEM_LIMIT):
-        packed = pack(place, qkv, readout_t, k, heads_local, piece, after, limit)
+    def send(k, piece, after):
+        packed = pack(place, qkv, readout_t, k, heads_local, piece, after)
         return packed, (swap(packed, "seq", k) if k else packed)
 
     far = [[None] * half for _ in chunks]
     near = [None] * half
     holds = [[] for _ in chunks]
-    gates = [None, None]
-    for c in range(len(chunks)):
-        for n in range(half):
-            k = seq_count - 1 - n
-            packed, far[c][k - half] = send(k, far_pieces[c], gates[n % 2], VMEM_LIMIT if c or n else WHOLE_VMEM)
-            if c:
-                holds[c - 1].append(packed)
-            else:
-                gates[n % 2] = far[c][k - half]
+    def far_send(c, n, after):
+        k = seq_count - 1 - n
+        packed, far[c][k - half] = send(k, far_pieces[c], after)
         if c:
-            gates = [far[c][1 % half], far[c][0]]
+            holds[c - 1].append(packed)
+
+    for n in range(half):
+        far_send(0, n, far[0][half + 1 - n] if n > 1 else None)
     for k in range(half):
         _, near[k] = send(k, near_piece, None)
+    for c in range(1, len(chunks)):
+        for n in range(half):
+            far_send(c, n, near[1 + n] if n < 2 and c == 1 else far[c - 1][half - 1 - n])
 
     result = None
     for c, heads in enumerate(chunks):

time: 92.2 us -> 89.8 us (0.974)
  Pallas kernels: 27.1 us -> 20.6 us
  starting transfers between devices: 40 us -> 42.6 us
  local copies, waits for them, and re-layouts: 4.34 us -> 6.23 us
    pallas_call x2, Pallas kernels: 13.2 us -> 8.66 us  [attend(): pl.pallas_call(functools.partial(attend_kernel, seq_count, heads, near_pi...]
    ppermute x18, starting transfers between devices: 40 us -> 42.6 us  [swap(): return lax.ppermute(array, axis, [(i, i ^ offset) for i in range(size)])]
    pallas_call x12, Pallas kernels: 13.9 us -> 12 us  [pack(): pl.pallas_call(functools.partial(pack_kernel, scores, values), grid_spec=...]
    unnamed x20, local copies, waits for them, and re-layouts: 2.48 us -> 4.36 us
  transfers between devices with their start and end apart: 18 -> 18, of which waited for: 7 -> 6; matrix products, arithmetic and copies ran while one was open for 2% -> 2% of each run, Pallas kernels for 22% -> 19%
where the time goes in v7:
time: 89.8 us; the launch traced here: 89.5 us
  starting transfers between devices  42.6 us (47%)
  Pallas kernels  20.6 us (23%)
  waiting for transfers between devices  16.4 us (18%)
  local copies, waits for them, and re-layouts  6.23 us (7%)
  between operations  2.83 us (3%)
    ppermute x18, starting transfers between devices, swap(): return lax.ppermute(array, axis, [(i, i ^ offset) for i in range(size)])  42.6 us
    ppermute x18, waiting for transfers between devices, swap(): return lax.ppermute(array, axis, [(i, i ^ offset) for i in range(size)])  16.4 us
    pallas_call x12, Pallas kernels, pack(): pl.pallas_call(functools.partial(pack_kernel, scores, values), grid_spec=...  12 us
    pallas_call x2, Pallas kernels, attend(): pl.pallas_call(functools.partial(attend_kernel, seq_count, heads, near_pi...  8.66 us
    unnamed x20, local copies, waits for them, and re-layouts  4.36 us
    dynamic_slice x2, local copies, waits for them, and re-layouts, body(): factor = (signed * step_weight[timestep[sample_index]]).reshape(1)  1.86 us
  transfers between devices with their start and end apart: 18, of which 6 were waited for; matrix products, arithmetic and copies ran while one was open for 2% of the time, Pallas kernels for 19%

profile of v7, /device:TPU:0, one launch (start us, length us, event | category | flops | bytes accessed | tf_op | source)
XLA Modules:
  0.0 89.5 jit_solution(4956029557012248802)
XLA Ops:
  0.0 0.1 pad_add_fusion.place_ref
  0.1 1.9 %copy-done = bf16[1,128,12288]{2,1,0:T(8,128)(2,1)S(1)} copy-done((bf16[1,128,12288]{2,1,0:T(8,128)(2,1)S(1)}, bf16[1,128,12288]{2,1,0:T(8,128)(2,1)}, u32[]{:S(2)}) %copy-start) | copy-done | bytes 3145752
  2.0 1.2 %copy-done.2 = bf16[2,4096,64]{1,2,0:T(8,128)(2,1)S(1)} copy-done((bf16[2,4096,64]{1,2,0:T(8,128)(2,1)S(1)}, bf16[2,4096,64]{1,2,0:T(8,128)(2,1)}, u32[]{:S(2)}) %copy-start.2) | copy-done | bytes 1048600
  3.2 0.8 pack.16
  4.0 5.1 %collective-permute-start.3 = (bf16[128,1024]{1,0:T(8,128)(2,1)S(1)}, bf16[128,1024]{1,0:T(8,128)(2,1)S(1)}, u32[]{:S(2)}, u32[]{:S(2)}) collective-permute-start(bf16[128,1024]{1,0:T(8,128)(2,1)S(1)} %pack.16), channel_id=1, source_target_pairs={{0,24},{4,28},{8,16},{12,20},{16,8},{20,12},{24,0},{28,4},{1,25},{... | collective-permute-start | bytes 786440 | tf_op jit(solution)/shard_map/ppermute | solution.py:245
  9.1 0.8 pack.18
  9.9 1.2 %collective-permute-start.5 = (bf16[128,1024]{1,0:T(8,128)(2,1)S(1)}, bf16[128,1024]{1,0:T(8,128)(2,1)S(1)}, u32[]{:S(2)}, u32[]{:S(2)}) collective-permute-start(bf16[128,1024]{1,0:T(8,128)(2,1)S(1)} %pack.18), channel_id=1, source_target_pairs={{0,28},{4,24},{8,20},{12,16},{16,12},{20,8},{24,4},{28,0},{1,29},{... | collective-permute-start | bytes 786440 | tf_op jit(solution)/shard_map/ppermute | solution.py:245
  11.1 1.5 %pack.14 = bf16[128,1280]{1,0:T(8,128)(2,1)} custom-call(s32[2]{0:T(128)S(1)} %pad_add_fusion.place_ref, bf16[1,128,12288]{2,1,0:T(8,128)(2,1)S(1)} %copy-done, bf16[2,64,4096]{2,1,0:T(8,128)(2,1)S(1)} %bitcast.12), custom_call_target="tpu_custom_call" | custom-call | flops 8388608 | bytes 655360 | tf_op jit(solution)/shard_map/pack/pallas_call | solution.py:51
  12.6 0.0 collective-permute-start.1
  12.6 1.5 %pack.13 = bf16[128,1280]{1,0:T(8,128)(2,1)} custom-call(s32[2]{0:T(128)S(1)} %pad_add_fusion.place_ref, bf16[1,128,12288]{2,1,0:T(8,128)(2,1)S(1)} %copy-done, bf16[2,64,4096]{2,1,0:T(8,128)(2,1)S(1)} %bitcast.13), custom_call_target="tpu_custom_call" | custom-call | flops 8388608 | bytes 655360 | tf_op jit(solution)/shard_map/pack/pallas_call | solution.py:51
  14.1 0.4 collective-permute-start
  14.4 1.5 %pack.15 = bf16[128,1280]{1,0:T(8,128)(2,1)} custom-call(s32[2]{0:T(128)S(1)} %pad_add_fusion.place_ref, bf16[1,128,12288]{2,1,0:T(8,128)(2,1)S(1)} %copy-done, bf16[2,64,4096]{2,1,0:T(8,128)(2,1)S(1)} %bitcast.14), custom_call_target="tpu_custom_call" | custom-call | flops 8388608 | bytes 655360 | tf_op jit(solution)/shard_map/pack/pallas_call | solution.py:51
  15.9 3.1 %collective-permute-start.2 = (bf16[128,1280]{1,0:T(8,128)(2,1)}, bf16[128,1280]{1,0:T(8,128)(2,1)}, u32[]{:S(2)}, u32[]{:S(2)}) collective-permute-start(bf16[128,1280]{1,0:T(8,128)(2,1)} %pack.15), channel_id=1, source_target_pairs={{0,12},{4,8},{8,4},{12,0},{16,28},{20,24},{24,20},{28,16},{1,13},{... | collective-permute-start | bytes 983048 | tf_op jit(solution)/shard_map/ppermute | solution.py:245
  19.1 1.5 %pack.17 = bf16[128,1024]{1,0:T(8,128)(2,1)} custom-call(s32[2]{0:T(128)S(1)} %pad_add_fusion.place_ref, bf16[1,128,12288]{2,1,0:T(8,128)(2,1)S(1)} %copy-done, bf16[2,64,4096]{2,1,0:T(8,128)(2,1)S(1)} %bitcast.15, bf16[128,1024]{1,0:T(8,128)(2,1)S(1)} %collective-permute-done.3.refs_0_.refs_6_), custom_call_target="tpu_custom_call" | custom-call | flops 8388608 | bytes 524288 | tf_op jit(solution)/shard_map/pack/pallas_call | solution.py:51
  20.5 9.4 %collective-permute-start.4 = (bf16[128,1024]{1,0:T(8,128)(2,1)}, bf16[128,1024]{1,0:T(8,128)(2,1)}, u32[]{:S(2)}, u32[]{:S(2)}) collective-permute-start(bf16[128,1024]{1,0:T(8,128)(2,1)} %pack.17), channel_id=1, source_target_pairs={{0,16},{4,20},{8,24},{12,28},{16,0},{20,4},{24,8},{28,12},{1,17},{... | collective-permute-start | bytes 786440 | tf_op jit(solution)/shard_map/ppermute | solution.py:245
  30.0 0.0 collective-permute-done.5.refs_0_.refs_7_
  30.0 1.5 %pack.19 = bf16[128,1024]{1,0:T(8,128)(2,1)} custom-call(s32[2]{0:T(128)S(1)} %pad_add_fusion.place_ref, bf16[1,128,12288]{2,1,0:T(8,128)(2,1)S(1)} %copy-done, bf16[2,64,4096]{2,1,0:T(8,128)(2,1)S(1)} %bitcast.16, bf16[128,1024]{1,0:T(8,128)(2,1)S(1)} %collective-permute-done.5.refs_0_.refs_7_), custom_call_target="tpu_custom_call" | custom-call | flops 8388608 | bytes 524288 | tf_op jit(solution)/shard_map/pack/pallas_call | solution.py:51
  31.5 8.1 %collective-permute-start.6 = (bf16[128,1024]{1,0:T(8,128)(2,1)}, bf16[128,1024]{1,0:T(8,128)(2,1)}, u32[]{:S(2)}, u32[]{:S(2)}) collective-permute-start(bf16[128,1024]{1,0:T(8,128)(2,1)} %pack.19), channel_id=1, source_target_pairs={{0,20},{4,16},{8,28},{12,24},{16,4},{20,0},{24,12},{28,8},{1,21},{... | collective-permute-start | bytes 786440 | tf_op jit(solution)/shard_map/ppermute | solution.py:245
  39.5 0.6 dynamic_slice.6
  42.0 1.3 %dynamic_slice.7 = f32[1]{0:T(128)} dynamic-slice(f32[1000]{0:T(1024)} %param.7, s32[]{:T(128)S(6)} %select_n.25), dynamic_slice_sizes={1} | dynamic-slice | bytes 12 | tf_op jit(solution)/shard_map/dynamic_slice | solution.py:259
  44.0 0.0 copy-start.3
  44.0 1.2 %copy-done.3 = bf16[2,4096,64]{1,2,0:T(8,128)(2,1)S(1)} copy-done((bf16[2,4096,64]{1,2,0:T(8,128)(2,1)S(1)}, bf16[2,4096,64]{1,2,0:T(8,128)(2,1)}, u32[]{:S(2)}) %copy-start.3) | copy-done | bytes 1048600
  45.2 0.8 pack.12.refs_0_
  46.0 0.6 pack.23.refs_8_
  46.6 0.8 collective-permute-start.10
  47.3 0.6 pack.22.refs_9_
  47.9 4.1 %collective-permute-start.9 = (bf16[128,256]{1,0:T(8,128)(2,1)S(1)}, bf16[128,256]{1,0:T(8,128)(2,1)S(1)}, u32[]{:S(2)}, u32[]{:S(2)}) collective-permute-start(bf16[128,256]{1,0:T(8,128)(2,1)S(1)} %pack.22.refs_9_), channel_id=1, source_target_pairs={{0,24},{4,28},{8,16},{12,20},{16,8},{20,12},{24,0},{28,4},{1,25},{... | collective-permute-start | bytes 196616 | tf_op jit(solution)/shard_map/ppermute | solution.py:245
  52.0 0.6 pack.20.refs_11_
  52.5 0.0 copy-start.8
  52.5 0.1 collective-permute-start.7
  52.6 7.9 %collective-permute-done.6.refs_0_.refs_5_ = bf16[128,1024]{1,0:T(8,128)(2,1)} collective-permute-done((bf16[128,1024]{1,0:T(8,128)(2,1)}, bf16[128,1024]{1,0:T(8,128)(2,1)}, u32[]{:S(2)}, u32[]{:S(2)}) %collective-permute-start.6) | collective-permute-done | bytes 262176 | tf_op jit(solution)/shard_map/ppermute | solution.py:245
  60.5 0.6 pack.21.refs_10_
  61.1 0.1 collective-permute-start.8
  61.2 6.0 %attend.2.refs_12_ = f32[8,64,128]{2,1,0:T(8,128)S(1)} custom-call(s32[4]{0:T(128)S(1)} %copy-done.8, f32[1]{0:T(128)} %bitcast.2.factor_ref, s32[1]{0:T(128)} %bitcast.3.me_ref, bf16[128,1280]{1,0:T(8,128)(2,1)S(1)} %pack.12.refs_0_, bf16[128,1280]{1,0:T(8,128)(2,1)} %collective-permute-done.refs_0_.refs_1_, ...), custom_call_target="tpu_custom_call" | custom-call | flops 1207959552 | bytes 2359296 | tf_op jit(solution)/shard_map/attend/pallas_call | solution.py:222
  67.3 2.7 %attend.3 = (f32[4,64,128]{2,1,0:T(8,128)S(1)}, bf16[4,64,128]{2,1,0:T(8,128)(2,1)S(1)}) custom-call(s32[4]{0:T(128)S(1)} %copy-done.8, f32[1]{0:T(128)} %bitcast.2.factor_ref, s32[1]{0:T(128)} %bitcast.3.me_ref, bf16[128,1280]{1,0:T(8,128)(2,1)S(1)} %pack.12.refs_0_, bf16[128,1280]{1,0:T(8,128)(2,1)} %collective-permute-done.refs_0_.refs_1_, ...), custom_call_target="tpu_custom_call" | custom-call | flops 402653184 | bytes 786432 | tf_op jit(solution)/shard_map/attend/pallas_call | solution.py:222
  69.9 1.4 %collective-permute-start.11 = (bf16[4,64,128]{2,1,0:T(8,128)(2,1)S(1)}, bf16[4,64,128]{2,1,0:T(8,128)(2,1)S(1)}, u32[]{:S(2)}, u32[]{:S(2)}) collective-permute-start(bf16[4,64,128]{2,1,0:T(8,128)(2,1)S(1)} %get-tuple-element.8), channel_id=1, source_target_pairs={{0,4},{4,0},{8,12},{12,8},{16,20},{20,16},{24,28},{28,24},{1,5},{5... | collective-permute-start | bytes 196616 | tf_op jit(solution)/shard_map/ppermute | solution.py:245
  71.3 2.9 %collective-permute-done.11 = bf16[4,64,128]{2,1,0:T(8,128)(2,1)S(1)} collective-permute-done((bf16[4,64,128]{2,1,0:T(8,128)(2,1)S(1)}, bf16[4,64,128]{2,1,0:T(8,128)(2,1)S(1)}, u32[]{:S(2)}, u32[]{:S(2)}) %collective-permute-start.11) | collective-permute-done | bytes 65568 | tf_op jit(solution)/shard_map/ppermute | solution.py:245
  74.3 5.0 %collective-permute-start.12 = (f32[1,64,128]{2,1,0:T(8,128)S(1)}, f32[1,64,128]{2,1,0:T(8,128)S(1)}, u32[]{:S(2)}, u32[]{:S(2)}) collective-permute-start(f32[1,64,128]{2,1,0:T(8,128)S(1)} %get-tuple-element.9), channel_id=1, source_target_pairs={{0,24},{4,28},{8,16},{12,20},{16,8},{20,12},{24,0},{28,4},{1,25},{... | collective-permute-start | bytes 98312 | tf_op jit(solution)/shard_map/ppermute | solution.py:245
  79.3 0.6 collective-permute-start.13
  79.9 1.4 %collective-permute-start.14 = (f32[1,64,128]{2,1,0:T(8,128)S(1)}, f32[1,64,128]{2,1,0:T(8,128)S(1)}, u32[]{:S(2)}, u32[]{:S(2)}) collective-permute-start(f32[1,64,128]{2,1,0:T(8,128)S(1)} %get-tuple-element.10), channel_id=1, source_target_pairs={{0,16},{4,20},{8,24},{12,28},{16,0},{20,4},{24,8},{28,12},{1,17},{... | collective-permute-start | bytes 98312 | tf_op jit(solution)/shard_map/ppermute | solution.py:245
  81.3 1.9 %collective-permute-done.13 = f32[1,64,128]{2,1,0:T(8,128)S(1)} collective-permute-done((f32[1,64,128]{2,1,0:T(8,128)S(1)}, f32[1,64,128]{2,1,0:T(8,128)S(1)}, u32[]{:S(2)}, u32[]{:S(2)}) %collective-permute-start.13) | collective-permute-done | bytes 32800 | tf_op jit(solution)/shard_map/ppermute | solution.py:245
  83.2 1.5 %collective-permute-done.14 = f32[1,64,128]{2,1,0:T(8,128)S(1)} collective-permute-done((f32[1,64,128]{2,1,0:T(8,128)S(1)}, f32[1,64,128]{2,1,0:T(8,128)S(1)}, u32[]{:S(2)}, u32[]{:S(2)}) %collective-permute-start.14) | collective-permute-done | bytes 32800 | tf_op jit(solution)/shard_map/ppermute | solution.py:245
  84.7 0.1 collective-permute-start.15
  84.8 1.6 %collective-permute-start.16 = (f32[64,128]{1,0:T(8,128)S(1)}, f32[64,128]{1,0:T(8,128)S(1)}, u32[]{:S(2)}, u32[]{:S(2)}) collective-permute-start(f32[64,128]{1,0:T(8,128)S(1)} %fusion.2), channel_id=1, source_target_pairs={{0,2},{1,3},{2,0},{3,1},{4,6},{5,7},{6,4},{7,5},{8,10},{9,11},{10,... | collective-permute-start | bytes 98312 | tf_op jit(solution)/shard_map/ppermute | solution.py:245
  86.4 0.3 collective-permute-start.17
  86.7 1.8 %collective-permute-done.15 = f32[64,128]{1,0:T(8,128)S(1)} collective-permute-done((f32[64,128]{1,0:T(8,128)S(1)}, f32[64,128]{1,0:T(8,128)S(1)}, u32[]{:S(2)}, u32[]{:S(2)}) %collective-permute-start.15) | collective-permute-done | bytes 32800 | tf_op jit(solution)/shard_map/ppermute | solution.py:245
  88.4 0.4 collective-permute-done.16
  88.9 0.6 add_bitcast_fusion
  (29 shorter events, 0.1 us)
Async XLA Ops:
  0.1 1.9 %copy-start = (bf16[1,128,12288]{2,1,0:T(8,128)(2,1)S(1)}, bf16[1,128,12288]{2,1,0:T(8,128)(2,1)}, u32[]{:S(2)}) copy-start(bf16[1,128,12288]{2,1,0:T(8,128)(2,1)} %qkv_ref.23) | copy-start | bytes 9437188
  2.0 1.2 %copy-start.2 = (bf16[2,4096,64]{1,2,0:T(8,128)(2,1)S(1)}, bf16[2,4096,64]{1,2,0:T(8,128)(2,1)}, u32[]{:S(2)}) copy-start(bf16[2,4096,64]{1,2,0:T(8,128)(2,1)} %param.6) | copy-start | bytes 3145732
  4.0 15.1 %collective-permute-start.3 = (bf16[128,1024]{1,0:T(8,128)(2,1)S(1)}, bf16[128,1024]{1,0:T(8,128)(2,1)S(1)}, u32[]{:S(2)}, u32[]{:S(2)}) collective-permute-start(bf16[128,1024]{1,0:T(8,128)(2,1)S(1)} %pack.16), channel_id=1, source_target_pairs={{0,24},{4,28},{8,16},{12,20},{16,8},{20,12},{24,0},{28,4},{1,25},{... | collective-permute-start | bytes 786440 | tf_op jit(solution)/shard_map/ppermute | solution.py:245
  9.9 20.1 %collective-permute-start.5 = (bf16[128,1024]{1,0:T(8,128)(2,1)S(1)}, bf16[128,1024]{1,0:T(8,128)(2,1)S(1)}, u32[]{:S(2)}, u32[]{:S(2)}) collective-permute-start(bf16[128,1024]{1,0:T(8,128)(2,1)S(1)} %pack.18), channel_id=1, source_target_pairs={{0,28},{4,24},{8,20},{12,16},{16,12},{20,8},{24,4},{28,0},{1,29},{... | collective-permute-start | bytes 786440 | tf_op jit(solution)/shard_map/ppermute | solution.py:245
  12.6 34.8 %collective-permute-start.1 = (bf16[128,1280]{1,0:T(8,128)(2,1)}, bf16[128,1280]{1,0:T(8,128)(2,1)S(1)}, u32[]{:S(2)}, u32[]{:S(2)}) collective-permute-start(bf16[128,1280]{1,0:T(8,128)(2,1)} %pack.14), channel_id=1, source_target_pairs={{0,8},{4,12},{8,0},{12,4},{16,24},{20,28},{24,16},{28,20},{1,9},{5... | collective-permute-start | bytes 983048 | tf_op jit(solution)/shard_map/ppermute | solution.py:245
  14.1 31.9 %collective-permute-start = (bf16[128,1280]{1,0:T(8,128)(2,1)}, bf16[128,1280]{1,0:T(8,128)(2,1)}, u32[]{:S(2)}, u32[]{:S(2)}) collective-permute-start(bf16[128,1280]{1,0:T(8,128)(2,1)} %pack.13), channel_id=1, source_target_pairs={{0,4},{4,0},{8,12},{12,8},{16,20},{20,16},{24,28},{28,24},{1,5},{5... | collective-permute-start | bytes 983048 | tf_op jit(solution)/shard_map/ppermute | solution.py:245
  15.9 45.2 %collective-permute-start.2 = (bf16[128,1280]{1,0:T(8,128)(2,1)}, bf16[128,1280]{1,0:T(8,128)(2,1)}, u32[]{:S(2)}, u32[]{:S(2)}) collective-permute-start(bf16[128,1280]{1,0:T(8,128)(2,1)} %pack.15), channel_id=1, source_target_pairs={{0,12},{4,8},{8,4},{12,0},{16,28},{20,24},{24,20},{28,16},{1,13},{... | collective-permute-start | bytes 983048 | tf_op jit(solution)/shard_map/ppermute | solution.py:245
  19.0 12.4 %copy-start.4 = (bf16[128,1024]{1,0:T(8,128)(2,1)}, bf16[128,1024]{1,0:T(8,128)(2,1)S(1)}, u32[]{:S(2)}) copy-start(bf16[128,1024]{1,0:T(8,128)(2,1)S(1)} %collective-permute-done.3.refs_0_.refs_6_) | copy-start | bytes 786436
  20.5 19.0 %copy-start.9 = (s32[2]{0:T(128)S(1)}, s32[2]{0:T(128)}, u32[]{:S(2)}) copy-start(s32[2]{0:T(128)} %param.8) | copy-start | bytes 28
  20.5 23.5 %copy-start.1 = (bf16[1,128,12288]{2,1,0:T(8,128)(2,1)S(1)}, bf16[1,128,12288]{2,1,0:T(8,128)(2,1)}, u32[]{:S(2)}) copy-start(bf16[1,128,12288]{2,1,0:T(8,128)(2,1)} %qkv_ref.23) | copy-start | bytes 9437188
  20.5 31.4 %collective-permute-start.4 = (bf16[128,1024]{1,0:T(8,128)(2,1)}, bf16[128,1024]{1,0:T(8,128)(2,1)}, u32[]{:S(2)}, u32[]{:S(2)}) collective-permute-start(bf16[128,1024]{1,0:T(8,128)(2,1)} %pack.17), channel_id=1, source_target_pairs={{0,16},{4,20},{8,24},{12,28},{16,0},{20,4},{24,8},{28,12},{1,17},{... | collective-permute-start | bytes 786440 | tf_op jit(solution)/shard_map/ppermute | solution.py:245
  30.0 1.5 %copy-start.6 = (bf16[128,1024]{1,0:T(8,128)(2,1)}, bf16[128,1024]{1,0:T(8,128)(2,1)S(1)}, u32[]{:S(2)}) copy-start(bf16[128,1024]{1,0:T(8,128)(2,1)S(1)} %collective-permute-done.5.refs_0_.refs_7_) | copy-start | bytes 786436
  31.5 29.1 %collective-permute-start.6 = (bf16[128,1024]{1,0:T(8,128)(2,1)}, bf16[128,1024]{1,0:T(8,128)(2,1)}, u32[]{:S(2)}, u32[]{:S(2)}) collective-permute-start(bf16[128,1024]{1,0:T(8,128)(2,1)} %pack.19), channel_id=1, source_target_pairs={{0,20},{4,16},{8,28},{12,24},{16,4},{20,0},{24,12},{28,8},{1,21},{... | collective-permute-start | bytes 786440 | tf_op jit(solution)/shard_map/ppermute | solution.py:245
  44.0 1.2 %copy-start.3 = (bf16[2,4096,64]{1,2,0:T(8,128)(2,1)S(1)}, bf16[2,4096,64]{1,2,0:T(8,128)(2,1)}, u32[]{:S(2)}) copy-start(bf16[2,4096,64]{1,2,0:T(8,128)(2,1)} %param.6) | copy-start | bytes 3145732
  46.6 20.7 %collective-permute-start.10 = (bf16[128,256]{1,0:T(8,128)(2,1)S(1)}, bf16[128,256]{1,0:T(8,128)(2,1)S(1)}, u32[]{:S(2)}, u32[]{:S(2)}) collective-permute-start(bf16[128,256]{1,0:T(8,128)(2,1)S(1)} %pack.23.refs_8_), channel_id=1, source_target_pairs={{0,28},{4,24},{8,20},{12,16},{16,12},{20,8},{24,4},{28,0},{1,29},{... | collective-permute-start | bytes 196616 | tf_op jit(solution)/shard_map/ppermute | solution.py:245
  47.9 19.3 %collective-permute-start.9 = (bf16[128,256]{1,0:T(8,128)(2,1)S(1)}, bf16[128,256]{1,0:T(8,128)(2,1)S(1)}, u32[]{:S(2)}, u32[]{:S(2)}) collective-permute-start(bf16[128,256]{1,0:T(8,128)(2,1)S(1)} %pack.22.refs_9_), channel_id=1, source_target_pairs={{0,24},{4,28},{8,16},{12,20},{16,8},{20,12},{24,0},{28,4},{1,25},{... | collective-permute-start | bytes 196616 | tf_op jit(solution)/shard_map/ppermute | solution.py:245
  52.5 8.7 %copy-start.5 = (bf16[128,1024]{1,0:T(8,128)(2,1)S(1)}, bf16[128,1024]{1,0:T(8,128)(2,1)}, u32[]{:S(2)}) copy-start(bf16[128,1024]{1,0:T(8,128)(2,1)} %copy-done.4) | copy-start | bytes 786436
  52.5 8.7 %copy-start.7 = (bf16[128,1024]{1,0:T(8,128)(2,1)S(1)}, bf16[128,1024]{1,0:T(8,128)(2,1)}, u32[]{:S(2)}) copy-start(bf16[128,1024]{1,0:T(8,128)(2,1)} %copy-done.6) | copy-start | bytes 786436
  52.5 8.7 %copy-start.8 = (s32[4]{0:T(128)S(1)}, s32[4]{0:T(128)}, u32[]{:S(2)}) copy-start(s32[4]{0:T(128)} %frames_ref.3) | copy-start | bytes 52
  52.5 14.7 %collective-permute-start.7 = (bf16[128,256]{1,0:T(8,128)(2,1)S(1)}, bf16[128,256]{1,0:T(8,128)(2,1)S(1)}, u32[]{:S(2)}, u32[]{:S(2)}) collective-permute-start(bf16[128,256]{1,0:T(8,128)(2,1)S(1)} %pack.20.refs_11_), channel_id=1, source_target_pairs={{0,16},{4,20},{8,24},{12,28},{16,0},{20,4},{24,8},{28,12},{1,17},{... | collective-permute-start | bytes 196616 | tf_op jit(solution)/shard_map/ppermute | solution.py:245
  61.1 6.2 %collective-permute-start.8 = (bf16[128,256]{1,0:T(8,128)(2,1)S(1)}, bf16[128,256]{1,0:T(8,128)(2,1)S(1)}, u32[]{:S(2)}, u32[]{:S(2)}) collective-permute-start(bf16[128,256]{1,0:T(8,128)(2,1)S(1)} %pack.21.refs_10_), channel_id=1, source_target_pairs={{0,20},{4,16},{8,28},{12,24},{16,4},{20,0},{24,12},{28,8},{1,21},{... | collective-permute-start | bytes 196616 | tf_op jit(solution)/shard_map/ppermute | solution.py:245
  69.9 4.3 %collective-permute-start.11 = (bf16[4,64,128]{2,1,0:T(8,128)(2,1)S(1)}, bf16[4,64,128]{2,1,0:T(8,128)(2,1)S(1)}, u32[]{:S(2)}, u32[]{:S(2)}) collective-permute-start(bf16[4,64,128]{2,1,0:T(8,128)(2,1)S(1)} %get-tuple-element.8), channel_id=1, source_target_pairs={{0,4},{4,0},{8,12},{12,8},{16,20},{20,16},{24,28},{28,24},{1,5},{5... | collective-permute-start | bytes 196616 | tf_op jit(solution)/shard_map/ppermute | solution.py:245
  74.3 7.0 %collective-permute-start.12 = (f32[1,64,128]{2,1,0:T(8,128)S(1)}, f32[1,64,128]{2,1,0:T(8,128)S(1)}, u32[]{:S(2)}, u32[]{:S(2)}) collective-permute-start(f32[1,64,128]{2,1,0:T(8,128)S(1)} %get-tuple-element.9), channel_id=1, source_target_pairs={{0,24},{4,28},{8,16},{12,20},{16,8},{20,12},{24,0},{28,4},{1,25},{... | collective-permute-start | bytes 98312 | tf_op jit(solution)/shard_map/ppermute | solution.py:245
  79.3 3.9 %collective-permute-start.13 = (f32[1,64,128]{2,1,0:T(8,128)S(1)}, f32[1,64,128]{2,1,0:T(8,128)S(1)}, u32[]{:S(2)}, u32[]{:S(2)}) collective-permute-start(f32[1,64,128]{2,1,0:T(8,128)S(1)} %get-tuple-element.11), channel_id=1, source_target_pairs={{0,8},{4,12},{8,0},{12,4},{16,24},{20,28},{24,16},{28,20},{1,9},{5... | collective-permute-start | bytes 98312 | tf_op jit(solution)/shard_map/ppermute | solution.py:245
  79.9 4.8 %collective-permute-start.14 = (f32[1,64,128]{2,1,0:T(8,128)S(1)}, f32[1,64,128]{2,1,0:T(8,128)S(1)}, u32[]{:S(2)}, u32[]{:S(2)}) collective-permute-start(f32[1,64,128]{2,1,0:T(8,128)S(1)} %get-tuple-element.10), channel_id=1, source_target_pairs={{0,16},{4,20},{8,24},{12,28},{16,0},{20,4},{24,8},{28,12},{1,17},{... | collective-permute-start | bytes 98312 | tf_op jit(solution)/shard_map/ppermute | solution.py:245
  84.7 3.7 %collective-permute-start.15 = (f32[64,128]{1,0:T(8,128)S(1)}, f32[64,128]{1,0:T(8,128)S(1)}, u32[]{:S(2)}, u32[]{:S(2)}) collective-permute-start(f32[64,128]{1,0:T(8,128)S(1)} %fusion.2), channel_id=1, source_target_pairs={{0,3},{1,2},{2,1},{3,0},{4,7},{5,6},{6,5},{7,4},{8,11},{9,10},{10,... | collective-permute-start | bytes 98312 | tf_op jit(solution)/shard_map/ppermute | solution.py:245
  84.8 4.0 %collective-permute-start.16 = (f32[64,128]{1,0:T(8,128)S(1)}, f32[64,128]{1,0:T(8,128)S(1)}, u32[]{:S(2)}, u32[]{:S(2)}) collective-permute-start(f32[64,128]{1,0:T(8,128)S(1)} %fusion.2), channel_id=1, source_target_pairs={{0,2},{1,3},{2,0},{3,1},{4,6},{5,7},{6,4},{7,5},{8,10},{9,11},{10,... | collective-permute-start | bytes 98312 | tf_op jit(solution)/shard_map/ppermute | solution.py:245
  86.4 2.5 %collective-permute-start.17 = (f32[64,128]{1,0:T(8,128)S(1)}, f32[64,128]{1,0:T(8,128)S(1)}, u32[]{:S(2)}, u32[]{:S(2)}) collective-permute-start(f32[64,128]{1,0:T(8,128)S(1)} %fusion.2), channel_id=1, source_target_pairs={{0,1},{1,0},{2,3},{3,2},{4,5},{5,4},{6,7},{7,6},{8,9},{9,8},{10,11... | collective-permute-start | bytes 98312 | tf_op jit(solution)/shard_map/ppermute | solution.py:245

commit v8 on v0

v8 whole, which is shorter than its diff:
```python
import functools
import math

import jax
import jax.numpy as jnp
from jax import lax
from jax.experimental import pallas as pl
from jax.experimental.pallas import tpu as pltpu
from jax.sharding import PartitionSpec as P

HEADS = 32
HD = 128
FRAME_TOK = 64
NT = (((1,), (1,)), ((), ()))
LOG2_SCALE = math.log2(math.e) / math.sqrt(HD)
LOWEST = -1e30
SECOND_WAVE = 3000000000
PACK_VMEM = 8 * 1024 * 1024
ATTEND_VMEM = 20 * 1024 * 1024
WHOLE_VMEM = 60 * 1024 * 1024
SMEM = pl.BlockSpec(memory_space=pltpu.SMEM)
VMEM = pl.BlockSpec(memory_space=pltpu.VMEM)
ANYWHERE = pl.BlockSpec(memory_space=pl.ANY)


def fold(readout, values):
    return lax.dot_general(readout, values, NT, preferred_element_type=jnp.float32).astype(jnp.bfloat16)


def value_place(h, count, lat):
    return (h * lat) % HD, count * 2 * HD + (h * lat // HD) * HD


def pack_near_kernel(split, place_ref, qkv_ref, readout_ref, whole_qkv_ref, whole_readout_ref, *refs):
    out_ref = refs[-1]
    lat = readout_ref.shape[1]
    for h in range(split + 1):
        source, rows, base = (qkv_ref, readout_ref, h) if h < split else (whole_qkv_ref, whole_readout_ref, 0)
        out_ref[:, h * 2 * HD : (h + 1) * 2 * HD] = source[0, :, base * 3 * HD : base * 3 * HD + 2 * HD]
        row, column = value_place(h, split + 1, lat)
        out_ref[row : row + lat, column : column + HD] = fold(
            rows[0, :, base * HD : (base + 1) * HD], source[0, :, base * 3 * HD + 2 * HD : (base + 1) * 3 * HD]
        )


def pack_far_kernel(count, place_ref, qkv_ref, *refs):
    for h in range(count):
        refs[-1][:, h * HD : (h + 1) * HD] = qkv_ref[0, :, h * 3 * HD : h * 3 * HD + HD]


def pack_whole_kernel(place_ref, qkv_ref, readout_ref, *refs):
    out_ref = refs[-1]
    rows = qkv_ref.shape[1]
    lat = readout_ref.shape[1]
    out_ref[:rows] = qkv_ref[0, :, : 2 * HD]
    folded = fold(readout_ref[0], qkv_ref[0, :, 2 * HD :])
    out_ref[rows:, :HD] = folded[: lat // 2]
    out_ref[rows:, HD:] = folded[lat // 2 :]


def pack(kind, place, qkv, readout_t, k, half, pair_heads, split, after):
    rows = qkv.shape[1]
    lat = readout_t.shape[1]

    def pair(m):
        return (m[0] ^ k) & (half - 1)

    def whole(m):
        return pair(m) * pair_heads + split + (m[0] ^ k) // half

    slab = pl.BlockSpec((1, rows, pair_heads * 3 * HD), lambda g, m: (0, 0, pair(m)))
    whole_specs = [
        pl.BlockSpec((1, rows, 3 * HD), lambda g, m: (0, 0, whole(m))),
        pl.BlockSpec((1, lat, HD), lambda g, m: (m[1], 0, whole(m))),
    ]
    if kind == "near":
        kernel = functools.partial(pack_near_kernel, split)
        shape = (rows, (split + 1) * 2 * HD + -(-(split + 1) * lat // HD) * HD)
        in_specs = [slab, pl.BlockSpec((1, lat, pair_heads * HD), lambda g, m: (m[1], 0, pair(m)))] + whole_specs
    elif kind == "far":
        kernel = functools.partial(pack_far_kernel, split)
        shape = (rows, split * HD)
        in_specs = [slab]
    else:
        kernel = pack_whole_kernel
        shape = (rows + lat // 2, 2 * HD)
        in_specs = whole_specs
    operands = [place] + ([qkv, readout_t] * 2)[: len(in_specs)]
    if after is not None:
        operands += [after]
        in_specs += [ANYWHERE]
    return pl.pallas_call(
        kernel,
        grid_spec=pltpu.PrefetchScalarGridSpec(
            num_scalar_prefetch=1,
            grid=(1,),
            in_specs=in_specs,
            out_specs=pl.BlockSpec(shape, lambda g, m: (0, 0)),
        ),
        out_shape=jax.ShapeDtypeStruct(shape, jnp.bfloat16),
        compiler_params=pltpu.CompilerParams(vmem_limit_bytes=PACK_VMEM),
        cost_estimate=pl.CostEstimate(
            flops=SECOND_WAVE if kind == "far" and after is not None else 0,
            bytes_accessed=shape[0] * shape[1] * 4,
            transcendentals=0,
        ),
        name="pack",
    )(*operands)


def place_of(me, n, bits):
    k = jnp.int32(0)
    for bit in range(bits):
        k = k | (((n >> bit) & 1) << (bits - 1 - bit))
    return me ^ k


def mask_rows(frames_ref, me, rows, bits, key_count, b):
    columns = lax.broadcasted_iota(jnp.int32, (1, rows), 1)
    places = jnp.concatenate([place_of(me, b * 2 + j, bits) * rows + columns for j in range(2)], axis=1)
    end = frames_ref[0] * FRAME_TOK
    bound = jnp.full((1, 2 * rows), end, jnp.int32)
    for c in range(1, frames_ref.shape[0]):
        later = end + frames_ref[c] * FRAME_TOK
        bound = jnp.where(places >= end, later, bound)
        end = later
    return [
        jnp.where((me ^ k) * rows + start < bound, 0.0, -jnp.inf)
        for k in range(key_count)
        for start in range(0, rows, FRAME_TOK)
    ]


def run_units(work, tiles, tile, score_tile, masks, folded, finish):
    lat = folded.shape[1] - 16
    frames = [score_tile(*work[0], t) for t in range(tiles)]
    shifts = None
    for u, (b, i) in enumerate(work):
        if u == 0 or b is not work[u - 1][0]:
            shifts = masks(b)
        each = len(frames[0])
        peaks = [jnp.max(f, axis=0, keepdims=True) + s for f, s in zip(sum(frames, []), shifts)]
        peak = jnp.maximum(functools.reduce(jnp.maximum, peaks), LOWEST)
        following, summed = [], None
        for t in range(tiles):
            if u + 1 < len(work):
                following.append(score_tile(*work[u + 1], t))
            weights = [
                jnp.exp2((f + (s - peak)) * LOG2_SCALE).astype(jnp.bfloat16)
                for f, s in zip(frames[t], shifts[t * each : (t + 1) * each])
            ]
            part = jnp.dot(
                folded[i, :, t * tile : (t + 1) * tile],
                jnp.concatenate(weights, axis=0),
                preferred_element_type=jnp.float32,
            )
            summed = part if summed is None else summed + part
        finish(b, i, summed[:lat], summed[lat : lat + 1], peak)
        frames = following


def score_tiles(asked, keys_of, rows):
    def score_tile(b, i, t):
        queries = asked[pl.ds(b * 2, 2), i].reshape(2 * rows, HD)
        keys = jnp.concatenate([keys_of(2 * t + j, i) for j in range(2)], axis=0)
        scores = lax.dot_general(keys, queries, NT, preferred_element_type=jnp.float32)
        return [scores[start : start + FRAME_TOK] for start in range(0, 2 * rows, FRAME_TOK)]

    return score_tile


def split_kernel(seq_count, count, order, frames_ref, me_ref, *refs):
    half = seq_count // 2
    near_refs, far_refs = refs[:half], refs[half:seq_count]
    sums_ref, stats_ref, asked, folded = refs[-4:]
    me = me_ref[0]
    rows = near_refs[0].shape[0]
    lat = sums_ref.shape[2]
    bits = seq_count.bit_length() - 1
    for n, k in enumerate(order):
        for i in range(count):
            if k < half:
                asked[n, i] = near_refs[k][:, i * 2 * HD : i * 2 * HD + HD]
            else:
                asked[n, i] = far_refs[k - half][:, i * HD : (i + 1) * HD]
    for i in range(count):
        row, column = value_place(i, count + 1, lat)
        for k in range(half):
            folded[i, :lat, k * rows : (k + 1) * rows] = near_refs[k][row : row + lat, column : column + HD]
        folded[i, lat:] = jnp.ones_like(folded[i, lat:])

    def keys_of(k, i):
        return near_refs[k][:, i * 2 * HD + HD : (i + 1) * 2 * HD]

    def some_blocks(b, carry):
        peaks, totals = [], []

        def finish(b, i, summed, total, peak):
            sums_ref[b, i] = summed
            peaks.append(peak)
            totals.append(total)

        work = [(b, i) for i in range(count)]
        run_units(
            work, half // 2, 2 * rows, score_tiles(asked, keys_of, rows),
            lambda b: mask_rows(frames_ref, me, rows, bits, half, b), folded, finish,
        )
        rest = [jnp.ones_like(peaks[0])] * (stats_ref.shape[2] - count)
        stats_ref[b, 0] = jnp.concatenate(peaks + rest, axis=0)
        stats_ref[b, 1] = jnp.concatenate(totals + rest, axis=0)
        return carry

    lax.fori_loop(0, half, some_blocks, 0)


def attend_split(near, far, after, span_frames, me, count, lat, order):
    half = len(near)
    rows = near[0].shape[0]
    seq_count = 2 * half
    tokens = seq_count * rows
    padded = -(-count // 8) * 8
    return pl.pallas_call(
        functools.partial(split_kernel, seq_count, count, order),
        in_specs=[SMEM, SMEM] + [VMEM] * seq_count + [ANYWHERE] * len(after),
        out_specs=[VMEM, VMEM],
        out_shape=[
            jax.ShapeDtypeStruct((half, count, lat, 2 * rows), jnp.float32),
            jax.ShapeDtypeStruct((half, 2, padded, 2 * rows), jnp.float32),
        ],
        scratch_shapes=[
            pltpu.VMEM((seq_count, count, rows, HD), jnp.bfloat16),
            pltpu.VMEM((count, lat + 16, half * rows), jnp.bfloat16),
        ],
        compiler_params=pltpu.CompilerParams(vmem_limit_bytes=ATTEND_VMEM),
        cost_estimate=pl.CostEstimate(
            flops=0, bytes_accessed=tokens * count * 3 * HD * 2, transcendentals=0
        ),
        name="attend_split",
    )(span_frames, me, *near, *far, *after)


def combine_kernel(count, sums_ref, stats_ref, other_ref, out_ref):
    rows = out_ref.shape[2]

    def one_block(b, carry):
        peak, total = stats_ref[b, 0], stats_ref[b, 1]
        swapped = [jnp.concatenate([other_ref[b, w, :, rows:], other_ref[b, w, :, :rows]], axis=1) for w in range(2)]
        highest = jnp.maximum(peak, swapped[0])
        own = jnp.exp2((peak - highest) * LOG2_SCALE)
        both = total * own + swapped[1] * jnp.exp2((swapped[0] - highest) * LOG2_SCALE)
        weight = own / both
        result = sums_ref[b, 0] * weight[:1]
        for i in range(1, count):
            result = result + sums_ref[b, i] * weight[i : i + 1]
        for j in range(2):
            out_ref[b * 2 + j] = result[:, j * rows : (j + 1) * rows]
        return carry

    lax.fori_loop(0, sums_ref.shape[0], one_block, 0)


def combine(sums, stats, other):
    half, count, lat, block = sums.shape
    return pl.pallas_call(
        functools.partial(combine_kernel, count),
        in_specs=[VMEM] * 3,
        out_specs=VMEM,
        out_shape=jax.ShapeDtypeStruct((2 * half, lat, block // 2), jnp.float32),
        compiler_params=pltpu.CompilerParams(vmem_limit_bytes=PACK_VMEM),
        cost_estimate=pl.CostEstimate(flops=0, bytes_accessed=sums.size * 4, transcendentals=0),
        name="combine",
    )(sums, stats, other)


def whole_kernel(seq_count, split, order, frames_ref, factor_ref, me_ref, *refs):
    half = seq_count // 2
    pieces = refs[:seq_count]
    earlier = refs[seq_count] if len(refs) > seq_count + 4 else None
    keep_ref, give_ref, asked, folded = refs[-4:]
    me = me_ref[0]
    rows = keep_ref.shape[2]
    lat = keep_ref.shape[1]
    bits = seq_count.bit_length() - 1
    start = split * 2 * HD

    def cell(k, what):
        column = what * HD + (start if k < half else 0)
        return pieces[k][:rows, column : column + HD]

    for n, k in enumerate(order):
        asked[n, 0] = cell(k, 0)
    for k in range(seq_count):
        if k < half:
            row, column = value_place(split, split + 1, lat)
            folded[0, :lat, k * rows : (k + 1) * rows] = pieces[k][row : row + lat, column : column + HD]
        else:
            folded[0, : lat // 2, k * rows : (k + 1) * rows] = pieces[k][rows:, :HD]
            folded[0, lat // 2 : lat, k * rows : (k + 1) * rows] = pieces[k][rows:, HD:]
    folded[0, lat:] = jnp.ones_like(folded[0, lat:])

    def finish(b, i, summed, total, peak):
        result = summed / total
        for j in range(2):
            part = result[:, j * rows : (j + 1) * rows]
            n = b * 2 + j
            if earlier is not None:
                part = part + earlier[n]
            part = part * factor_ref[0]

            @pl.when(n < half)
            def _():
                keep_ref[n] = part

            @pl.when(n >= half)
            def _():
                give_ref[n - half] = part.astype(jnp.bfloat16)

    together = min(half, 4)

    def some_blocks(b, carry):
        run_units(
            [(b * together + j, 0) for j in range(together)], half, 2 * rows,
            score_tiles(asked, lambda k, i: cell(k, 1), rows),
            lambda b: mask_rows(frames_ref, me, rows, bits, seq_count, b), folded, finish,
        )
        return carry

    lax.fori_loop(0, half // together, some_blocks, 0)


def attend_whole(pieces, earlier, span_frames, factor, me, split, rows, lat, order):
    seq_count = len(pieces)
    tokens = seq_count * rows
    operands = [span_frames, factor, me] + list(pieces) + ([] if earlier is None else [earlier])
    return pl.pallas_call(
        functools.partial(whole_kernel, seq_count, split, order),
        in_specs=[SMEM] * 3 + [VMEM] * (len(operands) - 3),
        out_specs=[VMEM, VMEM],
        out_shape=[
            jax.ShapeDtypeStruct((seq_count // 2, lat, rows), jnp.float32),
            jax.ShapeDtypeStruct((seq_count // 2, lat, rows), jnp.bfloat16),
        ],
        scratch_shapes=[
            pltpu.VMEM((seq_count, 1, rows, HD), jnp.bfloat16),
            pltpu.VMEM((1, lat + 16, tokens), jnp.bfloat16),
        ],
        compiler_params=pltpu.CompilerParams(vmem_limit_bytes=ATTEND_VMEM if seq_count <= 8 else WHOLE_VMEM),
        cost_estimate=pl.CostEstimate(
            flops=tokens * tokens * 2 * (HD + lat),
            bytes_accessed=tokens * 3 * HD * 2,
            transcendentals=tokens * tokens,
        ),
        name="attend_whole",
    )(*operands)


def swap(array, axis, offset):
    size = lax.axis_size(axis)
    return lax.ppermute(array, axis, [(i, i ^ offset) for i in range(size)])


def body(qkv, readout, step_weight, timestep, span_frames):
    seq_count = lax.axis_size("seq")
    mp_count = lax.axis_size("mp")
    half = seq_count // 2
    pair_heads = 2 * HEADS // seq_count
    split = pair_heads - 2
    rows = qkv.shape[1]
    lat = readout.shape[2]
    me = lax.axis_index("seq").astype(jnp.int32)
    mp_index = lax.axis_index("mp")
    sample_count = mp_count // 2
    model_index = (mp_index // sample_count).astype(jnp.int32)
    sample_index = mp_index % sample_count
    signed = jnp.where(model_index == 1, 1.0, -1.0).astype(jnp.float32)
    factor = (signed * step_weight[timestep[sample_index]]).reshape(1)
    readout_t = jnp.swapaxes(readout, 1, 2)
    place = jnp.stack([me, model_index])
    bits = seq_count.bit_length() - 1
    order = [sum(((n >> b) & 1) << (bits - 1 - b) for b in range(bits)) for n in range(seq_count)]

    def send(kind, k, after=None):
        packed = pack(kind, place, qkv, readout_t, k, half, pair_heads, split, after)
        return packed, (swap(packed, "seq", k) if k else packed)

    near, far, whole, holds = [None] * half, [None] * half, [None] * half, []
    for n in range(half):
        k = seq_count - 1 - n
        if split:
            _, far[k - half] = send("far", k, far[k - half + 2] if n > 1 else None)
    for k in range(half):
        _, near[k] = send("near", k)
    for n in range(half):
        k = seq_count - 1 - n
        packed, whole[k - half] = send("whole", k, far[k - half] if split else None)
        holds.append(packed)
    earlier = None
    if split:
        sums, stats = attend_split(near, far, holds, span_frames, me.reshape(1), split, lat, order)
        earlier = combine(sums, stats, swap(stats, "seq", half))
    keep, give = attend_whole(near + whole, earlier, span_frames, factor, me.reshape(1), split, rows, lat, order)

    keep = keep + swap(give, "seq", 1).astype(jnp.float32)
    offset = 2
    while offset < seq_count:
        radix = min(4, seq_count // offset)
        size = keep.shape[0] // radix
        parts = [keep[n * size : (n + 1) * size] for n in range(radix)]
        keep = parts[0]
        for n in range(radix - 1, 0, -1):
            bits_n = (n >> 1) | ((n & 1) << 1) if radix == 4 else n
            keep = keep + swap(parts[n], "seq", offset * bits_n)
        offset *= radix
    total = keep[0]
    offset = 1
    while offset < mp_count:
        radix = min(4, mp_count // offset)
        own = total
        for n in range(radix - 1, 0, -1):
            total = total + swap(own, "mp", offset * n)
        offset *= radix
    return total.T


def solution(mesh):
    return jax.shard_map(
        body,
        mesh=mesh,
        in_specs=(P("mp", "seq", None), P(), P(), P(), P()),
        out_specs=P("seq", None),
        check_vma=False,
    )
```

time: 172 us -> 98.7 us (0.57); the launches traced: 174 us -> 98.5 us
  waiting for transfers between devices: 91.9 us -> 42 us
  local copies, waits for them, and re-layouts: 31.4 us -> 6.34 us
  starting transfers between devices: 11 us -> 29.8 us
  Pallas kernels: 0 us -> 16.8 us
  other arithmetic: 12.8 us -> 0.73 us
  matrix products: 11.5 us -> 0 us
  blocking collectives: 10.9 us -> 0 us
    all_to_all x2 -> x0, waiting for transfers between devices: 91.9 us -> none  [the longest x1 70.4 us: body(): lax.all_to_all(grouped, 'seq', split_axis=1, concat_axis=0, tiled=True)]
    ppermute x0 -> x19, waiting for transfers between devices: none -> 42 us  [swap(): return lax.ppermute(array, axis, [(i, i ^ offset) for i in range(size)])]
    ppermute x0 -> x19, starting transfers between devices: none -> 29.8 us  [swap(): return lax.ppermute(array, axis, [(i, i ^ offset) for i in range(size)])]
    pallas_call x0 -> x15, Pallas kernels: none -> 16.8 us  [the longest x12 8.65 us: pack(): pl.pallas_call(kernel, grid_spec=pltpu.PrefetchScalarGridSpec(num_scalar_...]
    dot_general x9 -> x0, matrix products: 11.5 us -> none  [the longest x4 7.21 us: key_block(): jnp.dot(weights, values_here, preferred_element_type=jnp.float32)]
    all_to_all x2 -> x0, starting transfers between devices: 11 us -> none  [the longest x1 7.38 us: body(): lax.all_to_all(grouped, 'seq', split_axis=1, concat_axis=0, tiled=True)]
    psum x1 -> x0, blocking collectives: 10.9 us -> none  [body(): return lax.psum(partial_sum, 'mp')]
    another operation x9 -> x0, local copies, waits for them, and re-layouts: 9.28 us -> none  [the longest x1 4.64 us: body(): grouped = own_rows.reshape(row_count, seq_count, heads_local, 3 * HD)]
  transfers between devices with their start and end apart: 2 -> 19, of which waited for: 2 -> 10; matrix products, arithmetic and copies ran while one was open for 1% -> 2% of each run, Pallas kernels for 0% -> 14%
where the time goes in v8:
time: 98.7 us; the launch traced here: 98.5 us
  waiting for transfers between devices  42 us (43%)
  starting transfers between devices  29.8 us (30%)
  Pallas kernels  16.8 us (17%)
  local copies, waits for them, and re-layouts  6.34 us (6%)
  between operations  2.78 us (3%)
    ppermute x19, waiting for transfers between devices, swap(): return lax.ppermute(array, axis, [(i, i ^ offset) for i in range(size)])  42 us
    ppermute x19, starting transfers between devices, swap(): return lax.ppermute(array, axis, [(i, i ^ offset) for i in range(size)])  29.8 us
    pallas_call x12, Pallas kernels, pack(): pl.pallas_call(kernel, grid_spec=pltpu.PrefetchScalarGridSpec(num_scalar_...  8.65 us
    pallas_call x1, Pallas kernels, attend_split(): pl.pallas_call(functools.partial(split_kernel, seq_count, count, order),...  6.02 us
    unnamed x12, local copies, waits for them, and re-layouts  4.48 us
  transfers between devices with their start and end apart: 19, of which 10 were waited for; matrix products, arithmetic and copies ran while one was open for 2% of the time, Pallas kernels for 14%

profile of v8, /device:TPU:0, one launch (start us, length us, event | category | flops | bytes accessed | tf_op | source)
XLA Modules:
  0.0 98.5 jit_solution(3746230347928149557)
XLA Ops:
  0.0 0.1 pad_add_fusion.place_ref
  0.1 1.9 %copy-done = bf16[1,128,12288]{2,1,0:T(8,128)(2,1)S(1)} copy-done((bf16[1,128,12288]{2,1,0:T(8,128)(2,1)S(1)}, bf16[1,128,12288]{2,1,0:T(8,128)(2,1)}, u32[]{:S(2)}) %copy-start) | copy-done | bytes 3145752
  2.0 0.6 pack.16
  2.6 5.1 %collective-permute-start.3 = (bf16[128,768]{1,0:T(8,128)(2,1)S(1)}, bf16[128,768]{1,0:T(8,128)(2,1)S(1)}, u32[]{:S(2)}, u32[]{:S(2)}) collective-permute-start(bf16[128,768]{1,0:T(8,128)(2,1)S(1)} %pack.16), channel_id=1, source_target_pairs={{0,24},{4,28},{8,16},{12,20},{16,8},{20,12},{24,0},{28,4},{1,25},{... | collective-permute-start | bytes 589832 | tf_op jit(solution)/shard_map/ppermute | solution.py:359
  7.7 0.9 pack.13
  8.6 1.5 %collective-permute-start = (bf16[128,2304]{1,0:T(8,128)(2,1)S(1)}, bf16[128,2304]{1,0:T(8,128)(2,1)S(1)}, u32[]{:S(2)}, u32[]{:S(2)}) collective-permute-start(bf16[128,2304]{1,0:T(8,128)(2,1)S(1)} %pack.13), channel_id=1, source_target_pairs={{0,4},{4,0},{8,12},{12,8},{16,20},{20,16},{24,28},{28,24},{1,5},{5... | collective-permute-start | bytes 1769480 | tf_op jit(solution)/shard_map/ppermute | solution.py:359
  10.1 0.9 pack.14
  11.0 0.9 pack.15
  11.9 2.0 %collective-permute-start.2 = (bf16[128,2304]{1,0:T(8,128)(2,1)S(1)}, bf16[128,2304]{1,0:T(8,128)(2,1)S(1)}, u32[]{:S(2)}, u32[]{:S(2)}) collective-permute-start(bf16[128,2304]{1,0:T(8,128)(2,1)S(1)} %pack.15), channel_id=1, source_target_pairs={{0,12},{4,8},{8,4},{12,0},{16,28},{20,24},{24,20},{28,16},{1,13},{... | collective-permute-start | bytes 1769480 | tf_op jit(solution)/shard_map/ppermute | solution.py:359
  13.9 0.6 pack.19
  14.5 1.6 %collective-permute-start.6 = (bf16[128,768]{1,0:T(8,128)(2,1)S(1)}, bf16[128,768]{1,0:T(8,128)(2,1)S(1)}, u32[]{:S(2)}, u32[]{:S(2)}) collective-permute-start(bf16[128,768]{1,0:T(8,128)(2,1)S(1)} %pack.19), channel_id=1, source_target_pairs={{0,28},{4,24},{8,20},{12,16},{16,12},{20,8},{24,4},{28,0},{1,29},{... | collective-permute-start | bytes 589832 | tf_op jit(solution)/shard_map/ppermute | solution.py:359
  16.1 0.6 pack.17
  16.7 2.4 %collective-permute-start.4 = (bf16[128,768]{1,0:T(8,128)(2,1)S(1)}, bf16[128,768]{1,0:T(8,128)(2,1)S(1)}, u32[]{:S(2)}, u32[]{:S(2)}) collective-permute-start(bf16[128,768]{1,0:T(8,128)(2,1)S(1)} %pack.17), channel_id=1, source_target_pairs={{0,16},{4,20},{8,24},{12,28},{16,0},{20,4},{24,8},{28,12},{1,17},{... | collective-permute-start | bytes 589832 | tf_op jit(solution)/shard_map/ppermute | solution.py:359
  19.1 25.1 %collective-permute-done.6.refs_0_.refs_7_ = bf16[128,768]{1,0:T(8,128)(2,1)S(1)} collective-permute-done((bf16[128,768]{1,0:T(8,128)(2,1)S(1)}, bf16[128,768]{1,0:T(8,128)(2,1)S(1)}, u32[]{:S(2)}, u32[]{:S(2)}) %collective-permute-start.6) | collective-permute-done | bytes 196640 | tf_op jit(solution)/shard_map/ppermute | solution.py:359
  44.2 0.6 pack.20
  44.8 0.1 collective-permute-start.7
  44.9 0.7 pack.22.refs_9_
  45.6 0.7 pack.23.refs_8_
  46.3 0.5 collective-permute-done.4.refs_0_.refs_4_
  46.8 3.1 %collective-permute-start.10 = (bf16[160,256]{1,0:T(8,128)(2,1)S(1)}, bf16[160,256]{1,0:T(8,128)(2,1)S(1)}, u32[]{:S(2)}, u32[]{:S(2)}) collective-permute-start(bf16[160,256]{1,0:T(8,128)(2,1)S(1)} %pack.23.refs_8_), channel_id=1, source_target_pairs={{0,28},{4,24},{8,20},{12,16},{16,12},{20,8},{24,4},{28,0},{1,29},{... | collective-permute-start | bytes 245768 | tf_op jit(solution)/shard_map/ppermute | solution.py:359
  49.9 0.7 pack.18.refs_11_
  50.6 7.5 %collective-permute-done.7.refs_0_.refs_5_ = bf16[128,768]{1,0:T(8,128)(2,1)S(1)} collective-permute-done((bf16[128,768]{1,0:T(8,128)(2,1)S(1)}, bf16[128,768]{1,0:T(8,128)(2,1)S(1)}, u32[]{:S(2)}, u32[]{:S(2)}) %collective-permute-start.7) | collective-permute-done | bytes 196640 | tf_op jit(solution)/shard_map/ppermute | solution.py:359
  58.1 3.0 %collective-permute-start.9 = (bf16[160,256]{1,0:T(8,128)(2,1)S(1)}, bf16[160,256]{1,0:T(8,128)(2,1)S(1)}, u32[]{:S(2)}, u32[]{:S(2)}) collective-permute-start(bf16[160,256]{1,0:T(8,128)(2,1)S(1)} %pack.22.refs_9_), channel_id=1, source_target_pairs={{0,24},{4,28},{8,16},{12,20},{16,8},{20,12},{24,0},{28,4},{1,25},{... | collective-permute-start | bytes 245768 | tf_op jit(solution)/shard_map/ppermute | solution.py:359
  61.1 0.7 pack.21.refs_10_
  61.9 2.9 %collective-permute-start.8 = (bf16[160,256]{1,0:T(8,128)(2,1)S(1)}, bf16[160,256]{1,0:T(8,128)(2,1)S(1)}, u32[]{:S(2)}, u32[]{:S(2)}) collective-permute-start(bf16[160,256]{1,0:T(8,128)(2,1)S(1)} %pack.21.refs_10_), channel_id=1, source_target_pairs={{0,20},{4,16},{8,28},{12,24},{16,4},{20,0},{24,12},{28,8},{1,21},{... | collective-permute-start | bytes 245768 | tf_op jit(solution)/shard_map/ppermute | solution.py:359
  64.8 0.9 pack.12.refs_0_
  65.7 6.0 %attend_split.1 = (f32[4,6,64,256]{3,2,1,0:T(8,128)S(1)}, f32[4,2,8,256]{3,2,1,0:T(8,128)S(1)}) custom-call(s32[4]{0:T(128)S(1)} %copy-done.4, s32[1]{0:T(128)} %bitcast.3.me_ref, bf16[128,2304]{1,0:T(8,128)(2,1)S(1)} %pack.12.refs_0_, bf16[128,2304]{1,0:T(8,128)(2,1)S(1)} %collective-permute-done.refs_1_, ...), custom_call_target="tpu_custom_call" | custom-call | bytes 4718592 | tf_op jit(solution)/shard_map/attend_split/pallas_call | solution.py:222
  71.8 1.2 %copy-done.2 = f32[4,6,64,256]{3,2,1,0:T(8,128)} copy-done((f32[4,6,64,256]{3,2,1,0:T(8,128)}, f32[4,6,64,256]{3,2,1,0:T(8,128)S(1)}, u32[]{:S(2)}) %copy-start.2) | copy-done | bytes 1572888
  72.9 0.1 collective-permute-start.11
  73.0 0.6 dynamic_slice.6
  75.5 1.3 %dynamic_slice.7 = f32[1]{0:T(128)} dynamic-slice(f32[1000]{0:T(1024)} %param.7, s32[]{:T(128)S(6)} %select_n.25), dynamic_slice_sizes={1} | dynamic-slice | bytes 12 | tf_op jit(solution)/shard_map/dynamic_slice | solution.py:376
  77.5 0.6 collective-permute-done.11.other_ref
  78.1 1.4 %copy-done.3 = f32[4,6,64,256]{3,2,1,0:T(8,128)S(1)} copy-done((f32[4,6,64,256]{3,2,1,0:T(8,128)S(1)}, f32[4,6,64,256]{3,2,1,0:T(8,128)}, u32[]{:S(2)}) %copy-start.3) | copy-done | bytes 1572888
  79.5 0.2 combine.1.refs_8_
  79.8 1.9 %attend_whole.1 = (f32[4,64,128]{2,1,0:T(8,128)S(1)}, bf16[4,64,128]{2,1,0:T(8,128)(2,1)S(1)}) custom-call(s32[4]{0:T(128)S(1)} %copy-done.4, f32[1]{0:T(128)} %bitcast.2.factor_ref, s32[1]{0:T(128)} %bitcast.3.me_ref, bf16[128,2304]{1,0:T(8,128)(2,1)S(1)} %pack.12.refs_0_, bf16[128,2304]{1,0:T(8,128)(2,1)S(1)} %collective-permute-done.refs_1_, ...), custom_call_target="tpu_custom_call" | custom-call | flops 402653184 | bytes 786432 | tf_op jit(solution)/shard_map/attend_whole/pallas_call | solution.py:335
  81.7 1.5 %collective-permute-start.12 = (bf16[4,64,128]{2,1,0:T(8,128)(2,1)S(1)}, bf16[4,64,128]{2,1,0:T(8,128)(2,1)S(1)}, u32[]{:S(2)}, u32[]{:S(2)}) collective-permute-start(bf16[4,64,128]{2,1,0:T(8,128)(2,1)S(1)} %get-tuple-element.12), channel_id=1, source_target_pairs={{0,4},{4,0},{8,12},{12,8},{16,20},{20,16},{24,28},{28,24},{1,5},{5... | collective-permute-start | bytes 196616 | tf_op jit(solution)/shard_map/ppermute | solution.py:359
  83.2 2.8 %collective-permute-done.12 = bf16[4,64,128]{2,1,0:T(8,128)(2,1)S(1)} collective-permute-done((bf16[4,64,128]{2,1,0:T(8,128)(2,1)S(1)}, bf16[4,64,128]{2,1,0:T(8,128)(2,1)S(1)}, u32[]{:S(2)}, u32[]{:S(2)}) %collective-permute-start.12) | collective-permute-done | bytes 65568 | tf_op jit(solution)/shard_map/ppermute | solution.py:359
  86.1 1.8 %collective-permute-start.13 = (f32[1,64,128]{2,1,0:T(8,128)S(1)}, f32[1,64,128]{2,1,0:T(8,128)S(1)}, u32[]{:S(2)}, u32[]{:S(2)}) collective-permute-start(f32[1,64,128]{2,1,0:T(8,128)S(1)} %get-tuple-element.13), channel_id=1, source_target_pairs={{0,24},{4,28},{8,16},{12,20},{16,8},{20,12},{24,0},{28,4},{1,25},{... | collective-permute-start | bytes 98312 | tf_op jit(solution)/shard_map/ppermute | solution.py:359
  87.8 1.1 %collective-permute-start.14 = (f32[1,64,128]{2,1,0:T(8,128)S(1)}, f32[1,64,128]{2,1,0:T(8,128)S(1)}, u32[]{:S(2)}, u32[]{:S(2)}) collective-permute-start(f32[1,64,128]{2,1,0:T(8,128)S(1)} %get-tuple-element.15), channel_id=1, source_target_pairs={{0,8},{4,12},{8,0},{12,4},{16,24},{20,28},{24,16},{28,20},{1,9},{5... | collective-permute-start | bytes 98312 | tf_op jit(solution)/shard_map/ppermute | solution.py:359
  88.9 1.6 %collective-permute-start.15 = (f32[1,64,128]{2,1,0:T(8,128)S(1)}, f32[1,64,128]{2,1,0:T(8,128)S(1)}, u32[]{:S(2)}, u32[]{:S(2)}) collective-permute-start(f32[1,64,128]{2,1,0:T(8,128)S(1)} %get-tuple-element.14), channel_id=1, source_target_pairs={{0,16},{4,20},{8,24},{12,28},{16,0},{20,4},{24,8},{28,12},{1,17},{... | collective-permute-start | bytes 98312 | tf_op jit(solution)/shard_map/ppermute | solution.py:359
  90.5 1.4 %collective-permute-done.13 = f32[1,64,128]{2,1,0:T(8,128)S(1)} collective-permute-done((f32[1,64,128]{2,1,0:T(8,128)S(1)}, f32[1,64,128]{2,1,0:T(8,128)S(1)}, u32[]{:S(2)}, u32[]{:S(2)}) %collective-permute-start.13) | collective-permute-done | bytes 32800 | tf_op jit(solution)/shard_map/ppermute | solution.py:359
  92.0 0.1 collective-permute-done.14
  92.1 1.6 %collective-permute-done.15 = f32[1,64,128]{2,1,0:T(8,128)S(1)} collective-permute-done((f32[1,64,128]{2,1,0:T(8,128)S(1)}, f32[1,64,128]{2,1,0:T(8,128)S(1)}, u32[]{:S(2)}, u32[]{:S(2)}) %collective-permute-start.15) | collective-permute-done | bytes 32800 | tf_op jit(solution)/shard_map/ppermute | solution.py:359
  93.8 1.6 %collective-permute-start.17 = (f32[64,128]{1,0:T(8,128)S(1)}, f32[64,128]{1,0:T(8,128)S(1)}, u32[]{:S(2)}, u32[]{:S(2)}) collective-permute-start(f32[64,128]{1,0:T(8,128)S(1)} %fusion.2), channel_id=1, source_target_pairs={{0,2},{1,3},{2,0},{3,1},{4,6},{5,7},{6,4},{7,5},{8,10},{9,11},{10,... | collective-permute-start | bytes 98312 | tf_op jit(solution)/shard_map/ppermute | solution.py:359
  95.4 0.3 collective-permute-start.18
  95.7 1.7 %collective-permute-done.16 = f32[64,128]{1,0:T(8,128)S(1)} collective-permute-done((f32[64,128]{1,0:T(8,128)S(1)}, f32[64,128]{1,0:T(8,128)S(1)}, u32[]{:S(2)}, u32[]{:S(2)}) %collective-permute-start.16) | collective-permute-done | bytes 32800 | tf_op jit(solution)/shard_map/ppermute | solution.py:359
  97.4 0.4 collective-permute-done.17
  97.9 0.6 add_bitcast_fusion
  (24 shorter events, 0.3 us)
Async XLA Ops:
  0.1 1.9 %copy-start = (bf16[1,128,12288]{2,1,0:T(8,128)(2,1)S(1)}, bf16[1,128,12288]{2,1,0:T(8,128)(2,1)}, u32[]{:S(2)}) copy-start(bf16[1,128,12288]{2,1,0:T(8,128)(2,1)} %qkv_ref.23) | copy-start | bytes 9437188
  2.0 5.7 %copy-start.1 = (bf16[2,4096,64]{1,2,0:T(8,128)(2,1)S(1)}, bf16[2,4096,64]{1,2,0:T(8,128)(2,1)}, u32[]{:S(2)}) copy-start(bf16[2,4096,64]{1,2,0:T(8,128)(2,1)} %param.6) | copy-start | bytes 3145732
  2.6 13.5 %collective-permute-start.3 = (bf16[128,768]{1,0:T(8,128)(2,1)S(1)}, bf16[128,768]{1,0:T(8,128)(2,1)S(1)}, u32[]{:S(2)}, u32[]{:S(2)}) collective-permute-start(bf16[128,768]{1,0:T(8,128)(2,1)S(1)} %pack.16), channel_id=1, source_target_pairs={{0,24},{4,28},{8,16},{12,20},{16,8},{20,12},{24,0},{28,4},{1,25},{... | collective-permute-start | bytes 589832 | tf_op jit(solution)/shard_map/ppermute | solution.py:359
  8.6 53.3 %collective-permute-start = (bf16[128,2304]{1,0:T(8,128)(2,1)S(1)}, bf16[128,2304]{1,0:T(8,128)(2,1)S(1)}, u32[]{:S(2)}, u32[]{:S(2)}) collective-permute-start(bf16[128,2304]{1,0:T(8,128)(2,1)S(1)} %pack.13), channel_id=1, source_target_pairs={{0,4},{4,0},{8,12},{12,8},{16,20},{20,16},{24,28},{28,24},{1,5},{5... | collective-permute-start | bytes 1769480 | tf_op jit(solution)/shard_map/ppermute | solution.py:359
  10.9 51.0 %collective-permute-start.1 = (bf16[128,2304]{1,0:T(8,128)(2,1)S(1)}, bf16[128,2304]{1,0:T(8,128)(2,1)S(1)}, u32[]{:S(2)}, u32[]{:S(2)}) collective-permute-start(bf16[128,2304]{1,0:T(8,128)(2,1)S(1)} %pack.14), channel_id=1, source_target_pairs={{0,8},{4,12},{8,0},{12,4},{16,24},{20,28},{24,16},{28,20},{1,9},{5... | collective-permute-start | bytes 1769480 | tf_op jit(solution)/shard_map/ppermute | solution.py:359
  11.9 53.8 %collective-permute-start.2 = (bf16[128,2304]{1,0:T(8,128)(2,1)S(1)}, bf16[128,2304]{1,0:T(8,128)(2,1)S(1)}, u32[]{:S(2)}, u32[]{:S(2)}) collective-permute-start(bf16[128,2304]{1,0:T(8,128)(2,1)S(1)} %pack.15), channel_id=1, source_target_pairs={{0,12},{4,8},{8,4},{12,0},{16,28},{20,24},{24,20},{28,16},{1,13},{... | collective-permute-start | bytes 1769480 | tf_op jit(solution)/shard_map/ppermute | solution.py:359
  14.5 29.7 %collective-permute-start.6 = (bf16[128,768]{1,0:T(8,128)(2,1)S(1)}, bf16[128,768]{1,0:T(8,128)(2,1)S(1)}, u32[]{:S(2)}, u32[]{:S(2)}) collective-permute-start(bf16[128,768]{1,0:T(8,128)(2,1)S(1)} %pack.19), channel_id=1, source_target_pairs={{0,28},{4,24},{8,20},{12,16},{16,12},{20,8},{24,4},{28,0},{1,29},{... | collective-permute-start | bytes 589832 | tf_op jit(solution)/shard_map/ppermute | solution.py:359
  16.7 30.1 %collective-permute-start.4 = (bf16[128,768]{1,0:T(8,128)(2,1)S(1)}, bf16[128,768]{1,0:T(8,128)(2,1)S(1)}, u32[]{:S(2)}, u32[]{:S(2)}) collective-permute-start(bf16[128,768]{1,0:T(8,128)(2,1)S(1)} %pack.17), channel_id=1, source_target_pairs={{0,16},{4,20},{8,24},{12,28},{16,0},{20,4},{24,8},{28,12},{1,17},{... | collective-permute-start | bytes 589832 | tf_op jit(solution)/shard_map/ppermute | solution.py:359
  44.8 13.3 %collective-permute-start.7 = (bf16[128,768]{1,0:T(8,128)(2,1)S(1)}, bf16[128,768]{1,0:T(8,128)(2,1)S(1)}, u32[]{:S(2)}, u32[]{:S(2)}) collective-permute-start(bf16[128,768]{1,0:T(8,128)(2,1)S(1)} %pack.20), channel_id=1, source_target_pairs={{0,20},{4,16},{8,28},{12,24},{16,4},{20,0},{24,12},{28,8},{1,21},{... | collective-permute-start | bytes 589832 | tf_op jit(solution)/shard_map/ppermute | solution.py:359
  46.8 32.9 %collective-permute-start.10 = (bf16[160,256]{1,0:T(8,128)(2,1)S(1)}, bf16[160,256]{1,0:T(8,128)(2,1)S(1)}, u32[]{:S(2)}, u32[]{:S(2)}) collective-permute-start(bf16[160,256]{1,0:T(8,128)(2,1)S(1)} %pack.23.refs_8_), channel_id=1, source_target_pairs={{0,28},{4,24},{8,20},{12,16},{16,12},{20,8},{24,4},{28,0},{1,29},{... | collective-permute-start | bytes 245768 | tf_op jit(solution)/shard_map/ppermute | solution.py:359
  58.1 21.6 %collective-permute-start.9 = (bf16[160,256]{1,0:T(8,128)(2,1)S(1)}, bf16[160,256]{1,0:T(8,128)(2,1)S(1)}, u32[]{:S(2)}, u32[]{:S(2)}) collective-permute-start(bf16[160,256]{1,0:T(8,128)(2,1)S(1)} %pack.22.refs_9_), channel_id=1, source_target_pairs={{0,24},{4,28},{8,16},{12,20},{16,8},{20,12},{24,0},{28,4},{1,25},{... | collective-permute-start | bytes 245768 | tf_op jit(solution)/shard_map/ppermute | solution.py:359
  61.8 3.9 %copy-start.4 = (s32[4]{0:T(128)S(1)}, s32[4]{0:T(128)}, u32[]{:S(2)}) copy-start(s32[4]{0:T(128)} %frames_ref.3) | copy-start | bytes 52
  61.8 17.9 %collective-permute-start.5 = (bf16[160,256]{1,0:T(8,128)(2,1)S(1)}, bf16[160,256]{1,0:T(8,128)(2,1)S(1)}, u32[]{:S(2)}, u32[]{:S(2)}) collective-permute-start(bf16[160,256]{1,0:T(8,128)(2,1)S(1)} %pack.18.refs_11_), channel_id=1, source_target_pairs={{0,16},{4,20},{8,24},{12,28},{16,0},{20,4},{24,8},{28,12},{1,17},{... | collective-permute-start | bytes 245768 | tf_op jit(solution)/shard_map/ppermute | solution.py:359
  61.9 17.8 %collective-permute-start.8 = (bf16[160,256]{1,0:T(8,128)(2,1)S(1)}, bf16[160,256]{1,0:T(8,128)(2,1)S(1)}, u32[]{:S(2)}, u32[]{:S(2)}) collective-permute-start(bf16[160,256]{1,0:T(8,128)(2,1)S(1)} %pack.21.refs_10_), channel_id=1, source_target_pairs={{0,20},{4,16},{8,28},{12,24},{16,4},{20,0},{24,12},{28,8},{1,21},{... | collective-permute-start | bytes 245768 | tf_op jit(solution)/shard_map/ppermute | solution.py:359
  65.7 7.3 %copy-start.5 = (s32[2]{0:T(128)S(1)}, s32[2]{0:T(128)}, u32[]{:S(2)}) copy-start(s32[2]{0:T(128)} %param.8) | copy-start | bytes 28
  71.7 1.2 %copy-start.2 = (f32[4,6,64,256]{3,2,1,0:T(8,128)}, f32[4,6,64,256]{3,2,1,0:T(8,128)S(1)}, u32[]{:S(2)}) copy-start(f32[4,6,64,256]{3,2,1,0:T(8,128)S(1)} %get-tuple-element.9.sums_ref) | copy-start | bytes 4718596
  72.9 5.2 %collective-permute-start.11 = (f32[4,2,8,256]{3,2,1,0:T(8,128)S(1)}, f32[4,2,8,256]{3,2,1,0:T(8,128)S(1)}, u32[]{:S(2)}, u32[]{:S(2)}) collective-permute-start(f32[4,2,8,256]{3,2,1,0:T(8,128)S(1)} %get-tuple-element.10.stats_ref), channel_id=1, source_target_pairs={{0,16},{4,20},{8,24},{12,28},{16,0},{20,4},{24,8},{28,12},{1,17},{... | collective-permute-start | bytes 196616 | tf_op jit(solution)/shard_map/ppermute | solution.py:359
  78.1 1.4 %copy-start.3 = (f32[4,6,64,256]{3,2,1,0:T(8,128)S(1)}, f32[4,6,64,256]{3,2,1,0:T(8,128)}, u32[]{:S(2)}) copy-start(f32[4,6,64,256]{3,2,1,0:T(8,128)} %copy-done.2) | copy-start | bytes 4718596
  81.7 4.3 %collective-permute-start.12 = (bf16[4,64,128]{2,1,0:T(8,128)(2,1)S(1)}, bf16[4,64,128]{2,1,0:T(8,128)(2,1)S(1)}, u32[]{:S(2)}, u32[]{:S(2)}) collective-permute-start(bf16[4,64,128]{2,1,0:T(8,128)(2,1)S(1)} %get-tuple-element.12), channel_id=1, source_target_pairs={{0,4},{4,0},{8,12},{12,8},{16,20},{20,16},{24,28},{28,24},{1,5},{5... | collective-permute-start | bytes 196616 | tf_op jit(solution)/shard_map/ppermute | solution.py:359
  86.1 5.9 %collective-permute-start.13 = (f32[1,64,128]{2,1,0:T(8,128)S(1)}, f32[1,64,128]{2,1,0:T(8,128)S(1)}, u32[]{:S(2)}, u32[]{:S(2)}) collective-permute-start(f32[1,64,128]{2,1,0:T(8,128)S(1)} %get-tuple-element.13), channel_id=1, source_target_pairs={{0,24},{4,28},{8,16},{12,20},{16,8},{20,12},{24,0},{28,4},{1,25},{... | collective-permute-start | bytes 98312 | tf_op jit(solution)/shard_map/ppermute | solution.py:359
  87.8 4.3 %collective-permute-start.14 = (f32[1,64,128]{2,1,0:T(8,128)S(1)}, f32[1,64,128]{2,1,0:T(8,128)S(1)}, u32[]{:S(2)}, u32[]{:S(2)}) collective-permute-start(f32[1,64,128]{2,1,0:T(8,128)S(1)} %get-tuple-element.15), channel_id=1, source_target_pairs={{0,8},{4,12},{8,0},{12,4},{16,24},{20,28},{24,16},{28,20},{1,9},{5... | collective-permute-start | bytes 98312 | tf_op jit(solution)/shard_map/ppermute | solution.py:359
  88.9 4.8 %collective-permute-start.15 = (f32[1,64,128]{2,1,0:T(8,128)S(1)}, f32[1,64,128]{2,1,0:T(8,128)S(1)}, u32[]{:S(2)}, u32[]{:S(2)}) collective-permute-start(f32[1,64,128]{2,1,0:T(8,128)S(1)} %get-tuple-element.14), channel_id=1, source_target_pairs={{0,16},{4,20},{8,24},{12,28},{16,0},{20,4},{24,8},{28,12},{1,17},{... | collective-permute-start | bytes 98312 | tf_op jit(solution)/shard_map/ppermute | solution.py:359
  93.8 3.7 %collective-permute-start.16 = (f32[64,128]{1,0:T(8,128)S(1)}, f32[64,128]{1,0:T(8,128)S(1)}, u32[]{:S(2)}, u32[]{:S(2)}) collective-permute-start(f32[64,128]{1,0:T(8,128)S(1)} %fusion.2), channel_id=1, source_target_pairs={{0,3},{1,2},{2,1},{3,0},{4,7},{5,6},{6,5},{7,4},{8,11},{9,10},{10,... | collective-permute-start | bytes 98312 | tf_op jit(solution)/shard_map/ppermute | solution.py:359
  93.8 4.0 %collective-permute-start.17 = (f32[64,128]{1,0:T(8,128)S(1)}, f32[64,128]{1,0:T(8,128)S(1)}, u32[]{:S(2)}, u32[]{:S(2)}) collective-permute-start(f32[64,128]{1,0:T(8,128)S(1)} %fusion.2), channel_id=1, source_target_pairs={{0,2},{1,3},{2,0},{3,1},{4,6},{5,7},{6,4},{7,5},{8,10},{9,11},{10,... | collective-permute-start | bytes 98312 | tf_op jit(solution)/shard_map/ppermute | solution.py:359
  95.4 2.4 %collective-permute-start.18 = (f32[64,128]{1,0:T(8,128)S(1)}, f32[64,128]{1,0:T(8,128)S(1)}, u32[]{:S(2)}, u32[]{:S(2)}) collective-permute-start(f32[64,128]{1,0:T(8,128)S(1)} %fusion.2), channel_id=1, source_target_pairs={{0,1},{1,0},{2,3},{3,2},{4,5},{5,4},{6,7},{7,6},{8,9},{9,8},{10,11... | collective-permute-start | bytes 98312 | tf_op jit(solution)/shard_map/ppermute | solution.py:359

commit v9 on v0

v9 whole, which is shorter than its diff:
```python
import functools
import math

import jax
import jax.numpy as jnp
from jax import lax
from jax.experimental import pallas as pl
from jax.experimental.pallas import tpu as pltpu
from jax.sharding import PartitionSpec as P

HEADS = 32
HD = 128
FRAME_TOK = 64
NT = (((1,), (1,)), ((), ()))
LOG2_SCALE = math.log2(math.e) / math.sqrt(HD)
LOWEST = -1e30
PACK_VMEM = 8 * 1024 * 1024
ATTEND_VMEM = 20 * 1024 * 1024
WHOLE_VMEM = 60 * 1024 * 1024
SMEM = pl.BlockSpec(memory_space=pltpu.SMEM)
VMEM = pl.BlockSpec(memory_space=pltpu.VMEM)
ANYWHERE = pl.BlockSpec(memory_space=pl.ANY)


def fold(readout, values):
    return lax.dot_general(readout, values, NT, preferred_element_type=jnp.float32).astype(jnp.bfloat16)


def value_place(h, count, lat):
    return (h * lat) % HD, count * 2 * HD + (h * lat // HD) * HD


def pack_kernel(place_ref, qkv_ref, readout_ref, *refs):
    out_ref = refs[-1]
    lat = readout_ref.shape[1]
    count = readout_ref.shape[2] // HD
    for h in range(count):
        base = h * 3 * HD
        out_ref[:, h * 2 * HD : (h + 1) * 2 * HD] = qkv_ref[0, :, base : base + 2 * HD]
        row, column = value_place(h, count, lat)
        out_ref[row : row + lat, column : column + HD] = fold(
            readout_ref[0, :, h * HD : (h + 1) * HD], qkv_ref[0, :, base + 2 * HD : base + 3 * HD]
        )


def pack(place, qkv, readout_t, k, count, after):
    rows = qkv.shape[1]
    lat = readout_t.shape[1]
    width = count * 2 * HD + -(-count * lat // HD) * HD
    operands = [place, qkv, readout_t]
    in_specs = [
        pl.BlockSpec((1, rows, count * 3 * HD), lambda g, m: (0, 0, m[0] ^ k)),
        pl.BlockSpec((1, lat, count * HD), lambda g, m: (m[1], 0, m[0] ^ k)),
    ]
    if after is not None:
        operands += [after]
        in_specs += [ANYWHERE]
    return pl.pallas_call(
        pack_kernel,
        grid_spec=pltpu.PrefetchScalarGridSpec(
            num_scalar_prefetch=1,
            grid=(1,),
            in_specs=in_specs,
            out_specs=pl.BlockSpec((rows, width), lambda g, m: (0, 0)),
        ),
        out_shape=jax.ShapeDtypeStruct((rows, width), jnp.bfloat16),
        compiler_params=pltpu.CompilerParams(vmem_limit_bytes=PACK_VMEM),
        cost_estimate=pl.CostEstimate(flops=0, bytes_accessed=rows * width * 4, transcendentals=0),
        name="pack",
    )(*operands)


def mask_rows(frames_ref, me, rows, query_offsets, key_offsets):
    columns = lax.broadcasted_iota(jnp.int32, (1, rows), 1)
    places = jnp.concatenate([(me ^ k) * rows + columns for k in query_offsets], axis=1)
    end = frames_ref[0] * FRAME_TOK
    bound = jnp.full(places.shape, end, jnp.int32)
    for c in range(1, frames_ref.shape[0]):
        later = end + frames_ref[c] * FRAME_TOK
        bound = jnp.where(places >= end, later, bound)
        end = later
    return [
        jnp.where((me ^ k) * rows + start < bound, 0.0, -jnp.inf)
        for k in key_offsets
        for start in range(0, rows, FRAME_TOK)
    ]


def run_units(units, lat):
    frames = [tile() for tile in units[0][0]]
    for u, (_, values, shifts, finish) in enumerate(units):
        ahead = list(units[u + 1][0]) if u + 1 < len(units) else []
        peaks = [jnp.max(f, axis=0, keepdims=True) + s for f, s in zip(sum(frames, []), shifts)]
        peak = jnp.maximum(functools.reduce(jnp.maximum, peaks), LOWEST)
        following, summed, start = [], None, 0
        for t, tile in enumerate(frames):
            for _ in range(-(-(len(ahead) - len(following)) // (len(frames) - t))):
                following.append(ahead[len(following)]())
            weights = [
                jnp.exp2((f + (s - peak)) * LOG2_SCALE).astype(jnp.bfloat16)
                for f, s in zip(tile, shifts[start : start + len(tile)])
            ]
            start += len(tile)
            part = jnp.dot(values[t](), jnp.concatenate(weights, axis=0), preferred_element_type=jnp.float32)
            summed = part if summed is None else summed + part
        finish(summed[:lat], summed[lat : lat + 1], peak)
        frames = following


def score_tile(keys, queries):
    scores = lax.dot_general(keys(), queries(), NT, preferred_element_type=jnp.float32)
    return [scores[start : start + FRAME_TOK] for start in range(0, scores.shape[0], FRAME_TOK)]


def stage_values(folded, pieces, lat):
    count = folded.shape[0]
    rows = pieces[0].shape[0]
    for i in range(count):
        row, column = value_place(i, count, lat)
        for n, piece in enumerate(pieces):
            folded[i, :lat, n * rows : (n + 1) * rows] = piece[row : row + lat, column : column + HD]
        folded[i, lat:] = jnp.ones_like(folded[i, lat:])


def pairs_of(pieces, i, what):
    column = (2 * i + what) * HD

    def read(n):
        return lambda: jnp.concatenate([pieces[n][:, column : column + HD], pieces[n + 1][:, column : column + HD]], axis=0)

    return [read(n) for n in range(0, len(pieces), 2)]


def early_kernel(offsets, frames_ref, factor_ref, me_ref, *refs):
    count_pieces = len(offsets)
    pieces = refs[:count_pieces]
    sums_ref, stats_ref, asked, folded = refs[-4:]
    me = me_ref[0]
    rows = pieces[0].shape[0]
    lat = sums_ref.shape[2]
    count = folded.shape[0]
    blocks = count_pieces // 2
    stage_values(folded, pieces, lat)
    for i in range(count):
        for b, read in enumerate(pairs_of(pieces, i, 0)):
            asked[b, i] = read()
    half = count_pieces // 2 + 1

    def some_blocks(b, carry):
        q = [2 * b, 2 * b + 1]
        shifts = mask_rows(frames_ref, me, rows, [jnp.where(n < half, n, n + 2) for n in q], offsets)
        peaks, totals, units = [], [], []
        for i in range(count):

            def finish(summed, total, peak, i=i):
                sums_ref[b, i] = summed
                peaks.append(peak)
                totals.append(total)

            tiles = [
                functools.partial(score_tile, keys, lambda i=i: asked[b, i]) for keys in pairs_of(pieces, i, 1)
            ]
            values = [lambda i=i, t=t: folded[i, :, t * 2 * rows : (t + 1) * 2 * rows] for t in range(blocks)]
            units.append((tiles, values, shifts, finish))
        run_units(units, lat)
        rest = [jnp.ones_like(peaks[0])] * (stats_ref.shape[2] - count)
        stats_ref[b, 0] = jnp.concatenate(peaks + rest, axis=0)
        stats_ref[b, 1] = jnp.concatenate(totals + rest, axis=0)
        return carry

    lax.fori_loop(0, blocks, some_blocks, 0)


def late_kernel(offsets, late, frames_ref, factor_ref, me_ref, *refs):
    early = len(offsets)
    pieces = refs[: early + 2]
    sums_ref, stats_ref, keep_ref, give_ref, folded = refs[early + 2 :]
    me = me_ref[0]
    half, lat, rows = keep_ref.shape
    bits = half.bit_length()
    count = folded.shape[0]
    stage_values(folded, pieces, lat)
    every = list(offsets) + list(late)
    results = {}

    def add(b, part):
        results[b] = part if b not in results else results[b] + part

    def write(b):
        for j in range(2):
            k = every[2 * b + j]
            n = sum(((k >> bit) & 1) << (bits - 1 - bit) for bit in range(bits))
            part = results[b][:, j * rows : (j + 1) * rows] * factor_ref[0]
            if n < half:
                keep_ref[n] = part
            else:
                give_ref[n - half] = part.astype(jnp.bfloat16)

    units = []
    blocks = early // 2
    for b in [blocks] + list(range(blocks)):
        keys_in = range(blocks + 1) if b == blocks else [blocks]
        key_offsets = [every[2 * t + j] for t in keys_in for j in range(2)]
        shifts = mask_rows(frames_ref, me, rows, every[2 * b : 2 * b + 2], key_offsets)
        for i in range(count):

            def finish(summed, total, peak, b=b, i=i):
                if b < blocks:
                    before = stats_ref[b, 0, i : i + 1]
                    highest = jnp.maximum(before, peak)
                    old = jnp.exp2((before - highest) * LOG2_SCALE)
                    new = jnp.exp2((peak - highest) * LOG2_SCALE)
                    both = stats_ref[b, 1, i : i + 1] * old + total * new
                    add(b, sums_ref[b, i] * (old / both) + summed * (new / both))
                else:
                    add(b, summed / total)
                if i == count - 1:
                    write(b)

            queries = pairs_of(pieces, i, 0)[b]
            keys = pairs_of(pieces, i, 1)
            tiles = [functools.partial(score_tile, keys[t], queries) for t in keys_in]
            values = [lambda i=i, t=t: folded[i, :, t * 2 * rows : (t + 1) * 2 * rows] for t in keys_in]
            units.append((tiles, values, shifts, finish))
    run_units(units, lat)


def attend_early(pieces, offsets, span_frames, factor, me, count, lat):
    rows = pieces[0].shape[0]
    blocks = len(pieces) // 2
    tokens = len(pieces) * rows
    return pl.pallas_call(
        functools.partial(early_kernel, offsets),
        in_specs=[SMEM] * 3 + [VMEM] * len(pieces),
        out_specs=[VMEM, VMEM],
        out_shape=[
            jax.ShapeDtypeStruct((blocks, count, lat, 2 * rows), jnp.float32),
            jax.ShapeDtypeStruct((blocks, 2, 8, 2 * rows), jnp.float32),
        ],
        scratch_shapes=[
            pltpu.VMEM((blocks, count, 2 * rows, HD), jnp.bfloat16),
            pltpu.VMEM((count, lat + 16, tokens), jnp.bfloat16),
        ],
        compiler_params=pltpu.CompilerParams(vmem_limit_bytes=ATTEND_VMEM if len(pieces) <= 8 else WHOLE_VMEM),
        cost_estimate=pl.CostEstimate(
            flops=count * tokens * tokens * 2 * (HD + lat),
            bytes_accessed=tokens * count * 3 * HD * 2,
            transcendentals=count * tokens * tokens,
        ),
        name="attend_early",
    )(span_frames, factor, me, *pieces)


def attend_late(pieces, offsets, late, sums, stats, span_frames, factor, me, count, lat):
    rows = pieces[0].shape[0]
    tokens = len(pieces) * rows
    half = len(pieces) // 2
    return pl.pallas_call(
        functools.partial(late_kernel, offsets, late),
        in_specs=[SMEM] * 3 + [VMEM] * (len(pieces) + 2),
        out_specs=[VMEM, VMEM],
        out_shape=[
            jax.ShapeDtypeStruct((half, lat, rows), jnp.float32),
            jax.ShapeDtypeStruct((half, lat, rows), jnp.bfloat16),
        ],
        scratch_shapes=[pltpu.VMEM((count, lat + 16, tokens), jnp.bfloat16)],
        compiler_params=pltpu.CompilerParams(vmem_limit_bytes=ATTEND_VMEM if len(pieces) <= 8 else WHOLE_VMEM),
        cost_estimate=pl.CostEstimate(
            flops=count * tokens * rows * 4 * (HD + lat),
            bytes_accessed=tokens * count * 3 * HD * 2,
            transcendentals=count * tokens * rows * 2,
        ),
        name="attend_late",
    )(span_frames, factor, me, *pieces, sums, stats)


def swap(array, axis, offset):
    size = lax.axis_size(axis)
    return lax.ppermute(array, axis, [(i, i ^ offset) for i in range(size)])


def body(qkv, readout, step_weight, timestep, span_frames):
    seq_count = lax.axis_size("seq")
    mp_count = lax.axis_size("mp")
    half = seq_count // 2
    count = HEADS // seq_count
    lat = readout.shape[2]
    me = lax.axis_index("seq").astype(jnp.int32)
    mp_index = lax.axis_index("mp")
    sample_count = mp_count // 2
    model_index = (mp_index // sample_count).astype(jnp.int32)
    sample_index = mp_index % sample_count
    signed = jnp.where(model_index == 1, 1.0, -1.0).astype(jnp.float32)
    factor = (signed * step_weight[timestep[sample_index]]).reshape(1)
    readout_t = jnp.swapaxes(readout, 1, 2)
    place = jnp.stack([me, model_index])

    pieces = [None] * seq_count
    for n in range(half):
        k = seq_count - 1 - n
        pieces[k] = swap(pack(place, qkv, readout_t, k, count, pieces[k + 2] if n > 1 else None), "seq", k)
    for k in range(half):
        packed = pack(place, qkv, readout_t, k, count, None)
        pieces[k] = swap(packed, "seq", k) if k else packed
    late = [half, half + 1]
    early = [k for k in range(seq_count) if k not in late]
    sums, stats = attend_early([pieces[k] for k in early], early, span_frames, factor, me.reshape(1), count, lat)
    keep, give = attend_late(
        [pieces[k] for k in early + late], early, late, sums, stats, span_frames, factor, me.reshape(1), count, lat
    )

    keep = keep + swap(give, "seq", 1).astype(jnp.float32)
    offset = 2
    while offset < seq_count:
        radix = min(4, seq_count // offset)
        size = keep.shape[0] // radix
        parts = [keep[n * size : (n + 1) * size] for n in range(radix)]
        keep = parts[0]
        for n in range(radix - 1, 0, -1):
            bits_n = (n >> 1) | ((n & 1) << 1) if radix == 4 else n
            keep = keep + swap(parts[n], "seq", offset * bits_n)
        offset *= radix
    total = keep[0]
    offset = 1
    while offset < mp_count:
        radix = min(4, mp_count // offset)
        own = total
        for n in range(radix - 1, 0, -1):
            total = total + swap(own, "mp", offset * n)
        offset *= radix
    return total.T


def solution(mesh):
    return jax.shard_map(
        body,
        mesh=mesh,
        in_specs=(P("mp", "seq", None), P(), P(), P(), P()),
        out_specs=P("seq", None),
        check_vma=False,
    )
```

time: 172 us -> 92.1 us (0.54); the launches traced: 174 us -> 91.7 us
  waiting for transfers between devices: 91.9 us -> 18.3 us
  starting transfers between devices: 11 us -> 41.7 us
  local copies, waits for them, and re-layouts: 31.4 us -> 8.87 us
  Pallas kernels: 0 us -> 19.3 us
  other arithmetic: 12.8 us -> 0.72 us
  matrix products: 11.5 us -> 0 us
  blocking collectives: 10.9 us -> 0 us
    all_to_all x2 -> x0, waiting for transfers between devices: 91.9 us -> none  [the longest x1 70.4 us: body(): lax.all_to_all(grouped, 'seq', split_axis=1, concat_axis=0, tiled=True)]
    ppermute x0 -> x14, starting transfers between devices: none -> 41.7 us  [swap(): return lax.ppermute(array, axis, [(i, i ^ offset) for i in range(size)])]
    pallas_call x0 -> x10, Pallas kernels: none -> 19.3 us  [the longest x8 9.84 us: pack(): pl.pallas_call(pack_kernel, grid_spec=pltpu.PrefetchScalarGridSpec(num_sc...]
    ppermute x0 -> x14, waiting for transfers between devices: none -> 18.3 us  [swap(): return lax.ppermute(array, axis, [(i, i ^ offset) for i in range(size)])]
    dot_general x9 -> x0, matrix products: 11.5 us -> none  [the longest x4 7.21 us: key_block(): jnp.dot(weights, values_here, preferred_element_type=jnp.float32)]
    all_to_all x2 -> x0, starting transfers between devices: 11 us -> none  [the longest x1 7.38 us: body(): lax.all_to_all(grouped, 'seq', split_axis=1, concat_axis=0, tiled=True)]
    psum x1 -> x0, blocking collectives: 10.9 us -> none  [body(): return lax.psum(partial_sum, 'mp')]
    another operation x9 -> x0, local copies, waits for them, and re-layouts: 9.28 us -> none  [the longest x1 4.64 us: body(): grouped = own_rows.reshape(row_count, seq_count, heads_local, 3 * HD)]
  transfers between devices with their start and end apart: 2 -> 14, of which waited for: 2 -> 7; matrix products, arithmetic and copies ran while one was open for 1% -> 2% of each run, Pallas kernels for 0% -> 15%
where the time goes in v9:
time: 92.1 us; the launch traced here: 91.7 us
  starting transfers between devices  41.7 us (45%)
  Pallas kernels  19.3 us (21%)
  waiting for transfers between devices  18.3 us (20%)
  local copies, waits for them, and re-layouts  8.87 us (10%)
  between operations  2.73 us (3%)
    ppermute x14, starting transfers between devices, swap(): return lax.ppermute(array, axis, [(i, i ^ offset) for i in range(size)])  41.7 us
    ppermute x14, waiting for transfers between devices, swap(): return lax.ppermute(array, axis, [(i, i ^ offset) for i in range(size)])  18.3 us
    pallas_call x8, Pallas kernels, pack(): pl.pallas_call(pack_kernel, grid_spec=pltpu.PrefetchScalarGridSpec(num_sc...  9.84 us
    unnamed x20, local copies, waits for them, and re-layouts  7 us
    pallas_call x1, Pallas kernels, attend_early(): pl.pallas_call(functools.partial(early_kernel, offsets), in_specs=[SMEM]...  5.07 us
    pallas_call x1, Pallas kernels, attend_late(): pl.pallas_call(functools.partial(late_kernel, offsets, late), in_specs=[S...  4.37 us
    dynamic_slice x2, local copies, waits for them, and re-layouts, body(): factor = (signed * step_weight[timestep[sample_index]]).reshape(1)  1.86 us
  transfers between devices with their start and end apart: 14, of which 7 were waited for; matrix products, arithmetic and copies ran while one was open for 2% of the time, Pallas kernels for 15%

profile of v9, /device:TPU:0, one launch (start us, length us, event | category | flops | bytes accessed | tf_op | source)
XLA Modules:
  0.0 91.7 jit_solution(4664601658701695887)
XLA Ops:
  0.0 0.1 pad_add_fusion.place_ref
  0.1 1.9 %copy-done = bf16[1,128,12288]{2,1,0:T(8,128)(2,1)S(1)} copy-done((bf16[1,128,12288]{2,1,0:T(8,128)(2,1)S(1)}, bf16[1,128,12288]{2,1,0:T(8,128)(2,1)}, u32[]{:S(2)}) %copy-start) | copy-done | bytes 3145752
  2.0 1.2 %copy-done.2 = bf16[2,4096,64]{1,2,0:T(8,128)(2,1)S(1)} copy-done((bf16[2,4096,64]{1,2,0:T(8,128)(2,1)S(1)}, bf16[2,4096,64]{1,2,0:T(8,128)(2,1)}, u32[]{:S(2)}) %copy-start.2) | copy-done | bytes 1048600
  3.2 0.8 pack.12
  4.0 5.1 %collective-permute-start.3 = (bf16[128,1280]{1,0:T(8,128)(2,1)S(1)}, bf16[128,1280]{1,0:T(8,128)(2,1)S(1)}, u32[]{:S(2)}, u32[]{:S(2)}) collective-permute-start(bf16[128,1280]{1,0:T(8,128)(2,1)S(1)} %pack.12), channel_id=1, source_target_pairs={{0,24},{4,28},{8,16},{12,20},{16,8},{20,12},{24,0},{28,4},{1,25},{... | collective-permute-start | bytes 983048 | tf_op jit(solution)/shard_map/ppermute | solution.py:279
  9.1 0.8 pack.13
  9.9 1.2 %collective-permute-start.4 = (bf16[128,1280]{1,0:T(8,128)(2,1)S(1)}, bf16[128,1280]{1,0:T(8,128)(2,1)S(1)}, u32[]{:S(2)}, u32[]{:S(2)}) collective-permute-start(bf16[128,1280]{1,0:T(8,128)(2,1)S(1)} %pack.13), channel_id=1, source_target_pairs={{0,28},{4,24},{8,20},{12,16},{16,12},{20,8},{24,4},{28,0},{1,29},{... | collective-permute-start | bytes 983048 | tf_op jit(solution)/shard_map/ppermute | solution.py:279
  11.1 1.5 %pack.9 = bf16[128,1280]{1,0:T(8,128)(2,1)} custom-call(s32[2]{0:T(128)S(1)} %pad_add_fusion.place_ref, bf16[1,128,12288]{2,1,0:T(8,128)(2,1)S(1)} %copy-done, bf16[2,64,4096]{2,1,0:T(8,128)(2,1)S(1)} %bitcast.12), custom_call_target="tpu_custom_call" | custom-call | bytes 655360 | tf_op jit(solution)/shard_map/pack/pallas_call | solution.py:58
  12.6 0.4 collective-permute-start
  13.0 1.5 %pack.10 = bf16[128,1280]{1,0:T(8,128)(2,1)} custom-call(s32[2]{0:T(128)S(1)} %pad_add_fusion.place_ref, bf16[1,128,12288]{2,1,0:T(8,128)(2,1)S(1)} %copy-done, bf16[2,64,4096]{2,1,0:T(8,128)(2,1)S(1)} %bitcast.13), custom_call_target="tpu_custom_call" | custom-call | bytes 655360 | tf_op jit(solution)/shard_map/pack/pallas_call | solution.py:58
  14.5 0.0 collective-permute-start.1
  14.5 1.5 %pack.11 = bf16[128,1280]{1,0:T(8,128)(2,1)} custom-call(s32[2]{0:T(128)S(1)} %pad_add_fusion.place_ref, bf16[1,128,12288]{2,1,0:T(8,128)(2,1)S(1)} %copy-done, bf16[2,64,4096]{2,1,0:T(8,128)(2,1)S(1)} %bitcast.14), custom_call_target="tpu_custom_call" | custom-call | bytes 655360 | tf_op jit(solution)/shard_map/pack/pallas_call | solution.py:58
  16.0 3.1 %collective-permute-start.2 = (bf16[128,1280]{1,0:T(8,128)(2,1)}, bf16[128,1280]{1,0:T(8,128)(2,1)}, u32[]{:S(2)}, u32[]{:S(2)}) collective-permute-start(bf16[128,1280]{1,0:T(8,128)(2,1)} %pack.11), channel_id=1, source_target_pairs={{0,12},{4,8},{8,4},{12,0},{16,28},{20,24},{24,20},{28,16},{1,13},{... | collective-permute-start | bytes 983048 | tf_op jit(solution)/shard_map/ppermute | solution.py:279
  19.1 0.0 collective-permute-done.3.refs_0_.refs_4_
  19.1 1.5 %pack.14 = bf16[128,1280]{1,0:T(8,128)(2,1)} custom-call(s32[2]{0:T(128)S(1)} %pad_add_fusion.place_ref, bf16[1,128,12288]{2,1,0:T(8,128)(2,1)S(1)} %copy-done, bf16[2,64,4096]{2,1,0:T(8,128)(2,1)S(1)} %bitcast.15, bf16[128,1280]{1,0:T(8,128)(2,1)S(1)} %collective-permute-done.3.refs_0_.refs_4_), custom_call_target="tpu_custom_call" | custom-call | bytes 655360 | tf_op jit(solution)/shard_map/pack/pallas_call | solution.py:58
  20.6 13.6 %collective-permute-start.5 = (bf16[128,1280]{1,0:T(8,128)(2,1)}, bf16[128,1280]{1,0:T(8,128)(2,1)}, u32[]{:S(2)}, u32[]{:S(2)}) collective-permute-start(bf16[128,1280]{1,0:T(8,128)(2,1)} %pack.14), channel_id=1, source_target_pairs={{0,16},{4,20},{8,24},{12,28},{16,0},{20,4},{24,8},{28,12},{1,17},{... | collective-permute-start | bytes 983048 | tf_op jit(solution)/shard_map/ppermute | solution.py:279
  34.2 0.0 collective-permute-done.4.refs_0_.refs_5_
  34.2 1.5 %pack.15 = bf16[128,1280]{1,0:T(8,128)(2,1)} custom-call(s32[2]{0:T(128)S(1)} %pad_add_fusion.place_ref, bf16[1,128,12288]{2,1,0:T(8,128)(2,1)S(1)} %copy-done, bf16[2,64,4096]{2,1,0:T(8,128)(2,1)S(1)} %bitcast.16, bf16[128,1280]{1,0:T(8,128)(2,1)S(1)} %collective-permute-done.4.refs_0_.refs_5_), custom_call_target="tpu_custom_call" | custom-call | bytes 655360 | tf_op jit(solution)/shard_map/pack/pallas_call | solution.py:58
  35.7 11.3 %collective-permute-start.6 = (bf16[128,1280]{1,0:T(8,128)(2,1)}, bf16[128,1280]{1,0:T(8,128)(2,1)}, u32[]{:S(2)}, u32[]{:S(2)}) collective-permute-start(bf16[128,1280]{1,0:T(8,128)(2,1)} %pack.15), channel_id=1, source_target_pairs={{0,20},{4,16},{8,28},{12,24},{16,4},{20,0},{24,12},{28,8},{1,21},{... | collective-permute-start | bytes 983048 | tf_op jit(solution)/shard_map/ppermute | solution.py:279
  47.0 1.2 %copy-done.3 = bf16[2,4096,64]{1,2,0:T(8,128)(2,1)S(1)} copy-done((bf16[2,4096,64]{1,2,0:T(8,128)(2,1)S(1)}, bf16[2,4096,64]{1,2,0:T(8,128)(2,1)}, u32[]{:S(2)}) %copy-start.3) | copy-done | bytes 1048600
  48.2 0.8 pack.8.refs_0_
  49.0 0.7 copy-done.6
  49.7 0.6 dynamic_slice.6
  52.3 1.3 %dynamic_slice.7 = f32[1]{0:T(128)} dynamic-slice(f32[1000]{0:T(1024)} %param.7, s32[]{:T(128)S(6)} %select_n.25), dynamic_slice_sizes={1} | dynamic-slice | bytes 12 | tf_op jit(solution)/shard_map/dynamic_slice | solution.py:294
  54.2 0.0 collective-permute-done.refs_1_
  54.2 0.0 collective-permute-done.1.refs_2_
  54.2 0.0 collective-permute-done.2.refs_3_
  54.2 1.0 %copy-done.5 = bf16[128,1280]{1,0:T(8,128)(2,1)S(1)} copy-done((bf16[128,1280]{1,0:T(8,128)(2,1)S(1)}, bf16[128,1280]{1,0:T(8,128)(2,1)}, u32[]{:S(2)}) %copy-start.5) | copy-done | bytes 327704
  55.2 1.0 %copy-done.7 = bf16[128,1280]{1,0:T(8,128)(2,1)S(1)} copy-done((bf16[128,1280]{1,0:T(8,128)(2,1)S(1)}, bf16[128,1280]{1,0:T(8,128)(2,1)}, u32[]{:S(2)}) %copy-start.7) | copy-done | bytes 327704
  56.2 5.1 %attend_early.1 = (f32[3,4,64,256]{3,2,1,0:T(8,128)S(1)}, f32[3,2,8,256]{3,2,1,0:T(8,128)S(1)}) custom-call(s32[4]{0:T(128)S(1)} %copy-done.8, f32[1]{0:T(128)} %bitcast.2.factor_ref, s32[1]{0:T(128)} %bitcast.3.me_ref, bf16[128,1280]{1,0:T(8,128)(2,1)S(1)} %copy-done.7, bf16[128,1280]{1,0:T(8,128)(2,1)} %collective-permute-done.refs_1_, ...), custom_call_target="tpu_custom_call" | custom-call | flops 905969664 | bytes 2359296 | tf_op jit(solution)/shard_map/attend_early/pallas_call | solution.py:232
  61.3 1.3 %collective-permute-done.5.refs_6_ = bf16[128,1280]{1,0:T(8,128)(2,1)} collective-permute-done((bf16[128,1280]{1,0:T(8,128)(2,1)}, bf16[128,1280]{1,0:T(8,128)(2,1)}, u32[]{:S(2)}, u32[]{:S(2)}) %collective-permute-start.5) | collective-permute-done | bytes 327712 | tf_op jit(solution)/shard_map/ppermute | solution.py:279
  62.6 7.0 %collective-permute-done.6.refs_7_ = bf16[128,1280]{1,0:T(8,128)(2,1)} collective-permute-done((bf16[128,1280]{1,0:T(8,128)(2,1)}, bf16[128,1280]{1,0:T(8,128)(2,1)}, u32[]{:S(2)}, u32[]{:S(2)}) %collective-permute-start.6) | collective-permute-done | bytes 327712 | tf_op jit(solution)/shard_map/ppermute | solution.py:279
  69.6 4.4 %attend_late.1 = (f32[4,64,128]{2,1,0:T(8,128)S(1)}, bf16[4,64,128]{2,1,0:T(8,128)(2,1)S(1)}) custom-call(s32[4]{0:T(128)S(1)} %copy-done.8, f32[1]{0:T(128)} %bitcast.2.factor_ref, s32[1]{0:T(128)} %bitcast.3.me_ref, bf16[128,1280]{1,0:T(8,128)(2,1)S(1)} %copy-done.7, bf16[128,1280]{1,0:T(8,128)(2,1)} %collective-permute-done.refs_1_, ...), custom_call_target="tpu_custom_call" | custom-call | flops 402653184 | bytes 3145728 | tf_op jit(solution)/shard_map/attend_late/pallas_call | solution.py:258
  73.9 0.6 collective-permute-start.7
  74.5 3.7 %collective-permute-done.7 = bf16[4,64,128]{2,1,0:T(8,128)(2,1)S(1)} collective-permute-done((bf16[4,64,128]{2,1,0:T(8,128)(2,1)S(1)}, bf16[4,64,128]{2,1,0:T(8,128)(2,1)S(1)}, u32[]{:S(2)}, u32[]{:S(2)}) %collective-permute-start.7) | collective-permute-done | bytes 65568 | tf_op jit(solution)/shard_map/ppermute | solution.py:279
  78.3 2.9 %collective-permute-start.8 = (f32[1,64,128]{2,1,0:T(8,128)S(1)}, f32[1,64,128]{2,1,0:T(8,128)S(1)}, u32[]{:S(2)}, u32[]{:S(2)}) collective-permute-start(f32[1,64,128]{2,1,0:T(8,128)S(1)} %get-tuple-element.13), channel_id=1, source_target_pairs={{0,24},{4,28},{8,16},{12,20},{16,8},{20,12},{24,0},{28,4},{1,25},{... | collective-permute-start | bytes 98312 | tf_op jit(solution)/shard_map/ppermute | solution.py:279
  81.2 0.0 collective-permute-start.10
  81.2 1.5 %collective-permute-start.9 = (f32[1,64,128]{2,1,0:T(8,128)S(1)}, f32[1,64,128]{2,1,0:T(8,128)S(1)}, u32[]{:S(2)}, u32[]{:S(2)}) collective-permute-start(f32[1,64,128]{2,1,0:T(8,128)S(1)} %get-tuple-element.15), channel_id=1, source_target_pairs={{0,8},{4,12},{8,0},{12,4},{16,24},{20,28},{24,16},{28,20},{1,9},{5... | collective-permute-start | bytes 98312 | tf_op jit(solution)/shard_map/ppermute | solution.py:279
  82.7 1.4 %collective-permute-done.8 = f32[1,64,128]{2,1,0:T(8,128)S(1)} collective-permute-done((f32[1,64,128]{2,1,0:T(8,128)S(1)}, f32[1,64,128]{2,1,0:T(8,128)S(1)}, u32[]{:S(2)}, u32[]{:S(2)}) %collective-permute-start.8) | collective-permute-done | bytes 32800 | tf_op jit(solution)/shard_map/ppermute | solution.py:279
  84.1 1.9 %collective-permute-done.10 = f32[1,64,128]{2,1,0:T(8,128)S(1)} collective-permute-done((f32[1,64,128]{2,1,0:T(8,128)S(1)}, f32[1,64,128]{2,1,0:T(8,128)S(1)}, u32[]{:S(2)}, u32[]{:S(2)}) %collective-permute-start.10) | collective-permute-done | bytes 32800 | tf_op jit(solution)/shard_map/ppermute | solution.py:279
  86.0 0.0 collective-permute-done.9
  86.0 0.1 collective-permute-start.13
  86.1 1.6 %collective-permute-start.12 = (f32[64,128]{1,0:T(8,128)S(1)}, f32[64,128]{1,0:T(8,128)S(1)}, u32[]{:S(2)}, u32[]{:S(2)}) collective-permute-start(f32[64,128]{1,0:T(8,128)S(1)} %fusion.2), channel_id=1, source_target_pairs={{0,2},{1,3},{2,0},{3,1},{4,6},{5,7},{6,4},{7,5},{8,10},{9,11},{10,... | collective-permute-start | bytes 98312 | tf_op jit(solution)/shard_map/ppermute | solution.py:279
  87.7 0.3 collective-permute-start.11
  88.0 0.0 collective-permute-done.13
  88.0 2.1 %collective-permute-done.12 = f32[64,128]{1,0:T(8,128)S(1)} collective-permute-done((f32[64,128]{1,0:T(8,128)S(1)}, f32[64,128]{1,0:T(8,128)S(1)}, u32[]{:S(2)}, u32[]{:S(2)}) %collective-permute-start.12) | collective-permute-done | bytes 32800 | tf_op jit(solution)/shard_map/ppermute | solution.py:279
  90.1 0.9 %collective-permute-done.11 = f32[64,128]{1,0:T(8,128)S(1)} collective-permute-done((f32[64,128]{1,0:T(8,128)S(1)}, f32[64,128]{1,0:T(8,128)S(1)}, u32[]{:S(2)}, u32[]{:S(2)}) %collective-permute-start.11) | collective-permute-done | bytes 32800 | tf_op jit(solution)/shard_map/ppermute | solution.py:279
  91.0 0.6 add_bitcast_fusion
  (17 shorter events, 0.1 us)
Async XLA Ops:
  0.1 1.9 %copy-start = (bf16[1,128,12288]{2,1,0:T(8,128)(2,1)S(1)}, bf16[1,128,12288]{2,1,0:T(8,128)(2,1)}, u32[]{:S(2)}) copy-start(bf16[1,128,12288]{2,1,0:T(8,128)(2,1)} %qkv_ref.15) | copy-start | bytes 9437188
  2.0 1.2 %copy-start.2 = (bf16[2,4096,64]{1,2,0:T(8,128)(2,1)S(1)}, bf16[2,4096,64]{1,2,0:T(8,128)(2,1)}, u32[]{:S(2)}) copy-start(bf16[2,4096,64]{1,2,0:T(8,128)(2,1)} %param.6) | copy-start | bytes 3145732
  4.0 15.1 %collective-permute-start.3 = (bf16[128,1280]{1,0:T(8,128)(2,1)S(1)}, bf16[128,1280]{1,0:T(8,128)(2,1)S(1)}, u32[]{:S(2)}, u32[]{:S(2)}) collective-permute-start(bf16[128,1280]{1,0:T(8,128)(2,1)S(1)} %pack.12), channel_id=1, source_target_pairs={{0,24},{4,28},{8,16},{12,20},{16,8},{20,12},{24,0},{28,4},{1,25},{... | collective-permute-start | bytes 983048 | tf_op jit(solution)/shard_map/ppermute | solution.py:279
  9.9 24.4 %collective-permute-start.4 = (bf16[128,1280]{1,0:T(8,128)(2,1)S(1)}, bf16[128,1280]{1,0:T(8,128)(2,1)S(1)}, u32[]{:S(2)}, u32[]{:S(2)}) collective-permute-start(bf16[128,1280]{1,0:T(8,128)(2,1)S(1)} %pack.13), channel_id=1, source_target_pairs={{0,28},{4,24},{8,20},{12,16},{16,12},{20,8},{24,4},{28,0},{1,29},{... | collective-permute-start | bytes 983048 | tf_op jit(solution)/shard_map/ppermute | solution.py:279
  12.6 41.6 %collective-permute-start = (bf16[128,1280]{1,0:T(8,128)(2,1)}, bf16[128,1280]{1,0:T(8,128)(2,1)}, u32[]{:S(2)}, u32[]{:S(2)}) collective-permute-start(bf16[128,1280]{1,0:T(8,128)(2,1)} %pack.9), channel_id=1, source_target_pairs={{0,4},{4,0},{8,12},{12,8},{16,20},{20,16},{24,28},{28,24},{1,5},{5... | collective-permute-start | bytes 983048 | tf_op jit(solution)/shard_map/ppermute | solution.py:279
  14.5 39.8 %collective-permute-start.1 = (bf16[128,1280]{1,0:T(8,128)(2,1)}, bf16[128,1280]{1,0:T(8,128)(2,1)}, u32[]{:S(2)}, u32[]{:S(2)}) collective-permute-start(bf16[128,1280]{1,0:T(8,128)(2,1)} %pack.10), channel_id=1, source_target_pairs={{0,8},{4,12},{8,0},{12,4},{16,24},{20,28},{24,16},{28,20},{1,9},{5... | collective-permute-start | bytes 983048 | tf_op jit(solution)/shard_map/ppermute | solution.py:279
  16.0 38.2 %collective-permute-start.2 = (bf16[128,1280]{1,0:T(8,128)(2,1)}, bf16[128,1280]{1,0:T(8,128)(2,1)}, u32[]{:S(2)}, u32[]{:S(2)}) collective-permute-start(bf16[128,1280]{1,0:T(8,128)(2,1)} %pack.11), channel_id=1, source_target_pairs={{0,12},{4,8},{8,4},{12,0},{16,28},{20,24},{24,20},{28,16},{1,13},{... | collective-permute-start | bytes 983048 | tf_op jit(solution)/shard_map/ppermute | solution.py:279
  20.6 26.4 %copy-start.1 = (bf16[1,128,12288]{2,1,0:T(8,128)(2,1)S(1)}, bf16[1,128,12288]{2,1,0:T(8,128)(2,1)}, u32[]{:S(2)}) copy-start(bf16[1,128,12288]{2,1,0:T(8,128)(2,1)} %qkv_ref.15) | copy-start | bytes 9437188
  20.6 42.0 %collective-permute-start.5 = (bf16[128,1280]{1,0:T(8,128)(2,1)}, bf16[128,1280]{1,0:T(8,128)(2,1)}, u32[]{:S(2)}, u32[]{:S(2)}) collective-permute-start(bf16[128,1280]{1,0:T(8,128)(2,1)} %pack.14), channel_id=1, source_target_pairs={{0,16},{4,20},{8,24},{12,28},{16,0},{20,4},{24,8},{28,12},{1,17},{... | collective-permute-start | bytes 983048 | tf_op jit(solution)/shard_map/ppermute | solution.py:279
  34.2 1.5 %copy-start.4 = (bf16[128,1280]{1,0:T(8,128)(2,1)}, bf16[128,1280]{1,0:T(8,128)(2,1)S(1)}, u32[]{:S(2)}) copy-start(bf16[128,1280]{1,0:T(8,128)(2,1)S(1)} %collective-permute-done.4.refs_0_.refs_5_) | copy-start | bytes 983044
  35.7 14.0 %copy-start.9 = (s32[2]{0:T(128)S(1)}, s32[2]{0:T(128)}, u32[]{:S(2)}) copy-start(s32[2]{0:T(128)} %param.8) | copy-start | bytes 28
  35.7 18.5 %copy-start.8 = (s32[4]{0:T(128)S(1)}, s32[4]{0:T(128)}, u32[]{:S(2)}) copy-start(s32[4]{0:T(128)} %frames_ref.3) | copy-start | bytes 52
  35.7 33.8 %collective-permute-start.6 = (bf16[128,1280]{1,0:T(8,128)(2,1)}, bf16[128,1280]{1,0:T(8,128)(2,1)}, u32[]{:S(2)}, u32[]{:S(2)}) collective-permute-start(bf16[128,1280]{1,0:T(8,128)(2,1)} %pack.15), channel_id=1, source_target_pairs={{0,20},{4,16},{8,28},{12,24},{16,4},{20,0},{24,12},{28,8},{1,21},{... | collective-permute-start | bytes 983048 | tf_op jit(solution)/shard_map/ppermute | solution.py:279
  47.0 1.2 %copy-start.3 = (bf16[2,4096,64]{1,2,0:T(8,128)(2,1)S(1)}, bf16[2,4096,64]{1,2,0:T(8,128)(2,1)}, u32[]{:S(2)}) copy-start(bf16[2,4096,64]{1,2,0:T(8,128)(2,1)} %param.6) | copy-start | bytes 3145732
  49.0 0.7 copy-start.6
  54.2 1.0 %copy-start.5 = (bf16[128,1280]{1,0:T(8,128)(2,1)S(1)}, bf16[128,1280]{1,0:T(8,128)(2,1)}, u32[]{:S(2)}) copy-start(bf16[128,1280]{1,0:T(8,128)(2,1)} %copy-done.4) | copy-start | bytes 983044
  55.2 1.0 %copy-start.7 = (bf16[128,1280]{1,0:T(8,128)(2,1)S(1)}, bf16[128,1280]{1,0:T(8,128)(2,1)}, u32[]{:S(2)}) copy-start(bf16[128,1280]{1,0:T(8,128)(2,1)} %copy-done.6) | copy-start | bytes 983044
  73.9 4.3 %collective-permute-start.7 = (bf16[4,64,128]{2,1,0:T(8,128)(2,1)S(1)}, bf16[4,64,128]{2,1,0:T(8,128)(2,1)S(1)}, u32[]{:S(2)}, u32[]{:S(2)}) collective-permute-start(bf16[4,64,128]{2,1,0:T(8,128)(2,1)S(1)} %get-tuple-element.12), channel_id=1, source_target_pairs={{0,4},{4,0},{8,12},{12,8},{16,20},{20,16},{24,28},{28,24},{1,5},{5... | collective-permute-start | bytes 196616 | tf_op jit(solution)/shard_map/ppermute | solution.py:279
  78.3 5.8 %collective-permute-start.8 = (f32[1,64,128]{2,1,0:T(8,128)S(1)}, f32[1,64,128]{2,1,0:T(8,128)S(1)}, u32[]{:S(2)}, u32[]{:S(2)}) collective-permute-start(f32[1,64,128]{2,1,0:T(8,128)S(1)} %get-tuple-element.13), channel_id=1, source_target_pairs={{0,24},{4,28},{8,16},{12,20},{16,8},{20,12},{24,0},{28,4},{1,25},{... | collective-permute-start | bytes 98312 | tf_op jit(solution)/shard_map/ppermute | solution.py:279
  81.2 4.8 %collective-permute-start.10 = (f32[1,64,128]{2,1,0:T(8,128)S(1)}, f32[1,64,128]{2,1,0:T(8,128)S(1)}, u32[]{:S(2)}, u32[]{:S(2)}) collective-permute-start(f32[1,64,128]{2,1,0:T(8,128)S(1)} %get-tuple-element.14), channel_id=1, source_target_pairs={{0,16},{4,20},{8,24},{12,28},{16,0},{20,4},{24,8},{28,12},{1,17},{... | collective-permute-start | bytes 98312 | tf_op jit(solution)/shard_map/ppermute | solution.py:279
  81.2 4.8 %collective-permute-start.9 = (f32[1,64,128]{2,1,0:T(8,128)S(1)}, f32[1,64,128]{2,1,0:T(8,128)S(1)}, u32[]{:S(2)}, u32[]{:S(2)}) collective-permute-start(f32[1,64,128]{2,1,0:T(8,128)S(1)} %get-tuple-element.15), channel_id=1, source_target_pairs={{0,8},{4,12},{8,0},{12,4},{16,24},{20,28},{24,16},{28,20},{1,9},{5... | collective-permute-start | bytes 98312 | tf_op jit(solution)/shard_map/ppermute | solution.py:279
  86.0 1.9 %collective-permute-start.13 = (f32[64,128]{1,0:T(8,128)S(1)}, f32[64,128]{1,0:T(8,128)S(1)}, u32[]{:S(2)}, u32[]{:S(2)}) collective-permute-start(f32[64,128]{1,0:T(8,128)S(1)} %fusion.2), channel_id=1, source_target_pairs={{0,1},{1,0},{2,3},{3,2},{4,5},{5,4},{6,7},{7,6},{8,9},{9,8},{10,11... | collective-permute-start | bytes 98312 | tf_op jit(solution)/shard_map/ppermute | solution.py:279
  86.1 4.0 %collective-permute-start.12 = (f32[64,128]{1,0:T(8,128)S(1)}, f32[64,128]{1,0:T(8,128)S(1)}, u32[]{:S(2)}, u32[]{:S(2)}) collective-permute-start(f32[64,128]{1,0:T(8,128)S(1)} %fusion.2), channel_id=1, source_target_pairs={{0,2},{1,3},{2,0},{3,1},{4,6},{5,7},{6,4},{7,5},{8,10},{9,11},{10,... | collective-permute-start | bytes 98312 | tf_op jit(solution)/shard_map/ppermute | solution.py:279
  87.7 3.3 %collective-permute-start.11 = (f32[64,128]{1,0:T(8,128)S(1)}, f32[64,128]{1,0:T(8,128)S(1)}, u32[]{:S(2)}, u32[]{:S(2)}) collective-permute-start(f32[64,128]{1,0:T(8,128)S(1)} %fusion.2), channel_id=1, source_target_pairs={{0,3},{1,2},{2,1},{3,0},{4,7},{5,6},{6,5},{7,4},{8,11},{9,10},{10,... | collective-permute-start | bytes 98312 | tf_op jit(solution)/shard_map/ppermute | solution.py:279

commit v10 on v9

--- a/solution.py
+++ b/solution.py
@@ -14,6 +14,7 @@
 NT = (((1,), (1,)), ((), ()))
 LOG2_SCALE = math.log2(math.e) / math.sqrt(HD)
 LOWEST = -1e30
+NEXT_WAVE = 5000000000
 PACK_VMEM = 8 * 1024 * 1024
 ATTEND_VMEM = 20 * 1024 * 1024
 WHOLE_VMEM = 60 * 1024 * 1024
@@ -65,7 +66,9 @@
         ),
         out_shape=jax.ShapeDtypeStruct((rows, width), jnp.bfloat16),
         compiler_params=pltpu.CompilerParams(vmem_limit_bytes=PACK_VMEM),
-        cost_estimate=pl.CostEstimate(flops=0, bytes_accessed=rows * width * 4, transcendentals=0),
+        cost_estimate=pl.CostEstimate(
+            flops=NEXT_WAVE if after is not None and k >= 4 else 0, bytes_accessed=rows * width * 4, transcendentals=0
+        ),
         name="pack",
     )(*operands)
 
@@ -299,9 +302,10 @@
     for n in range(half):
         k = seq_count - 1 - n
         pieces[k] = swap(pack(place, qkv, readout_t, k, count, pieces[k + 2] if n > 1 else None), "seq", k)
-    for k in range(half):
-        packed = pack(place, qkv, readout_t, k, count, None)
-        pieces[k] = swap(packed, "seq", k) if k else packed
+    before = None
+    for k in range(1, half):
+        before = pieces[k] = swap(pack(place, qkv, readout_t, k, count, before), "seq", k)
+    pieces[0] = pack(place, qkv, readout_t, 0, count, None)
     late = [half, half + 1]
     early = [k for k in range(seq_count) if k not in late]
     sums, stats = attend_early([pieces[k] for k in early], early, span_frames, factor, me.reshape(1), count, lat)

time: 92.1 us -> 89.6 us (0.973)
  waiting for transfers between devices: 18.3 us -> 14.5 us
  local copies, waits for them, and re-layouts: 8.87 us -> 10.8 us
  Pallas kernels: 19.3 us -> 17.4 us
  starting transfers between devices: 41.7 us -> 42.9 us
    ppermute x14, waiting for transfers between devices: 18.3 us -> 14.5 us  [swap(): return lax.ppermute(array, axis, [(i, i ^ offset) for i in range(size)])]
    unnamed x20 -> x28, local copies, waits for them, and re-layouts: 7 us -> 8.97 us
    pallas_call x8, Pallas kernels: 9.84 us -> 8.36 us  [pack(): pl.pallas_call(pack_kernel, grid_spec=pltpu.PrefetchScalarGridSpec(num_sc...]
    ppermute x14, starting transfers between devices: 41.7 us -> 42.9 us  [swap(): return lax.ppermute(array, axis, [(i, i ^ offset) for i in range(size)])]
  transfers between devices with their start and end apart: 14 -> 14, of which waited for: 7 -> 8; matrix products, arithmetic and copies ran while one was open for 2% -> 2% of each run, Pallas kernels for 15% -> 14%
where the time goes in v10:
time: 89.6 us; the launch traced here: 89.1 us
  starting transfers between devices  42.9 us (48%)
  Pallas kernels  17.4 us (19%)
  waiting for transfers between devices  14.5 us (16%)
  local copies, waits for them, and re-layouts  10.8 us (12%)
  between operations  2.77 us (3%)
    ppermute x14, starting transfers between devices, swap(): return lax.ppermute(array, axis, [(i, i ^ offset) for i in range(size)])  42.9 us
    ppermute x14, waiting for transfers between devices, swap(): return lax.ppermute(array, axis, [(i, i ^ offset) for i in range(size)])  14.5 us
    unnamed x28, local copies, waits for them, and re-layouts  8.97 us
    pallas_call x8, Pallas kernels, pack(): pl.pallas_call(pack_kernel, grid_spec=pltpu.PrefetchScalarGridSpec(num_sc...  8.36 us
    pallas_call x1, Pallas kernels, attend_early(): pl.pallas_call(functools.partial(early_kernel, offsets), in_specs=[SMEM]...  4.89 us
    pallas_call x1, Pallas kernels, attend_late(): pl.pallas_call(functools.partial(late_kernel, offsets, late), in_specs=[S...  4.18 us
    dynamic_slice x2, local copies, waits for them, and re-layouts, body(): factor = (signed * step_weight[timestep[sample_index]]).reshape(1)  1.86 us
  transfers between devices with their start and end apart: 14, of which 8 were waited for; matrix products, arithmetic and copies ran while one was open for 2% of the time, Pallas kernels for 14%

profile of v10, /device:TPU:0, one launch (start us, length us, event | category | flops | bytes accessed | tf_op | source)
XLA Modules:
  0.0 89.1 jit_solution(4729575140093059134)
XLA Ops:
  0.0 0.1 pad_add_fusion.place_ref
  0.1 1.9 %copy-done = bf16[1,128,12288]{2,1,0:T(8,128)(2,1)S(1)} copy-done((bf16[1,128,12288]{2,1,0:T(8,128)(2,1)S(1)}, bf16[1,128,12288]{2,1,0:T(8,128)(2,1)}, u32[]{:S(2)}) %copy-start) | copy-done | bytes 3145752
  2.0 1.2 %copy-done.2 = bf16[2,4096,64]{1,2,0:T(8,128)(2,1)S(1)} copy-done((bf16[2,4096,64]{1,2,0:T(8,128)(2,1)S(1)}, bf16[2,4096,64]{1,2,0:T(8,128)(2,1)}, u32[]{:S(2)}) %copy-start.2) | copy-done | bytes 1048600
  3.2 0.8 pack.9
  4.0 3.0 %collective-permute-start = (bf16[128,1280]{1,0:T(8,128)(2,1)S(1)}, bf16[128,1280]{1,0:T(8,128)(2,1)S(1)}, u32[]{:S(2)}, u32[]{:S(2)}) collective-permute-start(bf16[128,1280]{1,0:T(8,128)(2,1)S(1)} %pack.9), channel_id=1, source_target_pairs={{0,4},{4,0},{8,12},{12,8},{16,20},{20,16},{24,28},{28,24},{1,5},{5... | collective-permute-start | bytes 983048 | tf_op jit(solution)/shard_map/ppermute | solution.py:282
  7.0 0.8 pack.12
  7.7 3.7 %collective-permute-start.3 = (bf16[128,1280]{1,0:T(8,128)(2,1)S(1)}, bf16[128,1280]{1,0:T(8,128)(2,1)S(1)}, u32[]{:S(2)}, u32[]{:S(2)}) collective-permute-start(bf16[128,1280]{1,0:T(8,128)(2,1)S(1)} %pack.12), channel_id=1, source_target_pairs={{0,24},{4,28},{8,16},{12,20},{16,8},{20,12},{24,0},{28,4},{1,25},{... | collective-permute-start | bytes 983048 | tf_op jit(solution)/shard_map/ppermute | solution.py:282
  11.4 0.8 pack.13
  12.2 0.1 collective-permute-start.4
  12.3 2.4 %collective-permute-done.refs_0_.refs_1_ = bf16[128,1280]{1,0:T(8,128)(2,1)S(1)} collective-permute-done((bf16[128,1280]{1,0:T(8,128)(2,1)S(1)}, bf16[128,1280]{1,0:T(8,128)(2,1)S(1)}, u32[]{:S(2)}, u32[]{:S(2)}) %collective-permute-start) | collective-permute-done | bytes 327712 | tf_op jit(solution)/shard_map/ppermute | solution.py:282
  14.7 0.8 pack.10
  15.5 1.9 %collective-permute-start.1 = (bf16[128,1280]{1,0:T(8,128)(2,1)S(1)}, bf16[128,1280]{1,0:T(8,128)(2,1)S(1)}, u32[]{:S(2)}, u32[]{:S(2)}) collective-permute-start(bf16[128,1280]{1,0:T(8,128)(2,1)S(1)} %pack.10), channel_id=1, source_target_pairs={{0,8},{4,12},{8,0},{12,4},{16,24},{20,28},{24,16},{28,20},{1,9},{5... | collective-permute-start | bytes 983048 | tf_op jit(solution)/shard_map/ppermute | solution.py:282
  17.3 3.0 %collective-permute-done.3.refs_0_.refs_4_ = bf16[128,1280]{1,0:T(8,128)(2,1)S(1)} collective-permute-done((bf16[128,1280]{1,0:T(8,128)(2,1)S(1)}, bf16[128,1280]{1,0:T(8,128)(2,1)S(1)}, u32[]{:S(2)}, u32[]{:S(2)}) %collective-permute-start.3) | collective-permute-done | bytes 327712 | tf_op jit(solution)/shard_map/ppermute | solution.py:282
  20.4 1.5 %pack.14 = bf16[128,1280]{1,0:T(8,128)(2,1)} custom-call(s32[2]{0:T(128)S(1)} %pad_add_fusion.place_ref, bf16[1,128,12288]{2,1,0:T(8,128)(2,1)S(1)} %copy-done, bf16[2,64,4096]{2,1,0:T(8,128)(2,1)S(1)} %bitcast.14, bf16[128,1280]{1,0:T(8,128)(2,1)S(1)} %collective-permute-done.3.refs_0_.refs_4_), custom_call_target="tpu_custom_call" | custom-call | flops 5000000000 | bytes 655360 | tf_op jit(solution)/shard_map/pack/pallas_call | solution.py:59
  21.9 14.7 %collective-permute-start.5 = (bf16[128,1280]{1,0:T(8,128)(2,1)}, bf16[128,1280]{1,0:T(8,128)(2,1)}, u32[]{:S(2)}, u32[]{:S(2)}) collective-permute-start(bf16[128,1280]{1,0:T(8,128)(2,1)} %pack.14), channel_id=1, source_target_pairs={{0,16},{4,20},{8,24},{12,28},{16,0},{20,4},{24,8},{28,12},{1,17},{... | collective-permute-start | bytes 983048 | tf_op jit(solution)/shard_map/ppermute | solution.py:282
  36.6 0.0 collective-permute-done.1.refs_0_.refs_2_
  36.6 1.5 %pack.11 = bf16[128,1280]{1,0:T(8,128)(2,1)} custom-call(s32[2]{0:T(128)S(1)} %pad_add_fusion.place_ref, bf16[1,128,12288]{2,1,0:T(8,128)(2,1)S(1)} %copy-done, bf16[2,64,4096]{2,1,0:T(8,128)(2,1)S(1)} %bitcast.15, bf16[128,1280]{1,0:T(8,128)(2,1)S(1)} %collective-permute-done.1.refs_0_.refs_2_), custom_call_target="tpu_custom_call" | custom-call | bytes 655360 | tf_op jit(solution)/shard_map/pack/pallas_call | solution.py:59
  38.1 0.0 collective-permute-start.2
  38.1 0.0 collective-permute-done.4.refs_0_.refs_5_
  38.1 1.5 %pack.15 = bf16[128,1280]{1,0:T(8,128)(2,1)} custom-call(s32[2]{0:T(128)S(1)} %pad_add_fusion.place_ref, bf16[1,128,12288]{2,1,0:T(8,128)(2,1)S(1)} %copy-done, bf16[2,64,4096]{2,1,0:T(8,128)(2,1)S(1)} %bitcast.16, bf16[128,1280]{1,0:T(8,128)(2,1)S(1)} %collective-permute-done.4.refs_0_.refs_5_), custom_call_target="tpu_custom_call" | custom-call | flops 5000000000 | bytes 655360 | tf_op jit(solution)/shard_map/pack/pallas_call | solution.py:59
  39.6 12.6 %collective-permute-start.6 = (bf16[128,1280]{1,0:T(8,128)(2,1)}, bf16[128,1280]{1,0:T(8,128)(2,1)}, u32[]{:S(2)}, u32[]{:S(2)}) collective-permute-start(bf16[128,1280]{1,0:T(8,128)(2,1)} %pack.15), channel_id=1, source_target_pairs={{0,20},{4,16},{8,28},{12,24},{16,4},{20,0},{24,12},{28,8},{1,21},{... | collective-permute-start | bytes 983048 | tf_op jit(solution)/shard_map/ppermute | solution.py:282
  52.2 1.2 %copy-done.3 = bf16[2,4096,64]{1,2,0:T(8,128)(2,1)S(1)} copy-done((bf16[2,4096,64]{1,2,0:T(8,128)(2,1)S(1)}, bf16[2,4096,64]{1,2,0:T(8,128)(2,1)}, u32[]{:S(2)}) %copy-start.3) | copy-done | bytes 1048600
  53.4 0.8 pack.8.refs_0_
  54.2 0.7 copy-done.6
  54.9 0.6 dynamic_slice.6
  57.5 1.3 %dynamic_slice.7 = f32[1]{0:T(128)} dynamic-slice(f32[1000]{0:T(1024)} %param.7, s32[]{:T(128)S(6)} %select_n.25), dynamic_slice_sizes={1} | dynamic-slice | bytes 12 | tf_op jit(solution)/shard_map/dynamic_slice | solution.py:297
  59.4 0.0 collective-permute-done.2.refs_3_
  59.4 1.0 %copy-done.5 = bf16[128,1280]{1,0:T(8,128)(2,1)S(1)} copy-done((bf16[128,1280]{1,0:T(8,128)(2,1)S(1)}, bf16[128,1280]{1,0:T(8,128)(2,1)}, u32[]{:S(2)}) %copy-start.5) | copy-done | bytes 327704
  60.4 1.0 %copy-done.7 = bf16[128,1280]{1,0:T(8,128)(2,1)S(1)} copy-done((bf16[128,1280]{1,0:T(8,128)(2,1)S(1)}, bf16[128,1280]{1,0:T(8,128)(2,1)}, u32[]{:S(2)}) %copy-start.7) | copy-done | bytes 327704
  61.4 1.0 %copy-done.9 = bf16[128,1280]{1,0:T(8,128)(2,1)S(1)} copy-done((bf16[128,1280]{1,0:T(8,128)(2,1)S(1)}, bf16[128,1280]{1,0:T(8,128)(2,1)}, u32[]{:S(2)}) %copy-start.9) | copy-done | bytes 327704
  62.3 1.0 %copy-done.11 = bf16[128,1280]{1,0:T(8,128)(2,1)S(1)} copy-done((bf16[128,1280]{1,0:T(8,128)(2,1)S(1)}, bf16[128,1280]{1,0:T(8,128)(2,1)}, u32[]{:S(2)}) %copy-start.11) | copy-done | bytes 327704
  63.3 4.9 %attend_early.1 = (f32[3,4,64,256]{3,2,1,0:T(8,128)S(1)}, f32[3,2,8,256]{3,2,1,0:T(8,128)S(1)}) custom-call(s32[4]{0:T(128)S(1)} %copy-done.12, f32[1]{0:T(128)} %bitcast.2.factor_ref, s32[1]{0:T(128)} %bitcast.3.me_ref, bf16[128,1280]{1,0:T(8,128)(2,1)S(1)} %copy-done.7, bf16[128,1280]{1,0:T(8,128)(2,1)S(1)} %collective-permute-done.refs_0_.refs_1_, ...), custom_call_target="tpu_custom_call" | custom-call | flops 905969664 | bytes 2359296 | tf_op jit(solution)/shard_map/attend_early/pallas_call | solution.py:235
  68.2 0.0 collective-permute-done.6.refs_7_
  68.2 4.2 %attend_late.1 = (f32[4,64,128]{2,1,0:T(8,128)S(1)}, bf16[4,64,128]{2,1,0:T(8,128)(2,1)S(1)}) custom-call(s32[4]{0:T(128)S(1)} %copy-done.12, f32[1]{0:T(128)} %bitcast.2.factor_ref, s32[1]{0:T(128)} %bitcast.3.me_ref, bf16[128,1280]{1,0:T(8,128)(2,1)S(1)} %copy-done.7, bf16[128,1280]{1,0:T(8,128)(2,1)S(1)} %collective-permute-done.refs_0_.refs_1_, ...), custom_call_target="tpu_custom_call" | custom-call | flops 402653184 | bytes 3145728 | tf_op jit(solution)/shard_map/attend_late/pallas_call | solution.py:261
  72.4 0.6 collective-permute-start.7
  73.0 3.7 %collective-permute-done.7 = bf16[4,64,128]{2,1,0:T(8,128)(2,1)S(1)} collective-permute-done((bf16[4,64,128]{2,1,0:T(8,128)(2,1)S(1)}, bf16[4,64,128]{2,1,0:T(8,128)(2,1)S(1)}, u32[]{:S(2)}, u32[]{:S(2)}) %collective-permute-start.7) | collective-permute-done | bytes 65568 | tf_op jit(solution)/shard_map/ppermute | solution.py:282
  76.8 1.6 %collective-permute-start.8 = (f32[1,64,128]{2,1,0:T(8,128)S(1)}, f32[1,64,128]{2,1,0:T(8,128)S(1)}, u32[]{:S(2)}, u32[]{:S(2)}) collective-permute-start(f32[1,64,128]{2,1,0:T(8,128)S(1)} %get-tuple-element.13), channel_id=1, source_target_pairs={{0,24},{4,28},{8,16},{12,20},{16,8},{20,12},{24,0},{28,4},{1,25},{... | collective-permute-start | bytes 98312 | tf_op jit(solution)/shard_map/ppermute | solution.py:282
  78.4 2.9 %collective-permute-start.9 = (f32[1,64,128]{2,1,0:T(8,128)S(1)}, f32[1,64,128]{2,1,0:T(8,128)S(1)}, u32[]{:S(2)}, u32[]{:S(2)}) collective-permute-start(f32[1,64,128]{2,1,0:T(8,128)S(1)} %get-tuple-element.15), channel_id=1, source_target_pairs={{0,8},{4,12},{8,0},{12,4},{16,24},{20,28},{24,16},{28,20},{1,9},{5... | collective-permute-start | bytes 98312 | tf_op jit(solution)/shard_map/ppermute | solution.py:282
  81.2 1.3 %collective-permute-done.8 = f32[1,64,128]{2,1,0:T(8,128)S(1)} collective-permute-done((f32[1,64,128]{2,1,0:T(8,128)S(1)}, f32[1,64,128]{2,1,0:T(8,128)S(1)}, u32[]{:S(2)}, u32[]{:S(2)}) %collective-permute-start.8) | collective-permute-done | bytes 32800 | tf_op jit(solution)/shard_map/ppermute | solution.py:282
  82.6 0.8 collective-permute-done.10
  83.4 0.1 collective-permute-done.9
  83.5 0.1 collective-permute-start.13
  83.6 1.6 %collective-permute-start.12 = (f32[64,128]{1,0:T(8,128)S(1)}, f32[64,128]{1,0:T(8,128)S(1)}, u32[]{:S(2)}, u32[]{:S(2)}) collective-permute-start(f32[64,128]{1,0:T(8,128)S(1)} %fusion.2), channel_id=1, source_target_pairs={{0,2},{1,3},{2,0},{3,1},{4,6},{5,7},{6,4},{7,5},{8,10},{9,11},{10,... | collective-permute-start | bytes 98312 | tf_op jit(solution)/shard_map/ppermute | solution.py:282
  85.2 0.3 collective-permute-start.11
  85.4 0.0 collective-permute-done.13
  85.4 2.1 %collective-permute-done.12 = f32[64,128]{1,0:T(8,128)S(1)} collective-permute-done((f32[64,128]{1,0:T(8,128)S(1)}, f32[64,128]{1,0:T(8,128)S(1)}, u32[]{:S(2)}, u32[]{:S(2)}) %collective-permute-start.12) | collective-permute-done | bytes 32800 | tf_op jit(solution)/shard_map/ppermute | solution.py:282
  87.6 0.9 %collective-permute-done.11 = f32[64,128]{1,0:T(8,128)S(1)} collective-permute-done((f32[64,128]{1,0:T(8,128)S(1)}, f32[64,128]{1,0:T(8,128)S(1)}, u32[]{:S(2)}, u32[]{:S(2)}) %collective-permute-start.11) | collective-permute-done | bytes 32800 | tf_op jit(solution)/shard_map/ppermute | solution.py:282
  88.5 0.6 add_bitcast_fusion
  (25 shorter events, 0.1 us)
Async XLA Ops:
  0.1 1.9 %copy-start = (bf16[1,128,12288]{2,1,0:T(8,128)(2,1)S(1)}, bf16[1,128,12288]{2,1,0:T(8,128)(2,1)}, u32[]{:S(2)}) copy-start(bf16[1,128,12288]{2,1,0:T(8,128)(2,1)} %qkv_ref.15) | copy-start | bytes 9437188
  2.0 1.2 %copy-start.2 = (bf16[2,4096,64]{1,2,0:T(8,128)(2,1)S(1)}, bf16[2,4096,64]{1,2,0:T(8,128)(2,1)}, u32[]{:S(2)}) copy-start(bf16[2,4096,64]{1,2,0:T(8,128)(2,1)} %param.6) | copy-start | bytes 3145732
  4.0 10.7 %collective-permute-start = (bf16[128,1280]{1,0:T(8,128)(2,1)S(1)}, bf16[128,1280]{1,0:T(8,128)(2,1)S(1)}, u32[]{:S(2)}, u32[]{:S(2)}) collective-permute-start(bf16[128,1280]{1,0:T(8,128)(2,1)S(1)} %pack.9), channel_id=1, source_target_pairs={{0,4},{4,0},{8,12},{12,8},{16,20},{20,16},{24,28},{28,24},{1,5},{5... | collective-permute-start | bytes 983048 | tf_op jit(solution)/shard_map/ppermute | solution.py:282
  7.7 12.7 %collective-permute-start.3 = (bf16[128,1280]{1,0:T(8,128)(2,1)S(1)}, bf16[128,1280]{1,0:T(8,128)(2,1)S(1)}, u32[]{:S(2)}, u32[]{:S(2)}) collective-permute-start(bf16[128,1280]{1,0:T(8,128)(2,1)S(1)} %pack.12), channel_id=1, source_target_pairs={{0,24},{4,28},{8,16},{12,20},{16,8},{20,12},{24,0},{28,4},{1,25},{... | collective-permute-start | bytes 983048 | tf_op jit(solution)/shard_map/ppermute | solution.py:282
  12.2 25.9 %collective-permute-start.4 = (bf16[128,1280]{1,0:T(8,128)(2,1)S(1)}, bf16[128,1280]{1,0:T(8,128)(2,1)S(1)}, u32[]{:S(2)}, u32[]{:S(2)}) collective-permute-start(bf16[128,1280]{1,0:T(8,128)(2,1)S(1)} %pack.13), channel_id=1, source_target_pairs={{0,28},{4,24},{8,20},{12,16},{16,12},{20,8},{24,4},{28,0},{1,29},{... | collective-permute-start | bytes 983048 | tf_op jit(solution)/shard_map/ppermute | solution.py:282
  15.5 21.1 %collective-permute-start.1 = (bf16[128,1280]{1,0:T(8,128)(2,1)S(1)}, bf16[128,1280]{1,0:T(8,128)(2,1)S(1)}, u32[]{:S(2)}, u32[]{:S(2)}) collective-permute-start(bf16[128,1280]{1,0:T(8,128)(2,1)S(1)} %pack.10), channel_id=1, source_target_pairs={{0,8},{4,12},{8,0},{12,4},{16,24},{20,28},{24,16},{28,20},{1,9},{5... | collective-permute-start | bytes 983048 | tf_op jit(solution)/shard_map/ppermute | solution.py:282
  20.4 1.5 %copy-start.8 = (bf16[128,1280]{1,0:T(8,128)(2,1)}, bf16[128,1280]{1,0:T(8,128)(2,1)S(1)}, u32[]{:S(2)}) copy-start(bf16[128,1280]{1,0:T(8,128)(2,1)S(1)} %collective-permute-done.3.refs_0_.refs_4_) | copy-start | bytes 983044
  21.9 46.3 %collective-permute-start.5 = (bf16[128,1280]{1,0:T(8,128)(2,1)}, bf16[128,1280]{1,0:T(8,128)(2,1)}, u32[]{:S(2)}, u32[]{:S(2)}) collective-permute-start(bf16[128,1280]{1,0:T(8,128)(2,1)} %pack.14), channel_id=1, source_target_pairs={{0,16},{4,20},{8,24},{12,28},{16,0},{20,4},{24,8},{28,12},{1,17},{... | collective-permute-start | bytes 983048 | tf_op jit(solution)/shard_map/ppermute | solution.py:282
  36.6 3.0 %copy-start.4 = (bf16[128,1280]{1,0:T(8,128)(2,1)}, bf16[128,1280]{1,0:T(8,128)(2,1)S(1)}, u32[]{:S(2)}) copy-start(bf16[128,1280]{1,0:T(8,128)(2,1)S(1)} %collective-permute-done.1.refs_0_.refs_2_) | copy-start | bytes 983044
  38.1 14.1 %copy-start.1 = (bf16[1,128,12288]{2,1,0:T(8,128)(2,1)S(1)}, bf16[1,128,12288]{2,1,0:T(8,128)(2,1)}, u32[]{:S(2)}) copy-start(bf16[1,128,12288]{2,1,0:T(8,128)(2,1)} %qkv_ref.15) | copy-start | bytes 9437188
  38.1 21.3 %collective-permute-start.2 = (bf16[128,1280]{1,0:T(8,128)(2,1)}, bf16[128,1280]{1,0:T(8,128)(2,1)}, u32[]{:S(2)}, u32[]{:S(2)}) collective-permute-start(bf16[128,1280]{1,0:T(8,128)(2,1)} %pack.11), channel_id=1, source_target_pairs={{0,12},{4,8},{8,4},{12,0},{16,28},{20,24},{24,20},{28,16},{1,13},{... | collective-permute-start | bytes 983048 | tf_op jit(solution)/shard_map/ppermute | solution.py:282
  38.1 1.5 %copy-start.10 = (bf16[128,1280]{1,0:T(8,128)(2,1)}, bf16[128,1280]{1,0:T(8,128)(2,1)S(1)}, u32[]{:S(2)}) copy-start(bf16[128,1280]{1,0:T(8,128)(2,1)S(1)} %collective-permute-done.4.refs_0_.refs_5_) | copy-start | bytes 983044
  39.6 15.3 %copy-start.13 = (s32[2]{0:T(128)S(1)}, s32[2]{0:T(128)}, u32[]{:S(2)}) copy-start(s32[2]{0:T(128)} %param.8) | copy-start | bytes 28
  39.6 19.8 %copy-start.12 = (s32[4]{0:T(128)S(1)}, s32[4]{0:T(128)}, u32[]{:S(2)}) copy-start(s32[4]{0:T(128)} %frames_ref.3) | copy-start | bytes 52
  39.6 28.6 %collective-permute-start.6 = (bf16[128,1280]{1,0:T(8,128)(2,1)}, bf16[128,1280]{1,0:T(8,128)(2,1)}, u32[]{:S(2)}, u32[]{:S(2)}) collective-permute-start(bf16[128,1280]{1,0:T(8,128)(2,1)} %pack.15), channel_id=1, source_target_pairs={{0,20},{4,16},{8,28},{12,24},{16,4},{20,0},{24,12},{28,8},{1,21},{... | collective-permute-start | bytes 983048 | tf_op jit(solution)/shard_map/ppermute | solution.py:282
  52.2 1.2 %copy-start.3 = (bf16[2,4096,64]{1,2,0:T(8,128)(2,1)S(1)}, bf16[2,4096,64]{1,2,0:T(8,128)(2,1)}, u32[]{:S(2)}) copy-start(bf16[2,4096,64]{1,2,0:T(8,128)(2,1)} %param.6) | copy-start | bytes 3145732
  54.2 0.7 copy-start.6
  59.4 1.0 %copy-start.5 = (bf16[128,1280]{1,0:T(8,128)(2,1)S(1)}, bf16[128,1280]{1,0:T(8,128)(2,1)}, u32[]{:S(2)}) copy-start(bf16[128,1280]{1,0:T(8,128)(2,1)} %copy-done.4) | copy-start | bytes 983044
  60.4 1.0 %copy-start.7 = (bf16[128,1280]{1,0:T(8,128)(2,1)S(1)}, bf16[128,1280]{1,0:T(8,128)(2,1)}, u32[]{:S(2)}) copy-start(bf16[128,1280]{1,0:T(8,128)(2,1)} %copy-done.6) | copy-start | bytes 983044
  61.4 1.0 %copy-start.9 = (bf16[128,1280]{1,0:T(8,128)(2,1)S(1)}, bf16[128,1280]{1,0:T(8,128)(2,1)}, u32[]{:S(2)}) copy-start(bf16[128,1280]{1,0:T(8,128)(2,1)} %copy-done.8) | copy-start | bytes 983044
  62.3 1.0 %copy-start.11 = (bf16[128,1280]{1,0:T(8,128)(2,1)S(1)}, bf16[128,1280]{1,0:T(8,128)(2,1)}, u32[]{:S(2)}) copy-start(bf16[128,1280]{1,0:T(8,128)(2,1)} %copy-done.10) | copy-start | bytes 983044
  72.4 4.3 %collective-permute-start.7 = (bf16[4,64,128]{2,1,0:T(8,128)(2,1)S(1)}, bf16[4,64,128]{2,1,0:T(8,128)(2,1)S(1)}, u32[]{:S(2)}, u32[]{:S(2)}) collective-permute-start(bf16[4,64,128]{2,1,0:T(8,128)(2,1)S(1)} %get-tuple-element.12), channel_id=1, source_target_pairs={{0,4},{4,0},{8,12},{12,8},{16,20},{20,16},{24,28},{28,24},{1,5},{5... | collective-permute-start | bytes 196616 | tf_op jit(solution)/shard_map/ppermute | solution.py:282
  76.8 5.8 %collective-permute-start.8 = (f32[1,64,128]{2,1,0:T(8,128)S(1)}, f32[1,64,128]{2,1,0:T(8,128)S(1)}, u32[]{:S(2)}, u32[]{:S(2)}) collective-permute-start(f32[1,64,128]{2,1,0:T(8,128)S(1)} %get-tuple-element.13), channel_id=1, source_target_pairs={{0,24},{4,28},{8,16},{12,20},{16,8},{20,12},{24,0},{28,4},{1,25},{... | collective-permute-start | bytes 98312 | tf_op jit(solution)/shard_map/ppermute | solution.py:282
  78.4 5.0 %collective-permute-start.10 = (f32[1,64,128]{2,1,0:T(8,128)S(1)}, f32[1,64,128]{2,1,0:T(8,128)S(1)}, u32[]{:S(2)}, u32[]{:S(2)}) collective-permute-start(f32[1,64,128]{2,1,0:T(8,128)S(1)} %get-tuple-element.14), channel_id=1, source_target_pairs={{0,16},{4,20},{8,24},{12,28},{16,0},{20,4},{24,8},{28,12},{1,17},{... | collective-permute-start | bytes 98312 | tf_op jit(solution)/shard_map/ppermute | solution.py:282
  78.4 5.1 %collective-permute-start.9 = (f32[1,64,128]{2,1,0:T(8,128)S(1)}, f32[1,64,128]{2,1,0:T(8,128)S(1)}, u32[]{:S(2)}, u32[]{:S(2)}) collective-permute-start(f32[1,64,128]{2,1,0:T(8,128)S(1)} %get-tuple-element.15), channel_id=1, source_target_pairs={{0,8},{4,12},{8,0},{12,4},{16,24},{20,28},{24,16},{28,20},{1,9},{5... | collective-permute-start | bytes 98312 | tf_op jit(solution)/shard_map/ppermute | solution.py:282
  83.5 1.9 %collective-permute-start.13 = (f32[64,128]{1,0:T(8,128)S(1)}, f32[64,128]{1,0:T(8,128)S(1)}, u32[]{:S(2)}, u32[]{:S(2)}) collective-permute-start(f32[64,128]{1,0:T(8,128)S(1)} %fusion.2), channel_id=1, source_target_pairs={{0,1},{1,0},{2,3},{3,2},{4,5},{5,4},{6,7},{7,6},{8,9},{9,8},{10,11... | collective-permute-start | bytes 98312 | tf_op jit(solution)/shard_map/ppermute | solution.py:282
  83.6 4.0 %collective-permute-start.12 = (f32[64,128]{1,0:T(8,128)S(1)}, f32[64,128]{1,0:T(8,128)S(1)}, u32[]{:S(2)}, u32[]{:S(2)}) collective-permute-start(f32[64,128]{1,0:T(8,128)S(1)} %fusion.2), channel_id=1, source_target_pairs={{0,2},{1,3},{2,0},{3,1},{4,6},{5,7},{6,4},{7,5},{8,10},{9,11},{10,... | collective-permute-start | bytes 98312 | tf_op jit(solution)/shard_map/ppermute | solution.py:282
  85.2 3.3 %collective-permute-start.11 = (f32[64,128]{1,0:T(8,128)S(1)}, f32[64,128]{1,0:T(8,128)S(1)}, u32[]{:S(2)}, u32[]{:S(2)}) collective-permute-start(f32[64,128]{1,0:T(8,128)S(1)} %fusion.2), channel_id=1, source_target_pairs={{0,3},{1,2},{2,1},{3,0},{4,7},{5,6},{6,5},{7,4},{8,11},{9,10},{10,... | collective-permute-start | bytes 98312 | tf_op jit(solution)/shard_map/ppermute | solution.py:282

commit v11 on v10

--- a/solution.py
+++ b/solution.py
@@ -14,13 +14,12 @@
 NT = (((1,), (1,)), ((), ()))
 LOG2_SCALE = math.log2(math.e) / math.sqrt(HD)
 LOWEST = -1e30
-NEXT_WAVE = 5000000000
-PACK_VMEM = 8 * 1024 * 1024
-ATTEND_VMEM = 20 * 1024 * 1024
-WHOLE_VMEM = 60 * 1024 * 1024
+NEXT_WAVE = 3000000000
+SMALL_VMEM = 24 * 1024 * 1024
+LARGE_VMEM = 60 * 1024 * 1024
 SMEM = pl.BlockSpec(memory_space=pltpu.SMEM)
 VMEM = pl.BlockSpec(memory_space=pltpu.VMEM)
-ANYWHERE = pl.BlockSpec(memory_space=pl.ANY)
+HBM = pl.BlockSpec(memory_space=pltpu.HBM)
 
 
 def fold(readout, values):
@@ -31,46 +30,56 @@
     return (h * lat) % HD, count * 2 * HD + (h * lat // HD) * HD
 
 
-def pack_kernel(place_ref, qkv_ref, readout_ref, *refs):
-    out_ref = refs[-1]
-    lat = readout_ref.shape[1]
-    count = readout_ref.shape[2] // HD
+def pack_kernel(k, me_ref, model_ref, qkv_ref, readout_ref, *refs):
+    out_ref, values, readout, sems = refs[-4:]
+    rows = out_ref.shape[0]
+    count, lat = values.shape[0], readout.shape[0]
+    first = (me_ref[0] ^ k) * count
+
+    def columns(h, part, width):
+        return pl.ds(pl.multiple_of(((first + h) * 3 + part) * HD, HD), width)
+
+    copies = [
+        pltpu.make_async_copy(
+            readout_ref.at[model_ref[0], :, pl.ds(pl.multiple_of(first * HD, HD), count * HD)], readout, sems.at[2 * count]
+        )
+    ]
     for h in range(count):
-        base = h * 3 * HD
-        out_ref[:, h * 2 * HD : (h + 1) * 2 * HD] = qkv_ref[0, :, base : base + 2 * HD]
+        copies.append(pltpu.make_async_copy(qkv_ref.at[0, :, columns(h, 2, HD)], values.at[h], sems.at[h]))
+    for h in range(count):
+        target = out_ref.at[:, h * 2 * HD : (h + 1) * 2 * HD]
+        copies.append(pltpu.make_async_copy(qkv_ref.at[0, :, columns(h, 0, 2 * HD)], target, sems.at[count + h]))
+    for copy in copies:
+        copy.start()
+    copies[0].wait()
+    for h in range(count):
+        copies[1 + h].wait()
         row, column = value_place(h, count, lat)
-        out_ref[row : row + lat, column : column + HD] = fold(
-            readout_ref[0, :, h * HD : (h + 1) * HD], qkv_ref[0, :, base + 2 * HD : base + 3 * HD]
-        )
-
-
-def pack(place, qkv, readout_t, k, count, after):
+        out_ref[row : row + lat, column : column + HD] = fold(readout[:, h * HD : (h + 1) * HD], values[h])
+    for copy in copies[1 + count :]:
+        copy.wait()
+
+
+def pack(me, model, qkv, readout_t, k, count, after, wave=False):
     rows = qkv.shape[1]
     lat = readout_t.shape[1]
     width = count * 2 * HD + -(-count * lat // HD) * HD
-    operands = [place, qkv, readout_t]
-    in_specs = [
-        pl.BlockSpec((1, rows, count * 3 * HD), lambda g, m: (0, 0, m[0] ^ k)),
-        pl.BlockSpec((1, lat, count * HD), lambda g, m: (m[1], 0, m[0] ^ k)),
-    ]
-    if after is not None:
-        operands += [after]
-        in_specs += [ANYWHERE]
     return pl.pallas_call(
-        pack_kernel,
-        grid_spec=pltpu.PrefetchScalarGridSpec(
-            num_scalar_prefetch=1,
-            grid=(1,),
-            in_specs=in_specs,
-            out_specs=pl.BlockSpec((rows, width), lambda g, m: (0, 0)),
-        ),
+        functools.partial(pack_kernel, k),
+        in_specs=[SMEM, SMEM] + [HBM] * (2 + len(after)),
+        out_specs=VMEM,
         out_shape=jax.ShapeDtypeStruct((rows, width), jnp.bfloat16),
-        compiler_params=pltpu.CompilerParams(vmem_limit_bytes=PACK_VMEM),
+        scratch_shapes=[
+            pltpu.VMEM((count, rows, HD), jnp.bfloat16),
+            pltpu.VMEM((lat, count * HD), jnp.bfloat16),
+            pltpu.SemaphoreType.DMA((2 * count + 1,)),
+        ],
+        compiler_params=pltpu.CompilerParams(vmem_limit_bytes=SMALL_VMEM),
         cost_estimate=pl.CostEstimate(
-            flops=NEXT_WAVE if after is not None and k >= 4 else 0, bytes_accessed=rows * width * 4, transcendentals=0
+            flops=NEXT_WAVE if wave else 0, bytes_accessed=rows * width * 4, transcendentals=0
         ),
         name="pack",
-    )(*operands)
+    )(me, model, qkv, readout_t, *after)
 
 
 def mask_rows(frames_ref, me, rows, query_offsets, key_offsets):
@@ -134,15 +143,22 @@
     return [read(n) for n in range(0, len(pieces), 2)]
 
 
-def early_kernel(offsets, frames_ref, factor_ref, me_ref, *refs):
+def early_kernel(offsets, frames_ref, me_ref, timestep_ref, step_weight_ref, sign_ref, sample_ref, *refs):
     count_pieces = len(offsets)
-    pieces = refs[:count_pieces]
-    sums_ref, stats_ref, asked, folded = refs[-4:]
+    arrived = refs[:count_pieces]
+    sums_ref, stats_ref, factor_ref, pieces, folded, asked, sems = refs[-7:]
     me = me_ref[0]
-    rows = pieces[0].shape[0]
+    rows = pieces.shape[1]
     lat = sums_ref.shape[2]
     count = folded.shape[0]
     blocks = count_pieces // 2
+    copies = [pltpu.make_async_copy(arrived[n], pieces.at[n], sems.at[n]) for n in range(count_pieces)]
+    for copy in copies:
+        copy.start()
+    factor_ref[...] = jnp.full(factor_ref.shape, sign_ref[0] * step_weight_ref[timestep_ref[sample_ref[0]]])
+    for copy in copies:
+        copy.wait()
+    pieces = [pieces.at[n] for n in range(count_pieces)]
     stage_values(folded, pieces, lat)
     for i in range(count):
         for b, read in enumerate(pairs_of(pieces, i, 0)):
@@ -174,15 +190,22 @@
     lax.fori_loop(0, blocks, some_blocks, 0)
 
 
-def late_kernel(offsets, late, frames_ref, factor_ref, me_ref, *refs):
+def late_kernel(offsets, late, frames_ref, me_ref, *refs):
     early = len(offsets)
-    pieces = refs[: early + 2]
-    sums_ref, stats_ref, keep_ref, give_ref, folded = refs[early + 2 :]
+    arrived = refs[:2]
+    sums_ref, stats_ref, factor_ref, early_ref, early_folded, keep_ref, give_ref, late_pieces, folded, sems = refs[2:]
+    copies = [pltpu.make_async_copy(arrived[n], late_pieces.at[n], sems.at[n]) for n in range(2)]
+    for copy in copies:
+        copy.start()
     me = me_ref[0]
     half, lat, rows = keep_ref.shape
     bits = half.bit_length()
     count = folded.shape[0]
-    stage_values(folded, pieces, lat)
+    for copy in copies:
+        copy.wait()
+    pieces = [early_ref.at[n] for n in range(early)] + [late_pieces.at[n] for n in range(2)]
+    stage_values(folded, pieces[early:], lat)
+    factor = factor_ref[:1]
     every = list(offsets) + list(late)
     results = {}
 
@@ -193,7 +216,7 @@
         for j in range(2):
             k = every[2 * b + j]
             n = sum(((k >> bit) & 1) << (bits - 1 - bit) for bit in range(bits))
-            part = results[b][:, j * rows : (j + 1) * rows] * factor_ref[0]
+            part = results[b][:, j * rows : (j + 1) * rows] * factor
             if n < half:
                 keep_ref[n] = part
             else:
@@ -223,58 +246,68 @@
             queries = pairs_of(pieces, i, 0)[b]
             keys = pairs_of(pieces, i, 1)
             tiles = [functools.partial(score_tile, keys[t], queries) for t in keys_in]
-            values = [lambda i=i, t=t: folded[i, :, t * 2 * rows : (t + 1) * 2 * rows] for t in keys_in]
+            values = [
+                lambda i=i, t=t: folded[i] if t == blocks else early_folded[i, :, t * 2 * rows : (t + 1) * 2 * rows]
+                for t in keys_in
+            ]
             units.append((tiles, values, shifts, finish))
     run_units(units, lat)
 
 
-def attend_early(pieces, offsets, span_frames, factor, me, count, lat):
-    rows = pieces[0].shape[0]
+def attend_early(pieces, offsets, span_frames, me, timestep, step_weight, sign, sample, count, lat):
+    rows, width = pieces[0].shape
     blocks = len(pieces) // 2
     tokens = len(pieces) * rows
     return pl.pallas_call(
         functools.partial(early_kernel, offsets),
-        in_specs=[SMEM] * 3 + [VMEM] * len(pieces),
-        out_specs=[VMEM, VMEM],
+        in_specs=[SMEM] * 6 + [HBM] * len(pieces),
+        out_specs=[VMEM] * 5,
         out_shape=[
             jax.ShapeDtypeStruct((blocks, count, lat, 2 * rows), jnp.float32),
             jax.ShapeDtypeStruct((blocks, 2, 8, 2 * rows), jnp.float32),
+            jax.ShapeDtypeStruct((8, rows), jnp.float32),
+            jax.ShapeDtypeStruct((len(pieces), rows, width), jnp.bfloat16),
+            jax.ShapeDtypeStruct((count, lat + 16, tokens), jnp.bfloat16),
         ],
         scratch_shapes=[
             pltpu.VMEM((blocks, count, 2 * rows, HD), jnp.bfloat16),
-            pltpu.VMEM((count, lat + 16, tokens), jnp.bfloat16),
-        ],
-        compiler_params=pltpu.CompilerParams(vmem_limit_bytes=ATTEND_VMEM if len(pieces) <= 8 else WHOLE_VMEM),
+            pltpu.SemaphoreType.DMA((len(pieces),)),
+        ],
+        compiler_params=pltpu.CompilerParams(vmem_limit_bytes=SMALL_VMEM if len(pieces) <= 8 else LARGE_VMEM),
         cost_estimate=pl.CostEstimate(
             flops=count * tokens * tokens * 2 * (HD + lat),
             bytes_accessed=tokens * count * 3 * HD * 2,
             transcendentals=count * tokens * tokens,
         ),
         name="attend_early",
-    )(span_frames, factor, me, *pieces)
-
-
-def attend_late(pieces, offsets, late, sums, stats, span_frames, factor, me, count, lat):
-    rows = pieces[0].shape[0]
-    tokens = len(pieces) * rows
-    half = len(pieces) // 2
+    )(span_frames, me, timestep, step_weight, sign, sample, *pieces)
+
+
+def attend_late(pieces, offsets, late, early, span_frames, me, count, lat):
+    rows, width = pieces[0].shape
+    half = len(offsets) // 2 + 1
+    tokens = 2 * half * rows
     return pl.pallas_call(
         functools.partial(late_kernel, offsets, late),
-        in_specs=[SMEM] * 3 + [VMEM] * (len(pieces) + 2),
+        in_specs=[SMEM] * 2 + [HBM] * 2 + [VMEM] * len(early),
         out_specs=[VMEM, VMEM],
         out_shape=[
             jax.ShapeDtypeStruct((half, lat, rows), jnp.float32),
             jax.ShapeDtypeStruct((half, lat, rows), jnp.bfloat16),
         ],
-        scratch_shapes=[pltpu.VMEM((count, lat + 16, tokens), jnp.bfloat16)],
-        compiler_params=pltpu.CompilerParams(vmem_limit_bytes=ATTEND_VMEM if len(pieces) <= 8 else WHOLE_VMEM),
+        scratch_shapes=[
+            pltpu.VMEM((2, rows, width), jnp.bfloat16),
+            pltpu.VMEM((count, lat + 16, 2 * rows), jnp.bfloat16),
+            pltpu.SemaphoreType.DMA((2,)),
+        ],
+        compiler_params=pltpu.CompilerParams(vmem_limit_bytes=SMALL_VMEM if half <= 4 else LARGE_VMEM),
         cost_estimate=pl.CostEstimate(
             flops=count * tokens * rows * 4 * (HD + lat),
             bytes_accessed=tokens * count * 3 * HD * 2,
             transcendentals=count * tokens * rows * 2,
         ),
         name="attend_late",
-    )(span_frames, factor, me, *pieces, sums, stats)
+    )(span_frames, me, *pieces, *early)
 
 
 def swap(array, axis, offset):
@@ -288,30 +321,32 @@
     half = seq_count // 2
     count = HEADS // seq_count
     lat = readout.shape[2]
-    me = lax.axis_index("seq").astype(jnp.int32)
-    mp_index = lax.axis_index("mp")
+    me = lax.axis_index("seq").astype(jnp.int32).reshape(1)
+    mp_index = lax.axis_index("mp").astype(jnp.int32)
     sample_count = mp_count // 2
-    model_index = (mp_index // sample_count).astype(jnp.int32)
-    sample_index = mp_index % sample_count
-    signed = jnp.where(model_index == 1, 1.0, -1.0).astype(jnp.float32)
-    factor = (signed * step_weight[timestep[sample_index]]).reshape(1)
+    model_index = mp_index // sample_count
+    sample = (mp_index % sample_count).reshape(1)
+    sign = jnp.where(model_index == 1, 1.0, -1.0).astype(jnp.float32).reshape(1)
+    model = model_index.reshape(1)
     readout_t = jnp.swapaxes(readout, 1, 2)
-    place = jnp.stack([me, model_index])
 
     pieces = [None] * seq_count
+    packed = {}
     for n in range(half):
         k = seq_count - 1 - n
-        pieces[k] = swap(pack(place, qkv, readout_t, k, count, pieces[k + 2] if n > 1 else None), "seq", k)
-    before = None
+        after = [pieces[k + 2]] if n > 1 else []
+        packed[k] = pack(me, model, qkv, readout_t, k, count, after, n > 1)
+        pieces[k] = swap(packed[k], "seq", k)
     for k in range(1, half):
-        before = pieces[k] = swap(pack(place, qkv, readout_t, k, count, before), "seq", k)
-    pieces[0] = pack(place, qkv, readout_t, 0, count, None)
+        after = [pieces[k - 1]] if k > 2 else []
+        pieces[k] = swap(pack(me, model, qkv, readout_t, k, count, after), "seq", k)
+    pieces[0] = pack(me, model, qkv, readout_t, 0, count, [packed[seq_count - 2]])
     late = [half, half + 1]
     early = [k for k in range(seq_count) if k not in late]
-    sums, stats = attend_early([pieces[k] for k in early], early, span_frames, factor, me.reshape(1), count, lat)
-    keep, give = attend_late(
-        [pieces[k] for k in early + late], early, late, sums, stats, span_frames, factor, me.reshape(1), count, lat
+    merged = attend_early(
+        [pieces[k] for k in early], early, span_frames, me, timestep, step_weight, sign, sample, count, lat
     )
+    keep, give = attend_late([pieces[k] for k in late], early, late, merged, span_frames, me, count, lat)
 
     keep = keep + swap(give, "seq", 1).astype(jnp.float32)
     offset = 2

time: 89.6 us -> 87.8 us (0.980)
  local copies, waits for them, and re-layouts: 10.8 us -> 3.14 us
  waiting for transfers between devices: 14.5 us -> 20.9 us
  starting transfers between devices: 42.9 us -> 45.7 us
  between operations: 2.77 us -> 0.2 us
    ppermute x14, waiting for transfers between devices: 14.5 us -> 20.9 us  [swap(): return lax.ppermute(array, axis, [(i, i ^ offset) for i in range(size)])]
    unnamed x28 -> x10, local copies, waits for them, and re-layouts: 8.97 us -> 3.13 us
    ppermute x14, starting transfers between devices: 42.9 us -> 45.7 us  [swap(): return lax.ppermute(array, axis, [(i, i ^ offset) for i in range(size)])]
    dynamic_slice x2 -> x0, local copies, waits for them, and re-layouts: 1.86 us -> none  [body(): factor = (signed * step_weight[timestep[sample_index]]).reshape(1)]
  transfers between devices with their start and end apart: 14 -> 14, of which waited for: 8 -> 10; matrix products, arithmetic and copies ran while one was open for 2% -> 0% of each run, Pallas kernels for 14% -> 14%
where the time goes in v11:
time: 87.8 us; the launch traced here: 87.6 us
  starting transfers between devices  45.7 us (52%)
  waiting for transfers between devices  20.9 us (24%)
  Pallas kernels  17 us (19%)
  local copies, waits for them, and re-layouts  3.14 us (4%)
    ppermute x14, starting transfers between devices, swap(): return lax.ppermute(array, axis, [(i, i ^ offset) for i in range(size)])  45.7 us
    ppermute x14, waiting for transfers between devices, swap(): return lax.ppermute(array, axis, [(i, i ^ offset) for i in range(size)])  20.9 us
    pallas_call x8, Pallas kernels, pack(): pl.pallas_call(functools.partial(pack_kernel, k), in_specs=[SMEM, SMEM] +...  7.89 us
    pallas_call x1, Pallas kernels, attend_early(): pl.pallas_call(functools.partial(early_kernel, offsets), in_specs=[SMEM]...  5.3 us
    pallas_call x1, Pallas kernels, attend_late(): pl.pallas_call(functools.partial(late_kernel, offsets, late), in_specs=[S...  3.8 us
    unnamed x10, local copies, waits for them, and re-layouts  3.13 us
  transfers between devices with their start and end apart: 14, of which 10 were waited for; matrix products, arithmetic and copies ran while one was open for 0% of the time, Pallas kernels for 14%

profile of v11, /device:TPU:0, one launch (start us, length us, event | category | flops | bytes accessed | tf_op | source)
XLA Modules:
  0.0 87.6 jit_solution(1501382424323841520)
XLA Ops:
  0.0 0.0 copy-start
  0.0 1.9 %copy-done = bf16[1,128,12288]{2,1,0:T(8,128)(2,1)S(1)} copy-done((bf16[1,128,12288]{2,1,0:T(8,128)(2,1)S(1)}, bf16[1,128,12288]{2,1,0:T(8,128)(2,1)}, u32[]{:S(2)}) %copy-start) | copy-done | bytes 3145752
  1.9 1.2 %copy-done.1 = bf16[2,4096,64]{1,2,0:T(8,128)(2,1)S(1)} copy-done((bf16[2,4096,64]{1,2,0:T(8,128)(2,1)S(1)}, bf16[2,4096,64]{1,2,0:T(8,128)(2,1)}, u32[]{:S(2)}) %copy-start.1) | copy-done | bytes 1048600
  3.1 0.8 pack.14
  3.9 3.1 %collective-permute-start.5 = (bf16[128,1280]{1,0:T(8,128)(2,1)S(1)}, bf16[128,1280]{1,0:T(8,128)(2,1)S(1)}, u32[]{:S(2)}, u32[]{:S(2)}) collective-permute-start(bf16[128,1280]{1,0:T(8,128)(2,1)S(1)} %pack.14), channel_id=1, source_target_pairs={{0,8},{4,12},{8,0},{12,4},{16,24},{20,28},{24,16},{28,20},{1,9},{5... | collective-permute-start | bytes 983048 | tf_op jit(solution)/shard_map/ppermute | solution.py:315
  7.0 0.8 pack.10
  7.8 3.5 %collective-permute-start.2 = (bf16[128,1280]{1,0:T(8,128)(2,1)S(1)}, bf16[128,1280]{1,0:T(8,128)(2,1)S(1)}, u32[]{:S(2)}, u32[]{:S(2)}) collective-permute-start(bf16[128,1280]{1,0:T(8,128)(2,1)S(1)} %pack.10), channel_id=1, source_target_pairs={{0,28},{4,24},{8,20},{12,16},{16,12},{20,8},{24,4},{28,0},{1,29},{... | collective-permute-start | bytes 983048 | tf_op jit(solution)/shard_map/ppermute | solution.py:315
  11.3 0.8 pack.8.refs_0_
  12.1 1.4 %collective-permute-start = (bf16[128,1280]{1,0:T(8,128)(2,1)S(1)}, bf16[128,1280]{1,0:T(8,128)(2,1)S(1)}, u32[]{:S(2)}, u32[]{:S(2)}) collective-permute-start(bf16[128,1280]{1,0:T(8,128)(2,1)S(1)} %pack.8.refs_0_), channel_id=1, source_target_pairs={{0,24},{4,28},{8,16},{12,20},{16,8},{20,12},{24,0},{28,4},{1,25},{... | collective-permute-start | bytes 983048 | tf_op jit(solution)/shard_map/ppermute | solution.py:315
  13.5 0.8 pack.13
  14.3 0.6 collective-permute-start.4
  14.9 0.2 collective-permute-done.5.refs_0_.refs_2_
  15.1 0.8 pack.15
  15.9 3.5 %collective-permute-start.6 = (bf16[128,1280]{1,0:T(8,128)(2,1)S(1)}, bf16[128,1280]{1,0:T(8,128)(2,1)S(1)}, u32[]{:S(2)}, u32[]{:S(2)}) collective-permute-start(bf16[128,1280]{1,0:T(8,128)(2,1)S(1)} %pack.15), channel_id=1, source_target_pairs={{0,12},{4,8},{8,4},{12,0},{16,28},{20,24},{24,20},{28,16},{1,13},{... | collective-permute-start | bytes 983048 | tf_op jit(solution)/shard_map/ppermute | solution.py:315
  19.4 6.7 %collective-permute-done.2.refs_0_.refs_5_ = bf16[128,1280]{1,0:T(8,128)(2,1)S(1)} collective-permute-done((bf16[128,1280]{1,0:T(8,128)(2,1)S(1)}, bf16[128,1280]{1,0:T(8,128)(2,1)S(1)}, u32[]{:S(2)}, u32[]{:S(2)}) %collective-permute-start.2) | collective-permute-done | bytes 327712 | tf_op jit(solution)/shard_map/ppermute | solution.py:315
  26.2 1.5 %pack.11 = bf16[128,1280]{1,0:T(8,128)(2,1)} custom-call(s32[1]{0:T(128)} %bitcast.me_ref, s32[1]{0:T(128)} %bitcast.1.model_ref, bf16[1,128,12288]{2,1,0:T(8,128)(2,1)S(1)} %copy-done, bf16[2,64,4096]{2,1,0:T(8,128)(2,1)S(1)} %bitcast.14, bf16[128,1280]{1,0:T(8,128)(2,1)S(1)} %collective-permute-done.2.refs_0_.refs_5_), custom_call_target="tpu_custom_call" | custom-call | flops 3000000000 | bytes 655360 | tf_op jit(solution)/shard_map/pack/pallas_call | solution.py:67
  27.7 11.8 %collective-permute-start.3 = (bf16[128,1280]{1,0:T(8,128)(2,1)}, bf16[128,1280]{1,0:T(8,128)(2,1)S(1)}, u32[]{:S(2)}, u32[]{:S(2)}) collective-permute-start(bf16[128,1280]{1,0:T(8,128)(2,1)} %pack.11), channel_id=1, source_target_pairs={{0,20},{4,16},{8,28},{12,24},{16,4},{20,0},{24,12},{28,8},{1,21},{... | collective-permute-start | bytes 983048 | tf_op jit(solution)/shard_map/ppermute | solution.py:315
  39.5 0.0 collective-permute-done.refs_0_.refs_4_
  39.5 1.5 %pack.9 = bf16[128,1280]{1,0:T(8,128)(2,1)} custom-call(s32[1]{0:T(128)} %bitcast.me_ref, s32[1]{0:T(128)} %bitcast.1.model_ref, bf16[1,128,12288]{2,1,0:T(8,128)(2,1)S(1)} %copy-done, bf16[2,64,4096]{2,1,0:T(8,128)(2,1)S(1)} %bitcast.15, bf16[128,1280]{1,0:T(8,128)(2,1)S(1)} %collective-permute-done.refs_0_.refs_4_), custom_call_target="tpu_custom_call" | custom-call | flops 3000000000 | bytes 655360 | tf_op jit(solution)/shard_map/pack/pallas_call | solution.py:67
  41.0 0.0 copy-start.2
  41.0 0.0 copy-start.3
  41.0 0.0 copy-start.4
  41.1 14.2 %collective-permute-start.1 = (bf16[128,1280]{1,0:T(8,128)(2,1)}, bf16[128,1280]{1,0:T(8,128)(2,1)S(1)}, u32[]{:S(2)}, u32[]{:S(2)}) collective-permute-start(bf16[128,1280]{1,0:T(8,128)(2,1)} %pack.9), channel_id=1, source_target_pairs={{0,16},{4,20},{8,24},{12,28},{16,0},{20,4},{24,8},{28,12},{1,17},{... | collective-permute-start | bytes 983048 | tf_op jit(solution)/shard_map/ppermute | solution.py:315
  55.3 0.8 pack.12.refs_0_
  56.1 0.0 collective-permute-done.4.refs_1_
  56.1 0.0 collective-permute-done.6.refs_3_
  56.1 0.0 copy-done.2
  56.2 0.0 copy-done.3
  56.2 0.0 copy-done.4
  56.2 5.3 %attend_early.1 = (f32[3,4,64,256]{3,2,1,0:T(8,128)S(1)}, f32[3,2,8,256]{3,2,1,0:T(8,128)S(1)}, f32[8,128]{1,0:T(8,128)S(1)}, bf16[6,128,1280]{2,1,0:T(8,128)(2,1)S(1)}, bf16[4,80,768]{2,1,0:T(8,128)(2,1)S(1)}) custom-call(s32[4]{0:T(128)S(1)} %copy-done.2, s32[1]{0:T(128)} %bitcast.me_ref, s32[2]{0:T(128)S(1)} %copy-done.4, f32[1000]{0:T(1024)S(1)} %copy-done.3, ...), custom_call_target="tpu_custom_call" | custom-call | flops 905969664 | bytes 2359296 | tf_op jit(solution)/shard_map/attend_early/pallas_call | solution.py:261
  61.5 0.7 collective-permute-done.3.refs_1_
  62.1 4.9 %collective-permute-done.1.refs_0_ = bf16[128,1280]{1,0:T(8,128)(2,1)S(1)} collective-permute-done((bf16[128,1280]{1,0:T(8,128)(2,1)}, bf16[128,1280]{1,0:T(8,128)(2,1)S(1)}, u32[]{:S(2)}, u32[]{:S(2)}) %collective-permute-start.1) | collective-permute-done | bytes 327712 | tf_op jit(solution)/shard_map/ppermute | solution.py:315
  67.1 3.8 %attend_late.1 = (f32[4,64,128]{2,1,0:T(8,128)S(1)}, bf16[4,64,128]{2,1,0:T(8,128)(2,1)S(1)}) custom-call(s32[4]{0:T(128)S(1)} %copy-done.2, s32[1]{0:T(128)} %bitcast.me_ref, bf16[128,1280]{1,0:T(8,128)(2,1)S(1)} %collective-permute-done.1.refs_0_, bf16[128,1280]{1,0:T(8,128)(2,1)S(1)} %collective-permute-done.3.refs_1_, ...), custom_call_target="tpu_custom_call" | custom-call | flops 402653184 | bytes 3145728 | tf_op jit(solution)/shard_map/attend_late/pallas_call | solution.py:290
  70.9 1.6 %collective-permute-start.7 = (bf16[4,64,128]{2,1,0:T(8,128)(2,1)S(1)}, bf16[4,64,128]{2,1,0:T(8,128)(2,1)S(1)}, u32[]{:S(2)}, u32[]{:S(2)}) collective-permute-start(bf16[4,64,128]{2,1,0:T(8,128)(2,1)S(1)} %get-tuple-element.18), channel_id=1, source_target_pairs={{0,4},{4,0},{8,12},{12,8},{16,20},{20,16},{24,28},{28,24},{1,5},{5... | collective-permute-start | bytes 196616 | tf_op jit(solution)/shard_map/ppermute | solution.py:315
  72.4 2.8 %collective-permute-done.7 = bf16[4,64,128]{2,1,0:T(8,128)(2,1)S(1)} collective-permute-done((bf16[4,64,128]{2,1,0:T(8,128)(2,1)S(1)}, bf16[4,64,128]{2,1,0:T(8,128)(2,1)S(1)}, u32[]{:S(2)}, u32[]{:S(2)}) %collective-permute-start.7) | collective-permute-done | bytes 65568 | tf_op jit(solution)/shard_map/ppermute | solution.py:315
  75.3 0.1 collective-permute-start.10
  75.3 3.6 %collective-permute-start.8 = (f32[1,64,128]{2,1,0:T(8,128)S(1)}, f32[1,64,128]{2,1,0:T(8,128)S(1)}, u32[]{:S(2)}, u32[]{:S(2)}) collective-permute-start(f32[1,64,128]{2,1,0:T(8,128)S(1)} %get-tuple-element.19), channel_id=1, source_target_pairs={{0,24},{4,28},{8,16},{12,20},{16,8},{20,12},{24,0},{28,4},{1,25},{... | collective-permute-start | bytes 98312 | tf_op jit(solution)/shard_map/ppermute | solution.py:315
  78.9 0.5 collective-permute-start.9
  79.4 0.7 collective-permute-done.10
  80.1 1.0 %collective-permute-done.8 = f32[1,64,128]{2,1,0:T(8,128)S(1)} collective-permute-done((f32[1,64,128]{2,1,0:T(8,128)S(1)}, f32[1,64,128]{2,1,0:T(8,128)S(1)}, u32[]{:S(2)}, u32[]{:S(2)}) %collective-permute-start.8) | collective-permute-done | bytes 32800 | tf_op jit(solution)/shard_map/ppermute | solution.py:315
  81.1 1.7 %collective-permute-done.9 = f32[1,64,128]{2,1,0:T(8,128)S(1)} collective-permute-done((f32[1,64,128]{2,1,0:T(8,128)S(1)}, f32[1,64,128]{2,1,0:T(8,128)S(1)}, u32[]{:S(2)}, u32[]{:S(2)}) %collective-permute-start.9) | collective-permute-done | bytes 32800 | tf_op jit(solution)/shard_map/ppermute | solution.py:315
  82.9 0.1 collective-permute-start.11
  82.9 1.6 %collective-permute-start.12 = (f32[64,128]{1,0:T(8,128)S(1)}, f32[64,128]{1,0:T(8,128)S(1)}, u32[]{:S(2)}, u32[]{:S(2)}) collective-permute-start(f32[64,128]{1,0:T(8,128)S(1)} %fusion.2), channel_id=1, source_target_pairs={{0,2},{1,3},{2,0},{3,1},{4,6},{5,7},{6,4},{7,5},{8,10},{9,11},{10,... | collective-permute-start | bytes 98312 | tf_op jit(solution)/shard_map/ppermute | solution.py:315
  84.5 0.3 collective-permute-start.13
  84.8 1.8 %collective-permute-done.11 = f32[64,128]{1,0:T(8,128)S(1)} collective-permute-done((f32[64,128]{1,0:T(8,128)S(1)}, f32[64,128]{1,0:T(8,128)S(1)}, u32[]{:S(2)}, u32[]{:S(2)}) %collective-permute-start.11) | collective-permute-done | bytes 32800 | tf_op jit(solution)/shard_map/ppermute | solution.py:315
  86.5 0.4 collective-permute-done.12
  87.0 0.0 collective-permute-done.13
  87.0 0.6 add_bitcast_fusion
  (4 shorter events, 0.0 us)
Async XLA Ops:
  0.0 1.9 %copy-start = (bf16[1,128,12288]{2,1,0:T(8,128)(2,1)S(1)}, bf16[1,128,12288]{2,1,0:T(8,128)(2,1)}, u32[]{:S(2)}) copy-start(bf16[1,128,12288]{2,1,0:T(8,128)(2,1)} %qkv_ref.15) | copy-start | bytes 9437188
  1.9 1.2 %copy-start.1 = (bf16[2,4096,64]{1,2,0:T(8,128)(2,1)S(1)}, bf16[2,4096,64]{1,2,0:T(8,128)(2,1)}, u32[]{:S(2)}) copy-start(bf16[2,4096,64]{1,2,0:T(8,128)(2,1)} %param.6) | copy-start | bytes 3145732
  3.9 11.2 %collective-permute-start.5 = (bf16[128,1280]{1,0:T(8,128)(2,1)S(1)}, bf16[128,1280]{1,0:T(8,128)(2,1)S(1)}, u32[]{:S(2)}, u32[]{:S(2)}) collective-permute-start(bf16[128,1280]{1,0:T(8,128)(2,1)S(1)} %pack.14), channel_id=1, source_target_pairs={{0,8},{4,12},{8,0},{12,4},{16,24},{20,28},{24,16},{28,20},{1,9},{5... | collective-permute-start | bytes 983048 | tf_op jit(solution)/shard_map/ppermute | solution.py:315
  7.8 18.3 %collective-permute-start.2 = (bf16[128,1280]{1,0:T(8,128)(2,1)S(1)}, bf16[128,1280]{1,0:T(8,128)(2,1)S(1)}, u32[]{:S(2)}, u32[]{:S(2)}) collective-permute-start(bf16[128,1280]{1,0:T(8,128)(2,1)S(1)} %pack.10), channel_id=1, source_target_pairs={{0,28},{4,24},{8,20},{12,16},{16,12},{20,8},{24,4},{28,0},{1,29},{... | collective-permute-start | bytes 983048 | tf_op jit(solution)/shard_map/ppermute | solution.py:315
  12.1 27.4 %collective-permute-start = (bf16[128,1280]{1,0:T(8,128)(2,1)S(1)}, bf16[128,1280]{1,0:T(8,128)(2,1)S(1)}, u32[]{:S(2)}, u32[]{:S(2)}) collective-permute-start(bf16[128,1280]{1,0:T(8,128)(2,1)S(1)} %pack.8.refs_0_), channel_id=1, source_target_pairs={{0,24},{4,28},{8,16},{12,20},{16,8},{20,12},{24,0},{28,4},{1,25},{... | collective-permute-start | bytes 983048 | tf_op jit(solution)/shard_map/ppermute | solution.py:315
  14.3 41.8 %collective-permute-start.4 = (bf16[128,1280]{1,0:T(8,128)(2,1)S(1)}, bf16[128,1280]{1,0:T(8,128)(2,1)S(1)}, u32[]{:S(2)}, u32[]{:S(2)}) collective-permute-start(bf16[128,1280]{1,0:T(8,128)(2,1)S(1)} %pack.13), channel_id=1, source_target_pairs={{0,4},{4,0},{8,12},{12,8},{16,20},{20,16},{24,28},{28,24},{1,5},{5... | collective-permute-start | bytes 983048 | tf_op jit(solution)/shard_map/ppermute | solution.py:315
  15.9 40.2 %collective-permute-start.6 = (bf16[128,1280]{1,0:T(8,128)(2,1)S(1)}, bf16[128,1280]{1,0:T(8,128)(2,1)S(1)}, u32[]{:S(2)}, u32[]{:S(2)}) collective-permute-start(bf16[128,1280]{1,0:T(8,128)(2,1)S(1)} %pack.15), channel_id=1, source_target_pairs={{0,12},{4,8},{8,4},{12,0},{16,28},{20,24},{24,20},{28,16},{1,13},{... | collective-permute-start | bytes 983048 | tf_op jit(solution)/shard_map/ppermute | solution.py:315
  27.7 34.4 %collective-permute-start.3 = (bf16[128,1280]{1,0:T(8,128)(2,1)}, bf16[128,1280]{1,0:T(8,128)(2,1)S(1)}, u32[]{:S(2)}, u32[]{:S(2)}) collective-permute-start(bf16[128,1280]{1,0:T(8,128)(2,1)} %pack.11), channel_id=1, source_target_pairs={{0,20},{4,16},{8,28},{12,24},{16,4},{20,0},{24,12},{28,8},{1,21},{... | collective-permute-start | bytes 983048 | tf_op jit(solution)/shard_map/ppermute | solution.py:315
  41.0 15.1 %copy-start.2 = (s32[4]{0:T(128)S(1)}, s32[4]{0:T(128)}, u32[]{:S(2)}) copy-start(s32[4]{0:T(128)} %frames_ref.3) | copy-start | bytes 52
  41.0 15.1 %copy-start.3 = (f32[1000]{0:T(1024)S(1)}, f32[1000]{0:T(1024)}, u32[]{:S(2)}) copy-start(f32[1000]{0:T(1024)} %step_weight_ref.1) | copy-start | bytes 12004
  41.0 15.1 %copy-start.4 = (s32[2]{0:T(128)S(1)}, s32[2]{0:T(128)}, u32[]{:S(2)}) copy-start(s32[2]{0:T(128)} %timestep_ref.1) | copy-start | bytes 28
  41.1 26.0 %collective-permute-start.1 = (bf16[128,1280]{1,0:T(8,128)(2,1)}, bf16[128,1280]{1,0:T(8,128)(2,1)S(1)}, u32[]{:S(2)}, u32[]{:S(2)}) collective-permute-start(bf16[128,1280]{1,0:T(8,128)(2,1)} %pack.9), channel_id=1, source_target_pairs={{0,16},{4,20},{8,24},{12,28},{16,0},{20,4},{24,8},{28,12},{1,17},{... | collective-permute-start | bytes 983048 | tf_op jit(solution)/shard_map/ppermute | solution.py:315
  70.9 4.3 %collective-permute-start.7 = (bf16[4,64,128]{2,1,0:T(8,128)(2,1)S(1)}, bf16[4,64,128]{2,1,0:T(8,128)(2,1)S(1)}, u32[]{:S(2)}, u32[]{:S(2)}) collective-permute-start(bf16[4,64,128]{2,1,0:T(8,128)(2,1)S(1)} %get-tuple-element.18), channel_id=1, source_target_pairs={{0,4},{4,0},{8,12},{12,8},{16,20},{20,16},{24,28},{28,24},{1,5},{5... | collective-permute-start | bytes 196616 | tf_op jit(solution)/shard_map/ppermute | solution.py:315
  75.3 4.9 %collective-permute-start.10 = (f32[1,64,128]{2,1,0:T(8,128)S(1)}, f32[1,64,128]{2,1,0:T(8,128)S(1)}, u32[]{:S(2)}, u32[]{:S(2)}) collective-permute-start(f32[1,64,128]{2,1,0:T(8,128)S(1)} %get-tuple-element.20), channel_id=1, source_target_pairs={{0,16},{4,20},{8,24},{12,28},{16,0},{20,4},{24,8},{28,12},{1,17},{... | collective-permute-start | bytes 98312 | tf_op jit(solution)/shard_map/ppermute | solution.py:315
  75.3 5.8 %collective-permute-start.8 = (f32[1,64,128]{2,1,0:T(8,128)S(1)}, f32[1,64,128]{2,1,0:T(8,128)S(1)}, u32[]{:S(2)}, u32[]{:S(2)}) collective-permute-start(f32[1,64,128]{2,1,0:T(8,128)S(1)} %get-tuple-element.19), channel_id=1, source_target_pairs={{0,24},{4,28},{8,16},{12,20},{16,8},{20,12},{24,0},{28,4},{1,25},{... | collective-permute-start | bytes 98312 | tf_op jit(solution)/shard_map/ppermute | solution.py:315
  78.9 3.9 %collective-permute-start.9 = (f32[1,64,128]{2,1,0:T(8,128)S(1)}, f32[1,64,128]{2,1,0:T(8,128)S(1)}, u32[]{:S(2)}, u32[]{:S(2)}) collective-permute-start(f32[1,64,128]{2,1,0:T(8,128)S(1)} %get-tuple-element.21), channel_id=1, source_target_pairs={{0,8},{4,12},{8,0},{12,4},{16,24},{20,28},{24,16},{28,20},{1,9},{5... | collective-permute-start | bytes 98312 | tf_op jit(solution)/shard_map/ppermute | solution.py:315
  82.9 3.7 %collective-permute-start.11 = (f32[64,128]{1,0:T(8,128)S(1)}, f32[64,128]{1,0:T(8,128)S(1)}, u32[]{:S(2)}, u32[]{:S(2)}) collective-permute-start(f32[64,128]{1,0:T(8,128)S(1)} %fusion.2), channel_id=1, source_target_pairs={{0,3},{1,2},{2,1},{3,0},{4,7},{5,6},{6,5},{7,4},{8,11},{9,10},{10,... | collective-permute-start | bytes 98312 | tf_op jit(solution)/shard_map/ppermute | solution.py:315
  82.9 4.0 %collective-permute-start.12 = (f32[64,128]{1,0:T(8,128)S(1)}, f32[64,128]{1,0:T(8,128)S(1)}, u32[]{:S(2)}, u32[]{:S(2)}) collective-permute-start(f32[64,128]{1,0:T(8,128)S(1)} %fusion.2), channel_id=1, source_target_pairs={{0,2},{1,3},{2,0},{3,1},{4,6},{5,7},{6,4},{7,5},{8,10},{9,11},{10,... | collective-permute-start | bytes 98312 | tf_op jit(solution)/shard_map/ppermute | solution.py:315
  84.5 2.4 %collective-permute-start.13 = (f32[64,128]{1,0:T(8,128)S(1)}, f32[64,128]{1,0:T(8,128)S(1)}, u32[]{:S(2)}, u32[]{:S(2)}) collective-permute-start(f32[64,128]{1,0:T(8,128)S(1)} %fusion.2), channel_id=1, source_target_pairs={{0,1},{1,0},{2,3},{3,2},{4,5},{5,4},{6,7},{7,6},{8,9},{9,8},{10,11... | collective-permute-start | bytes 98312 | tf_op jit(solution)/shard_map/ppermute | solution.py:315

commit v12 on v11

--- a/solution.py
+++ b/solution.py
@@ -14,7 +14,7 @@
 NT = (((1,), (1,)), ((), ()))
 LOG2_SCALE = math.log2(math.e) / math.sqrt(HD)
 LOWEST = -1e30
-NEXT_WAVE = 3000000000
+NEXT_WAVE = 0
 SMALL_VMEM = 24 * 1024 * 1024
 LARGE_VMEM = 60 * 1024 * 1024
 SMEM = pl.BlockSpec(memory_space=pltpu.SMEM)
@@ -60,7 +60,7 @@
         copy.wait()
 
 
-def pack(me, model, qkv, readout_t, k, count, after, wave=False):
+def pack(me, model, qkv, readout_t, k, count, after, wave=False, first=False):
     rows = qkv.shape[1]
     lat = readout_t.shape[1]
     width = count * 2 * HD + -(-count * lat // HD) * HD
@@ -74,7 +74,7 @@
             pltpu.VMEM((lat, count * HD), jnp.bfloat16),
             pltpu.SemaphoreType.DMA((2 * count + 1,)),
         ],
-        compiler_params=pltpu.CompilerParams(vmem_limit_bytes=SMALL_VMEM),
+        compiler_params=pltpu.CompilerParams(vmem_limit_bytes=LARGE_VMEM if first else SMALL_VMEM),
         cost_estimate=pl.CostEstimate(
             flops=NEXT_WAVE if wave else 0, bytes_accessed=rows * width * 4, transcendentals=0
         ),
@@ -331,16 +331,13 @@
     readout_t = jnp.swapaxes(readout, 1, 2)
 
     pieces = [None] * seq_count
-    packed = {}
     for n in range(half):
         k = seq_count - 1 - n
-        after = [pieces[k + 2]] if n > 1 else []
-        packed[k] = pack(me, model, qkv, readout_t, k, count, after, n > 1)
-        pieces[k] = swap(packed[k], "seq", k)
-    for k in range(1, half):
-        after = [pieces[k - 1]] if k > 2 else []
+        pieces[k] = swap(pack(me, model, qkv, readout_t, k, count, [pieces[k + 2]] if n > 1 else [], n > 1, n == 0), "seq", k)
+    for k in range(half - 1, 0, -1):
+        after = [] if k == half - 1 else [pieces[k + 1], pieces[seq_count - 1]] if k > 1 else [pieces[half - 1]]
         pieces[k] = swap(pack(me, model, qkv, readout_t, k, count, after), "seq", k)
-    pieces[0] = pack(me, model, qkv, readout_t, 0, count, [packed[seq_count - 2]])
+    pieces[0] = pack(me, model, qkv, readout_t, 0, count, [pieces[half - 1]])
     late = [half, half + 1]
     early = [k for k in range(seq_count) if k not in late]
     merged = attend_early(

time: 87.8 us -> 87.8 us (level)
  starting transfers between devices: 45.7 us -> 22.4 us
  waiting for transfers between devices: 20.9 us -> 40.2 us
  Pallas kernels: 17 us -> 21.4 us
    ppermute x14, starting transfers between devices: 45.7 us -> 22.4 us  [swap(): return lax.ppermute(array, axis, [(i, i ^ offset) for i in range(size)])]
    ppermute x14, waiting for transfers between devices: 20.9 us -> 40.2 us  [swap(): return lax.ppermute(array, axis, [(i, i ^ offset) for i in range(size)])]
    pallas_call x8, Pallas kernels: 7.89 us -> 11 us  [pack(): pl.pallas_call(functools.partial(pack_kernel, k), in_specs=[SMEM, SMEM] +...]
    unnamed x10 -> x20, local copies, waits for them, and re-layouts: 3.13 us -> 2.69 us
  transfers between devices with their start and end apart: 14 -> 14, of which waited for: 10 -> 10; matrix products, arithmetic and copies ran while one was open for 0% -> 0% of each run, Pallas kernels for 14% -> 16%
where the time goes in v12:
time: 87.8 us; the launch traced here: 87.6 us
  waiting for transfers between devices  40.2 us (46%)
  starting transfers between devices  22.4 us (26%)
  Pallas kernels  21.4 us (24%)
  local copies, waits for them, and re-layouts  2.69 us (3%)
    ppermute x14, waiting for transfers between devices, swap(): return lax.ppermute(array, axis, [(i, i ^ offset) for i in range(size)])  40.2 us
    ppermute x14, starting transfers between devices, swap(): return lax.ppermute(array, axis, [(i, i ^ offset) for i in range(size)])  22.4 us
    pallas_call x8, Pallas kernels, pack(): pl.pallas_call(functools.partial(pack_kernel, k), in_specs=[SMEM, SMEM] +...  11 us
    pallas_call x1, Pallas kernels, attend_early(): pl.pallas_call(functools.partial(early_kernel, offsets), in_specs=[SMEM]...  5.77 us
    pallas_call x1, Pallas kernels, attend_late(): pl.pallas_call(functools.partial(late_kernel, offsets, late), in_specs=[S...  4.63 us
    unnamed x20, local copies, waits for them, and re-layouts  2.69 us
  transfers between devices with their start and end apart: 14, of which 10 were waited for; matrix products, arithmetic and copies ran while one was open for 0% of the time, Pallas kernels for 16%

profile of v12, /device:TPU:0, one launch (start us, length us, event | category | flops | bytes accessed | tf_op | source)
XLA Modules:
  0.0 87.6 jit_solution(15881842695601306784)
XLA Ops:
  0.0 2.4 %pack.10 = bf16[128,1280]{1,0:T(8,128)(2,1)} custom-call(s32[1]{0:T(128)} %bitcast.me_ref, s32[1]{0:T(128)} %bitcast.1.model_ref, bf16[1,128,12288]{2,1,0:T(8,128)(2,1)} %qkv_ref.15, bf16[2,64,4096]{2,1,0:T(8,128)(2,1)} %bitcast.9), custom_call_target="tpu_custom_call" | custom-call | bytes 655360 | tf_op jit(solution)/shard_map/pack/pallas_call | solution.py:67
  2.4 6.0 %collective-permute-start.2 = (bf16[128,1280]{1,0:T(8,128)(2,1)}, bf16[128,1280]{1,0:T(8,128)(2,1)S(1)}, u32[]{:S(2)}, u32[]{:S(2)}) collective-permute-start(bf16[128,1280]{1,0:T(8,128)(2,1)} %pack.10), channel_id=1, source_target_pairs={{0,28},{4,24},{8,20},{12,16},{16,12},{20,8},{24,4},{28,0},{1,29},{... | collective-permute-start | bytes 983048 | tf_op jit(solution)/shard_map/ppermute | solution.py:315
  8.5 0.0 copy-done
  8.5 1.2 %copy-done.1 = bf16[2,4096,64]{1,2,0:T(8,128)(2,1)S(1)} copy-done((bf16[2,4096,64]{1,2,0:T(8,128)(2,1)S(1)}, bf16[2,4096,64]{1,2,0:T(8,128)(2,1)}, u32[]{:S(2)}) %copy-start.1) | copy-done | bytes 1048600
  9.7 0.8 pack.12
  10.5 0.1 collective-permute-start.4
  10.6 0.8 pack.8
  11.4 0.9 %collective-permute-start = (bf16[128,1280]{1,0:T(8,128)(2,1)S(1)}, bf16[128,1280]{1,0:T(8,128)(2,1)S(1)}, u32[]{:S(2)}, u32[]{:S(2)}) collective-permute-start(bf16[128,1280]{1,0:T(8,128)(2,1)S(1)} %pack.8), channel_id=1, source_target_pairs={{0,24},{4,28},{8,16},{12,20},{16,8},{20,12},{24,0},{28,4},{1,25},{... | collective-permute-start | bytes 983048 | tf_op jit(solution)/shard_map/ppermute | solution.py:315
  12.3 4.9 %collective-permute-done.2.refs_0_.refs_1_.refs_5_ = bf16[128,1280]{1,0:T(8,128)(2,1)S(1)} collective-permute-done((bf16[128,1280]{1,0:T(8,128)(2,1)}, bf16[128,1280]{1,0:T(8,128)(2,1)S(1)}, u32[]{:S(2)}, u32[]{:S(2)}) %collective-permute-start.2) | collective-permute-done | bytes 327712 | tf_op jit(solution)/shard_map/ppermute | solution.py:315
  17.3 10.7 %collective-permute-done.4.refs_0_.refs_3_ = bf16[128,1280]{1,0:T(8,128)(2,1)S(1)} collective-permute-done((bf16[128,1280]{1,0:T(8,128)(2,1)S(1)}, bf16[128,1280]{1,0:T(8,128)(2,1)S(1)}, u32[]{:S(2)}, u32[]{:S(2)}) %collective-permute-start.4) | collective-permute-done | bytes 327712 | tf_op jit(solution)/shard_map/ppermute | solution.py:315
  28.0 1.5 %pack.15 = bf16[128,1280]{1,0:T(8,128)(2,1)} custom-call(s32[1]{0:T(128)} %bitcast.me_ref, s32[1]{0:T(128)} %bitcast.1.model_ref, bf16[1,128,12288]{2,1,0:T(8,128)(2,1)S(1)} %copy-done, bf16[2,64,4096]{2,1,0:T(8,128)(2,1)S(1)} %bitcast.12, bf16[128,1280]{1,0:T(8,128)(2,1)S(1)} %collective-permute-done.4.refs_0_.refs_3_, ...), custom_call_target="tpu_custom_call" | custom-call | bytes 655360 | tf_op jit(solution)/shard_map/pack/pallas_call | solution.py:67
  29.5 2.7 %collective-permute-start.6 = (bf16[128,1280]{1,0:T(8,128)(2,1)}, bf16[128,1280]{1,0:T(8,128)(2,1)}, u32[]{:S(2)}, u32[]{:S(2)}) collective-permute-start(bf16[128,1280]{1,0:T(8,128)(2,1)} %pack.15), channel_id=1, source_target_pairs={{0,8},{4,12},{8,0},{12,4},{16,24},{20,28},{24,16},{28,20},{1,9},{5... | collective-permute-start | bytes 983048 | tf_op jit(solution)/shard_map/ppermute | solution.py:315
  32.2 1.5 %pack.14 = bf16[128,1280]{1,0:T(8,128)(2,1)} custom-call(s32[1]{0:T(128)} %bitcast.me_ref, s32[1]{0:T(128)} %bitcast.1.model_ref, bf16[1,128,12288]{2,1,0:T(8,128)(2,1)S(1)} %copy-done, bf16[2,64,4096]{2,1,0:T(8,128)(2,1)S(1)} %bitcast.13, bf16[128,1280]{1,0:T(8,128)(2,1)S(1)} %collective-permute-done.4.refs_0_.refs_3_), custom_call_target="tpu_custom_call" | custom-call | bytes 655360 | tf_op jit(solution)/shard_map/pack/pallas_call | solution.py:67
  33.8 1.4 %collective-permute-start.5 = (bf16[128,1280]{1,0:T(8,128)(2,1)}, bf16[128,1280]{1,0:T(8,128)(2,1)}, u32[]{:S(2)}, u32[]{:S(2)}) collective-permute-start(bf16[128,1280]{1,0:T(8,128)(2,1)} %pack.14), channel_id=1, source_target_pairs={{0,4},{4,0},{8,12},{12,8},{16,20},{20,16},{24,28},{28,24},{1,5},{5... | collective-permute-start | bytes 983048 | tf_op jit(solution)/shard_map/ppermute | solution.py:315
  35.2 1.5 %pack.11 = bf16[128,1280]{1,0:T(8,128)(2,1)} custom-call(s32[1]{0:T(128)} %bitcast.me_ref, s32[1]{0:T(128)} %bitcast.1.model_ref, bf16[1,128,12288]{2,1,0:T(8,128)(2,1)S(1)} %copy-done, bf16[2,64,4096]{2,1,0:T(8,128)(2,1)S(1)} %bitcast.14, bf16[128,1280]{1,0:T(8,128)(2,1)S(1)} %collective-permute-done.2.refs_0_.refs_1_.refs_5_), custom_call_target="tpu_custom_call" | custom-call | bytes 655360 | tf_op jit(solution)/shard_map/pack/pallas_call | solution.py:67
  36.7 0.1 collective-permute-start.3
  36.8 0.0 collective-permute-done.refs_0_.refs_4_
  36.8 0.0 copy-start.5
  36.8 1.6 %pack.9 = bf16[128,1280]{1,0:T(8,128)(2,1)} custom-call(s32[1]{0:T(128)} %bitcast.me_ref, s32[1]{0:T(128)} %bitcast.1.model_ref, bf16[1,128,12288]{2,1,0:T(8,128)(2,1)S(1)} %copy-done, bf16[2,64,4096]{2,1,0:T(8,128)(2,1)S(1)} %bitcast.15, bf16[128,1280]{1,0:T(8,128)(2,1)S(1)} %collective-permute-done.refs_0_.refs_4_), custom_call_target="tpu_custom_call" | custom-call | bytes 655360 | tf_op jit(solution)/shard_map/pack/pallas_call | solution.py:67
  38.4 0.0 copy-start.7
  38.4 0.0 copy-start.8
  38.4 0.0 copy-start.9
  38.4 5.0 %collective-permute-start.1 = (bf16[128,1280]{1,0:T(8,128)(2,1)}, bf16[128,1280]{1,0:T(8,128)(2,1)}, u32[]{:S(2)}, u32[]{:S(2)}) collective-permute-start(bf16[128,1280]{1,0:T(8,128)(2,1)} %pack.9), channel_id=1, source_target_pairs={{0,16},{4,20},{8,24},{12,28},{16,0},{20,4},{24,8},{28,12},{1,17},{... | collective-permute-start | bytes 983048 | tf_op jit(solution)/shard_map/ppermute | solution.py:315
  43.5 1.2 %copy-done.2 = bf16[2,4096,64]{1,2,0:T(8,128)(2,1)S(1)} copy-done((bf16[2,4096,64]{1,2,0:T(8,128)(2,1)S(1)}, bf16[2,4096,64]{1,2,0:T(8,128)(2,1)}, u32[]{:S(2)}) %copy-start.2) | copy-done | bytes 1048600
  44.7 0.8 pack.13.refs_0_
  45.5 0.0 collective-permute-done.6.refs_2_
  45.5 0.0 collective-permute-done.5.refs_1_
  45.6 0.1 copy-done.4
  45.7 0.1 copy-done.6
  45.8 5.8 %attend_early.1 = (f32[3,4,64,256]{3,2,1,0:T(8,128)S(1)}, f32[3,2,8,256]{3,2,1,0:T(8,128)S(1)}, f32[8,128]{1,0:T(8,128)S(1)}, bf16[6,128,1280]{2,1,0:T(8,128)(2,1)S(1)}, bf16[4,80,768]{2,1,0:T(8,128)(2,1)S(1)}) custom-call(s32[4]{0:T(128)S(1)} %copy-done.7, s32[1]{0:T(128)} %bitcast.me_ref, s32[2]{0:T(128)S(1)} %copy-done.9, f32[1000]{0:T(1024)S(1)} %copy-done.8, ...), custom_call_target="tpu_custom_call" | custom-call | flops 905969664 | bytes 2359296 | tf_op jit(solution)/shard_map/attend_early/pallas_call | solution.py:261
  51.6 10.8 %collective-permute-done.3.refs_1_ = bf16[128,1280]{1,0:T(8,128)(2,1)} collective-permute-done((bf16[128,1280]{1,0:T(8,128)(2,1)}, bf16[128,1280]{1,0:T(8,128)(2,1)}, u32[]{:S(2)}, u32[]{:S(2)}) %collective-permute-start.3) | collective-permute-done | bytes 327712 | tf_op jit(solution)/shard_map/ppermute | solution.py:315
  62.4 5.2 %collective-permute-done.1.refs_0_ = bf16[128,1280]{1,0:T(8,128)(2,1)} collective-permute-done((bf16[128,1280]{1,0:T(8,128)(2,1)}, bf16[128,1280]{1,0:T(8,128)(2,1)}, u32[]{:S(2)}, u32[]{:S(2)}) %collective-permute-start.1) | collective-permute-done | bytes 327712 | tf_op jit(solution)/shard_map/ppermute | solution.py:315
  67.6 4.6 %attend_late.1 = (f32[4,64,128]{2,1,0:T(8,128)S(1)}, bf16[4,64,128]{2,1,0:T(8,128)(2,1)S(1)}) custom-call(s32[4]{0:T(128)S(1)} %copy-done.7, s32[1]{0:T(128)} %bitcast.me_ref, bf16[128,1280]{1,0:T(8,128)(2,1)} %collective-permute-done.1.refs_0_, bf16[128,1280]{1,0:T(8,128)(2,1)} %collective-permute-done.3.refs_1_, ...), custom_call_target="tpu_custom_call" | custom-call | flops 402653184 | bytes 3145728 | tf_op jit(solution)/shard_map/attend_late/pallas_call | solution.py:290
  72.3 0.7 collective-permute-start.7
  72.9 3.7 %collective-permute-done.7 = bf16[4,64,128]{2,1,0:T(8,128)(2,1)S(1)} collective-permute-done((bf16[4,64,128]{2,1,0:T(8,128)(2,1)S(1)}, bf16[4,64,128]{2,1,0:T(8,128)(2,1)S(1)}, u32[]{:S(2)}, u32[]{:S(2)}) %collective-permute-start.7) | collective-permute-done | bytes 65568 | tf_op jit(solution)/shard_map/ppermute | solution.py:315
  76.6 0.1 collective-permute-start.10
  76.7 2.2 %collective-permute-start.8 = (f32[1,64,128]{2,1,0:T(8,128)S(1)}, f32[1,64,128]{2,1,0:T(8,128)S(1)}, u32[]{:S(2)}, u32[]{:S(2)}) collective-permute-start(f32[1,64,128]{2,1,0:T(8,128)S(1)} %get-tuple-element.19), channel_id=1, source_target_pairs={{0,24},{4,28},{8,16},{12,20},{16,8},{20,12},{24,0},{28,4},{1,25},{... | collective-permute-start | bytes 98312 | tf_op jit(solution)/shard_map/ppermute | solution.py:315
  78.9 1.2 %collective-permute-start.9 = (f32[1,64,128]{2,1,0:T(8,128)S(1)}, f32[1,64,128]{2,1,0:T(8,128)S(1)}, u32[]{:S(2)}, u32[]{:S(2)}) collective-permute-start(f32[1,64,128]{2,1,0:T(8,128)S(1)} %get-tuple-element.21), channel_id=1, source_target_pairs={{0,8},{4,12},{8,0},{12,4},{16,24},{20,28},{24,16},{28,20},{1,9},{5... | collective-permute-start | bytes 98312 | tf_op jit(solution)/shard_map/ppermute | solution.py:315
  80.2 1.3 %collective-permute-done.10 = f32[1,64,128]{2,1,0:T(8,128)S(1)} collective-permute-done((f32[1,64,128]{2,1,0:T(8,128)S(1)}, f32[1,64,128]{2,1,0:T(8,128)S(1)}, u32[]{:S(2)}, u32[]{:S(2)}) %collective-permute-start.10) | collective-permute-done | bytes 32800 | tf_op jit(solution)/shard_map/ppermute | solution.py:315
  81.5 1.0 %collective-permute-done.8 = f32[1,64,128]{2,1,0:T(8,128)S(1)} collective-permute-done((f32[1,64,128]{2,1,0:T(8,128)S(1)}, f32[1,64,128]{2,1,0:T(8,128)S(1)}, u32[]{:S(2)}, u32[]{:S(2)}) %collective-permute-start.8) | collective-permute-done | bytes 32800 | tf_op jit(solution)/shard_map/ppermute | solution.py:315
  82.5 0.4 collective-permute-done.9
  82.9 0.1 collective-permute-start.11
  82.9 1.6 %collective-permute-start.12 = (f32[64,128]{1,0:T(8,128)S(1)}, f32[64,128]{1,0:T(8,128)S(1)}, u32[]{:S(2)}, u32[]{:S(2)}) collective-permute-start(f32[64,128]{1,0:T(8,128)S(1)} %fusion.2), channel_id=1, source_target_pairs={{0,2},{1,3},{2,0},{3,1},{4,6},{5,7},{6,4},{7,5},{8,10},{9,11},{10,... | collective-permute-start | bytes 98312 | tf_op jit(solution)/shard_map/ppermute | solution.py:315
  84.5 0.3 collective-permute-start.13
  84.8 1.8 %collective-permute-done.11 = f32[64,128]{1,0:T(8,128)S(1)} collective-permute-done((f32[64,128]{1,0:T(8,128)S(1)}, f32[64,128]{1,0:T(8,128)S(1)}, u32[]{:S(2)}, u32[]{:S(2)}) %collective-permute-start.11) | collective-permute-done | bytes 32800 | tf_op jit(solution)/shard_map/ppermute | solution.py:315
  86.5 0.4 collective-permute-done.12
  87.0 0.0 collective-permute-done.13
  87.0 0.6 add_bitcast_fusion
  (14 shorter events, 0.1 us)
Async XLA Ops:
  0.0 8.5 %copy-start = (bf16[1,128,12288]{2,1,0:T(8,128)(2,1)S(1)}, bf16[1,128,12288]{2,1,0:T(8,128)(2,1)}, u32[]{:S(2)}) copy-start(bf16[1,128,12288]{2,1,0:T(8,128)(2,1)} %qkv_ref.15) | copy-start | bytes 9437188
  2.4 14.8 %collective-permute-start.2 = (bf16[128,1280]{1,0:T(8,128)(2,1)}, bf16[128,1280]{1,0:T(8,128)(2,1)S(1)}, u32[]{:S(2)}, u32[]{:S(2)}) collective-permute-start(bf16[128,1280]{1,0:T(8,128)(2,1)} %pack.10), channel_id=1, source_target_pairs={{0,28},{4,24},{8,20},{12,16},{16,12},{20,8},{24,4},{28,0},{1,29},{... | collective-permute-start | bytes 983048 | tf_op jit(solution)/shard_map/ppermute | solution.py:315
  8.5 1.2 %copy-start.1 = (bf16[2,4096,64]{1,2,0:T(8,128)(2,1)S(1)}, bf16[2,4096,64]{1,2,0:T(8,128)(2,1)}, u32[]{:S(2)}) copy-start(bf16[2,4096,64]{1,2,0:T(8,128)(2,1)} %param.6) | copy-start | bytes 3145732
  10.5 17.5 %collective-permute-start.4 = (bf16[128,1280]{1,0:T(8,128)(2,1)S(1)}, bf16[128,1280]{1,0:T(8,128)(2,1)S(1)}, u32[]{:S(2)}, u32[]{:S(2)}) collective-permute-start(bf16[128,1280]{1,0:T(8,128)(2,1)S(1)} %pack.12), channel_id=1, source_target_pairs={{0,12},{4,8},{8,4},{12,0},{16,28},{20,24},{24,20},{28,16},{1,13},{... | collective-permute-start | bytes 983048 | tf_op jit(solution)/shard_map/ppermute | solution.py:315
  11.4 25.4 %collective-permute-start = (bf16[128,1280]{1,0:T(8,128)(2,1)S(1)}, bf16[128,1280]{1,0:T(8,128)(2,1)S(1)}, u32[]{:S(2)}, u32[]{:S(2)}) collective-permute-start(bf16[128,1280]{1,0:T(8,128)(2,1)S(1)} %pack.8), channel_id=1, source_target_pairs={{0,24},{4,28},{8,16},{12,20},{16,8},{20,12},{24,0},{28,4},{1,25},{... | collective-permute-start | bytes 983048 | tf_op jit(solution)/shard_map/ppermute | solution.py:315
  17.3 17.9 %copy-start.3 = (bf16[128,1280]{1,0:T(8,128)(2,1)}, bf16[128,1280]{1,0:T(8,128)(2,1)S(1)}, u32[]{:S(2)}) copy-start(bf16[128,1280]{1,0:T(8,128)(2,1)S(1)} %collective-permute-done.2.refs_0_.refs_1_.refs_5_) | copy-start | bytes 983044
  29.5 16.0 %collective-permute-start.6 = (bf16[128,1280]{1,0:T(8,128)(2,1)}, bf16[128,1280]{1,0:T(8,128)(2,1)}, u32[]{:S(2)}, u32[]{:S(2)}) collective-permute-start(bf16[128,1280]{1,0:T(8,128)(2,1)} %pack.15), channel_id=1, source_target_pairs={{0,8},{4,12},{8,0},{12,4},{16,24},{20,28},{24,16},{28,20},{1,9},{5... | collective-permute-start | bytes 983048 | tf_op jit(solution)/shard_map/ppermute | solution.py:315
  33.8 11.8 %collective-permute-start.5 = (bf16[128,1280]{1,0:T(8,128)(2,1)}, bf16[128,1280]{1,0:T(8,128)(2,1)}, u32[]{:S(2)}, u32[]{:S(2)}) collective-permute-start(bf16[128,1280]{1,0:T(8,128)(2,1)} %pack.14), channel_id=1, source_target_pairs={{0,4},{4,0},{8,12},{12,8},{16,20},{20,16},{24,28},{28,24},{1,5},{5... | collective-permute-start | bytes 983048 | tf_op jit(solution)/shard_map/ppermute | solution.py:315
  36.7 25.7 %collective-permute-start.3 = (bf16[128,1280]{1,0:T(8,128)(2,1)}, bf16[128,1280]{1,0:T(8,128)(2,1)}, u32[]{:S(2)}, u32[]{:S(2)}) collective-permute-start(bf16[128,1280]{1,0:T(8,128)(2,1)} %pack.11), channel_id=1, source_target_pairs={{0,20},{4,16},{8,28},{12,24},{16,4},{20,0},{24,12},{28,8},{1,21},{... | collective-permute-start | bytes 983048 | tf_op jit(solution)/shard_map/ppermute | solution.py:315
  36.8 1.6 %copy-start.5 = (bf16[128,1280]{1,0:T(8,128)(2,1)}, bf16[128,1280]{1,0:T(8,128)(2,1)S(1)}, u32[]{:S(2)}) copy-start(bf16[128,1280]{1,0:T(8,128)(2,1)S(1)} %collective-permute-done.refs_0_.refs_4_) | copy-start | bytes 983044
  38.4 7.2 %copy-start.7 = (s32[4]{0:T(128)S(1)}, s32[4]{0:T(128)}, u32[]{:S(2)}) copy-start(s32[4]{0:T(128)} %frames_ref.3) | copy-start | bytes 52
  38.4 7.1 %copy-start.8 = (f32[1000]{0:T(1024)S(1)}, f32[1000]{0:T(1024)}, u32[]{:S(2)}) copy-start(f32[1000]{0:T(1024)} %step_weight_ref.1) | copy-start | bytes 12004
  38.4 7.1 %copy-start.9 = (s32[2]{0:T(128)S(1)}, s32[2]{0:T(128)}, u32[]{:S(2)}) copy-start(s32[2]{0:T(128)} %timestep_ref.1) | copy-start | bytes 28
  38.4 29.2 %collective-permute-start.1 = (bf16[128,1280]{1,0:T(8,128)(2,1)}, bf16[128,1280]{1,0:T(8,128)(2,1)}, u32[]{:S(2)}, u32[]{:S(2)}) collective-permute-start(bf16[128,1280]{1,0:T(8,128)(2,1)} %pack.9), channel_id=1, source_target_pairs={{0,16},{4,20},{8,24},{12,28},{16,0},{20,4},{24,8},{28,12},{1,17},{... | collective-permute-start | bytes 983048 | tf_op jit(solution)/shard_map/ppermute | solution.py:315
  43.5 1.2 %copy-start.2 = (bf16[2,4096,64]{1,2,0:T(8,128)(2,1)S(1)}, bf16[2,4096,64]{1,2,0:T(8,128)(2,1)}, u32[]{:S(2)}) copy-start(bf16[2,4096,64]{1,2,0:T(8,128)(2,1)} %param.6) | copy-start | bytes 3145732
  44.7 1.0 %copy-start.4 = (bf16[128,1280]{1,0:T(8,128)(2,1)S(1)}, bf16[128,1280]{1,0:T(8,128)(2,1)}, u32[]{:S(2)}) copy-start(bf16[128,1280]{1,0:T(8,128)(2,1)} %copy-done.3) | copy-start | bytes 983044
  44.7 1.1 %copy-start.6 = (bf16[128,1280]{1,0:T(8,128)(2,1)S(1)}, bf16[128,1280]{1,0:T(8,128)(2,1)}, u32[]{:S(2)}) copy-start(bf16[128,1280]{1,0:T(8,128)(2,1)} %copy-done.5) | copy-start | bytes 983044
  72.3 4.3 %collective-permute-start.7 = (bf16[4,64,128]{2,1,0:T(8,128)(2,1)S(1)}, bf16[4,64,128]{2,1,0:T(8,128)(2,1)S(1)}, u32[]{:S(2)}, u32[]{:S(2)}) collective-permute-start(bf16[4,64,128]{2,1,0:T(8,128)(2,1)S(1)} %get-tuple-element.18), channel_id=1, source_target_pairs={{0,4},{4,0},{8,12},{12,8},{16,20},{20,16},{24,28},{28,24},{1,5},{5... | collective-permute-start | bytes 196616 | tf_op jit(solution)/shard_map/ppermute | solution.py:315
  76.6 4.9 %collective-permute-start.10 = (f32[1,64,128]{2,1,0:T(8,128)S(1)}, f32[1,64,128]{2,1,0:T(8,128)S(1)}, u32[]{:S(2)}, u32[]{:S(2)}) collective-permute-start(f32[1,64,128]{2,1,0:T(8,128)S(1)} %get-tuple-element.20), channel_id=1, source_target_pairs={{0,16},{4,20},{8,24},{12,28},{16,0},{20,4},{24,8},{28,12},{1,17},{... | collective-permute-start | bytes 98312 | tf_op jit(solution)/shard_map/ppermute | solution.py:315
  76.7 5.8 %collective-permute-start.8 = (f32[1,64,128]{2,1,0:T(8,128)S(1)}, f32[1,64,128]{2,1,0:T(8,128)S(1)}, u32[]{:S(2)}, u32[]{:S(2)}) collective-permute-start(f32[1,64,128]{2,1,0:T(8,128)S(1)} %get-tuple-element.19), channel_id=1, source_target_pairs={{0,24},{4,28},{8,16},{12,20},{16,8},{20,12},{24,0},{28,4},{1,25},{... | collective-permute-start | bytes 98312 | tf_op jit(solution)/shard_map/ppermute | solution.py:315
  78.9 3.9 %collective-permute-start.9 = (f32[1,64,128]{2,1,0:T(8,128)S(1)}, f32[1,64,128]{2,1,0:T(8,128)S(1)}, u32[]{:S(2)}, u32[]{:S(2)}) collective-permute-start(f32[1,64,128]{2,1,0:T(8,128)S(1)} %get-tuple-element.21), channel_id=1, source_target_pairs={{0,8},{4,12},{8,0},{12,4},{16,24},{20,28},{24,16},{28,20},{1,9},{5... | collective-permute-start | bytes 98312 | tf_op jit(solution)/shard_map/ppermute | solution.py:315
  82.9 3.7 %collective-permute-start.11 = (f32[64,128]{1,0:T(8,128)S(1)}, f32[64,128]{1,0:T(8,128)S(1)}, u32[]{:S(2)}, u32[]{:S(2)}) collective-permute-start(f32[64,128]{1,0:T(8,128)S(1)} %fusion.2), channel_id=1, source_target_pairs={{0,3},{1,2},{2,1},{3,0},{4,7},{5,6},{6,5},{7,4},{8,11},{9,10},{10,... | collective-permute-start | bytes 98312 | tf_op jit(solution)/shard_map/ppermute | solution.py:315
  82.9 4.0 %collective-permute-start.12 = (f32[64,128]{1,0:T(8,128)S(1)}, f32[64,128]{1,0:T(8,128)S(1)}, u32[]{:S(2)}, u32[]{:S(2)}) collective-permute-start(f32[64,128]{1,0:T(8,128)S(1)} %fusion.2), channel_id=1, source_target_pairs={{0,2},{1,3},{2,0},{3,1},{4,6},{5,7},{6,4},{7,5},{8,10},{9,11},{10,... | collective-permute-start | bytes 98312 | tf_op jit(solution)/shard_map/ppermute | solution.py:315
  84.5 2.4 %collective-permute-start.13 = (f32[64,128]{1,0:T(8,128)S(1)}, f32[64,128]{1,0:T(8,128)S(1)}, u32[]{:S(2)}, u32[]{:S(2)}) collective-permute-start(f32[64,128]{1,0:T(8,128)S(1)} %fusion.2), channel_id=1, source_target_pairs={{0,1},{1,0},{2,3},{3,2},{4,5},{5,4},{6,7},{7,6},{8,9},{9,8},{10,11... | collective-permute-start | bytes 98312 | tf_op jit(solution)/shard_map/ppermute | solution.py:315

commit v13 on v12

--- a/solution.py
+++ b/solution.py
@@ -190,16 +190,15 @@
     lax.fori_loop(0, blocks, some_blocks, 0)
 
 
-def late_kernel(offsets, late, frames_ref, me_ref, *refs):
+def late_kernel(offsets, late, chosen, groups, frames_ref, me_ref, *refs):
     early = len(offsets)
     arrived = refs[:2]
-    sums_ref, stats_ref, factor_ref, early_ref, early_folded, keep_ref, give_ref, late_pieces, folded, sems = refs[2:]
+    sums_ref, stats_ref, factor_ref, early_ref, early_folded, *out_refs, late_pieces, folded, sems = refs[2:]
     copies = [pltpu.make_async_copy(arrived[n], late_pieces.at[n], sems.at[n]) for n in range(2)]
     for copy in copies:
         copy.start()
     me = me_ref[0]
-    half, lat, rows = keep_ref.shape
-    bits = half.bit_length()
+    size, lat, rows = out_refs[0].shape
     count = folded.shape[0]
     for copy in copies:
         copy.wait()
@@ -215,16 +214,12 @@
     def write(b):
         for j in range(2):
             k = every[2 * b + j]
-            n = sum(((k >> bit) & 1) << (bits - 1 - bit) for bit in range(bits))
-            part = results[b][:, j * rows : (j + 1) * rows] * factor
-            if n < half:
-                keep_ref[n] = part
-            else:
-                give_ref[n - half] = part.astype(jnp.bfloat16)
+            out_ref = out_refs[groups.index(k // size)]
+            out_ref[k % size] = (results[b][:, j * rows : (j + 1) * rows] * factor).astype(out_ref.dtype)
 
     units = []
     blocks = early // 2
-    for b in [blocks] + list(range(blocks)):
+    for b in chosen:
         keys_in = range(blocks + 1) if b == blocks else [blocks]
         key_offsets = [every[2 * t + j] for t in keys_in for j in range(2)]
         shifts = mask_rows(frames_ref, me, rows, every[2 * b : 2 * b + 2], key_offsets)
@@ -283,17 +278,16 @@
     )(span_frames, me, timestep, step_weight, sign, sample, *pieces)
 
 
-def attend_late(pieces, offsets, late, early, span_frames, me, count, lat):
+def attend_late(pieces, offsets, late, chosen, groups, early, span_frames, me, count, lat):
     rows, width = pieces[0].shape
     half = len(offsets) // 2 + 1
     tokens = 2 * half * rows
     return pl.pallas_call(
-        functools.partial(late_kernel, offsets, late),
+        functools.partial(late_kernel, offsets, late, chosen, groups),
         in_specs=[SMEM] * 2 + [HBM] * 2 + [VMEM] * len(early),
-        out_specs=[VMEM, VMEM],
+        out_specs=[VMEM] * len(groups),
         out_shape=[
-            jax.ShapeDtypeStruct((half, lat, rows), jnp.float32),
-            jax.ShapeDtypeStruct((half, lat, rows), jnp.bfloat16),
+            jax.ShapeDtypeStruct((half // 2, lat, rows), jnp.bfloat16 if g else jnp.float32) for g in groups
         ],
         scratch_shapes=[
             pltpu.VMEM((2, rows, width), jnp.bfloat16),
@@ -302,9 +296,9 @@
         ],
         compiler_params=pltpu.CompilerParams(vmem_limit_bytes=SMALL_VMEM if half <= 4 else LARGE_VMEM),
         cost_estimate=pl.CostEstimate(
-            flops=count * tokens * rows * 4 * (HD + lat),
+            flops=count * tokens * rows * 2 * (HD + lat),
             bytes_accessed=tokens * count * 3 * HD * 2,
-            transcendentals=count * tokens * rows * 2,
+            transcendentals=count * tokens * rows,
         ),
         name="attend_late",
     )(span_frames, me, *pieces, *early)
@@ -343,19 +337,22 @@
     merged = attend_early(
         [pieces[k] for k in early], early, span_frames, me, timestep, step_weight, sign, sample, count, lat
     )
-    keep, give = attend_late([pieces[k] for k in late], early, late, merged, span_frames, me, count, lat)
-
-    keep = keep + swap(give, "seq", 1).astype(jnp.float32)
-    offset = 2
-    while offset < seq_count:
-        radix = min(4, seq_count // offset)
-        size = keep.shape[0] // radix
-        parts = [keep[n * size : (n + 1) * size] for n in range(radix)]
-        keep = parts[0]
-        for n in range(radix - 1, 0, -1):
-            bits_n = (n >> 1) | ((n & 1) << 1) if radix == 4 else n
-            keep = keep + swap(parts[n], "seq", offset * bits_n)
-        offset *= radix
+    blocks = len(early) // 2
+    far_blocks = [blocks] + list(range(half // 2, blocks))
+    ends = [pieces[k] for k in late]
+    given = attend_late(ends, early, late, far_blocks, [2, 3], merged, span_frames, me, count, lat)
+    near_blocks = list(range(half // 2 - 1, -1, -1))
+    given = attend_late(ends, early, late, near_blocks, [0, 1], merged, span_frames, me, count, lat) + given
+    size = half // 2
+    while True:
+        keep = given[0]
+        for n in range(len(given) - 1, 0, -1):
+            keep = keep + swap(given[n], "seq", n * size).astype(jnp.float32)
+        if size == 1:
+            break
+        radix = min(4, size)
+        size //= radix
+        given = [keep[n * size : (n + 1) * size] for n in range(radix)]
     total = keep[0]
     offset = 1
     while offset < mp_count:

time: 87.8 us -> 89.5 us (1.019)
  Pallas kernels: 21.4 us -> 23.3 us
  waiting for transfers between devices: 40.2 us -> 39.1 us
  starting transfers between devices: 22.4 us -> 23.3 us
    pallas_call x1 -> x2, Pallas kernels: 4.63 us -> 6.46 us  [attend_late(): pl.pallas_call(functools.partial(late_kernel, offsets, late, chosen, grou...]
    ppermute x14, waiting for transfers between devices: 40.2 us -> 39.1 us  [swap(): return lax.ppermute(array, axis, [(i, i ^ offset) for i in range(size)])]
    ppermute x14, starting transfers between devices: 22.4 us -> 23.3 us  [swap(): return lax.ppermute(array, axis, [(i, i ^ offset) for i in range(size)])]
  transfers between devices with their start and end apart: 14 -> 14, of which waited for: 10 -> 8; matrix products, arithmetic and copies ran while one was open for 0% -> 0% of each run, Pallas kernels for 16% -> 19%
where the time goes in v13:
time: 89.5 us; the launch traced here: 89.2 us
  waiting for transfers between devices  39.1 us (44%)
  Pallas kernels  23.3 us (26%)
  starting transfers between devices  23.3 us (26%)
  local copies, waits for them, and re-layouts  2.69 us (3%)
    ppermute x14, waiting for transfers between devices, swap(): return lax.ppermute(array, axis, [(i, i ^ offset) for i in range(size)])  39.1 us
    ppermute x14, starting transfers between devices, swap(): return lax.ppermute(array, axis, [(i, i ^ offset) for i in range(size)])  23.3 us
    pallas_call x8, Pallas kernels, pack(): pl.pallas_call(functools.partial(pack_kernel, k), in_specs=[SMEM, SMEM] +...  11 us
    pallas_call x2, Pallas kernels, attend_late(): pl.pallas_call(functools.partial(late_kernel, offsets, late, chosen, grou...  6.46 us
    pallas_call x1, Pallas kernels, attend_early(): pl.pallas_call(functools.partial(early_kernel, offsets), in_specs=[SMEM]...  5.77 us
    unnamed x20, local copies, waits for them, and re-layouts  2.69 us
  transfers between devices with their start and end apart: 14, of which 8 were waited for; matrix products, arithmetic and copies ran while one was open for 0% of the time, Pallas kernels for 19%

profile of v13, /device:TPU:0, one launch (start us, length us, event | category | flops | bytes accessed | tf_op | source)
XLA Modules:
  0.0 89.2 jit_solution(2295605085205923508)
XLA Ops:
  0.0 2.4 %pack.10 = bf16[128,1280]{1,0:T(8,128)(2,1)} custom-call(s32[1]{0:T(128)} %bitcast.me_ref, s32[1]{0:T(128)} %bitcast.1.model_ref, bf16[1,128,12288]{2,1,0:T(8,128)(2,1)} %qkv_ref.15, bf16[2,64,4096]{2,1,0:T(8,128)(2,1)} %bitcast.9), custom_call_target="tpu_custom_call" | custom-call | bytes 655360 | tf_op jit(solution)/shard_map/pack/pallas_call | solution.py:67
  2.4 6.0 %collective-permute-start.2 = (bf16[128,1280]{1,0:T(8,128)(2,1)}, bf16[128,1280]{1,0:T(8,128)(2,1)S(1)}, u32[]{:S(2)}, u32[]{:S(2)}) collective-permute-start(bf16[128,1280]{1,0:T(8,128)(2,1)} %pack.10), channel_id=1, source_target_pairs={{0,28},{4,24},{8,20},{12,16},{16,12},{20,8},{24,4},{28,0},{1,29},{... | collective-permute-start | bytes 983048 | tf_op jit(solution)/shard_map/ppermute | solution.py:309
  8.5 1.2 %copy-done.1 = bf16[2,4096,64]{1,2,0:T(8,128)(2,1)S(1)} copy-done((bf16[2,4096,64]{1,2,0:T(8,128)(2,1)S(1)}, bf16[2,4096,64]{1,2,0:T(8,128)(2,1)}, u32[]{:S(2)}) %copy-start.1) | copy-done | bytes 1048600
  9.7 0.8 pack.12
  10.5 0.1 collective-permute-start.4
  10.6 0.8 pack.8
  11.4 0.9 %collective-permute-start = (bf16[128,1280]{1,0:T(8,128)(2,1)S(1)}, bf16[128,1280]{1,0:T(8,128)(2,1)S(1)}, u32[]{:S(2)}, u32[]{:S(2)}) collective-permute-start(bf16[128,1280]{1,0:T(8,128)(2,1)S(1)} %pack.8), channel_id=1, source_target_pairs={{0,24},{4,28},{8,16},{12,20},{16,8},{20,12},{24,0},{28,4},{1,25},{... | collective-permute-start | bytes 983048 | tf_op jit(solution)/shard_map/ppermute | solution.py:309
  12.3 4.9 %collective-permute-done.2.refs_0_.refs_1_.refs_5_ = bf16[128,1280]{1,0:T(8,128)(2,1)S(1)} collective-permute-done((bf16[128,1280]{1,0:T(8,128)(2,1)}, bf16[128,1280]{1,0:T(8,128)(2,1)S(1)}, u32[]{:S(2)}, u32[]{:S(2)}) %collective-permute-start.2) | collective-permute-done | bytes 327712 | tf_op jit(solution)/shard_map/ppermute | solution.py:309
  17.3 10.7 %collective-permute-done.4.refs_0_.refs_3_ = bf16[128,1280]{1,0:T(8,128)(2,1)S(1)} collective-permute-done((bf16[128,1280]{1,0:T(8,128)(2,1)S(1)}, bf16[128,1280]{1,0:T(8,128)(2,1)S(1)}, u32[]{:S(2)}, u32[]{:S(2)}) %collective-permute-start.4) | collective-permute-done | bytes 327712 | tf_op jit(solution)/shard_map/ppermute | solution.py:309
  28.0 1.5 %pack.15 = bf16[128,1280]{1,0:T(8,128)(2,1)} custom-call(s32[1]{0:T(128)} %bitcast.me_ref, s32[1]{0:T(128)} %bitcast.1.model_ref, bf16[1,128,12288]{2,1,0:T(8,128)(2,1)S(1)} %copy-done, bf16[2,64,4096]{2,1,0:T(8,128)(2,1)S(1)} %bitcast.12, bf16[128,1280]{1,0:T(8,128)(2,1)S(1)} %collective-permute-done.4.refs_0_.refs_3_, ...), custom_call_target="tpu_custom_call" | custom-call | bytes 655360 | tf_op jit(solution)/shard_map/pack/pallas_call | solution.py:67
  29.5 2.7 %collective-permute-start.6 = (bf16[128,1280]{1,0:T(8,128)(2,1)}, bf16[128,1280]{1,0:T(8,128)(2,1)}, u32[]{:S(2)}, u32[]{:S(2)}) collective-permute-start(bf16[128,1280]{1,0:T(8,128)(2,1)} %pack.15), channel_id=1, source_target_pairs={{0,8},{4,12},{8,0},{12,4},{16,24},{20,28},{24,16},{28,20},{1,9},{5... | collective-permute-start | bytes 983048 | tf_op jit(solution)/shard_map/ppermute | solution.py:309
  32.2 1.5 %pack.14 = bf16[128,1280]{1,0:T(8,128)(2,1)} custom-call(s32[1]{0:T(128)} %bitcast.me_ref, s32[1]{0:T(128)} %bitcast.1.model_ref, bf16[1,128,12288]{2,1,0:T(8,128)(2,1)S(1)} %copy-done, bf16[2,64,4096]{2,1,0:T(8,128)(2,1)S(1)} %bitcast.13, bf16[128,1280]{1,0:T(8,128)(2,1)S(1)} %collective-permute-done.4.refs_0_.refs_3_), custom_call_target="tpu_custom_call" | custom-call | bytes 655360 | tf_op jit(solution)/shard_map/pack/pallas_call | solution.py:67
  33.8 1.4 %collective-permute-start.5 = (bf16[128,1280]{1,0:T(8,128)(2,1)}, bf16[128,1280]{1,0:T(8,128)(2,1)}, u32[]{:S(2)}, u32[]{:S(2)}) collective-permute-start(bf16[128,1280]{1,0:T(8,128)(2,1)} %pack.14), channel_id=1, source_target_pairs={{0,4},{4,0},{8,12},{12,8},{16,20},{20,16},{24,28},{28,24},{1,5},{5... | collective-permute-start | bytes 983048 | tf_op jit(solution)/shard_map/ppermute | solution.py:309
  35.2 0.0 copy-done.3
  35.2 1.5 %pack.11 = bf16[128,1280]{1,0:T(8,128)(2,1)} custom-call(s32[1]{0:T(128)} %bitcast.me_ref, s32[1]{0:T(128)} %bitcast.1.model_ref, bf16[1,128,12288]{2,1,0:T(8,128)(2,1)S(1)} %copy-done, bf16[2,64,4096]{2,1,0:T(8,128)(2,1)S(1)} %bitcast.14, bf16[128,1280]{1,0:T(8,128)(2,1)S(1)} %collective-permute-done.2.refs_0_.refs_1_.refs_5_), custom_call_target="tpu_custom_call" | custom-call | bytes 655360 | tf_op jit(solution)/shard_map/pack/pallas_call | solution.py:67
  36.7 0.1 collective-permute-start.3
  36.8 0.0 collective-permute-done.refs_0_.refs_4_
  36.8 1.6 %pack.9 = bf16[128,1280]{1,0:T(8,128)(2,1)} custom-call(s32[1]{0:T(128)} %bitcast.me_ref, s32[1]{0:T(128)} %bitcast.1.model_ref, bf16[1,128,12288]{2,1,0:T(8,128)(2,1)S(1)} %copy-done, bf16[2,64,4096]{2,1,0:T(8,128)(2,1)S(1)} %bitcast.15, bf16[128,1280]{1,0:T(8,128)(2,1)S(1)} %collective-permute-done.refs_0_.refs_4_), custom_call_target="tpu_custom_call" | custom-call | bytes 655360 | tf_op jit(solution)/shard_map/pack/pallas_call | solution.py:67
  38.4 0.0 copy-start.7
  38.4 0.0 copy-start.8
  38.4 0.0 copy-start.9
  38.4 5.0 %collective-permute-start.1 = (bf16[128,1280]{1,0:T(8,128)(2,1)}, bf16[128,1280]{1,0:T(8,128)(2,1)}, u32[]{:S(2)}, u32[]{:S(2)}) collective-permute-start(bf16[128,1280]{1,0:T(8,128)(2,1)} %pack.9), channel_id=1, source_target_pairs={{0,16},{4,20},{8,24},{12,28},{16,0},{20,4},{24,8},{28,12},{1,17},{... | collective-permute-start | bytes 983048 | tf_op jit(solution)/shard_map/ppermute | solution.py:309
  43.5 1.2 %copy-done.2 = bf16[2,4096,64]{1,2,0:T(8,128)(2,1)S(1)} copy-done((bf16[2,4096,64]{1,2,0:T(8,128)(2,1)S(1)}, bf16[2,4096,64]{1,2,0:T(8,128)(2,1)}, u32[]{:S(2)}) %copy-start.2) | copy-done | bytes 1048600
  44.7 0.8 pack.13.refs_0_
  45.5 0.0 collective-permute-done.6.refs_2_
  45.5 0.0 collective-permute-done.5.refs_1_
  45.6 0.1 copy-done.4
  45.7 0.1 copy-done.6
  45.8 5.8 %attend_early.1 = (f32[3,4,64,256]{3,2,1,0:T(8,128)S(1)}, f32[3,2,8,256]{3,2,1,0:T(8,128)S(1)}, f32[8,128]{1,0:T(8,128)S(1)}, bf16[6,128,1280]{2,1,0:T(8,128)(2,1)S(1)}, bf16[4,80,768]{2,1,0:T(8,128)(2,1)S(1)}) custom-call(s32[4]{0:T(128)S(1)} %copy-done.7, s32[1]{0:T(128)} %bitcast.me_ref, s32[2]{0:T(128)S(1)} %copy-done.9, f32[1000]{0:T(1024)S(1)} %copy-done.8, ...), custom_call_target="tpu_custom_call" | custom-call | flops 905969664 | bytes 2359296 | tf_op jit(solution)/shard_map/attend_early/pallas_call | solution.py:256
  51.6 10.8 %collective-permute-done.3.refs_1_ = bf16[128,1280]{1,0:T(8,128)(2,1)} collective-permute-done((bf16[128,1280]{1,0:T(8,128)(2,1)}, bf16[128,1280]{1,0:T(8,128)(2,1)}, u32[]{:S(2)}, u32[]{:S(2)}) %collective-permute-start.3) | collective-permute-done | bytes 327712 | tf_op jit(solution)/shard_map/ppermute | solution.py:309
  62.4 5.2 %collective-permute-done.1.refs_0_ = bf16[128,1280]{1,0:T(8,128)(2,1)} collective-permute-done((bf16[128,1280]{1,0:T(8,128)(2,1)}, bf16[128,1280]{1,0:T(8,128)(2,1)}, u32[]{:S(2)}, u32[]{:S(2)}) %collective-permute-start.1) | collective-permute-done | bytes 327712 | tf_op jit(solution)/shard_map/ppermute | solution.py:309
  67.6 3.5 %attend_late.3 = (bf16[2,64,128]{2,1,0:T(8,128)(2,1)S(1)}, bf16[2,64,128]{2,1,0:T(8,128)(2,1)S(1)}) custom-call(s32[4]{0:T(128)S(1)} %copy-done.7, s32[1]{0:T(128)} %bitcast.me_ref, bf16[128,1280]{1,0:T(8,128)(2,1)} %collective-permute-done.1.refs_0_, bf16[128,1280]{1,0:T(8,128)(2,1)} %collective-permute-done.3.refs_1_, ...), custom_call_target="tpu_custom_call" | custom-call | flops 201326592 | bytes 3145728 | tf_op jit(solution)/shard_map/attend_late/pallas_call | solution.py:285
  71.1 2.2 %collective-permute-start.7 = (bf16[2,64,128]{2,1,0:T(8,128)(2,1)S(1)}, bf16[2,64,128]{2,1,0:T(8,128)(2,1)S(1)}, u32[]{:S(2)}, u32[]{:S(2)}) collective-permute-start(bf16[2,64,128]{2,1,0:T(8,128)(2,1)S(1)} %get-tuple-element.20), channel_id=1, source_target_pairs={{0,24},{4,28},{8,16},{12,20},{16,8},{20,12},{24,0},{28,4},{1,25},{... | collective-permute-start | bytes 98312 | tf_op jit(solution)/shard_map/ppermute | solution.py:309
  73.3 0.0 collective-permute-start.8
  73.3 3.0 %attend_late.2 = (f32[2,64,128]{2,1,0:T(8,128)S(1)}, bf16[2,64,128]{2,1,0:T(8,128)(2,1)S(1)}) custom-call(s32[4]{0:T(128)S(1)} %copy-done.7, s32[1]{0:T(128)} %bitcast.me_ref, bf16[128,1280]{1,0:T(8,128)(2,1)} %collective-permute-done.1.refs_0_, bf16[128,1280]{1,0:T(8,128)(2,1)} %collective-permute-done.3.refs_1_, ...), custom_call_target="tpu_custom_call" | custom-call | flops 201326592 | bytes 3145728 | tf_op jit(solution)/shard_map/attend_late/pallas_call | solution.py:285
  76.3 2.3 %collective-permute-start.9 = (bf16[2,64,128]{2,1,0:T(8,128)(2,1)S(1)}, bf16[2,64,128]{2,1,0:T(8,128)(2,1)S(1)}, u32[]{:S(2)}, u32[]{:S(2)}) collective-permute-start(bf16[2,64,128]{2,1,0:T(8,128)(2,1)S(1)} %get-tuple-element.22), channel_id=1, source_target_pairs={{0,8},{4,12},{8,0},{12,4},{16,24},{20,28},{24,16},{28,20},{1,9},{5... | collective-permute-start | bytes 98312 | tf_op jit(solution)/shard_map/ppermute | solution.py:309
  78.6 0.0 collective-permute-done.7
  78.6 0.0 collective-permute-done.8
  78.6 1.9 %collective-permute-done.9 = bf16[2,64,128]{2,1,0:T(8,128)(2,1)S(1)} collective-permute-done((bf16[2,64,128]{2,1,0:T(8,128)(2,1)S(1)}, bf16[2,64,128]{2,1,0:T(8,128)(2,1)S(1)}, u32[]{:S(2)}, u32[]{:S(2)}) %collective-permute-start.9) | collective-permute-done | bytes 32800 | tf_op jit(solution)/shard_map/ppermute | solution.py:309
  80.5 0.7 collective-permute-start.10
  81.2 3.3 %collective-permute-done.10 = f32[1,64,128]{2,1,0:T(8,128)S(1)} collective-permute-done((f32[1,64,128]{2,1,0:T(8,128)S(1)}, f32[1,64,128]{2,1,0:T(8,128)S(1)}, u32[]{:S(2)}, u32[]{:S(2)}) %collective-permute-start.10) | collective-permute-done | bytes 32800 | tf_op jit(solution)/shard_map/ppermute | solution.py:309
  84.5 0.0 collective-permute-start.11
  84.5 1.6 %collective-permute-start.12 = (f32[64,128]{1,0:T(8,128)S(1)}, f32[64,128]{1,0:T(8,128)S(1)}, u32[]{:S(2)}, u32[]{:S(2)}) collective-permute-start(f32[64,128]{1,0:T(8,128)S(1)} %fusion), channel_id=1, source_target_pairs={{0,2},{1,3},{2,0},{3,1},{4,6},{5,7},{6,4},{7,5},{8,10},{9,11},{10,... | collective-permute-start | bytes 98312 | tf_op jit(solution)/shard_map/ppermute | solution.py:309
  86.1 0.2 collective-permute-start.13
  86.4 1.7 %collective-permute-done.11 = f32[64,128]{1,0:T(8,128)S(1)} collective-permute-done((f32[64,128]{1,0:T(8,128)S(1)}, f32[64,128]{1,0:T(8,128)S(1)}, u32[]{:S(2)}, u32[]{:S(2)}) %collective-permute-start.11) | collective-permute-done | bytes 32800 | tf_op jit(solution)/shard_map/ppermute | solution.py:309
  88.1 0.4 collective-permute-done.12
  88.6 0.0 collective-permute-done.13
  88.6 0.6 add_bitcast_fusion
  (15 shorter events, 0.0 us)
Async XLA Ops:
  0.0 8.5 %copy-start = (bf16[1,128,12288]{2,1,0:T(8,128)(2,1)S(1)}, bf16[1,128,12288]{2,1,0:T(8,128)(2,1)}, u32[]{:S(2)}) copy-start(bf16[1,128,12288]{2,1,0:T(8,128)(2,1)} %qkv_ref.15) | copy-start | bytes 9437188
  2.4 14.8 %collective-permute-start.2 = (bf16[128,1280]{1,0:T(8,128)(2,1)}, bf16[128,1280]{1,0:T(8,128)(2,1)S(1)}, u32[]{:S(2)}, u32[]{:S(2)}) collective-permute-start(bf16[128,1280]{1,0:T(8,128)(2,1)} %pack.10), channel_id=1, source_target_pairs={{0,28},{4,24},{8,20},{12,16},{16,12},{20,8},{24,4},{28,0},{1,29},{... | collective-permute-start | bytes 983048 | tf_op jit(solution)/shard_map/ppermute | solution.py:309
  8.5 1.2 %copy-start.1 = (bf16[2,4096,64]{1,2,0:T(8,128)(2,1)S(1)}, bf16[2,4096,64]{1,2,0:T(8,128)(2,1)}, u32[]{:S(2)}) copy-start(bf16[2,4096,64]{1,2,0:T(8,128)(2,1)} %param.6) | copy-start | bytes 3145732
  10.5 17.5 %collective-permute-start.4 = (bf16[128,1280]{1,0:T(8,128)(2,1)S(1)}, bf16[128,1280]{1,0:T(8,128)(2,1)S(1)}, u32[]{:S(2)}, u32[]{:S(2)}) collective-permute-start(bf16[128,1280]{1,0:T(8,128)(2,1)S(1)} %pack.12), channel_id=1, source_target_pairs={{0,12},{4,8},{8,4},{12,0},{16,28},{20,24},{24,20},{28,16},{1,13},{... | collective-permute-start | bytes 983048 | tf_op jit(solution)/shard_map/ppermute | solution.py:309
  11.4 25.4 %collective-permute-start = (bf16[128,1280]{1,0:T(8,128)(2,1)S(1)}, bf16[128,1280]{1,0:T(8,128)(2,1)S(1)}, u32[]{:S(2)}, u32[]{:S(2)}) collective-permute-start(bf16[128,1280]{1,0:T(8,128)(2,1)S(1)} %pack.8), channel_id=1, source_target_pairs={{0,24},{4,28},{8,16},{12,20},{16,8},{20,12},{24,0},{28,4},{1,25},{... | collective-permute-start | bytes 983048 | tf_op jit(solution)/shard_map/ppermute | solution.py:309
  17.3 17.9 %copy-start.3 = (bf16[128,1280]{1,0:T(8,128)(2,1)}, bf16[128,1280]{1,0:T(8,128)(2,1)S(1)}, u32[]{:S(2)}) copy-start(bf16[128,1280]{1,0:T(8,128)(2,1)S(1)} %collective-permute-done.2.refs_0_.refs_1_.refs_5_) | copy-start | bytes 983044
  29.5 16.0 %collective-permute-start.6 = (bf16[128,1280]{1,0:T(8,128)(2,1)}, bf16[128,1280]{1,0:T(8,128)(2,1)}, u32[]{:S(2)}, u32[]{:S(2)}) collective-permute-start(bf16[128,1280]{1,0:T(8,128)(2,1)} %pack.15), channel_id=1, source_target_pairs={{0,8},{4,12},{8,0},{12,4},{16,24},{20,28},{24,16},{28,20},{1,9},{5... | collective-permute-start | bytes 983048 | tf_op jit(solution)/shard_map/ppermute | solution.py:309
  33.8 11.8 %collective-permute-start.5 = (bf16[128,1280]{1,0:T(8,128)(2,1)}, bf16[128,1280]{1,0:T(8,128)(2,1)}, u32[]{:S(2)}, u32[]{:S(2)}) collective-permute-start(bf16[128,1280]{1,0:T(8,128)(2,1)} %pack.14), channel_id=1, source_target_pairs={{0,4},{4,0},{8,12},{12,8},{16,20},{20,16},{24,28},{28,24},{1,5},{5... | collective-permute-start | bytes 983048 | tf_op jit(solution)/shard_map/ppermute | solution.py:309
  36.7 25.7 %collective-permute-start.3 = (bf16[128,1280]{1,0:T(8,128)(2,1)}, bf16[128,1280]{1,0:T(8,128)(2,1)}, u32[]{:S(2)}, u32[]{:S(2)}) collective-permute-start(bf16[128,1280]{1,0:T(8,128)(2,1)} %pack.11), channel_id=1, source_target_pairs={{0,20},{4,16},{8,28},{12,24},{16,4},{20,0},{24,12},{28,8},{1,21},{... | collective-permute-start | bytes 983048 | tf_op jit(solution)/shard_map/ppermute | solution.py:309
  36.8 1.6 %copy-start.5 = (bf16[128,1280]{1,0:T(8,128)(2,1)}, bf16[128,1280]{1,0:T(8,128)(2,1)S(1)}, u32[]{:S(2)}) copy-start(bf16[128,1280]{1,0:T(8,128)(2,1)S(1)} %collective-permute-done.refs_0_.refs_4_) | copy-start | bytes 983044
  38.4 7.2 %copy-start.7 = (s32[4]{0:T(128)S(1)}, s32[4]{0:T(128)}, u32[]{:S(2)}) copy-start(s32[4]{0:T(128)} %frames_ref.5) | copy-start | bytes 52
  38.4 7.1 %copy-start.8 = (f32[1000]{0:T(1024)S(1)}, f32[1000]{0:T(1024)}, u32[]{:S(2)}) copy-start(f32[1000]{0:T(1024)} %step_weight_ref.1) | copy-start | bytes 12004
  38.4 7.1 %copy-start.9 = (s32[2]{0:T(128)S(1)}, s32[2]{0:T(128)}, u32[]{:S(2)}) copy-start(s32[2]{0:T(128)} %timestep_ref.1) | copy-start | bytes 28
  38.4 29.2 %collective-permute-start.1 = (bf16[128,1280]{1,0:T(8,128)(2,1)}, bf16[128,1280]{1,0:T(8,128)(2,1)}, u32[]{:S(2)}, u32[]{:S(2)}) collective-permute-start(bf16[128,1280]{1,0:T(8,128)(2,1)} %pack.9), channel_id=1, source_target_pairs={{0,16},{4,20},{8,24},{12,28},{16,0},{20,4},{24,8},{28,12},{1,17},{... | collective-permute-start | bytes 983048 | tf_op jit(solution)/shard_map/ppermute | solution.py:309
  43.5 1.2 %copy-start.2 = (bf16[2,4096,64]{1,2,0:T(8,128)(2,1)S(1)}, bf16[2,4096,64]{1,2,0:T(8,128)(2,1)}, u32[]{:S(2)}) copy-start(bf16[2,4096,64]{1,2,0:T(8,128)(2,1)} %param.6) | copy-start | bytes 3145732
  44.7 1.0 %copy-start.4 = (bf16[128,1280]{1,0:T(8,128)(2,1)S(1)}, bf16[128,1280]{1,0:T(8,128)(2,1)}, u32[]{:S(2)}) copy-start(bf16[128,1280]{1,0:T(8,128)(2,1)} %copy-done.3) | copy-start | bytes 983044
  44.7 1.1 %copy-start.6 = (bf16[128,1280]{1,0:T(8,128)(2,1)S(1)}, bf16[128,1280]{1,0:T(8,128)(2,1)}, u32[]{:S(2)}) copy-start(bf16[128,1280]{1,0:T(8,128)(2,1)} %copy-done.5) | copy-start | bytes 983044
  71.1 7.5 %collective-permute-start.7 = (bf16[2,64,128]{2,1,0:T(8,128)(2,1)S(1)}, bf16[2,64,128]{2,1,0:T(8,128)(2,1)S(1)}, u32[]{:S(2)}, u32[]{:S(2)}) collective-permute-start(bf16[2,64,128]{2,1,0:T(8,128)(2,1)S(1)} %get-tuple-element.20), channel_id=1, source_target_pairs={{0,24},{4,28},{8,16},{12,20},{16,8},{20,12},{24,0},{28,4},{1,25},{... | collective-permute-start | bytes 98312 | tf_op jit(solution)/shard_map/ppermute | solution.py:309
  73.3 5.3 %collective-permute-start.8 = (bf16[2,64,128]{2,1,0:T(8,128)(2,1)S(1)}, bf16[2,64,128]{2,1,0:T(8,128)(2,1)S(1)}, u32[]{:S(2)}, u32[]{:S(2)}) collective-permute-start(bf16[2,64,128]{2,1,0:T(8,128)(2,1)S(1)} %get-tuple-element.21), channel_id=1, source_target_pairs={{0,16},{4,20},{8,24},{12,28},{16,0},{20,4},{24,8},{28,12},{1,17},{... | collective-permute-start | bytes 98312 | tf_op jit(solution)/shard_map/ppermute | solution.py:309
  76.3 4.2 %collective-permute-start.9 = (bf16[2,64,128]{2,1,0:T(8,128)(2,1)S(1)}, bf16[2,64,128]{2,1,0:T(8,128)(2,1)S(1)}, u32[]{:S(2)}, u32[]{:S(2)}) collective-permute-start(bf16[2,64,128]{2,1,0:T(8,128)(2,1)S(1)} %get-tuple-element.22), channel_id=1, source_target_pairs={{0,8},{4,12},{8,0},{12,4},{16,24},{20,28},{24,16},{28,20},{1,9},{5... | collective-permute-start | bytes 98312 | tf_op jit(solution)/shard_map/ppermute | solution.py:309
  80.5 4.0 %collective-permute-start.10 = (f32[1,64,128]{2,1,0:T(8,128)S(1)}, f32[1,64,128]{2,1,0:T(8,128)S(1)}, u32[]{:S(2)}, u32[]{:S(2)}) collective-permute-start(f32[1,64,128]{2,1,0:T(8,128)S(1)} %slice.9), channel_id=1, source_target_pairs={{0,4},{4,0},{8,12},{12,8},{16,20},{20,16},{24,28},{28,24},{1,5},{5... | collective-permute-start | bytes 98312 | tf_op jit(solution)/shard_map/ppermute | solution.py:309
  84.5 3.6 %collective-permute-start.11 = (f32[64,128]{1,0:T(8,128)S(1)}, f32[64,128]{1,0:T(8,128)S(1)}, u32[]{:S(2)}, u32[]{:S(2)}) collective-permute-start(f32[64,128]{1,0:T(8,128)S(1)} %fusion), channel_id=1, source_target_pairs={{0,3},{1,2},{2,1},{3,0},{4,7},{5,6},{6,5},{7,4},{8,11},{9,10},{10,... | collective-permute-start | bytes 98312 | tf_op jit(solution)/shard_map/ppermute | solution.py:309
  84.5 4.0 %collective-permute-start.12 = (f32[64,128]{1,0:T(8,128)S(1)}, f32[64,128]{1,0:T(8,128)S(1)}, u32[]{:S(2)}, u32[]{:S(2)}) collective-permute-start(f32[64,128]{1,0:T(8,128)S(1)} %fusion), channel_id=1, source_target_pairs={{0,2},{1,3},{2,0},{3,1},{4,6},{5,7},{6,4},{7,5},{8,10},{9,11},{10,... | collective-permute-start | bytes 98312 | tf_op jit(solution)/shard_map/ppermute | solution.py:309
  86.1 2.4 %collective-permute-start.13 = (f32[64,128]{1,0:T(8,128)S(1)}, f32[64,128]{1,0:T(8,128)S(1)}, u32[]{:S(2)}, u32[]{:S(2)}) collective-permute-start(f32[64,128]{1,0:T(8,128)S(1)} %fusion), channel_id=1, source_target_pairs={{0,1},{1,0},{2,3},{3,2},{4,5},{5,4},{6,7},{7,6},{8,9},{9,8},{10,11... | collective-permute-start | bytes 98312 | tf_op jit(solution)/shard_map/ppermute | solution.py:309

commit v14 on v13

--- a/solution.py
+++ b/solution.py
@@ -60,7 +60,7 @@
         copy.wait()
 
 
-def pack(me, model, qkv, readout_t, k, count, after, wave=False, first=False):
+def pack(me, model, qkv, readout_t, k, count, after, wave=False):
     rows = qkv.shape[1]
     lat = readout_t.shape[1]
     width = count * 2 * HD + -(-count * lat // HD) * HD
@@ -74,7 +74,7 @@
             pltpu.VMEM((lat, count * HD), jnp.bfloat16),
             pltpu.SemaphoreType.DMA((2 * count + 1,)),
         ],
-        compiler_params=pltpu.CompilerParams(vmem_limit_bytes=LARGE_VMEM if first else SMALL_VMEM),
+        compiler_params=pltpu.CompilerParams(vmem_limit_bytes=SMALL_VMEM),
         cost_estimate=pl.CostEstimate(
             flops=NEXT_WAVE if wave else 0, bytes_accessed=rows * width * 4, transcendentals=0
         ),
@@ -296,9 +296,9 @@
         ],
         compiler_params=pltpu.CompilerParams(vmem_limit_bytes=SMALL_VMEM if half <= 4 else LARGE_VMEM),
         cost_estimate=pl.CostEstimate(
-            flops=count * tokens * rows * 2 * (HD + lat),
+            flops=count * tokens * rows * 4 * (HD + lat),
             bytes_accessed=tokens * count * 3 * HD * 2,
-            transcendentals=count * tokens * rows,
+            transcendentals=count * tokens * rows * 2,
         ),
         name="attend_late",
     )(span_frames, me, *pieces, *early)
@@ -327,22 +327,20 @@
     pieces = [None] * seq_count
     for n in range(half):
         k = seq_count - 1 - n
-        pieces[k] = swap(pack(me, model, qkv, readout_t, k, count, [pieces[k + 2]] if n > 1 else [], n > 1, n == 0), "seq", k)
-    for k in range(half - 1, 0, -1):
-        after = [] if k == half - 1 else [pieces[k + 1], pieces[seq_count - 1]] if k > 1 else [pieces[half - 1]]
+        pieces[k] = swap(pack(me, model, qkv, readout_t, k, count, [pieces[k + 2]] if n > 1 else [], n > 1), "seq", k)
+    pieces[0] = pack(me, model, qkv, readout_t, 0, count, [pieces[seq_count - 1]])
+    for k in [half - 1] + list(range(1, half - 1)):
+        after = [pieces[k - 1], pieces[half - 1], pieces[seq_count - 1]] if k not in (1, half - 1) else []
         pieces[k] = swap(pack(me, model, qkv, readout_t, k, count, after), "seq", k)
-    pieces[0] = pack(me, model, qkv, readout_t, 0, count, [pieces[half - 1]])
     late = [half, half + 1]
     early = [k for k in range(seq_count) if k not in late]
     merged = attend_early(
         [pieces[k] for k in early], early, span_frames, me, timestep, step_weight, sign, sample, count, lat
     )
     blocks = len(early) // 2
-    far_blocks = [blocks] + list(range(half // 2, blocks))
     ends = [pieces[k] for k in late]
-    given = attend_late(ends, early, late, far_blocks, [2, 3], merged, span_frames, me, count, lat)
-    near_blocks = list(range(half // 2 - 1, -1, -1))
-    given = attend_late(ends, early, late, near_blocks, [0, 1], merged, span_frames, me, count, lat) + given
+    order = [blocks] + list(range(blocks))
+    given = attend_late(ends, early, late, order, [0, 1, 2, 3], merged, span_frames, me, count, lat)
     size = half // 2
     while True:
         keep = given[0]

time: 89.5 us -> 89.7 us (level)
  Pallas kernels: 23.3 us -> 19.1 us
  waiting for transfers between devices: 39.1 us -> 41.7 us
  local copies, waits for them, and re-layouts: 2.69 us -> 5.1 us
    ppermute x14, waiting for transfers between devices: 39.1 us -> 41.7 us  [swap(): return lax.ppermute(array, axis, [(i, i ^ offset) for i in range(size)])]
    unnamed x20 -> x26, local copies, waits for them, and re-layouts: 2.69 us -> 5.1 us
    pallas_call x8, Pallas kernels: 11 us -> 8.63 us  [pack(): pl.pallas_call(functools.partial(pack_kernel, k), in_specs=[SMEM, SMEM] +...]
    pallas_call x2 -> x1, Pallas kernels: 6.46 us -> 4.65 us  [attend_late(): pl.pallas_call(functools.partial(late_kernel, offsets, late, chosen, grou...]
  transfers between devices with their start and end apart: 14 -> 14, of which waited for: 8 -> 10; matrix products, arithmetic and copies ran while one was open for 0% -> 0% of each run, Pallas kernels for 19% -> 15%
where the time goes in v14:
time: 89.7 us; the launch traced here: 89.4 us
  waiting for transfers between devices  41.7 us (46%)
  starting transfers between devices  22.6 us (25%)
  Pallas kernels  19.1 us (21%)
  local copies, waits for them, and re-layouts  5.1 us (6%)
    ppermute x14, waiting for transfers between devices, swap(): return lax.ppermute(array, axis, [(i, i ^ offset) for i in range(size)])  41.7 us
    ppermute x14, starting transfers between devices, swap(): return lax.ppermute(array, axis, [(i, i ^ offset) for i in range(size)])  22.6 us
    pallas_call x8, Pallas kernels, pack(): pl.pallas_call(functools.partial(pack_kernel, k), in_specs=[SMEM, SMEM] +...  8.63 us
    pallas_call x1, Pallas kernels, attend_early(): pl.pallas_call(functools.partial(early_kernel, offsets), in_specs=[SMEM]...  5.85 us
    unnamed x26, local copies, waits for them, and re-layouts  5.1 us
    pallas_call x1, Pallas kernels, attend_late(): pl.pallas_call(functools.partial(late_kernel, offsets, late, chosen, grou...  4.65 us
  transfers between devices with their start and end apart: 14, of which 10 were waited for; matrix products, arithmetic and copies ran while one was open for 0% of the time, Pallas kernels for 15%

profile of v14, /device:TPU:0, one launch (start us, length us, event | category | flops | bytes accessed | tf_op | source)
XLA Modules:
  0.0 89.4 jit_solution(10849920125121162625)
XLA Ops:
  0.0 1.9 %copy-done = bf16[1,128,12288]{2,1,0:T(8,128)(2,1)S(1)} copy-done((bf16[1,128,12288]{2,1,0:T(8,128)(2,1)S(1)}, bf16[1,128,12288]{2,1,0:T(8,128)(2,1)}, u32[]{:S(2)}) %copy-start) | copy-done | bytes 3145752
  1.9 1.2 %copy-done.2 = bf16[2,4096,64]{1,2,0:T(8,128)(2,1)S(1)} copy-done((bf16[2,4096,64]{1,2,0:T(8,128)(2,1)S(1)}, bf16[2,4096,64]{1,2,0:T(8,128)(2,1)}, u32[]{:S(2)}) %copy-start.2) | copy-done | bytes 1048600
  3.1 0.8 pack.10
  3.9 6.0 %collective-permute-start.2 = (bf16[128,1280]{1,0:T(8,128)(2,1)S(1)}, bf16[128,1280]{1,0:T(8,128)(2,1)S(1)}, u32[]{:S(2)}, u32[]{:S(2)}) collective-permute-start(bf16[128,1280]{1,0:T(8,128)(2,1)S(1)} %pack.10), channel_id=1, source_target_pairs={{0,28},{4,24},{8,20},{12,16},{16,12},{20,8},{24,4},{28,0},{1,29},{... | collective-permute-start | bytes 983048 | tf_op jit(solution)/shard_map/ppermute | solution.py:309
  10.0 0.8 pack.13
  10.8 0.6 collective-permute-start.4
  11.4 0.8 pack.14
  12.2 0.5 collective-permute-start.5
  12.7 0.8 pack.8
  13.6 1.4 %collective-permute-start = (bf16[128,1280]{1,0:T(8,128)(2,1)S(1)}, bf16[128,1280]{1,0:T(8,128)(2,1)S(1)}, u32[]{:S(2)}, u32[]{:S(2)}) collective-permute-start(bf16[128,1280]{1,0:T(8,128)(2,1)S(1)} %pack.8), channel_id=1, source_target_pairs={{0,24},{4,28},{8,16},{12,20},{16,8},{20,12},{24,0},{28,4},{1,25},{... | collective-permute-start | bytes 983048 | tf_op jit(solution)/shard_map/ppermute | solution.py:309
  15.0 3.6 %collective-permute-done.2.refs_0_.refs_2_.refs_5_ = bf16[128,1280]{1,0:T(8,128)(2,1)S(1)} collective-permute-done((bf16[128,1280]{1,0:T(8,128)(2,1)S(1)}, bf16[128,1280]{1,0:T(8,128)(2,1)S(1)}, u32[]{:S(2)}, u32[]{:S(2)}) %collective-permute-start.2) | collective-permute-done | bytes 327712 | tf_op jit(solution)/shard_map/ppermute | solution.py:309
  18.6 13.2 %collective-permute-done.4.refs_0_.refs_1_ = bf16[128,1280]{1,0:T(8,128)(2,1)S(1)} collective-permute-done((bf16[128,1280]{1,0:T(8,128)(2,1)S(1)}, bf16[128,1280]{1,0:T(8,128)(2,1)S(1)}, u32[]{:S(2)}, u32[]{:S(2)}) %collective-permute-start.4) | collective-permute-done | bytes 327712 | tf_op jit(solution)/shard_map/ppermute | solution.py:309
  31.8 0.0 collective-permute-done.5.refs_1_.refs_3_
  31.8 1.5 %pack.15 = bf16[128,1280]{1,0:T(8,128)(2,1)} custom-call(s32[1]{0:T(128)} %bitcast.me_ref, s32[1]{0:T(128)} %bitcast.1.model_ref, bf16[1,128,12288]{2,1,0:T(8,128)(2,1)S(1)} %copy-done, bf16[2,64,4096]{2,1,0:T(8,128)(2,1)S(1)} %bitcast.13, bf16[128,1280]{1,0:T(8,128)(2,1)S(1)} %collective-permute-done.4.refs_0_.refs_1_, ...), custom_call_target="tpu_custom_call" | custom-call | bytes 655360 | tf_op jit(solution)/shard_map/pack/pallas_call | solution.py:67
  33.4 0.0 copy-start.6
  33.4 0.7 copy-done.6
  34.1 0.8 collective-permute-start.6
  34.9 1.5 %pack.11 = bf16[128,1280]{1,0:T(8,128)(2,1)} custom-call(s32[1]{0:T(128)} %bitcast.me_ref, s32[1]{0:T(128)} %bitcast.1.model_ref, bf16[1,128,12288]{2,1,0:T(8,128)(2,1)S(1)} %copy-done, bf16[2,64,4096]{2,1,0:T(8,128)(2,1)S(1)} %bitcast.14, bf16[128,1280]{1,0:T(8,128)(2,1)S(1)} %collective-permute-done.2.refs_0_.refs_2_.refs_5_), custom_call_target="tpu_custom_call" | custom-call | bytes 655360 | tf_op jit(solution)/shard_map/pack/pallas_call | solution.py:67
  36.5 0.0 copy-start.1
  36.5 2.4 %collective-permute-start.3 = (bf16[128,1280]{1,0:T(8,128)(2,1)}, bf16[128,1280]{1,0:T(8,128)(2,1)}, u32[]{:S(2)}, u32[]{:S(2)}) collective-permute-start(bf16[128,1280]{1,0:T(8,128)(2,1)} %pack.11), channel_id=1, source_target_pairs={{0,20},{4,16},{8,28},{12,24},{16,4},{20,0},{24,12},{28,8},{1,21},{... | collective-permute-start | bytes 983048 | tf_op jit(solution)/shard_map/ppermute | solution.py:309
  38.8 0.0 collective-permute-done.refs_0_.refs_4_
  38.8 1.5 %pack.9 = bf16[128,1280]{1,0:T(8,128)(2,1)} custom-call(s32[1]{0:T(128)} %bitcast.me_ref, s32[1]{0:T(128)} %bitcast.1.model_ref, bf16[1,128,12288]{2,1,0:T(8,128)(2,1)S(1)} %copy-done, bf16[2,64,4096]{2,1,0:T(8,128)(2,1)S(1)} %bitcast.15, bf16[128,1280]{1,0:T(8,128)(2,1)S(1)} %collective-permute-done.refs_0_.refs_4_), custom_call_target="tpu_custom_call" | custom-call | bytes 655360 | tf_op jit(solution)/shard_map/pack/pallas_call | solution.py:67
  40.4 0.0 copy-start.10
  40.4 0.0 copy-start.11
  40.4 0.0 copy-start.12
  40.4 4.0 %collective-permute-start.1 = (bf16[128,1280]{1,0:T(8,128)(2,1)}, bf16[128,1280]{1,0:T(8,128)(2,1)}, u32[]{:S(2)}, u32[]{:S(2)}) collective-permute-start(bf16[128,1280]{1,0:T(8,128)(2,1)} %pack.9), channel_id=1, source_target_pairs={{0,16},{4,20},{8,24},{12,28},{16,0},{20,4},{24,8},{28,12},{1,17},{... | collective-permute-start | bytes 983048 | tf_op jit(solution)/shard_map/ppermute | solution.py:309
  44.4 1.2 %copy-done.3 = bf16[2,4096,64]{1,2,0:T(8,128)(2,1)S(1)} copy-done((bf16[2,4096,64]{1,2,0:T(8,128)(2,1)S(1)}, bf16[2,4096,64]{1,2,0:T(8,128)(2,1)}, u32[]{:S(2)}) %copy-start.3) | copy-done | bytes 1048600
  45.6 0.8 pack.12.refs_0_
  46.4 0.5 collective-permute-done.6.refs_2_
  46.9 5.9 %attend_early.1 = (f32[3,4,64,256]{3,2,1,0:T(8,128)S(1)}, f32[3,2,8,256]{3,2,1,0:T(8,128)S(1)}, f32[8,128]{1,0:T(8,128)S(1)}, bf16[6,128,1280]{2,1,0:T(8,128)(2,1)S(1)}, bf16[4,80,768]{2,1,0:T(8,128)(2,1)S(1)}) custom-call(s32[4]{0:T(128)S(1)} %copy-done.10, s32[1]{0:T(128)} %bitcast.me_ref, s32[2]{0:T(128)S(1)} %copy-done.12, f32[1000]{0:T(1024)S(1)} %copy-done.11, ...), custom_call_target="tpu_custom_call" | custom-call | flops 905969664 | bytes 2359296 | tf_op jit(solution)/shard_map/attend_early/pallas_call | solution.py:256
  52.8 10.6 %collective-permute-done.3.refs_1_ = bf16[128,1280]{1,0:T(8,128)(2,1)} collective-permute-done((bf16[128,1280]{1,0:T(8,128)(2,1)}, bf16[128,1280]{1,0:T(8,128)(2,1)}, u32[]{:S(2)}, u32[]{:S(2)}) %collective-permute-start.3) | collective-permute-done | bytes 327712 | tf_op jit(solution)/shard_map/ppermute | solution.py:309
  63.4 5.7 %collective-permute-done.1.refs_0_ = bf16[128,1280]{1,0:T(8,128)(2,1)} collective-permute-done((bf16[128,1280]{1,0:T(8,128)(2,1)}, bf16[128,1280]{1,0:T(8,128)(2,1)}, u32[]{:S(2)}, u32[]{:S(2)}) %collective-permute-start.1) | collective-permute-done | bytes 327712 | tf_op jit(solution)/shard_map/ppermute | solution.py:309
  69.1 4.7 %attend_late.1 = (f32[2,64,128]{2,1,0:T(8,128)S(1)}, bf16[2,64,128]{2,1,0:T(8,128)(2,1)S(1)}, bf16[2,64,128]{2,1,0:T(8,128)(2,1)S(1)}, bf16[2,64,128]{2,1,0:T(8,128)(2,1)S(1)}) custom-call(s32[4]{0:T(128)S(1)} %copy-done.10, s32[1]{0:T(128)} %bitcast.me_ref, bf16[128,1280]{1,0:T(8,128)(2,1)} %collective-permute-done.1.refs_0_, ...), custom_call_target="tpu_custom_call" | custom-call | flops 402653184 | bytes 3145728 | tf_op jit(solution)/shard_map/attend_late/pallas_call | solution.py:285
  73.7 2.2 %collective-permute-start.7 = (bf16[2,64,128]{2,1,0:T(8,128)(2,1)S(1)}, bf16[2,64,128]{2,1,0:T(8,128)(2,1)S(1)}, u32[]{:S(2)}, u32[]{:S(2)}) collective-permute-start(bf16[2,64,128]{2,1,0:T(8,128)(2,1)S(1)} %get-tuple-element.20), channel_id=1, source_target_pairs={{0,24},{4,28},{8,16},{12,20},{16,8},{20,12},{24,0},{28,4},{1,25},{... | collective-permute-start | bytes 98312 | tf_op jit(solution)/shard_map/ppermute | solution.py:309
  75.9 0.0 collective-permute-start.8
  75.9 2.3 %collective-permute-start.9 = (bf16[2,64,128]{2,1,0:T(8,128)(2,1)S(1)}, bf16[2,64,128]{2,1,0:T(8,128)(2,1)S(1)}, u32[]{:S(2)}, u32[]{:S(2)}) collective-permute-start(bf16[2,64,128]{2,1,0:T(8,128)(2,1)S(1)} %get-tuple-element.22), channel_id=1, source_target_pairs={{0,8},{4,12},{8,0},{12,4},{16,24},{20,28},{24,16},{28,20},{1,9},{5... | collective-permute-start | bytes 98312 | tf_op jit(solution)/shard_map/ppermute | solution.py:309
  78.2 1.3 %collective-permute-done.7 = bf16[2,64,128]{2,1,0:T(8,128)(2,1)S(1)} collective-permute-done((bf16[2,64,128]{2,1,0:T(8,128)(2,1)S(1)}, bf16[2,64,128]{2,1,0:T(8,128)(2,1)S(1)}, u32[]{:S(2)}, u32[]{:S(2)}) %collective-permute-start.7) | collective-permute-done | bytes 32800 | tf_op jit(solution)/shard_map/ppermute | solution.py:309
  79.5 1.2 %collective-permute-done.8 = bf16[2,64,128]{2,1,0:T(8,128)(2,1)S(1)} collective-permute-done((bf16[2,64,128]{2,1,0:T(8,128)(2,1)S(1)}, bf16[2,64,128]{2,1,0:T(8,128)(2,1)S(1)}, u32[]{:S(2)}, u32[]{:S(2)}) %collective-permute-start.8) | collective-permute-done | bytes 32800 | tf_op jit(solution)/shard_map/ppermute | solution.py:309
  80.7 0.0 collective-permute-done.9
  80.7 0.6 collective-permute-start.10
  81.3 3.4 %collective-permute-done.10 = f32[1,64,128]{2,1,0:T(8,128)S(1)} collective-permute-done((f32[1,64,128]{2,1,0:T(8,128)S(1)}, f32[1,64,128]{2,1,0:T(8,128)S(1)}, u32[]{:S(2)}, u32[]{:S(2)}) %collective-permute-start.10) | collective-permute-done | bytes 32800 | tf_op jit(solution)/shard_map/ppermute | solution.py:309
  84.7 0.0 collective-permute-start.11
  84.7 1.6 %collective-permute-start.12 = (f32[64,128]{1,0:T(8,128)S(1)}, f32[64,128]{1,0:T(8,128)S(1)}, u32[]{:S(2)}, u32[]{:S(2)}) collective-permute-start(f32[64,128]{1,0:T(8,128)S(1)} %fusion), channel_id=1, source_target_pairs={{0,2},{1,3},{2,0},{3,1},{4,6},{5,7},{6,4},{7,5},{8,10},{9,11},{10,... | collective-permute-start | bytes 98312 | tf_op jit(solution)/shard_map/ppermute | solution.py:309
  86.3 0.3 collective-permute-start.13
  86.6 1.7 %collective-permute-done.11 = f32[64,128]{1,0:T(8,128)S(1)} collective-permute-done((f32[64,128]{1,0:T(8,128)S(1)}, f32[64,128]{1,0:T(8,128)S(1)}, u32[]{:S(2)}, u32[]{:S(2)}) %collective-permute-start.11) | collective-permute-done | bytes 32800 | tf_op jit(solution)/shard_map/ppermute | solution.py:309
  88.3 0.4 collective-permute-done.12
  88.8 0.0 collective-permute-done.13
  88.8 0.6 add_bitcast_fusion
  (20 shorter events, 0.1 us)
Async XLA Ops:
  0.0 1.9 %copy-start = (bf16[1,128,12288]{2,1,0:T(8,128)(2,1)S(1)}, bf16[1,128,12288]{2,1,0:T(8,128)(2,1)}, u32[]{:S(2)}) copy-start(bf16[1,128,12288]{2,1,0:T(8,128)(2,1)} %qkv_ref.15) | copy-start | bytes 9437188
  1.9 1.2 %copy-start.2 = (bf16[2,4096,64]{1,2,0:T(8,128)(2,1)S(1)}, bf16[2,4096,64]{1,2,0:T(8,128)(2,1)}, u32[]{:S(2)}) copy-start(bf16[2,4096,64]{1,2,0:T(8,128)(2,1)} %param.6) | copy-start | bytes 3145732
  3.9 14.7 %collective-permute-start.2 = (bf16[128,1280]{1,0:T(8,128)(2,1)S(1)}, bf16[128,1280]{1,0:T(8,128)(2,1)S(1)}, u32[]{:S(2)}, u32[]{:S(2)}) collective-permute-start(bf16[128,1280]{1,0:T(8,128)(2,1)S(1)} %pack.10), channel_id=1, source_target_pairs={{0,28},{4,24},{8,20},{12,16},{16,12},{20,8},{24,4},{28,0},{1,29},{... | collective-permute-start | bytes 983048 | tf_op jit(solution)/shard_map/ppermute | solution.py:309
  10.8 21.0 %collective-permute-start.4 = (bf16[128,1280]{1,0:T(8,128)(2,1)S(1)}, bf16[128,1280]{1,0:T(8,128)(2,1)S(1)}, u32[]{:S(2)}, u32[]{:S(2)}) collective-permute-start(bf16[128,1280]{1,0:T(8,128)(2,1)S(1)} %pack.13), channel_id=1, source_target_pairs={{0,4},{4,0},{8,12},{12,8},{16,20},{20,16},{24,28},{28,24},{1,5},{5... | collective-permute-start | bytes 983048 | tf_op jit(solution)/shard_map/ppermute | solution.py:309
  12.2 19.6 %collective-permute-start.5 = (bf16[128,1280]{1,0:T(8,128)(2,1)S(1)}, bf16[128,1280]{1,0:T(8,128)(2,1)S(1)}, u32[]{:S(2)}, u32[]{:S(2)}) collective-permute-start(bf16[128,1280]{1,0:T(8,128)(2,1)S(1)} %pack.14), channel_id=1, source_target_pairs={{0,12},{4,8},{8,4},{12,0},{16,28},{20,24},{24,20},{28,16},{1,13},{... | collective-permute-start | bytes 983048 | tf_op jit(solution)/shard_map/ppermute | solution.py:309
  13.6 25.3 %collective-permute-start = (bf16[128,1280]{1,0:T(8,128)(2,1)S(1)}, bf16[128,1280]{1,0:T(8,128)(2,1)S(1)}, u32[]{:S(2)}, u32[]{:S(2)}) collective-permute-start(bf16[128,1280]{1,0:T(8,128)(2,1)S(1)} %pack.8), channel_id=1, source_target_pairs={{0,24},{4,28},{8,16},{12,20},{16,8},{20,12},{24,0},{28,4},{1,25},{... | collective-permute-start | bytes 983048 | tf_op jit(solution)/shard_map/ppermute | solution.py:309
  31.8 4.6 %copy-start.4 = (bf16[128,1280]{1,0:T(8,128)(2,1)}, bf16[128,1280]{1,0:T(8,128)(2,1)S(1)}, u32[]{:S(2)}) copy-start(bf16[128,1280]{1,0:T(8,128)(2,1)S(1)} %collective-permute-done.4.refs_0_.refs_1_) | copy-start | bytes 983044
  33.4 0.7 copy-start.6
  34.1 12.8 %collective-permute-start.6 = (bf16[128,1280]{1,0:T(8,128)(2,1)}, bf16[128,1280]{1,0:T(8,128)(2,1)}, u32[]{:S(2)}, u32[]{:S(2)}) collective-permute-start(bf16[128,1280]{1,0:T(8,128)(2,1)} %pack.15), channel_id=1, source_target_pairs={{0,8},{4,12},{8,0},{12,4},{16,24},{20,28},{24,16},{28,20},{1,9},{5... | collective-permute-start | bytes 983048 | tf_op jit(solution)/shard_map/ppermute | solution.py:309
  36.5 7.9 %copy-start.1 = (bf16[1,128,12288]{2,1,0:T(8,128)(2,1)S(1)}, bf16[1,128,12288]{2,1,0:T(8,128)(2,1)}, u32[]{:S(2)}) copy-start(bf16[1,128,12288]{2,1,0:T(8,128)(2,1)} %qkv_ref.15) | copy-start | bytes 9437188
  36.5 26.9 %collective-permute-start.3 = (bf16[128,1280]{1,0:T(8,128)(2,1)}, bf16[128,1280]{1,0:T(8,128)(2,1)}, u32[]{:S(2)}, u32[]{:S(2)}) collective-permute-start(bf16[128,1280]{1,0:T(8,128)(2,1)} %pack.11), channel_id=1, source_target_pairs={{0,20},{4,16},{8,28},{12,24},{16,4},{20,0},{24,12},{28,8},{1,21},{... | collective-permute-start | bytes 983048 | tf_op jit(solution)/shard_map/ppermute | solution.py:309
  38.8 1.6 %copy-start.8 = (bf16[128,1280]{1,0:T(8,128)(2,1)}, bf16[128,1280]{1,0:T(8,128)(2,1)S(1)}, u32[]{:S(2)}) copy-start(bf16[128,1280]{1,0:T(8,128)(2,1)S(1)} %collective-permute-done.refs_0_.refs_4_) | copy-start | bytes 983044
  40.4 6.5 %copy-start.10 = (s32[4]{0:T(128)S(1)}, s32[4]{0:T(128)}, u32[]{:S(2)}) copy-start(s32[4]{0:T(128)} %frames_ref.3) | copy-start | bytes 52
  40.4 6.5 %copy-start.11 = (f32[1000]{0:T(1024)S(1)}, f32[1000]{0:T(1024)}, u32[]{:S(2)}) copy-start(f32[1000]{0:T(1024)} %step_weight_ref.1) | copy-start | bytes 12004
  40.4 6.5 %copy-start.12 = (s32[2]{0:T(128)S(1)}, s32[2]{0:T(128)}, u32[]{:S(2)}) copy-start(s32[2]{0:T(128)} %timestep_ref.1) | copy-start | bytes 28
  40.4 28.6 %collective-permute-start.1 = (bf16[128,1280]{1,0:T(8,128)(2,1)}, bf16[128,1280]{1,0:T(8,128)(2,1)}, u32[]{:S(2)}, u32[]{:S(2)}) collective-permute-start(bf16[128,1280]{1,0:T(8,128)(2,1)} %pack.9), channel_id=1, source_target_pairs={{0,16},{4,20},{8,24},{12,28},{16,0},{20,4},{24,8},{28,12},{1,17},{... | collective-permute-start | bytes 983048 | tf_op jit(solution)/shard_map/ppermute | solution.py:309
  44.4 1.2 %copy-start.3 = (bf16[2,4096,64]{1,2,0:T(8,128)(2,1)S(1)}, bf16[2,4096,64]{1,2,0:T(8,128)(2,1)}, u32[]{:S(2)}) copy-start(bf16[2,4096,64]{1,2,0:T(8,128)(2,1)} %param.6) | copy-start | bytes 3145732
  45.6 1.3 %copy-start.5 = (bf16[128,1280]{1,0:T(8,128)(2,1)S(1)}, bf16[128,1280]{1,0:T(8,128)(2,1)}, u32[]{:S(2)}) copy-start(bf16[128,1280]{1,0:T(8,128)(2,1)} %copy-done.4) | copy-start | bytes 983044
  45.6 1.3 %copy-start.7 = (bf16[128,1280]{1,0:T(8,128)(2,1)S(1)}, bf16[128,1280]{1,0:T(8,128)(2,1)}, u32[]{:S(2)}) copy-start(bf16[128,1280]{1,0:T(8,128)(2,1)} %copy-done.6) | copy-start | bytes 983044
  45.6 1.3 %copy-start.9 = (bf16[128,1280]{1,0:T(8,128)(2,1)S(1)}, bf16[128,1280]{1,0:T(8,128)(2,1)}, u32[]{:S(2)}) copy-start(bf16[128,1280]{1,0:T(8,128)(2,1)} %copy-done.8) | copy-start | bytes 983044
  73.7 5.8 %collective-permute-start.7 = (bf16[2,64,128]{2,1,0:T(8,128)(2,1)S(1)}, bf16[2,64,128]{2,1,0:T(8,128)(2,1)S(1)}, u32[]{:S(2)}, u32[]{:S(2)}) collective-permute-start(bf16[2,64,128]{2,1,0:T(8,128)(2,1)S(1)} %get-tuple-element.20), channel_id=1, source_target_pairs={{0,24},{4,28},{8,16},{12,20},{16,8},{20,12},{24,0},{28,4},{1,25},{... | collective-permute-start | bytes 98312 | tf_op jit(solution)/shard_map/ppermute | solution.py:309
  75.9 4.8 %collective-permute-start.8 = (bf16[2,64,128]{2,1,0:T(8,128)(2,1)S(1)}, bf16[2,64,128]{2,1,0:T(8,128)(2,1)S(1)}, u32[]{:S(2)}, u32[]{:S(2)}) collective-permute-start(bf16[2,64,128]{2,1,0:T(8,128)(2,1)S(1)} %get-tuple-element.21), channel_id=1, source_target_pairs={{0,16},{4,20},{8,24},{12,28},{16,0},{20,4},{24,8},{28,12},{1,17},{... | collective-permute-start | bytes 98312 | tf_op jit(solution)/shard_map/ppermute | solution.py:309
  75.9 4.8 %collective-permute-start.9 = (bf16[2,64,128]{2,1,0:T(8,128)(2,1)S(1)}, bf16[2,64,128]{2,1,0:T(8,128)(2,1)S(1)}, u32[]{:S(2)}, u32[]{:S(2)}) collective-permute-start(bf16[2,64,128]{2,1,0:T(8,128)(2,1)S(1)} %get-tuple-element.22), channel_id=1, source_target_pairs={{0,8},{4,12},{8,0},{12,4},{16,24},{20,28},{24,16},{28,20},{1,9},{5... | collective-permute-start | bytes 98312 | tf_op jit(solution)/shard_map/ppermute | solution.py:309
  80.7 4.0 %collective-permute-start.10 = (f32[1,64,128]{2,1,0:T(8,128)S(1)}, f32[1,64,128]{2,1,0:T(8,128)S(1)}, u32[]{:S(2)}, u32[]{:S(2)}) collective-permute-start(f32[1,64,128]{2,1,0:T(8,128)S(1)} %slice.9), channel_id=1, source_target_pairs={{0,4},{4,0},{8,12},{12,8},{16,20},{20,16},{24,28},{28,24},{1,5},{5... | collective-permute-start | bytes 98312 | tf_op jit(solution)/shard_map/ppermute | solution.py:309
  84.7 3.6 %collective-permute-start.11 = (f32[64,128]{1,0:T(8,128)S(1)}, f32[64,128]{1,0:T(8,128)S(1)}, u32[]{:S(2)}, u32[]{:S(2)}) collective-permute-start(f32[64,128]{1,0:T(8,128)S(1)} %fusion), channel_id=1, source_target_pairs={{0,3},{1,2},{2,1},{3,0},{4,7},{5,6},{6,5},{7,4},{8,11},{9,10},{10,... | collective-permute-start | bytes 98312 | tf_op jit(solution)/shard_map/ppermute | solution.py:309
  84.7 4.0 %collective-permute-start.12 = (f32[64,128]{1,0:T(8,128)S(1)}, f32[64,128]{1,0:T(8,128)S(1)}, u32[]{:S(2)}, u32[]{:S(2)}) collective-permute-start(f32[64,128]{1,0:T(8,128)S(1)} %fusion), channel_id=1, source_target_pairs={{0,2},{1,3},{2,0},{3,1},{4,6},{5,7},{6,4},{7,5},{8,10},{9,11},{10,... | collective-permute-start | bytes 98312 | tf_op jit(solution)/shard_map/ppermute | solution.py:309
  86.3 2.4 %collective-permute-start.13 = (f32[64,128]{1,0:T(8,128)S(1)}, f32[64,128]{1,0:T(8,128)S(1)}, u32[]{:S(2)}, u32[]{:S(2)}) collective-permute-start(f32[64,128]{1,0:T(8,128)S(1)} %fusion), channel_id=1, source_target_pairs={{0,1},{1,0},{2,3},{3,2},{4,5},{5,4},{6,7},{7,6},{8,9},{9,8},{10,11... | collective-permute-start | bytes 98312 | tf_op jit(solution)/shard_map/ppermute | solution.py:309

commit v15 on v14

--- a/solution.py
+++ b/solution.py
@@ -14,7 +14,7 @@
 NT = (((1,), (1,)), ((), ()))
 LOG2_SCALE = math.log2(math.e) / math.sqrt(HD)
 LOWEST = -1e30
-NEXT_WAVE = 0
+SPLIT_COST = 0
 SMALL_VMEM = 24 * 1024 * 1024
 LARGE_VMEM = 60 * 1024 * 1024
 SMEM = pl.BlockSpec(memory_space=pltpu.SMEM)
@@ -30,11 +30,11 @@
     return (h * lat) % HD, count * 2 * HD + (h * lat // HD) * HD
 
 
-def pack_kernel(k, me_ref, model_ref, qkv_ref, readout_ref, *refs):
+def pack_kernel(head_of, me_ref, model_ref, qkv_ref, readout_ref, *refs):
     out_ref, values, readout, sems = refs[-4:]
     rows = out_ref.shape[0]
     count, lat = values.shape[0], readout.shape[0]
-    first = (me_ref[0] ^ k) * count
+    first = head_of(me_ref[0])
 
     def columns(h, part, width):
         return pl.ds(pl.multiple_of(((first + h) * 3 + part) * HD, HD), width)
@@ -60,12 +60,12 @@
         copy.wait()
 
 
-def pack(me, model, qkv, readout_t, k, count, after, wave=False):
+def pack(me, model, qkv, readout_t, head_of, count, after):
     rows = qkv.shape[1]
     lat = readout_t.shape[1]
     width = count * 2 * HD + -(-count * lat // HD) * HD
     return pl.pallas_call(
-        functools.partial(pack_kernel, k),
+        functools.partial(pack_kernel, head_of),
         in_specs=[SMEM, SMEM] + [HBM] * (2 + len(after)),
         out_specs=VMEM,
         out_shape=jax.ShapeDtypeStruct((rows, width), jnp.bfloat16),
@@ -76,10 +76,38 @@
         ],
         compiler_params=pltpu.CompilerParams(vmem_limit_bytes=SMALL_VMEM),
         cost_estimate=pl.CostEstimate(
-            flops=NEXT_WAVE if wave else 0, bytes_accessed=rows * width * 4, transcendentals=0
+            flops=0, bytes_accessed=rows * width * 4, transcendentals=0
         ),
         name="pack",
     )(me, model, qkv, readout_t, *after)
+
+
+def queries_kernel(head_of, me_ref, qkv_ref, *refs):
+    out_ref, sems = refs[-2:]
+    count = out_ref.shape[1] // HD
+    first = head_of(me_ref[0])
+    copies = []
+    for h in range(count):
+        source = qkv_ref.at[0, :, pl.ds(pl.multiple_of((first + h) * 3 * HD, HD), HD)]
+        copies.append(pltpu.make_async_copy(source, out_ref.at[:, h * HD : (h + 1) * HD], sems.at[h]))
+    for copy in copies:
+        copy.start()
+    for copy in copies:
+        copy.wait()
+
+
+def pack_queries(me, qkv, head_of, count, after):
+    rows = qkv.shape[1]
+    return pl.pallas_call(
+        functools.partial(queries_kernel, head_of),
+        in_specs=[SMEM] + [HBM] * (1 + len(after)),
+        out_specs=VMEM,
+        out_shape=jax.ShapeDtypeStruct((rows, count * HD), jnp.bfloat16),
+        scratch_shapes=[pltpu.SemaphoreType.DMA((count,))],
+        compiler_params=pltpu.CompilerParams(vmem_limit_bytes=SMALL_VMEM),
+        cost_estimate=pl.CostEstimate(flops=0, bytes_accessed=rows * count * HD * 4, transcendentals=0),
+        name="pack_queries",
+    )(me, qkv, *after)
 
 
 def mask_rows(frames_ref, me, rows, query_offsets, key_offsets):
@@ -194,6 +222,7 @@
     early = len(offsets)
     arrived = refs[:2]
     sums_ref, stats_ref, factor_ref, early_ref, early_folded, *out_refs, late_pieces, folded, sems = refs[2:]
+    split_ref = out_refs.pop(0) if len(out_refs) > len(groups) else None
     copies = [pltpu.make_async_copy(arrived[n], late_pieces.at[n], sems.at[n]) for n in range(2)]
     for copy in copies:
         copy.start()
@@ -215,7 +244,10 @@
         for j in range(2):
             k = every[2 * b + j]
             out_ref = out_refs[groups.index(k // size)]
-            out_ref[k % size] = (results[b][:, j * rows : (j + 1) * rows] * factor).astype(out_ref.dtype)
+            part = results[b][:, j * rows : (j + 1) * rows]
+            if split_ref is not None:
+                part = part + split_ref[k]
+            out_ref[k % size] = (part * factor).astype(out_ref.dtype)
 
     units = []
     blocks = early // 2
@@ -247,6 +279,107 @@
             ]
             units.append((tiles, values, shifts, finish))
     run_units(units, lat)
+
+
+def split_kernel(half, frames_ref, me_ref, *refs):
+    near, far = refs[:half], refs[half : 2 * half]
+    sums_ref, stats_ref, near_pieces, far_pieces, folded, asked, sems = refs[-7:]
+    copies = [pltpu.make_async_copy(near[k], near_pieces.at[k], sems.at[k]) for k in range(half)]
+    copies += [pltpu.make_async_copy(far[k], far_pieces.at[k], sems.at[half + k]) for k in range(half)]
+    for copy in copies:
+        copy.start()
+    for copy in copies:
+        copy.wait()
+    me = me_ref[0]
+    rows = near_pieces.shape[1]
+    lat = sums_ref.shape[2]
+    count = folded.shape[0]
+    pieces = [near_pieces.at[k] for k in range(half)]
+    stage_values(folded, pieces, lat)
+    for i in range(count):
+        for b, read in enumerate(pairs_of(pieces, i, 0)):
+            asked[b, i] = read()
+        for k in range(half):
+            asked[half // 2 + k // 2, i, (k % 2) * rows : (k % 2 + 1) * rows] = far_pieces[k, :, i * HD : (i + 1) * HD]
+
+    def some_blocks(b, carry):
+        shifts = mask_rows(frames_ref, me, rows, [2 * b, 2 * b + 1], range(half))
+        peaks, totals, units = [], [], []
+        for i in range(count):
+
+            def finish(summed, total, peak, i=i):
+                sums_ref[b, i] = summed
+                peaks.append(peak)
+                totals.append(total)
+
+            tiles = [functools.partial(score_tile, keys, lambda i=i: asked[b, i]) for keys in pairs_of(pieces, i, 1)]
+            values = [lambda i=i, t=t: folded[i, :, t * 2 * rows : (t + 1) * 2 * rows] for t in range(half // 2)]
+            units.append((tiles, values, shifts, finish))
+        run_units(units, lat)
+        rest = [jnp.ones_like(peaks[0])] * (stats_ref.shape[2] - count)
+        stats_ref[b, 0] = jnp.concatenate(peaks + rest, axis=0)
+        stats_ref[b, 1] = jnp.concatenate(totals + rest, axis=0)
+        return carry
+
+    lax.fori_loop(0, half, some_blocks, 0)
+
+
+def attend_split(near, far, span_frames, me, count, lat):
+    half = len(near)
+    rows, width = near[0].shape
+    return pl.pallas_call(
+        functools.partial(split_kernel, half),
+        in_specs=[SMEM, SMEM] + [HBM] * (2 * half),
+        out_specs=[VMEM, VMEM],
+        out_shape=[
+            jax.ShapeDtypeStruct((half, count, lat, 2 * rows), jnp.float32),
+            jax.ShapeDtypeStruct((half, 2, 8, 2 * rows), jnp.float32),
+        ],
+        scratch_shapes=[
+            pltpu.VMEM((half, rows, width), jnp.bfloat16),
+            pltpu.VMEM((half, rows, count * HD), jnp.bfloat16),
+            pltpu.VMEM((count, lat + 16, half * rows), jnp.bfloat16),
+            pltpu.VMEM((half, count, 2 * rows, HD), jnp.bfloat16),
+            pltpu.SemaphoreType.DMA((2 * half,)),
+        ],
+        compiler_params=pltpu.CompilerParams(vmem_limit_bytes=SMALL_VMEM),
+        cost_estimate=pl.CostEstimate(
+            flops=SPLIT_COST,
+            bytes_accessed=0,
+            transcendentals=0,
+        ),
+        name="attend_split",
+    )(span_frames, me, *near, *far)
+
+
+def combine_kernel(count, sums_ref, stats_ref, other_ref, out_ref):
+    rows = out_ref.shape[2]
+    blocks = sums_ref.shape[0]
+    for b in range(blocks):
+        o = b ^ (blocks // 2)
+        peak, other_peak = stats_ref[b, 0], other_ref[o, 0]
+        highest = jnp.maximum(peak, other_peak)
+        own = jnp.exp2((peak - highest) * LOG2_SCALE)
+        both = stats_ref[b, 1] * own + other_ref[o, 1] * jnp.exp2((other_peak - highest) * LOG2_SCALE)
+        weight = own / both
+        result = sums_ref[b, 0] * weight[:1]
+        for i in range(1, count):
+            result = result + sums_ref[b, i] * weight[i : i + 1]
+        for j in range(2):
+            out_ref[b * 2 + j] = result[:, j * rows : (j + 1) * rows]
+
+
+def combine(sums, stats, other):
+    half, count, lat, block = sums.shape
+    return pl.pallas_call(
+        functools.partial(combine_kernel, count),
+        in_specs=[VMEM] * 3,
+        out_specs=VMEM,
+        out_shape=jax.ShapeDtypeStruct((2 * half, lat, block // 2), jnp.float32),
+        compiler_params=pltpu.CompilerParams(vmem_limit_bytes=SMALL_VMEM),
+        cost_estimate=pl.CostEstimate(flops=0, bytes_accessed=sums.size * 4, transcendentals=0),
+        name="combine",
+    )(sums, stats, other)
 
 
 def attend_early(pieces, offsets, span_frames, me, timestep, step_weight, sign, sample, count, lat):
@@ -313,7 +446,9 @@
     seq_count = lax.axis_size("seq")
     mp_count = lax.axis_size("mp")
     half = seq_count // 2
-    count = HEADS // seq_count
+    pair_heads = 2 * HEADS // seq_count
+    count = max(1, pair_heads // 4)
+    split = pair_heads - 2 * count
     lat = readout.shape[2]
     me = lax.axis_index("seq").astype(jnp.int32).reshape(1)
     mp_index = lax.axis_index("mp").astype(jnp.int32)
@@ -324,20 +459,43 @@
     model = model_index.reshape(1)
     readout_t = jnp.swapaxes(readout, 1, 2)
 
+    def whole_head(k):
+        return lambda m: ((m ^ k) & (half - 1)) * pair_heads + split + (m ^ k) // half * count
+
+    def split_head(k):
+        return lambda m: ((m ^ k) & (half - 1)) * pair_heads
+
+    def send(k, after):
+        packed = pack(me, model, qkv, readout_t, whole_head(k), count, after)
+        return swap(packed, "seq", k) if k else packed
+
     pieces = [None] * seq_count
-    for n in range(half):
-        k = seq_count - 1 - n
-        pieces[k] = swap(pack(me, model, qkv, readout_t, k, count, [pieces[k + 2]] if n > 1 else [], n > 1), "seq", k)
-    pieces[0] = pack(me, model, qkv, readout_t, 0, count, [pieces[seq_count - 1]])
+    near, far = [None] * half, [None] * half
+    tops = range(seq_count - 1, half - 1, -1)
+    if split:
+        for k in tops:
+            after = [far[k + 2 - half]] if k < seq_count - 2 else []
+            far[k - half] = swap(pack_queries(me, qkv, split_head(k), split, after), "seq", k)
+        for k in [half - 1] + list(range(1, half - 1)):
+            after = [near[k - 1], near[half - 1], far[half - 1], far[half - 2]] if k not in (1, half - 1) else []
+            near[k] = swap(pack(me, model, qkv, readout_t, split_head(k), split, after), "seq", k)
+        near[0] = pack(me, model, qkv, readout_t, split_head(0), split, [far[half - 1]])
+        sums, stats = attend_split(near, far, span_frames, me, split, lat)
+    for k in tops:
+        after = [pieces[k + 2], stats] if k < seq_count - 2 and split else [pieces[k + 2]] if k < seq_count - 2 else []
+        pieces[k] = send(k, after if k < seq_count - 2 or not split else [far[k - half - 2]])
+    pieces[0] = send(0, [pieces[seq_count - 1]])
     for k in [half - 1] + list(range(1, half - 1)):
-        after = [pieces[k - 1], pieces[half - 1], pieces[seq_count - 1]] if k not in (1, half - 1) else []
-        pieces[k] = swap(pack(me, model, qkv, readout_t, k, count, after), "seq", k)
+        after = [pieces[k - 1], pieces[half - 1]] if k not in (1, half - 1) else [near[half - 2]] if split else []
+        pieces[k] = send(k, after)
     late = [half, half + 1]
     early = [k for k in range(seq_count) if k not in late]
     merged = attend_early(
         [pieces[k] for k in early], early, span_frames, me, timestep, step_weight, sign, sample, count, lat
     )
     blocks = len(early) // 2
+    if split:
+        merged = list(merged) + [combine(sums, stats, swap(stats, "seq", half))]
     ends = [pieces[k] for k in late]
     order = [blocks] + list(range(blocks))
     given = attend_late(ends, early, late, order, [0, 1, 2, 3], merged, span_frames, me, count, lat)

time: 89.7 us -> 106 us (1.18)
  starting transfers between devices: 22.6 us -> 31.1 us
  waiting for transfers between devices: 41.7 us -> 45.8 us
  Pallas kernels: 19.1 us -> 23 us
    ppermute x14 -> x22, starting transfers between devices: 22.6 us -> 31.1 us  [swap(): return lax.ppermute(array, axis, [(i, i ^ offset) for i in range(size)])]
    pallas_call x8 -> x18, Pallas kernels: 8.63 us -> 15.5 us  [the longest x12 8.56 us: pack(): pl.pallas_call(functools.partial(pack_kernel, head_of), in_specs=[SMEM, S...]
    ppermute x14 -> x22, waiting for transfers between devices: 41.7 us -> 45.8 us  [swap(): return lax.ppermute(array, axis, [(i, i ^ offset) for i in range(size)])]
    pallas_call x1, Pallas kernels: 5.85 us -> 4.29 us  [attend_early(): pl.pallas_call(functools.partial(early_kernel, offsets), in_specs=[SMEM]...]
    pallas_call x1, Pallas kernels: 4.65 us -> 3.22 us  [attend_late(): pl.pallas_call(functools.partial(late_kernel, offsets, late, chosen, grou...]
    unnamed x26 -> x28, local copies, waits for them, and re-layouts: 5.1 us -> 4.39 us
  transfers between devices with their start and end apart: 14 -> 22, of which waited for: 10 -> 11; matrix products, arithmetic and copies ran while one was open for 0% -> 0% of each run, Pallas kernels for 15% -> 17%
where the time goes in v15:
time: 106 us; the launch traced here: 105 us
  waiting for transfers between devices  45.8 us (43%)
  starting transfers between devices  31.1 us (29%)
  Pallas kernels  23 us (22%)
  local copies, waits for them, and re-layouts  4.4 us (4%)
    ppermute x22, waiting for transfers between devices, swap(): return lax.ppermute(array, axis, [(i, i ^ offset) for i in range(size)])  45.8 us
    ppermute x22, starting transfers between devices, swap(): return lax.ppermute(array, axis, [(i, i ^ offset) for i in range(size)])  31.1 us
    pallas_call x12, Pallas kernels, pack(): pl.pallas_call(functools.partial(pack_kernel, head_of), in_specs=[SMEM, S...  8.56 us
    pallas_call x1, Pallas kernels, attend_split(): pl.pallas_call(functools.partial(split_kernel, half), in_specs=[SMEM, SME...  5.66 us
    unnamed x28, local copies, waits for them, and re-layouts  4.39 us
    pallas_call x1, Pallas kernels, attend_early(): pl.pallas_call(functools.partial(early_kernel, offsets), in_specs=[SMEM]...  4.29 us
    pallas_call x1, Pallas kernels, attend_late(): pl.pallas_call(functools.partial(late_kernel, offsets, late, chosen, grou...  3.22 us
  transfers between devices with their start and end apart: 22, of which 11 were waited for; matrix products, arithmetic and copies ran while one was open for 0% of the time, Pallas kernels for 17%

profile of v15, /device:TPU:0, one launch (start us, length us, event | category | flops | bytes accessed | tf_op | source)
XLA Modules:
  0.0 105.3 jit_solution(4287871655871959188)
XLA Ops:
  0.0 1.9 %copy-done = bf16[1,128,12288]{2,1,0:T(8,128)(2,1)S(1)} copy-done((bf16[1,128,12288]{2,1,0:T(8,128)(2,1)S(1)}, bf16[1,128,12288]{2,1,0:T(8,128)(2,1)}, u32[]{:S(2)}) %copy-start) | copy-done | bytes 3145752
  1.9 1.2 %copy-done.2 = bf16[2,4096,64]{1,2,0:T(8,128)(2,1)S(1)} copy-done((bf16[2,4096,64]{1,2,0:T(8,128)(2,1)S(1)}, bf16[2,4096,64]{1,2,0:T(8,128)(2,1)}, u32[]{:S(2)}) %copy-start.2) | copy-done | bytes 1048600
  3.1 0.8 pack.14
  3.9 3.0 %collective-permute-start.4 = (bf16[128,1280]{1,0:T(8,128)(2,1)S(1)}, bf16[128,1280]{1,0:T(8,128)(2,1)S(1)}, u32[]{:S(2)}, u32[]{:S(2)}) collective-permute-start(bf16[128,1280]{1,0:T(8,128)(2,1)S(1)} %pack.14), channel_id=1, source_target_pairs={{0,4},{4,0},{8,12},{12,8},{16,20},{20,16},{24,28},{28,24},{1,5},{5... | collective-permute-start | bytes 983048 | tf_op jit(solution)/shard_map/ppermute | solution.py:442
  6.9 0.8 pack.15
  7.8 1.6 %collective-permute-start.5 = (bf16[128,1280]{1,0:T(8,128)(2,1)S(1)}, bf16[128,1280]{1,0:T(8,128)(2,1)S(1)}, u32[]{:S(2)}, u32[]{:S(2)}) collective-permute-start(bf16[128,1280]{1,0:T(8,128)(2,1)S(1)} %pack.15), channel_id=1, source_target_pairs={{0,12},{4,8},{8,4},{12,0},{16,28},{20,24},{24,20},{28,16},{1,13},{... | collective-permute-start | bytes 983048 | tf_op jit(solution)/shard_map/ppermute | solution.py:442
  9.5 3.5 %collective-permute-start.3 = (bf16[128,512]{1,0:T(8,128)(2,1)S(1)}, bf16[128,512]{1,0:T(8,128)(2,1)S(1)}, u32[]{:S(2)}, u32[]{:S(2)}) collective-permute-start(bf16[128,512]{1,0:T(8,128)(2,1)S(1)} %pack_queries.6), channel_id=1, source_target_pairs={{0,28},{4,24},{8,20},{12,16},{16,12},{20,8},{24,4},{28,0},{1,29},{... | collective-permute-start | bytes 393224 | tf_op jit(solution)/shard_map/ppermute | solution.py:442
  13.0 1.4 %collective-permute-start = (bf16[128,512]{1,0:T(8,128)(2,1)S(1)}, bf16[128,512]{1,0:T(8,128)(2,1)S(1)}, u32[]{:S(2)}, u32[]{:S(2)}) collective-permute-start(bf16[128,512]{1,0:T(8,128)(2,1)S(1)} %pack_queries.4), channel_id=1, source_target_pairs={{0,24},{4,28},{8,16},{12,20},{16,8},{20,12},{24,0},{28,4},{1,25},{... | collective-permute-start | bytes 393224 | tf_op jit(solution)/shard_map/ppermute | solution.py:442
  14.4 12.6 %collective-permute-done.3.refs_0_.refs_2_.refs_7_ = bf16[128,512]{1,0:T(8,128)(2,1)S(1)} collective-permute-done((bf16[128,512]{1,0:T(8,128)(2,1)S(1)}, bf16[128,512]{1,0:T(8,128)(2,1)S(1)}, u32[]{:S(2)}, u32[]{:S(2)}) %collective-permute-start.3) | collective-permute-done | bytes 131104 | tf_op jit(solution)/shard_map/ppermute | solution.py:442
  27.0 0.8 pack.16
  27.9 0.1 pack_queries.7
  28.0 3.3 %collective-permute-start.7 = (bf16[128,512]{1,0:T(8,128)(2,1)S(1)}, bf16[128,512]{1,0:T(8,128)(2,1)S(1)}, u32[]{:S(2)}, u32[]{:S(2)}) collective-permute-start(bf16[128,512]{1,0:T(8,128)(2,1)S(1)} %pack_queries.7), channel_id=1, source_target_pairs={{0,20},{4,16},{8,28},{12,24},{16,4},{20,0},{24,12},{28,8},{1,21},{... | collective-permute-start | bytes 393224 | tf_op jit(solution)/shard_map/ppermute | solution.py:442
  31.4 1.1 %collective-permute-start.1 = (bf16[128,512]{1,0:T(8,128)(2,1)S(1)}, bf16[128,512]{1,0:T(8,128)(2,1)S(1)}, u32[]{:S(2)}, u32[]{:S(2)}) collective-permute-start(bf16[128,512]{1,0:T(8,128)(2,1)S(1)} %pack_queries.5), channel_id=1, source_target_pairs={{0,16},{4,20},{8,24},{12,28},{16,0},{20,4},{24,8},{28,12},{1,17},{... | collective-permute-start | bytes 393224 | tf_op jit(solution)/shard_map/ppermute | solution.py:442
  32.6 8.3 %collective-permute-done.6.refs_2_.refs_0_ = bf16[128,1280]{1,0:T(8,128)(2,1)S(1)} collective-permute-done((bf16[128,1280]{1,0:T(8,128)(2,1)S(1)}, bf16[128,1280]{1,0:T(8,128)(2,1)S(1)}, u32[]{:S(2)}, u32[]{:S(2)}) %collective-permute-start.6) | collective-permute-done | bytes 327712 | tf_op jit(solution)/shard_map/ppermute | solution.py:442
  40.8 0.4 pack.21
  41.2 2.7 %collective-permute-start.11 = (bf16[128,640]{1,0:T(8,128)(2,1)S(1)}, bf16[128,640]{1,0:T(8,128)(2,1)S(1)}, u32[]{:S(2)}, u32[]{:S(2)}) collective-permute-start(bf16[128,640]{1,0:T(8,128)(2,1)S(1)} %pack.21), channel_id=1, source_target_pairs={{0,4},{4,0},{8,12},{12,8},{16,20},{20,16},{24,28},{28,24},{1,5},{5... | collective-permute-start | bytes 491528 | tf_op jit(solution)/shard_map/ppermute | solution.py:442
  43.9 0.4 pack.22
  44.4 0.4 pack.18
  44.8 2.2 %collective-permute-start.9 = (bf16[128,640]{1,0:T(8,128)(2,1)S(1)}, bf16[128,640]{1,0:T(8,128)(2,1)S(1)}, u32[]{:S(2)}, u32[]{:S(2)}) collective-permute-start(bf16[128,640]{1,0:T(8,128)(2,1)S(1)} %pack.18), channel_id=1, source_target_pairs={{0,28},{4,24},{8,20},{12,16},{16,12},{20,8},{24,4},{28,0},{1,29},{... | collective-permute-start | bytes 491528 | tf_op jit(solution)/shard_map/ppermute | solution.py:442
  47.0 0.4 pack.12
  47.4 2.2 %collective-permute-start.2 = (bf16[128,640]{1,0:T(8,128)(2,1)S(1)}, bf16[128,640]{1,0:T(8,128)(2,1)S(1)}, u32[]{:S(2)}, u32[]{:S(2)}) collective-permute-start(bf16[128,640]{1,0:T(8,128)(2,1)S(1)} %pack.12), channel_id=1, source_target_pairs={{0,24},{4,28},{8,16},{12,20},{16,8},{20,12},{24,0},{28,4},{1,25},{... | collective-permute-start | bytes 491528 | tf_op jit(solution)/shard_map/ppermute | solution.py:442
  49.6 3.6 %collective-permute-done.11.refs_0_.refs_1_ = bf16[128,640]{1,0:T(8,128)(2,1)S(1)} collective-permute-done((bf16[128,640]{1,0:T(8,128)(2,1)S(1)}, bf16[128,640]{1,0:T(8,128)(2,1)S(1)}, u32[]{:S(2)}, u32[]{:S(2)}) %collective-permute-start.11) | collective-permute-done | bytes 163872 | tf_op jit(solution)/shard_map/ppermute | solution.py:442
  53.2 5.1 %collective-permute-done.12.refs_1_.refs_3_ = bf16[128,640]{1,0:T(8,128)(2,1)S(1)} collective-permute-done((bf16[128,640]{1,0:T(8,128)(2,1)S(1)}, bf16[128,640]{1,0:T(8,128)(2,1)S(1)}, u32[]{:S(2)}, u32[]{:S(2)}) %collective-permute-start.12) | collective-permute-done | bytes 163872 | tf_op jit(solution)/shard_map/ppermute | solution.py:442
  58.3 1.1 %pack.23 = bf16[128,640]{1,0:T(8,128)(2,1)} custom-call(s32[1]{0:T(128)} %bitcast.me_ref, s32[1]{0:T(128)} %bitcast.1.model_ref, bf16[1,128,12288]{2,1,0:T(8,128)(2,1)S(1)} %copy-done, bf16[2,64,4096]{2,1,0:T(8,128)(2,1)S(1)} %bitcast.16, bf16[128,640]{1,0:T(8,128)(2,1)S(1)} %collective-permute-done.11.refs_0_.refs_1_, ...), custom_call_target="tpu_custom_call" | custom-call | bytes 327680 | tf_op jit(solution)/shard_map/pack/pallas_call | solution.py:67
  59.5 0.8 pack.13.refs_0_
  60.3 5.7 %attend_split.1 = (f32[4,4,64,256]{3,2,1,0:T(8,128)S(1)}, f32[4,2,8,256]{3,2,1,0:T(8,128)S(1)}) custom-call(s32[4]{0:T(128)S(1)} %copy-done.11, s32[1]{0:T(128)} %bitcast.me_ref, bf16[128,1280]{1,0:T(8,128)(2,1)S(1)} %pack.13.refs_0_, bf16[128,1280]{1,0:T(8,128)(2,1)S(1)} %collective-permute-done.4.refs_0_.refs_1_, ...), custom_call_target="tpu_custom_call" | custom-call | tf_op jit(solution)/shard_map/attend_split/pallas_call | solution.py:330
  66.0 1.1 %pack.19 = bf16[128,640]{1,0:T(8,128)(2,1)} custom-call(s32[1]{0:T(128)} %bitcast.me_ref, s32[1]{0:T(128)} %bitcast.1.model_ref, bf16[1,128,12288]{2,1,0:T(8,128)(2,1)S(1)} %copy-done.1, bf16[2,64,4096]{2,1,0:T(8,128)(2,1)S(1)} %bitcast.18, bf16[128,640]{1,0:T(8,128)(2,1)S(1)} %collective-permute-done.9.refs_0_.refs_5_, ...), custom_call_target="tpu_custom_call" | custom-call | bytes 327680 | tf_op jit(solution)/shard_map/pack/pallas_call | solution.py:67
  67.2 1.1 %pack.17 = bf16[128,640]{1,0:T(8,128)(2,1)} custom-call(s32[1]{0:T(128)} %bitcast.me_ref, s32[1]{0:T(128)} %bitcast.1.model_ref, bf16[1,128,12288]{2,1,0:T(8,128)(2,1)S(1)} %copy-done.1, bf16[2,64,4096]{2,1,0:T(8,128)(2,1)S(1)} %bitcast.19, bf16[128,640]{1,0:T(8,128)(2,1)S(1)} %collective-permute-done.2.refs_0_.refs_4_, ...), custom_call_target="tpu_custom_call" | custom-call | bytes 327680 | tf_op jit(solution)/shard_map/pack/pallas_call | solution.py:67
  68.4 2.3 %collective-permute-start.8 = (bf16[128,640]{1,0:T(8,128)(2,1)}, bf16[128,640]{1,0:T(8,128)(2,1)}, u32[]{:S(2)}, u32[]{:S(2)}) collective-permute-start(bf16[128,640]{1,0:T(8,128)(2,1)} %pack.17), channel_id=1, source_target_pairs={{0,16},{4,20},{8,24},{12,28},{16,0},{20,4},{24,8},{28,12},{1,17},{... | collective-permute-start | bytes 491528 | tf_op jit(solution)/shard_map/ppermute | solution.py:442
  70.7 0.7 collective-permute-start.14
  71.4 1.2 %copy-done.4 = bf16[2,4096,64]{1,2,0:T(8,128)(2,1)S(1)} copy-done((bf16[2,4096,64]{1,2,0:T(8,128)(2,1)S(1)}, bf16[2,4096,64]{1,2,0:T(8,128)(2,1)}, u32[]{:S(2)}) %copy-start.4) | copy-done | bytes 1048600
  72.6 0.4 pack.20.refs_0_
  73.0 8.4 %collective-permute-done.14.other_ref = f32[4,2,8,256]{3,2,1,0:T(8,128)} collective-permute-done((f32[4,2,8,256]{3,2,1,0:T(8,128)S(1)}, f32[4,2,8,256]{3,2,1,0:T(8,128)}, u32[]{:S(2)}, u32[]{:S(2)}) %collective-permute-start.14) | collective-permute-done | bytes 65568 | tf_op jit(solution)/shard_map/ppermute | solution.py:442
  81.4 0.9 combine.1.refs_7_
  82.4 4.3 %attend_early.1 = (f32[3,2,64,256]{3,2,1,0:T(8,128)S(1)}, f32[3,2,8,256]{3,2,1,0:T(8,128)S(1)}, f32[8,128]{1,0:T(8,128)S(1)}, bf16[6,128,640]{2,1,0:T(8,128)(2,1)S(1)}, bf16[2,80,768]{2,1,0:T(8,128)(2,1)S(1)}) custom-call(s32[4]{0:T(128)S(1)} %copy-done.11, s32[1]{0:T(128)} %bitcast.me_ref, s32[2]{0:T(128)S(1)} %copy-done.13, f32[1000]{0:T(1024)S(1)} %copy-done.12, ...), custom_call_target="tpu_custom_call" | custom-call | flops 452984832 | bytes 1179648 | tf_op jit(solution)/shard_map/attend_early/pallas_call | solution.py:389
  86.7 3.2 %attend_late.1 = (f32[2,64,128]{2,1,0:T(8,128)S(1)}, bf16[2,64,128]{2,1,0:T(8,128)(2,1)S(1)}, bf16[2,64,128]{2,1,0:T(8,128)(2,1)S(1)}, bf16[2,64,128]{2,1,0:T(8,128)(2,1)S(1)}) custom-call(s32[4]{0:T(128)S(1)} %copy-done.11, s32[1]{0:T(128)} %bitcast.me_ref, bf16[128,640]{1,0:T(8,128)(2,1)} %collective-permute-done.8.refs_0_, ...), custom_call_target="tpu_custom_call" | custom-call | flops 201326592 | bytes 1572864 | tf_op jit(solution)/shard_map/attend_late/pallas_call | solution.py:418
  89.9 1.7 %collective-permute-start.15 = (bf16[2,64,128]{2,1,0:T(8,128)(2,1)S(1)}, bf16[2,64,128]{2,1,0:T(8,128)(2,1)S(1)}, u32[]{:S(2)}, u32[]{:S(2)}) collective-permute-start(bf16[2,64,128]{2,1,0:T(8,128)(2,1)S(1)} %get-tuple-element.24), channel_id=1, source_target_pairs={{0,24},{4,28},{8,16},{12,20},{16,8},{20,12},{24,0},{28,4},{1,25},{... | collective-permute-start | bytes 98312 | tf_op jit(solution)/shard_map/ppermute | solution.py:442
  91.6 2.8 %collective-permute-start.17 = (bf16[2,64,128]{2,1,0:T(8,128)(2,1)S(1)}, bf16[2,64,128]{2,1,0:T(8,128)(2,1)S(1)}, u32[]{:S(2)}, u32[]{:S(2)}) collective-permute-start(bf16[2,64,128]{2,1,0:T(8,128)(2,1)S(1)} %get-tuple-element.26), channel_id=1, source_target_pairs={{0,8},{4,12},{8,0},{12,4},{16,24},{20,28},{24,16},{28,20},{1,9},{5... | collective-permute-start | bytes 98312 | tf_op jit(solution)/shard_map/ppermute | solution.py:442
  94.4 1.3 %collective-permute-done.15 = bf16[2,64,128]{2,1,0:T(8,128)(2,1)S(1)} collective-permute-done((bf16[2,64,128]{2,1,0:T(8,128)(2,1)S(1)}, bf16[2,64,128]{2,1,0:T(8,128)(2,1)S(1)}, u32[]{:S(2)}, u32[]{:S(2)}) %collective-permute-start.15) | collective-permute-done | bytes 32800 | tf_op jit(solution)/shard_map/ppermute | solution.py:442
  95.7 0.8 collective-permute-done.16
  96.5 0.1 collective-permute-done.17
  96.7 0.6 collective-permute-start.18
  97.2 3.4 %collective-permute-done.18 = f32[1,64,128]{2,1,0:T(8,128)S(1)} collective-permute-done((f32[1,64,128]{2,1,0:T(8,128)S(1)}, f32[1,64,128]{2,1,0:T(8,128)S(1)}, u32[]{:S(2)}, u32[]{:S(2)}) %collective-permute-start.18) | collective-permute-done | bytes 32800 | tf_op jit(solution)/shard_map/ppermute | solution.py:442
  100.7 1.6 %collective-permute-start.20 = (f32[64,128]{1,0:T(8,128)S(1)}, f32[64,128]{1,0:T(8,128)S(1)}, u32[]{:S(2)}, u32[]{:S(2)}) collective-permute-start(f32[64,128]{1,0:T(8,128)S(1)} %fusion), channel_id=1, source_target_pairs={{0,2},{1,3},{2,0},{3,1},{4,6},{5,7},{6,4},{7,5},{8,10},{9,11},{10,... | collective-permute-start | bytes 98312 | tf_op jit(solution)/shard_map/ppermute | solution.py:442
  102.3 0.3 collective-permute-start.21
  102.5 1.8 %collective-permute-done.19 = f32[64,128]{1,0:T(8,128)S(1)} collective-permute-done((f32[64,128]{1,0:T(8,128)S(1)}, f32[64,128]{1,0:T(8,128)S(1)}, u32[]{:S(2)}, u32[]{:S(2)}) %collective-permute-start.19) | collective-permute-done | bytes 32800 | tf_op jit(solution)/shard_map/ppermute | solution.py:442
  104.3 0.4 collective-permute-done.20
  104.7 0.6 add_bitcast_fusion
  (48 shorter events, 0.6 us)
Async XLA Ops:
  0.0 1.9 %copy-start = (bf16[1,128,12288]{2,1,0:T(8,128)(2,1)S(1)}, bf16[1,128,12288]{2,1,0:T(8,128)(2,1)}, u32[]{:S(2)}) copy-start(bf16[1,128,12288]{2,1,0:T(8,128)(2,1)} %qkv_ref.31) | copy-start | bytes 9437188
  1.9 1.2 %copy-start.2 = (bf16[2,4096,64]{1,2,0:T(8,128)(2,1)S(1)}, bf16[2,4096,64]{1,2,0:T(8,128)(2,1)}, u32[]{:S(2)}) copy-start(bf16[2,4096,64]{1,2,0:T(8,128)(2,1)} %param.6) | copy-start | bytes 3145732
  3.9 23.1 %collective-permute-start.4 = (bf16[128,1280]{1,0:T(8,128)(2,1)S(1)}, bf16[128,1280]{1,0:T(8,128)(2,1)S(1)}, u32[]{:S(2)}, u32[]{:S(2)}) collective-permute-start(bf16[128,1280]{1,0:T(8,128)(2,1)S(1)} %pack.14), channel_id=1, source_target_pairs={{0,4},{4,0},{8,12},{12,8},{16,20},{20,16},{24,28},{28,24},{1,5},{5... | collective-permute-start | bytes 983048 | tf_op jit(solution)/shard_map/ppermute | solution.py:442
  7.7 19.3 %copy-start.3 = (bf16[2,4096,64]{1,2,0:T(8,128)(2,1)S(1)}, bf16[2,4096,64]{1,2,0:T(8,128)(2,1)}, u32[]{:S(2)}) copy-start(bf16[2,4096,64]{1,2,0:T(8,128)(2,1)} %param.6) | copy-start | bytes 3145732
  7.8 19.2 %collective-permute-start.5 = (bf16[128,1280]{1,0:T(8,128)(2,1)S(1)}, bf16[128,1280]{1,0:T(8,128)(2,1)S(1)}, u32[]{:S(2)}, u32[]{:S(2)}) collective-permute-start(bf16[128,1280]{1,0:T(8,128)(2,1)S(1)} %pack.15), channel_id=1, source_target_pairs={{0,12},{4,8},{8,4},{12,0},{16,28},{20,24},{24,20},{28,16},{1,13},{... | collective-permute-start | bytes 983048 | tf_op jit(solution)/shard_map/ppermute | solution.py:442
  9.5 17.5 %collective-permute-start.3 = (bf16[128,512]{1,0:T(8,128)(2,1)S(1)}, bf16[128,512]{1,0:T(8,128)(2,1)S(1)}, u32[]{:S(2)}, u32[]{:S(2)}) collective-permute-start(bf16[128,512]{1,0:T(8,128)(2,1)S(1)} %pack_queries.6), channel_id=1, source_target_pairs={{0,28},{4,24},{8,20},{12,16},{16,12},{20,8},{24,4},{28,0},{1,29},{... | collective-permute-start | bytes 393224 | tf_op jit(solution)/shard_map/ppermute | solution.py:442
  13.0 14.0 %collective-permute-start = (bf16[128,512]{1,0:T(8,128)(2,1)S(1)}, bf16[128,512]{1,0:T(8,128)(2,1)S(1)}, u32[]{:S(2)}, u32[]{:S(2)}) collective-permute-start(bf16[128,512]{1,0:T(8,128)(2,1)S(1)} %pack_queries.4), channel_id=1, source_target_pairs={{0,24},{4,28},{8,16},{12,20},{16,8},{20,12},{24,0},{28,4},{1,25},{... | collective-permute-start | bytes 393224 | tf_op jit(solution)/shard_map/ppermute | solution.py:442
  27.8 13.0 %collective-permute-start.6 = (bf16[128,1280]{1,0:T(8,128)(2,1)S(1)}, bf16[128,1280]{1,0:T(8,128)(2,1)S(1)}, u32[]{:S(2)}, u32[]{:S(2)}) collective-permute-start(bf16[128,1280]{1,0:T(8,128)(2,1)S(1)} %pack.16), channel_id=1, source_target_pairs={{0,8},{4,12},{8,0},{12,4},{16,24},{20,28},{24,16},{28,20},{1,9},{5... | collective-permute-start | bytes 983048 | tf_op jit(solution)/shard_map/ppermute | solution.py:442
  28.0 16.4 %collective-permute-start.7 = (bf16[128,512]{1,0:T(8,128)(2,1)S(1)}, bf16[128,512]{1,0:T(8,128)(2,1)S(1)}, u32[]{:S(2)}, u32[]{:S(2)}) collective-permute-start(bf16[128,512]{1,0:T(8,128)(2,1)S(1)} %pack_queries.7), channel_id=1, source_target_pairs={{0,20},{4,16},{8,28},{12,24},{16,4},{20,0},{24,12},{28,8},{1,21},{... | collective-permute-start | bytes 393224 | tf_op jit(solution)/shard_map/ppermute | solution.py:442
  31.4 15.6 %collective-permute-start.1 = (bf16[128,512]{1,0:T(8,128)(2,1)S(1)}, bf16[128,512]{1,0:T(8,128)(2,1)S(1)}, u32[]{:S(2)}, u32[]{:S(2)}) collective-permute-start(bf16[128,512]{1,0:T(8,128)(2,1)S(1)} %pack_queries.5), channel_id=1, source_target_pairs={{0,16},{4,20},{8,24},{12,28},{16,0},{20,4},{24,8},{28,12},{1,17},{... | collective-permute-start | bytes 393224 | tf_op jit(solution)/shard_map/ppermute | solution.py:442
  41.2 12.0 %collective-permute-start.11 = (bf16[128,640]{1,0:T(8,128)(2,1)S(1)}, bf16[128,640]{1,0:T(8,128)(2,1)S(1)}, u32[]{:S(2)}, u32[]{:S(2)}) collective-permute-start(bf16[128,640]{1,0:T(8,128)(2,1)S(1)} %pack.21), channel_id=1, source_target_pairs={{0,4},{4,0},{8,12},{12,8},{16,20},{20,16},{24,28},{28,24},{1,5},{5... | collective-permute-start | bytes 491528 | tf_op jit(solution)/shard_map/ppermute | solution.py:442
  44.3 14.0 %collective-permute-start.12 = (bf16[128,640]{1,0:T(8,128)(2,1)S(1)}, bf16[128,640]{1,0:T(8,128)(2,1)S(1)}, u32[]{:S(2)}, u32[]{:S(2)}) collective-permute-start(bf16[128,640]{1,0:T(8,128)(2,1)S(1)} %pack.22), channel_id=1, source_target_pairs={{0,12},{4,8},{8,4},{12,0},{16,28},{20,24},{24,20},{28,16},{1,13},{... | collective-permute-start | bytes 491528 | tf_op jit(solution)/shard_map/ppermute | solution.py:442
  44.8 21.2 %collective-permute-start.9 = (bf16[128,640]{1,0:T(8,128)(2,1)S(1)}, bf16[128,640]{1,0:T(8,128)(2,1)S(1)}, u32[]{:S(2)}, u32[]{:S(2)}) collective-permute-start(bf16[128,640]{1,0:T(8,128)(2,1)S(1)} %pack.18), channel_id=1, source_target_pairs={{0,28},{4,24},{8,20},{12,16},{16,12},{20,8},{24,4},{28,0},{1,29},{... | collective-permute-start | bytes 491528 | tf_op jit(solution)/shard_map/ppermute | solution.py:442
  47.4 19.8 %collective-permute-start.2 = (bf16[128,640]{1,0:T(8,128)(2,1)S(1)}, bf16[128,640]{1,0:T(8,128)(2,1)S(1)}, u32[]{:S(2)}, u32[]{:S(2)}) collective-permute-start(bf16[128,640]{1,0:T(8,128)(2,1)S(1)} %pack.12), channel_id=1, source_target_pairs={{0,24},{4,28},{8,16},{12,20},{16,8},{20,12},{24,0},{28,4},{1,25},{... | collective-permute-start | bytes 491528 | tf_op jit(solution)/shard_map/ppermute | solution.py:442
  58.3 2.0 %copy-start.7 = (bf16[128,640]{1,0:T(8,128)(2,1)}, bf16[128,640]{1,0:T(8,128)(2,1)S(1)}, u32[]{:S(2)}) copy-start(bf16[128,640]{1,0:T(8,128)(2,1)S(1)} %collective-permute-done.12.refs_1_.refs_3_) | copy-start | bytes 491524
  59.4 0.9 copy-start.11
  59.4 6.6 %copy-start.1 = (bf16[1,128,12288]{2,1,0:T(8,128)(2,1)S(1)}, bf16[1,128,12288]{2,1,0:T(8,128)(2,1)}, u32[]{:S(2)}) copy-start(bf16[1,128,12288]{2,1,0:T(8,128)(2,1)} %qkv_ref.31) | copy-start | bytes 9437188
  59.4 22.9 %collective-permute-start.13 = (bf16[128,640]{1,0:T(8,128)(2,1)}, bf16[128,640]{1,0:T(8,128)(2,1)}, u32[]{:S(2)}, u32[]{:S(2)}) collective-permute-start(bf16[128,640]{1,0:T(8,128)(2,1)} %pack.23), channel_id=1, source_target_pairs={{0,8},{4,12},{8,0},{12,4},{16,24},{20,28},{24,16},{28,20},{1,9},{5... | collective-permute-start | bytes 491528 | tf_op jit(solution)/shard_map/ppermute | solution.py:442
  66.0 2.3 %copy-start.5 = (f32[4,4,64,256]{3,2,1,0:T(8,128)}, f32[4,4,64,256]{3,2,1,0:T(8,128)S(1)}, u32[]{:S(2)}) copy-start(f32[4,4,64,256]{3,2,1,0:T(8,128)S(1)} %get-tuple-element.22.sums_ref) | copy-start | bytes 3145732
  67.1 19.6 %collective-permute-start.10 = (bf16[128,640]{1,0:T(8,128)(2,1)}, bf16[128,640]{1,0:T(8,128)(2,1)}, u32[]{:S(2)}, u32[]{:S(2)}) collective-permute-start(bf16[128,640]{1,0:T(8,128)(2,1)} %pack.19), channel_id=1, source_target_pairs={{0,20},{4,16},{8,28},{12,24},{16,4},{20,0},{24,12},{28,8},{1,21},{... | collective-permute-start | bytes 491528 | tf_op jit(solution)/shard_map/ppermute | solution.py:442
  67.2 3.4 %copy-start.9 = (bf16[128,640]{1,0:T(8,128)(2,1)}, bf16[128,640]{1,0:T(8,128)(2,1)S(1)}, u32[]{:S(2)}) copy-start(bf16[128,640]{1,0:T(8,128)(2,1)S(1)} %collective-permute-done.2.refs_0_.refs_4_) | copy-start | bytes 491524
  68.4 14.0 %copy-start.12 = (f32[1000]{0:T(1024)S(1)}, f32[1000]{0:T(1024)}, u32[]{:S(2)}) copy-start(f32[1000]{0:T(1024)} %step_weight_ref.1) | copy-start | bytes 12004
  68.4 14.0 %copy-start.13 = (s32[2]{0:T(128)S(1)}, s32[2]{0:T(128)}, u32[]{:S(2)}) copy-start(s32[2]{0:T(128)} %timestep_ref.1) | copy-start | bytes 28
  68.4 18.3 %collective-permute-start.8 = (bf16[128,640]{1,0:T(8,128)(2,1)}, bf16[128,640]{1,0:T(8,128)(2,1)}, u32[]{:S(2)}, u32[]{:S(2)}) collective-permute-start(bf16[128,640]{1,0:T(8,128)(2,1)} %pack.17), channel_id=1, source_target_pairs={{0,16},{4,20},{8,24},{12,28},{16,0},{20,4},{24,8},{28,12},{1,17},{... | collective-permute-start | bytes 491528 | tf_op jit(solution)/shard_map/ppermute | solution.py:442
  70.7 10.7 %collective-permute-start.14 = (f32[4,2,8,256]{3,2,1,0:T(8,128)S(1)}, f32[4,2,8,256]{3,2,1,0:T(8,128)}, u32[]{:S(2)}, u32[]{:S(2)}) collective-permute-start(f32[4,2,8,256]{3,2,1,0:T(8,128)S(1)} %get-tuple-element.16.refs_1_.stats_ref), channel_id=1, source_target_pairs={{0,16},{4,20},{8,24},{12,28},{16,0},{20,4},{24,8},{28,12},{1,17},{... | collective-permute-start | bytes 196616 | tf_op jit(solution)/shard_map/ppermute | solution.py:442
  71.4 1.2 %copy-start.4 = (bf16[2,4096,64]{1,2,0:T(8,128)(2,1)S(1)}, bf16[2,4096,64]{1,2,0:T(8,128)(2,1)}, u32[]{:S(2)}) copy-start(bf16[2,4096,64]{1,2,0:T(8,128)(2,1)} %param.6) | copy-start | bytes 3145732
  72.6 8.8 %copy-start.6 = (f32[4,4,64,256]{3,2,1,0:T(8,128)S(1)}, f32[4,4,64,256]{3,2,1,0:T(8,128)}, u32[]{:S(2)}) copy-start(f32[4,4,64,256]{3,2,1,0:T(8,128)} %copy-done.5) | copy-start | bytes 3145732
  72.6 9.8 %copy-start.8 = (bf16[128,640]{1,0:T(8,128)(2,1)S(1)}, bf16[128,640]{1,0:T(8,128)(2,1)}, u32[]{:S(2)}) copy-start(bf16[128,640]{1,0:T(8,128)(2,1)} %copy-done.7) | copy-start | bytes 491524
  72.6 9.8 %copy-start.10 = (bf16[128,640]{1,0:T(8,128)(2,1)S(1)}, bf16[128,640]{1,0:T(8,128)(2,1)}, u32[]{:S(2)}) copy-start(bf16[128,640]{1,0:T(8,128)(2,1)} %copy-done.9) | copy-start | bytes 491524
  89.9 5.8 %collective-permute-start.15 = (bf16[2,64,128]{2,1,0:T(8,128)(2,1)S(1)}, bf16[2,64,128]{2,1,0:T(8,128)(2,1)S(1)}, u32[]{:S(2)}, u32[]{:S(2)}) collective-permute-start(bf16[2,64,128]{2,1,0:T(8,128)(2,1)S(1)} %get-tuple-element.24), channel_id=1, source_target_pairs={{0,24},{4,28},{8,16},{12,20},{16,8},{20,12},{24,0},{28,4},{1,25},{... | collective-permute-start | bytes 98312 | tf_op jit(solution)/shard_map/ppermute | solution.py:442
  91.6 4.9 %collective-permute-start.16 = (bf16[2,64,128]{2,1,0:T(8,128)(2,1)S(1)}, bf16[2,64,128]{2,1,0:T(8,128)(2,1)S(1)}, u32[]{:S(2)}, u32[]{:S(2)}) collective-permute-start(bf16[2,64,128]{2,1,0:T(8,128)(2,1)S(1)} %get-tuple-element.25), channel_id=1, source_target_pairs={{0,16},{4,20},{8,24},{12,28},{16,0},{20,4},{24,8},{28,12},{1,17},{... | collective-permute-start | bytes 98312 | tf_op jit(solution)/shard_map/ppermute | solution.py:442
  91.6 5.0 %collective-permute-start.17 = (bf16[2,64,128]{2,1,0:T(8,128)(2,1)S(1)}, bf16[2,64,128]{2,1,0:T(8,128)(2,1)S(1)}, u32[]{:S(2)}, u32[]{:S(2)}) collective-permute-start(bf16[2,64,128]{2,1,0:T(8,128)(2,1)S(1)} %get-tuple-element.26), channel_id=1, source_target_pairs={{0,8},{4,12},{8,0},{12,4},{16,24},{20,28},{24,16},{28,20},{1,9},{5... | collective-permute-start | bytes 98312 | tf_op jit(solution)/shard_map/ppermute | solution.py:442
  96.7 4.0 %collective-permute-start.18 = (f32[1,64,128]{2,1,0:T(8,128)S(1)}, f32[1,64,128]{2,1,0:T(8,128)S(1)}, u32[]{:S(2)}, u32[]{:S(2)}) collective-permute-start(f32[1,64,128]{2,1,0:T(8,128)S(1)} %slice.9), channel_id=1, source_target_pairs={{0,4},{4,0},{8,12},{12,8},{16,20},{20,16},{24,28},{28,24},{1,5},{5... | collective-permute-start | bytes 98312 | tf_op jit(solution)/shard_map/ppermute | solution.py:442
  100.7 3.6 %collective-permute-start.19 = (f32[64,128]{1,0:T(8,128)S(1)}, f32[64,128]{1,0:T(8,128)S(1)}, u32[]{:S(2)}, u32[]{:S(2)}) collective-permute-start(f32[64,128]{1,0:T(8,128)S(1)} %fusion), channel_id=1, source_target_pairs={{0,3},{1,2},{2,1},{3,0},{4,7},{5,6},{6,5},{7,4},{8,11},{9,10},{10,... | collective-permute-start | bytes 98312 | tf_op jit(solution)/shard_map/ppermute | solution.py:442
  100.7 4.0 %collective-permute-start.20 = (f32[64,128]{1,0:T(8,128)S(1)}, f32[64,128]{1,0:T(8,128)S(1)}, u32[]{:S(2)}, u32[]{:S(2)}) collective-permute-start(f32[64,128]{1,0:T(8,128)S(1)} %fusion), channel_id=1, source_target_pairs={{0,2},{1,3},{2,0},{3,1},{4,6},{5,7},{6,4},{7,5},{8,10},{9,11},{10,... | collective-permute-start | bytes 98312 | tf_op jit(solution)/shard_map/ppermute | solution.py:442
  102.3 2.5 %collective-permute-start.21 = (f32[64,128]{1,0:T(8,128)S(1)}, f32[64,128]{1,0:T(8,128)S(1)}, u32[]{:S(2)}, u32[]{:S(2)}) collective-permute-start(f32[64,128]{1,0:T(8,128)S(1)} %fusion), channel_id=1, source_target_pairs={{0,1},{1,0},{2,3},{3,2},{4,5},{5,4},{6,7},{7,6},{8,9},{9,8},{10,11... | collective-permute-start | bytes 98312 | tf_op jit(solution)/shard_map/ppermute | solution.py:442

commit v16 on v14

--- a/solution.py
+++ b/solution.py
@@ -14,7 +14,7 @@
 NT = (((1,), (1,)), ((), ()))
 LOG2_SCALE = math.log2(math.e) / math.sqrt(HD)
 LOWEST = -1e30
-NEXT_WAVE = 0
+TAKE = 1000000000
 SMALL_VMEM = 24 * 1024 * 1024
 LARGE_VMEM = 60 * 1024 * 1024
 SMEM = pl.BlockSpec(memory_space=pltpu.SMEM)
@@ -60,7 +60,7 @@
         copy.wait()
 
 
-def pack(me, model, qkv, readout_t, k, count, after, wave=False):
+def pack(me, model, qkv, readout_t, k, count, after):
     rows = qkv.shape[1]
     lat = readout_t.shape[1]
     width = count * 2 * HD + -(-count * lat // HD) * HD
@@ -76,7 +76,7 @@
         ],
         compiler_params=pltpu.CompilerParams(vmem_limit_bytes=SMALL_VMEM),
         cost_estimate=pl.CostEstimate(
-            flops=NEXT_WAVE if wave else 0, bytes_accessed=rows * width * 4, transcendentals=0
+            flops=0, bytes_accessed=rows * width * 4, transcendentals=0
         ),
         name="pack",
     )(me, model, qkv, readout_t, *after)
@@ -134,128 +134,138 @@
         folded[i, lat:] = jnp.ones_like(folded[i, lat:])
 
 
-def pairs_of(pieces, i, what):
+def groups_of(count):
+    return [tuple(range(n, min(n + 2, count))) for n in range(0, count, 2)]
+
+
+def read_group(pieces, group, i, what):
     column = (2 * i + what) * HD
-
-    def read(n):
-        return lambda: jnp.concatenate([pieces[n][:, column : column + HD], pieces[n + 1][:, column : column + HD]], axis=0)
-
-    return [read(n) for n in range(0, len(pieces), 2)]
+    parts = [pieces[n][:, column : column + HD] for n in group]
+    return parts[0] if len(parts) == 1 else jnp.concatenate(parts, axis=0)
 
 
 def early_kernel(offsets, frames_ref, me_ref, timestep_ref, step_weight_ref, sign_ref, sample_ref, *refs):
-    count_pieces = len(offsets)
-    arrived = refs[:count_pieces]
-    sums_ref, stats_ref, factor_ref, pieces, folded, asked, sems = refs[-7:]
+    number = len(offsets)
+    arrived = refs[:number]
+    sums_ref, stats_ref, factor_ref, held, folded, asked, sems = refs[-7:]
     me = me_ref[0]
-    rows = pieces.shape[1]
+    rows = held.shape[1]
     lat = sums_ref.shape[2]
     count = folded.shape[0]
-    blocks = count_pieces // 2
-    copies = [pltpu.make_async_copy(arrived[n], pieces.at[n], sems.at[n]) for n in range(count_pieces)]
+    groups = groups_of(number)
+    full = number // 2
+    copies = [pltpu.make_async_copy(arrived[n], held.at[n], sems.at[n]) for n in range(number)]
     for copy in copies:
         copy.start()
     factor_ref[...] = jnp.full(factor_ref.shape, sign_ref[0] * step_weight_ref[timestep_ref[sample_ref[0]]])
     for copy in copies:
         copy.wait()
-    pieces = [pieces.at[n] for n in range(count_pieces)]
+    pieces = [held.at[n] for n in range(number)]
     stage_values(folded, pieces, lat)
     for i in range(count):
-        for b, read in enumerate(pairs_of(pieces, i, 0)):
-            asked[b, i] = read()
-    half = count_pieces // 2 + 1
-
-    def some_blocks(b, carry):
-        q = [2 * b, 2 * b + 1]
-        shifts = mask_rows(frames_ref, me, rows, [jnp.where(n < half, n, n + 2) for n in q], offsets)
+        for b in range(full):
+            asked[b, i] = read_group(pieces, groups[b], i, 0)
+    half = (number + 1) // 2
+
+    def block(b, queries_of, query_offsets):
+        width = rows * len(query_offsets)
+        shifts = mask_rows(frames_ref, me, rows, query_offsets, offsets)
         peaks, totals, units = [], [], []
         for i in range(count):
 
             def finish(summed, total, peak, i=i):
-                sums_ref[b, i] = summed
+                sums_ref[b, i, :, :width] = summed
                 peaks.append(peak)
                 totals.append(total)
 
             tiles = [
-                functools.partial(score_tile, keys, lambda i=i: asked[b, i]) for keys in pairs_of(pieces, i, 1)
+                functools.partial(score_tile, lambda g=g, i=i: read_group(pieces, g, i, 1), lambda i=i: queries_of(i))
+                for g in groups
             ]
-            values = [lambda i=i, t=t: folded[i, :, t * 2 * rows : (t + 1) * 2 * rows] for t in range(blocks)]
+            values = [lambda i=i, g=g: folded[i, :, g[0] * rows : (g[-1] + 1) * rows] for g in groups]
             units.append((tiles, values, shifts, finish))
         run_units(units, lat)
         rest = [jnp.ones_like(peaks[0])] * (stats_ref.shape[2] - count)
-        stats_ref[b, 0] = jnp.concatenate(peaks + rest, axis=0)
-        stats_ref[b, 1] = jnp.concatenate(totals + rest, axis=0)
+        stats_ref[b, 0, :, :width] = jnp.concatenate(peaks + rest, axis=0)
+        stats_ref[b, 1, :, :width] = jnp.concatenate(totals + rest, axis=0)
+
+    def some_blocks(b, carry):
+        q = [2 * b, 2 * b + 1]
+        block(b, lambda i: asked[b, i], [jnp.where(n < half, n, n + 2) for n in q])
         return carry
 
-    lax.fori_loop(0, blocks, some_blocks, 0)
-
-
-def late_kernel(offsets, late, chosen, groups, frames_ref, me_ref, *refs):
+    lax.fori_loop(0, full, some_blocks, 0)
+    block(full, lambda i: read_group(pieces, groups[full], i, 0), offsets[2 * full :])
+
+
+def late_kernel(offsets, late, frames_ref, me_ref, late_ref, *refs):
     early = len(offsets)
-    arrived = refs[:2]
-    sums_ref, stats_ref, factor_ref, early_ref, early_folded, *out_refs, late_pieces, folded, sems = refs[2:]
-    copies = [pltpu.make_async_copy(arrived[n], late_pieces.at[n], sems.at[n]) for n in range(2)]
-    for copy in copies:
-        copy.start()
+    sums_ref, stats_ref, factor_ref, early_ref, early_folded, *out_refs, late_piece, folded, sem = refs
+    copy = pltpu.make_async_copy(late_ref, late_piece, sem)
+    copy.start()
     me = me_ref[0]
     size, lat, rows = out_refs[0].shape
     count = folded.shape[0]
-    for copy in copies:
-        copy.wait()
-    pieces = [early_ref.at[n] for n in range(early)] + [late_pieces.at[n] for n in range(2)]
+    copy.wait()
+    pieces = [early_ref.at[n] for n in range(early)] + [late_piece]
     stage_values(folded, pieces[early:], lat)
     factor = factor_ref[:1]
-    every = list(offsets) + list(late)
+    every = list(offsets) + [late]
+    groups = groups_of(early) + [(early,)]
     results = {}
 
-    def add(b, part):
-        results[b] = part if b not in results else results[b] + part
-
     def write(b):
-        for j in range(2):
-            k = every[2 * b + j]
-            out_ref = out_refs[groups.index(k // size)]
+        for j, n in enumerate(groups[b]):
+            k = every[n]
+            out_ref = out_refs[k // size]
             out_ref[k % size] = (results[b][:, j * rows : (j + 1) * rows] * factor).astype(out_ref.dtype)
 
+    def value_tile(i, g):
+        return folded[i] if g[0] == early else early_folded[i, :, g[0] * rows : (g[-1] + 1) * rows]
+
     units = []
-    blocks = early // 2
-    for b in chosen:
-        keys_in = range(blocks + 1) if b == blocks else [blocks]
-        key_offsets = [every[2 * t + j] for t in keys_in for j in range(2)]
-        shifts = mask_rows(frames_ref, me, rows, every[2 * b : 2 * b + 2], key_offsets)
+    last = len(groups) - 1
+    for b in [last] + list(range(last)):
+        key_groups = groups if b == last else groups[last:]
+        key_offsets = [every[n] for g in key_groups for n in g]
+        width = rows * len(groups[b])
+        shifts = mask_rows(frames_ref, me, rows, [every[n] for n in groups[b]], key_offsets)
         for i in range(count):
 
-            def finish(summed, total, peak, b=b, i=i):
-                if b < blocks:
-                    before = stats_ref[b, 0, i : i + 1]
+            def finish(summed, total, peak, b=b, i=i, width=width):
+                if b < last:
+                    before = stats_ref[b, 0, i : i + 1, :width]
                     highest = jnp.maximum(before, peak)
                     old = jnp.exp2((before - highest) * LOG2_SCALE)
                     new = jnp.exp2((peak - highest) * LOG2_SCALE)
-                    both = stats_ref[b, 1, i : i + 1] * old + total * new
-                    add(b, sums_ref[b, i] * (old / both) + summed * (new / both))
+                    both = stats_ref[b, 1, i : i + 1, :width] * old + total * new
+                    part = sums_ref[b, i, :, :width] * (old / both) + summed * (new / both)
                 else:
-                    add(b, summed / total)
+                    part = summed / total
+                results[b] = part if i == 0 else results[b] + part
                 if i == count - 1:
                     write(b)
 
-            queries = pairs_of(pieces, i, 0)[b]
-            keys = pairs_of(pieces, i, 1)
-            tiles = [functools.partial(score_tile, keys[t], queries) for t in keys_in]
-            values = [
-                lambda i=i, t=t: folded[i] if t == blocks else early_folded[i, :, t * 2 * rows : (t + 1) * 2 * rows]
-                for t in keys_in
+            tiles = [
+                functools.partial(
+                    score_tile,
+                    lambda g=g, i=i: read_group(pieces, g, i, 1),
+                    lambda b=b, i=i: read_group(pieces, groups[b], i, 0),
+                )
+                for g in key_groups
             ]
+            values = [functools.partial(value_tile, i, g) for g in key_groups]
             units.append((tiles, values, shifts, finish))
     run_units(units, lat)
 
 
-def attend_early(pieces, offsets, span_frames, me, timestep, step_weight, sign, sample, count, lat):
+def attend_early(pieces, offsets, taken, span_frames, me, timestep, step_weight, sign, sample, count, lat):
     rows, width = pieces[0].shape
-    blocks = len(pieces) // 2
+    blocks = len(groups_of(len(pieces)))
     tokens = len(pieces) * rows
     return pl.pallas_call(
         functools.partial(early_kernel, offsets),
-        in_specs=[SMEM] * 6 + [HBM] * len(pieces),
+        in_specs=[SMEM] * 6 + [HBM] * (len(pieces) + 1),
         out_specs=[VMEM] * 5,
         out_shape=[
             jax.ShapeDtypeStruct((blocks, count, lat, 2 * rows), jnp.float32),
@@ -265,7 +275,7 @@
             jax.ShapeDtypeStruct((count, lat + 16, tokens), jnp.bfloat16),
         ],
         scratch_shapes=[
-            pltpu.VMEM((blocks, count, 2 * rows, HD), jnp.bfloat16),
+            pltpu.VMEM((len(pieces) // 2, count, 2 * rows, HD), jnp.bfloat16),
             pltpu.SemaphoreType.DMA((len(pieces),)),
         ],
         compiler_params=pltpu.CompilerParams(vmem_limit_bytes=SMALL_VMEM if len(pieces) <= 8 else LARGE_VMEM),
@@ -275,33 +285,49 @@
             transcendentals=count * tokens * tokens,
         ),
         name="attend_early",
-    )(span_frames, me, timestep, step_weight, sign, sample, *pieces)
-
-
-def attend_late(pieces, offsets, late, chosen, groups, early, span_frames, me, count, lat):
-    rows, width = pieces[0].shape
-    half = len(offsets) // 2 + 1
-    tokens = 2 * half * rows
+    )(span_frames, me, timestep, step_weight, sign, sample, *pieces, taken)
+
+
+def attend_late(piece, offsets, late, early, span_frames, me, count, lat):
+    rows, width = piece.shape
+    seq_count = len(offsets) + 1
+    tokens = seq_count * rows
     return pl.pallas_call(
-        functools.partial(late_kernel, offsets, late, chosen, groups),
-        in_specs=[SMEM] * 2 + [HBM] * 2 + [VMEM] * len(early),
-        out_specs=[VMEM] * len(groups),
+        functools.partial(late_kernel, offsets, late),
+        in_specs=[SMEM] * 2 + [HBM] + [VMEM] * len(early),
+        out_specs=[VMEM] * 4,
         out_shape=[
-            jax.ShapeDtypeStruct((half // 2, lat, rows), jnp.bfloat16 if g else jnp.float32) for g in groups
+            jax.ShapeDtypeStruct((seq_count // 4, lat, rows), jnp.bfloat16 if g else jnp.float32) for g in range(4)
         ],
         scratch_shapes=[
-            pltpu.VMEM((2, rows, width), jnp.bfloat16),
-            pltpu.VMEM((count, lat + 16, 2 * rows), jnp.bfloat16),
-            pltpu.SemaphoreType.DMA((2,)),
-        ],
-        compiler_params=pltpu.CompilerParams(vmem_limit_bytes=SMALL_VMEM if half <= 4 else LARGE_VMEM),
+            pltpu.VMEM((rows, width), jnp.bfloat16),
+            pltpu.VMEM((count, lat + 16, rows), jnp.bfloat16),
+            pltpu.SemaphoreType.DMA,
+        ],
+        compiler_params=pltpu.CompilerParams(vmem_limit_bytes=SMALL_VMEM if seq_count <= 8 else LARGE_VMEM),
         cost_estimate=pl.CostEstimate(
             flops=count * tokens * rows * 4 * (HD + lat),
             bytes_accessed=tokens * count * 3 * HD * 2,
             transcendentals=count * tokens * rows * 2,
         ),
         name="attend_late",
-    )(span_frames, me, *pieces, *early)
+    )(span_frames, me, piece, *early)
+
+
+def take_kernel(piece_ref, me_ref, out_ref):
+    out_ref[...] = jnp.full(out_ref.shape, me_ref[0], jnp.int32)
+
+
+def take(piece, me):
+    return pl.pallas_call(
+        take_kernel,
+        in_specs=[HBM, SMEM],
+        out_specs=VMEM,
+        out_shape=jax.ShapeDtypeStruct((8, HD), jnp.int32),
+        compiler_params=pltpu.CompilerParams(vmem_limit_bytes=SMALL_VMEM),
+        cost_estimate=pl.CostEstimate(flops=TAKE, bytes_accessed=0, transcendentals=0),
+        name="take",
+    )(piece, me)
 
 
 def swap(array, axis, offset):
@@ -327,20 +353,17 @@
     pieces = [None] * seq_count
     for n in range(half):
         k = seq_count - 1 - n
-        pieces[k] = swap(pack(me, model, qkv, readout_t, k, count, [pieces[k + 2]] if n > 1 else [], n > 1), "seq", k)
+        packed = pack(me, model, qkv, readout_t, k, count, [pieces[k + 2]] if n > 1 else [])
+        pieces[k] = swap(packed, "seq", k)
     pieces[0] = pack(me, model, qkv, readout_t, 0, count, [pieces[seq_count - 1]])
     for k in [half - 1] + list(range(1, half - 1)):
         after = [pieces[k - 1], pieces[half - 1], pieces[seq_count - 1]] if k not in (1, half - 1) else []
         pieces[k] = swap(pack(me, model, qkv, readout_t, k, count, after), "seq", k)
-    late = [half, half + 1]
-    early = [k for k in range(seq_count) if k not in late]
+    early = [k for k in range(seq_count) if k not in (half, half + 1)] + [half + 1]
     merged = attend_early(
-        [pieces[k] for k in early], early, span_frames, me, timestep, step_weight, sign, sample, count, lat
+        [pieces[k] for k in early], early, take(pieces[half + 1], me), span_frames, me, timestep, step_weight, sign, sample, count, lat
     )
-    blocks = len(early) // 2
-    ends = [pieces[k] for k in late]
-    order = [blocks] + list(range(blocks))
-    given = attend_late(ends, early, late, order, [0, 1, 2, 3], merged, span_frames, me, count, lat)
+    given = attend_late(pieces[half], early, half, merged, span_frames, me, count, lat)
     size = half // 2
     while True:
         keep = given[0]

time: 89.7 us -> 91.7 us (1.022)
  starting transfers between devices: 22.6 us -> 42.9 us
  waiting for transfers between devices: 41.7 us -> 22 us
  Pallas kernels: 19.1 us -> 21.2 us
    ppermute x14, starting transfers between devices: 22.6 us -> 42.9 us  [swap(): return lax.ppermute(array, axis, [(i, i ^ offset) for i in range(size)])]
    ppermute x14, waiting for transfers between devices: 41.7 us -> 22 us  [swap(): return lax.ppermute(array, axis, [(i, i ^ offset) for i in range(size)])]
    pallas_call x1, Pallas kernels: 5.85 us -> 7.83 us  [attend_early(): pl.pallas_call(functools.partial(early_kernel, offsets), in_specs=[SMEM]...]
    pallas_call x1 -> x2, Pallas kernels: 4.65 us -> 4.73 us  [the longest x1 4.73 us: attend_late(): pl.pallas_call(functools.partial(late_kernel, offsets, late), in_specs=[S...]
  transfers between devices with their start and end apart: 14 -> 14, of which waited for: 10 -> 8; matrix products, arithmetic and copies ran while one was open for 0% -> 0% of each run, Pallas kernels for 15% -> 17%
where the time goes in v16:
time: 91.7 us; the launch traced here: 91.4 us
  starting transfers between devices  42.9 us (47%)
  waiting for transfers between devices  22 us (24%)
  Pallas kernels  21.2 us (23%)
  local copies, waits for them, and re-layouts  4.39 us (5%)
    ppermute x14, starting transfers between devices, swap(): return lax.ppermute(array, axis, [(i, i ^ offset) for i in range(size)])  42.9 us
    ppermute x14, waiting for transfers between devices, swap(): return lax.ppermute(array, axis, [(i, i ^ offset) for i in range(size)])  22 us
    pallas_call x8, Pallas kernels, pack(): pl.pallas_call(functools.partial(pack_kernel, k), in_specs=[SMEM, SMEM] +...  8.66 us
    pallas_call x1, Pallas kernels, attend_early(): pl.pallas_call(functools.partial(early_kernel, offsets), in_specs=[SMEM]...  7.83 us
    pallas_call x1, Pallas kernels, attend_late(): pl.pallas_call(functools.partial(late_kernel, offsets, late), in_specs=[S...  4.73 us
    unnamed x26, local copies, waits for them, and re-layouts  4.38 us
  transfers between devices with their start and end apart: 14, of which 8 were waited for; matrix products, arithmetic and copies ran while one was open for 0% of the time, Pallas kernels for 17%

profile of v16, /device:TPU:0, one launch (start us, length us, event | category | flops | bytes accessed | tf_op | source)
XLA Modules:
  0.0 91.4 jit_solution(5677990856987854020)
XLA Ops:
  0.0 1.9 %copy-done = bf16[1,128,12288]{2,1,0:T(8,128)(2,1)S(1)} copy-done((bf16[1,128,12288]{2,1,0:T(8,128)(2,1)S(1)}, bf16[1,128,12288]{2,1,0:T(8,128)(2,1)}, u32[]{:S(2)}) %copy-start) | copy-done | bytes 3145752
  1.9 1.2 %copy-done.2 = bf16[2,4096,64]{1,2,0:T(8,128)(2,1)S(1)} copy-done((bf16[2,4096,64]{1,2,0:T(8,128)(2,1)S(1)}, bf16[2,4096,64]{1,2,0:T(8,128)(2,1)}, u32[]{:S(2)}) %copy-start.2) | copy-done | bytes 1048600
  3.1 0.8 pack.10
  3.9 6.0 %collective-permute-start.2 = (bf16[128,1280]{1,0:T(8,128)(2,1)S(1)}, bf16[128,1280]{1,0:T(8,128)(2,1)S(1)}, u32[]{:S(2)}, u32[]{:S(2)}) collective-permute-start(bf16[128,1280]{1,0:T(8,128)(2,1)S(1)} %pack.10), channel_id=1, source_target_pairs={{0,28},{4,24},{8,20},{12,16},{16,12},{20,8},{24,4},{28,0},{1,29},{... | collective-permute-start | bytes 983048 | tf_op jit(solution)/shard_map/ppermute | solution.py:335
  10.0 0.8 pack.12
  10.8 0.6 collective-permute-start.3
  11.4 0.8 pack.13
  12.2 0.5 collective-permute-start.4
  12.7 0.8 pack.8
  13.6 1.4 %collective-permute-start = (bf16[128,1280]{1,0:T(8,128)(2,1)S(1)}, bf16[128,1280]{1,0:T(8,128)(2,1)S(1)}, u32[]{:S(2)}, u32[]{:S(2)}) collective-permute-start(bf16[128,1280]{1,0:T(8,128)(2,1)S(1)} %pack.8), channel_id=1, source_target_pairs={{0,24},{4,28},{8,16},{12,20},{16,8},{20,12},{24,0},{28,4},{1,25},{... | collective-permute-start | bytes 983048 | tf_op jit(solution)/shard_map/ppermute | solution.py:335
  15.0 3.6 %collective-permute-done.2.refs_0_.refs_2_.refs_5_ = bf16[128,1280]{1,0:T(8,128)(2,1)S(1)} collective-permute-done((bf16[128,1280]{1,0:T(8,128)(2,1)S(1)}, bf16[128,1280]{1,0:T(8,128)(2,1)S(1)}, u32[]{:S(2)}, u32[]{:S(2)}) %collective-permute-start.2) | collective-permute-done | bytes 327712 | tf_op jit(solution)/shard_map/ppermute | solution.py:335
  18.6 1.5 %pack.15 = bf16[128,1280]{1,0:T(8,128)(2,1)} custom-call(s32[1]{0:T(128)} %bitcast.me_ref, s32[1]{0:T(128)} %bitcast.1.model_ref, bf16[1,128,12288]{2,1,0:T(8,128)(2,1)S(1)} %copy-done, bf16[2,64,4096]{2,1,0:T(8,128)(2,1)S(1)} %bitcast.13, bf16[128,1280]{1,0:T(8,128)(2,1)S(1)} %collective-permute-done.2.refs_0_.refs_2_.refs_5_), custom_call_target="tpu_custom_call" | custom-call | bytes 655360 | tf_op jit(solution)/shard_map/pack/pallas_call | solution.py:67
  20.1 12.4 %collective-permute-start.6 = (bf16[128,1280]{1,0:T(8,128)(2,1)}, bf16[128,1280]{1,0:T(8,128)(2,1)}, u32[]{:S(2)}, u32[]{:S(2)}) collective-permute-start(bf16[128,1280]{1,0:T(8,128)(2,1)} %pack.15), channel_id=1, source_target_pairs={{0,20},{4,16},{8,28},{12,24},{16,4},{20,0},{24,12},{28,8},{1,21},{... | collective-permute-start | bytes 983048 | tf_op jit(solution)/shard_map/ppermute | solution.py:335
  32.6 0.0 collective-permute-done.3.refs_0_.refs_1_
  32.6 0.0 collective-permute-done.4.refs_1_.refs_3_
  32.6 1.6 %pack.14 = bf16[128,1280]{1,0:T(8,128)(2,1)} custom-call(s32[1]{0:T(128)} %bitcast.me_ref, s32[1]{0:T(128)} %bitcast.1.model_ref, bf16[1,128,12288]{2,1,0:T(8,128)(2,1)S(1)} %copy-done, bf16[2,64,4096]{2,1,0:T(8,128)(2,1)S(1)} %bitcast.14, bf16[128,1280]{1,0:T(8,128)(2,1)S(1)} %collective-permute-done.3.refs_0_.refs_1_, ...), custom_call_target="tpu_custom_call" | custom-call | bytes 655360 | tf_op jit(solution)/shard_map/pack/pallas_call | solution.py:67
  34.2 0.0 copy-start.1
  34.2 0.1 collective-permute-start.5
  34.3 2.1 %collective-permute-done.refs_0_.refs_4_ = bf16[128,1280]{1,0:T(8,128)(2,1)S(1)} collective-permute-done((bf16[128,1280]{1,0:T(8,128)(2,1)S(1)}, bf16[128,1280]{1,0:T(8,128)(2,1)S(1)}, u32[]{:S(2)}, u32[]{:S(2)}) %collective-permute-start) | collective-permute-done | bytes 327712 | tf_op jit(solution)/shard_map/ppermute | solution.py:335
  36.4 1.5 %pack.9 = bf16[128,1280]{1,0:T(8,128)(2,1)} custom-call(s32[1]{0:T(128)} %bitcast.me_ref, s32[1]{0:T(128)} %bitcast.1.model_ref, bf16[1,128,12288]{2,1,0:T(8,128)(2,1)S(1)} %copy-done, bf16[2,64,4096]{2,1,0:T(8,128)(2,1)S(1)} %bitcast.15, bf16[128,1280]{1,0:T(8,128)(2,1)S(1)} %collective-permute-done.refs_0_.refs_4_), custom_call_target="tpu_custom_call" | custom-call | bytes 655360 | tf_op jit(solution)/shard_map/pack/pallas_call | solution.py:67
  38.0 13.8 %collective-permute-start.1 = (bf16[128,1280]{1,0:T(8,128)(2,1)}, bf16[128,1280]{1,0:T(8,128)(2,1)}, u32[]{:S(2)}, u32[]{:S(2)}) collective-permute-start(bf16[128,1280]{1,0:T(8,128)(2,1)} %pack.9), channel_id=1, source_target_pairs={{0,16},{4,20},{8,24},{12,28},{16,0},{20,4},{24,8},{28,12},{1,17},{... | collective-permute-start | bytes 983048 | tf_op jit(solution)/shard_map/ppermute | solution.py:335
  51.8 1.2 %copy-done.3 = bf16[2,4096,64]{1,2,0:T(8,128)(2,1)S(1)} copy-done((bf16[2,4096,64]{1,2,0:T(8,128)(2,1)S(1)}, bf16[2,4096,64]{1,2,0:T(8,128)(2,1)}, u32[]{:S(2)}) %copy-start.3) | copy-done | bytes 1048600
  53.1 0.0 copy-start.11
  53.1 0.0 copy-start.12
  53.1 0.8 pack.11.refs_0_
  53.9 9.1 %collective-permute-done.6.piece_ref.refs_6_ = bf16[128,1280]{1,0:T(8,128)(2,1)} collective-permute-done((bf16[128,1280]{1,0:T(8,128)(2,1)}, bf16[128,1280]{1,0:T(8,128)(2,1)}, u32[]{:S(2)}, u32[]{:S(2)}) %collective-permute-start.6) | collective-permute-done | bytes 327712 | tf_op jit(solution)/shard_map/ppermute | solution.py:335
  63.1 0.0 collective-permute-done.5.refs_2_
  63.1 0.0 copy-done.7
  63.1 0.0 copy-done.9
  63.1 0.0 copy-done.10
  63.1 7.8 %attend_early.1 = (f32[4,4,64,256]{3,2,1,0:T(8,128)S(1)}, f32[4,2,8,256]{3,2,1,0:T(8,128)S(1)}, f32[8,128]{1,0:T(8,128)S(1)}, bf16[7,128,1280]{2,1,0:T(8,128)(2,1)S(1)}, bf16[4,80,896]{2,1,0:T(8,128)(2,1)S(1)}) custom-call(s32[4]{0:T(128)S(1)} %copy-done.10, s32[1]{0:T(128)} %bitcast.me_ref, s32[2]{0:T(128)S(1)} %copy-done.12, f32[1000]{0:T(1024)S(1)} %copy-done.11, ...), custom_call_target="tpu_custom_call" | custom-call | flops 1233125376 | bytes 2752512 | tf_op jit(solution)/shard_map/attend_early/pallas_call | solution.py:266
  71.0 0.0 collective-permute-done.1.late_ref
  71.0 4.7 %attend_late.1 = (f32[2,64,128]{2,1,0:T(8,128)S(1)}, bf16[2,64,128]{2,1,0:T(8,128)(2,1)S(1)}, bf16[2,64,128]{2,1,0:T(8,128)(2,1)S(1)}, bf16[2,64,128]{2,1,0:T(8,128)(2,1)S(1)}) custom-call(s32[4]{0:T(128)S(1)} %copy-done.10, s32[1]{0:T(128)} %bitcast.me_ref, bf16[128,1280]{1,0:T(8,128)(2,1)} %collective-permute-done.1.late_ref, ...), custom_call_target="tpu_custom_call" | custom-call | flops 402653184 | bytes 3145728 | tf_op jit(solution)/shard_map/attend_late/pallas_call | solution.py:295
  75.7 2.2 %collective-permute-start.7 = (bf16[2,64,128]{2,1,0:T(8,128)(2,1)S(1)}, bf16[2,64,128]{2,1,0:T(8,128)(2,1)S(1)}, u32[]{:S(2)}, u32[]{:S(2)}) collective-permute-start(bf16[2,64,128]{2,1,0:T(8,128)(2,1)S(1)} %get-tuple-element.20), channel_id=1, source_target_pairs={{0,24},{4,28},{8,16},{12,20},{16,8},{20,12},{24,0},{28,4},{1,25},{... | collective-permute-start | bytes 98312 | tf_op jit(solution)/shard_map/ppermute | solution.py:335
  77.9 0.0 collective-permute-start.8
  77.9 2.3 %collective-permute-start.9 = (bf16[2,64,128]{2,1,0:T(8,128)(2,1)S(1)}, bf16[2,64,128]{2,1,0:T(8,128)(2,1)S(1)}, u32[]{:S(2)}, u32[]{:S(2)}) collective-permute-start(bf16[2,64,128]{2,1,0:T(8,128)(2,1)S(1)} %get-tuple-element.22), channel_id=1, source_target_pairs={{0,8},{4,12},{8,0},{12,4},{16,24},{20,28},{24,16},{28,20},{1,9},{5... | collective-permute-start | bytes 98312 | tf_op jit(solution)/shard_map/ppermute | solution.py:335
  80.2 1.3 %collective-permute-done.7 = bf16[2,64,128]{2,1,0:T(8,128)(2,1)S(1)} collective-permute-done((bf16[2,64,128]{2,1,0:T(8,128)(2,1)S(1)}, bf16[2,64,128]{2,1,0:T(8,128)(2,1)S(1)}, u32[]{:S(2)}, u32[]{:S(2)}) %collective-permute-start.7) | collective-permute-done | bytes 32800 | tf_op jit(solution)/shard_map/ppermute | solution.py:335
  81.5 1.2 %collective-permute-done.8 = bf16[2,64,128]{2,1,0:T(8,128)(2,1)S(1)} collective-permute-done((bf16[2,64,128]{2,1,0:T(8,128)(2,1)S(1)}, bf16[2,64,128]{2,1,0:T(8,128)(2,1)S(1)}, u32[]{:S(2)}, u32[]{:S(2)}) %collective-permute-start.8) | collective-permute-done | bytes 32800 | tf_op jit(solution)/shard_map/ppermute | solution.py:335
  82.7 0.0 collective-permute-done.9
  82.7 1.6 %collective-permute-start.10 = (f32[1,64,128]{2,1,0:T(8,128)S(1)}, f32[1,64,128]{2,1,0:T(8,128)S(1)}, u32[]{:S(2)}, u32[]{:S(2)}) collective-permute-start(f32[1,64,128]{2,1,0:T(8,128)S(1)} %slice.9), channel_id=1, source_target_pairs={{0,4},{4,0},{8,12},{12,8},{16,20},{20,16},{24,28},{28,24},{1,5},{5... | collective-permute-start | bytes 98312 | tf_op jit(solution)/shard_map/ppermute | solution.py:335
  84.3 2.3 %collective-permute-done.10 = f32[1,64,128]{2,1,0:T(8,128)S(1)} collective-permute-done((f32[1,64,128]{2,1,0:T(8,128)S(1)}, f32[1,64,128]{2,1,0:T(8,128)S(1)}, u32[]{:S(2)}, u32[]{:S(2)}) %collective-permute-start.10) | collective-permute-done | bytes 32800 | tf_op jit(solution)/shard_map/ppermute | solution.py:335
  86.7 0.0 collective-permute-start.11
  86.7 1.6 %collective-permute-start.12 = (f32[64,128]{1,0:T(8,128)S(1)}, f32[64,128]{1,0:T(8,128)S(1)}, u32[]{:S(2)}, u32[]{:S(2)}) collective-permute-start(f32[64,128]{1,0:T(8,128)S(1)} %fusion), channel_id=1, source_target_pairs={{0,2},{1,3},{2,0},{3,1},{4,6},{5,7},{6,4},{7,5},{8,10},{9,11},{10,... | collective-permute-start | bytes 98312 | tf_op jit(solution)/shard_map/ppermute | solution.py:335
  88.3 0.3 collective-permute-start.13
  88.6 1.7 %collective-permute-done.11 = f32[64,128]{1,0:T(8,128)S(1)} collective-permute-done((f32[64,128]{1,0:T(8,128)S(1)}, f32[64,128]{1,0:T(8,128)S(1)}, u32[]{:S(2)}, u32[]{:S(2)}) %collective-permute-start.11) | collective-permute-done | bytes 32800 | tf_op jit(solution)/shard_map/ppermute | solution.py:335
  90.3 0.4 collective-permute-done.12
  90.7 0.0 collective-permute-done.13
  90.8 0.6 add_bitcast_fusion
  (21 shorter events, 0.1 us)
Async XLA Ops:
  0.0 1.9 %copy-start = (bf16[1,128,12288]{2,1,0:T(8,128)(2,1)S(1)}, bf16[1,128,12288]{2,1,0:T(8,128)(2,1)}, u32[]{:S(2)}) copy-start(bf16[1,128,12288]{2,1,0:T(8,128)(2,1)} %qkv_ref.15) | copy-start | bytes 9437188
  1.9 1.2 %copy-start.2 = (bf16[2,4096,64]{1,2,0:T(8,128)(2,1)S(1)}, bf16[2,4096,64]{1,2,0:T(8,128)(2,1)}, u32[]{:S(2)}) copy-start(bf16[2,4096,64]{1,2,0:T(8,128)(2,1)} %param.6) | copy-start | bytes 3145732
  3.9 14.7 %collective-permute-start.2 = (bf16[128,1280]{1,0:T(8,128)(2,1)S(1)}, bf16[128,1280]{1,0:T(8,128)(2,1)S(1)}, u32[]{:S(2)}, u32[]{:S(2)}) collective-permute-start(bf16[128,1280]{1,0:T(8,128)(2,1)S(1)} %pack.10), channel_id=1, source_target_pairs={{0,28},{4,24},{8,20},{12,16},{16,12},{20,8},{24,4},{28,0},{1,29},{... | collective-permute-start | bytes 983048 | tf_op jit(solution)/shard_map/ppermute | solution.py:335
  10.8 21.8 %collective-permute-start.3 = (bf16[128,1280]{1,0:T(8,128)(2,1)S(1)}, bf16[128,1280]{1,0:T(8,128)(2,1)S(1)}, u32[]{:S(2)}, u32[]{:S(2)}) collective-permute-start(bf16[128,1280]{1,0:T(8,128)(2,1)S(1)} %pack.12), channel_id=1, source_target_pairs={{0,4},{4,0},{8,12},{12,8},{16,20},{20,16},{24,28},{28,24},{1,5},{5... | collective-permute-start | bytes 983048 | tf_op jit(solution)/shard_map/ppermute | solution.py:335
  12.2 20.4 %collective-permute-start.4 = (bf16[128,1280]{1,0:T(8,128)(2,1)S(1)}, bf16[128,1280]{1,0:T(8,128)(2,1)S(1)}, u32[]{:S(2)}, u32[]{:S(2)}) collective-permute-start(bf16[128,1280]{1,0:T(8,128)(2,1)S(1)} %pack.13), channel_id=1, source_target_pairs={{0,12},{4,8},{8,4},{12,0},{16,28},{20,24},{24,20},{28,16},{1,13},{... | collective-permute-start | bytes 983048 | tf_op jit(solution)/shard_map/ppermute | solution.py:335
  13.6 22.9 %collective-permute-start = (bf16[128,1280]{1,0:T(8,128)(2,1)S(1)}, bf16[128,1280]{1,0:T(8,128)(2,1)S(1)}, u32[]{:S(2)}, u32[]{:S(2)}) collective-permute-start(bf16[128,1280]{1,0:T(8,128)(2,1)S(1)} %pack.8), channel_id=1, source_target_pairs={{0,24},{4,28},{8,16},{12,20},{16,8},{20,12},{24,0},{28,4},{1,25},{... | collective-permute-start | bytes 983048 | tf_op jit(solution)/shard_map/ppermute | solution.py:335
  20.1 42.9 %collective-permute-start.6 = (bf16[128,1280]{1,0:T(8,128)(2,1)}, bf16[128,1280]{1,0:T(8,128)(2,1)}, u32[]{:S(2)}, u32[]{:S(2)}) collective-permute-start(bf16[128,1280]{1,0:T(8,128)(2,1)} %pack.15), channel_id=1, source_target_pairs={{0,20},{4,16},{8,28},{12,24},{16,4},{20,0},{24,12},{28,8},{1,21},{... | collective-permute-start | bytes 983048 | tf_op jit(solution)/shard_map/ppermute | solution.py:335
  32.6 5.4 %copy-start.4 = (bf16[128,1280]{1,0:T(8,128)(2,1)}, bf16[128,1280]{1,0:T(8,128)(2,1)S(1)}, u32[]{:S(2)}) copy-start(bf16[128,1280]{1,0:T(8,128)(2,1)S(1)} %collective-permute-done.3.refs_0_.refs_1_) | copy-start | bytes 983044
  32.6 5.4 %copy-start.6 = (bf16[128,1280]{1,0:T(8,128)(2,1)}, bf16[128,1280]{1,0:T(8,128)(2,1)S(1)}, u32[]{:S(2)}) copy-start(bf16[128,1280]{1,0:T(8,128)(2,1)S(1)} %collective-permute-done.4.refs_1_.refs_3_) | copy-start | bytes 983044
  34.2 17.7 %copy-start.1 = (bf16[1,128,12288]{2,1,0:T(8,128)(2,1)S(1)}, bf16[1,128,12288]{2,1,0:T(8,128)(2,1)}, u32[]{:S(2)}) copy-start(bf16[1,128,12288]{2,1,0:T(8,128)(2,1)} %qkv_ref.15) | copy-start | bytes 9437188
  34.2 28.9 %collective-permute-start.5 = (bf16[128,1280]{1,0:T(8,128)(2,1)}, bf16[128,1280]{1,0:T(8,128)(2,1)}, u32[]{:S(2)}, u32[]{:S(2)}) collective-permute-start(bf16[128,1280]{1,0:T(8,128)(2,1)} %pack.14), channel_id=1, source_target_pairs={{0,8},{4,12},{8,0},{12,4},{16,24},{20,28},{24,16},{28,20},{1,9},{5... | collective-permute-start | bytes 983048 | tf_op jit(solution)/shard_map/ppermute | solution.py:335
  36.4 1.6 %copy-start.8 = (bf16[128,1280]{1,0:T(8,128)(2,1)}, bf16[128,1280]{1,0:T(8,128)(2,1)S(1)}, u32[]{:S(2)}) copy-start(bf16[128,1280]{1,0:T(8,128)(2,1)S(1)} %collective-permute-done.refs_0_.refs_4_) | copy-start | bytes 983044
  38.0 33.0 %collective-permute-start.1 = (bf16[128,1280]{1,0:T(8,128)(2,1)}, bf16[128,1280]{1,0:T(8,128)(2,1)}, u32[]{:S(2)}, u32[]{:S(2)}) collective-permute-start(bf16[128,1280]{1,0:T(8,128)(2,1)} %pack.9), channel_id=1, source_target_pairs={{0,16},{4,20},{8,24},{12,28},{16,0},{20,4},{24,8},{28,12},{1,17},{... | collective-permute-start | bytes 983048 | tf_op jit(solution)/shard_map/ppermute | solution.py:335
  51.8 1.2 %copy-start.3 = (bf16[2,4096,64]{1,2,0:T(8,128)(2,1)S(1)}, bf16[2,4096,64]{1,2,0:T(8,128)(2,1)}, u32[]{:S(2)}) copy-start(bf16[2,4096,64]{1,2,0:T(8,128)(2,1)} %param.6) | copy-start | bytes 3145732
  53.1 10.0 %copy-start.5 = (bf16[128,1280]{1,0:T(8,128)(2,1)S(1)}, bf16[128,1280]{1,0:T(8,128)(2,1)}, u32[]{:S(2)}) copy-start(bf16[128,1280]{1,0:T(8,128)(2,1)} %copy-done.4) | copy-start | bytes 983044
  53.1 10.0 %copy-start.7 = (bf16[128,1280]{1,0:T(8,128)(2,1)S(1)}, bf16[128,1280]{1,0:T(8,128)(2,1)}, u32[]{:S(2)}) copy-start(bf16[128,1280]{1,0:T(8,128)(2,1)} %copy-done.6) | copy-start | bytes 983044
  53.1 10.0 %copy-start.9 = (bf16[128,1280]{1,0:T(8,128)(2,1)S(1)}, bf16[128,1280]{1,0:T(8,128)(2,1)}, u32[]{:S(2)}) copy-start(bf16[128,1280]{1,0:T(8,128)(2,1)} %copy-done.8) | copy-start | bytes 983044
  53.1 10.0 %copy-start.10 = (s32[4]{0:T(128)S(1)}, s32[4]{0:T(128)}, u32[]{:S(2)}) copy-start(s32[4]{0:T(128)} %frames_ref.3) | copy-start | bytes 52
  53.1 10.0 %copy-start.11 = (f32[1000]{0:T(1024)S(1)}, f32[1000]{0:T(1024)}, u32[]{:S(2)}) copy-start(f32[1000]{0:T(1024)} %step_weight_ref.1) | copy-start | bytes 12004
  53.1 10.0 %copy-start.12 = (s32[2]{0:T(128)S(1)}, s32[2]{0:T(128)}, u32[]{:S(2)}) copy-start(s32[2]{0:T(128)} %timestep_ref.1) | copy-start | bytes 28
  75.7 5.8 %collective-permute-start.7 = (bf16[2,64,128]{2,1,0:T(8,128)(2,1)S(1)}, bf16[2,64,128]{2,1,0:T(8,128)(2,1)S(1)}, u32[]{:S(2)}, u32[]{:S(2)}) collective-permute-start(bf16[2,64,128]{2,1,0:T(8,128)(2,1)S(1)} %get-tuple-element.20), channel_id=1, source_target_pairs={{0,24},{4,28},{8,16},{12,20},{16,8},{20,12},{24,0},{28,4},{1,25},{... | collective-permute-start | bytes 98312 | tf_op jit(solution)/shard_map/ppermute | solution.py:335
  77.9 4.8 %collective-permute-start.8 = (bf16[2,64,128]{2,1,0:T(8,128)(2,1)S(1)}, bf16[2,64,128]{2,1,0:T(8,128)(2,1)S(1)}, u32[]{:S(2)}, u32[]{:S(2)}) collective-permute-start(bf16[2,64,128]{2,1,0:T(8,128)(2,1)S(1)} %get-tuple-element.21), channel_id=1, source_target_pairs={{0,16},{4,20},{8,24},{12,28},{16,0},{20,4},{24,8},{28,12},{1,17},{... | collective-permute-start | bytes 98312 | tf_op jit(solution)/shard_map/ppermute | solution.py:335
  77.9 4.8 %collective-permute-start.9 = (bf16[2,64,128]{2,1,0:T(8,128)(2,1)S(1)}, bf16[2,64,128]{2,1,0:T(8,128)(2,1)S(1)}, u32[]{:S(2)}, u32[]{:S(2)}) collective-permute-start(bf16[2,64,128]{2,1,0:T(8,128)(2,1)S(1)} %get-tuple-element.22), channel_id=1, source_target_pairs={{0,8},{4,12},{8,0},{12,4},{16,24},{20,28},{24,16},{28,20},{1,9},{5... | collective-permute-start | bytes 98312 | tf_op jit(solution)/shard_map/ppermute | solution.py:335
  82.7 4.0 %collective-permute-start.10 = (f32[1,64,128]{2,1,0:T(8,128)S(1)}, f32[1,64,128]{2,1,0:T(8,128)S(1)}, u32[]{:S(2)}, u32[]{:S(2)}) collective-permute-start(f32[1,64,128]{2,1,0:T(8,128)S(1)} %slice.9), channel_id=1, source_target_pairs={{0,4},{4,0},{8,12},{12,8},{16,20},{20,16},{24,28},{28,24},{1,5},{5... | collective-permute-start | bytes 98312 | tf_op jit(solution)/shard_map/ppermute | solution.py:335
  86.7 3.6 %collective-permute-start.11 = (f32[64,128]{1,0:T(8,128)S(1)}, f32[64,128]{1,0:T(8,128)S(1)}, u32[]{:S(2)}, u32[]{:S(2)}) collective-permute-start(f32[64,128]{1,0:T(8,128)S(1)} %fusion), channel_id=1, source_target_pairs={{0,3},{1,2},{2,1},{3,0},{4,7},{5,6},{6,5},{7,4},{8,11},{9,10},{10,... | collective-permute-start | bytes 98312 | tf_op jit(solution)/shard_map/ppermute | solution.py:335
  86.7 4.0 %collective-permute-start.12 = (f32[64,128]{1,0:T(8,128)S(1)}, f32[64,128]{1,0:T(8,128)S(1)}, u32[]{:S(2)}, u32[]{:S(2)}) collective-permute-start(f32[64,128]{1,0:T(8,128)S(1)} %fusion), channel_id=1, source_target_pairs={{0,2},{1,3},{2,0},{3,1},{4,6},{5,7},{6,4},{7,5},{8,10},{9,11},{10,... | collective-permute-start | bytes 98312 | tf_op jit(solution)/shard_map/ppermute | solution.py:335
  88.3 2.4 %collective-permute-start.13 = (f32[64,128]{1,0:T(8,128)S(1)}, f32[64,128]{1,0:T(8,128)S(1)}, u32[]{:S(2)}, u32[]{:S(2)}) collective-permute-start(f32[64,128]{1,0:T(8,128)S(1)} %fusion), channel_id=1, source_target_pairs={{0,1},{1,0},{2,3},{3,2},{4,5},{5,4},{6,7},{7,6},{8,9},{9,8},{10,11... | collective-permute-start | bytes 98312 | tf_op jit(solution)/shard_map/ppermute | solution.py:335

commit v17 on v14

--- a/solution.py
+++ b/solution.py
@@ -14,8 +14,8 @@
 NT = (((1,), (1,)), ((), ()))
 LOG2_SCALE = math.log2(math.e) / math.sqrt(HD)
 LOWEST = -1e30
-NEXT_WAVE = 0
-SMALL_VMEM = 24 * 1024 * 1024
+PACK_VMEM = 4 * 1024 * 1024
+SMALL_VMEM = 16 * 1024 * 1024
 LARGE_VMEM = 60 * 1024 * 1024
 SMEM = pl.BlockSpec(memory_space=pltpu.SMEM)
 VMEM = pl.BlockSpec(memory_space=pltpu.VMEM)
@@ -60,7 +60,7 @@
         copy.wait()
 
 
-def pack(me, model, qkv, readout_t, k, count, after, wave=False):
+def pack(me, model, qkv, readout_t, k, count, after, first=False):
     rows = qkv.shape[1]
     lat = readout_t.shape[1]
     width = count * 2 * HD + -(-count * lat // HD) * HD
@@ -74,9 +74,9 @@
             pltpu.VMEM((lat, count * HD), jnp.bfloat16),
             pltpu.SemaphoreType.DMA((2 * count + 1,)),
         ],
-        compiler_params=pltpu.CompilerParams(vmem_limit_bytes=SMALL_VMEM),
+        compiler_params=pltpu.CompilerParams(vmem_limit_bytes=LARGE_VMEM if first else PACK_VMEM),
         cost_estimate=pl.CostEstimate(
-            flops=NEXT_WAVE if wave else 0, bytes_accessed=rows * width * 4, transcendentals=0
+            flops=0, bytes_accessed=rows * width * 4, transcendentals=0
         ),
         name="pack",
     )(me, model, qkv, readout_t, *after)
@@ -149,8 +149,7 @@
     sums_ref, stats_ref, factor_ref, pieces, folded, asked, sems = refs[-7:]
     me = me_ref[0]
     rows = pieces.shape[1]
-    lat = sums_ref.shape[2]
-    count = folded.shape[0]
+    count, lat, _ = sums_ref.shape
     blocks = count_pieces // 2
     copies = [pltpu.make_async_copy(arrived[n], pieces.at[n], sems.at[n]) for n in range(count_pieces)]
     for copy in copies:
@@ -167,12 +166,13 @@
 
     def some_blocks(b, carry):
         q = [2 * b, 2 * b + 1]
+        span = pl.ds(pl.multiple_of(b * 2 * rows, 2 * rows), 2 * rows)
         shifts = mask_rows(frames_ref, me, rows, [jnp.where(n < half, n, n + 2) for n in q], offsets)
         peaks, totals, units = [], [], []
         for i in range(count):
 
             def finish(summed, total, peak, i=i):
-                sums_ref[b, i] = summed
+                sums_ref[i, :, span] = summed
                 peaks.append(peak)
                 totals.append(total)
 
@@ -182,15 +182,15 @@
             values = [lambda i=i, t=t: folded[i, :, t * 2 * rows : (t + 1) * 2 * rows] for t in range(blocks)]
             units.append((tiles, values, shifts, finish))
         run_units(units, lat)
-        rest = [jnp.ones_like(peaks[0])] * (stats_ref.shape[2] - count)
-        stats_ref[b, 0] = jnp.concatenate(peaks + rest, axis=0)
-        stats_ref[b, 1] = jnp.concatenate(totals + rest, axis=0)
+        rest = [jnp.ones_like(peaks[0])] * (stats_ref.shape[1] - count)
+        stats_ref[0, :, span] = jnp.concatenate(peaks + rest, axis=0)
+        stats_ref[1, :, span] = jnp.concatenate(totals + rest, axis=0)
         return carry
 
     lax.fori_loop(0, blocks, some_blocks, 0)
 
 
-def late_kernel(offsets, late, chosen, groups, frames_ref, me_ref, *refs):
+def late_kernel(offsets, late, frames_ref, me_ref, *refs):
     early = len(offsets)
     arrived = refs[:2]
     sums_ref, stats_ref, factor_ref, early_ref, early_folded, *out_refs, late_pieces, folded, sems = refs[2:]
@@ -206,44 +206,44 @@
     stage_values(folded, pieces[early:], lat)
     factor = factor_ref[:1]
     every = list(offsets) + list(late)
+    blocks = early // 2
     results = {}
 
-    def add(b, part):
-        results[b] = part if b not in results else results[b] + part
-
-    def write(b):
-        for j in range(2):
-            k = every[2 * b + j]
-            out_ref = out_refs[groups.index(k // size)]
-            out_ref[k % size] = (results[b][:, j * rows : (j + 1) * rows] * factor).astype(out_ref.dtype)
+    def write(number, start):
+        for j in range(number):
+            k = every[start + j]
+            out_ref = out_refs[k // size]
+            out_ref[k % size] = (results[start][:, j * rows : (j + 1) * rows] * factor).astype(out_ref.dtype)
 
     units = []
-    blocks = early // 2
-    for b in chosen:
-        keys_in = range(blocks + 1) if b == blocks else [blocks]
-        key_offsets = [every[2 * t + j] for t in keys_in for j in range(2)]
-        shifts = mask_rows(frames_ref, me, rows, every[2 * b : 2 * b + 2], key_offsets)
+    for start, number, tiles_in in ((0, early, [blocks]), (early, 2, range(blocks + 1))):
+        key_offsets = [every[2 * t + j] for t in tiles_in for j in range(2)]
+        shifts = mask_rows(frames_ref, me, rows, every[start : start + number], key_offsets)
         for i in range(count):
 
-            def finish(summed, total, peak, b=b, i=i):
-                if b < blocks:
-                    before = stats_ref[b, 0, i : i + 1]
+            def finish(summed, total, peak, start=start, number=number, i=i):
+                if start == 0:
+                    before = stats_ref[0, i : i + 1]
                     highest = jnp.maximum(before, peak)
                     old = jnp.exp2((before - highest) * LOG2_SCALE)
                     new = jnp.exp2((peak - highest) * LOG2_SCALE)
-                    both = stats_ref[b, 1, i : i + 1] * old + total * new
-                    add(b, sums_ref[b, i] * (old / both) + summed * (new / both))
+                    both = stats_ref[1, i : i + 1] * old + total * new
+                    part = sums_ref[i] * (old / both) + summed * (new / both)
                 else:
-                    add(b, summed / total)
+                    part = summed / total
+                results[start] = part if i == 0 else results[start] + part
                 if i == count - 1:
-                    write(b)
-
-            queries = pairs_of(pieces, i, 0)[b]
+                    write(number, start)
+
+            def queries(start=start, number=number, i=i):
+                column = 2 * i * HD
+                return jnp.concatenate([p[:, column : column + HD] for p in pieces[start : start + number]], axis=0)
+
             keys = pairs_of(pieces, i, 1)
-            tiles = [functools.partial(score_tile, keys[t], queries) for t in keys_in]
+            tiles = [functools.partial(score_tile, keys[t], queries) for t in tiles_in]
             values = [
                 lambda i=i, t=t: folded[i] if t == blocks else early_folded[i, :, t * 2 * rows : (t + 1) * 2 * rows]
-                for t in keys_in
+                for t in tiles_in
             ]
             units.append((tiles, values, shifts, finish))
     run_units(units, lat)
@@ -258,8 +258,8 @@
         in_specs=[SMEM] * 6 + [HBM] * len(pieces),
         out_specs=[VMEM] * 5,
         out_shape=[
-            jax.ShapeDtypeStruct((blocks, count, lat, 2 * rows), jnp.float32),
-            jax.ShapeDtypeStruct((blocks, 2, 8, 2 * rows), jnp.float32),
+            jax.ShapeDtypeStruct((count, lat, tokens), jnp.float32),
+            jax.ShapeDtypeStruct((2, 8, tokens), jnp.float32),
             jax.ShapeDtypeStruct((8, rows), jnp.float32),
             jax.ShapeDtypeStruct((len(pieces), rows, width), jnp.bfloat16),
             jax.ShapeDtypeStruct((count, lat + 16, tokens), jnp.bfloat16),
@@ -278,16 +278,16 @@
     )(span_frames, me, timestep, step_weight, sign, sample, *pieces)
 
 
-def attend_late(pieces, offsets, late, chosen, groups, early, span_frames, me, count, lat):
+def attend_late(pieces, offsets, late, early, span_frames, me, count, lat):
     rows, width = pieces[0].shape
     half = len(offsets) // 2 + 1
     tokens = 2 * half * rows
     return pl.pallas_call(
-        functools.partial(late_kernel, offsets, late, chosen, groups),
+        functools.partial(late_kernel, offsets, late),
         in_specs=[SMEM] * 2 + [HBM] * 2 + [VMEM] * len(early),
-        out_specs=[VMEM] * len(groups),
+        out_specs=[VMEM] * 4,
         out_shape=[
-            jax.ShapeDtypeStruct((half // 2, lat, rows), jnp.bfloat16 if g else jnp.float32) for g in groups
+            jax.ShapeDtypeStruct((half // 2, lat, rows), jnp.bfloat16 if g else jnp.float32) for g in range(4)
         ],
         scratch_shapes=[
             pltpu.VMEM((2, rows, width), jnp.bfloat16),
@@ -327,20 +327,18 @@
     pieces = [None] * seq_count
     for n in range(half):
         k = seq_count - 1 - n
-        pieces[k] = swap(pack(me, model, qkv, readout_t, k, count, [pieces[k + 2]] if n > 1 else [], n > 1), "seq", k)
-    pieces[0] = pack(me, model, qkv, readout_t, 0, count, [pieces[seq_count - 1]])
-    for k in [half - 1] + list(range(1, half - 1)):
-        after = [pieces[k - 1], pieces[half - 1], pieces[seq_count - 1]] if k not in (1, half - 1) else []
+        pieces[k] = swap(pack(me, model, qkv, readout_t, k, count, [pieces[k + 2]] if n > 1 else [], n == 0), "seq", k)
+    for k in range(half - 1, 0, -1):
+        after = [] if k == half - 1 else [pieces[k + 1], pieces[seq_count - 1]] if k > 1 else [pieces[half - 1]]
         pieces[k] = swap(pack(me, model, qkv, readout_t, k, count, after), "seq", k)
+    pieces[0] = pack(me, model, qkv, readout_t, 0, count, [pieces[half - 1]])
     late = [half, half + 1]
     early = [k for k in range(seq_count) if k not in late]
     merged = attend_early(
         [pieces[k] for k in early], early, span_frames, me, timestep, step_weight, sign, sample, count, lat
     )
-    blocks = len(early) // 2
     ends = [pieces[k] for k in late]
-    order = [blocks] + list(range(blocks))
-    given = attend_late(ends, early, late, order, [0, 1, 2, 3], merged, span_frames, me, count, lat)
+    given = attend_late(ends, early, late, merged, span_frames, me, count, lat)
     size = half // 2
     while True:
         keep = given[0]

time: 89.7 us -> 87.6 us (0.977)
  local copies, waits for them, and re-layouts: 5.1 us -> 2.69 us
  waiting for transfers between devices: 41.7 us -> 39.9 us
  Pallas kernels: 19.1 us -> 20.7 us
    unnamed x26 -> x20, local copies, waits for them, and re-layouts: 5.1 us -> 2.69 us
    pallas_call x8, Pallas kernels: 8.63 us -> 11 us  [pack(): pl.pallas_call(functools.partial(pack_kernel, k), in_specs=[SMEM, SMEM] +...]
    ppermute x14, waiting for transfers between devices: 41.7 us -> 39.9 us  [swap(): return lax.ppermute(array, axis, [(i, i ^ offset) for i in range(size)])]
  transfers between devices with their start and end apart: 14 -> 14, of which waited for: 10 -> 9; matrix products, arithmetic and copies ran while one was open for 0% -> 0% of each run, Pallas kernels for 15% -> 16%
where the time goes in v17:
time: 87.6 us; the launch traced here: 87.3 us
  waiting for transfers between devices  39.9 us (46%)
  starting transfers between devices  23.1 us (26%)
  Pallas kernels  20.7 us (24%)
  local copies, waits for them, and re-layouts  2.69 us (3%)
    ppermute x14, waiting for transfers between devices, swap(): return lax.ppermute(array, axis, [(i, i ^ offset) for i in range(size)])  39.9 us
    ppermute x14, starting transfers between devices, swap(): return lax.ppermute(array, axis, [(i, i ^ offset) for i in range(size)])  23.1 us
    pallas_call x8, Pallas kernels, pack(): pl.pallas_call(functools.partial(pack_kernel, k), in_specs=[SMEM, SMEM] +...  11 us
    pallas_call x1, Pallas kernels, attend_early(): pl.pallas_call(functools.partial(early_kernel, offsets), in_specs=[SMEM]...  5.76 us
    pallas_call x1, Pallas kernels, attend_late(): pl.pallas_call(functools.partial(late_kernel, offsets, late), in_specs=[S...  3.94 us
    unnamed x20, local copies, waits for them, and re-layouts  2.69 us
  transfers between devices with their start and end apart: 14, of which 9 were waited for; matrix products, arithmetic and copies ran while one was open for 0% of the time, Pallas kernels for 16%

profile of v17, /device:TPU:0, one launch (start us, length us, event | category | flops | bytes accessed | tf_op | source)
XLA Modules:
  0.0 87.3 jit_solution(18343462056155632764)
XLA Ops:
  0.0 2.4 %pack.10 = bf16[128,1280]{1,0:T(8,128)(2,1)} custom-call(s32[1]{0:T(128)} %bitcast.me_ref, s32[1]{0:T(128)} %bitcast.1.model_ref, bf16[1,128,12288]{2,1,0:T(8,128)(2,1)} %qkv_ref.15, bf16[2,64,4096]{2,1,0:T(8,128)(2,1)} %bitcast.9), custom_call_target="tpu_custom_call" | custom-call | bytes 655360 | tf_op jit(solution)/shard_map/pack/pallas_call | solution.py:67
  2.4 6.0 %collective-permute-start.2 = (bf16[128,1280]{1,0:T(8,128)(2,1)}, bf16[128,1280]{1,0:T(8,128)(2,1)S(1)}, u32[]{:S(2)}, u32[]{:S(2)}) collective-permute-start(bf16[128,1280]{1,0:T(8,128)(2,1)} %pack.10), channel_id=1, source_target_pairs={{0,28},{4,24},{8,20},{12,16},{16,12},{20,8},{24,4},{28,0},{1,29},{... | collective-permute-start | bytes 983048 | tf_op jit(solution)/shard_map/ppermute | solution.py:309
  8.5 0.0 copy-done
  8.5 1.2 %copy-done.1 = bf16[2,4096,64]{1,2,0:T(8,128)(2,1)S(1)} copy-done((bf16[2,4096,64]{1,2,0:T(8,128)(2,1)S(1)}, bf16[2,4096,64]{1,2,0:T(8,128)(2,1)}, u32[]{:S(2)}) %copy-start.1) | copy-done | bytes 1048600
  9.7 0.8 pack.12
  10.5 0.1 collective-permute-start.4
  10.6 0.8 pack.8
  11.4 0.9 %collective-permute-start = (bf16[128,1280]{1,0:T(8,128)(2,1)S(1)}, bf16[128,1280]{1,0:T(8,128)(2,1)S(1)}, u32[]{:S(2)}, u32[]{:S(2)}) collective-permute-start(bf16[128,1280]{1,0:T(8,128)(2,1)S(1)} %pack.8), channel_id=1, source_target_pairs={{0,24},{4,28},{8,16},{12,20},{16,8},{20,12},{24,0},{28,4},{1,25},{... | collective-permute-start | bytes 983048 | tf_op jit(solution)/shard_map/ppermute | solution.py:309
  12.3 4.9 %collective-permute-done.2.refs_0_.refs_1_.refs_5_ = bf16[128,1280]{1,0:T(8,128)(2,1)S(1)} collective-permute-done((bf16[128,1280]{1,0:T(8,128)(2,1)}, bf16[128,1280]{1,0:T(8,128)(2,1)S(1)}, u32[]{:S(2)}, u32[]{:S(2)}) %collective-permute-start.2) | collective-permute-done | bytes 327712 | tf_op jit(solution)/shard_map/ppermute | solution.py:309
  17.3 10.7 %collective-permute-done.4.refs_0_.refs_3_ = bf16[128,1280]{1,0:T(8,128)(2,1)S(1)} collective-permute-done((bf16[128,1280]{1,0:T(8,128)(2,1)S(1)}, bf16[128,1280]{1,0:T(8,128)(2,1)S(1)}, u32[]{:S(2)}, u32[]{:S(2)}) %collective-permute-start.4) | collective-permute-done | bytes 327712 | tf_op jit(solution)/shard_map/ppermute | solution.py:309
  28.0 1.5 %pack.15 = bf16[128,1280]{1,0:T(8,128)(2,1)} custom-call(s32[1]{0:T(128)} %bitcast.me_ref, s32[1]{0:T(128)} %bitcast.1.model_ref, bf16[1,128,12288]{2,1,0:T(8,128)(2,1)S(1)} %copy-done, bf16[2,64,4096]{2,1,0:T(8,128)(2,1)S(1)} %bitcast.12, bf16[128,1280]{1,0:T(8,128)(2,1)S(1)} %collective-permute-done.4.refs_0_.refs_3_, ...), custom_call_target="tpu_custom_call" | custom-call | bytes 655360 | tf_op jit(solution)/shard_map/pack/pallas_call | solution.py:67
  29.5 2.7 %collective-permute-start.6 = (bf16[128,1280]{1,0:T(8,128)(2,1)}, bf16[128,1280]{1,0:T(8,128)(2,1)}, u32[]{:S(2)}, u32[]{:S(2)}) collective-permute-start(bf16[128,1280]{1,0:T(8,128)(2,1)} %pack.15), channel_id=1, source_target_pairs={{0,8},{4,12},{8,0},{12,4},{16,24},{20,28},{24,16},{28,20},{1,9},{5... | collective-permute-start | bytes 983048 | tf_op jit(solution)/shard_map/ppermute | solution.py:309
  32.2 1.6 %pack.14 = bf16[128,1280]{1,0:T(8,128)(2,1)} custom-call(s32[1]{0:T(128)} %bitcast.me_ref, s32[1]{0:T(128)} %bitcast.1.model_ref, bf16[1,128,12288]{2,1,0:T(8,128)(2,1)S(1)} %copy-done, bf16[2,64,4096]{2,1,0:T(8,128)(2,1)S(1)} %bitcast.13, bf16[128,1280]{1,0:T(8,128)(2,1)S(1)} %collective-permute-done.4.refs_0_.refs_3_), custom_call_target="tpu_custom_call" | custom-call | bytes 655360 | tf_op jit(solution)/shard_map/pack/pallas_call | solution.py:67
  33.8 1.4 %collective-permute-start.5 = (bf16[128,1280]{1,0:T(8,128)(2,1)}, bf16[128,1280]{1,0:T(8,128)(2,1)}, u32[]{:S(2)}, u32[]{:S(2)}) collective-permute-start(bf16[128,1280]{1,0:T(8,128)(2,1)} %pack.14), channel_id=1, source_target_pairs={{0,4},{4,0},{8,12},{12,8},{16,20},{20,16},{24,28},{28,24},{1,5},{5... | collective-permute-start | bytes 983048 | tf_op jit(solution)/shard_map/ppermute | solution.py:309
  35.2 0.0 copy-done.3
  35.2 1.5 %pack.11 = bf16[128,1280]{1,0:T(8,128)(2,1)} custom-call(s32[1]{0:T(128)} %bitcast.me_ref, s32[1]{0:T(128)} %bitcast.1.model_ref, bf16[1,128,12288]{2,1,0:T(8,128)(2,1)S(1)} %copy-done, bf16[2,64,4096]{2,1,0:T(8,128)(2,1)S(1)} %bitcast.14, bf16[128,1280]{1,0:T(8,128)(2,1)S(1)} %collective-permute-done.2.refs_0_.refs_1_.refs_5_), custom_call_target="tpu_custom_call" | custom-call | bytes 655360 | tf_op jit(solution)/shard_map/pack/pallas_call | solution.py:67
  36.7 0.1 collective-permute-start.3
  36.8 0.0 collective-permute-done.refs_0_.refs_4_
  36.8 1.6 %pack.9 = bf16[128,1280]{1,0:T(8,128)(2,1)} custom-call(s32[1]{0:T(128)} %bitcast.me_ref, s32[1]{0:T(128)} %bitcast.1.model_ref, bf16[1,128,12288]{2,1,0:T(8,128)(2,1)S(1)} %copy-done, bf16[2,64,4096]{2,1,0:T(8,128)(2,1)S(1)} %bitcast.15, bf16[128,1280]{1,0:T(8,128)(2,1)S(1)} %collective-permute-done.refs_0_.refs_4_), custom_call_target="tpu_custom_call" | custom-call | bytes 655360 | tf_op jit(solution)/shard_map/pack/pallas_call | solution.py:67
  38.4 0.0 copy-start.7
  38.4 0.0 copy-start.8
  38.4 0.0 copy-start.9
  38.4 5.0 %collective-permute-start.1 = (bf16[128,1280]{1,0:T(8,128)(2,1)}, bf16[128,1280]{1,0:T(8,128)(2,1)}, u32[]{:S(2)}, u32[]{:S(2)}) collective-permute-start(bf16[128,1280]{1,0:T(8,128)(2,1)} %pack.9), channel_id=1, source_target_pairs={{0,16},{4,20},{8,24},{12,28},{16,0},{20,4},{24,8},{28,12},{1,17},{... | collective-permute-start | bytes 983048 | tf_op jit(solution)/shard_map/ppermute | solution.py:309
  43.5 1.2 %copy-done.2 = bf16[2,4096,64]{1,2,0:T(8,128)(2,1)S(1)} copy-done((bf16[2,4096,64]{1,2,0:T(8,128)(2,1)S(1)}, bf16[2,4096,64]{1,2,0:T(8,128)(2,1)}, u32[]{:S(2)}) %copy-start.2) | copy-done | bytes 1048600
  44.7 0.8 pack.13.refs_0_
  45.5 0.0 collective-permute-done.6.refs_2_
  45.5 0.0 collective-permute-done.5.refs_1_
  45.6 0.1 copy-done.4
  45.7 0.1 copy-done.6
  45.8 5.8 %attend_early.1 = (f32[4,64,768]{2,1,0:T(8,128)S(1)}, f32[2,8,768]{2,1,0:T(8,128)S(1)}, f32[8,128]{1,0:T(8,128)S(1)}, bf16[6,128,1280]{2,1,0:T(8,128)(2,1)S(1)}, bf16[4,80,768]{2,1,0:T(8,128)(2,1)S(1)}) custom-call(s32[4]{0:T(128)S(1)} %copy-done.7, s32[1]{0:T(128)} %bitcast.me_ref, s32[2]{0:T(128)S(1)} %copy-done.9, f32[1000]{0:T(1024)S(1)} %copy-done.8, ...), custom_call_target="tpu_custom_call" | custom-call | flops 905969664 | bytes 2359296 | tf_op jit(solution)/shard_map/attend_early/pallas_call | solution.py:256
  51.5 10.8 %collective-permute-done.3.refs_1_ = bf16[128,1280]{1,0:T(8,128)(2,1)} collective-permute-done((bf16[128,1280]{1,0:T(8,128)(2,1)}, bf16[128,1280]{1,0:T(8,128)(2,1)}, u32[]{:S(2)}, u32[]{:S(2)}) %collective-permute-start.3) | collective-permute-done | bytes 327712 | tf_op jit(solution)/shard_map/ppermute | solution.py:309
  62.4 5.2 %collective-permute-done.1.refs_0_ = bf16[128,1280]{1,0:T(8,128)(2,1)} collective-permute-done((bf16[128,1280]{1,0:T(8,128)(2,1)}, bf16[128,1280]{1,0:T(8,128)(2,1)}, u32[]{:S(2)}, u32[]{:S(2)}) %collective-permute-start.1) | collective-permute-done | bytes 327712 | tf_op jit(solution)/shard_map/ppermute | solution.py:309
  67.6 3.9 %attend_late.1 = (f32[2,64,128]{2,1,0:T(8,128)S(1)}, bf16[2,64,128]{2,1,0:T(8,128)(2,1)S(1)}, bf16[2,64,128]{2,1,0:T(8,128)(2,1)S(1)}, bf16[2,64,128]{2,1,0:T(8,128)(2,1)S(1)}) custom-call(s32[4]{0:T(128)S(1)} %copy-done.7, s32[1]{0:T(128)} %bitcast.me_ref, bf16[128,1280]{1,0:T(8,128)(2,1)} %collective-permute-done.1.refs_0_, ...), custom_call_target="tpu_custom_call" | custom-call | flops 402653184 | bytes 3145728 | tf_op jit(solution)/shard_map/attend_late/pallas_call | solution.py:285
  71.6 2.2 %collective-permute-start.7 = (bf16[2,64,128]{2,1,0:T(8,128)(2,1)S(1)}, bf16[2,64,128]{2,1,0:T(8,128)(2,1)S(1)}, u32[]{:S(2)}, u32[]{:S(2)}) collective-permute-start(bf16[2,64,128]{2,1,0:T(8,128)(2,1)S(1)} %get-tuple-element.20), channel_id=1, source_target_pairs={{0,24},{4,28},{8,16},{12,20},{16,8},{20,12},{24,0},{28,4},{1,25},{... | collective-permute-start | bytes 98312 | tf_op jit(solution)/shard_map/ppermute | solution.py:309
  73.8 0.0 collective-permute-start.8
  73.8 2.2 %collective-permute-start.9 = (bf16[2,64,128]{2,1,0:T(8,128)(2,1)S(1)}, bf16[2,64,128]{2,1,0:T(8,128)(2,1)S(1)}, u32[]{:S(2)}, u32[]{:S(2)}) collective-permute-start(bf16[2,64,128]{2,1,0:T(8,128)(2,1)S(1)} %get-tuple-element.22), channel_id=1, source_target_pairs={{0,8},{4,12},{8,0},{12,4},{16,24},{20,28},{24,16},{28,20},{1,9},{5... | collective-permute-start | bytes 98312 | tf_op jit(solution)/shard_map/ppermute | solution.py:309
  76.0 1.5 %collective-permute-done.7 = bf16[2,64,128]{2,1,0:T(8,128)(2,1)S(1)} collective-permute-done((bf16[2,64,128]{2,1,0:T(8,128)(2,1)S(1)}, bf16[2,64,128]{2,1,0:T(8,128)(2,1)S(1)}, u32[]{:S(2)}, u32[]{:S(2)}) %collective-permute-start.7) | collective-permute-done | bytes 32800 | tf_op jit(solution)/shard_map/ppermute | solution.py:309
  77.5 1.1 %collective-permute-done.8 = bf16[2,64,128]{2,1,0:T(8,128)(2,1)S(1)} collective-permute-done((bf16[2,64,128]{2,1,0:T(8,128)(2,1)S(1)}, bf16[2,64,128]{2,1,0:T(8,128)(2,1)S(1)}, u32[]{:S(2)}, u32[]{:S(2)}) %collective-permute-start.8) | collective-permute-done | bytes 32800 | tf_op jit(solution)/shard_map/ppermute | solution.py:309
  78.6 0.0 collective-permute-done.9
  78.6 0.6 collective-permute-start.10
  79.3 3.4 %collective-permute-done.10 = f32[1,64,128]{2,1,0:T(8,128)S(1)} collective-permute-done((f32[1,64,128]{2,1,0:T(8,128)S(1)}, f32[1,64,128]{2,1,0:T(8,128)S(1)}, u32[]{:S(2)}, u32[]{:S(2)}) %collective-permute-start.10) | collective-permute-done | bytes 32800 | tf_op jit(solution)/shard_map/ppermute | solution.py:309
  82.6 0.0 collective-permute-start.11
  82.6 1.6 %collective-permute-start.12 = (f32[64,128]{1,0:T(8,128)S(1)}, f32[64,128]{1,0:T(8,128)S(1)}, u32[]{:S(2)}, u32[]{:S(2)}) collective-permute-start(f32[64,128]{1,0:T(8,128)S(1)} %fusion), channel_id=1, source_target_pairs={{0,2},{1,3},{2,0},{3,1},{4,6},{5,7},{6,4},{7,5},{8,10},{9,11},{10,... | collective-permute-start | bytes 98312 | tf_op jit(solution)/shard_map/ppermute | solution.py:309
  84.2 0.3 collective-permute-start.13
  84.5 1.8 %collective-permute-done.11 = f32[64,128]{1,0:T(8,128)S(1)} collective-permute-done((f32[64,128]{1,0:T(8,128)S(1)}, f32[64,128]{1,0:T(8,128)S(1)}, u32[]{:S(2)}, u32[]{:S(2)}) %collective-permute-start.11) | collective-permute-done | bytes 32800 | tf_op jit(solution)/shard_map/ppermute | solution.py:309
  86.2 0.4 collective-permute-done.12
  86.7 0.0 collective-permute-done.13
  86.7 0.6 add_bitcast_fusion
  (14 shorter events, 0.0 us)
Async XLA Ops:
  0.0 8.5 %copy-start = (bf16[1,128,12288]{2,1,0:T(8,128)(2,1)S(1)}, bf16[1,128,12288]{2,1,0:T(8,128)(2,1)}, u32[]{:S(2)}) copy-start(bf16[1,128,12288]{2,1,0:T(8,128)(2,1)} %qkv_ref.15) | copy-start | bytes 9437188
  2.4 14.8 %collective-permute-start.2 = (bf16[128,1280]{1,0:T(8,128)(2,1)}, bf16[128,1280]{1,0:T(8,128)(2,1)S(1)}, u32[]{:S(2)}, u32[]{:S(2)}) collective-permute-start(bf16[128,1280]{1,0:T(8,128)(2,1)} %pack.10), channel_id=1, source_target_pairs={{0,28},{4,24},{8,20},{12,16},{16,12},{20,8},{24,4},{28,0},{1,29},{... | collective-permute-start | bytes 983048 | tf_op jit(solution)/shard_map/ppermute | solution.py:309
  8.5 1.2 %copy-start.1 = (bf16[2,4096,64]{1,2,0:T(8,128)(2,1)S(1)}, bf16[2,4096,64]{1,2,0:T(8,128)(2,1)}, u32[]{:S(2)}) copy-start(bf16[2,4096,64]{1,2,0:T(8,128)(2,1)} %param.6) | copy-start | bytes 3145732
  10.5 17.5 %collective-permute-start.4 = (bf16[128,1280]{1,0:T(8,128)(2,1)S(1)}, bf16[128,1280]{1,0:T(8,128)(2,1)S(1)}, u32[]{:S(2)}, u32[]{:S(2)}) collective-permute-start(bf16[128,1280]{1,0:T(8,128)(2,1)S(1)} %pack.12), channel_id=1, source_target_pairs={{0,12},{4,8},{8,4},{12,0},{16,28},{20,24},{24,20},{28,16},{1,13},{... | collective-permute-start | bytes 983048 | tf_op jit(solution)/shard_map/ppermute | solution.py:309
  11.4 25.4 %collective-permute-start = (bf16[128,1280]{1,0:T(8,128)(2,1)S(1)}, bf16[128,1280]{1,0:T(8,128)(2,1)S(1)}, u32[]{:S(2)}, u32[]{:S(2)}) collective-permute-start(bf16[128,1280]{1,0:T(8,128)(2,1)S(1)} %pack.8), channel_id=1, source_target_pairs={{0,24},{4,28},{8,16},{12,20},{16,8},{20,12},{24,0},{28,4},{1,25},{... | collective-permute-start | bytes 983048 | tf_op jit(solution)/shard_map/ppermute | solution.py:309
  17.3 17.9 %copy-start.3 = (bf16[128,1280]{1,0:T(8,128)(2,1)}, bf16[128,1280]{1,0:T(8,128)(2,1)S(1)}, u32[]{:S(2)}) copy-start(bf16[128,1280]{1,0:T(8,128)(2,1)S(1)} %collective-permute-done.2.refs_0_.refs_1_.refs_5_) | copy-start | bytes 983044
  29.5 16.0 %collective-permute-start.6 = (bf16[128,1280]{1,0:T(8,128)(2,1)}, bf16[128,1280]{1,0:T(8,128)(2,1)}, u32[]{:S(2)}, u32[]{:S(2)}) collective-permute-start(bf16[128,1280]{1,0:T(8,128)(2,1)} %pack.15), channel_id=1, source_target_pairs={{0,8},{4,12},{8,0},{12,4},{16,24},{20,28},{24,16},{28,20},{1,9},{5... | collective-permute-start | bytes 983048 | tf_op jit(solution)/shard_map/ppermute | solution.py:309
  33.8 11.8 %collective-permute-start.5 = (bf16[128,1280]{1,0:T(8,128)(2,1)}, bf16[128,1280]{1,0:T(8,128)(2,1)}, u32[]{:S(2)}, u32[]{:S(2)}) collective-permute-start(bf16[128,1280]{1,0:T(8,128)(2,1)} %pack.14), channel_id=1, source_target_pairs={{0,4},{4,0},{8,12},{12,8},{16,20},{20,16},{24,28},{28,24},{1,5},{5... | collective-permute-start | bytes 983048 | tf_op jit(solution)/shard_map/ppermute | solution.py:309
  36.7 25.7 %collective-permute-start.3 = (bf16[128,1280]{1,0:T(8,128)(2,1)}, bf16[128,1280]{1,0:T(8,128)(2,1)}, u32[]{:S(2)}, u32[]{:S(2)}) collective-permute-start(bf16[128,1280]{1,0:T(8,128)(2,1)} %pack.11), channel_id=1, source_target_pairs={{0,20},{4,16},{8,28},{12,24},{16,4},{20,0},{24,12},{28,8},{1,21},{... | collective-permute-start | bytes 983048 | tf_op jit(solution)/shard_map/ppermute | solution.py:309
  36.8 1.6 %copy-start.5 = (bf16[128,1280]{1,0:T(8,128)(2,1)}, bf16[128,1280]{1,0:T(8,128)(2,1)S(1)}, u32[]{:S(2)}) copy-start(bf16[128,1280]{1,0:T(8,128)(2,1)S(1)} %collective-permute-done.refs_0_.refs_4_) | copy-start | bytes 983044
  38.4 7.1 %copy-start.7 = (s32[4]{0:T(128)S(1)}, s32[4]{0:T(128)}, u32[]{:S(2)}) copy-start(s32[4]{0:T(128)} %frames_ref.3) | copy-start | bytes 52
  38.4 7.1 %copy-start.8 = (f32[1000]{0:T(1024)S(1)}, f32[1000]{0:T(1024)}, u32[]{:S(2)}) copy-start(f32[1000]{0:T(1024)} %step_weight_ref.1) | copy-start | bytes 12004
  38.4 7.1 %copy-start.9 = (s32[2]{0:T(128)S(1)}, s32[2]{0:T(128)}, u32[]{:S(2)}) copy-start(s32[2]{0:T(128)} %timestep_ref.1) | copy-start | bytes 28
  38.4 29.2 %collective-permute-start.1 = (bf16[128,1280]{1,0:T(8,128)(2,1)}, bf16[128,1280]{1,0:T(8,128)(2,1)}, u32[]{:S(2)}, u32[]{:S(2)}) collective-permute-start(bf16[128,1280]{1,0:T(8,128)(2,1)} %pack.9), channel_id=1, source_target_pairs={{0,16},{4,20},{8,24},{12,28},{16,0},{20,4},{24,8},{28,12},{1,17},{... | collective-permute-start | bytes 983048 | tf_op jit(solution)/shard_map/ppermute | solution.py:309
  43.5 1.2 %copy-start.2 = (bf16[2,4096,64]{1,2,0:T(8,128)(2,1)S(1)}, bf16[2,4096,64]{1,2,0:T(8,128)(2,1)}, u32[]{:S(2)}) copy-start(bf16[2,4096,64]{1,2,0:T(8,128)(2,1)} %param.6) | copy-start | bytes 3145732
  44.7 1.0 %copy-start.4 = (bf16[128,1280]{1,0:T(8,128)(2,1)S(1)}, bf16[128,1280]{1,0:T(8,128)(2,1)}, u32[]{:S(2)}) copy-start(bf16[128,1280]{1,0:T(8,128)(2,1)} %copy-done.3) | copy-start | bytes 983044
  44.7 1.1 %copy-start.6 = (bf16[128,1280]{1,0:T(8,128)(2,1)S(1)}, bf16[128,1280]{1,0:T(8,128)(2,1)}, u32[]{:S(2)}) copy-start(bf16[128,1280]{1,0:T(8,128)(2,1)} %copy-done.5) | copy-start | bytes 983044
  71.6 5.9 %collective-permute-start.7 = (bf16[2,64,128]{2,1,0:T(8,128)(2,1)S(1)}, bf16[2,64,128]{2,1,0:T(8,128)(2,1)S(1)}, u32[]{:S(2)}, u32[]{:S(2)}) collective-permute-start(bf16[2,64,128]{2,1,0:T(8,128)(2,1)S(1)} %get-tuple-element.20), channel_id=1, source_target_pairs={{0,24},{4,28},{8,16},{12,20},{16,8},{20,12},{24,0},{28,4},{1,25},{... | collective-permute-start | bytes 98312 | tf_op jit(solution)/shard_map/ppermute | solution.py:309
  73.8 4.8 %collective-permute-start.8 = (bf16[2,64,128]{2,1,0:T(8,128)(2,1)S(1)}, bf16[2,64,128]{2,1,0:T(8,128)(2,1)S(1)}, u32[]{:S(2)}, u32[]{:S(2)}) collective-permute-start(bf16[2,64,128]{2,1,0:T(8,128)(2,1)S(1)} %get-tuple-element.21), channel_id=1, source_target_pairs={{0,16},{4,20},{8,24},{12,28},{16,0},{20,4},{24,8},{28,12},{1,17},{... | collective-permute-start | bytes 98312 | tf_op jit(solution)/shard_map/ppermute | solution.py:309
  73.8 4.8 %collective-permute-start.9 = (bf16[2,64,128]{2,1,0:T(8,128)(2,1)S(1)}, bf16[2,64,128]{2,1,0:T(8,128)(2,1)S(1)}, u32[]{:S(2)}, u32[]{:S(2)}) collective-permute-start(bf16[2,64,128]{2,1,0:T(8,128)(2,1)S(1)} %get-tuple-element.22), channel_id=1, source_target_pairs={{0,8},{4,12},{8,0},{12,4},{16,24},{20,28},{24,16},{28,20},{1,9},{5... | collective-permute-start | bytes 98312 | tf_op jit(solution)/shard_map/ppermute | solution.py:309
  78.6 4.0 %collective-permute-start.10 = (f32[1,64,128]{2,1,0:T(8,128)S(1)}, f32[1,64,128]{2,1,0:T(8,128)S(1)}, u32[]{:S(2)}, u32[]{:S(2)}) collective-permute-start(f32[1,64,128]{2,1,0:T(8,128)S(1)} %slice.9), channel_id=1, source_target_pairs={{0,4},{4,0},{8,12},{12,8},{16,20},{20,16},{24,28},{28,24},{1,5},{5... | collective-permute-start | bytes 98312 | tf_op jit(solution)/shard_map/ppermute | solution.py:309
  82.6 3.6 %collective-permute-start.11 = (f32[64,128]{1,0:T(8,128)S(1)}, f32[64,128]{1,0:T(8,128)S(1)}, u32[]{:S(2)}, u32[]{:S(2)}) collective-permute-start(f32[64,128]{1,0:T(8,128)S(1)} %fusion), channel_id=1, source_target_pairs={{0,3},{1,2},{2,1},{3,0},{4,7},{5,6},{6,5},{7,4},{8,11},{9,10},{10,... | collective-permute-start | bytes 98312 | tf_op jit(solution)/shard_map/ppermute | solution.py:309
  82.6 4.0 %collective-permute-start.12 = (f32[64,128]{1,0:T(8,128)S(1)}, f32[64,128]{1,0:T(8,128)S(1)}, u32[]{:S(2)}, u32[]{:S(2)}) collective-permute-start(f32[64,128]{1,0:T(8,128)S(1)} %fusion), channel_id=1, source_target_pairs={{0,2},{1,3},{2,0},{3,1},{4,6},{5,7},{6,4},{7,5},{8,10},{9,11},{10,... | collective-permute-start | bytes 98312 | tf_op jit(solution)/shard_map/ppermute | solution.py:309
  84.2 2.4 %collective-permute-start.13 = (f32[64,128]{1,0:T(8,128)S(1)}, f32[64,128]{1,0:T(8,128)S(1)}, u32[]{:S(2)}, u32[]{:S(2)}) collective-permute-start(f32[64,128]{1,0:T(8,128)S(1)} %fusion), channel_id=1, source_target_pairs={{0,1},{1,0},{2,3},{3,2},{4,5},{5,4},{6,7},{7,6},{8,9},{9,8},{10,11... | collective-permute-start | bytes 98312 | tf_op jit(solution)/shard_map/ppermute | solution.py:309

commit v18 on v17

--- a/solution.py
+++ b/solution.py
@@ -340,17 +340,20 @@
     ends = [pieces[k] for k in late]
     given = attend_late(ends, early, late, merged, span_frames, me, count, lat)
     size = half // 2
-    while True:
+    while size > 1:
         keep = given[0]
         for n in range(len(given) - 1, 0, -1):
             keep = keep + swap(given[n], "seq", n * size).astype(jnp.float32)
-        if size == 1:
+        radix = min(4, size // 2)
+        if radix == 1:
             break
-        radix = min(4, size)
         size //= radix
         given = [keep[n * size : (n + 1) * size] for n in range(radix)]
+    together = min(4, mp_count)
     total = keep[0]
-    offset = 1
+    for n in range(2 * together - 1, 0, -1):
+        total = total + swap(keep[n // together], ("seq", "mp"), n // together * mp_count + n % together)
+    offset = together
     while offset < mp_count:
         radix = min(4, mp_count // offset)
         own = total

time: 87.6 us -> 88 us (level)
  starting transfers between devices: 23.1 us -> 27 us
  waiting for transfers between devices: 39.9 us -> 36.5 us
    ppermute x14 -> x17, starting transfers between devices: 23.1 us -> 27 us  [swap(): return lax.ppermute(array, axis, [(i, i ^ offset) for i in range(size)])]
    ppermute x14 -> x17, waiting for transfers between devices: 39.9 us -> 36.5 us  [swap(): return lax.ppermute(array, axis, [(i, i ^ offset) for i in range(size)])]
  transfers between devices with their start and end apart: 14 -> 17, of which waited for: 9 -> 9; matrix products, arithmetic and copies ran while one was open for 0% -> 0% of each run, Pallas kernels for 16% -> 16%
where the time goes in v18:
time: 88 us; the launch traced here: 87.8 us
  waiting for transfers between devices  36.5 us (41%)
  starting transfers between devices  27 us (31%)
  Pallas kernels  20.7 us (24%)
  local copies, waits for them, and re-layouts  2.69 us (3%)
    ppermute x17, waiting for transfers between devices, swap(): return lax.ppermute(array, axis, [(i, i ^ offset) for i in range(size)])  36.5 us
    ppermute x17, starting transfers between devices, swap(): return lax.ppermute(array, axis, [(i, i ^ offset) for i in range(size)])  27 us
    pallas_call x8, Pallas kernels, pack(): pl.pallas_call(functools.partial(pack_kernel, k), in_specs=[SMEM, SMEM] +...  11 us
    pallas_call x1, Pallas kernels, attend_early(): pl.pallas_call(functools.partial(early_kernel, offsets), in_specs=[SMEM]...  5.77 us
    pallas_call x1, Pallas kernels, attend_late(): pl.pallas_call(functools.partial(late_kernel, offsets, late), in_specs=[S...  3.95 us
    unnamed x20, local copies, waits for them, and re-layouts  2.69 us
  transfers between devices with their start and end apart: 17, of which 9 were waited for; matrix products, arithmetic and copies ran while one was open for 0% of the time, Pallas kernels for 16%

profile of v18, /device:TPU:0, one launch (start us, length us, event | category | flops | bytes accessed | tf_op | source)
XLA Modules:
  0.0 87.8 jit_solution(10914051681123219378)
XLA Ops:
  0.0 2.4 %pack.10 = bf16[128,1280]{1,0:T(8,128)(2,1)} custom-call(s32[1]{0:T(128)} %bitcast.me_ref, s32[1]{0:T(128)} %bitcast.1.model_ref, bf16[1,128,12288]{2,1,0:T(8,128)(2,1)} %qkv_ref.15, bf16[2,64,4096]{2,1,0:T(8,128)(2,1)} %bitcast.13), custom_call_target="tpu_custom_call" | custom-call | bytes 655360 | tf_op jit(solution)/shard_map/pack/pallas_call | solution.py:67
  2.4 6.0 %collective-permute-start.2 = (bf16[128,1280]{1,0:T(8,128)(2,1)}, bf16[128,1280]{1,0:T(8,128)(2,1)S(1)}, u32[]{:S(2)}, u32[]{:S(2)}) collective-permute-start(bf16[128,1280]{1,0:T(8,128)(2,1)} %pack.10), channel_id=1, source_target_pairs={{0,28},{4,24},{8,20},{12,16},{16,12},{20,8},{24,4},{28,0},{1,29},{... | collective-permute-start | bytes 983048 | tf_op jit(solution)/shard_map/ppermute | solution.py:309
  8.5 1.2 %copy-done.1 = bf16[2,4096,64]{1,2,0:T(8,128)(2,1)S(1)} copy-done((bf16[2,4096,64]{1,2,0:T(8,128)(2,1)S(1)}, bf16[2,4096,64]{1,2,0:T(8,128)(2,1)}, u32[]{:S(2)}) %copy-start.1) | copy-done | bytes 1048600
  9.7 0.8 pack.12
  10.5 0.1 collective-permute-start.4
  10.6 0.8 pack.8
  11.4 0.9 %collective-permute-start = (bf16[128,1280]{1,0:T(8,128)(2,1)S(1)}, bf16[128,1280]{1,0:T(8,128)(2,1)S(1)}, u32[]{:S(2)}, u32[]{:S(2)}) collective-permute-start(bf16[128,1280]{1,0:T(8,128)(2,1)S(1)} %pack.8), channel_id=1, source_target_pairs={{0,24},{4,28},{8,16},{12,20},{16,8},{20,12},{24,0},{28,4},{1,25},{... | collective-permute-start | bytes 983048 | tf_op jit(solution)/shard_map/ppermute | solution.py:309
  12.3 4.9 %collective-permute-done.2.refs_0_.refs_1_.refs_5_ = bf16[128,1280]{1,0:T(8,128)(2,1)S(1)} collective-permute-done((bf16[128,1280]{1,0:T(8,128)(2,1)}, bf16[128,1280]{1,0:T(8,128)(2,1)S(1)}, u32[]{:S(2)}, u32[]{:S(2)}) %collective-permute-start.2) | collective-permute-done | bytes 327712 | tf_op jit(solution)/shard_map/ppermute | solution.py:309
  17.3 10.7 %collective-permute-done.4.refs_0_.refs_3_ = bf16[128,1280]{1,0:T(8,128)(2,1)S(1)} collective-permute-done((bf16[128,1280]{1,0:T(8,128)(2,1)S(1)}, bf16[128,1280]{1,0:T(8,128)(2,1)S(1)}, u32[]{:S(2)}, u32[]{:S(2)}) %collective-permute-start.4) | collective-permute-done | bytes 327712 | tf_op jit(solution)/shard_map/ppermute | solution.py:309
  28.0 1.5 %pack.15 = bf16[128,1280]{1,0:T(8,128)(2,1)} custom-call(s32[1]{0:T(128)} %bitcast.me_ref, s32[1]{0:T(128)} %bitcast.1.model_ref, bf16[1,128,12288]{2,1,0:T(8,128)(2,1)S(1)} %copy-done, bf16[2,64,4096]{2,1,0:T(8,128)(2,1)S(1)} %bitcast.16, bf16[128,1280]{1,0:T(8,128)(2,1)S(1)} %collective-permute-done.4.refs_0_.refs_3_, ...), custom_call_target="tpu_custom_call" | custom-call | bytes 655360 | tf_op jit(solution)/shard_map/pack/pallas_call | solution.py:67
  29.5 2.7 %collective-permute-start.6 = (bf16[128,1280]{1,0:T(8,128)(2,1)}, bf16[128,1280]{1,0:T(8,128)(2,1)}, u32[]{:S(2)}, u32[]{:S(2)}) collective-permute-start(bf16[128,1280]{1,0:T(8,128)(2,1)} %pack.15), channel_id=1, source_target_pairs={{0,8},{4,12},{8,0},{12,4},{16,24},{20,28},{24,16},{28,20},{1,9},{5... | collective-permute-start | bytes 983048 | tf_op jit(solution)/shard_map/ppermute | solution.py:309
  32.2 1.5 %pack.14 = bf16[128,1280]{1,0:T(8,128)(2,1)} custom-call(s32[1]{0:T(128)} %bitcast.me_ref, s32[1]{0:T(128)} %bitcast.1.model_ref, bf16[1,128,12288]{2,1,0:T(8,128)(2,1)S(1)} %copy-done, bf16[2,64,4096]{2,1,0:T(8,128)(2,1)S(1)} %bitcast.17, bf16[128,1280]{1,0:T(8,128)(2,1)S(1)} %collective-permute-done.4.refs_0_.refs_3_), custom_call_target="tpu_custom_call" | custom-call | bytes 655360 | tf_op jit(solution)/shard_map/pack/pallas_call | solution.py:67
  33.8 1.4 %collective-permute-start.5 = (bf16[128,1280]{1,0:T(8,128)(2,1)}, bf16[128,1280]{1,0:T(8,128)(2,1)}, u32[]{:S(2)}, u32[]{:S(2)}) collective-permute-start(bf16[128,1280]{1,0:T(8,128)(2,1)} %pack.14), channel_id=1, source_target_pairs={{0,4},{4,0},{8,12},{12,8},{16,20},{20,16},{24,28},{28,24},{1,5},{5... | collective-permute-start | bytes 983048 | tf_op jit(solution)/shard_map/ppermute | solution.py:309
  35.2 1.5 %pack.11 = bf16[128,1280]{1,0:T(8,128)(2,1)} custom-call(s32[1]{0:T(128)} %bitcast.me_ref, s32[1]{0:T(128)} %bitcast.1.model_ref, bf16[1,128,12288]{2,1,0:T(8,128)(2,1)S(1)} %copy-done, bf16[2,64,4096]{2,1,0:T(8,128)(2,1)S(1)} %bitcast.18, bf16[128,1280]{1,0:T(8,128)(2,1)S(1)} %collective-permute-done.2.refs_0_.refs_1_.refs_5_), custom_call_target="tpu_custom_call" | custom-call | bytes 655360 | tf_op jit(solution)/shard_map/pack/pallas_call | solution.py:67
  36.7 0.1 collective-permute-start.3
  36.8 0.0 collective-permute-done.refs_0_.refs_4_
  36.8 1.6 %pack.9 = bf16[128,1280]{1,0:T(8,128)(2,1)} custom-call(s32[1]{0:T(128)} %bitcast.me_ref, s32[1]{0:T(128)} %bitcast.1.model_ref, bf16[1,128,12288]{2,1,0:T(8,128)(2,1)S(1)} %copy-done, bf16[2,64,4096]{2,1,0:T(8,128)(2,1)S(1)} %bitcast.19, bf16[128,1280]{1,0:T(8,128)(2,1)S(1)} %collective-permute-done.refs_0_.refs_4_), custom_call_target="tpu_custom_call" | custom-call | bytes 655360 | tf_op jit(solution)/shard_map/pack/pallas_call | solution.py:67
  38.4 0.0 copy-start.7
  38.4 0.0 copy-start.8
  38.4 0.0 copy-start.9
  38.4 5.0 %collective-permute-start.1 = (bf16[128,1280]{1,0:T(8,128)(2,1)}, bf16[128,1280]{1,0:T(8,128)(2,1)}, u32[]{:S(2)}, u32[]{:S(2)}) collective-permute-start(bf16[128,1280]{1,0:T(8,128)(2,1)} %pack.9), channel_id=1, source_target_pairs={{0,16},{4,20},{8,24},{12,28},{16,0},{20,4},{24,8},{28,12},{1,17},{... | collective-permute-start | bytes 983048 | tf_op jit(solution)/shard_map/ppermute | solution.py:309
  43.5 1.2 %copy-done.2 = bf16[2,4096,64]{1,2,0:T(8,128)(2,1)S(1)} copy-done((bf16[2,4096,64]{1,2,0:T(8,128)(2,1)S(1)}, bf16[2,4096,64]{1,2,0:T(8,128)(2,1)}, u32[]{:S(2)}) %copy-start.2) | copy-done | bytes 1048600
  44.7 0.8 pack.13.refs_0_
  45.5 0.0 collective-permute-done.6.refs_2_
  45.6 0.1 copy-done.4
  45.7 0.1 copy-done.6
  45.8 5.8 %attend_early.1 = (f32[4,64,768]{2,1,0:T(8,128)S(1)}, f32[2,8,768]{2,1,0:T(8,128)S(1)}, f32[8,128]{1,0:T(8,128)S(1)}, bf16[6,128,1280]{2,1,0:T(8,128)(2,1)S(1)}, bf16[4,80,768]{2,1,0:T(8,128)(2,1)S(1)}) custom-call(s32[4]{0:T(128)S(1)} %copy-done.7, s32[1]{0:T(128)} %bitcast.me_ref, s32[2]{0:T(128)S(1)} %copy-done.9, f32[1000]{0:T(1024)S(1)} %copy-done.8, ...), custom_call_target="tpu_custom_call" | custom-call | flops 905969664 | bytes 2359296 | tf_op jit(solution)/shard_map/attend_early/pallas_call | solution.py:256
  51.5 10.8 %collective-permute-done.3.refs_1_ = bf16[128,1280]{1,0:T(8,128)(2,1)} collective-permute-done((bf16[128,1280]{1,0:T(8,128)(2,1)}, bf16[128,1280]{1,0:T(8,128)(2,1)}, u32[]{:S(2)}, u32[]{:S(2)}) %collective-permute-start.3) | collective-permute-done | bytes 327712 | tf_op jit(solution)/shard_map/ppermute | solution.py:309
  62.4 5.2 %collective-permute-done.1.refs_0_ = bf16[128,1280]{1,0:T(8,128)(2,1)} collective-permute-done((bf16[128,1280]{1,0:T(8,128)(2,1)}, bf16[128,1280]{1,0:T(8,128)(2,1)}, u32[]{:S(2)}, u32[]{:S(2)}) %collective-permute-start.1) | collective-permute-done | bytes 327712 | tf_op jit(solution)/shard_map/ppermute | solution.py:309
  67.6 3.9 %attend_late.1 = (f32[2,64,128]{2,1,0:T(8,128)S(1)}, bf16[2,64,128]{2,1,0:T(8,128)(2,1)S(1)}, bf16[2,64,128]{2,1,0:T(8,128)(2,1)S(1)}, bf16[2,64,128]{2,1,0:T(8,128)(2,1)S(1)}) custom-call(s32[4]{0:T(128)S(1)} %copy-done.7, s32[1]{0:T(128)} %bitcast.me_ref, bf16[128,1280]{1,0:T(8,128)(2,1)} %collective-permute-done.1.refs_0_, ...), custom_call_target="tpu_custom_call" | custom-call | flops 402653184 | bytes 3145728 | tf_op jit(solution)/shard_map/attend_late/pallas_call | solution.py:285
  71.6 2.2 %collective-permute-start.7 = (bf16[2,64,128]{2,1,0:T(8,128)(2,1)S(1)}, bf16[2,64,128]{2,1,0:T(8,128)(2,1)S(1)}, u32[]{:S(2)}, u32[]{:S(2)}) collective-permute-start(bf16[2,64,128]{2,1,0:T(8,128)(2,1)S(1)} %get-tuple-element.20), channel_id=1, source_target_pairs={{0,24},{4,28},{8,16},{12,20},{16,8},{20,12},{24,0},{28,4},{1,25},{... | collective-permute-start | bytes 98312 | tf_op jit(solution)/shard_map/ppermute | solution.py:309
  73.8 0.0 collective-permute-start.8
  73.8 2.2 %collective-permute-start.9 = (bf16[2,64,128]{2,1,0:T(8,128)(2,1)S(1)}, bf16[2,64,128]{2,1,0:T(8,128)(2,1)S(1)}, u32[]{:S(2)}, u32[]{:S(2)}) collective-permute-start(bf16[2,64,128]{2,1,0:T(8,128)(2,1)S(1)} %get-tuple-element.22), channel_id=1, source_target_pairs={{0,8},{4,12},{8,0},{12,4},{16,24},{20,28},{24,16},{28,20},{1,9},{5... | collective-permute-start | bytes 98312 | tf_op jit(solution)/shard_map/ppermute | solution.py:309
  76.0 1.5 %collective-permute-done.7 = bf16[2,64,128]{2,1,0:T(8,128)(2,1)S(1)} collective-permute-done((bf16[2,64,128]{2,1,0:T(8,128)(2,1)S(1)}, bf16[2,64,128]{2,1,0:T(8,128)(2,1)S(1)}, u32[]{:S(2)}, u32[]{:S(2)}) %collective-permute-start.7) | collective-permute-done | bytes 32800 | tf_op jit(solution)/shard_map/ppermute | solution.py:309
  77.5 1.1 %collective-permute-done.8 = bf16[2,64,128]{2,1,0:T(8,128)(2,1)S(1)} collective-permute-done((bf16[2,64,128]{2,1,0:T(8,128)(2,1)S(1)}, bf16[2,64,128]{2,1,0:T(8,128)(2,1)S(1)}, u32[]{:S(2)}, u32[]{:S(2)}) %collective-permute-start.8) | collective-permute-done | bytes 32800 | tf_op jit(solution)/shard_map/ppermute | solution.py:309
  78.7 0.1 collective-permute-start.10
  78.7 1.6 %collective-permute-start.11 = (f32[64,128]{1,0:T(8,128)S(1)}, f32[64,128]{1,0:T(8,128)S(1)}, u32[]{:S(2)}, u32[]{:S(2)}) collective-permute-start(f32[64,128]{1,0:T(8,128)S(1)} %get-tuple-element.23), channel_id=1, source_target_pairs={{0,6},{1,7},{2,4},{3,5},{4,2},{5,3},{6,0},{7,1},{8,14},{9,15},{10,... | collective-permute-start | bytes 98312 | tf_op jit(solution)/shard_map/ppermute | solution.py:309
  80.3 1.3 %collective-permute-start.12 = (f32[64,128]{1,0:T(8,128)S(1)}, f32[64,128]{1,0:T(8,128)S(1)}, u32[]{:S(2)}, u32[]{:S(2)}) collective-permute-start(f32[64,128]{1,0:T(8,128)S(1)} %get-tuple-element.23), channel_id=1, source_target_pairs={{0,5},{1,4},{2,7},{3,6},{4,1},{5,0},{6,3},{7,2},{8,13},{9,12},{10,... | collective-permute-start | bytes 98312 | tf_op jit(solution)/shard_map/ppermute | solution.py:309
  81.6 1.5 %collective-permute-start.13 = (f32[64,128]{1,0:T(8,128)S(1)}, f32[64,128]{1,0:T(8,128)S(1)}, u32[]{:S(2)}, u32[]{:S(2)}) collective-permute-start(f32[64,128]{1,0:T(8,128)S(1)} %get-tuple-element.23), channel_id=1, source_target_pairs={{0,4},{1,5},{2,6},{3,7},{4,0},{5,1},{6,2},{7,3},{8,12},{9,13},{10,... | collective-permute-start | bytes 98312 | tf_op jit(solution)/shard_map/ppermute | solution.py:309
  83.1 0.0 collective-permute-start.14
  83.1 0.0 collective-permute-done.10
  83.1 1.5 %collective-permute-start.15 = (f32[64,128]{1,0:T(8,128)S(1)}, f32[64,128]{1,0:T(8,128)S(1)}, u32[]{:S(2)}, u32[]{:S(2)}) collective-permute-start(f32[64,128]{1,0:T(8,128)S(1)} %get-tuple-element.24), channel_id=1, source_target_pairs={{0,2},{1,3},{2,0},{3,1},{4,6},{5,7},{6,4},{7,5},{8,10},{9,11},{10,... | collective-permute-start | bytes 98312 | tf_op jit(solution)/shard_map/ppermute | solution.py:309
  84.7 0.3 collective-permute-start.16
  85.0 0.0 collective-permute-done.12
  85.0 0.6 collective-permute-done.13
  85.5 1.2 %collective-permute-done.14 = f32[64,128]{1,0:T(8,128)S(1)} collective-permute-done((f32[64,128]{1,0:T(8,128)S(1)}, f32[64,128]{1,0:T(8,128)S(1)}, u32[]{:S(2)}, u32[]{:S(2)}) %collective-permute-start.14) | collective-permute-done | bytes 32800 | tf_op jit(solution)/shard_map/ppermute | solution.py:309
  86.7 0.4 collective-permute-done.15
  87.2 0.6 add_bitcast_fusion
  (19 shorter events, 0.1 us)
Async XLA Ops:
  0.0 8.5 %copy-start = (bf16[1,128,12288]{2,1,0:T(8,128)(2,1)S(1)}, bf16[1,128,12288]{2,1,0:T(8,128)(2,1)}, u32[]{:S(2)}) copy-start(bf16[1,128,12288]{2,1,0:T(8,128)(2,1)} %qkv_ref.15) | copy-start | bytes 9437188
  2.4 14.8 %collective-permute-start.2 = (bf16[128,1280]{1,0:T(8,128)(2,1)}, bf16[128,1280]{1,0:T(8,128)(2,1)S(1)}, u32[]{:S(2)}, u32[]{:S(2)}) collective-permute-start(bf16[128,1280]{1,0:T(8,128)(2,1)} %pack.10), channel_id=1, source_target_pairs={{0,28},{4,24},{8,20},{12,16},{16,12},{20,8},{24,4},{28,0},{1,29},{... | collective-permute-start | bytes 983048 | tf_op jit(solution)/shard_map/ppermute | solution.py:309
  8.5 1.2 %copy-start.1 = (bf16[2,4096,64]{1,2,0:T(8,128)(2,1)S(1)}, bf16[2,4096,64]{1,2,0:T(8,128)(2,1)}, u32[]{:S(2)}) copy-start(bf16[2,4096,64]{1,2,0:T(8,128)(2,1)} %param.6) | copy-start | bytes 3145732
  10.5 17.5 %collective-permute-start.4 = (bf16[128,1280]{1,0:T(8,128)(2,1)S(1)}, bf16[128,1280]{1,0:T(8,128)(2,1)S(1)}, u32[]{:S(2)}, u32[]{:S(2)}) collective-permute-start(bf16[128,1280]{1,0:T(8,128)(2,1)S(1)} %pack.12), channel_id=1, source_target_pairs={{0,12},{4,8},{8,4},{12,0},{16,28},{20,24},{24,20},{28,16},{1,13},{... | collective-permute-start | bytes 983048 | tf_op jit(solution)/shard_map/ppermute | solution.py:309
  11.4 25.4 %collective-permute-start = (bf16[128,1280]{1,0:T(8,128)(2,1)S(1)}, bf16[128,1280]{1,0:T(8,128)(2,1)S(1)}, u32[]{:S(2)}, u32[]{:S(2)}) collective-permute-start(bf16[128,1280]{1,0:T(8,128)(2,1)S(1)} %pack.8), channel_id=1, source_target_pairs={{0,24},{4,28},{8,16},{12,20},{16,8},{20,12},{24,0},{28,4},{1,25},{... | collective-permute-start | bytes 983048 | tf_op jit(solution)/shard_map/ppermute | solution.py:309
  17.3 17.9 %copy-start.3 = (bf16[128,1280]{1,0:T(8,128)(2,1)}, bf16[128,1280]{1,0:T(8,128)(2,1)S(1)}, u32[]{:S(2)}) copy-start(bf16[128,1280]{1,0:T(8,128)(2,1)S(1)} %collective-permute-done.2.refs_0_.refs_1_.refs_5_) | copy-start | bytes 983044
  29.5 16.0 %collective-permute-start.6 = (bf16[128,1280]{1,0:T(8,128)(2,1)}, bf16[128,1280]{1,0:T(8,128)(2,1)}, u32[]{:S(2)}, u32[]{:S(2)}) collective-permute-start(bf16[128,1280]{1,0:T(8,128)(2,1)} %pack.15), channel_id=1, source_target_pairs={{0,8},{4,12},{8,0},{12,4},{16,24},{20,28},{24,16},{28,20},{1,9},{5... | collective-permute-start | bytes 983048 | tf_op jit(solution)/shard_map/ppermute | solution.py:309
  33.8 11.8 %collective-permute-start.5 = (bf16[128,1280]{1,0:T(8,128)(2,1)}, bf16[128,1280]{1,0:T(8,128)(2,1)}, u32[]{:S(2)}, u32[]{:S(2)}) collective-permute-start(bf16[128,1280]{1,0:T(8,128)(2,1)} %pack.14), channel_id=1, source_target_pairs={{0,4},{4,0},{8,12},{12,8},{16,20},{20,16},{24,28},{28,24},{1,5},{5... | collective-permute-start | bytes 983048 | tf_op jit(solution)/shard_map/ppermute | solution.py:309
  36.7 25.7 %collective-permute-start.3 = (bf16[128,1280]{1,0:T(8,128)(2,1)}, bf16[128,1280]{1,0:T(8,128)(2,1)}, u32[]{:S(2)}, u32[]{:S(2)}) collective-permute-start(bf16[128,1280]{1,0:T(8,128)(2,1)} %pack.11), channel_id=1, source_target_pairs={{0,20},{4,16},{8,28},{12,24},{16,4},{20,0},{24,12},{28,8},{1,21},{... | collective-permute-start | bytes 983048 | tf_op jit(solution)/shard_map/ppermute | solution.py:309
  36.8 1.6 %copy-start.5 = (bf16[128,1280]{1,0:T(8,128)(2,1)}, bf16[128,1280]{1,0:T(8,128)(2,1)S(1)}, u32[]{:S(2)}) copy-start(bf16[128,1280]{1,0:T(8,128)(2,1)S(1)} %collective-permute-done.refs_0_.refs_4_) | copy-start | bytes 983044
  38.4 7.1 %copy-start.7 = (s32[4]{0:T(128)S(1)}, s32[4]{0:T(128)}, u32[]{:S(2)}) copy-start(s32[4]{0:T(128)} %frames_ref.3) | copy-start | bytes 52
  38.4 7.1 %copy-start.8 = (f32[1000]{0:T(1024)S(1)}, f32[1000]{0:T(1024)}, u32[]{:S(2)}) copy-start(f32[1000]{0:T(1024)} %step_weight_ref.1) | copy-start | bytes 12004
  38.4 7.1 %copy-start.9 = (s32[2]{0:T(128)S(1)}, s32[2]{0:T(128)}, u32[]{:S(2)}) copy-start(s32[2]{0:T(128)} %timestep_ref.1) | copy-start | bytes 28
  38.4 29.2 %collective-permute-start.1 = (bf16[128,1280]{1,0:T(8,128)(2,1)}, bf16[128,1280]{1,0:T(8,128)(2,1)}, u32[]{:S(2)}, u32[]{:S(2)}) collective-permute-start(bf16[128,1280]{1,0:T(8,128)(2,1)} %pack.9), channel_id=1, source_target_pairs={{0,16},{4,20},{8,24},{12,28},{16,0},{20,4},{24,8},{28,12},{1,17},{... | collective-permute-start | bytes 983048 | tf_op jit(solution)/shard_map/ppermute | solution.py:309
  43.5 1.2 %copy-start.2 = (bf16[2,4096,64]{1,2,0:T(8,128)(2,1)S(1)}, bf16[2,4096,64]{1,2,0:T(8,128)(2,1)}, u32[]{:S(2)}) copy-start(bf16[2,4096,64]{1,2,0:T(8,128)(2,1)} %param.6) | copy-start | bytes 3145732
  44.7 1.0 %copy-start.4 = (bf16[128,1280]{1,0:T(8,128)(2,1)S(1)}, bf16[128,1280]{1,0:T(8,128)(2,1)}, u32[]{:S(2)}) copy-start(bf16[128,1280]{1,0:T(8,128)(2,1)} %copy-done.3) | copy-start | bytes 983044
  44.7 1.1 %copy-start.6 = (bf16[128,1280]{1,0:T(8,128)(2,1)S(1)}, bf16[128,1280]{1,0:T(8,128)(2,1)}, u32[]{:S(2)}) copy-start(bf16[128,1280]{1,0:T(8,128)(2,1)} %copy-done.5) | copy-start | bytes 983044
  71.6 6.0 %collective-permute-start.7 = (bf16[2,64,128]{2,1,0:T(8,128)(2,1)S(1)}, bf16[2,64,128]{2,1,0:T(8,128)(2,1)S(1)}, u32[]{:S(2)}, u32[]{:S(2)}) collective-permute-start(bf16[2,64,128]{2,1,0:T(8,128)(2,1)S(1)} %get-tuple-element.20), channel_id=1, source_target_pairs={{0,24},{4,28},{8,16},{12,20},{16,8},{20,12},{24,0},{28,4},{1,25},{... | collective-permute-start | bytes 98312 | tf_op jit(solution)/shard_map/ppermute | solution.py:309
  73.8 4.8 %collective-permute-start.8 = (bf16[2,64,128]{2,1,0:T(8,128)(2,1)S(1)}, bf16[2,64,128]{2,1,0:T(8,128)(2,1)S(1)}, u32[]{:S(2)}, u32[]{:S(2)}) collective-permute-start(bf16[2,64,128]{2,1,0:T(8,128)(2,1)S(1)} %get-tuple-element.21), channel_id=1, source_target_pairs={{0,16},{4,20},{8,24},{12,28},{16,0},{20,4},{24,8},{28,12},{1,17},{... | collective-permute-start | bytes 98312 | tf_op jit(solution)/shard_map/ppermute | solution.py:309
  73.8 4.8 %collective-permute-start.9 = (bf16[2,64,128]{2,1,0:T(8,128)(2,1)S(1)}, bf16[2,64,128]{2,1,0:T(8,128)(2,1)S(1)}, u32[]{:S(2)}, u32[]{:S(2)}) collective-permute-start(bf16[2,64,128]{2,1,0:T(8,128)(2,1)S(1)} %get-tuple-element.22), channel_id=1, source_target_pairs={{0,8},{4,12},{8,0},{12,4},{16,24},{20,28},{24,16},{28,20},{1,9},{5... | collective-permute-start | bytes 98312 | tf_op jit(solution)/shard_map/ppermute | solution.py:309
  78.7 4.5 %collective-permute-start.10 = (f32[64,128]{1,0:T(8,128)S(1)}, f32[64,128]{1,0:T(8,128)S(1)}, u32[]{:S(2)}, u32[]{:S(2)}) collective-permute-start(f32[64,128]{1,0:T(8,128)S(1)} %get-tuple-element.23), channel_id=1, source_target_pairs={{0,7},{1,6},{2,5},{3,4},{4,3},{5,2},{6,1},{7,0},{8,15},{9,14},{10,... | collective-permute-start | bytes 98312 | tf_op jit(solution)/shard_map/ppermute | solution.py:309
  78.7 5.9 %collective-permute-start.11 = (f32[64,128]{1,0:T(8,128)S(1)}, f32[64,128]{1,0:T(8,128)S(1)}, u32[]{:S(2)}, u32[]{:S(2)}) collective-permute-start(f32[64,128]{1,0:T(8,128)S(1)} %get-tuple-element.23), channel_id=1, source_target_pairs={{0,6},{1,7},{2,4},{3,5},{4,2},{5,3},{6,0},{7,1},{8,14},{9,15},{10,... | collective-permute-start | bytes 98312 | tf_op jit(solution)/shard_map/ppermute | solution.py:309
  80.3 4.7 %collective-permute-start.12 = (f32[64,128]{1,0:T(8,128)S(1)}, f32[64,128]{1,0:T(8,128)S(1)}, u32[]{:S(2)}, u32[]{:S(2)}) collective-permute-start(f32[64,128]{1,0:T(8,128)S(1)} %get-tuple-element.23), channel_id=1, source_target_pairs={{0,5},{1,4},{2,7},{3,6},{4,1},{5,0},{6,3},{7,2},{8,13},{9,12},{10,... | collective-permute-start | bytes 98312 | tf_op jit(solution)/shard_map/ppermute | solution.py:309
  81.6 3.9 %collective-permute-start.13 = (f32[64,128]{1,0:T(8,128)S(1)}, f32[64,128]{1,0:T(8,128)S(1)}, u32[]{:S(2)}, u32[]{:S(2)}) collective-permute-start(f32[64,128]{1,0:T(8,128)S(1)} %get-tuple-element.23), channel_id=1, source_target_pairs={{0,4},{1,5},{2,6},{3,7},{4,0},{5,1},{6,2},{7,3},{8,12},{9,13},{10,... | collective-permute-start | bytes 98312 | tf_op jit(solution)/shard_map/ppermute | solution.py:309
  83.1 3.6 %collective-permute-start.14 = (f32[64,128]{1,0:T(8,128)S(1)}, f32[64,128]{1,0:T(8,128)S(1)}, u32[]{:S(2)}, u32[]{:S(2)}) collective-permute-start(f32[64,128]{1,0:T(8,128)S(1)} %get-tuple-element.24), channel_id=1, source_target_pairs={{0,3},{1,2},{2,1},{3,0},{4,7},{5,6},{6,5},{7,4},{8,11},{9,10},{10,... | collective-permute-start | bytes 98312 | tf_op jit(solution)/shard_map/ppermute | solution.py:309
  83.1 4.0 %collective-permute-start.15 = (f32[64,128]{1,0:T(8,128)S(1)}, f32[64,128]{1,0:T(8,128)S(1)}, u32[]{:S(2)}, u32[]{:S(2)}) collective-permute-start(f32[64,128]{1,0:T(8,128)S(1)} %get-tuple-element.24), channel_id=1, source_target_pairs={{0,2},{1,3},{2,0},{3,1},{4,6},{5,7},{6,4},{7,5},{8,10},{9,11},{10,... | collective-permute-start | bytes 98312 | tf_op jit(solution)/shard_map/ppermute | solution.py:309
  84.7 2.5 %collective-permute-start.16 = (f32[64,128]{1,0:T(8,128)S(1)}, f32[64,128]{1,0:T(8,128)S(1)}, u32[]{:S(2)}, u32[]{:S(2)}) collective-permute-start(f32[64,128]{1,0:T(8,128)S(1)} %get-tuple-element.24), channel_id=1, source_target_pairs={{0,1},{1,0},{2,3},{3,2},{4,5},{5,4},{6,7},{7,6},{8,9},{9,8},{10,11... | collective-permute-start | bytes 98312 | tf_op jit(solution)/shard_map/ppermute | solution.py:309

commit v19 on v17

--- a/solution.py
+++ b/solution.py
@@ -327,10 +327,11 @@
     pieces = [None] * seq_count
     for n in range(half):
         k = seq_count - 1 - n
-        pieces[k] = swap(pack(me, model, qkv, readout_t, k, count, [pieces[k + 2]] if n > 1 else [], n == 0), "seq", k)
+        packed = pack(me, model, qkv, readout_t, k, count, [pieces[k + 2]] if n > 1 else [], n < 2)
+        pieces[k] = swap(packed, "seq", k)
     for k in range(half - 1, 0, -1):
         after = [] if k == half - 1 else [pieces[k + 1], pieces[seq_count - 1]] if k > 1 else [pieces[half - 1]]
-        pieces[k] = swap(pack(me, model, qkv, readout_t, k, count, after), "seq", k)
+        pieces[k] = swap(pack(me, model, qkv, readout_t, k, count, after, k == half - 1), "seq", k)
     pieces[0] = pack(me, model, qkv, readout_t, 0, count, [pieces[half - 1]])
     late = [half, half + 1]
     early = [k for k in range(seq_count) if k not in late]

time: 87.6 us -> 87.5 us (level)
  Pallas kernels: 20.7 us -> 23.7 us
  waiting for transfers between devices: 39.9 us -> 37.9 us
  starting transfers between devices: 23.1 us -> 22 us
    pallas_call x8, Pallas kernels: 11 us -> 13.9 us  [pack(): pl.pallas_call(functools.partial(pack_kernel, k), in_specs=[SMEM, SMEM] +...]
    ppermute x14, waiting for transfers between devices: 39.9 us -> 37.9 us  [swap(): return lax.ppermute(array, axis, [(i, i ^ offset) for i in range(size)])]
    ppermute x14, starting transfers between devices: 23.1 us -> 22 us  [swap(): return lax.ppermute(array, axis, [(i, i ^ offset) for i in range(size)])]
  transfers between devices with their start and end apart: 14 -> 14, of which waited for: 9 -> 9; matrix products, arithmetic and copies ran while one was open for 0% -> 0% of each run, Pallas kernels for 16% -> 20%
where the time goes in v19:
time: 87.5 us; the launch traced here: 87.2 us
  waiting for transfers between devices  37.9 us (43%)
  Pallas kernels  23.7 us (27%)
  starting transfers between devices  22 us (25%)
  local copies, waits for them, and re-layouts  2.69 us (3%)
    ppermute x14, waiting for transfers between devices, swap(): return lax.ppermute(array, axis, [(i, i ^ offset) for i in range(size)])  37.9 us
    ppermute x14, starting transfers between devices, swap(): return lax.ppermute(array, axis, [(i, i ^ offset) for i in range(size)])  22 us
    pallas_call x8, Pallas kernels, pack(): pl.pallas_call(functools.partial(pack_kernel, k), in_specs=[SMEM, SMEM] +...  13.9 us
    pallas_call x1, Pallas kernels, attend_early(): pl.pallas_call(functools.partial(early_kernel, offsets), in_specs=[SMEM]...  5.77 us
    pallas_call x1, Pallas kernels, attend_late(): pl.pallas_call(functools.partial(late_kernel, offsets, late), in_specs=[S...  3.95 us
    unnamed x20, local copies, waits for them, and re-layouts  2.69 us
  transfers between devices with their start and end apart: 14, of which 9 were waited for; matrix products, arithmetic and copies ran while one was open for 0% of the time, Pallas kernels for 20%

profile of v19, /device:TPU:0, one launch (start us, length us, event | category | flops | bytes accessed | tf_op | source)
XLA Modules:
  0.0 87.2 jit_solution(16283295170615956319)
XLA Ops:
  0.0 2.3 %pack.10 = bf16[128,1280]{1,0:T(8,128)(2,1)} custom-call(s32[1]{0:T(128)} %bitcast.me_ref, s32[1]{0:T(128)} %bitcast.1.model_ref, bf16[1,128,12288]{2,1,0:T(8,128)(2,1)} %qkv_ref.15, bf16[2,64,4096]{2,1,0:T(8,128)(2,1)} %bitcast.9), custom_call_target="tpu_custom_call" | custom-call | bytes 655360 | tf_op jit(solution)/shard_map/pack/pallas_call | solution.py:67
  2.3 6.0 %collective-permute-start.2 = (bf16[128,1280]{1,0:T(8,128)(2,1)}, bf16[128,1280]{1,0:T(8,128)(2,1)S(1)}, u32[]{:S(2)}, u32[]{:S(2)}) collective-permute-start(bf16[128,1280]{1,0:T(8,128)(2,1)} %pack.10), channel_id=1, source_target_pairs={{0,28},{4,24},{8,20},{12,16},{16,12},{20,8},{24,4},{28,0},{1,29},{... | collective-permute-start | bytes 983048 | tf_op jit(solution)/shard_map/ppermute | solution.py:309
  8.3 2.3 %pack.12 = bf16[128,1280]{1,0:T(8,128)(2,1)} custom-call(s32[1]{0:T(128)} %bitcast.me_ref, s32[1]{0:T(128)} %bitcast.1.model_ref, bf16[1,128,12288]{2,1,0:T(8,128)(2,1)} %qkv_ref.15, bf16[2,64,4096]{2,1,0:T(8,128)(2,1)} %bitcast.10), custom_call_target="tpu_custom_call" | custom-call | bytes 655360 | tf_op jit(solution)/shard_map/pack/pallas_call | solution.py:67
  10.6 0.0 copy-start
  10.6 0.1 collective-permute-start.4
  10.7 2.4 %pack.8 = bf16[128,1280]{1,0:T(8,128)(2,1)} custom-call(s32[1]{0:T(128)} %bitcast.me_ref, s32[1]{0:T(128)} %bitcast.1.model_ref, bf16[1,128,12288]{2,1,0:T(8,128)(2,1)} %qkv_ref.15, bf16[2,64,4096]{2,1,0:T(8,128)(2,1)} %bitcast.11), custom_call_target="tpu_custom_call" | custom-call | bytes 655360 | tf_op jit(solution)/shard_map/pack/pallas_call | solution.py:67
  13.1 1.0 %collective-permute-start = (bf16[128,1280]{1,0:T(8,128)(2,1)}, bf16[128,1280]{1,0:T(8,128)(2,1)S(1)}, u32[]{:S(2)}, u32[]{:S(2)}) collective-permute-start(bf16[128,1280]{1,0:T(8,128)(2,1)} %pack.8), channel_id=1, source_target_pairs={{0,24},{4,28},{8,16},{12,20},{16,8},{20,12},{24,0},{28,4},{1,25},{... | collective-permute-start | bytes 983048 | tf_op jit(solution)/shard_map/ppermute | solution.py:309
  14.1 3.0 %collective-permute-done.2.refs_0_.refs_1_.refs_5_ = bf16[128,1280]{1,0:T(8,128)(2,1)S(1)} collective-permute-done((bf16[128,1280]{1,0:T(8,128)(2,1)}, bf16[128,1280]{1,0:T(8,128)(2,1)S(1)}, u32[]{:S(2)}, u32[]{:S(2)}) %collective-permute-start.2) | collective-permute-done | bytes 327712 | tf_op jit(solution)/shard_map/ppermute | solution.py:309
  17.1 10.8 %collective-permute-done.4.refs_0_.refs_3_ = bf16[128,1280]{1,0:T(8,128)(2,1)S(1)} collective-permute-done((bf16[128,1280]{1,0:T(8,128)(2,1)}, bf16[128,1280]{1,0:T(8,128)(2,1)S(1)}, u32[]{:S(2)}, u32[]{:S(2)}) %collective-permute-start.4) | collective-permute-done | bytes 327712 | tf_op jit(solution)/shard_map/ppermute | solution.py:309
  27.9 1.2 %copy-done.1 = bf16[2,4096,64]{1,2,0:T(8,128)(2,1)S(1)} copy-done((bf16[2,4096,64]{1,2,0:T(8,128)(2,1)S(1)}, bf16[2,4096,64]{1,2,0:T(8,128)(2,1)}, u32[]{:S(2)}) %copy-start.1) | copy-done | bytes 1048600
  29.2 1.5 %pack.15 = bf16[128,1280]{1,0:T(8,128)(2,1)} custom-call(s32[1]{0:T(128)} %bitcast.me_ref, s32[1]{0:T(128)} %bitcast.1.model_ref, bf16[1,128,12288]{2,1,0:T(8,128)(2,1)S(1)} %copy-done, bf16[2,64,4096]{2,1,0:T(8,128)(2,1)S(1)} %bitcast.12, bf16[128,1280]{1,0:T(8,128)(2,1)S(1)} %collective-permute-done.4.refs_0_.refs_3_, ...), custom_call_target="tpu_custom_call" | custom-call | bytes 655360 | tf_op jit(solution)/shard_map/pack/pallas_call | solution.py:67
  30.7 2.6 %collective-permute-start.6 = (bf16[128,1280]{1,0:T(8,128)(2,1)}, bf16[128,1280]{1,0:T(8,128)(2,1)}, u32[]{:S(2)}, u32[]{:S(2)}) collective-permute-start(bf16[128,1280]{1,0:T(8,128)(2,1)} %pack.15), channel_id=1, source_target_pairs={{0,8},{4,12},{8,0},{12,4},{16,24},{20,28},{24,16},{28,20},{1,9},{5... | collective-permute-start | bytes 983048 | tf_op jit(solution)/shard_map/ppermute | solution.py:309
  33.3 1.6 %pack.14 = bf16[128,1280]{1,0:T(8,128)(2,1)} custom-call(s32[1]{0:T(128)} %bitcast.me_ref, s32[1]{0:T(128)} %bitcast.1.model_ref, bf16[1,128,12288]{2,1,0:T(8,128)(2,1)S(1)} %copy-done, bf16[2,64,4096]{2,1,0:T(8,128)(2,1)S(1)} %bitcast.13, bf16[128,1280]{1,0:T(8,128)(2,1)S(1)} %collective-permute-done.4.refs_0_.refs_3_), custom_call_target="tpu_custom_call" | custom-call | bytes 655360 | tf_op jit(solution)/shard_map/pack/pallas_call | solution.py:67
  34.9 1.4 %collective-permute-start.5 = (bf16[128,1280]{1,0:T(8,128)(2,1)}, bf16[128,1280]{1,0:T(8,128)(2,1)}, u32[]{:S(2)}, u32[]{:S(2)}) collective-permute-start(bf16[128,1280]{1,0:T(8,128)(2,1)} %pack.14), channel_id=1, source_target_pairs={{0,4},{4,0},{8,12},{12,8},{16,20},{20,16},{24,28},{28,24},{1,5},{5... | collective-permute-start | bytes 983048 | tf_op jit(solution)/shard_map/ppermute | solution.py:309
  36.2 0.0 copy-done.3
  36.2 1.5 %pack.11 = bf16[128,1280]{1,0:T(8,128)(2,1)} custom-call(s32[1]{0:T(128)} %bitcast.me_ref, s32[1]{0:T(128)} %bitcast.1.model_ref, bf16[1,128,12288]{2,1,0:T(8,128)(2,1)S(1)} %copy-done, bf16[2,64,4096]{2,1,0:T(8,128)(2,1)S(1)} %bitcast.14, bf16[128,1280]{1,0:T(8,128)(2,1)S(1)} %collective-permute-done.2.refs_0_.refs_1_.refs_5_), custom_call_target="tpu_custom_call" | custom-call | bytes 655360 | tf_op jit(solution)/shard_map/pack/pallas_call | solution.py:67
  37.8 0.1 collective-permute-start.3
  37.9 0.0 collective-permute-done.refs_0_.refs_4_
  37.9 1.5 %pack.9 = bf16[128,1280]{1,0:T(8,128)(2,1)} custom-call(s32[1]{0:T(128)} %bitcast.me_ref, s32[1]{0:T(128)} %bitcast.1.model_ref, bf16[1,128,12288]{2,1,0:T(8,128)(2,1)S(1)} %copy-done, bf16[2,64,4096]{2,1,0:T(8,128)(2,1)S(1)} %bitcast.15, bf16[128,1280]{1,0:T(8,128)(2,1)S(1)} %collective-permute-done.refs_0_.refs_4_), custom_call_target="tpu_custom_call" | custom-call | bytes 655360 | tf_op jit(solution)/shard_map/pack/pallas_call | solution.py:67
  39.4 0.0 copy-start.7
  39.5 0.0 copy-start.8
  39.5 0.0 copy-start.9
  39.5 3.8 %collective-permute-start.1 = (bf16[128,1280]{1,0:T(8,128)(2,1)}, bf16[128,1280]{1,0:T(8,128)(2,1)}, u32[]{:S(2)}, u32[]{:S(2)}) collective-permute-start(bf16[128,1280]{1,0:T(8,128)(2,1)} %pack.9), channel_id=1, source_target_pairs={{0,16},{4,20},{8,24},{12,28},{16,0},{20,4},{24,8},{28,12},{1,17},{... | collective-permute-start | bytes 983048 | tf_op jit(solution)/shard_map/ppermute | solution.py:309
  43.3 1.2 %copy-done.2 = bf16[2,4096,64]{1,2,0:T(8,128)(2,1)S(1)} copy-done((bf16[2,4096,64]{1,2,0:T(8,128)(2,1)S(1)}, bf16[2,4096,64]{1,2,0:T(8,128)(2,1)}, u32[]{:S(2)}) %copy-start.2) | copy-done | bytes 1048600
  44.5 0.8 pack.13.refs_0_
  45.3 0.0 collective-permute-done.6.refs_2_
  45.3 0.0 collective-permute-done.5.refs_1_
  45.4 0.1 copy-done.4
  45.5 0.1 copy-done.6
  45.6 5.8 %attend_early.1 = (f32[4,64,768]{2,1,0:T(8,128)S(1)}, f32[2,8,768]{2,1,0:T(8,128)S(1)}, f32[8,128]{1,0:T(8,128)S(1)}, bf16[6,128,1280]{2,1,0:T(8,128)(2,1)S(1)}, bf16[4,80,768]{2,1,0:T(8,128)(2,1)S(1)}) custom-call(s32[4]{0:T(128)S(1)} %copy-done.7, s32[1]{0:T(128)} %bitcast.me_ref, s32[2]{0:T(128)S(1)} %copy-done.9, f32[1000]{0:T(1024)S(1)} %copy-done.8, ...), custom_call_target="tpu_custom_call" | custom-call | flops 905969664 | bytes 2359296 | tf_op jit(solution)/shard_map/attend_early/pallas_call | solution.py:256
  51.4 10.9 %collective-permute-done.3.refs_1_ = bf16[128,1280]{1,0:T(8,128)(2,1)} collective-permute-done((bf16[128,1280]{1,0:T(8,128)(2,1)}, bf16[128,1280]{1,0:T(8,128)(2,1)}, u32[]{:S(2)}, u32[]{:S(2)}) %collective-permute-start.3) | collective-permute-done | bytes 327712 | tf_op jit(solution)/shard_map/ppermute | solution.py:309
  62.2 5.2 %collective-permute-done.1.refs_0_ = bf16[128,1280]{1,0:T(8,128)(2,1)} collective-permute-done((bf16[128,1280]{1,0:T(8,128)(2,1)}, bf16[128,1280]{1,0:T(8,128)(2,1)}, u32[]{:S(2)}, u32[]{:S(2)}) %collective-permute-start.1) | collective-permute-done | bytes 327712 | tf_op jit(solution)/shard_map/ppermute | solution.py:309
  67.5 3.9 %attend_late.1 = (f32[2,64,128]{2,1,0:T(8,128)S(1)}, bf16[2,64,128]{2,1,0:T(8,128)(2,1)S(1)}, bf16[2,64,128]{2,1,0:T(8,128)(2,1)S(1)}, bf16[2,64,128]{2,1,0:T(8,128)(2,1)S(1)}) custom-call(s32[4]{0:T(128)S(1)} %copy-done.7, s32[1]{0:T(128)} %bitcast.me_ref, bf16[128,1280]{1,0:T(8,128)(2,1)} %collective-permute-done.1.refs_0_, ...), custom_call_target="tpu_custom_call" | custom-call | flops 402653184 | bytes 3145728 | tf_op jit(solution)/shard_map/attend_late/pallas_call | solution.py:285
  71.4 2.2 %collective-permute-start.7 = (bf16[2,64,128]{2,1,0:T(8,128)(2,1)S(1)}, bf16[2,64,128]{2,1,0:T(8,128)(2,1)S(1)}, u32[]{:S(2)}, u32[]{:S(2)}) collective-permute-start(bf16[2,64,128]{2,1,0:T(8,128)(2,1)S(1)} %get-tuple-element.20), channel_id=1, source_target_pairs={{0,24},{4,28},{8,16},{12,20},{16,8},{20,12},{24,0},{28,4},{1,25},{... | collective-permute-start | bytes 98312 | tf_op jit(solution)/shard_map/ppermute | solution.py:309
  73.7 0.0 collective-permute-start.8
  73.7 2.2 %collective-permute-start.9 = (bf16[2,64,128]{2,1,0:T(8,128)(2,1)S(1)}, bf16[2,64,128]{2,1,0:T(8,128)(2,1)S(1)}, u32[]{:S(2)}, u32[]{:S(2)}) collective-permute-start(bf16[2,64,128]{2,1,0:T(8,128)(2,1)S(1)} %get-tuple-element.22), channel_id=1, source_target_pairs={{0,8},{4,12},{8,0},{12,4},{16,24},{20,28},{24,16},{28,20},{1,9},{5... | collective-permute-start | bytes 98312 | tf_op jit(solution)/shard_map/ppermute | solution.py:309
  75.9 1.5 %collective-permute-done.7 = bf16[2,64,128]{2,1,0:T(8,128)(2,1)S(1)} collective-permute-done((bf16[2,64,128]{2,1,0:T(8,128)(2,1)S(1)}, bf16[2,64,128]{2,1,0:T(8,128)(2,1)S(1)}, u32[]{:S(2)}, u32[]{:S(2)}) %collective-permute-start.7) | collective-permute-done | bytes 32800 | tf_op jit(solution)/shard_map/ppermute | solution.py:309
  77.4 1.1 %collective-permute-done.8 = bf16[2,64,128]{2,1,0:T(8,128)(2,1)S(1)} collective-permute-done((bf16[2,64,128]{2,1,0:T(8,128)(2,1)S(1)}, bf16[2,64,128]{2,1,0:T(8,128)(2,1)S(1)}, u32[]{:S(2)}, u32[]{:S(2)}) %collective-permute-start.8) | collective-permute-done | bytes 32800 | tf_op jit(solution)/shard_map/ppermute | solution.py:309
  78.5 0.0 collective-permute-done.9
  78.5 0.7 collective-permute-start.10
  79.2 3.2 %collective-permute-done.10 = f32[1,64,128]{2,1,0:T(8,128)S(1)} collective-permute-done((f32[1,64,128]{2,1,0:T(8,128)S(1)}, f32[1,64,128]{2,1,0:T(8,128)S(1)}, u32[]{:S(2)}, u32[]{:S(2)}) %collective-permute-start.10) | collective-permute-done | bytes 32800 | tf_op jit(solution)/shard_map/ppermute | solution.py:309
  82.5 0.0 collective-permute-start.11
  82.5 1.6 %collective-permute-start.12 = (f32[64,128]{1,0:T(8,128)S(1)}, f32[64,128]{1,0:T(8,128)S(1)}, u32[]{:S(2)}, u32[]{:S(2)}) collective-permute-start(f32[64,128]{1,0:T(8,128)S(1)} %fusion), channel_id=1, source_target_pairs={{0,2},{1,3},{2,0},{3,1},{4,6},{5,7},{6,4},{7,5},{8,10},{9,11},{10,... | collective-permute-start | bytes 98312 | tf_op jit(solution)/shard_map/ppermute | solution.py:309
  84.1 0.3 collective-permute-start.13
  84.4 1.8 %collective-permute-done.11 = f32[64,128]{1,0:T(8,128)S(1)} collective-permute-done((f32[64,128]{1,0:T(8,128)S(1)}, f32[64,128]{1,0:T(8,128)S(1)}, u32[]{:S(2)}, u32[]{:S(2)}) %collective-permute-start.11) | collective-permute-done | bytes 32800 | tf_op jit(solution)/shard_map/ppermute | solution.py:309
  86.1 0.4 collective-permute-done.12
  86.5 0.0 collective-permute-done.13
  86.5 0.6 add_bitcast_fusion
  (14 shorter events, 0.0 us)
Async XLA Ops:
  2.3 14.8 %collective-permute-start.2 = (bf16[128,1280]{1,0:T(8,128)(2,1)}, bf16[128,1280]{1,0:T(8,128)(2,1)S(1)}, u32[]{:S(2)}, u32[]{:S(2)}) collective-permute-start(bf16[128,1280]{1,0:T(8,128)(2,1)} %pack.10), channel_id=1, source_target_pairs={{0,28},{4,24},{8,20},{12,16},{16,12},{20,8},{24,4},{28,0},{1,29},{... | collective-permute-start | bytes 983048 | tf_op jit(solution)/shard_map/ppermute | solution.py:309
  10.6 17.3 %copy-start = (bf16[1,128,12288]{2,1,0:T(8,128)(2,1)S(1)}, bf16[1,128,12288]{2,1,0:T(8,128)(2,1)}, u32[]{:S(2)}) copy-start(bf16[1,128,12288]{2,1,0:T(8,128)(2,1)} %qkv_ref.15) | copy-start | bytes 9437188
  10.6 17.3 %collective-permute-start.4 = (bf16[128,1280]{1,0:T(8,128)(2,1)}, bf16[128,1280]{1,0:T(8,128)(2,1)S(1)}, u32[]{:S(2)}, u32[]{:S(2)}) collective-permute-start(bf16[128,1280]{1,0:T(8,128)(2,1)} %pack.12), channel_id=1, source_target_pairs={{0,12},{4,8},{8,4},{12,0},{16,28},{20,24},{24,20},{28,16},{1,13},{... | collective-permute-start | bytes 983048 | tf_op jit(solution)/shard_map/ppermute | solution.py:309
  13.1 24.7 %collective-permute-start = (bf16[128,1280]{1,0:T(8,128)(2,1)}, bf16[128,1280]{1,0:T(8,128)(2,1)S(1)}, u32[]{:S(2)}, u32[]{:S(2)}) collective-permute-start(bf16[128,1280]{1,0:T(8,128)(2,1)} %pack.8), channel_id=1, source_target_pairs={{0,24},{4,28},{8,16},{12,20},{16,8},{20,12},{24,0},{28,4},{1,25},{... | collective-permute-start | bytes 983048 | tf_op jit(solution)/shard_map/ppermute | solution.py:309
  17.1 19.1 %copy-start.3 = (bf16[128,1280]{1,0:T(8,128)(2,1)}, bf16[128,1280]{1,0:T(8,128)(2,1)S(1)}, u32[]{:S(2)}) copy-start(bf16[128,1280]{1,0:T(8,128)(2,1)S(1)} %collective-permute-done.2.refs_0_.refs_1_.refs_5_) | copy-start | bytes 983044
  27.9 1.2 %copy-start.1 = (bf16[2,4096,64]{1,2,0:T(8,128)(2,1)S(1)}, bf16[2,4096,64]{1,2,0:T(8,128)(2,1)}, u32[]{:S(2)}) copy-start(bf16[2,4096,64]{1,2,0:T(8,128)(2,1)} %param.6) | copy-start | bytes 3145732
  30.7 14.6 %collective-permute-start.6 = (bf16[128,1280]{1,0:T(8,128)(2,1)}, bf16[128,1280]{1,0:T(8,128)(2,1)}, u32[]{:S(2)}, u32[]{:S(2)}) collective-permute-start(bf16[128,1280]{1,0:T(8,128)(2,1)} %pack.15), channel_id=1, source_target_pairs={{0,8},{4,12},{8,0},{12,4},{16,24},{20,28},{24,16},{28,20},{1,9},{5... | collective-permute-start | bytes 983048 | tf_op jit(solution)/shard_map/ppermute | solution.py:309
  34.9 10.5 %collective-permute-start.5 = (bf16[128,1280]{1,0:T(8,128)(2,1)}, bf16[128,1280]{1,0:T(8,128)(2,1)}, u32[]{:S(2)}, u32[]{:S(2)}) collective-permute-start(bf16[128,1280]{1,0:T(8,128)(2,1)} %pack.14), channel_id=1, source_target_pairs={{0,4},{4,0},{8,12},{12,8},{16,20},{20,16},{24,28},{28,24},{1,5},{5... | collective-permute-start | bytes 983048 | tf_op jit(solution)/shard_map/ppermute | solution.py:309
  37.8 24.5 %collective-permute-start.3 = (bf16[128,1280]{1,0:T(8,128)(2,1)}, bf16[128,1280]{1,0:T(8,128)(2,1)}, u32[]{:S(2)}, u32[]{:S(2)}) collective-permute-start(bf16[128,1280]{1,0:T(8,128)(2,1)} %pack.11), channel_id=1, source_target_pairs={{0,20},{4,16},{8,28},{12,24},{16,4},{20,0},{24,12},{28,8},{1,21},{... | collective-permute-start | bytes 983048 | tf_op jit(solution)/shard_map/ppermute | solution.py:309
  37.9 1.6 %copy-start.5 = (bf16[128,1280]{1,0:T(8,128)(2,1)}, bf16[128,1280]{1,0:T(8,128)(2,1)S(1)}, u32[]{:S(2)}) copy-start(bf16[128,1280]{1,0:T(8,128)(2,1)S(1)} %collective-permute-done.refs_0_.refs_4_) | copy-start | bytes 983044
  39.4 5.9 %copy-start.7 = (s32[4]{0:T(128)S(1)}, s32[4]{0:T(128)}, u32[]{:S(2)}) copy-start(s32[4]{0:T(128)} %frames_ref.3) | copy-start | bytes 52
  39.5 5.9 %copy-start.8 = (f32[1000]{0:T(1024)S(1)}, f32[1000]{0:T(1024)}, u32[]{:S(2)}) copy-start(f32[1000]{0:T(1024)} %step_weight_ref.1) | copy-start | bytes 12004
  39.5 5.9 %copy-start.9 = (s32[2]{0:T(128)S(1)}, s32[2]{0:T(128)}, u32[]{:S(2)}) copy-start(s32[2]{0:T(128)} %timestep_ref.1) | copy-start | bytes 28
  39.5 28.0 %collective-permute-start.1 = (bf16[128,1280]{1,0:T(8,128)(2,1)}, bf16[128,1280]{1,0:T(8,128)(2,1)}, u32[]{:S(2)}, u32[]{:S(2)}) collective-permute-start(bf16[128,1280]{1,0:T(8,128)(2,1)} %pack.9), channel_id=1, source_target_pairs={{0,16},{4,20},{8,24},{12,28},{16,0},{20,4},{24,8},{28,12},{1,17},{... | collective-permute-start | bytes 983048 | tf_op jit(solution)/shard_map/ppermute | solution.py:309
  43.3 1.2 %copy-start.2 = (bf16[2,4096,64]{1,2,0:T(8,128)(2,1)S(1)}, bf16[2,4096,64]{1,2,0:T(8,128)(2,1)}, u32[]{:S(2)}) copy-start(bf16[2,4096,64]{1,2,0:T(8,128)(2,1)} %param.6) | copy-start | bytes 3145732
  44.5 1.0 %copy-start.4 = (bf16[128,1280]{1,0:T(8,128)(2,1)S(1)}, bf16[128,1280]{1,0:T(8,128)(2,1)}, u32[]{:S(2)}) copy-start(bf16[128,1280]{1,0:T(8,128)(2,1)} %copy-done.3) | copy-start | bytes 983044
  44.5 1.1 %copy-start.6 = (bf16[128,1280]{1,0:T(8,128)(2,1)S(1)}, bf16[128,1280]{1,0:T(8,128)(2,1)}, u32[]{:S(2)}) copy-start(bf16[128,1280]{1,0:T(8,128)(2,1)} %copy-done.5) | copy-start | bytes 983044
  71.4 6.0 %collective-permute-start.7 = (bf16[2,64,128]{2,1,0:T(8,128)(2,1)S(1)}, bf16[2,64,128]{2,1,0:T(8,128)(2,1)S(1)}, u32[]{:S(2)}, u32[]{:S(2)}) collective-permute-start(bf16[2,64,128]{2,1,0:T(8,128)(2,1)S(1)} %get-tuple-element.20), channel_id=1, source_target_pairs={{0,24},{4,28},{8,16},{12,20},{16,8},{20,12},{24,0},{28,4},{1,25},{... | collective-permute-start | bytes 98312 | tf_op jit(solution)/shard_map/ppermute | solution.py:309
  73.7 4.8 %collective-permute-start.8 = (bf16[2,64,128]{2,1,0:T(8,128)(2,1)S(1)}, bf16[2,64,128]{2,1,0:T(8,128)(2,1)S(1)}, u32[]{:S(2)}, u32[]{:S(2)}) collective-permute-start(bf16[2,64,128]{2,1,0:T(8,128)(2,1)S(1)} %get-tuple-element.21), channel_id=1, source_target_pairs={{0,16},{4,20},{8,24},{12,28},{16,0},{20,4},{24,8},{28,12},{1,17},{... | collective-permute-start | bytes 98312 | tf_op jit(solution)/shard_map/ppermute | solution.py:309
  73.7 4.8 %collective-permute-start.9 = (bf16[2,64,128]{2,1,0:T(8,128)(2,1)S(1)}, bf16[2,64,128]{2,1,0:T(8,128)(2,1)S(1)}, u32[]{:S(2)}, u32[]{:S(2)}) collective-permute-start(bf16[2,64,128]{2,1,0:T(8,128)(2,1)S(1)} %get-tuple-element.22), channel_id=1, source_target_pairs={{0,8},{4,12},{8,0},{12,4},{16,24},{20,28},{24,16},{28,20},{1,9},{5... | collective-permute-start | bytes 98312 | tf_op jit(solution)/shard_map/ppermute | solution.py:309
  78.5 4.0 %collective-permute-start.10 = (f32[1,64,128]{2,1,0:T(8,128)S(1)}, f32[1,64,128]{2,1,0:T(8,128)S(1)}, u32[]{:S(2)}, u32[]{:S(2)}) collective-permute-start(f32[1,64,128]{2,1,0:T(8,128)S(1)} %slice.9), channel_id=1, source_target_pairs={{0,4},{4,0},{8,12},{12,8},{16,20},{20,16},{24,28},{28,24},{1,5},{5... | collective-permute-start | bytes 98312 | tf_op jit(solution)/shard_map/ppermute | solution.py:309
  82.5 3.6 %collective-permute-start.11 = (f32[64,128]{1,0:T(8,128)S(1)}, f32[64,128]{1,0:T(8,128)S(1)}, u32[]{:S(2)}, u32[]{:S(2)}) collective-permute-start(f32[64,128]{1,0:T(8,128)S(1)} %fusion), channel_id=1, source_target_pairs={{0,3},{1,2},{2,1},{3,0},{4,7},{5,6},{6,5},{7,4},{8,11},{9,10},{10,... | collective-permute-start | bytes 98312 | tf_op jit(solution)/shard_map/ppermute | solution.py:309
  82.5 4.0 %collective-permute-start.12 = (f32[64,128]{1,0:T(8,128)S(1)}, f32[64,128]{1,0:T(8,128)S(1)}, u32[]{:S(2)}, u32[]{:S(2)}) collective-permute-start(f32[64,128]{1,0:T(8,128)S(1)} %fusion), channel_id=1, source_target_pairs={{0,2},{1,3},{2,0},{3,1},{4,6},{5,7},{6,4},{7,5},{8,10},{9,11},{10,... | collective-permute-start | bytes 98312 | tf_op jit(solution)/shard_map/ppermute | solution.py:309
  84.1 2.5 %collective-permute-start.13 = (f32[64,128]{1,0:T(8,128)S(1)}, f32[64,128]{1,0:T(8,128)S(1)}, u32[]{:S(2)}, u32[]{:S(2)}) collective-permute-start(f32[64,128]{1,0:T(8,128)S(1)} %fusion), channel_id=1, source_target_pairs={{0,1},{1,0},{2,3},{3,2},{4,5},{5,4},{6,7},{7,6},{8,9},{9,8},{10,11... | collective-permute-start | bytes 98312 | tf_op jit(solution)/shard_map/ppermute | solution.py:309

commit v20 on v17

--- a/solution.py
+++ b/solution.py
@@ -162,12 +162,11 @@
     for i in range(count):
         for b, read in enumerate(pairs_of(pieces, i, 0)):
             asked[b, i] = read()
-    half = count_pieces // 2 + 1
 
     def some_blocks(b, carry):
         q = [2 * b, 2 * b + 1]
         span = pl.ds(pl.multiple_of(b * 2 * rows, 2 * rows), 2 * rows)
-        shifts = mask_rows(frames_ref, me, rows, [jnp.where(n < half, n, n + 2) for n in q], offsets)
+        shifts = mask_rows(frames_ref, me, rows, [sum(jnp.where(n == j, k, 0) for j, k in enumerate(offsets)) for n in q], offsets)
         peaks, totals, units = [], [], []
         for i in range(count):
 
@@ -325,14 +324,15 @@
     readout_t = jnp.swapaxes(readout, 1, 2)
 
     pieces = [None] * seq_count
-    for n in range(half):
-        k = seq_count - 1 - n
-        pieces[k] = swap(pack(me, model, qkv, readout_t, k, count, [pieces[k + 2]] if n > 1 else [], n == 0), "seq", k)
+    tops = [seq_count - 1, half] + list(range(seq_count - 2, half, -1))
+    for n, k in enumerate(tops):
+        after = [pieces[tops[n - 2]]] if n > 1 else []
+        pieces[k] = swap(pack(me, model, qkv, readout_t, k, count, after, n == 0), "seq", k)
     for k in range(half - 1, 0, -1):
-        after = [] if k == half - 1 else [pieces[k + 1], pieces[seq_count - 1]] if k > 1 else [pieces[half - 1]]
+        after = [] if k == half - 1 else [pieces[k + 1], pieces[tops[0]]] if k > 1 else [pieces[half - 1]]
         pieces[k] = swap(pack(me, model, qkv, readout_t, k, count, after), "seq", k)
     pieces[0] = pack(me, model, qkv, readout_t, 0, count, [pieces[half - 1]])
-    late = [half, half + 1]
+    late = sorted(tops[-2:])
     early = [k for k in range(seq_count) if k not in late]
     merged = attend_early(
         [pieces[k] for k in early], early, span_frames, me, timestep, step_weight, sign, sample, count, lat

time: 87.6 us -> 87.4 us (level)
  waiting for transfers between devices: 39.9 us -> 44.2 us
  starting transfers between devices: 23.1 us -> 18.9 us
    ppermute x14, waiting for transfers between devices: 39.9 us -> 44.2 us  [swap(): return lax.ppermute(array, axis, [(i, i ^ offset) for i in range(size)])]
    ppermute x14, starting transfers between devices: 23.1 us -> 18.9 us  [swap(): return lax.ppermute(array, axis, [(i, i ^ offset) for i in range(size)])]
  transfers between devices with their start and end apart: 14 -> 14, of which waited for: 9 -> 10; matrix products, arithmetic and copies ran while one was open for 0% -> 0% of each run, Pallas kernels for 16% -> 16%
where the time goes in v20:
time: 87.4 us; the launch traced here: 87.2 us
  waiting for transfers between devices  44.2 us (51%)
  Pallas kernels  20.8 us (24%)
  starting transfers between devices  18.9 us (22%)
  local copies, waits for them, and re-layouts  2.49 us (3%)
    ppermute x14, waiting for transfers between devices, swap(): return lax.ppermute(array, axis, [(i, i ^ offset) for i in range(size)])  44.2 us
    ppermute x14, starting transfers between devices, swap(): return lax.ppermute(array, axis, [(i, i ^ offset) for i in range(size)])  18.9 us
    pallas_call x8, Pallas kernels, pack(): pl.pallas_call(functools.partial(pack_kernel, k), in_specs=[SMEM, SMEM] +...  11 us
    pallas_call x1, Pallas kernels, attend_early(): pl.pallas_call(functools.partial(early_kernel, offsets), in_specs=[SMEM]...  5.78 us
    pallas_call x1, Pallas kernels, attend_late(): pl.pallas_call(functools.partial(late_kernel, offsets, late), in_specs=[S...  3.95 us
    unnamed x20, local copies, waits for them, and re-layouts  2.48 us
  transfers between devices with their start and end apart: 14, of which 10 were waited for; matrix products, arithmetic and copies ran while one was open for 0% of the time, Pallas kernels for 16%

profile of v20, /device:TPU:0, one launch (start us, length us, event | category | flops | bytes accessed | tf_op | source)
XLA Modules:
  0.0 87.2 jit_solution(11345113902031768453)
XLA Ops:
  0.0 2.4 %pack.10 = bf16[128,1280]{1,0:T(8,128)(2,1)} custom-call(s32[1]{0:T(128)} %bitcast.me_ref, s32[1]{0:T(128)} %bitcast.1.model_ref, bf16[1,128,12288]{2,1,0:T(8,128)(2,1)} %qkv_ref.15, bf16[2,64,4096]{2,1,0:T(8,128)(2,1)} %bitcast.9), custom_call_target="tpu_custom_call" | custom-call | bytes 655360 | tf_op jit(solution)/shard_map/pack/pallas_call | solution.py:67
  2.4 6.0 %collective-permute-start.2 = (bf16[128,1280]{1,0:T(8,128)(2,1)}, bf16[128,1280]{1,0:T(8,128)(2,1)S(1)}, u32[]{:S(2)}, u32[]{:S(2)}) collective-permute-start(bf16[128,1280]{1,0:T(8,128)(2,1)} %pack.10), channel_id=1, source_target_pairs={{0,28},{4,24},{8,20},{12,16},{16,12},{20,8},{24,4},{28,0},{1,29},{... | collective-permute-start | bytes 983048 | tf_op jit(solution)/shard_map/ppermute | solution.py:308
  8.5 0.0 copy-done
  8.5 1.2 %copy-done.1 = bf16[2,4096,64]{1,2,0:T(8,128)(2,1)S(1)} copy-done((bf16[2,4096,64]{1,2,0:T(8,128)(2,1)S(1)}, bf16[2,4096,64]{1,2,0:T(8,128)(2,1)}, u32[]{:S(2)}) %copy-start.1) | copy-done | bytes 1048600
  9.7 0.8 pack.12
  10.5 0.1 collective-permute-start.4
  10.6 0.8 pack.8
  11.4 0.6 collective-permute-start
  12.0 5.2 %collective-permute-done.2.refs_0_.refs_1_.refs_5_ = bf16[128,1280]{1,0:T(8,128)(2,1)S(1)} collective-permute-done((bf16[128,1280]{1,0:T(8,128)(2,1)}, bf16[128,1280]{1,0:T(8,128)(2,1)S(1)}, u32[]{:S(2)}, u32[]{:S(2)}) %collective-permute-start.2) | collective-permute-done | bytes 327712 | tf_op jit(solution)/shard_map/ppermute | solution.py:308
  17.3 10.7 %collective-permute-done.4.refs_0_.refs_3_ = bf16[128,1280]{1,0:T(8,128)(2,1)S(1)} collective-permute-done((bf16[128,1280]{1,0:T(8,128)(2,1)S(1)}, bf16[128,1280]{1,0:T(8,128)(2,1)S(1)}, u32[]{:S(2)}, u32[]{:S(2)}) %collective-permute-start.4) | collective-permute-done | bytes 327712 | tf_op jit(solution)/shard_map/ppermute | solution.py:308
  28.0 1.5 %pack.15 = bf16[128,1280]{1,0:T(8,128)(2,1)} custom-call(s32[1]{0:T(128)} %bitcast.me_ref, s32[1]{0:T(128)} %bitcast.1.model_ref, bf16[1,128,12288]{2,1,0:T(8,128)(2,1)S(1)} %copy-done, bf16[2,64,4096]{2,1,0:T(8,128)(2,1)S(1)} %bitcast.12, bf16[128,1280]{1,0:T(8,128)(2,1)S(1)} %collective-permute-done.4.refs_0_.refs_3_, ...), custom_call_target="tpu_custom_call" | custom-call | bytes 655360 | tf_op jit(solution)/shard_map/pack/pallas_call | solution.py:67
  29.5 2.7 %collective-permute-start.6 = (bf16[128,1280]{1,0:T(8,128)(2,1)}, bf16[128,1280]{1,0:T(8,128)(2,1)}, u32[]{:S(2)}, u32[]{:S(2)}) collective-permute-start(bf16[128,1280]{1,0:T(8,128)(2,1)} %pack.15), channel_id=1, source_target_pairs={{0,8},{4,12},{8,0},{12,4},{16,24},{20,28},{24,16},{28,20},{1,9},{5... | collective-permute-start | bytes 983048 | tf_op jit(solution)/shard_map/ppermute | solution.py:308
  32.2 1.6 %pack.14 = bf16[128,1280]{1,0:T(8,128)(2,1)} custom-call(s32[1]{0:T(128)} %bitcast.me_ref, s32[1]{0:T(128)} %bitcast.1.model_ref, bf16[1,128,12288]{2,1,0:T(8,128)(2,1)S(1)} %copy-done, bf16[2,64,4096]{2,1,0:T(8,128)(2,1)S(1)} %bitcast.13, bf16[128,1280]{1,0:T(8,128)(2,1)S(1)} %collective-permute-done.4.refs_0_.refs_3_), custom_call_target="tpu_custom_call" | custom-call | bytes 655360 | tf_op jit(solution)/shard_map/pack/pallas_call | solution.py:67
  33.8 1.4 %collective-permute-start.5 = (bf16[128,1280]{1,0:T(8,128)(2,1)}, bf16[128,1280]{1,0:T(8,128)(2,1)}, u32[]{:S(2)}, u32[]{:S(2)}) collective-permute-start(bf16[128,1280]{1,0:T(8,128)(2,1)} %pack.14), channel_id=1, source_target_pairs={{0,4},{4,0},{8,12},{12,8},{16,20},{20,16},{24,28},{28,24},{1,5},{5... | collective-permute-start | bytes 983048 | tf_op jit(solution)/shard_map/ppermute | solution.py:308
  35.2 0.0 copy-done.3
  35.2 1.5 %pack.11 = bf16[128,1280]{1,0:T(8,128)(2,1)} custom-call(s32[1]{0:T(128)} %bitcast.me_ref, s32[1]{0:T(128)} %bitcast.1.model_ref, bf16[1,128,12288]{2,1,0:T(8,128)(2,1)S(1)} %copy-done, bf16[2,64,4096]{2,1,0:T(8,128)(2,1)S(1)} %bitcast.14, bf16[128,1280]{1,0:T(8,128)(2,1)S(1)} %collective-permute-done.2.refs_0_.refs_1_.refs_5_), custom_call_target="tpu_custom_call" | custom-call | bytes 655360 | tf_op jit(solution)/shard_map/pack/pallas_call | solution.py:67
  36.7 0.1 collective-permute-start.3
  36.8 4.3 %collective-permute-done.refs_0_.refs_4_ = bf16[128,1280]{1,0:T(8,128)(2,1)S(1)} collective-permute-done((bf16[128,1280]{1,0:T(8,128)(2,1)S(1)}, bf16[128,1280]{1,0:T(8,128)(2,1)S(1)}, u32[]{:S(2)}, u32[]{:S(2)}) %collective-permute-start) | collective-permute-done | bytes 327712 | tf_op jit(solution)/shard_map/ppermute | solution.py:308
  41.1 1.6 %pack.9 = bf16[128,1280]{1,0:T(8,128)(2,1)} custom-call(s32[1]{0:T(128)} %bitcast.me_ref, s32[1]{0:T(128)} %bitcast.1.model_ref, bf16[1,128,12288]{2,1,0:T(8,128)(2,1)S(1)} %copy-done, bf16[2,64,4096]{2,1,0:T(8,128)(2,1)S(1)} %bitcast.15, bf16[128,1280]{1,0:T(8,128)(2,1)S(1)} %collective-permute-done.refs_0_.refs_4_), custom_call_target="tpu_custom_call" | custom-call | bytes 655360 | tf_op jit(solution)/shard_map/pack/pallas_call | solution.py:67
  42.7 0.0 copy-done.5
  42.7 0.0 copy-start.7
  42.7 0.0 copy-start.8
  42.7 0.0 copy-start.9
  42.7 0.1 collective-permute-start.1
  42.8 0.0 copy-start.2
  42.8 1.2 %copy-done.2 = bf16[2,4096,64]{1,2,0:T(8,128)(2,1)S(1)} copy-done((bf16[2,4096,64]{1,2,0:T(8,128)(2,1)S(1)}, bf16[2,4096,64]{1,2,0:T(8,128)(2,1)}, u32[]{:S(2)}) %copy-start.2) | copy-done | bytes 1048600
  44.1 0.8 pack.13.refs_0_
  44.9 6.1 %collective-permute-done.6.refs_2_ = bf16[128,1280]{1,0:T(8,128)(2,1)} collective-permute-done((bf16[128,1280]{1,0:T(8,128)(2,1)}, bf16[128,1280]{1,0:T(8,128)(2,1)}, u32[]{:S(2)}, u32[]{:S(2)}) %collective-permute-start.6) | collective-permute-done | bytes 327712 | tf_op jit(solution)/shard_map/ppermute | solution.py:308
  51.0 0.0 collective-permute-done.5.refs_1_
  51.0 5.8 %attend_early.1 = (f32[4,64,768]{2,1,0:T(8,128)S(1)}, f32[2,8,768]{2,1,0:T(8,128)S(1)}, f32[8,128]{1,0:T(8,128)S(1)}, bf16[6,128,1280]{2,1,0:T(8,128)(2,1)S(1)}, bf16[4,80,768]{2,1,0:T(8,128)(2,1)S(1)}) custom-call(s32[4]{0:T(128)S(1)} %copy-done.7, s32[1]{0:T(128)} %bitcast.me_ref, s32[2]{0:T(128)S(1)} %copy-done.9, f32[1000]{0:T(1024)S(1)} %copy-done.8, ...), custom_call_target="tpu_custom_call" | custom-call | flops 905969664 | bytes 2359296 | tf_op jit(solution)/shard_map/attend_early/pallas_call | solution.py:255
  56.8 0.0 collective-permute-done.3.refs_1_
  56.8 10.9 %collective-permute-done.1.refs_0_ = bf16[128,1280]{1,0:T(8,128)(2,1)} collective-permute-done((bf16[128,1280]{1,0:T(8,128)(2,1)}, bf16[128,1280]{1,0:T(8,128)(2,1)}, u32[]{:S(2)}, u32[]{:S(2)}) %collective-permute-start.1) | collective-permute-done | bytes 327712 | tf_op jit(solution)/shard_map/ppermute | solution.py:308
  67.7 4.0 %attend_late.1 = (f32[2,64,128]{2,1,0:T(8,128)S(1)}, bf16[2,64,128]{2,1,0:T(8,128)(2,1)S(1)}, bf16[2,64,128]{2,1,0:T(8,128)(2,1)S(1)}, bf16[2,64,128]{2,1,0:T(8,128)(2,1)S(1)}) custom-call(s32[4]{0:T(128)S(1)} %copy-done.7, s32[1]{0:T(128)} %bitcast.me_ref, bf16[128,1280]{1,0:T(8,128)(2,1)} %collective-permute-done.1.refs_0_, ...), custom_call_target="tpu_custom_call" | custom-call | flops 402653184 | bytes 3145728 | tf_op jit(solution)/shard_map/attend_late/pallas_call | solution.py:284
  71.7 2.1 %collective-permute-start.7 = (bf16[2,64,128]{2,1,0:T(8,128)(2,1)S(1)}, bf16[2,64,128]{2,1,0:T(8,128)(2,1)S(1)}, u32[]{:S(2)}, u32[]{:S(2)}) collective-permute-start(bf16[2,64,128]{2,1,0:T(8,128)(2,1)S(1)} %get-tuple-element.20), channel_id=1, source_target_pairs={{0,24},{4,28},{8,16},{12,20},{16,8},{20,12},{24,0},{28,4},{1,25},{... | collective-permute-start | bytes 98312 | tf_op jit(solution)/shard_map/ppermute | solution.py:308
  73.7 0.0 collective-permute-start.8
  73.7 2.4 %collective-permute-start.9 = (bf16[2,64,128]{2,1,0:T(8,128)(2,1)S(1)}, bf16[2,64,128]{2,1,0:T(8,128)(2,1)S(1)}, u32[]{:S(2)}, u32[]{:S(2)}) collective-permute-start(bf16[2,64,128]{2,1,0:T(8,128)(2,1)S(1)} %get-tuple-element.22), channel_id=1, source_target_pairs={{0,8},{4,12},{8,0},{12,4},{16,24},{20,28},{24,16},{28,20},{1,9},{5... | collective-permute-start | bytes 98312 | tf_op jit(solution)/shard_map/ppermute | solution.py:308
  76.1 1.7 %collective-permute-done.7 = bf16[2,64,128]{2,1,0:T(8,128)(2,1)S(1)} collective-permute-done((bf16[2,64,128]{2,1,0:T(8,128)(2,1)S(1)}, bf16[2,64,128]{2,1,0:T(8,128)(2,1)S(1)}, u32[]{:S(2)}, u32[]{:S(2)}) %collective-permute-start.7) | collective-permute-done | bytes 32800 | tf_op jit(solution)/shard_map/ppermute | solution.py:308
  77.8 0.8 collective-permute-done.8
  78.5 0.0 collective-permute-done.9
  78.6 1.6 %collective-permute-start.10 = (f32[1,64,128]{2,1,0:T(8,128)S(1)}, f32[1,64,128]{2,1,0:T(8,128)S(1)}, u32[]{:S(2)}, u32[]{:S(2)}) collective-permute-start(f32[1,64,128]{2,1,0:T(8,128)S(1)} %slice.9), channel_id=1, source_target_pairs={{0,4},{4,0},{8,12},{12,8},{16,20},{20,16},{24,28},{28,24},{1,5},{5... | collective-permute-start | bytes 98312 | tf_op jit(solution)/shard_map/ppermute | solution.py:308
  80.2 2.4 %collective-permute-done.10 = f32[1,64,128]{2,1,0:T(8,128)S(1)} collective-permute-done((f32[1,64,128]{2,1,0:T(8,128)S(1)}, f32[1,64,128]{2,1,0:T(8,128)S(1)}, u32[]{:S(2)}, u32[]{:S(2)}) %collective-permute-start.10) | collective-permute-done | bytes 32800 | tf_op jit(solution)/shard_map/ppermute | solution.py:308
  82.6 0.0 collective-permute-start.11
  82.6 1.6 %collective-permute-start.12 = (f32[64,128]{1,0:T(8,128)S(1)}, f32[64,128]{1,0:T(8,128)S(1)}, u32[]{:S(2)}, u32[]{:S(2)}) collective-permute-start(f32[64,128]{1,0:T(8,128)S(1)} %fusion), channel_id=1, source_target_pairs={{0,2},{1,3},{2,0},{3,1},{4,6},{5,7},{6,4},{7,5},{8,10},{9,11},{10,... | collective-permute-start | bytes 98312 | tf_op jit(solution)/shard_map/ppermute | solution.py:308
  84.2 0.2 collective-permute-start.13
  84.4 1.7 %collective-permute-done.11 = f32[64,128]{1,0:T(8,128)S(1)} collective-permute-done((f32[64,128]{1,0:T(8,128)S(1)}, f32[64,128]{1,0:T(8,128)S(1)}, u32[]{:S(2)}, u32[]{:S(2)}) %collective-permute-start.11) | collective-permute-done | bytes 32800 | tf_op jit(solution)/shard_map/ppermute | solution.py:308
  86.1 0.5 collective-permute-done.12
  86.6 0.0 collective-permute-done.13
  86.6 0.6 add_bitcast_fusion
  (14 shorter events, 0.0 us)
Async XLA Ops:
  0.0 8.5 %copy-start = (bf16[1,128,12288]{2,1,0:T(8,128)(2,1)S(1)}, bf16[1,128,12288]{2,1,0:T(8,128)(2,1)}, u32[]{:S(2)}) copy-start(bf16[1,128,12288]{2,1,0:T(8,128)(2,1)} %qkv_ref.15) | copy-start | bytes 9437188
  2.4 14.8 %collective-permute-start.2 = (bf16[128,1280]{1,0:T(8,128)(2,1)}, bf16[128,1280]{1,0:T(8,128)(2,1)S(1)}, u32[]{:S(2)}, u32[]{:S(2)}) collective-permute-start(bf16[128,1280]{1,0:T(8,128)(2,1)} %pack.10), channel_id=1, source_target_pairs={{0,28},{4,24},{8,20},{12,16},{16,12},{20,8},{24,4},{28,0},{1,29},{... | collective-permute-start | bytes 983048 | tf_op jit(solution)/shard_map/ppermute | solution.py:308
  8.5 1.2 %copy-start.1 = (bf16[2,4096,64]{1,2,0:T(8,128)(2,1)S(1)}, bf16[2,4096,64]{1,2,0:T(8,128)(2,1)}, u32[]{:S(2)}) copy-start(bf16[2,4096,64]{1,2,0:T(8,128)(2,1)} %param.6) | copy-start | bytes 3145732
  10.5 17.5 %collective-permute-start.4 = (bf16[128,1280]{1,0:T(8,128)(2,1)S(1)}, bf16[128,1280]{1,0:T(8,128)(2,1)S(1)}, u32[]{:S(2)}, u32[]{:S(2)}) collective-permute-start(bf16[128,1280]{1,0:T(8,128)(2,1)S(1)} %pack.12), channel_id=1, source_target_pairs={{0,12},{4,8},{8,4},{12,0},{16,28},{20,24},{24,20},{28,16},{1,13},{... | collective-permute-start | bytes 983048 | tf_op jit(solution)/shard_map/ppermute | solution.py:308
  11.4 29.7 %collective-permute-start = (bf16[128,1280]{1,0:T(8,128)(2,1)S(1)}, bf16[128,1280]{1,0:T(8,128)(2,1)S(1)}, u32[]{:S(2)}, u32[]{:S(2)}) collective-permute-start(bf16[128,1280]{1,0:T(8,128)(2,1)S(1)} %pack.8), channel_id=1, source_target_pairs={{0,16},{4,20},{8,24},{12,28},{16,0},{20,4},{24,8},{28,12},{1,17},{... | collective-permute-start | bytes 983048 | tf_op jit(solution)/shard_map/ppermute | solution.py:308
  17.3 17.9 %copy-start.3 = (bf16[128,1280]{1,0:T(8,128)(2,1)}, bf16[128,1280]{1,0:T(8,128)(2,1)S(1)}, u32[]{:S(2)}) copy-start(bf16[128,1280]{1,0:T(8,128)(2,1)S(1)} %collective-permute-done.2.refs_0_.refs_1_.refs_5_) | copy-start | bytes 983044
  29.5 21.5 %collective-permute-start.6 = (bf16[128,1280]{1,0:T(8,128)(2,1)}, bf16[128,1280]{1,0:T(8,128)(2,1)}, u32[]{:S(2)}, u32[]{:S(2)}) collective-permute-start(bf16[128,1280]{1,0:T(8,128)(2,1)} %pack.15), channel_id=1, source_target_pairs={{0,8},{4,12},{8,0},{12,4},{16,24},{20,28},{24,16},{28,20},{1,9},{5... | collective-permute-start | bytes 983048 | tf_op jit(solution)/shard_map/ppermute | solution.py:308
  33.8 17.2 %collective-permute-start.5 = (bf16[128,1280]{1,0:T(8,128)(2,1)}, bf16[128,1280]{1,0:T(8,128)(2,1)}, u32[]{:S(2)}, u32[]{:S(2)}) collective-permute-start(bf16[128,1280]{1,0:T(8,128)(2,1)} %pack.14), channel_id=1, source_target_pairs={{0,4},{4,0},{8,12},{12,8},{16,20},{20,16},{24,28},{28,24},{1,5},{5... | collective-permute-start | bytes 983048 | tf_op jit(solution)/shard_map/ppermute | solution.py:308
  36.7 20.1 %collective-permute-start.3 = (bf16[128,1280]{1,0:T(8,128)(2,1)}, bf16[128,1280]{1,0:T(8,128)(2,1)}, u32[]{:S(2)}, u32[]{:S(2)}) collective-permute-start(bf16[128,1280]{1,0:T(8,128)(2,1)} %pack.11), channel_id=1, source_target_pairs={{0,24},{4,28},{8,16},{12,20},{16,8},{20,12},{24,0},{28,4},{1,25},{... | collective-permute-start | bytes 983048 | tf_op jit(solution)/shard_map/ppermute | solution.py:308
  41.1 1.6 %copy-start.5 = (bf16[128,1280]{1,0:T(8,128)(2,1)}, bf16[128,1280]{1,0:T(8,128)(2,1)S(1)}, u32[]{:S(2)}) copy-start(bf16[128,1280]{1,0:T(8,128)(2,1)S(1)} %collective-permute-done.refs_0_.refs_4_) | copy-start | bytes 983044
  42.7 8.3 %copy-start.7 = (s32[4]{0:T(128)S(1)}, s32[4]{0:T(128)}, u32[]{:S(2)}) copy-start(s32[4]{0:T(128)} %frames_ref.3) | copy-start | bytes 52
  42.7 8.3 %copy-start.8 = (f32[1000]{0:T(1024)S(1)}, f32[1000]{0:T(1024)}, u32[]{:S(2)}) copy-start(f32[1000]{0:T(1024)} %step_weight_ref.1) | copy-start | bytes 12004
  42.7 8.3 %copy-start.9 = (s32[2]{0:T(128)S(1)}, s32[2]{0:T(128)}, u32[]{:S(2)}) copy-start(s32[2]{0:T(128)} %timestep_ref.1) | copy-start | bytes 28
  42.7 25.0 %collective-permute-start.1 = (bf16[128,1280]{1,0:T(8,128)(2,1)}, bf16[128,1280]{1,0:T(8,128)(2,1)}, u32[]{:S(2)}, u32[]{:S(2)}) collective-permute-start(bf16[128,1280]{1,0:T(8,128)(2,1)} %pack.9), channel_id=1, source_target_pairs={{0,20},{4,16},{8,28},{12,24},{16,4},{20,0},{24,12},{28,8},{1,21},{... | collective-permute-start | bytes 983048 | tf_op jit(solution)/shard_map/ppermute | solution.py:308
  42.8 1.2 %copy-start.2 = (bf16[2,4096,64]{1,2,0:T(8,128)(2,1)S(1)}, bf16[2,4096,64]{1,2,0:T(8,128)(2,1)}, u32[]{:S(2)}) copy-start(bf16[2,4096,64]{1,2,0:T(8,128)(2,1)} %param.6) | copy-start | bytes 3145732
  44.1 7.0 %copy-start.4 = (bf16[128,1280]{1,0:T(8,128)(2,1)S(1)}, bf16[128,1280]{1,0:T(8,128)(2,1)}, u32[]{:S(2)}) copy-start(bf16[128,1280]{1,0:T(8,128)(2,1)} %copy-done.3) | copy-start | bytes 983044
  44.1 7.0 %copy-start.6 = (bf16[128,1280]{1,0:T(8,128)(2,1)S(1)}, bf16[128,1280]{1,0:T(8,128)(2,1)}, u32[]{:S(2)}) copy-start(bf16[128,1280]{1,0:T(8,128)(2,1)} %copy-done.5) | copy-start | bytes 983044
  71.7 6.1 %collective-permute-start.7 = (bf16[2,64,128]{2,1,0:T(8,128)(2,1)S(1)}, bf16[2,64,128]{2,1,0:T(8,128)(2,1)S(1)}, u32[]{:S(2)}, u32[]{:S(2)}) collective-permute-start(bf16[2,64,128]{2,1,0:T(8,128)(2,1)S(1)} %get-tuple-element.20), channel_id=1, source_target_pairs={{0,24},{4,28},{8,16},{12,20},{16,8},{20,12},{24,0},{28,4},{1,25},{... | collective-permute-start | bytes 98312 | tf_op jit(solution)/shard_map/ppermute | solution.py:308
  73.7 4.8 %collective-permute-start.8 = (bf16[2,64,128]{2,1,0:T(8,128)(2,1)S(1)}, bf16[2,64,128]{2,1,0:T(8,128)(2,1)S(1)}, u32[]{:S(2)}, u32[]{:S(2)}) collective-permute-start(bf16[2,64,128]{2,1,0:T(8,128)(2,1)S(1)} %get-tuple-element.21), channel_id=1, source_target_pairs={{0,16},{4,20},{8,24},{12,28},{16,0},{20,4},{24,8},{28,12},{1,17},{... | collective-permute-start | bytes 98312 | tf_op jit(solution)/shard_map/ppermute | solution.py:308
  73.7 4.8 %collective-permute-start.9 = (bf16[2,64,128]{2,1,0:T(8,128)(2,1)S(1)}, bf16[2,64,128]{2,1,0:T(8,128)(2,1)S(1)}, u32[]{:S(2)}, u32[]{:S(2)}) collective-permute-start(bf16[2,64,128]{2,1,0:T(8,128)(2,1)S(1)} %get-tuple-element.22), channel_id=1, source_target_pairs={{0,8},{4,12},{8,0},{12,4},{16,24},{20,28},{24,16},{28,20},{1,9},{5... | collective-permute-start | bytes 98312 | tf_op jit(solution)/shard_map/ppermute | solution.py:308
  78.6 4.0 %collective-permute-start.10 = (f32[1,64,128]{2,1,0:T(8,128)S(1)}, f32[1,64,128]{2,1,0:T(8,128)S(1)}, u32[]{:S(2)}, u32[]{:S(2)}) collective-permute-start(f32[1,64,128]{2,1,0:T(8,128)S(1)} %slice.9), channel_id=1, source_target_pairs={{0,4},{4,0},{8,12},{12,8},{16,20},{20,16},{24,28},{28,24},{1,5},{5... | collective-permute-start | bytes 98312 | tf_op jit(solution)/shard_map/ppermute | solution.py:308
  82.6 3.6 %collective-permute-start.11 = (f32[64,128]{1,0:T(8,128)S(1)}, f32[64,128]{1,0:T(8,128)S(1)}, u32[]{:S(2)}, u32[]{:S(2)}) collective-permute-start(f32[64,128]{1,0:T(8,128)S(1)} %fusion), channel_id=1, source_target_pairs={{0,3},{1,2},{2,1},{3,0},{4,7},{5,6},{6,5},{7,4},{8,11},{9,10},{10,... | collective-permute-start | bytes 98312 | tf_op jit(solution)/shard_map/ppermute | solution.py:308
  82.6 4.0 %collective-permute-start.12 = (f32[64,128]{1,0:T(8,128)S(1)}, f32[64,128]{1,0:T(8,128)S(1)}, u32[]{:S(2)}, u32[]{:S(2)}) collective-permute-start(f32[64,128]{1,0:T(8,128)S(1)} %fusion), channel_id=1, source_target_pairs={{0,2},{1,3},{2,0},{3,1},{4,6},{5,7},{6,4},{7,5},{8,10},{9,11},{10,... | collective-permute-start | bytes 98312 | tf_op jit(solution)/shard_map/ppermute | solution.py:308
  84.2 2.4 %collective-permute-start.13 = (f32[64,128]{1,0:T(8,128)S(1)}, f32[64,128]{1,0:T(8,128)S(1)}, u32[]{:S(2)}, u32[]{:S(2)}) collective-permute-start(f32[64,128]{1,0:T(8,128)S(1)} %fusion), channel_id=1, source_target_pairs={{0,1},{1,0},{2,3},{3,2},{4,5},{5,4},{6,7},{7,6},{8,9},{9,8},{10,11... | collective-permute-start | bytes 98312 | tf_op jit(solution)/shard_map/ppermute | solution.py:308

commit v21 on v20

--- a/solution.py
+++ b/solution.py
@@ -189,62 +189,81 @@
     lax.fori_loop(0, blocks, some_blocks, 0)
 
 
-def late_kernel(offsets, late, frames_ref, me_ref, *refs):
-    early = len(offsets)
-    arrived = refs[:2]
-    sums_ref, stats_ref, factor_ref, early_ref, early_folded, *out_refs, late_pieces, folded, sems = refs[2:]
-    copies = [pltpu.make_async_copy(arrived[n], late_pieces.at[n], sems.at[n]) for n in range(2)]
-    for copy in copies:
-        copy.start()
+def join_kernel(every, early, last, frames_ref, me_ref, *refs):
+    known = len(every) - 1
+    new_ref, early_ref, early_folded, sums_ref, stats_ref, *refs = refs
+    if last:
+        joined_ref, joined_folded, factor_ref, *out_refs, piece, folded, sem = refs
+        size = out_refs[0].shape[0]
+        factor = factor_ref[:1]
+    else:
+        new_sums, new_stats, piece, folded, sem = refs
+    lat = sums_ref.shape[1]
+    rows = piece.shape[0]
+    count = folded.shape[0]
+    copy = pltpu.make_async_copy(new_ref, piece, sem)
+    copy.start()
     me = me_ref[0]
-    size, lat, rows = out_refs[0].shape
-    count = folded.shape[0]
-    for copy in copies:
-        copy.wait()
-    pieces = [early_ref.at[n] for n in range(early)] + [late_pieces.at[n] for n in range(2)]
-    stage_values(folded, pieces[early:], lat)
-    factor = factor_ref[:1]
-    every = list(offsets) + list(late)
-    blocks = early // 2
-    results = {}
-
-    def write(number, start):
+    copy.wait()
+    pieces = [early_ref.at[n] for n in range(early)] + ([joined_ref] if last else []) + [piece]
+    stage_values(folded, [piece], lat)
+    results, peaks, totals = {}, {0: [], known: []}, {0: [], known: []}
+
+    def read(numbers, i, what):
+        column = (2 * i + what) * HD
+        parts = [pieces[n][:, column : column + HD] for n in numbers]
+        return parts[0] if len(parts) == 1 else jnp.concatenate(parts, axis=0)
+
+    def value_tile(numbers, i):
+        if numbers[0] < early:
+            return early_folded[i, :, numbers[0] * rows : (numbers[-1] + 1) * rows]
+        parts = [folded[i] if n == known else joined_folded[i] for n in numbers]
+        return parts[0] if len(parts) == 1 else jnp.concatenate(parts, axis=1)
+
+    def write(start, number):
         for j in range(number):
             k = every[start + j]
             out_ref = out_refs[k // size]
             out_ref[k % size] = (results[start][:, j * rows : (j + 1) * rows] * factor).astype(out_ref.dtype)
 
     units = []
-    for start, number, tiles_in in ((0, early, [blocks]), (early, 2, range(blocks + 1))):
-        key_offsets = [every[2 * t + j] for t in tiles_in for j in range(2)]
-        shifts = mask_rows(frames_ref, me, rows, every[start : start + number], key_offsets)
+    all_tiles = [tuple(range(n, min(n + 2, known + 1))) for n in range(0, known + 1, 2)]
+    for start, number, key_tiles in ((0, known, [(known,)]), (known, 1, all_tiles)):
+        shifts = mask_rows(
+            frames_ref, me, rows, every[start : start + number], [every[n] for tile in key_tiles for n in tile]
+        )
         for i in range(count):
 
             def finish(summed, total, peak, start=start, number=number, i=i):
+                part = summed
                 if start == 0:
                     before = stats_ref[0, i : i + 1]
                     highest = jnp.maximum(before, peak)
                     old = jnp.exp2((before - highest) * LOG2_SCALE)
                     new = jnp.exp2((peak - highest) * LOG2_SCALE)
-                    both = stats_ref[1, i : i + 1] * old + total * new
-                    part = sums_ref[i] * (old / both) + summed * (new / both)
-                else:
+                    peak, total = highest, stats_ref[1, i : i + 1] * old + total * new
+                    if last:
+                        old, new = old / total, new / total
+                    part = sums_ref[i] * old + summed * new
+                elif last:
                     part = summed / total
-                results[start] = part if i == 0 else results[start] + part
+                if last:
+                    results[start] = part if i == 0 else results[start] + part
+                    if i == count - 1:
+                        write(start, number)
+                    return
+                span = slice(start * rows, (start + number) * rows)
+                new_sums[i, :, span] = part
+                peaks[start].append(peak)
+                totals[start].append(total)
                 if i == count - 1:
-                    write(number, start)
-
-            def queries(start=start, number=number, i=i):
-                column = 2 * i * HD
-                return jnp.concatenate([p[:, column : column + HD] for p in pieces[start : start + number]], axis=0)
-
-            keys = pairs_of(pieces, i, 1)
-            tiles = [functools.partial(score_tile, keys[t], queries) for t in tiles_in]
-            values = [
-                lambda i=i, t=t: folded[i] if t == blocks else early_folded[i, :, t * 2 * rows : (t + 1) * 2 * rows]
-                for t in tiles_in
-            ]
-            units.append((tiles, values, shifts, finish))
+                    rest = [jnp.ones_like(peak)] * (new_stats.shape[1] - count)
+                    new_stats[0, :, span] = jnp.concatenate(peaks[start] + rest, axis=0)
+                    new_stats[1, :, span] = jnp.concatenate(totals[start] + rest, axis=0)
+
+            queries = functools.partial(read, range(start, start + number), i, 0)
+            tiles = [functools.partial(score_tile, functools.partial(read, t, i, 1), queries) for t in key_tiles]
+            units.append((tiles, [functools.partial(value_tile, t, i) for t in key_tiles], shifts, finish))
     run_units(units, lat)
 
 
@@ -277,30 +296,33 @@
     )(span_frames, me, timestep, step_weight, sign, sample, *pieces)
 
 
-def attend_late(pieces, offsets, late, early, span_frames, me, count, lat):
-    rows, width = pieces[0].shape
-    half = len(offsets) // 2 + 1
-    tokens = 2 * half * rows
+def join(piece, every, early, state, joined, span_frames, me, count, lat):
+    last = bool(joined)
+    rows, width = piece.shape
+    tokens = len(every) * rows
+    if last:
+        shape = (len(every) // 4, lat, rows)
+        out_shape = [jax.ShapeDtypeStruct(shape, jnp.bfloat16 if g else jnp.float32) for g in range(4)]
+    else:
+        out_shape = [
+            jax.ShapeDtypeStruct((count, lat, tokens), jnp.float32),
+            jax.ShapeDtypeStruct((2, 8, tokens), jnp.float32),
+            jax.ShapeDtypeStruct((rows, width), jnp.bfloat16),
+            jax.ShapeDtypeStruct((count, lat + 16, rows), jnp.bfloat16),
+        ]
+    held = [pltpu.VMEM((rows, width), jnp.bfloat16), pltpu.VMEM((count, lat + 16, rows), jnp.bfloat16)]
     return pl.pallas_call(
-        functools.partial(late_kernel, offsets, late),
-        in_specs=[SMEM] * 2 + [HBM] * 2 + [VMEM] * len(early),
+        functools.partial(join_kernel, every, early, last),
+        in_specs=[SMEM] * 2 + [HBM] + [VMEM] * (len(state) + len(joined)),
         out_specs=[VMEM] * 4,
-        out_shape=[
-            jax.ShapeDtypeStruct((half // 2, lat, rows), jnp.bfloat16 if g else jnp.float32) for g in range(4)
-        ],
-        scratch_shapes=[
-            pltpu.VMEM((2, rows, width), jnp.bfloat16),
-            pltpu.VMEM((count, lat + 16, 2 * rows), jnp.bfloat16),
-            pltpu.SemaphoreType.DMA((2,)),
-        ],
-        compiler_params=pltpu.CompilerParams(vmem_limit_bytes=SMALL_VMEM if half <= 4 else LARGE_VMEM),
+        out_shape=out_shape,
+        scratch_shapes=(held if last else []) + [pltpu.SemaphoreType.DMA],
+        compiler_params=pltpu.CompilerParams(vmem_limit_bytes=SMALL_VMEM if len(every) <= 8 else LARGE_VMEM),
         cost_estimate=pl.CostEstimate(
-            flops=count * tokens * rows * 4 * (HD + lat),
-            bytes_accessed=tokens * count * 3 * HD * 2,
-            transcendentals=count * tokens * rows * 2,
+            flops=0, bytes_accessed=rows * width * 2, transcendentals=0
         ),
-        name="attend_late",
-    )(span_frames, me, *pieces, *early)
+        name="join",
+    )(span_frames, me, piece, *state, *joined)
 
 
 def swap(array, axis, offset):
@@ -329,16 +351,19 @@
         after = [pieces[tops[n - 2]]] if n > 1 else []
         pieces[k] = swap(pack(me, model, qkv, readout_t, k, count, after, n == 0), "seq", k)
     for k in range(half - 1, 0, -1):
-        after = [] if k == half - 1 else [pieces[k + 1], pieces[tops[0]]] if k > 1 else [pieces[half - 1]]
+        after = [] if k == half - 1 else [pieces[k + 1]] if k > 1 else [pieces[tops[0]]]
         pieces[k] = swap(pack(me, model, qkv, readout_t, k, count, after), "seq", k)
     pieces[0] = pack(me, model, qkv, readout_t, 0, count, [pieces[half - 1]])
-    late = sorted(tops[-2:])
-    early = [k for k in range(seq_count) if k not in late]
-    merged = attend_early(
+    early = [k for k in range(seq_count) if k not in tops[-2:]]
+    sums, stats, factor, held, folded = attend_early(
         [pieces[k] for k in early], early, span_frames, me, timestep, step_weight, sign, sample, count, lat
     )
-    ends = [pieces[k] for k in late]
-    given = attend_late(ends, early, late, merged, span_frames, me, count, lat)
+    every = early + tops[-2:]
+    state = [held, folded, sums, stats]
+    sums, stats, third, third_folded = join(pieces[every[-2]], every[:-1], len(early), state, [], span_frames, me, count, lat)
+    state = [held, folded, sums, stats]
+    joined = [third, third_folded, factor]
+    given = join(pieces[every[-1]], every, len(early), state, joined, span_frames, me, count, lat)
     size = half // 2
     while True:
         keep = given[0]

time: 87.4 us -> 87.2 us (level)
  waiting for transfers between devices: 44.2 us -> 36.9 us
  Pallas kernels: 20.8 us -> 23.8 us
  starting transfers between devices: 18.9 us -> 21.8 us
  local copies, waits for them, and re-layouts: 2.49 us -> 3.46 us
    ppermute x14, waiting for transfers between devices: 44.2 us -> 36.9 us  [swap(): return lax.ppermute(array, axis, [(i, i ^ offset) for i in range(size)])]
    pallas_call x1 -> x2, Pallas kernels: 3.95 us -> 6.99 us  [join(): pl.pallas_call(functools.partial(join_kernel, every, early, last), in_spe...]
    ppermute x14, starting transfers between devices: 18.9 us -> 21.8 us  [swap(): return lax.ppermute(array, axis, [(i, i ^ offset) for i in range(size)])]
    unnamed x20 -> x22, local copies, waits for them, and re-layouts: 2.48 us -> 3.45 us
  transfers between devices with their start and end apart: 14 -> 14, of which waited for: 10 -> 10; matrix products, arithmetic and copies ran while one was open for 0% -> 0% of each run, Pallas kernels for 16% -> 20%
where the time goes in v21:
time: 87.2 us; the launch traced here: 86.9 us
  waiting for transfers between devices  36.9 us (42%)
  Pallas kernels  23.8 us (27%)
  starting transfers between devices  21.8 us (25%)
  local copies, waits for them, and re-layouts  3.46 us (4%)
    ppermute x14, waiting for transfers between devices, swap(): return lax.ppermute(array, axis, [(i, i ^ offset) for i in range(size)])  36.9 us
    ppermute x14, starting transfers between devices, swap(): return lax.ppermute(array, axis, [(i, i ^ offset) for i in range(size)])  21.8 us
    pallas_call x8, Pallas kernels, pack(): pl.pallas_call(functools.partial(pack_kernel, k), in_specs=[SMEM, SMEM] +...  11 us
    pallas_call x2, Pallas kernels, join(): pl.pallas_call(functools.partial(join_kernel, every, early, last), in_spe...  6.99 us
    pallas_call x1, Pallas kernels, attend_early(): pl.pallas_call(functools.partial(early_kernel, offsets), in_specs=[SMEM]...  5.77 us
    unnamed x22, local copies, waits for them, and re-layouts  3.45 us
  transfers between devices with their start and end apart: 14, of which 10 were waited for; matrix products, arithmetic and copies ran while one was open for 0% of the time, Pallas kernels for 20%

profile of v21, /device:TPU:0, one launch (start us, length us, event | category | flops | bytes accessed | tf_op | source)
XLA Modules:
  0.0 86.9 jit_solution(2828354584849233650)
XLA Ops:
  0.0 2.4 %pack.12 = bf16[128,1280]{1,0:T(8,128)(2,1)} custom-call(s32[1]{0:T(128)} %bitcast.me_ref, s32[1]{0:T(128)} %bitcast.1.model_ref, bf16[1,128,12288]{2,1,0:T(8,128)(2,1)} %qkv_ref.15, bf16[2,64,4096]{2,1,0:T(8,128)(2,1)} %bitcast.9), custom_call_target="tpu_custom_call" | custom-call | bytes 655360 | tf_op jit(solution)/shard_map/pack/pallas_call | solution.py:67
  2.4 6.0 %collective-permute-start.3 = (bf16[128,1280]{1,0:T(8,128)(2,1)}, bf16[128,1280]{1,0:T(8,128)(2,1)S(1)}, u32[]{:S(2)}, u32[]{:S(2)}) collective-permute-start(bf16[128,1280]{1,0:T(8,128)(2,1)} %pack.12), channel_id=1, source_target_pairs={{0,28},{4,24},{8,20},{12,16},{16,12},{20,8},{24,4},{28,0},{1,29},{... | collective-permute-start | bytes 983048 | tf_op jit(solution)/shard_map/ppermute | solution.py:330
  8.5 0.0 copy-done
  8.5 1.2 %copy-done.1 = bf16[2,4096,64]{1,2,0:T(8,128)(2,1)S(1)} copy-done((bf16[2,4096,64]{1,2,0:T(8,128)(2,1)S(1)}, bf16[2,4096,64]{1,2,0:T(8,128)(2,1)}, u32[]{:S(2)}) %copy-start.1) | copy-done | bytes 1048600
  9.7 0.8 pack.10
  10.5 0.1 collective-permute-start.2
  10.6 0.8 pack.8
  11.4 0.6 collective-permute-start
  12.0 5.2 %collective-permute-done.3.refs_0_.refs_5_ = bf16[128,1280]{1,0:T(8,128)(2,1)S(1)} collective-permute-done((bf16[128,1280]{1,0:T(8,128)(2,1)}, bf16[128,1280]{1,0:T(8,128)(2,1)S(1)}, u32[]{:S(2)}, u32[]{:S(2)}) %collective-permute-start.3) | collective-permute-done | bytes 327712 | tf_op jit(solution)/shard_map/ppermute | solution.py:330
  17.3 1.5 %pack.13 = bf16[128,1280]{1,0:T(8,128)(2,1)} custom-call(s32[1]{0:T(128)} %bitcast.me_ref, s32[1]{0:T(128)} %bitcast.1.model_ref, bf16[1,128,12288]{2,1,0:T(8,128)(2,1)S(1)} %copy-done, bf16[2,64,4096]{2,1,0:T(8,128)(2,1)S(1)} %bitcast.12, bf16[128,1280]{1,0:T(8,128)(2,1)S(1)} %collective-permute-done.3.refs_0_.refs_5_), custom_call_target="tpu_custom_call" | custom-call | bytes 655360 | tf_op jit(solution)/shard_map/pack/pallas_call | solution.py:67
  18.8 1.8 %collective-permute-start.4 = (bf16[128,1280]{1,0:T(8,128)(2,1)}, bf16[128,1280]{1,0:T(8,128)(2,1)}, u32[]{:S(2)}, u32[]{:S(2)}) collective-permute-start(bf16[128,1280]{1,0:T(8,128)(2,1)} %pack.13), channel_id=1, source_target_pairs={{0,4},{4,0},{8,12},{12,8},{16,20},{20,16},{24,28},{28,24},{1,5},{5... | collective-permute-start | bytes 983048 | tf_op jit(solution)/shard_map/ppermute | solution.py:330
  20.6 7.4 %collective-permute-done.2.refs_0_.refs_3_ = bf16[128,1280]{1,0:T(8,128)(2,1)S(1)} collective-permute-done((bf16[128,1280]{1,0:T(8,128)(2,1)S(1)}, bf16[128,1280]{1,0:T(8,128)(2,1)S(1)}, u32[]{:S(2)}, u32[]{:S(2)}) %collective-permute-start.2) | collective-permute-done | bytes 327712 | tf_op jit(solution)/shard_map/ppermute | solution.py:330
  28.0 1.6 %pack.14 = bf16[128,1280]{1,0:T(8,128)(2,1)} custom-call(s32[1]{0:T(128)} %bitcast.me_ref, s32[1]{0:T(128)} %bitcast.1.model_ref, bf16[1,128,12288]{2,1,0:T(8,128)(2,1)S(1)} %copy-done, bf16[2,64,4096]{2,1,0:T(8,128)(2,1)S(1)} %bitcast.13, bf16[128,1280]{1,0:T(8,128)(2,1)S(1)} %collective-permute-done.2.refs_0_.refs_3_), custom_call_target="tpu_custom_call" | custom-call | bytes 655360 | tf_op jit(solution)/shard_map/pack/pallas_call | solution.py:67
  29.6 3.4 %collective-permute-start.5 = (bf16[128,1280]{1,0:T(8,128)(2,1)}, bf16[128,1280]{1,0:T(8,128)(2,1)}, u32[]{:S(2)}, u32[]{:S(2)}) collective-permute-start(bf16[128,1280]{1,0:T(8,128)(2,1)} %pack.14), channel_id=1, source_target_pairs={{0,8},{4,12},{8,0},{12,4},{16,24},{20,28},{24,16},{28,20},{1,9},{5... | collective-permute-start | bytes 983048 | tf_op jit(solution)/shard_map/ppermute | solution.py:330
  32.9 1.5 %pack.15 = bf16[128,1280]{1,0:T(8,128)(2,1)} custom-call(s32[1]{0:T(128)} %bitcast.me_ref, s32[1]{0:T(128)} %bitcast.1.model_ref, bf16[1,128,12288]{2,1,0:T(8,128)(2,1)S(1)} %copy-done, bf16[2,64,4096]{2,1,0:T(8,128)(2,1)S(1)} %bitcast.14, bf16[128,1280]{1,0:T(8,128)(2,1)S(1)} %collective-permute-done.3.refs_0_.refs_5_), custom_call_target="tpu_custom_call" | custom-call | bytes 655360 | tf_op jit(solution)/shard_map/pack/pallas_call | solution.py:67
  34.5 2.0 %collective-permute-start.6 = (bf16[128,1280]{1,0:T(8,128)(2,1)}, bf16[128,1280]{1,0:T(8,128)(2,1)}, u32[]{:S(2)}, u32[]{:S(2)}) collective-permute-start(bf16[128,1280]{1,0:T(8,128)(2,1)} %pack.15), channel_id=1, source_target_pairs={{0,24},{4,28},{8,16},{12,20},{16,8},{20,12},{24,0},{28,4},{1,25},{... | collective-permute-start | bytes 983048 | tf_op jit(solution)/shard_map/ppermute | solution.py:330
  36.5 6.5 %collective-permute-done.refs_0_.refs_4_ = bf16[128,1280]{1,0:T(8,128)(2,1)S(1)} collective-permute-done((bf16[128,1280]{1,0:T(8,128)(2,1)S(1)}, bf16[128,1280]{1,0:T(8,128)(2,1)S(1)}, u32[]{:S(2)}, u32[]{:S(2)}) %collective-permute-start) | collective-permute-done | bytes 327712 | tf_op jit(solution)/shard_map/ppermute | solution.py:330
  43.0 1.5 %pack.9 = bf16[128,1280]{1,0:T(8,128)(2,1)} custom-call(s32[1]{0:T(128)} %bitcast.me_ref, s32[1]{0:T(128)} %bitcast.1.model_ref, bf16[1,128,12288]{2,1,0:T(8,128)(2,1)S(1)} %copy-done, bf16[2,64,4096]{2,1,0:T(8,128)(2,1)S(1)} %bitcast.15, bf16[128,1280]{1,0:T(8,128)(2,1)S(1)} %collective-permute-done.refs_0_.refs_4_), custom_call_target="tpu_custom_call" | custom-call | bytes 655360 | tf_op jit(solution)/shard_map/pack/pallas_call | solution.py:67
  44.5 0.0 copy-start.8
  44.6 0.0 copy-start.9
  44.6 0.0 copy-start.10
  44.6 0.1 collective-permute-start.1
  44.7 0.0 copy-start.2
  44.7 1.2 %copy-done.2 = bf16[2,4096,64]{1,2,0:T(8,128)(2,1)S(1)} copy-done((bf16[2,4096,64]{1,2,0:T(8,128)(2,1)S(1)}, bf16[2,4096,64]{1,2,0:T(8,128)(2,1)}, u32[]{:S(2)}) %copy-start.2) | copy-done | bytes 1048600
  45.9 1.0 %copy-done.4 = bf16[128,1280]{1,0:T(8,128)(2,1)S(1)} copy-done((bf16[128,1280]{1,0:T(8,128)(2,1)S(1)}, bf16[128,1280]{1,0:T(8,128)(2,1)}, u32[]{:S(2)}) %copy-start.4) | copy-done | bytes 327704
  46.9 0.8 pack.11.refs_0_
  47.7 0.0 collective-permute-done.4.refs_1_
  47.7 3.3 %collective-permute-done.5.refs_2_ = bf16[128,1280]{1,0:T(8,128)(2,1)} collective-permute-done((bf16[128,1280]{1,0:T(8,128)(2,1)}, bf16[128,1280]{1,0:T(8,128)(2,1)}, u32[]{:S(2)}, u32[]{:S(2)}) %collective-permute-start.5) | collective-permute-done | bytes 327712 | tf_op jit(solution)/shard_map/ppermute | solution.py:330
  51.1 5.8 %attend_early.1 = (f32[4,64,768]{2,1,0:T(8,128)S(1)}, f32[2,8,768]{2,1,0:T(8,128)S(1)}, f32[8,128]{1,0:T(8,128)S(1)}, bf16[6,128,1280]{2,1,0:T(8,128)(2,1)S(1)}, bf16[4,80,768]{2,1,0:T(8,128)(2,1)S(1)}) custom-call(s32[4]{0:T(128)S(1)} %copy-done.8, s32[1]{0:T(128)} %bitcast.me_ref, s32[2]{0:T(128)S(1)} %copy-done.10, f32[1000]{0:T(1024)S(1)} %copy-done.9, ...), custom_call_target="tpu_custom_call" | custom-call | flops 905969664 | bytes 2359296 | tf_op jit(solution)/shard_map/attend_early/pallas_call | solution.py:274
  56.8 0.0 collective-permute-done.6.refs_0_
  56.9 3.4 %join.2 = (f32[4,64,896]{2,1,0:T(8,128)S(1)}, f32[2,8,896]{2,1,0:T(8,128)S(1)}, bf16[128,1280]{1,0:T(8,128)(2,1)S(1)}, bf16[4,80,128]{2,1,0:T(8,128)(2,1)S(1)}) custom-call(s32[4]{0:T(128)S(1)} %copy-done.8, s32[1]{0:T(128)} %bitcast.me_ref, bf16[128,1280]{1,0:T(8,128)(2,1)} %collective-permute-done.6.refs_0_, ...), custom_call_target="tpu_custom_call" | custom-call | bytes 327680 | tf_op jit(solution)/shard_map/join/pallas_call | solution.py:314
  60.3 7.5 %collective-permute-done.1.refs_0_ = bf16[128,1280]{1,0:T(8,128)(2,1)} collective-permute-done((bf16[128,1280]{1,0:T(8,128)(2,1)}, bf16[128,1280]{1,0:T(8,128)(2,1)}, u32[]{:S(2)}, u32[]{:S(2)}) %collective-permute-start.1) | collective-permute-done | bytes 327712 | tf_op jit(solution)/shard_map/ppermute | solution.py:330
  67.7 3.6 %join.3 = (f32[2,64,128]{2,1,0:T(8,128)S(1)}, bf16[2,64,128]{2,1,0:T(8,128)(2,1)S(1)}, bf16[2,64,128]{2,1,0:T(8,128)(2,1)S(1)}, bf16[2,64,128]{2,1,0:T(8,128)(2,1)S(1)}) custom-call(s32[4]{0:T(128)S(1)} %copy-done.8, s32[1]{0:T(128)} %bitcast.me_ref, bf16[128,1280]{1,0:T(8,128)(2,1)} %collective-permute-done.1.refs_0_, ...), custom_call_target="tpu_custom_call" | custom-call | bytes 327680 | tf_op jit(solution)/shard_map/join/pallas_call | solution.py:314
  71.3 2.1 %collective-permute-start.7 = (bf16[2,64,128]{2,1,0:T(8,128)(2,1)S(1)}, bf16[2,64,128]{2,1,0:T(8,128)(2,1)S(1)}, u32[]{:S(2)}, u32[]{:S(2)}) collective-permute-start(bf16[2,64,128]{2,1,0:T(8,128)(2,1)S(1)} %get-tuple-element.28), channel_id=1, source_target_pairs={{0,24},{4,28},{8,16},{12,20},{16,8},{20,12},{24,0},{28,4},{1,25},{... | collective-permute-start | bytes 98312 | tf_op jit(solution)/shard_map/ppermute | solution.py:330
  73.4 0.0 collective-permute-start.8
  73.4 2.4 %collective-permute-start.9 = (bf16[2,64,128]{2,1,0:T(8,128)(2,1)S(1)}, bf16[2,64,128]{2,1,0:T(8,128)(2,1)S(1)}, u32[]{:S(2)}, u32[]{:S(2)}) collective-permute-start(bf16[2,64,128]{2,1,0:T(8,128)(2,1)S(1)} %get-tuple-element.30), channel_id=1, source_target_pairs={{0,8},{4,12},{8,0},{12,4},{16,24},{20,28},{24,16},{28,20},{1,9},{5... | collective-permute-start | bytes 98312 | tf_op jit(solution)/shard_map/ppermute | solution.py:330
  75.8 1.7 %collective-permute-done.7 = bf16[2,64,128]{2,1,0:T(8,128)(2,1)S(1)} collective-permute-done((bf16[2,64,128]{2,1,0:T(8,128)(2,1)S(1)}, bf16[2,64,128]{2,1,0:T(8,128)(2,1)S(1)}, u32[]{:S(2)}, u32[]{:S(2)}) %collective-permute-start.7) | collective-permute-done | bytes 32800 | tf_op jit(solution)/shard_map/ppermute | solution.py:330
  77.4 0.8 collective-permute-done.8
  78.2 0.0 collective-permute-done.9
  78.3 1.6 %collective-permute-start.10 = (f32[1,64,128]{2,1,0:T(8,128)S(1)}, f32[1,64,128]{2,1,0:T(8,128)S(1)}, u32[]{:S(2)}, u32[]{:S(2)}) collective-permute-start(f32[1,64,128]{2,1,0:T(8,128)S(1)} %slice.9), channel_id=1, source_target_pairs={{0,4},{4,0},{8,12},{12,8},{16,20},{20,16},{24,28},{28,24},{1,5},{5... | collective-permute-start | bytes 98312 | tf_op jit(solution)/shard_map/ppermute | solution.py:330
  79.9 2.4 %collective-permute-done.10 = f32[1,64,128]{2,1,0:T(8,128)S(1)} collective-permute-done((f32[1,64,128]{2,1,0:T(8,128)S(1)}, f32[1,64,128]{2,1,0:T(8,128)S(1)}, u32[]{:S(2)}, u32[]{:S(2)}) %collective-permute-start.10) | collective-permute-done | bytes 32800 | tf_op jit(solution)/shard_map/ppermute | solution.py:330
  82.2 0.0 collective-permute-start.11
  82.2 1.6 %collective-permute-start.12 = (f32[64,128]{1,0:T(8,128)S(1)}, f32[64,128]{1,0:T(8,128)S(1)}, u32[]{:S(2)}, u32[]{:S(2)}) collective-permute-start(f32[64,128]{1,0:T(8,128)S(1)} %fusion), channel_id=1, source_target_pairs={{0,2},{1,3},{2,0},{3,1},{4,6},{5,7},{6,4},{7,5},{8,10},{9,11},{10,... | collective-permute-start | bytes 98312 | tf_op jit(solution)/shard_map/ppermute | solution.py:330
  83.9 0.2 collective-permute-start.13
  84.1 1.7 %collective-permute-done.11 = f32[64,128]{1,0:T(8,128)S(1)} collective-permute-done((f32[64,128]{1,0:T(8,128)S(1)}, f32[64,128]{1,0:T(8,128)S(1)}, u32[]{:S(2)}, u32[]{:S(2)}) %collective-permute-start.11) | collective-permute-done | bytes 32800 | tf_op jit(solution)/shard_map/ppermute | solution.py:330
  85.8 0.5 collective-permute-done.12
  86.3 0.0 collective-permute-done.13
  86.3 0.6 add_bitcast_fusion
  (17 shorter events, 0.1 us)
Async XLA Ops:
  0.0 8.5 %copy-start = (bf16[1,128,12288]{2,1,0:T(8,128)(2,1)S(1)}, bf16[1,128,12288]{2,1,0:T(8,128)(2,1)}, u32[]{:S(2)}) copy-start(bf16[1,128,12288]{2,1,0:T(8,128)(2,1)} %qkv_ref.15) | copy-start | bytes 9437188
  2.4 14.8 %collective-permute-start.3 = (bf16[128,1280]{1,0:T(8,128)(2,1)}, bf16[128,1280]{1,0:T(8,128)(2,1)S(1)}, u32[]{:S(2)}, u32[]{:S(2)}) collective-permute-start(bf16[128,1280]{1,0:T(8,128)(2,1)} %pack.12), channel_id=1, source_target_pairs={{0,28},{4,24},{8,20},{12,16},{16,12},{20,8},{24,4},{28,0},{1,29},{... | collective-permute-start | bytes 983048 | tf_op jit(solution)/shard_map/ppermute | solution.py:330
  8.5 1.2 %copy-start.1 = (bf16[2,4096,64]{1,2,0:T(8,128)(2,1)S(1)}, bf16[2,4096,64]{1,2,0:T(8,128)(2,1)}, u32[]{:S(2)}) copy-start(bf16[2,4096,64]{1,2,0:T(8,128)(2,1)} %param.6) | copy-start | bytes 3145732
  10.5 17.5 %collective-permute-start.2 = (bf16[128,1280]{1,0:T(8,128)(2,1)S(1)}, bf16[128,1280]{1,0:T(8,128)(2,1)S(1)}, u32[]{:S(2)}, u32[]{:S(2)}) collective-permute-start(bf16[128,1280]{1,0:T(8,128)(2,1)S(1)} %pack.10), channel_id=1, source_target_pairs={{0,12},{4,8},{8,4},{12,0},{16,28},{20,24},{24,20},{28,16},{1,13},{... | collective-permute-start | bytes 983048 | tf_op jit(solution)/shard_map/ppermute | solution.py:330
  11.4 31.6 %collective-permute-start = (bf16[128,1280]{1,0:T(8,128)(2,1)S(1)}, bf16[128,1280]{1,0:T(8,128)(2,1)S(1)}, u32[]{:S(2)}, u32[]{:S(2)}) collective-permute-start(bf16[128,1280]{1,0:T(8,128)(2,1)S(1)} %pack.8), channel_id=1, source_target_pairs={{0,16},{4,20},{8,24},{12,28},{16,0},{20,4},{24,8},{28,12},{1,17},{... | collective-permute-start | bytes 983048 | tf_op jit(solution)/shard_map/ppermute | solution.py:330
  18.8 28.9 %collective-permute-start.4 = (bf16[128,1280]{1,0:T(8,128)(2,1)}, bf16[128,1280]{1,0:T(8,128)(2,1)}, u32[]{:S(2)}, u32[]{:S(2)}) collective-permute-start(bf16[128,1280]{1,0:T(8,128)(2,1)} %pack.13), channel_id=1, source_target_pairs={{0,4},{4,0},{8,12},{12,8},{16,20},{20,16},{24,28},{28,24},{1,5},{5... | collective-permute-start | bytes 983048 | tf_op jit(solution)/shard_map/ppermute | solution.py:330
  28.0 6.5 %copy-start.3 = (bf16[128,1280]{1,0:T(8,128)(2,1)}, bf16[128,1280]{1,0:T(8,128)(2,1)S(1)}, u32[]{:S(2)}) copy-start(bf16[128,1280]{1,0:T(8,128)(2,1)S(1)} %collective-permute-done.2.refs_0_.refs_3_) | copy-start | bytes 983044
  29.6 21.5 %collective-permute-start.5 = (bf16[128,1280]{1,0:T(8,128)(2,1)}, bf16[128,1280]{1,0:T(8,128)(2,1)}, u32[]{:S(2)}, u32[]{:S(2)}) collective-permute-start(bf16[128,1280]{1,0:T(8,128)(2,1)} %pack.14), channel_id=1, source_target_pairs={{0,8},{4,12},{8,0},{12,4},{16,24},{20,28},{24,16},{28,20},{1,9},{5... | collective-permute-start | bytes 983048 | tf_op jit(solution)/shard_map/ppermute | solution.py:330
  34.5 22.4 %collective-permute-start.6 = (bf16[128,1280]{1,0:T(8,128)(2,1)}, bf16[128,1280]{1,0:T(8,128)(2,1)}, u32[]{:S(2)}, u32[]{:S(2)}) collective-permute-start(bf16[128,1280]{1,0:T(8,128)(2,1)} %pack.15), channel_id=1, source_target_pairs={{0,24},{4,28},{8,16},{12,20},{16,8},{20,12},{24,0},{28,4},{1,25},{... | collective-permute-start | bytes 983048 | tf_op jit(solution)/shard_map/ppermute | solution.py:330
  43.0 1.5 %copy-start.6 = (bf16[128,1280]{1,0:T(8,128)(2,1)}, bf16[128,1280]{1,0:T(8,128)(2,1)S(1)}, u32[]{:S(2)}) copy-start(bf16[128,1280]{1,0:T(8,128)(2,1)S(1)} %collective-permute-done.refs_0_.refs_4_) | copy-start | bytes 983044
  44.5 6.5 %copy-start.8 = (s32[4]{0:T(128)S(1)}, s32[4]{0:T(128)}, u32[]{:S(2)}) copy-start(s32[4]{0:T(128)} %frames_ref.5) | copy-start | bytes 52
  44.6 6.5 %copy-start.9 = (f32[1000]{0:T(1024)S(1)}, f32[1000]{0:T(1024)}, u32[]{:S(2)}) copy-start(f32[1000]{0:T(1024)} %step_weight_ref.1) | copy-start | bytes 12004
  44.6 6.5 %copy-start.10 = (s32[2]{0:T(128)S(1)}, s32[2]{0:T(128)}, u32[]{:S(2)}) copy-start(s32[2]{0:T(128)} %timestep_ref.1) | copy-start | bytes 28
  44.6 23.1 %collective-permute-start.1 = (bf16[128,1280]{1,0:T(8,128)(2,1)}, bf16[128,1280]{1,0:T(8,128)(2,1)}, u32[]{:S(2)}, u32[]{:S(2)}) collective-permute-start(bf16[128,1280]{1,0:T(8,128)(2,1)} %pack.9), channel_id=1, source_target_pairs={{0,20},{4,16},{8,28},{12,24},{16,4},{20,0},{24,12},{28,8},{1,21},{... | collective-permute-start | bytes 983048 | tf_op jit(solution)/shard_map/ppermute | solution.py:330
  44.7 1.2 %copy-start.2 = (bf16[2,4096,64]{1,2,0:T(8,128)(2,1)S(1)}, bf16[2,4096,64]{1,2,0:T(8,128)(2,1)}, u32[]{:S(2)}) copy-start(bf16[2,4096,64]{1,2,0:T(8,128)(2,1)} %param.6) | copy-start | bytes 3145732
  45.9 1.0 %copy-start.4 = (bf16[128,1280]{1,0:T(8,128)(2,1)S(1)}, bf16[128,1280]{1,0:T(8,128)(2,1)}, u32[]{:S(2)}) copy-start(bf16[128,1280]{1,0:T(8,128)(2,1)} %copy-done.3) | copy-start | bytes 983044
  46.9 4.2 %copy-start.5 = (bf16[128,1280]{1,0:T(8,128)(2,1)S(1)}, bf16[128,1280]{1,0:T(8,128)(2,1)}, u32[]{:S(2)}) copy-start(bf16[128,1280]{1,0:T(8,128)(2,1)} %copy-done.3) | copy-start | bytes 983044
  46.9 4.2 %copy-start.7 = (bf16[128,1280]{1,0:T(8,128)(2,1)S(1)}, bf16[128,1280]{1,0:T(8,128)(2,1)}, u32[]{:S(2)}) copy-start(bf16[128,1280]{1,0:T(8,128)(2,1)} %copy-done.6) | copy-start | bytes 983044
  71.3 6.1 %collective-permute-start.7 = (bf16[2,64,128]{2,1,0:T(8,128)(2,1)S(1)}, bf16[2,64,128]{2,1,0:T(8,128)(2,1)S(1)}, u32[]{:S(2)}, u32[]{:S(2)}) collective-permute-start(bf16[2,64,128]{2,1,0:T(8,128)(2,1)S(1)} %get-tuple-element.28), channel_id=1, source_target_pairs={{0,24},{4,28},{8,16},{12,20},{16,8},{20,12},{24,0},{28,4},{1,25},{... | collective-permute-start | bytes 98312 | tf_op jit(solution)/shard_map/ppermute | solution.py:330
  73.4 4.8 %collective-permute-start.8 = (bf16[2,64,128]{2,1,0:T(8,128)(2,1)S(1)}, bf16[2,64,128]{2,1,0:T(8,128)(2,1)S(1)}, u32[]{:S(2)}, u32[]{:S(2)}) collective-permute-start(bf16[2,64,128]{2,1,0:T(8,128)(2,1)S(1)} %get-tuple-element.29), channel_id=1, source_target_pairs={{0,16},{4,20},{8,24},{12,28},{16,0},{20,4},{24,8},{28,12},{1,17},{... | collective-permute-start | bytes 98312 | tf_op jit(solution)/shard_map/ppermute | solution.py:330
  73.4 4.8 %collective-permute-start.9 = (bf16[2,64,128]{2,1,0:T(8,128)(2,1)S(1)}, bf16[2,64,128]{2,1,0:T(8,128)(2,1)S(1)}, u32[]{:S(2)}, u32[]{:S(2)}) collective-permute-start(bf16[2,64,128]{2,1,0:T(8,128)(2,1)S(1)} %get-tuple-element.30), channel_id=1, source_target_pairs={{0,8},{4,12},{8,0},{12,4},{16,24},{20,28},{24,16},{28,20},{1,9},{5... | collective-permute-start | bytes 98312 | tf_op jit(solution)/shard_map/ppermute | solution.py:330
  78.3 4.0 %collective-permute-start.10 = (f32[1,64,128]{2,1,0:T(8,128)S(1)}, f32[1,64,128]{2,1,0:T(8,128)S(1)}, u32[]{:S(2)}, u32[]{:S(2)}) collective-permute-start(f32[1,64,128]{2,1,0:T(8,128)S(1)} %slice.9), channel_id=1, source_target_pairs={{0,4},{4,0},{8,12},{12,8},{16,20},{20,16},{24,28},{28,24},{1,5},{5... | collective-permute-start | bytes 98312 | tf_op jit(solution)/shard_map/ppermute | solution.py:330
  82.2 3.6 %collective-permute-start.11 = (f32[64,128]{1,0:T(8,128)S(1)}, f32[64,128]{1,0:T(8,128)S(1)}, u32[]{:S(2)}, u32[]{:S(2)}) collective-permute-start(f32[64,128]{1,0:T(8,128)S(1)} %fusion), channel_id=1, source_target_pairs={{0,3},{1,2},{2,1},{3,0},{4,7},{5,6},{6,5},{7,4},{8,11},{9,10},{10,... | collective-permute-start | bytes 98312 | tf_op jit(solution)/shard_map/ppermute | solution.py:330
  82.2 4.0 %collective-permute-start.12 = (f32[64,128]{1,0:T(8,128)S(1)}, f32[64,128]{1,0:T(8,128)S(1)}, u32[]{:S(2)}, u32[]{:S(2)}) collective-permute-start(f32[64,128]{1,0:T(8,128)S(1)} %fusion), channel_id=1, source_target_pairs={{0,2},{1,3},{2,0},{3,1},{4,6},{5,7},{6,4},{7,5},{8,10},{9,11},{10,... | collective-permute-start | bytes 98312 | tf_op jit(solution)/shard_map/ppermute | solution.py:330
  83.9 2.4 %collective-permute-start.13 = (f32[64,128]{1,0:T(8,128)S(1)}, f32[64,128]{1,0:T(8,128)S(1)}, u32[]{:S(2)}, u32[]{:S(2)}) collective-permute-start(f32[64,128]{1,0:T(8,128)S(1)} %fusion), channel_id=1, source_target_pairs={{0,1},{1,0},{2,3},{3,2},{4,5},{5,4},{6,7},{7,6},{8,9},{9,8},{10,11... | collective-permute-start | bytes 98312 | tf_op jit(solution)/shard_map/ppermute | solution.py:330

commit v22 on v17

--- a/solution.py
+++ b/solution.py
@@ -143,10 +143,10 @@
     return [read(n) for n in range(0, len(pieces), 2)]
 
 
-def early_kernel(offsets, frames_ref, me_ref, timestep_ref, step_weight_ref, sign_ref, sample_ref, *refs):
+def early_kernel(offsets, late, frames_ref, me_ref, timestep_ref, step_weight_ref, sign_ref, sample_ref, *refs):
     count_pieces = len(offsets)
     arrived = refs[:count_pieces]
-    sums_ref, stats_ref, factor_ref, pieces, folded, asked, sems = refs[-7:]
+    sums_ref, stats_ref, factor_ref, pieces, folded, wide_ref, late_ref, asked, sems = refs[-9:]
     me = me_ref[0]
     rows = pieces.shape[1]
     count, lat, _ = sums_ref.shape
@@ -155,6 +155,9 @@
     for copy in copies:
         copy.start()
     factor_ref[...] = jnp.full(factor_ref.shape, sign_ref[0] * step_weight_ref[timestep_ref[sample_ref[0]]])
+    for ref, queries, keys in ((wide_ref, offsets, late), (late_ref, late, list(offsets) + list(late))):
+        for n, row in enumerate(mask_rows(frames_ref, me, rows, queries, keys)):
+            ref[n : n + 1] = row
     for copy in copies:
         copy.wait()
     pieces = [pieces.at[n] for n in range(count_pieces)]
@@ -190,19 +193,13 @@
     lax.fori_loop(0, blocks, some_blocks, 0)
 
 
-def late_kernel(offsets, late, frames_ref, me_ref, *refs):
+def late_kernel(offsets, late, *refs):
     early = len(offsets)
     arrived = refs[:2]
-    sums_ref, stats_ref, factor_ref, early_ref, early_folded, *out_refs, late_pieces, folded, sems = refs[2:]
-    copies = [pltpu.make_async_copy(arrived[n], late_pieces.at[n], sems.at[n]) for n in range(2)]
-    for copy in copies:
-        copy.start()
-    me = me_ref[0]
+    sums_ref, stats_ref, factor_ref, early_ref, early_folded, wide_ref, late_ref, *out_refs, folded = refs[2:]
     size, lat, rows = out_refs[0].shape
     count = folded.shape[0]
-    for copy in copies:
-        copy.wait()
-    pieces = [early_ref.at[n] for n in range(early)] + [late_pieces.at[n] for n in range(2)]
+    pieces = [early_ref.at[n] for n in range(early)] + list(arrived)
     stage_values(folded, pieces[early:], lat)
     factor = factor_ref[:1]
     every = list(offsets) + list(late)
@@ -217,8 +214,8 @@
 
     units = []
     for start, number, tiles_in in ((0, early, [blocks]), (early, 2, range(blocks + 1))):
-        key_offsets = [every[2 * t + j] for t in tiles_in for j in range(2)]
-        shifts = mask_rows(frames_ref, me, rows, every[start : start + number], key_offsets)
+        rows_ref = late_ref if start else wide_ref
+        shifts = [rows_ref[n : n + 1] for n in range(rows_ref.shape[0])]
         for i in range(count):
 
             def finish(summed, total, peak, start=start, number=number, i=i):
@@ -249,20 +246,23 @@
     run_units(units, lat)
 
 
-def attend_early(pieces, offsets, span_frames, me, timestep, step_weight, sign, sample, count, lat):
+def attend_early(pieces, offsets, late, span_frames, me, timestep, step_weight, sign, sample, count, lat):
     rows, width = pieces[0].shape
     blocks = len(pieces) // 2
     tokens = len(pieces) * rows
+    frames = rows // FRAME_TOK
     return pl.pallas_call(
-        functools.partial(early_kernel, offsets),
+        functools.partial(early_kernel, offsets, late),
         in_specs=[SMEM] * 6 + [HBM] * len(pieces),
-        out_specs=[VMEM] * 5,
+        out_specs=[VMEM] * 7,
         out_shape=[
             jax.ShapeDtypeStruct((count, lat, tokens), jnp.float32),
             jax.ShapeDtypeStruct((2, 8, tokens), jnp.float32),
             jax.ShapeDtypeStruct((8, rows), jnp.float32),
             jax.ShapeDtypeStruct((len(pieces), rows, width), jnp.bfloat16),
             jax.ShapeDtypeStruct((count, lat + 16, tokens), jnp.bfloat16),
+            jax.ShapeDtypeStruct((2 * frames, tokens), jnp.float32),
+            jax.ShapeDtypeStruct(((len(pieces) + 2) * frames, 2 * rows), jnp.float32),
         ],
         scratch_shapes=[
             pltpu.VMEM((blocks, count, 2 * rows, HD), jnp.bfloat16),
@@ -278,22 +278,18 @@
     )(span_frames, me, timestep, step_weight, sign, sample, *pieces)
 
 
-def attend_late(pieces, offsets, late, early, span_frames, me, count, lat):
+def attend_late(pieces, offsets, late, early, count, lat):
     rows, width = pieces[0].shape
     half = len(offsets) // 2 + 1
     tokens = 2 * half * rows
     return pl.pallas_call(
         functools.partial(late_kernel, offsets, late),
-        in_specs=[SMEM] * 2 + [HBM] * 2 + [VMEM] * len(early),
+        in_specs=[VMEM] * (2 + len(early)),
         out_specs=[VMEM] * 4,
         out_shape=[
             jax.ShapeDtypeStruct((half // 2, lat, rows), jnp.bfloat16 if g else jnp.float32) for g in range(4)
         ],
-        scratch_shapes=[
-            pltpu.VMEM((2, rows, width), jnp.bfloat16),
-            pltpu.VMEM((count, lat + 16, 2 * rows), jnp.bfloat16),
-            pltpu.SemaphoreType.DMA((2,)),
-        ],
+        scratch_shapes=[pltpu.VMEM((count, lat + 16, 2 * rows), jnp.bfloat16)],
         compiler_params=pltpu.CompilerParams(vmem_limit_bytes=SMALL_VMEM if half <= 4 else LARGE_VMEM),
         cost_estimate=pl.CostEstimate(
             flops=count * tokens * rows * 4 * (HD + lat),
@@ -301,7 +297,7 @@
             transcendentals=count * tokens * rows * 2,
         ),
         name="attend_late",
-    )(span_frames, me, *pieces, *early)
+    )(*pieces, *early)
 
 
 def swap(array, axis, offset):
@@ -335,10 +331,10 @@
     late = [half, half + 1]
     early = [k for k in range(seq_count) if k not in late]
     merged = attend_early(
-        [pieces[k] for k in early], early, span_frames, me, timestep, step_weight, sign, sample, count, lat
+        [pieces[k] for k in early], early, late, span_frames, me, timestep, step_weight, sign, sample, count, lat
     )
     ends = [pieces[k] for k in late]
-    given = attend_late(ends, early, late, merged, span_frames, me, count, lat)
+    given = attend_late(ends, early, late, merged, count, lat)
     size = half // 2
     while True:
         keep = given[0]

time: 87.6 us -> 87.1 us (level)
  transfers between devices with their start and end apart: 14 -> 14, of which waited for: 9 -> 9; matrix products, arithmetic and copies ran while one was open for 0% -> 0% of each run, Pallas kernels for 16% -> 17%
where the time goes in v22:
time: 87.1 us; the launch traced here: 86.8 us
  waiting for transfers between devices  39.9 us (46%)
  starting transfers between devices  23.1 us (27%)
  Pallas kernels  20.3 us (23%)
  local copies, waits for them, and re-layouts  2.69 us (3%)
    ppermute x14, waiting for transfers between devices, swap(): return lax.ppermute(array, axis, [(i, i ^ offset) for i in range(size)])  39.9 us
    ppermute x14, starting transfers between devices, swap(): return lax.ppermute(array, axis, [(i, i ^ offset) for i in range(size)])  23.1 us
    pallas_call x8, Pallas kernels, pack(): pl.pallas_call(functools.partial(pack_kernel, k), in_specs=[SMEM, SMEM] +...  11 us
    pallas_call x1, Pallas kernels, attend_early(): pl.pallas_call(functools.partial(early_kernel, offsets, late), in_specs=[...  5.77 us
    pallas_call x1, Pallas kernels, attend_late(): pl.pallas_call(functools.partial(late_kernel, offsets, late), in_specs=[V...  3.48 us
    unnamed x20, local copies, waits for them, and re-layouts  2.69 us
  transfers between devices with their start and end apart: 14, of which 9 were waited for; matrix products, arithmetic and copies ran while one was open for 0% of the time, Pallas kernels for 17%

profile of v22, /device:TPU:0, one launch (start us, length us, event | category | flops | bytes accessed | tf_op | source)
XLA Modules:
  0.0 86.8 jit_solution(3376727949649939798)
XLA Ops:
  0.0 2.4 %pack.10 = bf16[128,1280]{1,0:T(8,128)(2,1)} custom-call(s32[1]{0:T(128)} %bitcast.me_ref, s32[1]{0:T(128)} %bitcast.1.model_ref, bf16[1,128,12288]{2,1,0:T(8,128)(2,1)} %qkv_ref.15, bf16[2,64,4096]{2,1,0:T(8,128)(2,1)} %bitcast.9), custom_call_target="tpu_custom_call" | custom-call | bytes 655360 | tf_op jit(solution)/shard_map/pack/pallas_call | solution.py:67
  2.4 6.0 %collective-permute-start.2 = (bf16[128,1280]{1,0:T(8,128)(2,1)}, bf16[128,1280]{1,0:T(8,128)(2,1)S(1)}, u32[]{:S(2)}, u32[]{:S(2)}) collective-permute-start(bf16[128,1280]{1,0:T(8,128)(2,1)} %pack.10), channel_id=1, source_target_pairs={{0,28},{4,24},{8,20},{12,16},{16,12},{20,8},{24,4},{28,0},{1,29},{... | collective-permute-start | bytes 983048 | tf_op jit(solution)/shard_map/ppermute | solution.py:305
  8.5 0.0 copy-done
  8.5 1.2 %copy-done.1 = bf16[2,4096,64]{1,2,0:T(8,128)(2,1)S(1)} copy-done((bf16[2,4096,64]{1,2,0:T(8,128)(2,1)S(1)}, bf16[2,4096,64]{1,2,0:T(8,128)(2,1)}, u32[]{:S(2)}) %copy-start.1) | copy-done | bytes 1048600
  9.7 0.8 pack.12
  10.5 0.1 collective-permute-start.4
  10.6 0.8 pack.8
  11.4 0.9 %collective-permute-start = (bf16[128,1280]{1,0:T(8,128)(2,1)S(1)}, bf16[128,1280]{1,0:T(8,128)(2,1)S(1)}, u32[]{:S(2)}, u32[]{:S(2)}) collective-permute-start(bf16[128,1280]{1,0:T(8,128)(2,1)S(1)} %pack.8), channel_id=1, source_target_pairs={{0,24},{4,28},{8,16},{12,20},{16,8},{20,12},{24,0},{28,4},{1,25},{... | collective-permute-start | bytes 983048 | tf_op jit(solution)/shard_map/ppermute | solution.py:305
  12.3 4.9 %collective-permute-done.2.refs_0_.refs_1_.refs_5_ = bf16[128,1280]{1,0:T(8,128)(2,1)S(1)} collective-permute-done((bf16[128,1280]{1,0:T(8,128)(2,1)}, bf16[128,1280]{1,0:T(8,128)(2,1)S(1)}, u32[]{:S(2)}, u32[]{:S(2)}) %collective-permute-start.2) | collective-permute-done | bytes 327712 | tf_op jit(solution)/shard_map/ppermute | solution.py:305
  17.3 10.7 %collective-permute-done.4.refs_0_.refs_3_ = bf16[128,1280]{1,0:T(8,128)(2,1)S(1)} collective-permute-done((bf16[128,1280]{1,0:T(8,128)(2,1)S(1)}, bf16[128,1280]{1,0:T(8,128)(2,1)S(1)}, u32[]{:S(2)}, u32[]{:S(2)}) %collective-permute-start.4) | collective-permute-done | bytes 327712 | tf_op jit(solution)/shard_map/ppermute | solution.py:305
  28.0 1.5 %pack.15 = bf16[128,1280]{1,0:T(8,128)(2,1)} custom-call(s32[1]{0:T(128)} %bitcast.me_ref, s32[1]{0:T(128)} %bitcast.1.model_ref, bf16[1,128,12288]{2,1,0:T(8,128)(2,1)S(1)} %copy-done, bf16[2,64,4096]{2,1,0:T(8,128)(2,1)S(1)} %bitcast.12, bf16[128,1280]{1,0:T(8,128)(2,1)S(1)} %collective-permute-done.4.refs_0_.refs_3_, ...), custom_call_target="tpu_custom_call" | custom-call | bytes 655360 | tf_op jit(solution)/shard_map/pack/pallas_call | solution.py:67
  29.5 2.7 %collective-permute-start.6 = (bf16[128,1280]{1,0:T(8,128)(2,1)}, bf16[128,1280]{1,0:T(8,128)(2,1)}, u32[]{:S(2)}, u32[]{:S(2)}) collective-permute-start(bf16[128,1280]{1,0:T(8,128)(2,1)} %pack.15), channel_id=1, source_target_pairs={{0,8},{4,12},{8,0},{12,4},{16,24},{20,28},{24,16},{28,20},{1,9},{5... | collective-permute-start | bytes 983048 | tf_op jit(solution)/shard_map/ppermute | solution.py:305
  32.2 1.6 %pack.14 = bf16[128,1280]{1,0:T(8,128)(2,1)} custom-call(s32[1]{0:T(128)} %bitcast.me_ref, s32[1]{0:T(128)} %bitcast.1.model_ref, bf16[1,128,12288]{2,1,0:T(8,128)(2,1)S(1)} %copy-done, bf16[2,64,4096]{2,1,0:T(8,128)(2,1)S(1)} %bitcast.13, bf16[128,1280]{1,0:T(8,128)(2,1)S(1)} %collective-permute-done.4.refs_0_.refs_3_), custom_call_target="tpu_custom_call" | custom-call | bytes 655360 | tf_op jit(solution)/shard_map/pack/pallas_call | solution.py:67
  33.8 1.4 %collective-permute-start.5 = (bf16[128,1280]{1,0:T(8,128)(2,1)}, bf16[128,1280]{1,0:T(8,128)(2,1)}, u32[]{:S(2)}, u32[]{:S(2)}) collective-permute-start(bf16[128,1280]{1,0:T(8,128)(2,1)} %pack.14), channel_id=1, source_target_pairs={{0,4},{4,0},{8,12},{12,8},{16,20},{20,16},{24,28},{28,24},{1,5},{5... | collective-permute-start | bytes 983048 | tf_op jit(solution)/shard_map/ppermute | solution.py:305
  35.2 0.0 copy-done.3
  35.2 1.5 %pack.11 = bf16[128,1280]{1,0:T(8,128)(2,1)} custom-call(s32[1]{0:T(128)} %bitcast.me_ref, s32[1]{0:T(128)} %bitcast.1.model_ref, bf16[1,128,12288]{2,1,0:T(8,128)(2,1)S(1)} %copy-done, bf16[2,64,4096]{2,1,0:T(8,128)(2,1)S(1)} %bitcast.14, bf16[128,1280]{1,0:T(8,128)(2,1)S(1)} %collective-permute-done.2.refs_0_.refs_1_.refs_5_), custom_call_target="tpu_custom_call" | custom-call | bytes 655360 | tf_op jit(solution)/shard_map/pack/pallas_call | solution.py:67
  36.7 0.1 collective-permute-start.3
  36.8 0.0 collective-permute-done.refs_0_.refs_4_
  36.8 1.6 %pack.9 = bf16[128,1280]{1,0:T(8,128)(2,1)} custom-call(s32[1]{0:T(128)} %bitcast.me_ref, s32[1]{0:T(128)} %bitcast.1.model_ref, bf16[1,128,12288]{2,1,0:T(8,128)(2,1)S(1)} %copy-done, bf16[2,64,4096]{2,1,0:T(8,128)(2,1)S(1)} %bitcast.15, bf16[128,1280]{1,0:T(8,128)(2,1)S(1)} %collective-permute-done.refs_0_.refs_4_), custom_call_target="tpu_custom_call" | custom-call | bytes 655360 | tf_op jit(solution)/shard_map/pack/pallas_call | solution.py:67
  38.4 0.0 copy-start.7
  38.4 0.0 copy-start.8
  38.4 0.0 copy-start.9
  38.4 5.0 %collective-permute-start.1 = (bf16[128,1280]{1,0:T(8,128)(2,1)}, bf16[128,1280]{1,0:T(8,128)(2,1)}, u32[]{:S(2)}, u32[]{:S(2)}) collective-permute-start(bf16[128,1280]{1,0:T(8,128)(2,1)} %pack.9), channel_id=1, source_target_pairs={{0,16},{4,20},{8,24},{12,28},{16,0},{20,4},{24,8},{28,12},{1,17},{... | collective-permute-start | bytes 983048 | tf_op jit(solution)/shard_map/ppermute | solution.py:305
  43.5 1.2 %copy-done.2 = bf16[2,4096,64]{1,2,0:T(8,128)(2,1)S(1)} copy-done((bf16[2,4096,64]{1,2,0:T(8,128)(2,1)S(1)}, bf16[2,4096,64]{1,2,0:T(8,128)(2,1)}, u32[]{:S(2)}) %copy-start.2) | copy-done | bytes 1048600
  44.7 0.8 pack.13.refs_0_
  45.5 0.0 collective-permute-done.6.refs_2_
  45.5 0.0 collective-permute-done.5.refs_1_
  45.6 0.1 copy-done.4
  45.7 0.1 copy-done.6
  45.8 5.8 %attend_early.1 = (f32[4,64,768]{2,1,0:T(8,128)S(1)}, f32[2,8,768]{2,1,0:T(8,128)S(1)}, f32[8,128]{1,0:T(8,128)S(1)}, bf16[6,128,1280]{2,1,0:T(8,128)(2,1)S(1)},...) custom-call(s32[4]{0:T(128)S(1)} %copy-done.8, s32[1]{0:T(128)} %bitcast.me_ref, ...), custom_call_target="tpu_custom_call" | custom-call | flops 905969664 | bytes 2359296 | tf_op jit(solution)/shard_map/attend_early/pallas_call | solution.py:254
  51.5 10.8 %collective-permute-done.3.refs_1_ = bf16[128,1280]{1,0:T(8,128)(2,1)} collective-permute-done((bf16[128,1280]{1,0:T(8,128)(2,1)}, bf16[128,1280]{1,0:T(8,128)(2,1)}, u32[]{:S(2)}, u32[]{:S(2)}) %collective-permute-start.3) | collective-permute-done | bytes 327712 | tf_op jit(solution)/shard_map/ppermute | solution.py:305
  62.4 5.2 %collective-permute-done.1.refs_0_ = bf16[128,1280]{1,0:T(8,128)(2,1)} collective-permute-done((bf16[128,1280]{1,0:T(8,128)(2,1)}, bf16[128,1280]{1,0:T(8,128)(2,1)}, u32[]{:S(2)}, u32[]{:S(2)}) %collective-permute-start.1) | collective-permute-done | bytes 327712 | tf_op jit(solution)/shard_map/ppermute | solution.py:305
  67.6 3.5 %attend_late.1 = (f32[2,64,128]{2,1,0:T(8,128)S(1)}, bf16[2,64,128]{2,1,0:T(8,128)(2,1)S(1)}, bf16[2,64,128]{2,1,0:T(8,128)(2,1)S(1)}, bf16[2,64,128]{2,1,0:T(8,128)(2,1)S(1)}) custom-call(bf16[128,1280]{1,0:T(8,128)(2,1)} %collective-permute-done.1.refs_0_, bf16[128,1280]{1,0:T(8,128)(2,1)} %collective-permute-done.3.refs_1_, ...), custom_call_target="tpu_custom_call" | custom-call | flops 402653184 | bytes 3145728 | tf_op jit(solution)/shard_map/attend_late/pallas_call | solution.py:285
  71.1 2.2 %collective-permute-start.7 = (bf16[2,64,128]{2,1,0:T(8,128)(2,1)S(1)}, bf16[2,64,128]{2,1,0:T(8,128)(2,1)S(1)}, u32[]{:S(2)}, u32[]{:S(2)}) collective-permute-start(bf16[2,64,128]{2,1,0:T(8,128)(2,1)S(1)} %get-tuple-element.24), channel_id=1, source_target_pairs={{0,24},{4,28},{8,16},{12,20},{16,8},{20,12},{24,0},{28,4},{1,25},{... | collective-permute-start | bytes 98312 | tf_op jit(solution)/shard_map/ppermute | solution.py:305
  73.3 0.0 collective-permute-start.8
  73.3 2.2 %collective-permute-start.9 = (bf16[2,64,128]{2,1,0:T(8,128)(2,1)S(1)}, bf16[2,64,128]{2,1,0:T(8,128)(2,1)S(1)}, u32[]{:S(2)}, u32[]{:S(2)}) collective-permute-start(bf16[2,64,128]{2,1,0:T(8,128)(2,1)S(1)} %get-tuple-element.26), channel_id=1, source_target_pairs={{0,8},{4,12},{8,0},{12,4},{16,24},{20,28},{24,16},{28,20},{1,9},{5... | collective-permute-start | bytes 98312 | tf_op jit(solution)/shard_map/ppermute | solution.py:305
  75.5 1.5 %collective-permute-done.7 = bf16[2,64,128]{2,1,0:T(8,128)(2,1)S(1)} collective-permute-done((bf16[2,64,128]{2,1,0:T(8,128)(2,1)S(1)}, bf16[2,64,128]{2,1,0:T(8,128)(2,1)S(1)}, u32[]{:S(2)}, u32[]{:S(2)}) %collective-permute-start.7) | collective-permute-done | bytes 32800 | tf_op jit(solution)/shard_map/ppermute | solution.py:305
  77.1 1.1 %collective-permute-done.8 = bf16[2,64,128]{2,1,0:T(8,128)(2,1)S(1)} collective-permute-done((bf16[2,64,128]{2,1,0:T(8,128)(2,1)S(1)}, bf16[2,64,128]{2,1,0:T(8,128)(2,1)S(1)}, u32[]{:S(2)}, u32[]{:S(2)}) %collective-permute-start.8) | collective-permute-done | bytes 32800 | tf_op jit(solution)/shard_map/ppermute | solution.py:305
  78.1 0.0 collective-permute-done.9
  78.2 0.6 collective-permute-start.10
  78.8 3.4 %collective-permute-done.10 = f32[1,64,128]{2,1,0:T(8,128)S(1)} collective-permute-done((f32[1,64,128]{2,1,0:T(8,128)S(1)}, f32[1,64,128]{2,1,0:T(8,128)S(1)}, u32[]{:S(2)}, u32[]{:S(2)}) %collective-permute-start.10) | collective-permute-done | bytes 32800 | tf_op jit(solution)/shard_map/ppermute | solution.py:305
  82.2 0.0 collective-permute-start.11
  82.2 1.6 %collective-permute-start.12 = (f32[64,128]{1,0:T(8,128)S(1)}, f32[64,128]{1,0:T(8,128)S(1)}, u32[]{:S(2)}, u32[]{:S(2)}) collective-permute-start(f32[64,128]{1,0:T(8,128)S(1)} %fusion), channel_id=1, source_target_pairs={{0,2},{1,3},{2,0},{3,1},{4,6},{5,7},{6,4},{7,5},{8,10},{9,11},{10,... | collective-permute-start | bytes 98312 | tf_op jit(solution)/shard_map/ppermute | solution.py:305
  83.8 0.3 collective-permute-start.13
  84.0 1.8 %collective-permute-done.11 = f32[64,128]{1,0:T(8,128)S(1)} collective-permute-done((f32[64,128]{1,0:T(8,128)S(1)}, f32[64,128]{1,0:T(8,128)S(1)}, u32[]{:S(2)}, u32[]{:S(2)}) %collective-permute-start.11) | collective-permute-done | bytes 32800 | tf_op jit(solution)/shard_map/ppermute | solution.py:305
  85.8 0.4 collective-permute-done.12
  86.2 0.0 collective-permute-done.13
  86.2 0.6 add_bitcast_fusion
  (14 shorter events, 0.0 us)
Async XLA Ops:
  0.0 8.5 %copy-start = (bf16[1,128,12288]{2,1,0:T(8,128)(2,1)S(1)}, bf16[1,128,12288]{2,1,0:T(8,128)(2,1)}, u32[]{:S(2)}) copy-start(bf16[1,128,12288]{2,1,0:T(8,128)(2,1)} %qkv_ref.15) | copy-start | bytes 9437188
  2.4 14.8 %collective-permute-start.2 = (bf16[128,1280]{1,0:T(8,128)(2,1)}, bf16[128,1280]{1,0:T(8,128)(2,1)S(1)}, u32[]{:S(2)}, u32[]{:S(2)}) collective-permute-start(bf16[128,1280]{1,0:T(8,128)(2,1)} %pack.10), channel_id=1, source_target_pairs={{0,28},{4,24},{8,20},{12,16},{16,12},{20,8},{24,4},{28,0},{1,29},{... | collective-permute-start | bytes 983048 | tf_op jit(solution)/shard_map/ppermute | solution.py:305
  8.5 1.2 %copy-start.1 = (bf16[2,4096,64]{1,2,0:T(8,128)(2,1)S(1)}, bf16[2,4096,64]{1,2,0:T(8,128)(2,1)}, u32[]{:S(2)}) copy-start(bf16[2,4096,64]{1,2,0:T(8,128)(2,1)} %param.6) | copy-start | bytes 3145732
  10.5 17.5 %collective-permute-start.4 = (bf16[128,1280]{1,0:T(8,128)(2,1)S(1)}, bf16[128,1280]{1,0:T(8,128)(2,1)S(1)}, u32[]{:S(2)}, u32[]{:S(2)}) collective-permute-start(bf16[128,1280]{1,0:T(8,128)(2,1)S(1)} %pack.12), channel_id=1, source_target_pairs={{0,12},{4,8},{8,4},{12,0},{16,28},{20,24},{24,20},{28,16},{1,13},{... | collective-permute-start | bytes 983048 | tf_op jit(solution)/shard_map/ppermute | solution.py:305
  11.4 25.4 %collective-permute-start = (bf16[128,1280]{1,0:T(8,128)(2,1)S(1)}, bf16[128,1280]{1,0:T(8,128)(2,1)S(1)}, u32[]{:S(2)}, u32[]{:S(2)}) collective-permute-start(bf16[128,1280]{1,0:T(8,128)(2,1)S(1)} %pack.8), channel_id=1, source_target_pairs={{0,24},{4,28},{8,16},{12,20},{16,8},{20,12},{24,0},{28,4},{1,25},{... | collective-permute-start | bytes 983048 | tf_op jit(solution)/shard_map/ppermute | solution.py:305
  17.3 17.9 %copy-start.3 = (bf16[128,1280]{1,0:T(8,128)(2,1)}, bf16[128,1280]{1,0:T(8,128)(2,1)S(1)}, u32[]{:S(2)}) copy-start(bf16[128,1280]{1,0:T(8,128)(2,1)S(1)} %collective-permute-done.2.refs_0_.refs_1_.refs_5_) | copy-start | bytes 983044
  29.5 16.0 %collective-permute-start.6 = (bf16[128,1280]{1,0:T(8,128)(2,1)}, bf16[128,1280]{1,0:T(8,128)(2,1)}, u32[]{:S(2)}, u32[]{:S(2)}) collective-permute-start(bf16[128,1280]{1,0:T(8,128)(2,1)} %pack.15), channel_id=1, source_target_pairs={{0,8},{4,12},{8,0},{12,4},{16,24},{20,28},{24,16},{28,20},{1,9},{5... | collective-permute-start | bytes 983048 | tf_op jit(solution)/shard_map/ppermute | solution.py:305
  33.8 11.8 %collective-permute-start.5 = (bf16[128,1280]{1,0:T(8,128)(2,1)}, bf16[128,1280]{1,0:T(8,128)(2,1)}, u32[]{:S(2)}, u32[]{:S(2)}) collective-permute-start(bf16[128,1280]{1,0:T(8,128)(2,1)} %pack.14), channel_id=1, source_target_pairs={{0,4},{4,0},{8,12},{12,8},{16,20},{20,16},{24,28},{28,24},{1,5},{5... | collective-permute-start | bytes 983048 | tf_op jit(solution)/shard_map/ppermute | solution.py:305
  36.7 25.7 %collective-permute-start.3 = (bf16[128,1280]{1,0:T(8,128)(2,1)}, bf16[128,1280]{1,0:T(8,128)(2,1)}, u32[]{:S(2)}, u32[]{:S(2)}) collective-permute-start(bf16[128,1280]{1,0:T(8,128)(2,1)} %pack.11), channel_id=1, source_target_pairs={{0,20},{4,16},{8,28},{12,24},{16,4},{20,0},{24,12},{28,8},{1,21},{... | collective-permute-start | bytes 983048 | tf_op jit(solution)/shard_map/ppermute | solution.py:305
  36.8 1.6 %copy-start.5 = (bf16[128,1280]{1,0:T(8,128)(2,1)}, bf16[128,1280]{1,0:T(8,128)(2,1)S(1)}, u32[]{:S(2)}) copy-start(bf16[128,1280]{1,0:T(8,128)(2,1)S(1)} %collective-permute-done.refs_0_.refs_4_) | copy-start | bytes 983044
  38.4 7.1 %copy-start.7 = (f32[1000]{0:T(1024)S(1)}, f32[1000]{0:T(1024)}, u32[]{:S(2)}) copy-start(f32[1000]{0:T(1024)} %step_weight_ref.1) | copy-start | bytes 12004
  38.4 7.1 %copy-start.8 = (s32[4]{0:T(128)S(1)}, s32[4]{0:T(128)}, u32[]{:S(2)}) copy-start(s32[4]{0:T(128)} %frames_ref.1) | copy-start | bytes 52
  38.4 7.1 %copy-start.9 = (s32[2]{0:T(128)S(1)}, s32[2]{0:T(128)}, u32[]{:S(2)}) copy-start(s32[2]{0:T(128)} %timestep_ref.1) | copy-start | bytes 28
  38.4 29.2 %collective-permute-start.1 = (bf16[128,1280]{1,0:T(8,128)(2,1)}, bf16[128,1280]{1,0:T(8,128)(2,1)}, u32[]{:S(2)}, u32[]{:S(2)}) collective-permute-start(bf16[128,1280]{1,0:T(8,128)(2,1)} %pack.9), channel_id=1, source_target_pairs={{0,16},{4,20},{8,24},{12,28},{16,0},{20,4},{24,8},{28,12},{1,17},{... | collective-permute-start | bytes 983048 | tf_op jit(solution)/shard_map/ppermute | solution.py:305
  43.5 1.2 %copy-start.2 = (bf16[2,4096,64]{1,2,0:T(8,128)(2,1)S(1)}, bf16[2,4096,64]{1,2,0:T(8,128)(2,1)}, u32[]{:S(2)}) copy-start(bf16[2,4096,64]{1,2,0:T(8,128)(2,1)} %param.6) | copy-start | bytes 3145732
  44.7 1.0 %copy-start.4 = (bf16[128,1280]{1,0:T(8,128)(2,1)S(1)}, bf16[128,1280]{1,0:T(8,128)(2,1)}, u32[]{:S(2)}) copy-start(bf16[128,1280]{1,0:T(8,128)(2,1)} %copy-done.3) | copy-start | bytes 983044
  44.7 1.1 %copy-start.6 = (bf16[128,1280]{1,0:T(8,128)(2,1)S(1)}, bf16[128,1280]{1,0:T(8,128)(2,1)}, u32[]{:S(2)}) copy-start(bf16[128,1280]{1,0:T(8,128)(2,1)} %copy-done.5) | copy-start | bytes 983044
  71.1 6.0 %collective-permute-start.7 = (bf16[2,64,128]{2,1,0:T(8,128)(2,1)S(1)}, bf16[2,64,128]{2,1,0:T(8,128)(2,1)S(1)}, u32[]{:S(2)}, u32[]{:S(2)}) collective-permute-start(bf16[2,64,128]{2,1,0:T(8,128)(2,1)S(1)} %get-tuple-element.24), channel_id=1, source_target_pairs={{0,24},{4,28},{8,16},{12,20},{16,8},{20,12},{24,0},{28,4},{1,25},{... | collective-permute-start | bytes 98312 | tf_op jit(solution)/shard_map/ppermute | solution.py:305
  73.3 4.8 %collective-permute-start.8 = (bf16[2,64,128]{2,1,0:T(8,128)(2,1)S(1)}, bf16[2,64,128]{2,1,0:T(8,128)(2,1)S(1)}, u32[]{:S(2)}, u32[]{:S(2)}) collective-permute-start(bf16[2,64,128]{2,1,0:T(8,128)(2,1)S(1)} %get-tuple-element.25), channel_id=1, source_target_pairs={{0,16},{4,20},{8,24},{12,28},{16,0},{20,4},{24,8},{28,12},{1,17},{... | collective-permute-start | bytes 98312 | tf_op jit(solution)/shard_map/ppermute | solution.py:305
  73.3 4.8 %collective-permute-start.9 = (bf16[2,64,128]{2,1,0:T(8,128)(2,1)S(1)}, bf16[2,64,128]{2,1,0:T(8,128)(2,1)S(1)}, u32[]{:S(2)}, u32[]{:S(2)}) collective-permute-start(bf16[2,64,128]{2,1,0:T(8,128)(2,1)S(1)} %get-tuple-element.26), channel_id=1, source_target_pairs={{0,8},{4,12},{8,0},{12,4},{16,24},{20,28},{24,16},{28,20},{1,9},{5... | collective-permute-start | bytes 98312 | tf_op jit(solution)/shard_map/ppermute | solution.py:305
  78.2 4.0 %collective-permute-start.10 = (f32[1,64,128]{2,1,0:T(8,128)S(1)}, f32[1,64,128]{2,1,0:T(8,128)S(1)}, u32[]{:S(2)}, u32[]{:S(2)}) collective-permute-start(f32[1,64,128]{2,1,0:T(8,128)S(1)} %slice.9), channel_id=1, source_target_pairs={{0,4},{4,0},{8,12},{12,8},{16,20},{20,16},{24,28},{28,24},{1,5},{5... | collective-permute-start | bytes 98312 | tf_op jit(solution)/shard_map/ppermute | solution.py:305
  82.2 3.6 %collective-permute-start.11 = (f32[64,128]{1,0:T(8,128)S(1)}, f32[64,128]{1,0:T(8,128)S(1)}, u32[]{:S(2)}, u32[]{:S(2)}) collective-permute-start(f32[64,128]{1,0:T(8,128)S(1)} %fusion), channel_id=1, source_target_pairs={{0,3},{1,2},{2,1},{3,0},{4,7},{5,6},{6,5},{7,4},{8,11},{9,10},{10,... | collective-permute-start | bytes 98312 | tf_op jit(solution)/shard_map/ppermute | solution.py:305
  82.2 4.0 %collective-permute-start.12 = (f32[64,128]{1,0:T(8,128)S(1)}, f32[64,128]{1,0:T(8,128)S(1)}, u32[]{:S(2)}, u32[]{:S(2)}) collective-permute-start(f32[64,128]{1,0:T(8,128)S(1)} %fusion), channel_id=1, source_target_pairs={{0,2},{1,3},{2,0},{3,1},{4,6},{5,7},{6,4},{7,5},{8,10},{9,11},{10,... | collective-permute-start | bytes 98312 | tf_op jit(solution)/shard_map/ppermute | solution.py:305
  83.8 2.5 %collective-permute-start.13 = (f32[64,128]{1,0:T(8,128)S(1)}, f32[64,128]{1,0:T(8,128)S(1)}, u32[]{:S(2)}, u32[]{:S(2)}) collective-permute-start(f32[64,128]{1,0:T(8,128)S(1)} %fusion), channel_id=1, source_target_pairs={{0,1},{1,0},{2,3},{3,2},{4,5},{5,4},{6,7},{7,6},{8,9},{9,8},{10,11... | collective-permute-start | bytes 98312 | tf_op jit(solution)/shard_map/ppermute | solution.py:305

commit v23 on v22

--- a/solution.py
+++ b/solution.py
@@ -338,7 +338,7 @@
     size = half // 2
     while True:
         keep = given[0]
-        for n in range(len(given) - 1, 0, -1):
+        for n in [2, 3, 1] if len(given) == 4 else range(1, len(given)):
             keep = keep + swap(given[n], "seq", n * size).astype(jnp.float32)
         if size == 1:
             break

time: 87.1 us -> 86.3 us (level)
  transfers between devices with their start and end apart: 14 -> 14, of which waited for: 9 -> 10; matrix products, arithmetic and copies ran while one was open for 0% -> 0% of each run, Pallas kernels for 17% -> 17%
where the time goes in v23:
time: 86.3 us; the launch traced here: 86 us
  waiting for transfers between devices  39.9 us (46%)
  starting transfers between devices  22.3 us (26%)
  Pallas kernels  20.3 us (24%)
  local copies, waits for them, and re-layouts  2.69 us (3%)
    ppermute x14, waiting for transfers between devices, swap(): return lax.ppermute(array, axis, [(i, i ^ offset) for i in range(size)])  39.9 us
    ppermute x14, starting transfers between devices, swap(): return lax.ppermute(array, axis, [(i, i ^ offset) for i in range(size)])  22.3 us
    pallas_call x8, Pallas kernels, pack(): pl.pallas_call(functools.partial(pack_kernel, k), in_specs=[SMEM, SMEM] +...  11 us
    pallas_call x1, Pallas kernels, attend_early(): pl.pallas_call(functools.partial(early_kernel, offsets, late), in_specs=[...  5.77 us
    pallas_call x1, Pallas kernels, attend_late(): pl.pallas_call(functools.partial(late_kernel, offsets, late), in_specs=[V...  3.48 us
    unnamed x20, local copies, waits for them, and re-layouts  2.69 us
  transfers between devices with their start and end apart: 14, of which 10 were waited for; matrix products, arithmetic and copies ran while one was open for 0% of the time, Pallas kernels for 17%

profile of v23, /device:TPU:0, one launch (start us, length us, event | category | flops | bytes accessed | tf_op | source)
XLA Modules:
  0.0 86.0 jit_solution(10719524539574933949)
XLA Ops:
  0.0 2.4 %pack.10 = bf16[128,1280]{1,0:T(8,128)(2,1)} custom-call(s32[1]{0:T(128)} %bitcast.me_ref, s32[1]{0:T(128)} %bitcast.1.model_ref, bf16[1,128,12288]{2,1,0:T(8,128)(2,1)} %qkv_ref.15, bf16[2,64,4096]{2,1,0:T(8,128)(2,1)} %bitcast.9), custom_call_target="tpu_custom_call" | custom-call | bytes 655360 | tf_op jit(solution)/shard_map/pack/pallas_call | solution.py:67
  2.4 6.0 %collective-permute-start.2 = (bf16[128,1280]{1,0:T(8,128)(2,1)}, bf16[128,1280]{1,0:T(8,128)(2,1)S(1)}, u32[]{:S(2)}, u32[]{:S(2)}) collective-permute-start(bf16[128,1280]{1,0:T(8,128)(2,1)} %pack.10), channel_id=1, source_target_pairs={{0,28},{4,24},{8,20},{12,16},{16,12},{20,8},{24,4},{28,0},{1,29},{... | collective-permute-start | bytes 983048 | tf_op jit(solution)/shard_map/ppermute | solution.py:305
  8.5 1.2 %copy-done.1 = bf16[2,4096,64]{1,2,0:T(8,128)(2,1)S(1)} copy-done((bf16[2,4096,64]{1,2,0:T(8,128)(2,1)S(1)}, bf16[2,4096,64]{1,2,0:T(8,128)(2,1)}, u32[]{:S(2)}) %copy-start.1) | copy-done | bytes 1048600
  9.7 0.8 pack.12
  10.5 0.1 collective-permute-start.4
  10.6 0.8 pack.8
  11.4 0.9 %collective-permute-start = (bf16[128,1280]{1,0:T(8,128)(2,1)S(1)}, bf16[128,1280]{1,0:T(8,128)(2,1)S(1)}, u32[]{:S(2)}, u32[]{:S(2)}) collective-permute-start(bf16[128,1280]{1,0:T(8,128)(2,1)S(1)} %pack.8), channel_id=1, source_target_pairs={{0,24},{4,28},{8,16},{12,20},{16,8},{20,12},{24,0},{28,4},{1,25},{... | collective-permute-start | bytes 983048 | tf_op jit(solution)/shard_map/ppermute | solution.py:305
  12.3 4.9 %collective-permute-done.2.refs_0_.refs_1_.refs_5_ = bf16[128,1280]{1,0:T(8,128)(2,1)S(1)} collective-permute-done((bf16[128,1280]{1,0:T(8,128)(2,1)}, bf16[128,1280]{1,0:T(8,128)(2,1)S(1)}, u32[]{:S(2)}, u32[]{:S(2)}) %collective-permute-start.2) | collective-permute-done | bytes 327712 | tf_op jit(solution)/shard_map/ppermute | solution.py:305
  17.3 10.7 %collective-permute-done.4.refs_0_.refs_3_ = bf16[128,1280]{1,0:T(8,128)(2,1)S(1)} collective-permute-done((bf16[128,1280]{1,0:T(8,128)(2,1)S(1)}, bf16[128,1280]{1,0:T(8,128)(2,1)S(1)}, u32[]{:S(2)}, u32[]{:S(2)}) %collective-permute-start.4) | collective-permute-done | bytes 327712 | tf_op jit(solution)/shard_map/ppermute | solution.py:305
  28.0 1.5 %pack.15 = bf16[128,1280]{1,0:T(8,128)(2,1)} custom-call(s32[1]{0:T(128)} %bitcast.me_ref, s32[1]{0:T(128)} %bitcast.1.model_ref, bf16[1,128,12288]{2,1,0:T(8,128)(2,1)S(1)} %copy-done, bf16[2,64,4096]{2,1,0:T(8,128)(2,1)S(1)} %bitcast.12, bf16[128,1280]{1,0:T(8,128)(2,1)S(1)} %collective-permute-done.4.refs_0_.refs_3_, ...), custom_call_target="tpu_custom_call" | custom-call | bytes 655360 | tf_op jit(solution)/shard_map/pack/pallas_call | solution.py:67
  29.5 2.7 %collective-permute-start.6 = (bf16[128,1280]{1,0:T(8,128)(2,1)}, bf16[128,1280]{1,0:T(8,128)(2,1)}, u32[]{:S(2)}, u32[]{:S(2)}) collective-permute-start(bf16[128,1280]{1,0:T(8,128)(2,1)} %pack.15), channel_id=1, source_target_pairs={{0,8},{4,12},{8,0},{12,4},{16,24},{20,28},{24,16},{28,20},{1,9},{5... | collective-permute-start | bytes 983048 | tf_op jit(solution)/shard_map/ppermute | solution.py:305
  32.2 1.6 %pack.14 = bf16[128,1280]{1,0:T(8,128)(2,1)} custom-call(s32[1]{0:T(128)} %bitcast.me_ref, s32[1]{0:T(128)} %bitcast.1.model_ref, bf16[1,128,12288]{2,1,0:T(8,128)(2,1)S(1)} %copy-done, bf16[2,64,4096]{2,1,0:T(8,128)(2,1)S(1)} %bitcast.13, bf16[128,1280]{1,0:T(8,128)(2,1)S(1)} %collective-permute-done.4.refs_0_.refs_3_), custom_call_target="tpu_custom_call" | custom-call | bytes 655360 | tf_op jit(solution)/shard_map/pack/pallas_call | solution.py:67
  33.8 1.4 %collective-permute-start.5 = (bf16[128,1280]{1,0:T(8,128)(2,1)}, bf16[128,1280]{1,0:T(8,128)(2,1)}, u32[]{:S(2)}, u32[]{:S(2)}) collective-permute-start(bf16[128,1280]{1,0:T(8,128)(2,1)} %pack.14), channel_id=1, source_target_pairs={{0,4},{4,0},{8,12},{12,8},{16,20},{20,16},{24,28},{28,24},{1,5},{5... | collective-permute-start | bytes 983048 | tf_op jit(solution)/shard_map/ppermute | solution.py:305
  35.2 0.0 copy-done.3
  35.2 1.5 %pack.11 = bf16[128,1280]{1,0:T(8,128)(2,1)} custom-call(s32[1]{0:T(128)} %bitcast.me_ref, s32[1]{0:T(128)} %bitcast.1.model_ref, bf16[1,128,12288]{2,1,0:T(8,128)(2,1)S(1)} %copy-done, bf16[2,64,4096]{2,1,0:T(8,128)(2,1)S(1)} %bitcast.14, bf16[128,1280]{1,0:T(8,128)(2,1)S(1)} %collective-permute-done.2.refs_0_.refs_1_.refs_5_), custom_call_target="tpu_custom_call" | custom-call | bytes 655360 | tf_op jit(solution)/shard_map/pack/pallas_call | solution.py:67
  36.7 0.1 collective-permute-start.3
  36.8 0.0 collective-permute-done.refs_0_.refs_4_
  36.8 1.6 %pack.9 = bf16[128,1280]{1,0:T(8,128)(2,1)} custom-call(s32[1]{0:T(128)} %bitcast.me_ref, s32[1]{0:T(128)} %bitcast.1.model_ref, bf16[1,128,12288]{2,1,0:T(8,128)(2,1)S(1)} %copy-done, bf16[2,64,4096]{2,1,0:T(8,128)(2,1)S(1)} %bitcast.15, bf16[128,1280]{1,0:T(8,128)(2,1)S(1)} %collective-permute-done.refs_0_.refs_4_), custom_call_target="tpu_custom_call" | custom-call | bytes 655360 | tf_op jit(solution)/shard_map/pack/pallas_call | solution.py:67
  38.4 0.0 copy-start.7
  38.4 0.0 copy-start.8
  38.4 0.0 copy-start.9
  38.4 5.0 %collective-permute-start.1 = (bf16[128,1280]{1,0:T(8,128)(2,1)}, bf16[128,1280]{1,0:T(8,128)(2,1)}, u32[]{:S(2)}, u32[]{:S(2)}) collective-permute-start(bf16[128,1280]{1,0:T(8,128)(2,1)} %pack.9), channel_id=1, source_target_pairs={{0,16},{4,20},{8,24},{12,28},{16,0},{20,4},{24,8},{28,12},{1,17},{... | collective-permute-start | bytes 983048 | tf_op jit(solution)/shard_map/ppermute | solution.py:305
  43.5 1.2 %copy-done.2 = bf16[2,4096,64]{1,2,0:T(8,128)(2,1)S(1)} copy-done((bf16[2,4096,64]{1,2,0:T(8,128)(2,1)S(1)}, bf16[2,4096,64]{1,2,0:T(8,128)(2,1)}, u32[]{:S(2)}) %copy-start.2) | copy-done | bytes 1048600
  44.7 0.8 pack.13.refs_0_
  45.5 0.0 collective-permute-done.6.refs_2_
  45.5 0.0 collective-permute-done.5.refs_1_
  45.5 0.0 copy-done.7
  45.6 0.1 copy-done.4
  45.7 0.1 copy-done.6
  45.8 5.8 %attend_early.1 = (f32[4,64,768]{2,1,0:T(8,128)S(1)}, f32[2,8,768]{2,1,0:T(8,128)S(1)}, f32[8,128]{1,0:T(8,128)S(1)}, bf16[6,128,1280]{2,1,0:T(8,128)(2,1)S(1)},...) custom-call(s32[4]{0:T(128)S(1)} %copy-done.8, s32[1]{0:T(128)} %bitcast.me_ref, ...), custom_call_target="tpu_custom_call" | custom-call | flops 905969664 | bytes 2359296 | tf_op jit(solution)/shard_map/attend_early/pallas_call | solution.py:254
  51.5 10.8 %collective-permute-done.3.refs_1_ = bf16[128,1280]{1,0:T(8,128)(2,1)} collective-permute-done((bf16[128,1280]{1,0:T(8,128)(2,1)}, bf16[128,1280]{1,0:T(8,128)(2,1)}, u32[]{:S(2)}, u32[]{:S(2)}) %collective-permute-start.3) | collective-permute-done | bytes 327712 | tf_op jit(solution)/shard_map/ppermute | solution.py:305
  62.4 5.2 %collective-permute-done.1.refs_0_ = bf16[128,1280]{1,0:T(8,128)(2,1)} collective-permute-done((bf16[128,1280]{1,0:T(8,128)(2,1)}, bf16[128,1280]{1,0:T(8,128)(2,1)}, u32[]{:S(2)}, u32[]{:S(2)}) %collective-permute-start.1) | collective-permute-done | bytes 327712 | tf_op jit(solution)/shard_map/ppermute | solution.py:305
  67.6 3.5 %attend_late.1 = (f32[2,64,128]{2,1,0:T(8,128)S(1)}, bf16[2,64,128]{2,1,0:T(8,128)(2,1)S(1)}, bf16[2,64,128]{2,1,0:T(8,128)(2,1)S(1)}, bf16[2,64,128]{2,1,0:T(8,128)(2,1)S(1)}) custom-call(bf16[128,1280]{1,0:T(8,128)(2,1)} %collective-permute-done.1.refs_0_, bf16[128,1280]{1,0:T(8,128)(2,1)} %collective-permute-done.3.refs_1_, ...), custom_call_target="tpu_custom_call" | custom-call | flops 402653184 | bytes 3145728 | tf_op jit(solution)/shard_map/attend_late/pallas_call | solution.py:285
  71.1 0.1 collective-permute-start.7
  71.2 2.2 %collective-permute-start.8 = (bf16[2,64,128]{2,1,0:T(8,128)(2,1)S(1)}, bf16[2,64,128]{2,1,0:T(8,128)(2,1)S(1)}, u32[]{:S(2)}, u32[]{:S(2)}) collective-permute-start(bf16[2,64,128]{2,1,0:T(8,128)(2,1)S(1)} %get-tuple-element.25), channel_id=1, source_target_pairs={{0,24},{4,28},{8,16},{12,20},{16,8},{20,12},{24,0},{28,4},{1,25},{... | collective-permute-start | bytes 98312 | tf_op jit(solution)/shard_map/ppermute | solution.py:305
  73.4 1.2 %collective-permute-start.9 = (bf16[2,64,128]{2,1,0:T(8,128)(2,1)S(1)}, bf16[2,64,128]{2,1,0:T(8,128)(2,1)S(1)}, u32[]{:S(2)}, u32[]{:S(2)}) collective-permute-start(bf16[2,64,128]{2,1,0:T(8,128)(2,1)S(1)} %get-tuple-element.26), channel_id=1, source_target_pairs={{0,8},{4,12},{8,0},{12,4},{16,24},{20,28},{24,16},{28,20},{1,9},{5... | collective-permute-start | bytes 98312 | tf_op jit(solution)/shard_map/ppermute | solution.py:305
  74.6 1.3 %collective-permute-done.7 = bf16[2,64,128]{2,1,0:T(8,128)(2,1)S(1)} collective-permute-done((bf16[2,64,128]{2,1,0:T(8,128)(2,1)S(1)}, bf16[2,64,128]{2,1,0:T(8,128)(2,1)S(1)}, u32[]{:S(2)}, u32[]{:S(2)}) %collective-permute-start.7) | collective-permute-done | bytes 32800 | tf_op jit(solution)/shard_map/ppermute | solution.py:305
  76.0 1.0 %collective-permute-done.8 = bf16[2,64,128]{2,1,0:T(8,128)(2,1)S(1)} collective-permute-done((bf16[2,64,128]{2,1,0:T(8,128)(2,1)S(1)}, bf16[2,64,128]{2,1,0:T(8,128)(2,1)S(1)}, u32[]{:S(2)}, u32[]{:S(2)}) %collective-permute-start.8) | collective-permute-done | bytes 32800 | tf_op jit(solution)/shard_map/ppermute | solution.py:305
  76.9 0.4 collective-permute-done.9
  77.4 0.7 collective-permute-start.10
  78.0 3.3 %collective-permute-done.10 = f32[1,64,128]{2,1,0:T(8,128)S(1)} collective-permute-done((f32[1,64,128]{2,1,0:T(8,128)S(1)}, f32[1,64,128]{2,1,0:T(8,128)S(1)}, u32[]{:S(2)}, u32[]{:S(2)}) %collective-permute-start.10) | collective-permute-done | bytes 32800 | tf_op jit(solution)/shard_map/ppermute | solution.py:305
  81.3 0.0 collective-permute-start.11
  81.4 1.6 %collective-permute-start.12 = (f32[64,128]{1,0:T(8,128)S(1)}, f32[64,128]{1,0:T(8,128)S(1)}, u32[]{:S(2)}, u32[]{:S(2)}) collective-permute-start(f32[64,128]{1,0:T(8,128)S(1)} %fusion), channel_id=1, source_target_pairs={{0,2},{1,3},{2,0},{3,1},{4,6},{5,7},{6,4},{7,5},{8,10},{9,11},{10,... | collective-permute-start | bytes 98312 | tf_op jit(solution)/shard_map/ppermute | solution.py:305
  82.9 0.3 collective-permute-start.13
  83.2 1.8 %collective-permute-done.11 = f32[64,128]{1,0:T(8,128)S(1)} collective-permute-done((f32[64,128]{1,0:T(8,128)S(1)}, f32[64,128]{1,0:T(8,128)S(1)}, u32[]{:S(2)}, u32[]{:S(2)}) %collective-permute-start.11) | collective-permute-done | bytes 32800 | tf_op jit(solution)/shard_map/ppermute | solution.py:305
  85.0 0.4 collective-permute-done.12
  85.4 0.0 collective-permute-done.13
  85.4 0.6 add_bitcast_fusion
  (14 shorter events, 0.0 us)
Async XLA Ops:
  0.0 8.5 %copy-start = (bf16[1,128,12288]{2,1,0:T(8,128)(2,1)S(1)}, bf16[1,128,12288]{2,1,0:T(8,128)(2,1)}, u32[]{:S(2)}) copy-start(bf16[1,128,12288]{2,1,0:T(8,128)(2,1)} %qkv_ref.15) | copy-start | bytes 9437188
  2.4 14.8 %collective-permute-start.2 = (bf16[128,1280]{1,0:T(8,128)(2,1)}, bf16[128,1280]{1,0:T(8,128)(2,1)S(1)}, u32[]{:S(2)}, u32[]{:S(2)}) collective-permute-start(bf16[128,1280]{1,0:T(8,128)(2,1)} %pack.10), channel_id=1, source_target_pairs={{0,28},{4,24},{8,20},{12,16},{16,12},{20,8},{24,4},{28,0},{1,29},{... | collective-permute-start | bytes 983048 | tf_op jit(solution)/shard_map/ppermute | solution.py:305
  8.5 1.2 %copy-start.1 = (bf16[2,4096,64]{1,2,0:T(8,128)(2,1)S(1)}, bf16[2,4096,64]{1,2,0:T(8,128)(2,1)}, u32[]{:S(2)}) copy-start(bf16[2,4096,64]{1,2,0:T(8,128)(2,1)} %param.6) | copy-start | bytes 3145732
  10.5 17.5 %collective-permute-start.4 = (bf16[128,1280]{1,0:T(8,128)(2,1)S(1)}, bf16[128,1280]{1,0:T(8,128)(2,1)S(1)}, u32[]{:S(2)}, u32[]{:S(2)}) collective-permute-start(bf16[128,1280]{1,0:T(8,128)(2,1)S(1)} %pack.12), channel_id=1, source_target_pairs={{0,12},{4,8},{8,4},{12,0},{16,28},{20,24},{24,20},{28,16},{1,13},{... | collective-permute-start | bytes 983048 | tf_op jit(solution)/shard_map/ppermute | solution.py:305
  11.4 25.4 %collective-permute-start = (bf16[128,1280]{1,0:T(8,128)(2,1)S(1)}, bf16[128,1280]{1,0:T(8,128)(2,1)S(1)}, u32[]{:S(2)}, u32[]{:S(2)}) collective-permute-start(bf16[128,1280]{1,0:T(8,128)(2,1)S(1)} %pack.8), channel_id=1, source_target_pairs={{0,24},{4,28},{8,16},{12,20},{16,8},{20,12},{24,0},{28,4},{1,25},{... | collective-permute-start | bytes 983048 | tf_op jit(solution)/shard_map/ppermute | solution.py:305
  17.3 17.9 %copy-start.3 = (bf16[128,1280]{1,0:T(8,128)(2,1)}, bf16[128,1280]{1,0:T(8,128)(2,1)S(1)}, u32[]{:S(2)}) copy-start(bf16[128,1280]{1,0:T(8,128)(2,1)S(1)} %collective-permute-done.2.refs_0_.refs_1_.refs_5_) | copy-start | bytes 983044
  29.5 16.0 %collective-permute-start.6 = (bf16[128,1280]{1,0:T(8,128)(2,1)}, bf16[128,1280]{1,0:T(8,128)(2,1)}, u32[]{:S(2)}, u32[]{:S(2)}) collective-permute-start(bf16[128,1280]{1,0:T(8,128)(2,1)} %pack.15), channel_id=1, source_target_pairs={{0,8},{4,12},{8,0},{12,4},{16,24},{20,28},{24,16},{28,20},{1,9},{5... | collective-permute-start | bytes 983048 | tf_op jit(solution)/shard_map/ppermute | solution.py:305
  33.8 11.8 %collective-permute-start.5 = (bf16[128,1280]{1,0:T(8,128)(2,1)}, bf16[128,1280]{1,0:T(8,128)(2,1)}, u32[]{:S(2)}, u32[]{:S(2)}) collective-permute-start(bf16[128,1280]{1,0:T(8,128)(2,1)} %pack.14), channel_id=1, source_target_pairs={{0,4},{4,0},{8,12},{12,8},{16,20},{20,16},{24,28},{28,24},{1,5},{5... | collective-permute-start | bytes 983048 | tf_op jit(solution)/shard_map/ppermute | solution.py:305
  36.7 25.7 %collective-permute-start.3 = (bf16[128,1280]{1,0:T(8,128)(2,1)}, bf16[128,1280]{1,0:T(8,128)(2,1)}, u32[]{:S(2)}, u32[]{:S(2)}) collective-permute-start(bf16[128,1280]{1,0:T(8,128)(2,1)} %pack.11), channel_id=1, source_target_pairs={{0,20},{4,16},{8,28},{12,24},{16,4},{20,0},{24,12},{28,8},{1,21},{... | collective-permute-start | bytes 983048 | tf_op jit(solution)/shard_map/ppermute | solution.py:305
  36.8 1.6 %copy-start.5 = (bf16[128,1280]{1,0:T(8,128)(2,1)}, bf16[128,1280]{1,0:T(8,128)(2,1)S(1)}, u32[]{:S(2)}) copy-start(bf16[128,1280]{1,0:T(8,128)(2,1)S(1)} %collective-permute-done.refs_0_.refs_4_) | copy-start | bytes 983044
  38.4 7.1 %copy-start.7 = (f32[1000]{0:T(1024)S(1)}, f32[1000]{0:T(1024)}, u32[]{:S(2)}) copy-start(f32[1000]{0:T(1024)} %step_weight_ref.1) | copy-start | bytes 12004
  38.4 7.1 %copy-start.8 = (s32[4]{0:T(128)S(1)}, s32[4]{0:T(128)}, u32[]{:S(2)}) copy-start(s32[4]{0:T(128)} %frames_ref.1) | copy-start | bytes 52
  38.4 7.1 %copy-start.9 = (s32[2]{0:T(128)S(1)}, s32[2]{0:T(128)}, u32[]{:S(2)}) copy-start(s32[2]{0:T(128)} %timestep_ref.1) | copy-start | bytes 28
  38.4 29.2 %collective-permute-start.1 = (bf16[128,1280]{1,0:T(8,128)(2,1)}, bf16[128,1280]{1,0:T(8,128)(2,1)}, u32[]{:S(2)}, u32[]{:S(2)}) collective-permute-start(bf16[128,1280]{1,0:T(8,128)(2,1)} %pack.9), channel_id=1, source_target_pairs={{0,16},{4,20},{8,24},{12,28},{16,0},{20,4},{24,8},{28,12},{1,17},{... | collective-permute-start | bytes 983048 | tf_op jit(solution)/shard_map/ppermute | solution.py:305
  43.5 1.2 %copy-start.2 = (bf16[2,4096,64]{1,2,0:T(8,128)(2,1)S(1)}, bf16[2,4096,64]{1,2,0:T(8,128)(2,1)}, u32[]{:S(2)}) copy-start(bf16[2,4096,64]{1,2,0:T(8,128)(2,1)} %param.6) | copy-start | bytes 3145732
  44.7 1.0 %copy-start.4 = (bf16[128,1280]{1,0:T(8,128)(2,1)S(1)}, bf16[128,1280]{1,0:T(8,128)(2,1)}, u32[]{:S(2)}) copy-start(bf16[128,1280]{1,0:T(8,128)(2,1)} %copy-done.3) | copy-start | bytes 983044
  44.7 1.1 %copy-start.6 = (bf16[128,1280]{1,0:T(8,128)(2,1)S(1)}, bf16[128,1280]{1,0:T(8,128)(2,1)}, u32[]{:S(2)}) copy-start(bf16[128,1280]{1,0:T(8,128)(2,1)} %copy-done.5) | copy-start | bytes 983044
  71.1 4.9 %collective-permute-start.7 = (bf16[2,64,128]{2,1,0:T(8,128)(2,1)S(1)}, bf16[2,64,128]{2,1,0:T(8,128)(2,1)S(1)}, u32[]{:S(2)}, u32[]{:S(2)}) collective-permute-start(bf16[2,64,128]{2,1,0:T(8,128)(2,1)S(1)} %get-tuple-element.24), channel_id=1, source_target_pairs={{0,16},{4,20},{8,24},{12,28},{16,0},{20,4},{24,8},{28,12},{1,17},{... | collective-permute-start | bytes 98312 | tf_op jit(solution)/shard_map/ppermute | solution.py:305
  71.2 5.8 %collective-permute-start.8 = (bf16[2,64,128]{2,1,0:T(8,128)(2,1)S(1)}, bf16[2,64,128]{2,1,0:T(8,128)(2,1)S(1)}, u32[]{:S(2)}, u32[]{:S(2)}) collective-permute-start(bf16[2,64,128]{2,1,0:T(8,128)(2,1)S(1)} %get-tuple-element.25), channel_id=1, source_target_pairs={{0,24},{4,28},{8,16},{12,20},{16,8},{20,12},{24,0},{28,4},{1,25},{... | collective-permute-start | bytes 98312 | tf_op jit(solution)/shard_map/ppermute | solution.py:305
  73.4 3.9 %collective-permute-start.9 = (bf16[2,64,128]{2,1,0:T(8,128)(2,1)S(1)}, bf16[2,64,128]{2,1,0:T(8,128)(2,1)S(1)}, u32[]{:S(2)}, u32[]{:S(2)}) collective-permute-start(bf16[2,64,128]{2,1,0:T(8,128)(2,1)S(1)} %get-tuple-element.26), channel_id=1, source_target_pairs={{0,8},{4,12},{8,0},{12,4},{16,24},{20,28},{24,16},{28,20},{1,9},{5... | collective-permute-start | bytes 98312 | tf_op jit(solution)/shard_map/ppermute | solution.py:305
  77.4 4.0 %collective-permute-start.10 = (f32[1,64,128]{2,1,0:T(8,128)S(1)}, f32[1,64,128]{2,1,0:T(8,128)S(1)}, u32[]{:S(2)}, u32[]{:S(2)}) collective-permute-start(f32[1,64,128]{2,1,0:T(8,128)S(1)} %slice.9), channel_id=1, source_target_pairs={{0,4},{4,0},{8,12},{12,8},{16,20},{20,16},{24,28},{28,24},{1,5},{5... | collective-permute-start | bytes 98312 | tf_op jit(solution)/shard_map/ppermute | solution.py:305
  81.3 3.6 %collective-permute-start.11 = (f32[64,128]{1,0:T(8,128)S(1)}, f32[64,128]{1,0:T(8,128)S(1)}, u32[]{:S(2)}, u32[]{:S(2)}) collective-permute-start(f32[64,128]{1,0:T(8,128)S(1)} %fusion), channel_id=1, source_target_pairs={{0,3},{1,2},{2,1},{3,0},{4,7},{5,6},{6,5},{7,4},{8,11},{9,10},{10,... | collective-permute-start | bytes 98312 | tf_op jit(solution)/shard_map/ppermute | solution.py:305
  81.4 4.0 %collective-permute-start.12 = (f32[64,128]{1,0:T(8,128)S(1)}, f32[64,128]{1,0:T(8,128)S(1)}, u32[]{:S(2)}, u32[]{:S(2)}) collective-permute-start(f32[64,128]{1,0:T(8,128)S(1)} %fusion), channel_id=1, source_target_pairs={{0,2},{1,3},{2,0},{3,1},{4,6},{5,7},{6,4},{7,5},{8,10},{9,11},{10,... | collective-permute-start | bytes 98312 | tf_op jit(solution)/shard_map/ppermute | solution.py:305
  82.9 2.5 %collective-permute-start.13 = (f32[64,128]{1,0:T(8,128)S(1)}, f32[64,128]{1,0:T(8,128)S(1)}, u32[]{:S(2)}, u32[]{:S(2)}) collective-permute-start(f32[64,128]{1,0:T(8,128)S(1)} %fusion), channel_id=1, source_target_pairs={{0,1},{1,0},{2,3},{3,2},{4,5},{5,4},{6,7},{7,6},{8,9},{9,8},{10,11... | collective-permute-start | bytes 98312 | tf_op jit(solution)/shard_map/ppermute | solution.py:305

commit v24 on v23

--- a/solution.py
+++ b/solution.py
@@ -338,7 +338,7 @@
     size = half // 2
     while True:
         keep = given[0]
-        for n in [2, 3, 1] if len(given) == 4 else range(1, len(given)):
+        for n in [2, 1, 3] if len(given) == 4 else range(1, len(given)):
             keep = keep + swap(given[n], "seq", n * size).astype(jnp.float32)
         if size == 1:
             break

time: 86.3 us -> 88.5 us (1.025)
  waiting for transfers between devices: 39.9 us -> 41.4 us
    ppermute x14, waiting for transfers between devices: 39.9 us -> 41.4 us  [swap(): return lax.ppermute(array, axis, [(i, i ^ offset) for i in range(size)])]
  transfers between devices with their start and end apart: 14 -> 14, of which waited for: 10 -> 10; matrix products, arithmetic and copies ran while one was open for 0% -> 0% of each run, Pallas kernels for 17% -> 16%
where the time goes in v24:
time: 88.5 us; the launch traced here: 88.3 us
  waiting for transfers between devices  41.4 us (47%)
  starting transfers between devices  23.1 us (26%)
  Pallas kernels  20.3 us (23%)
  local copies, waits for them, and re-layouts  2.69 us (3%)
    ppermute x14, waiting for transfers between devices, swap(): return lax.ppermute(array, axis, [(i, i ^ offset) for i in range(size)])  41.4 us
    ppermute x14, starting transfers between devices, swap(): return lax.ppermute(array, axis, [(i, i ^ offset) for i in range(size)])  23.1 us
    pallas_call x8, Pallas kernels, pack(): pl.pallas_call(functools.partial(pack_kernel, k), in_specs=[SMEM, SMEM] +...  11 us
    pallas_call x1, Pallas kernels, attend_early(): pl.pallas_call(functools.partial(early_kernel, offsets, late), in_specs=[...  5.77 us
    pallas_call x1, Pallas kernels, attend_late(): pl.pallas_call(functools.partial(late_kernel, offsets, late), in_specs=[V...  3.48 us
    unnamed x20, local copies, waits for them, and re-layouts  2.69 us
  transfers between devices with their start and end apart: 14, of which 10 were waited for; matrix products, arithmetic and copies ran while one was open for 0% of the time, Pallas kernels for 16%

profile of v24, /device:TPU:0, one launch (start us, length us, event | category | flops | bytes accessed | tf_op | source)
XLA Modules:
  0.0 88.3 jit_solution(7046250251438582532)
XLA Ops:
  0.0 2.4 %pack.10 = bf16[128,1280]{1,0:T(8,128)(2,1)} custom-call(s32[1]{0:T(128)} %bitcast.me_ref, s32[1]{0:T(128)} %bitcast.1.model_ref, bf16[1,128,12288]{2,1,0:T(8,128)(2,1)} %qkv_ref.15, bf16[2,64,4096]{2,1,0:T(8,128)(2,1)} %bitcast.9), custom_call_target="tpu_custom_call" | custom-call | bytes 655360 | tf_op jit(solution)/shard_map/pack/pallas_call | solution.py:67
  2.4 6.0 %collective-permute-start.2 = (bf16[128,1280]{1,0:T(8,128)(2,1)}, bf16[128,1280]{1,0:T(8,128)(2,1)S(1)}, u32[]{:S(2)}, u32[]{:S(2)}) collective-permute-start(bf16[128,1280]{1,0:T(8,128)(2,1)} %pack.10), channel_id=1, source_target_pairs={{0,28},{4,24},{8,20},{12,16},{16,12},{20,8},{24,4},{28,0},{1,29},{... | collective-permute-start | bytes 983048 | tf_op jit(solution)/shard_map/ppermute | solution.py:305
  8.5 1.2 %copy-done.1 = bf16[2,4096,64]{1,2,0:T(8,128)(2,1)S(1)} copy-done((bf16[2,4096,64]{1,2,0:T(8,128)(2,1)S(1)}, bf16[2,4096,64]{1,2,0:T(8,128)(2,1)}, u32[]{:S(2)}) %copy-start.1) | copy-done | bytes 1048600
  9.7 0.8 pack.12
  10.5 0.1 collective-permute-start.4
  10.6 0.8 pack.8
  11.4 0.9 %collective-permute-start = (bf16[128,1280]{1,0:T(8,128)(2,1)S(1)}, bf16[128,1280]{1,0:T(8,128)(2,1)S(1)}, u32[]{:S(2)}, u32[]{:S(2)}) collective-permute-start(bf16[128,1280]{1,0:T(8,128)(2,1)S(1)} %pack.8), channel_id=1, source_target_pairs={{0,24},{4,28},{8,16},{12,20},{16,8},{20,12},{24,0},{28,4},{1,25},{... | collective-permute-start | bytes 983048 | tf_op jit(solution)/shard_map/ppermute | solution.py:305
  12.3 4.9 %collective-permute-done.2.refs_0_.refs_1_.refs_5_ = bf16[128,1280]{1,0:T(8,128)(2,1)S(1)} collective-permute-done((bf16[128,1280]{1,0:T(8,128)(2,1)}, bf16[128,1280]{1,0:T(8,128)(2,1)S(1)}, u32[]{:S(2)}, u32[]{:S(2)}) %collective-permute-start.2) | collective-permute-done | bytes 327712 | tf_op jit(solution)/shard_map/ppermute | solution.py:305
  17.3 10.7 %collective-permute-done.4.refs_0_.refs_3_ = bf16[128,1280]{1,0:T(8,128)(2,1)S(1)} collective-permute-done((bf16[128,1280]{1,0:T(8,128)(2,1)S(1)}, bf16[128,1280]{1,0:T(8,128)(2,1)S(1)}, u32[]{:S(2)}, u32[]{:S(2)}) %collective-permute-start.4) | collective-permute-done | bytes 327712 | tf_op jit(solution)/shard_map/ppermute | solution.py:305
  28.0 1.5 %pack.15 = bf16[128,1280]{1,0:T(8,128)(2,1)} custom-call(s32[1]{0:T(128)} %bitcast.me_ref, s32[1]{0:T(128)} %bitcast.1.model_ref, bf16[1,128,12288]{2,1,0:T(8,128)(2,1)S(1)} %copy-done, bf16[2,64,4096]{2,1,0:T(8,128)(2,1)S(1)} %bitcast.12, bf16[128,1280]{1,0:T(8,128)(2,1)S(1)} %collective-permute-done.4.refs_0_.refs_3_, ...), custom_call_target="tpu_custom_call" | custom-call | bytes 655360 | tf_op jit(solution)/shard_map/pack/pallas_call | solution.py:67
  29.5 2.7 %collective-permute-start.6 = (bf16[128,1280]{1,0:T(8,128)(2,1)}, bf16[128,1280]{1,0:T(8,128)(2,1)}, u32[]{:S(2)}, u32[]{:S(2)}) collective-permute-start(bf16[128,1280]{1,0:T(8,128)(2,1)} %pack.15), channel_id=1, source_target_pairs={{0,8},{4,12},{8,0},{12,4},{16,24},{20,28},{24,16},{28,20},{1,9},{5... | collective-permute-start | bytes 983048 | tf_op jit(solution)/shard_map/ppermute | solution.py:305
  32.2 1.6 %pack.14 = bf16[128,1280]{1,0:T(8,128)(2,1)} custom-call(s32[1]{0:T(128)} %bitcast.me_ref, s32[1]{0:T(128)} %bitcast.1.model_ref, bf16[1,128,12288]{2,1,0:T(8,128)(2,1)S(1)} %copy-done, bf16[2,64,4096]{2,1,0:T(8,128)(2,1)S(1)} %bitcast.13, bf16[128,1280]{1,0:T(8,128)(2,1)S(1)} %collective-permute-done.4.refs_0_.refs_3_), custom_call_target="tpu_custom_call" | custom-call | bytes 655360 | tf_op jit(solution)/shard_map/pack/pallas_call | solution.py:67
  33.8 1.4 %collective-permute-start.5 = (bf16[128,1280]{1,0:T(8,128)(2,1)}, bf16[128,1280]{1,0:T(8,128)(2,1)}, u32[]{:S(2)}, u32[]{:S(2)}) collective-permute-start(bf16[128,1280]{1,0:T(8,128)(2,1)} %pack.14), channel_id=1, source_target_pairs={{0,4},{4,0},{8,12},{12,8},{16,20},{20,16},{24,28},{28,24},{1,5},{5... | collective-permute-start | bytes 983048 | tf_op jit(solution)/shard_map/ppermute | solution.py:305
  35.2 0.0 copy-done.3
  35.2 1.5 %pack.11 = bf16[128,1280]{1,0:T(8,128)(2,1)} custom-call(s32[1]{0:T(128)} %bitcast.me_ref, s32[1]{0:T(128)} %bitcast.1.model_ref, bf16[1,128,12288]{2,1,0:T(8,128)(2,1)S(1)} %copy-done, bf16[2,64,4096]{2,1,0:T(8,128)(2,1)S(1)} %bitcast.14, bf16[128,1280]{1,0:T(8,128)(2,1)S(1)} %collective-permute-done.2.refs_0_.refs_1_.refs_5_), custom_call_target="tpu_custom_call" | custom-call | bytes 655360 | tf_op jit(solution)/shard_map/pack/pallas_call | solution.py:67
  36.7 0.1 collective-permute-start.3
  36.8 0.0 collective-permute-done.refs_0_.refs_4_
  36.8 0.0 copy-start.5
  36.8 1.6 %pack.9 = bf16[128,1280]{1,0:T(8,128)(2,1)} custom-call(s32[1]{0:T(128)} %bitcast.me_ref, s32[1]{0:T(128)} %bitcast.1.model_ref, bf16[1,128,12288]{2,1,0:T(8,128)(2,1)S(1)} %copy-done, bf16[2,64,4096]{2,1,0:T(8,128)(2,1)S(1)} %bitcast.15, bf16[128,1280]{1,0:T(8,128)(2,1)S(1)} %collective-permute-done.refs_0_.refs_4_), custom_call_target="tpu_custom_call" | custom-call | bytes 655360 | tf_op jit(solution)/shard_map/pack/pallas_call | solution.py:67
  38.4 0.0 copy-start.7
  38.4 0.0 copy-start.8
  38.4 0.0 copy-start.9
  38.4 5.0 %collective-permute-start.1 = (bf16[128,1280]{1,0:T(8,128)(2,1)}, bf16[128,1280]{1,0:T(8,128)(2,1)}, u32[]{:S(2)}, u32[]{:S(2)}) collective-permute-start(bf16[128,1280]{1,0:T(8,128)(2,1)} %pack.9), channel_id=1, source_target_pairs={{0,16},{4,20},{8,24},{12,28},{16,0},{20,4},{24,8},{28,12},{1,17},{... | collective-permute-start | bytes 983048 | tf_op jit(solution)/shard_map/ppermute | solution.py:305
  43.5 1.2 %copy-done.2 = bf16[2,4096,64]{1,2,0:T(8,128)(2,1)S(1)} copy-done((bf16[2,4096,64]{1,2,0:T(8,128)(2,1)S(1)}, bf16[2,4096,64]{1,2,0:T(8,128)(2,1)}, u32[]{:S(2)}) %copy-start.2) | copy-done | bytes 1048600
  44.7 0.8 pack.13.refs_0_
  45.5 0.0 collective-permute-done.6.refs_2_
  45.5 0.0 collective-permute-done.5.refs_1_
  45.6 0.1 copy-done.4
  45.7 0.1 copy-done.6
  45.8 5.8 %attend_early.1 = (f32[4,64,768]{2,1,0:T(8,128)S(1)}, f32[2,8,768]{2,1,0:T(8,128)S(1)}, f32[8,128]{1,0:T(8,128)S(1)}, bf16[6,128,1280]{2,1,0:T(8,128)(2,1)S(1)},...) custom-call(s32[4]{0:T(128)S(1)} %copy-done.8, s32[1]{0:T(128)} %bitcast.me_ref, ...), custom_call_target="tpu_custom_call" | custom-call | flops 905969664 | bytes 2359296 | tf_op jit(solution)/shard_map/attend_early/pallas_call | solution.py:254
  51.5 10.8 %collective-permute-done.3.refs_1_ = bf16[128,1280]{1,0:T(8,128)(2,1)} collective-permute-done((bf16[128,1280]{1,0:T(8,128)(2,1)}, bf16[128,1280]{1,0:T(8,128)(2,1)}, u32[]{:S(2)}, u32[]{:S(2)}) %collective-permute-start.3) | collective-permute-done | bytes 327712 | tf_op jit(solution)/shard_map/ppermute | solution.py:305
  62.4 5.2 %collective-permute-done.1.refs_0_ = bf16[128,1280]{1,0:T(8,128)(2,1)} collective-permute-done((bf16[128,1280]{1,0:T(8,128)(2,1)}, bf16[128,1280]{1,0:T(8,128)(2,1)}, u32[]{:S(2)}, u32[]{:S(2)}) %collective-permute-start.1) | collective-permute-done | bytes 327712 | tf_op jit(solution)/shard_map/ppermute | solution.py:305
  67.6 3.5 %attend_late.1 = (f32[2,64,128]{2,1,0:T(8,128)S(1)}, bf16[2,64,128]{2,1,0:T(8,128)(2,1)S(1)}, bf16[2,64,128]{2,1,0:T(8,128)(2,1)S(1)}, bf16[2,64,128]{2,1,0:T(8,128)(2,1)S(1)}) custom-call(bf16[128,1280]{1,0:T(8,128)(2,1)} %collective-permute-done.1.refs_0_, bf16[128,1280]{1,0:T(8,128)(2,1)} %collective-permute-done.3.refs_1_, ...), custom_call_target="tpu_custom_call" | custom-call | flops 402653184 | bytes 3145728 | tf_op jit(solution)/shard_map/attend_late/pallas_call | solution.py:285
  71.1 0.1 collective-permute-start.7
  71.2 2.7 %collective-permute-start.8 = (bf16[2,64,128]{2,1,0:T(8,128)(2,1)S(1)}, bf16[2,64,128]{2,1,0:T(8,128)(2,1)S(1)}, u32[]{:S(2)}, u32[]{:S(2)}) collective-permute-start(bf16[2,64,128]{2,1,0:T(8,128)(2,1)S(1)} %get-tuple-element.25), channel_id=1, source_target_pairs={{0,8},{4,12},{8,0},{12,4},{16,24},{20,28},{24,16},{28,20},{1,9},{5... | collective-permute-start | bytes 98312 | tf_op jit(solution)/shard_map/ppermute | solution.py:305
  73.9 1.6 %collective-permute-start.9 = (bf16[2,64,128]{2,1,0:T(8,128)(2,1)S(1)}, bf16[2,64,128]{2,1,0:T(8,128)(2,1)S(1)}, u32[]{:S(2)}, u32[]{:S(2)}) collective-permute-start(bf16[2,64,128]{2,1,0:T(8,128)(2,1)S(1)} %get-tuple-element.26), channel_id=1, source_target_pairs={{0,24},{4,28},{8,16},{12,20},{16,8},{20,12},{24,0},{28,4},{1,25},{... | collective-permute-start | bytes 98312 | tf_op jit(solution)/shard_map/ppermute | solution.py:305
  75.5 0.5 collective-permute-done.7
  76.1 0.1 collective-permute-done.8
  76.1 3.5 %collective-permute-done.9 = bf16[2,64,128]{2,1,0:T(8,128)(2,1)S(1)} collective-permute-done((bf16[2,64,128]{2,1,0:T(8,128)(2,1)S(1)}, bf16[2,64,128]{2,1,0:T(8,128)(2,1)S(1)}, u32[]{:S(2)}, u32[]{:S(2)}) %collective-permute-start.9) | collective-permute-done | bytes 32800 | tf_op jit(solution)/shard_map/ppermute | solution.py:305
  79.6 0.6 collective-permute-start.10
  80.2 3.4 %collective-permute-done.10 = f32[1,64,128]{2,1,0:T(8,128)S(1)} collective-permute-done((f32[1,64,128]{2,1,0:T(8,128)S(1)}, f32[1,64,128]{2,1,0:T(8,128)S(1)}, u32[]{:S(2)}, u32[]{:S(2)}) %collective-permute-start.10) | collective-permute-done | bytes 32800 | tf_op jit(solution)/shard_map/ppermute | solution.py:305
  83.6 0.0 collective-permute-start.11
  83.6 1.6 %collective-permute-start.12 = (f32[64,128]{1,0:T(8,128)S(1)}, f32[64,128]{1,0:T(8,128)S(1)}, u32[]{:S(2)}, u32[]{:S(2)}) collective-permute-start(f32[64,128]{1,0:T(8,128)S(1)} %fusion), channel_id=1, source_target_pairs={{0,2},{1,3},{2,0},{3,1},{4,6},{5,7},{6,4},{7,5},{8,10},{9,11},{10,... | collective-permute-start | bytes 98312 | tf_op jit(solution)/shard_map/ppermute | solution.py:305
  85.2 0.3 collective-permute-start.13
  85.5 1.8 %collective-permute-done.11 = f32[64,128]{1,0:T(8,128)S(1)} collective-permute-done((f32[64,128]{1,0:T(8,128)S(1)}, f32[64,128]{1,0:T(8,128)S(1)}, u32[]{:S(2)}, u32[]{:S(2)}) %collective-permute-start.11) | collective-permute-done | bytes 32800 | tf_op jit(solution)/shard_map/ppermute | solution.py:305
  87.2 0.4 collective-permute-done.12
  87.7 0.0 collective-permute-done.13
  87.7 0.6 add_bitcast_fusion
  (14 shorter events, 0.0 us)
Async XLA Ops:
  0.0 8.5 %copy-start = (bf16[1,128,12288]{2,1,0:T(8,128)(2,1)S(1)}, bf16[1,128,12288]{2,1,0:T(8,128)(2,1)}, u32[]{:S(2)}) copy-start(bf16[1,128,12288]{2,1,0:T(8,128)(2,1)} %qkv_ref.15) | copy-start | bytes 9437188
  2.4 14.8 %collective-permute-start.2 = (bf16[128,1280]{1,0:T(8,128)(2,1)}, bf16[128,1280]{1,0:T(8,128)(2,1)S(1)}, u32[]{:S(2)}, u32[]{:S(2)}) collective-permute-start(bf16[128,1280]{1,0:T(8,128)(2,1)} %pack.10), channel_id=1, source_target_pairs={{0,28},{4,24},{8,20},{12,16},{16,12},{20,8},{24,4},{28,0},{1,29},{... | collective-permute-start | bytes 983048 | tf_op jit(solution)/shard_map/ppermute | solution.py:305
  8.5 1.2 %copy-start.1 = (bf16[2,4096,64]{1,2,0:T(8,128)(2,1)S(1)}, bf16[2,4096,64]{1,2,0:T(8,128)(2,1)}, u32[]{:S(2)}) copy-start(bf16[2,4096,64]{1,2,0:T(8,128)(2,1)} %param.6) | copy-start | bytes 3145732
  10.5 17.5 %collective-permute-start.4 = (bf16[128,1280]{1,0:T(8,128)(2,1)S(1)}, bf16[128,1280]{1,0:T(8,128)(2,1)S(1)}, u32[]{:S(2)}, u32[]{:S(2)}) collective-permute-start(bf16[128,1280]{1,0:T(8,128)(2,1)S(1)} %pack.12), channel_id=1, source_target_pairs={{0,12},{4,8},{8,4},{12,0},{16,28},{20,24},{24,20},{28,16},{1,13},{... | collective-permute-start | bytes 983048 | tf_op jit(solution)/shard_map/ppermute | solution.py:305
  11.4 25.4 %collective-permute-start = (bf16[128,1280]{1,0:T(8,128)(2,1)S(1)}, bf16[128,1280]{1,0:T(8,128)(2,1)S(1)}, u32[]{:S(2)}, u32[]{:S(2)}) collective-permute-start(bf16[128,1280]{1,0:T(8,128)(2,1)S(1)} %pack.8), channel_id=1, source_target_pairs={{0,24},{4,28},{8,16},{12,20},{16,8},{20,12},{24,0},{28,4},{1,25},{... | collective-permute-start | bytes 983048 | tf_op jit(solution)/shard_map/ppermute | solution.py:305
  17.3 17.9 %copy-start.3 = (bf16[128,1280]{1,0:T(8,128)(2,1)}, bf16[128,1280]{1,0:T(8,128)(2,1)S(1)}, u32[]{:S(2)}) copy-start(bf16[128,1280]{1,0:T(8,128)(2,1)S(1)} %collective-permute-done.2.refs_0_.refs_1_.refs_5_) | copy-start | bytes 983044
  29.5 16.0 %collective-permute-start.6 = (bf16[128,1280]{1,0:T(8,128)(2,1)}, bf16[128,1280]{1,0:T(8,128)(2,1)}, u32[]{:S(2)}, u32[]{:S(2)}) collective-permute-start(bf16[128,1280]{1,0:T(8,128)(2,1)} %pack.15), channel_id=1, source_target_pairs={{0,8},{4,12},{8,0},{12,4},{16,24},{20,28},{24,16},{28,20},{1,9},{5... | collective-permute-start | bytes 983048 | tf_op jit(solution)/shard_map/ppermute | solution.py:305
  33.8 11.8 %collective-permute-start.5 = (bf16[128,1280]{1,0:T(8,128)(2,1)}, bf16[128,1280]{1,0:T(8,128)(2,1)}, u32[]{:S(2)}, u32[]{:S(2)}) collective-permute-start(bf16[128,1280]{1,0:T(8,128)(2,1)} %pack.14), channel_id=1, source_target_pairs={{0,4},{4,0},{8,12},{12,8},{16,20},{20,16},{24,28},{28,24},{1,5},{5... | collective-permute-start | bytes 983048 | tf_op jit(solution)/shard_map/ppermute | solution.py:305
  36.7 25.7 %collective-permute-start.3 = (bf16[128,1280]{1,0:T(8,128)(2,1)}, bf16[128,1280]{1,0:T(8,128)(2,1)}, u32[]{:S(2)}, u32[]{:S(2)}) collective-permute-start(bf16[128,1280]{1,0:T(8,128)(2,1)} %pack.11), channel_id=1, source_target_pairs={{0,20},{4,16},{8,28},{12,24},{16,4},{20,0},{24,12},{28,8},{1,21},{... | collective-permute-start | bytes 983048 | tf_op jit(solution)/shard_map/ppermute | solution.py:305
  36.8 1.6 %copy-start.5 = (bf16[128,1280]{1,0:T(8,128)(2,1)}, bf16[128,1280]{1,0:T(8,128)(2,1)S(1)}, u32[]{:S(2)}) copy-start(bf16[128,1280]{1,0:T(8,128)(2,1)S(1)} %collective-permute-done.refs_0_.refs_4_) | copy-start | bytes 983044
  38.4 7.1 %copy-start.7 = (f32[1000]{0:T(1024)S(1)}, f32[1000]{0:T(1024)}, u32[]{:S(2)}) copy-start(f32[1000]{0:T(1024)} %step_weight_ref.1) | copy-start | bytes 12004
  38.4 7.1 %copy-start.8 = (s32[4]{0:T(128)S(1)}, s32[4]{0:T(128)}, u32[]{:S(2)}) copy-start(s32[4]{0:T(128)} %frames_ref.1) | copy-start | bytes 52
  38.4 7.1 %copy-start.9 = (s32[2]{0:T(128)S(1)}, s32[2]{0:T(128)}, u32[]{:S(2)}) copy-start(s32[2]{0:T(128)} %timestep_ref.1) | copy-start | bytes 28
  38.4 29.2 %collective-permute-start.1 = (bf16[128,1280]{1,0:T(8,128)(2,1)}, bf16[128,1280]{1,0:T(8,128)(2,1)}, u32[]{:S(2)}, u32[]{:S(2)}) collective-permute-start(bf16[128,1280]{1,0:T(8,128)(2,1)} %pack.9), channel_id=1, source_target_pairs={{0,16},{4,20},{8,24},{12,28},{16,0},{20,4},{24,8},{28,12},{1,17},{... | collective-permute-start | bytes 983048 | tf_op jit(solution)/shard_map/ppermute | solution.py:305
  43.5 1.2 %copy-start.2 = (bf16[2,4096,64]{1,2,0:T(8,128)(2,1)S(1)}, bf16[2,4096,64]{1,2,0:T(8,128)(2,1)}, u32[]{:S(2)}) copy-start(bf16[2,4096,64]{1,2,0:T(8,128)(2,1)} %param.6) | copy-start | bytes 3145732
  44.7 1.0 %copy-start.4 = (bf16[128,1280]{1,0:T(8,128)(2,1)S(1)}, bf16[128,1280]{1,0:T(8,128)(2,1)}, u32[]{:S(2)}) copy-start(bf16[128,1280]{1,0:T(8,128)(2,1)} %copy-done.3) | copy-start | bytes 983044
  44.7 1.1 %copy-start.6 = (bf16[128,1280]{1,0:T(8,128)(2,1)S(1)}, bf16[128,1280]{1,0:T(8,128)(2,1)}, u32[]{:S(2)}) copy-start(bf16[128,1280]{1,0:T(8,128)(2,1)} %copy-done.5) | copy-start | bytes 983044
  71.1 5.0 %collective-permute-start.7 = (bf16[2,64,128]{2,1,0:T(8,128)(2,1)S(1)}, bf16[2,64,128]{2,1,0:T(8,128)(2,1)S(1)}, u32[]{:S(2)}, u32[]{:S(2)}) collective-permute-start(bf16[2,64,128]{2,1,0:T(8,128)(2,1)S(1)} %get-tuple-element.24), channel_id=1, source_target_pairs={{0,16},{4,20},{8,24},{12,28},{16,0},{20,4},{24,8},{28,12},{1,17},{... | collective-permute-start | bytes 98312 | tf_op jit(solution)/shard_map/ppermute | solution.py:305
  71.2 5.0 %collective-permute-start.8 = (bf16[2,64,128]{2,1,0:T(8,128)(2,1)S(1)}, bf16[2,64,128]{2,1,0:T(8,128)(2,1)S(1)}, u32[]{:S(2)}, u32[]{:S(2)}) collective-permute-start(bf16[2,64,128]{2,1,0:T(8,128)(2,1)S(1)} %get-tuple-element.25), channel_id=1, source_target_pairs={{0,8},{4,12},{8,0},{12,4},{16,24},{20,28},{24,16},{28,20},{1,9},{5... | collective-permute-start | bytes 98312 | tf_op jit(solution)/shard_map/ppermute | solution.py:305
  73.9 5.7 %collective-permute-start.9 = (bf16[2,64,128]{2,1,0:T(8,128)(2,1)S(1)}, bf16[2,64,128]{2,1,0:T(8,128)(2,1)S(1)}, u32[]{:S(2)}, u32[]{:S(2)}) collective-permute-start(bf16[2,64,128]{2,1,0:T(8,128)(2,1)S(1)} %get-tuple-element.26), channel_id=1, source_target_pairs={{0,24},{4,28},{8,16},{12,20},{16,8},{20,12},{24,0},{28,4},{1,25},{... | collective-permute-start | bytes 98312 | tf_op jit(solution)/shard_map/ppermute | solution.py:305
  79.6 4.0 %collective-permute-start.10 = (f32[1,64,128]{2,1,0:T(8,128)S(1)}, f32[1,64,128]{2,1,0:T(8,128)S(1)}, u32[]{:S(2)}, u32[]{:S(2)}) collective-permute-start(f32[1,64,128]{2,1,0:T(8,128)S(1)} %slice.9), channel_id=1, source_target_pairs={{0,4},{4,0},{8,12},{12,8},{16,20},{20,16},{24,28},{28,24},{1,5},{5... | collective-permute-start | bytes 98312 | tf_op jit(solution)/shard_map/ppermute | solution.py:305
  83.6 3.6 %collective-permute-start.11 = (f32[64,128]{1,0:T(8,128)S(1)}, f32[64,128]{1,0:T(8,128)S(1)}, u32[]{:S(2)}, u32[]{:S(2)}) collective-permute-start(f32[64,128]{1,0:T(8,128)S(1)} %fusion), channel_id=1, source_target_pairs={{0,3},{1,2},{2,1},{3,0},{4,7},{5,6},{6,5},{7,4},{8,11},{9,10},{10,... | collective-permute-start | bytes 98312 | tf_op jit(solution)/shard_map/ppermute | solution.py:305
  83.6 4.0 %collective-permute-start.12 = (f32[64,128]{1,0:T(8,128)S(1)}, f32[64,128]{1,0:T(8,128)S(1)}, u32[]{:S(2)}, u32[]{:S(2)}) collective-permute-start(f32[64,128]{1,0:T(8,128)S(1)} %fusion), channel_id=1, source_target_pairs={{0,2},{1,3},{2,0},{3,1},{4,6},{5,7},{6,4},{7,5},{8,10},{9,11},{10,... | collective-permute-start | bytes 98312 | tf_op jit(solution)/shard_map/ppermute | solution.py:305
  85.2 2.5 %collective-permute-start.13 = (f32[64,128]{1,0:T(8,128)S(1)}, f32[64,128]{1,0:T(8,128)S(1)}, u32[]{:S(2)}, u32[]{:S(2)}) collective-permute-start(f32[64,128]{1,0:T(8,128)S(1)} %fusion), channel_id=1, source_target_pairs={{0,1},{1,0},{2,3},{3,2},{4,5},{5,4},{6,7},{7,6},{8,9},{9,8},{10,11... | collective-permute-start | bytes 98312 | tf_op jit(solution)/shard_map/ppermute | solution.py:305

commit v25 on v23

--- a/solution.py
+++ b/solution.py
@@ -31,33 +31,29 @@
 
 
 def pack_kernel(k, me_ref, model_ref, qkv_ref, readout_ref, *refs):
-    out_ref, values, readout, sems = refs[-4:]
-    rows = out_ref.shape[0]
-    count, lat = values.shape[0], readout.shape[0]
-    first = (me_ref[0] ^ k) * count
-
-    def columns(h, part, width):
-        return pl.ds(pl.multiple_of(((first + h) * 3 + part) * HD, HD), width)
+    out_ref, slab, readout, sems = refs[-4:]
+    lat = readout.shape[0]
+    count = readout.shape[1] // HD
+    target = me_ref[0] ^ k
+
+    def columns(width):
+        return pl.ds(pl.multiple_of(target * count * width, HD), count * width)
 
     copies = [
-        pltpu.make_async_copy(
-            readout_ref.at[model_ref[0], :, pl.ds(pl.multiple_of(first * HD, HD), count * HD)], readout, sems.at[2 * count]
-        )
+        pltpu.make_async_copy(qkv_ref.at[0, :, columns(3 * HD)], slab, sems.at[0]),
+        pltpu.make_async_copy(readout_ref.at[model_ref[0], :, columns(HD)], readout, sems.at[1]),
     ]
-    for h in range(count):
-        copies.append(pltpu.make_async_copy(qkv_ref.at[0, :, columns(h, 2, HD)], values.at[h], sems.at[h]))
-    for h in range(count):
-        target = out_ref.at[:, h * 2 * HD : (h + 1) * 2 * HD]
-        copies.append(pltpu.make_async_copy(qkv_ref.at[0, :, columns(h, 0, 2 * HD)], target, sems.at[count + h]))
     for copy in copies:
         copy.start()
-    copies[0].wait()
+    for copy in copies:
+        copy.wait()
     for h in range(count):
-        copies[1 + h].wait()
+        base = h * 3 * HD
+        out_ref[:, h * 2 * HD : (h + 1) * 2 * HD] = slab[:, base : base + 2 * HD]
         row, column = value_place(h, count, lat)
-        out_ref[row : row + lat, column : column + HD] = fold(readout[:, h * HD : (h + 1) * HD], values[h])
-    for copy in copies[1 + count :]:
-        copy.wait()
+        out_ref[row : row + lat, column : column + HD] = fold(
+            readout[:, h * HD : (h + 1) * HD], slab[:, base + 2 * HD : base + 3 * HD]
+        )
 
 
 def pack(me, model, qkv, readout_t, k, count, after, first=False):
@@ -70,9 +66,9 @@
         out_specs=VMEM,
         out_shape=jax.ShapeDtypeStruct((rows, width), jnp.bfloat16),
         scratch_shapes=[
-            pltpu.VMEM((count, rows, HD), jnp.bfloat16),
+            pltpu.VMEM((rows, count * 3 * HD), jnp.bfloat16),
             pltpu.VMEM((lat, count * HD), jnp.bfloat16),
-            pltpu.SemaphoreType.DMA((2 * count + 1,)),
+            pltpu.SemaphoreType.DMA((2,)),
         ],
         compiler_params=pltpu.CompilerParams(vmem_limit_bytes=LARGE_VMEM if first else PACK_VMEM),
         cost_estimate=pl.CostEstimate(

time: 86.3 us -> 86 us (level)
  Pallas kernels: 20.3 us -> 16.2 us
  waiting for transfers between devices: 39.9 us -> 41.5 us
  starting transfers between devices: 22.3 us -> 23.9 us
    pallas_call x8, Pallas kernels: 11 us -> 6.94 us  [pack(): pl.pallas_call(functools.partial(pack_kernel, k), in_specs=[SMEM, SMEM] +...]
    ppermute x14, starting transfers between devices: 22.3 us -> 23.9 us  [swap(): return lax.ppermute(array, axis, [(i, i ^ offset) for i in range(size)])]
    ppermute x14, waiting for transfers between devices: 39.9 us -> 41.5 us  [swap(): return lax.ppermute(array, axis, [(i, i ^ offset) for i in range(size)])]
  transfers between devices with their start and end apart: 14 -> 14, of which waited for: 10 -> 10; matrix products, arithmetic and copies ran while one was open for 0% -> 0% of each run, Pallas kernels for 17% -> 12%
where the time goes in v25:
time: 86 us; the launch traced here: 85.7 us
  waiting for transfers between devices  41.5 us (48%)
  starting transfers between devices  23.9 us (28%)
  Pallas kernels  16.2 us (19%)
  local copies, waits for them, and re-layouts  3.22 us (4%)
    ppermute x14, waiting for transfers between devices, swap(): return lax.ppermute(array, axis, [(i, i ^ offset) for i in range(size)])  41.5 us
    ppermute x14, starting transfers between devices, swap(): return lax.ppermute(array, axis, [(i, i ^ offset) for i in range(size)])  23.9 us
    pallas_call x8, Pallas kernels, pack(): pl.pallas_call(functools.partial(pack_kernel, k), in_specs=[SMEM, SMEM] +...  6.94 us
    pallas_call x1, Pallas kernels, attend_early(): pl.pallas_call(functools.partial(early_kernel, offsets, late), in_specs=[...  5.77 us
    pallas_call x1, Pallas kernels, attend_late(): pl.pallas_call(functools.partial(late_kernel, offsets, late), in_specs=[V...  3.48 us
    unnamed x20, local copies, waits for them, and re-layouts  3.21 us
  transfers between devices with their start and end apart: 14, of which 10 were waited for; matrix products, arithmetic and copies ran while one was open for 0% of the time, Pallas kernels for 12%

profile of v25, /device:TPU:0, one launch (start us, length us, event | category | flops | bytes accessed | tf_op | source)
XLA Modules:
  0.0 85.7 jit_solution(14504583257194817924)
XLA Ops:
  0.0 2.1 %pack.10 = bf16[128,1280]{1,0:T(8,128)(2,1)} custom-call(s32[1]{0:T(128)} %bitcast.me_ref, s32[1]{0:T(128)} %bitcast.1.model_ref, bf16[1,128,12288]{2,1,0:T(8,128)(2,1)} %qkv_ref.15, bf16[2,64,4096]{2,1,0:T(8,128)(2,1)} %bitcast.9), custom_call_target="tpu_custom_call" | custom-call | bytes 655360 | tf_op jit(solution)/shard_map/pack/pallas_call | solution.py:63
  2.1 6.0 %collective-permute-start.2 = (bf16[128,1280]{1,0:T(8,128)(2,1)}, bf16[128,1280]{1,0:T(8,128)(2,1)S(1)}, u32[]{:S(2)}, u32[]{:S(2)}) collective-permute-start(bf16[128,1280]{1,0:T(8,128)(2,1)} %pack.10), channel_id=1, source_target_pairs={{0,28},{4,24},{8,20},{12,16},{16,12},{20,8},{24,4},{28,0},{1,29},{... | collective-permute-start | bytes 983048 | tf_op jit(solution)/shard_map/ppermute | solution.py:301
  8.1 0.0 copy-done
  8.1 1.2 %copy-done.1 = bf16[2,4096,64]{1,2,0:T(8,128)(2,1)S(1)} copy-done((bf16[2,4096,64]{1,2,0:T(8,128)(2,1)S(1)}, bf16[2,4096,64]{1,2,0:T(8,128)(2,1)}, u32[]{:S(2)}) %copy-start.1) | copy-done | bytes 1048600
  9.4 0.3 pack.12
  9.6 0.1 collective-permute-start.4
  9.7 0.3 pack.8
  10.0 0.9 %collective-permute-start = (bf16[128,1280]{1,0:T(8,128)(2,1)S(1)}, bf16[128,1280]{1,0:T(8,128)(2,1)S(1)}, u32[]{:S(2)}, u32[]{:S(2)}) collective-permute-start(bf16[128,1280]{1,0:T(8,128)(2,1)S(1)} %pack.8), channel_id=1, source_target_pairs={{0,24},{4,28},{8,16},{12,20},{16,8},{20,12},{24,0},{28,4},{1,25},{... | collective-permute-start | bytes 983048 | tf_op jit(solution)/shard_map/ppermute | solution.py:301
  10.9 6.0 %collective-permute-done.2.refs_0_.refs_1_.refs_5_ = bf16[128,1280]{1,0:T(8,128)(2,1)S(1)} collective-permute-done((bf16[128,1280]{1,0:T(8,128)(2,1)}, bf16[128,1280]{1,0:T(8,128)(2,1)S(1)}, u32[]{:S(2)}, u32[]{:S(2)}) %collective-permute-start.2) | collective-permute-done | bytes 327712 | tf_op jit(solution)/shard_map/ppermute | solution.py:301
  16.9 10.7 %collective-permute-done.4.refs_0_.refs_3_ = bf16[128,1280]{1,0:T(8,128)(2,1)S(1)} collective-permute-done((bf16[128,1280]{1,0:T(8,128)(2,1)S(1)}, bf16[128,1280]{1,0:T(8,128)(2,1)S(1)}, u32[]{:S(2)}, u32[]{:S(2)}) %collective-permute-start.4) | collective-permute-done | bytes 327712 | tf_op jit(solution)/shard_map/ppermute | solution.py:301
  27.6 1.0 %pack.15 = bf16[128,1280]{1,0:T(8,128)(2,1)} custom-call(s32[1]{0:T(128)} %bitcast.me_ref, s32[1]{0:T(128)} %bitcast.1.model_ref, bf16[1,128,12288]{2,1,0:T(8,128)(2,1)S(1)} %copy-done, bf16[2,64,4096]{2,1,0:T(8,128)(2,1)S(1)} %bitcast.12, bf16[128,1280]{1,0:T(8,128)(2,1)S(1)} %collective-permute-done.4.refs_0_.refs_3_, ...), custom_call_target="tpu_custom_call" | custom-call | bytes 655360 | tf_op jit(solution)/shard_map/pack/pallas_call | solution.py:63
  28.6 2.7 %collective-permute-start.6 = (bf16[128,1280]{1,0:T(8,128)(2,1)}, bf16[128,1280]{1,0:T(8,128)(2,1)}, u32[]{:S(2)}, u32[]{:S(2)}) collective-permute-start(bf16[128,1280]{1,0:T(8,128)(2,1)} %pack.15), channel_id=1, source_target_pairs={{0,8},{4,12},{8,0},{12,4},{16,24},{20,28},{24,16},{28,20},{1,9},{5... | collective-permute-start | bytes 983048 | tf_op jit(solution)/shard_map/ppermute | solution.py:301
  31.3 1.0 %pack.14 = bf16[128,1280]{1,0:T(8,128)(2,1)} custom-call(s32[1]{0:T(128)} %bitcast.me_ref, s32[1]{0:T(128)} %bitcast.1.model_ref, bf16[1,128,12288]{2,1,0:T(8,128)(2,1)S(1)} %copy-done, bf16[2,64,4096]{2,1,0:T(8,128)(2,1)S(1)} %bitcast.13, bf16[128,1280]{1,0:T(8,128)(2,1)S(1)} %collective-permute-done.4.refs_0_.refs_3_), custom_call_target="tpu_custom_call" | custom-call | bytes 655360 | tf_op jit(solution)/shard_map/pack/pallas_call | solution.py:63
  32.4 1.4 %collective-permute-start.5 = (bf16[128,1280]{1,0:T(8,128)(2,1)}, bf16[128,1280]{1,0:T(8,128)(2,1)}, u32[]{:S(2)}, u32[]{:S(2)}) collective-permute-start(bf16[128,1280]{1,0:T(8,128)(2,1)} %pack.14), channel_id=1, source_target_pairs={{0,4},{4,0},{8,12},{12,8},{16,20},{20,16},{24,28},{28,24},{1,5},{5... | collective-permute-start | bytes 983048 | tf_op jit(solution)/shard_map/ppermute | solution.py:301
  33.7 0.0 copy-done.3
  33.7 1.0 %pack.11 = bf16[128,1280]{1,0:T(8,128)(2,1)} custom-call(s32[1]{0:T(128)} %bitcast.me_ref, s32[1]{0:T(128)} %bitcast.1.model_ref, bf16[1,128,12288]{2,1,0:T(8,128)(2,1)S(1)} %copy-done, bf16[2,64,4096]{2,1,0:T(8,128)(2,1)S(1)} %bitcast.14, bf16[128,1280]{1,0:T(8,128)(2,1)S(1)} %collective-permute-done.2.refs_0_.refs_1_.refs_5_), custom_call_target="tpu_custom_call" | custom-call | bytes 655360 | tf_op jit(solution)/shard_map/pack/pallas_call | solution.py:63
  34.7 0.1 collective-permute-start.3
  34.8 0.0 collective-permute-done.refs_0_.refs_4_
  34.8 1.0 %pack.9 = bf16[128,1280]{1,0:T(8,128)(2,1)} custom-call(s32[1]{0:T(128)} %bitcast.me_ref, s32[1]{0:T(128)} %bitcast.1.model_ref, bf16[1,128,12288]{2,1,0:T(8,128)(2,1)S(1)} %copy-done, bf16[2,64,4096]{2,1,0:T(8,128)(2,1)S(1)} %bitcast.15, bf16[128,1280]{1,0:T(8,128)(2,1)S(1)} %collective-permute-done.refs_0_.refs_4_), custom_call_target="tpu_custom_call" | custom-call | bytes 655360 | tf_op jit(solution)/shard_map/pack/pallas_call | solution.py:63
  35.9 0.0 copy-start.7
  35.9 0.0 copy-start.8
  35.9 0.0 copy-start.9
  35.9 6.7 %collective-permute-start.1 = (bf16[128,1280]{1,0:T(8,128)(2,1)}, bf16[128,1280]{1,0:T(8,128)(2,1)}, u32[]{:S(2)}, u32[]{:S(2)}) collective-permute-start(bf16[128,1280]{1,0:T(8,128)(2,1)} %pack.9), channel_id=1, source_target_pairs={{0,16},{4,20},{8,24},{12,28},{16,0},{20,4},{24,8},{28,12},{1,17},{... | collective-permute-start | bytes 983048 | tf_op jit(solution)/shard_map/ppermute | solution.py:301
  42.6 1.2 %copy-done.2 = bf16[2,4096,64]{1,2,0:T(8,128)(2,1)S(1)} copy-done((bf16[2,4096,64]{1,2,0:T(8,128)(2,1)S(1)}, bf16[2,4096,64]{1,2,0:T(8,128)(2,1)}, u32[]{:S(2)}) %copy-start.2) | copy-done | bytes 1048600
  43.9 0.3 pack.13.refs_0_
  44.2 0.0 collective-permute-done.6.refs_2_
  44.2 0.0 collective-permute-done.5.refs_1_
  44.2 0.6 copy-done.4
  44.8 0.1 copy-done.6
  44.9 5.8 %attend_early.1 = (f32[4,64,768]{2,1,0:T(8,128)S(1)}, f32[2,8,768]{2,1,0:T(8,128)S(1)}, f32[8,128]{1,0:T(8,128)S(1)}, bf16[6,128,1280]{2,1,0:T(8,128)(2,1)S(1)},...) custom-call(s32[4]{0:T(128)S(1)} %copy-done.8, s32[1]{0:T(128)} %bitcast.me_ref, ...), custom_call_target="tpu_custom_call" | custom-call | flops 905969664 | bytes 2359296 | tf_op jit(solution)/shard_map/attend_early/pallas_call | solution.py:250
  50.7 10.6 %collective-permute-done.3.refs_1_ = bf16[128,1280]{1,0:T(8,128)(2,1)} collective-permute-done((bf16[128,1280]{1,0:T(8,128)(2,1)}, bf16[128,1280]{1,0:T(8,128)(2,1)}, u32[]{:S(2)}, u32[]{:S(2)}) %collective-permute-start.3) | collective-permute-done | bytes 327712 | tf_op jit(solution)/shard_map/ppermute | solution.py:301
  61.4 5.9 %collective-permute-done.1.refs_0_ = bf16[128,1280]{1,0:T(8,128)(2,1)} collective-permute-done((bf16[128,1280]{1,0:T(8,128)(2,1)}, bf16[128,1280]{1,0:T(8,128)(2,1)}, u32[]{:S(2)}, u32[]{:S(2)}) %collective-permute-start.1) | collective-permute-done | bytes 327712 | tf_op jit(solution)/shard_map/ppermute | solution.py:301
  67.3 3.5 %attend_late.1 = (f32[2,64,128]{2,1,0:T(8,128)S(1)}, bf16[2,64,128]{2,1,0:T(8,128)(2,1)S(1)}, bf16[2,64,128]{2,1,0:T(8,128)(2,1)S(1)}, bf16[2,64,128]{2,1,0:T(8,128)(2,1)S(1)}) custom-call(bf16[128,1280]{1,0:T(8,128)(2,1)} %collective-permute-done.1.refs_0_, bf16[128,1280]{1,0:T(8,128)(2,1)} %collective-permute-done.3.refs_1_, ...), custom_call_target="tpu_custom_call" | custom-call | flops 402653184 | bytes 3145728 | tf_op jit(solution)/shard_map/attend_late/pallas_call | solution.py:281
  70.7 0.1 collective-permute-start.7
  70.8 2.3 %collective-permute-start.8 = (bf16[2,64,128]{2,1,0:T(8,128)(2,1)S(1)}, bf16[2,64,128]{2,1,0:T(8,128)(2,1)S(1)}, u32[]{:S(2)}, u32[]{:S(2)}) collective-permute-start(bf16[2,64,128]{2,1,0:T(8,128)(2,1)S(1)} %get-tuple-element.25), channel_id=1, source_target_pairs={{0,24},{4,28},{8,16},{12,20},{16,8},{20,12},{24,0},{28,4},{1,25},{... | collective-permute-start | bytes 98312 | tf_op jit(solution)/shard_map/ppermute | solution.py:301
  73.1 1.2 %collective-permute-start.9 = (bf16[2,64,128]{2,1,0:T(8,128)(2,1)S(1)}, bf16[2,64,128]{2,1,0:T(8,128)(2,1)S(1)}, u32[]{:S(2)}, u32[]{:S(2)}) collective-permute-start(bf16[2,64,128]{2,1,0:T(8,128)(2,1)S(1)} %get-tuple-element.26), channel_id=1, source_target_pairs={{0,8},{4,12},{8,0},{12,4},{16,24},{20,28},{24,16},{28,20},{1,9},{5... | collective-permute-start | bytes 98312 | tf_op jit(solution)/shard_map/ppermute | solution.py:301
  74.3 1.4 %collective-permute-done.7 = bf16[2,64,128]{2,1,0:T(8,128)(2,1)S(1)} collective-permute-done((bf16[2,64,128]{2,1,0:T(8,128)(2,1)S(1)}, bf16[2,64,128]{2,1,0:T(8,128)(2,1)S(1)}, u32[]{:S(2)}, u32[]{:S(2)}) %collective-permute-start.7) | collective-permute-done | bytes 32800 | tf_op jit(solution)/shard_map/ppermute | solution.py:301
  75.7 0.9 %collective-permute-done.8 = bf16[2,64,128]{2,1,0:T(8,128)(2,1)S(1)} collective-permute-done((bf16[2,64,128]{2,1,0:T(8,128)(2,1)S(1)}, bf16[2,64,128]{2,1,0:T(8,128)(2,1)S(1)}, u32[]{:S(2)}, u32[]{:S(2)}) %collective-permute-start.8) | collective-permute-done | bytes 32800 | tf_op jit(solution)/shard_map/ppermute | solution.py:301
  76.6 0.4 collective-permute-done.9
  77.1 0.6 collective-permute-start.10
  77.7 3.4 %collective-permute-done.10 = f32[1,64,128]{2,1,0:T(8,128)S(1)} collective-permute-done((f32[1,64,128]{2,1,0:T(8,128)S(1)}, f32[1,64,128]{2,1,0:T(8,128)S(1)}, u32[]{:S(2)}, u32[]{:S(2)}) %collective-permute-start.10) | collective-permute-done | bytes 32800 | tf_op jit(solution)/shard_map/ppermute | solution.py:301
  81.0 0.0 collective-permute-start.11
  81.1 1.6 %collective-permute-start.12 = (f32[64,128]{1,0:T(8,128)S(1)}, f32[64,128]{1,0:T(8,128)S(1)}, u32[]{:S(2)}, u32[]{:S(2)}) collective-permute-start(f32[64,128]{1,0:T(8,128)S(1)} %fusion), channel_id=1, source_target_pairs={{0,2},{1,3},{2,0},{3,1},{4,6},{5,7},{6,4},{7,5},{8,10},{9,11},{10,... | collective-permute-start | bytes 98312 | tf_op jit(solution)/shard_map/ppermute | solution.py:301
  82.6 0.3 collective-permute-start.13
  82.9 1.8 %collective-permute-done.11 = f32[64,128]{1,0:T(8,128)S(1)} collective-permute-done((f32[64,128]{1,0:T(8,128)S(1)}, f32[64,128]{1,0:T(8,128)S(1)}, u32[]{:S(2)}, u32[]{:S(2)}) %collective-permute-start.11) | collective-permute-done | bytes 32800 | tf_op jit(solution)/shard_map/ppermute | solution.py:301
  84.7 0.4 collective-permute-done.12
  85.1 0.0 collective-permute-done.13
  85.1 0.6 add_bitcast_fusion
  (14 shorter events, 0.0 us)
Async XLA Ops:
  0.0 8.1 %copy-start = (bf16[1,128,12288]{2,1,0:T(8,128)(2,1)S(1)}, bf16[1,128,12288]{2,1,0:T(8,128)(2,1)}, u32[]{:S(2)}) copy-start(bf16[1,128,12288]{2,1,0:T(8,128)(2,1)} %qkv_ref.15) | copy-start | bytes 9437188
  2.1 14.9 %collective-permute-start.2 = (bf16[128,1280]{1,0:T(8,128)(2,1)}, bf16[128,1280]{1,0:T(8,128)(2,1)S(1)}, u32[]{:S(2)}, u32[]{:S(2)}) collective-permute-start(bf16[128,1280]{1,0:T(8,128)(2,1)} %pack.10), channel_id=1, source_target_pairs={{0,28},{4,24},{8,20},{12,16},{16,12},{20,8},{24,4},{28,0},{1,29},{... | collective-permute-start | bytes 983048 | tf_op jit(solution)/shard_map/ppermute | solution.py:301
  8.1 1.2 %copy-start.1 = (bf16[2,4096,64]{1,2,0:T(8,128)(2,1)S(1)}, bf16[2,4096,64]{1,2,0:T(8,128)(2,1)}, u32[]{:S(2)}) copy-start(bf16[2,4096,64]{1,2,0:T(8,128)(2,1)} %param.6) | copy-start | bytes 3145732
  9.6 18.0 %collective-permute-start.4 = (bf16[128,1280]{1,0:T(8,128)(2,1)S(1)}, bf16[128,1280]{1,0:T(8,128)(2,1)S(1)}, u32[]{:S(2)}, u32[]{:S(2)}) collective-permute-start(bf16[128,1280]{1,0:T(8,128)(2,1)S(1)} %pack.12), channel_id=1, source_target_pairs={{0,12},{4,8},{8,4},{12,0},{16,28},{20,24},{24,20},{28,16},{1,13},{... | collective-permute-start | bytes 983048 | tf_op jit(solution)/shard_map/ppermute | solution.py:301
  10.0 24.8 %collective-permute-start = (bf16[128,1280]{1,0:T(8,128)(2,1)S(1)}, bf16[128,1280]{1,0:T(8,128)(2,1)S(1)}, u32[]{:S(2)}, u32[]{:S(2)}) collective-permute-start(bf16[128,1280]{1,0:T(8,128)(2,1)S(1)} %pack.8), channel_id=1, source_target_pairs={{0,24},{4,28},{8,16},{12,20},{16,8},{20,12},{24,0},{28,4},{1,25},{... | collective-permute-start | bytes 983048 | tf_op jit(solution)/shard_map/ppermute | solution.py:301
  16.9 16.8 %copy-start.3 = (bf16[128,1280]{1,0:T(8,128)(2,1)}, bf16[128,1280]{1,0:T(8,128)(2,1)S(1)}, u32[]{:S(2)}) copy-start(bf16[128,1280]{1,0:T(8,128)(2,1)S(1)} %collective-permute-done.2.refs_0_.refs_1_.refs_5_) | copy-start | bytes 983044
  28.6 15.5 %collective-permute-start.6 = (bf16[128,1280]{1,0:T(8,128)(2,1)}, bf16[128,1280]{1,0:T(8,128)(2,1)}, u32[]{:S(2)}, u32[]{:S(2)}) collective-permute-start(bf16[128,1280]{1,0:T(8,128)(2,1)} %pack.15), channel_id=1, source_target_pairs={{0,8},{4,12},{8,0},{12,4},{16,24},{20,28},{24,16},{28,20},{1,9},{5... | collective-permute-start | bytes 983048 | tf_op jit(solution)/shard_map/ppermute | solution.py:301
  32.4 11.8 %collective-permute-start.5 = (bf16[128,1280]{1,0:T(8,128)(2,1)}, bf16[128,1280]{1,0:T(8,128)(2,1)}, u32[]{:S(2)}, u32[]{:S(2)}) collective-permute-start(bf16[128,1280]{1,0:T(8,128)(2,1)} %pack.14), channel_id=1, source_target_pairs={{0,4},{4,0},{8,12},{12,8},{16,20},{20,16},{24,28},{28,24},{1,5},{5... | collective-permute-start | bytes 983048 | tf_op jit(solution)/shard_map/ppermute | solution.py:301
  34.7 26.6 %collective-permute-start.3 = (bf16[128,1280]{1,0:T(8,128)(2,1)}, bf16[128,1280]{1,0:T(8,128)(2,1)}, u32[]{:S(2)}, u32[]{:S(2)}) collective-permute-start(bf16[128,1280]{1,0:T(8,128)(2,1)} %pack.11), channel_id=1, source_target_pairs={{0,20},{4,16},{8,28},{12,24},{16,4},{20,0},{24,12},{28,8},{1,21},{... | collective-permute-start | bytes 983048 | tf_op jit(solution)/shard_map/ppermute | solution.py:301
  34.8 1.1 %copy-start.5 = (bf16[128,1280]{1,0:T(8,128)(2,1)}, bf16[128,1280]{1,0:T(8,128)(2,1)S(1)}, u32[]{:S(2)}) copy-start(bf16[128,1280]{1,0:T(8,128)(2,1)S(1)} %collective-permute-done.refs_0_.refs_4_) | copy-start | bytes 983044
  35.9 8.3 %copy-start.7 = (f32[1000]{0:T(1024)S(1)}, f32[1000]{0:T(1024)}, u32[]{:S(2)}) copy-start(f32[1000]{0:T(1024)} %step_weight_ref.1) | copy-start | bytes 12004
  35.9 8.3 %copy-start.8 = (s32[4]{0:T(128)S(1)}, s32[4]{0:T(128)}, u32[]{:S(2)}) copy-start(s32[4]{0:T(128)} %frames_ref.1) | copy-start | bytes 52
  35.9 8.3 %copy-start.9 = (s32[2]{0:T(128)S(1)}, s32[2]{0:T(128)}, u32[]{:S(2)}) copy-start(s32[2]{0:T(128)} %timestep_ref.1) | copy-start | bytes 28
  35.9 31.4 %collective-permute-start.1 = (bf16[128,1280]{1,0:T(8,128)(2,1)}, bf16[128,1280]{1,0:T(8,128)(2,1)}, u32[]{:S(2)}, u32[]{:S(2)}) collective-permute-start(bf16[128,1280]{1,0:T(8,128)(2,1)} %pack.9), channel_id=1, source_target_pairs={{0,16},{4,20},{8,24},{12,28},{16,0},{20,4},{24,8},{28,12},{1,17},{... | collective-permute-start | bytes 983048 | tf_op jit(solution)/shard_map/ppermute | solution.py:301
  42.6 1.2 %copy-start.2 = (bf16[2,4096,64]{1,2,0:T(8,128)(2,1)S(1)}, bf16[2,4096,64]{1,2,0:T(8,128)(2,1)}, u32[]{:S(2)}) copy-start(bf16[2,4096,64]{1,2,0:T(8,128)(2,1)} %param.6) | copy-start | bytes 3145732
  43.9 1.0 %copy-start.4 = (bf16[128,1280]{1,0:T(8,128)(2,1)S(1)}, bf16[128,1280]{1,0:T(8,128)(2,1)}, u32[]{:S(2)}) copy-start(bf16[128,1280]{1,0:T(8,128)(2,1)} %copy-done.3) | copy-start | bytes 983044
  43.9 1.1 %copy-start.6 = (bf16[128,1280]{1,0:T(8,128)(2,1)S(1)}, bf16[128,1280]{1,0:T(8,128)(2,1)}, u32[]{:S(2)}) copy-start(bf16[128,1280]{1,0:T(8,128)(2,1)} %copy-done.5) | copy-start | bytes 983044
  70.7 5.0 %collective-permute-start.7 = (bf16[2,64,128]{2,1,0:T(8,128)(2,1)S(1)}, bf16[2,64,128]{2,1,0:T(8,128)(2,1)S(1)}, u32[]{:S(2)}, u32[]{:S(2)}) collective-permute-start(bf16[2,64,128]{2,1,0:T(8,128)(2,1)S(1)} %get-tuple-element.24), channel_id=1, source_target_pairs={{0,16},{4,20},{8,24},{12,28},{16,0},{20,4},{24,8},{28,12},{1,17},{... | collective-permute-start | bytes 98312 | tf_op jit(solution)/shard_map/ppermute | solution.py:301
  70.8 5.8 %collective-permute-start.8 = (bf16[2,64,128]{2,1,0:T(8,128)(2,1)S(1)}, bf16[2,64,128]{2,1,0:T(8,128)(2,1)S(1)}, u32[]{:S(2)}, u32[]{:S(2)}) collective-permute-start(bf16[2,64,128]{2,1,0:T(8,128)(2,1)S(1)} %get-tuple-element.25), channel_id=1, source_target_pairs={{0,24},{4,28},{8,16},{12,20},{16,8},{20,12},{24,0},{28,4},{1,25},{... | collective-permute-start | bytes 98312 | tf_op jit(solution)/shard_map/ppermute | solution.py:301
  73.1 3.9 %collective-permute-start.9 = (bf16[2,64,128]{2,1,0:T(8,128)(2,1)S(1)}, bf16[2,64,128]{2,1,0:T(8,128)(2,1)S(1)}, u32[]{:S(2)}, u32[]{:S(2)}) collective-permute-start(bf16[2,64,128]{2,1,0:T(8,128)(2,1)S(1)} %get-tuple-element.26), channel_id=1, source_target_pairs={{0,8},{4,12},{8,0},{12,4},{16,24},{20,28},{24,16},{28,20},{1,9},{5... | collective-permute-start | bytes 98312 | tf_op jit(solution)/shard_map/ppermute | solution.py:301
  77.1 4.0 %collective-permute-start.10 = (f32[1,64,128]{2,1,0:T(8,128)S(1)}, f32[1,64,128]{2,1,0:T(8,128)S(1)}, u32[]{:S(2)}, u32[]{:S(2)}) collective-permute-start(f32[1,64,128]{2,1,0:T(8,128)S(1)} %slice.9), channel_id=1, source_target_pairs={{0,4},{4,0},{8,12},{12,8},{16,20},{20,16},{24,28},{28,24},{1,5},{5... | collective-permute-start | bytes 98312 | tf_op jit(solution)/shard_map/ppermute | solution.py:301
  81.0 3.6 %collective-permute-start.11 = (f32[64,128]{1,0:T(8,128)S(1)}, f32[64,128]{1,0:T(8,128)S(1)}, u32[]{:S(2)}, u32[]{:S(2)}) collective-permute-start(f32[64,128]{1,0:T(8,128)S(1)} %fusion), channel_id=1, source_target_pairs={{0,3},{1,2},{2,1},{3,0},{4,7},{5,6},{6,5},{7,4},{8,11},{9,10},{10,... | collective-permute-start | bytes 98312 | tf_op jit(solution)/shard_map/ppermute | solution.py:301
  81.1 4.0 %collective-permute-start.12 = (f32[64,128]{1,0:T(8,128)S(1)}, f32[64,128]{1,0:T(8,128)S(1)}, u32[]{:S(2)}, u32[]{:S(2)}) collective-permute-start(f32[64,128]{1,0:T(8,128)S(1)} %fusion), channel_id=1, source_target_pairs={{0,2},{1,3},{2,0},{3,1},{4,6},{5,7},{6,4},{7,5},{8,10},{9,11},{10,... | collective-permute-start | bytes 98312 | tf_op jit(solution)/shard_map/ppermute | solution.py:301
  82.6 2.5 %collective-permute-start.13 = (f32[64,128]{1,0:T(8,128)S(1)}, f32[64,128]{1,0:T(8,128)S(1)}, u32[]{:S(2)}, u32[]{:S(2)}) collective-permute-start(f32[64,128]{1,0:T(8,128)S(1)} %fusion), channel_id=1, source_target_pairs={{0,1},{1,0},{2,3},{3,2},{4,5},{5,4},{6,7},{7,6},{8,9},{9,8},{10,11... | collective-permute-start | bytes 98312 | tf_op jit(solution)/shard_map/ppermute | solution.py:301

commit v26 on v25

--- a/solution.py
+++ b/solution.py
@@ -319,10 +319,10 @@
     pieces = [None] * seq_count
     for n in range(half):
         k = seq_count - 1 - n
-        pieces[k] = swap(pack(me, model, qkv, readout_t, k, count, [pieces[k + 2]] if n > 1 else [], n == 0), "seq", k)
+        pieces[k] = swap(pack(me, model, qkv, readout_t, k, count, [pieces[k + 2]] if n > 1 else [], n < 2), "seq", k)
     for k in range(half - 1, 0, -1):
         after = [] if k == half - 1 else [pieces[k + 1], pieces[seq_count - 1]] if k > 1 else [pieces[half - 1]]
-        pieces[k] = swap(pack(me, model, qkv, readout_t, k, count, after), "seq", k)
+        pieces[k] = swap(pack(me, model, qkv, readout_t, k, count, after, k == half - 1), "seq", k)
     pieces[0] = pack(me, model, qkv, readout_t, 0, count, [pieces[half - 1]])
     late = [half, half + 1]
     early = [k for k in range(seq_count) if k not in late]

time: 86 us -> 85.8 us (level)
  Pallas kernels: 16.2 us -> 19.5 us
  waiting for transfers between devices: 41.5 us -> 39.3 us
  starting transfers between devices: 23.9 us -> 22.6 us
    pallas_call x8, Pallas kernels: 6.94 us -> 10.2 us  [pack(): pl.pallas_call(functools.partial(pack_kernel, k), in_specs=[SMEM, SMEM] +...]
    ppermute x14, waiting for transfers between devices: 41.5 us -> 39.3 us  [swap(): return lax.ppermute(array, axis, [(i, i ^ offset) for i in range(size)])]
    ppermute x14, starting transfers between devices: 23.9 us -> 22.6 us  [swap(): return lax.ppermute(array, axis, [(i, i ^ offset) for i in range(size)])]
  transfers between devices with their start and end apart: 14 -> 14, of which waited for: 10 -> 10; matrix products, arithmetic and copies ran while one was open for 0% -> 0% of each run, Pallas kernels for 12% -> 16%
where the time goes in v26:
time: 85.8 us; the launch traced here: 85.5 us
  waiting for transfers between devices  39.3 us (46%)
  starting transfers between devices  22.6 us (26%)
  Pallas kernels  19.5 us (23%)
  local copies, waits for them, and re-layouts  3.22 us (4%)
    ppermute x14, waiting for transfers between devices, swap(): return lax.ppermute(array, axis, [(i, i ^ offset) for i in range(size)])  39.3 us
    ppermute x14, starting transfers between devices, swap(): return lax.ppermute(array, axis, [(i, i ^ offset) for i in range(size)])  22.6 us
    pallas_call x8, Pallas kernels, pack(): pl.pallas_call(functools.partial(pack_kernel, k), in_specs=[SMEM, SMEM] +...  10.2 us
    pallas_call x1, Pallas kernels, attend_early(): pl.pallas_call(functools.partial(early_kernel, offsets, late), in_specs=[...  5.77 us
    pallas_call x1, Pallas kernels, attend_late(): pl.pallas_call(functools.partial(late_kernel, offsets, late), in_specs=[V...  3.47 us
    unnamed x20, local copies, waits for them, and re-layouts  3.21 us
  transfers between devices with their start and end apart: 14, of which 10 were waited for; matrix products, arithmetic and copies ran while one was open for 0% of the time, Pallas kernels for 16%

profile of v26, /device:TPU:0, one launch (start us, length us, event | category | flops | bytes accessed | tf_op | source)
XLA Modules:
  0.0 85.5 jit_solution(7269820067130331973)
XLA Ops:
  0.0 1.9 %pack.10 = bf16[128,1280]{1,0:T(8,128)(2,1)} custom-call(s32[1]{0:T(128)} %bitcast.me_ref, s32[1]{0:T(128)} %bitcast.1.model_ref, bf16[1,128,12288]{2,1,0:T(8,128)(2,1)} %qkv_ref.15, bf16[2,64,4096]{2,1,0:T(8,128)(2,1)} %bitcast.9), custom_call_target="tpu_custom_call" | custom-call | bytes 655360 | tf_op jit(solution)/shard_map/pack/pallas_call | solution.py:63
  1.9 6.0 %collective-permute-start.2 = (bf16[128,1280]{1,0:T(8,128)(2,1)}, bf16[128,1280]{1,0:T(8,128)(2,1)S(1)}, u32[]{:S(2)}, u32[]{:S(2)}) collective-permute-start(bf16[128,1280]{1,0:T(8,128)(2,1)} %pack.10), channel_id=1, source_target_pairs={{0,28},{4,24},{8,20},{12,16},{16,12},{20,8},{24,4},{28,0},{1,29},{... | collective-permute-start | bytes 983048 | tf_op jit(solution)/shard_map/ppermute | solution.py:301
  8.0 1.9 %pack.12 = bf16[128,1280]{1,0:T(8,128)(2,1)} custom-call(s32[1]{0:T(128)} %bitcast.me_ref, s32[1]{0:T(128)} %bitcast.1.model_ref, bf16[1,128,12288]{2,1,0:T(8,128)(2,1)} %qkv_ref.15, bf16[2,64,4096]{2,1,0:T(8,128)(2,1)} %bitcast.10), custom_call_target="tpu_custom_call" | custom-call | bytes 655360 | tf_op jit(solution)/shard_map/pack/pallas_call | solution.py:63
  9.9 0.0 copy-start
  9.9 0.1 collective-permute-start.4
  10.0 2.1 %pack.8 = bf16[128,1280]{1,0:T(8,128)(2,1)} custom-call(s32[1]{0:T(128)} %bitcast.me_ref, s32[1]{0:T(128)} %bitcast.1.model_ref, bf16[1,128,12288]{2,1,0:T(8,128)(2,1)} %qkv_ref.15, bf16[2,64,4096]{2,1,0:T(8,128)(2,1)} %bitcast.11), custom_call_target="tpu_custom_call" | custom-call | bytes 655360 | tf_op jit(solution)/shard_map/pack/pallas_call | solution.py:63
  12.1 1.0 %collective-permute-start = (bf16[128,1280]{1,0:T(8,128)(2,1)}, bf16[128,1280]{1,0:T(8,128)(2,1)S(1)}, u32[]{:S(2)}, u32[]{:S(2)}) collective-permute-start(bf16[128,1280]{1,0:T(8,128)(2,1)} %pack.8), channel_id=1, source_target_pairs={{0,24},{4,28},{8,16},{12,20},{16,8},{20,12},{24,0},{28,4},{1,25},{... | collective-permute-start | bytes 983048 | tf_op jit(solution)/shard_map/ppermute | solution.py:301
  13.1 3.7 %collective-permute-done.2.refs_0_.refs_1_.refs_5_ = bf16[128,1280]{1,0:T(8,128)(2,1)S(1)} collective-permute-done((bf16[128,1280]{1,0:T(8,128)(2,1)}, bf16[128,1280]{1,0:T(8,128)(2,1)S(1)}, u32[]{:S(2)}, u32[]{:S(2)}) %collective-permute-start.2) | collective-permute-done | bytes 327712 | tf_op jit(solution)/shard_map/ppermute | solution.py:301
  16.8 10.8 %collective-permute-done.4.refs_0_.refs_3_ = bf16[128,1280]{1,0:T(8,128)(2,1)S(1)} collective-permute-done((bf16[128,1280]{1,0:T(8,128)(2,1)}, bf16[128,1280]{1,0:T(8,128)(2,1)S(1)}, u32[]{:S(2)}, u32[]{:S(2)}) %collective-permute-start.4) | collective-permute-done | bytes 327712 | tf_op jit(solution)/shard_map/ppermute | solution.py:301
  27.6 1.2 %copy-done.1 = bf16[2,4096,64]{1,2,0:T(8,128)(2,1)S(1)} copy-done((bf16[2,4096,64]{1,2,0:T(8,128)(2,1)S(1)}, bf16[2,4096,64]{1,2,0:T(8,128)(2,1)}, u32[]{:S(2)}) %copy-start.1) | copy-done | bytes 1048600
  28.8 1.0 %pack.15 = bf16[128,1280]{1,0:T(8,128)(2,1)} custom-call(s32[1]{0:T(128)} %bitcast.me_ref, s32[1]{0:T(128)} %bitcast.1.model_ref, bf16[1,128,12288]{2,1,0:T(8,128)(2,1)S(1)} %copy-done, bf16[2,64,4096]{2,1,0:T(8,128)(2,1)S(1)} %bitcast.12, bf16[128,1280]{1,0:T(8,128)(2,1)S(1)} %collective-permute-done.4.refs_0_.refs_3_, ...), custom_call_target="tpu_custom_call" | custom-call | bytes 655360 | tf_op jit(solution)/shard_map/pack/pallas_call | solution.py:63
  29.8 2.6 %collective-permute-start.6 = (bf16[128,1280]{1,0:T(8,128)(2,1)}, bf16[128,1280]{1,0:T(8,128)(2,1)}, u32[]{:S(2)}, u32[]{:S(2)}) collective-permute-start(bf16[128,1280]{1,0:T(8,128)(2,1)} %pack.15), channel_id=1, source_target_pairs={{0,8},{4,12},{8,0},{12,4},{16,24},{20,28},{24,16},{28,20},{1,9},{5... | collective-permute-start | bytes 983048 | tf_op jit(solution)/shard_map/ppermute | solution.py:301
  32.5 1.0 %pack.14 = bf16[128,1280]{1,0:T(8,128)(2,1)} custom-call(s32[1]{0:T(128)} %bitcast.me_ref, s32[1]{0:T(128)} %bitcast.1.model_ref, bf16[1,128,12288]{2,1,0:T(8,128)(2,1)S(1)} %copy-done, bf16[2,64,4096]{2,1,0:T(8,128)(2,1)S(1)} %bitcast.13, bf16[128,1280]{1,0:T(8,128)(2,1)S(1)} %collective-permute-done.4.refs_0_.refs_3_), custom_call_target="tpu_custom_call" | custom-call | bytes 655360 | tf_op jit(solution)/shard_map/pack/pallas_call | solution.py:63
  33.5 1.3 %collective-permute-start.5 = (bf16[128,1280]{1,0:T(8,128)(2,1)}, bf16[128,1280]{1,0:T(8,128)(2,1)}, u32[]{:S(2)}, u32[]{:S(2)}) collective-permute-start(bf16[128,1280]{1,0:T(8,128)(2,1)} %pack.14), channel_id=1, source_target_pairs={{0,4},{4,0},{8,12},{12,8},{16,20},{20,16},{24,28},{28,24},{1,5},{5... | collective-permute-start | bytes 983048 | tf_op jit(solution)/shard_map/ppermute | solution.py:301
  34.8 0.0 copy-done.3
  34.8 1.0 %pack.11 = bf16[128,1280]{1,0:T(8,128)(2,1)} custom-call(s32[1]{0:T(128)} %bitcast.me_ref, s32[1]{0:T(128)} %bitcast.1.model_ref, bf16[1,128,12288]{2,1,0:T(8,128)(2,1)S(1)} %copy-done, bf16[2,64,4096]{2,1,0:T(8,128)(2,1)S(1)} %bitcast.14, bf16[128,1280]{1,0:T(8,128)(2,1)S(1)} %collective-permute-done.2.refs_0_.refs_1_.refs_5_), custom_call_target="tpu_custom_call" | custom-call | bytes 655360 | tf_op jit(solution)/shard_map/pack/pallas_call | solution.py:63
  35.8 0.1 collective-permute-start.3
  35.9 0.0 collective-permute-done.refs_0_.refs_4_
  35.9 1.0 %pack.9 = bf16[128,1280]{1,0:T(8,128)(2,1)} custom-call(s32[1]{0:T(128)} %bitcast.me_ref, s32[1]{0:T(128)} %bitcast.1.model_ref, bf16[1,128,12288]{2,1,0:T(8,128)(2,1)S(1)} %copy-done, bf16[2,64,4096]{2,1,0:T(8,128)(2,1)S(1)} %bitcast.15, bf16[128,1280]{1,0:T(8,128)(2,1)S(1)} %collective-permute-done.refs_0_.refs_4_), custom_call_target="tpu_custom_call" | custom-call | bytes 655360 | tf_op jit(solution)/shard_map/pack/pallas_call | solution.py:63
  36.9 0.0 copy-start.7
  36.9 0.0 copy-start.8
  37.0 0.0 copy-start.9
  37.0 5.4 %collective-permute-start.1 = (bf16[128,1280]{1,0:T(8,128)(2,1)}, bf16[128,1280]{1,0:T(8,128)(2,1)}, u32[]{:S(2)}, u32[]{:S(2)}) collective-permute-start(bf16[128,1280]{1,0:T(8,128)(2,1)} %pack.9), channel_id=1, source_target_pairs={{0,16},{4,20},{8,24},{12,28},{16,0},{20,4},{24,8},{28,12},{1,17},{... | collective-permute-start | bytes 983048 | tf_op jit(solution)/shard_map/ppermute | solution.py:301
  42.4 1.2 %copy-done.2 = bf16[2,4096,64]{1,2,0:T(8,128)(2,1)S(1)} copy-done((bf16[2,4096,64]{1,2,0:T(8,128)(2,1)S(1)}, bf16[2,4096,64]{1,2,0:T(8,128)(2,1)}, u32[]{:S(2)}) %copy-start.2) | copy-done | bytes 1048600
  43.6 0.3 pack.13.refs_0_
  43.9 0.0 collective-permute-done.6.refs_2_
  43.9 0.0 collective-permute-done.5.refs_1_
  44.0 0.6 copy-done.4
  44.6 0.1 copy-done.6
  44.7 5.8 %attend_early.1 = (f32[4,64,768]{2,1,0:T(8,128)S(1)}, f32[2,8,768]{2,1,0:T(8,128)S(1)}, f32[8,128]{1,0:T(8,128)S(1)}, bf16[6,128,1280]{2,1,0:T(8,128)(2,1)S(1)},...) custom-call(s32[4]{0:T(128)S(1)} %copy-done.8, s32[1]{0:T(128)} %bitcast.me_ref, ...), custom_call_target="tpu_custom_call" | custom-call | flops 905969664 | bytes 2359296 | tf_op jit(solution)/shard_map/attend_early/pallas_call | solution.py:250
  50.5 11.0 %collective-permute-done.3.refs_1_ = bf16[128,1280]{1,0:T(8,128)(2,1)} collective-permute-done((bf16[128,1280]{1,0:T(8,128)(2,1)}, bf16[128,1280]{1,0:T(8,128)(2,1)}, u32[]{:S(2)}, u32[]{:S(2)}) %collective-permute-start.3) | collective-permute-done | bytes 327712 | tf_op jit(solution)/shard_map/ppermute | solution.py:301
  61.5 5.6 %collective-permute-done.1.refs_0_ = bf16[128,1280]{1,0:T(8,128)(2,1)} collective-permute-done((bf16[128,1280]{1,0:T(8,128)(2,1)}, bf16[128,1280]{1,0:T(8,128)(2,1)}, u32[]{:S(2)}, u32[]{:S(2)}) %collective-permute-start.1) | collective-permute-done | bytes 327712 | tf_op jit(solution)/shard_map/ppermute | solution.py:301
  67.1 3.5 %attend_late.1 = (f32[2,64,128]{2,1,0:T(8,128)S(1)}, bf16[2,64,128]{2,1,0:T(8,128)(2,1)S(1)}, bf16[2,64,128]{2,1,0:T(8,128)(2,1)S(1)}, bf16[2,64,128]{2,1,0:T(8,128)(2,1)S(1)}) custom-call(bf16[128,1280]{1,0:T(8,128)(2,1)} %collective-permute-done.1.refs_0_, bf16[128,1280]{1,0:T(8,128)(2,1)} %collective-permute-done.3.refs_1_, ...), custom_call_target="tpu_custom_call" | custom-call | flops 402653184 | bytes 3145728 | tf_op jit(solution)/shard_map/attend_late/pallas_call | solution.py:281
  70.6 0.1 collective-permute-start.7
  70.7 2.2 %collective-permute-start.8 = (bf16[2,64,128]{2,1,0:T(8,128)(2,1)S(1)}, bf16[2,64,128]{2,1,0:T(8,128)(2,1)S(1)}, u32[]{:S(2)}, u32[]{:S(2)}) collective-permute-start(bf16[2,64,128]{2,1,0:T(8,128)(2,1)S(1)} %get-tuple-element.25), channel_id=1, source_target_pairs={{0,24},{4,28},{8,16},{12,20},{16,8},{20,12},{24,0},{28,4},{1,25},{... | collective-permute-start | bytes 98312 | tf_op jit(solution)/shard_map/ppermute | solution.py:301
  72.9 1.3 %collective-permute-start.9 = (bf16[2,64,128]{2,1,0:T(8,128)(2,1)S(1)}, bf16[2,64,128]{2,1,0:T(8,128)(2,1)S(1)}, u32[]{:S(2)}, u32[]{:S(2)}) collective-permute-start(bf16[2,64,128]{2,1,0:T(8,128)(2,1)S(1)} %get-tuple-element.26), channel_id=1, source_target_pairs={{0,8},{4,12},{8,0},{12,4},{16,24},{20,28},{24,16},{28,20},{1,9},{5... | collective-permute-start | bytes 98312 | tf_op jit(solution)/shard_map/ppermute | solution.py:301
  74.2 1.3 %collective-permute-done.7 = bf16[2,64,128]{2,1,0:T(8,128)(2,1)S(1)} collective-permute-done((bf16[2,64,128]{2,1,0:T(8,128)(2,1)S(1)}, bf16[2,64,128]{2,1,0:T(8,128)(2,1)S(1)}, u32[]{:S(2)}, u32[]{:S(2)}) %collective-permute-start.7) | collective-permute-done | bytes 32800 | tf_op jit(solution)/shard_map/ppermute | solution.py:301
  75.5 1.0 %collective-permute-done.8 = bf16[2,64,128]{2,1,0:T(8,128)(2,1)S(1)} collective-permute-done((bf16[2,64,128]{2,1,0:T(8,128)(2,1)S(1)}, bf16[2,64,128]{2,1,0:T(8,128)(2,1)S(1)}, u32[]{:S(2)}, u32[]{:S(2)}) %collective-permute-start.8) | collective-permute-done | bytes 32800 | tf_op jit(solution)/shard_map/ppermute | solution.py:301
  76.5 0.4 collective-permute-done.9
  76.9 0.7 collective-permute-start.10
  77.5 3.3 %collective-permute-done.10 = f32[1,64,128]{2,1,0:T(8,128)S(1)} collective-permute-done((f32[1,64,128]{2,1,0:T(8,128)S(1)}, f32[1,64,128]{2,1,0:T(8,128)S(1)}, u32[]{:S(2)}, u32[]{:S(2)}) %collective-permute-start.10) | collective-permute-done | bytes 32800 | tf_op jit(solution)/shard_map/ppermute | solution.py:301
  80.8 0.0 collective-permute-start.11
  80.9 1.6 %collective-permute-start.12 = (f32[64,128]{1,0:T(8,128)S(1)}, f32[64,128]{1,0:T(8,128)S(1)}, u32[]{:S(2)}, u32[]{:S(2)}) collective-permute-start(f32[64,128]{1,0:T(8,128)S(1)} %fusion), channel_id=1, source_target_pairs={{0,2},{1,3},{2,0},{3,1},{4,6},{5,7},{6,4},{7,5},{8,10},{9,11},{10,... | collective-permute-start | bytes 98312 | tf_op jit(solution)/shard_map/ppermute | solution.py:301
  82.4 0.3 collective-permute-start.13
  82.7 1.8 %collective-permute-done.11 = f32[64,128]{1,0:T(8,128)S(1)} collective-permute-done((f32[64,128]{1,0:T(8,128)S(1)}, f32[64,128]{1,0:T(8,128)S(1)}, u32[]{:S(2)}, u32[]{:S(2)}) %collective-permute-start.11) | collective-permute-done | bytes 32800 | tf_op jit(solution)/shard_map/ppermute | solution.py:301
  84.5 0.4 collective-permute-done.12
  84.9 0.0 collective-permute-done.13
  84.9 0.6 add_bitcast_fusion
  (14 shorter events, 0.0 us)
Async XLA Ops:
  1.9 14.8 %collective-permute-start.2 = (bf16[128,1280]{1,0:T(8,128)(2,1)}, bf16[128,1280]{1,0:T(8,128)(2,1)S(1)}, u32[]{:S(2)}, u32[]{:S(2)}) collective-permute-start(bf16[128,1280]{1,0:T(8,128)(2,1)} %pack.10), channel_id=1, source_target_pairs={{0,28},{4,24},{8,20},{12,16},{16,12},{20,8},{24,4},{28,0},{1,29},{... | collective-permute-start | bytes 983048 | tf_op jit(solution)/shard_map/ppermute | solution.py:301
  9.9 17.7 %copy-start = (bf16[1,128,12288]{2,1,0:T(8,128)(2,1)S(1)}, bf16[1,128,12288]{2,1,0:T(8,128)(2,1)}, u32[]{:S(2)}) copy-start(bf16[1,128,12288]{2,1,0:T(8,128)(2,1)} %qkv_ref.15) | copy-start | bytes 9437188
  9.9 17.7 %collective-permute-start.4 = (bf16[128,1280]{1,0:T(8,128)(2,1)}, bf16[128,1280]{1,0:T(8,128)(2,1)S(1)}, u32[]{:S(2)}, u32[]{:S(2)}) collective-permute-start(bf16[128,1280]{1,0:T(8,128)(2,1)} %pack.12), channel_id=1, source_target_pairs={{0,12},{4,8},{8,4},{12,0},{16,28},{20,24},{24,20},{28,16},{1,13},{... | collective-permute-start | bytes 983048 | tf_op jit(solution)/shard_map/ppermute | solution.py:301
  12.1 23.8 %collective-permute-start = (bf16[128,1280]{1,0:T(8,128)(2,1)}, bf16[128,1280]{1,0:T(8,128)(2,1)S(1)}, u32[]{:S(2)}, u32[]{:S(2)}) collective-permute-start(bf16[128,1280]{1,0:T(8,128)(2,1)} %pack.8), channel_id=1, source_target_pairs={{0,24},{4,28},{8,16},{12,20},{16,8},{20,12},{24,0},{28,4},{1,25},{... | collective-permute-start | bytes 983048 | tf_op jit(solution)/shard_map/ppermute | solution.py:301
  16.8 18.0 %copy-start.3 = (bf16[128,1280]{1,0:T(8,128)(2,1)}, bf16[128,1280]{1,0:T(8,128)(2,1)S(1)}, u32[]{:S(2)}) copy-start(bf16[128,1280]{1,0:T(8,128)(2,1)S(1)} %collective-permute-done.2.refs_0_.refs_1_.refs_5_) | copy-start | bytes 983044
  27.6 1.2 %copy-start.1 = (bf16[2,4096,64]{1,2,0:T(8,128)(2,1)S(1)}, bf16[2,4096,64]{1,2,0:T(8,128)(2,1)}, u32[]{:S(2)}) copy-start(bf16[2,4096,64]{1,2,0:T(8,128)(2,1)} %param.6) | copy-start | bytes 3145732
  29.8 14.1 %collective-permute-start.6 = (bf16[128,1280]{1,0:T(8,128)(2,1)}, bf16[128,1280]{1,0:T(8,128)(2,1)}, u32[]{:S(2)}, u32[]{:S(2)}) collective-permute-start(bf16[128,1280]{1,0:T(8,128)(2,1)} %pack.15), channel_id=1, source_target_pairs={{0,8},{4,12},{8,0},{12,4},{16,24},{20,28},{24,16},{28,20},{1,9},{5... | collective-permute-start | bytes 983048 | tf_op jit(solution)/shard_map/ppermute | solution.py:301
  33.5 10.5 %collective-permute-start.5 = (bf16[128,1280]{1,0:T(8,128)(2,1)}, bf16[128,1280]{1,0:T(8,128)(2,1)}, u32[]{:S(2)}, u32[]{:S(2)}) collective-permute-start(bf16[128,1280]{1,0:T(8,128)(2,1)} %pack.14), channel_id=1, source_target_pairs={{0,4},{4,0},{8,12},{12,8},{16,20},{20,16},{24,28},{28,24},{1,5},{5... | collective-permute-start | bytes 983048 | tf_op jit(solution)/shard_map/ppermute | solution.py:301
  35.8 25.7 %collective-permute-start.3 = (bf16[128,1280]{1,0:T(8,128)(2,1)}, bf16[128,1280]{1,0:T(8,128)(2,1)}, u32[]{:S(2)}, u32[]{:S(2)}) collective-permute-start(bf16[128,1280]{1,0:T(8,128)(2,1)} %pack.11), channel_id=1, source_target_pairs={{0,20},{4,16},{8,28},{12,24},{16,4},{20,0},{24,12},{28,8},{1,21},{... | collective-permute-start | bytes 983048 | tf_op jit(solution)/shard_map/ppermute | solution.py:301
  35.9 1.0 %copy-start.5 = (bf16[128,1280]{1,0:T(8,128)(2,1)}, bf16[128,1280]{1,0:T(8,128)(2,1)S(1)}, u32[]{:S(2)}) copy-start(bf16[128,1280]{1,0:T(8,128)(2,1)S(1)} %collective-permute-done.refs_0_.refs_4_) | copy-start | bytes 983044
  36.9 7.0 %copy-start.7 = (f32[1000]{0:T(1024)S(1)}, f32[1000]{0:T(1024)}, u32[]{:S(2)}) copy-start(f32[1000]{0:T(1024)} %step_weight_ref.1) | copy-start | bytes 12004
  36.9 7.0 %copy-start.8 = (s32[4]{0:T(128)S(1)}, s32[4]{0:T(128)}, u32[]{:S(2)}) copy-start(s32[4]{0:T(128)} %frames_ref.1) | copy-start | bytes 52
  37.0 7.0 %copy-start.9 = (s32[2]{0:T(128)S(1)}, s32[2]{0:T(128)}, u32[]{:S(2)}) copy-start(s32[2]{0:T(128)} %timestep_ref.1) | copy-start | bytes 28
  37.0 30.2 %collective-permute-start.1 = (bf16[128,1280]{1,0:T(8,128)(2,1)}, bf16[128,1280]{1,0:T(8,128)(2,1)}, u32[]{:S(2)}, u32[]{:S(2)}) collective-permute-start(bf16[128,1280]{1,0:T(8,128)(2,1)} %pack.9), channel_id=1, source_target_pairs={{0,16},{4,20},{8,24},{12,28},{16,0},{20,4},{24,8},{28,12},{1,17},{... | collective-permute-start | bytes 983048 | tf_op jit(solution)/shard_map/ppermute | solution.py:301
  42.4 1.2 %copy-start.2 = (bf16[2,4096,64]{1,2,0:T(8,128)(2,1)S(1)}, bf16[2,4096,64]{1,2,0:T(8,128)(2,1)}, u32[]{:S(2)}) copy-start(bf16[2,4096,64]{1,2,0:T(8,128)(2,1)} %param.6) | copy-start | bytes 3145732
  43.6 1.0 %copy-start.4 = (bf16[128,1280]{1,0:T(8,128)(2,1)S(1)}, bf16[128,1280]{1,0:T(8,128)(2,1)}, u32[]{:S(2)}) copy-start(bf16[128,1280]{1,0:T(8,128)(2,1)} %copy-done.3) | copy-start | bytes 983044
  43.6 1.1 %copy-start.6 = (bf16[128,1280]{1,0:T(8,128)(2,1)S(1)}, bf16[128,1280]{1,0:T(8,128)(2,1)}, u32[]{:S(2)}) copy-start(bf16[128,1280]{1,0:T(8,128)(2,1)} %copy-done.5) | copy-start | bytes 983044
  70.6 4.9 %collective-permute-start.7 = (bf16[2,64,128]{2,1,0:T(8,128)(2,1)S(1)}, bf16[2,64,128]{2,1,0:T(8,128)(2,1)S(1)}, u32[]{:S(2)}, u32[]{:S(2)}) collective-permute-start(bf16[2,64,128]{2,1,0:T(8,128)(2,1)S(1)} %get-tuple-element.24), channel_id=1, source_target_pairs={{0,16},{4,20},{8,24},{12,28},{16,0},{20,4},{24,8},{28,12},{1,17},{... | collective-permute-start | bytes 98312 | tf_op jit(solution)/shard_map/ppermute | solution.py:301
  70.7 5.8 %collective-permute-start.8 = (bf16[2,64,128]{2,1,0:T(8,128)(2,1)S(1)}, bf16[2,64,128]{2,1,0:T(8,128)(2,1)S(1)}, u32[]{:S(2)}, u32[]{:S(2)}) collective-permute-start(bf16[2,64,128]{2,1,0:T(8,128)(2,1)S(1)} %get-tuple-element.25), channel_id=1, source_target_pairs={{0,24},{4,28},{8,16},{12,20},{16,8},{20,12},{24,0},{28,4},{1,25},{... | collective-permute-start | bytes 98312 | tf_op jit(solution)/shard_map/ppermute | solution.py:301
  72.9 3.9 %collective-permute-start.9 = (bf16[2,64,128]{2,1,0:T(8,128)(2,1)S(1)}, bf16[2,64,128]{2,1,0:T(8,128)(2,1)S(1)}, u32[]{:S(2)}, u32[]{:S(2)}) collective-permute-start(bf16[2,64,128]{2,1,0:T(8,128)(2,1)S(1)} %get-tuple-element.26), channel_id=1, source_target_pairs={{0,8},{4,12},{8,0},{12,4},{16,24},{20,28},{24,16},{28,20},{1,9},{5... | collective-permute-start | bytes 98312 | tf_op jit(solution)/shard_map/ppermute | solution.py:301
  76.9 4.0 %collective-permute-start.10 = (f32[1,64,128]{2,1,0:T(8,128)S(1)}, f32[1,64,128]{2,1,0:T(8,128)S(1)}, u32[]{:S(2)}, u32[]{:S(2)}) collective-permute-start(f32[1,64,128]{2,1,0:T(8,128)S(1)} %slice.9), channel_id=1, source_target_pairs={{0,4},{4,0},{8,12},{12,8},{16,20},{20,16},{24,28},{28,24},{1,5},{5... | collective-permute-start | bytes 98312 | tf_op jit(solution)/shard_map/ppermute | solution.py:301
  80.8 3.6 %collective-permute-start.11 = (f32[64,128]{1,0:T(8,128)S(1)}, f32[64,128]{1,0:T(8,128)S(1)}, u32[]{:S(2)}, u32[]{:S(2)}) collective-permute-start(f32[64,128]{1,0:T(8,128)S(1)} %fusion), channel_id=1, source_target_pairs={{0,3},{1,2},{2,1},{3,0},{4,7},{5,6},{6,5},{7,4},{8,11},{9,10},{10,... | collective-permute-start | bytes 98312 | tf_op jit(solution)/shard_map/ppermute | solution.py:301
  80.9 4.0 %collective-permute-start.12 = (f32[64,128]{1,0:T(8,128)S(1)}, f32[64,128]{1,0:T(8,128)S(1)}, u32[]{:S(2)}, u32[]{:S(2)}) collective-permute-start(f32[64,128]{1,0:T(8,128)S(1)} %fusion), channel_id=1, source_target_pairs={{0,2},{1,3},{2,0},{3,1},{4,6},{5,7},{6,4},{7,5},{8,10},{9,11},{10,... | collective-permute-start | bytes 98312 | tf_op jit(solution)/shard_map/ppermute | solution.py:301
  82.4 2.5 %collective-permute-start.13 = (f32[64,128]{1,0:T(8,128)S(1)}, f32[64,128]{1,0:T(8,128)S(1)}, u32[]{:S(2)}, u32[]{:S(2)}) collective-permute-start(f32[64,128]{1,0:T(8,128)S(1)} %fusion), channel_id=1, source_target_pairs={{0,1},{1,0},{2,3},{3,2},{4,5},{5,4},{6,7},{7,6},{8,9},{9,8},{10,11... | collective-permute-start | bytes 98312 | tf_op jit(solution)/shard_map/ppermute | solution.py:301

commit v27 on v26

--- a/solution.py
+++ b/solution.py
@@ -30,18 +30,19 @@
     return (h * lat) % HD, count * 2 * HD + (h * lat // HD) * HD
 
 
-def pack_kernel(k, me_ref, model_ref, qkv_ref, readout_ref, *refs):
+def pack_kernel(k, members, qkv_ref, readout_ref, *refs):
     out_ref, slab, readout, sems = refs[-4:]
     lat = readout.shape[0]
     count = readout.shape[1] // HD
-    target = me_ref[0] ^ k
+    target = lax.axis_index("seq") ^ k
+    model = lax.axis_index("mp") // members
 
     def columns(width):
         return pl.ds(pl.multiple_of(target * count * width, HD), count * width)
 
     copies = [
         pltpu.make_async_copy(qkv_ref.at[0, :, columns(3 * HD)], slab, sems.at[0]),
-        pltpu.make_async_copy(readout_ref.at[model_ref[0], :, columns(HD)], readout, sems.at[1]),
+        pltpu.make_async_copy(readout_ref.at[model, :, columns(HD)], readout, sems.at[1]),
     ]
     for copy in copies:
         copy.start()
@@ -56,13 +57,13 @@
         )
 
 
-def pack(me, model, qkv, readout_t, k, count, after, first=False):
+def pack(members, qkv, readout_t, k, count, after, first=False):
     rows = qkv.shape[1]
     lat = readout_t.shape[1]
     width = count * 2 * HD + -(-count * lat // HD) * HD
     return pl.pallas_call(
-        functools.partial(pack_kernel, k),
-        in_specs=[SMEM, SMEM] + [HBM] * (2 + len(after)),
+        functools.partial(pack_kernel, k, members),
+        in_specs=[HBM] * (2 + len(after)),
         out_specs=VMEM,
         out_shape=jax.ShapeDtypeStruct((rows, width), jnp.bfloat16),
         scratch_shapes=[
@@ -75,7 +76,7 @@
             flops=0, bytes_accessed=rows * width * 4, transcendentals=0
         ),
         name="pack",
-    )(me, model, qkv, readout_t, *after)
+    )(qkv, readout_t, *after)
 
 
 def mask_rows(frames_ref, me, rows, query_offsets, key_offsets):
@@ -313,17 +314,16 @@
     model_index = mp_index // sample_count
     sample = (mp_index % sample_count).reshape(1)
     sign = jnp.where(model_index == 1, 1.0, -1.0).astype(jnp.float32).reshape(1)
-    model = model_index.reshape(1)
     readout_t = jnp.swapaxes(readout, 1, 2)
 
     pieces = [None] * seq_count
     for n in range(half):
         k = seq_count - 1 - n
-        pieces[k] = swap(pack(me, model, qkv, readout_t, k, count, [pieces[k + 2]] if n > 1 else [], n < 2), "seq", k)
+        pieces[k] = swap(pack(sample_count, qkv, readout_t, k, count, [pieces[k + 2]] if n > 1 else [], n == 0), "seq", k)
     for k in range(half - 1, 0, -1):
-        after = [] if k == half - 1 else [pieces[k + 1], pieces[seq_count - 1]] if k > 1 else [pieces[half - 1]]
-        pieces[k] = swap(pack(me, model, qkv, readout_t, k, count, after, k == half - 1), "seq", k)
-    pieces[0] = pack(me, model, qkv, readout_t, 0, count, [pieces[half - 1]])
+        after = [] if k == half - 1 else [pieces[seq_count - 1], pieces[k + 1]] if k > 1 else [pieces[half - 1], pieces[seq_count - 1]]
+        pieces[k] = swap(pack(sample_count, qkv, readout_t, k, count, after), "seq", k)
+    pieces[0] = pack(sample_count, qkv, readout_t, 0, count, [pieces[half - 1]])
     late = [half, half + 1]
     early = [k for k in range(seq_count) if k not in late]
     merged = attend_early(

time: 85.8 us -> 86 us (level)
  Pallas kernels: 19.5 us -> 16.2 us
  waiting for transfers between devices: 39.3 us -> 40.6 us
  starting transfers between devices: 22.6 us -> 23.9 us
  local copies, waits for them, and re-layouts: 3.22 us -> 4.19 us
    pallas_call x8, Pallas kernels: 10.2 us -> 6.96 us  [pack(): pl.pallas_call(functools.partial(pack_kernel, k, members), in_specs=[HBM]...]
    ppermute x14, starting transfers between devices: 22.6 us -> 23.9 us  [swap(): return lax.ppermute(array, axis, [(i, i ^ offset) for i in range(size)])]
    ppermute x14, waiting for transfers between devices: 39.3 us -> 40.6 us  [swap(): return lax.ppermute(array, axis, [(i, i ^ offset) for i in range(size)])]
    unnamed x20 -> x22, local copies, waits for them, and re-layouts: 3.21 us -> 4.18 us
  transfers between devices with their start and end apart: 14 -> 14, of which waited for: 10 -> 10; matrix products, arithmetic and copies ran while one was open for 0% -> 0% of each run, Pallas kernels for 16% -> 12%
where the time goes in v27:
time: 86 us; the launch traced here: 85.7 us
  waiting for transfers between devices  40.6 us (47%)
  starting transfers between devices  23.9 us (28%)
  Pallas kernels  16.2 us (19%)
  local copies, waits for them, and re-layouts  4.19 us (5%)
    ppermute x14, waiting for transfers between devices, swap(): return lax.ppermute(array, axis, [(i, i ^ offset) for i in range(size)])  40.6 us
    ppermute x14, starting transfers between devices, swap(): return lax.ppermute(array, axis, [(i, i ^ offset) for i in range(size)])  23.9 us
    pallas_call x8, Pallas kernels, pack(): pl.pallas_call(functools.partial(pack_kernel, k, members), in_specs=[HBM]...  6.96 us
    pallas_call x1, Pallas kernels, attend_early(): pl.pallas_call(functools.partial(early_kernel, offsets, late), in_specs=[...  5.77 us
    unnamed x22, local copies, waits for them, and re-layouts  4.18 us
    pallas_call x1, Pallas kernels, attend_late(): pl.pallas_call(functools.partial(late_kernel, offsets, late), in_specs=[V...  3.47 us
  transfers between devices with their start and end apart: 14, of which 10 were waited for; matrix products, arithmetic and copies ran while one was open for 0% of the time, Pallas kernels for 12%

profile of v27, /device:TPU:0, one launch (start us, length us, event | category | flops | bytes accessed | tf_op | source)
XLA Modules:
  0.0 85.7 jit_solution(8790855636084615107)
XLA Ops:
  0.0 2.1 %pack.10 = bf16[128,1280]{1,0:T(8,128)(2,1)} custom-call(bf16[1,128,12288]{2,1,0:T(8,128)(2,1)} %qkv_ref.15, bf16[2,64,4096]{2,1,0:T(8,128)(2,1)} %bitcast.8), custom_call_target="tpu_custom_call" | custom-call | bytes 655360 | tf_op jit(solution)/shard_map/pack/pallas_call | solution.py:64
  2.1 6.0 %collective-permute-start.2 = (bf16[128,1280]{1,0:T(8,128)(2,1)}, bf16[128,1280]{1,0:T(8,128)(2,1)S(1)}, u32[]{:S(2)}, u32[]{:S(2)}) collective-permute-start(bf16[128,1280]{1,0:T(8,128)(2,1)} %pack.10), channel_id=1, source_target_pairs={{0,28},{4,24},{8,20},{12,16},{16,12},{20,8},{24,4},{28,0},{1,29},{... | collective-permute-start | bytes 983048 | tf_op jit(solution)/shard_map/ppermute | solution.py:302
  8.1 1.2 %copy-done.1 = bf16[2,4096,64]{1,2,0:T(8,128)(2,1)S(1)} copy-done((bf16[2,4096,64]{1,2,0:T(8,128)(2,1)S(1)}, bf16[2,4096,64]{1,2,0:T(8,128)(2,1)}, u32[]{:S(2)}) %copy-start.1) | copy-done | bytes 1048600
  9.4 0.3 pack.12
  9.7 0.1 collective-permute-start.4
  9.7 0.3 pack.8
  10.0 0.9 %collective-permute-start = (bf16[128,1280]{1,0:T(8,128)(2,1)S(1)}, bf16[128,1280]{1,0:T(8,128)(2,1)S(1)}, u32[]{:S(2)}, u32[]{:S(2)}) collective-permute-start(bf16[128,1280]{1,0:T(8,128)(2,1)S(1)} %pack.8), channel_id=1, source_target_pairs={{0,24},{4,28},{8,16},{12,20},{16,8},{20,12},{24,0},{28,4},{1,25},{... | collective-permute-start | bytes 983048 | tf_op jit(solution)/shard_map/ppermute | solution.py:302
  10.9 6.0 %collective-permute-done.2.refs_0_.refs_1_.refs_5_ = bf16[128,1280]{1,0:T(8,128)(2,1)S(1)} collective-permute-done((bf16[128,1280]{1,0:T(8,128)(2,1)}, bf16[128,1280]{1,0:T(8,128)(2,1)S(1)}, u32[]{:S(2)}, u32[]{:S(2)}) %collective-permute-start.2) | collective-permute-done | bytes 327712 | tf_op jit(solution)/shard_map/ppermute | solution.py:302
  17.0 10.7 %collective-permute-done.4.refs_0_.refs_1_.refs_3_ = bf16[128,1280]{1,0:T(8,128)(2,1)S(1)} collective-permute-done((bf16[128,1280]{1,0:T(8,128)(2,1)S(1)}, bf16[128,1280]{1,0:T(8,128)(2,1)S(1)}, u32[]{:S(2)}, u32[]{:S(2)}) %collective-permute-start.4) | collective-permute-done | bytes 327712 | tf_op jit(solution)/shard_map/ppermute | solution.py:302
  27.6 1.0 %pack.14 = bf16[128,1280]{1,0:T(8,128)(2,1)} custom-call(bf16[1,128,12288]{2,1,0:T(8,128)(2,1)S(1)} %copy-done, bf16[2,64,4096]{2,1,0:T(8,128)(2,1)S(1)} %bitcast.11, bf16[128,1280]{1,0:T(8,128)(2,1)S(1)} %collective-permute-done.4.refs_0_.refs_1_.refs_3_, bf16[128,1280]{1,0:T(8,128)(2,1)S(1)} %collective-permute-done.2.refs_0_.refs_1_.refs_5_), custom_call_target="tpu_custom_call" | custom-call | bytes 655360 | tf_op jit(solution)/shard_map/pack/pallas_call | solution.py:64
  28.6 0.8 collective-permute-start.5
  29.4 1.0 %pack.15 = bf16[128,1280]{1,0:T(8,128)(2,1)} custom-call(bf16[1,128,12288]{2,1,0:T(8,128)(2,1)S(1)} %copy-done, bf16[2,64,4096]{2,1,0:T(8,128)(2,1)S(1)} %bitcast.12, bf16[128,1280]{1,0:T(8,128)(2,1)S(1)} %collective-permute-done.2.refs_0_.refs_1_.refs_5_, bf16[128,1280]{1,0:T(8,128)(2,1)S(1)} %collective-permute-done.4.refs_0_.refs_1_.refs_3_), custom_call_target="tpu_custom_call" | custom-call | bytes 655360 | tf_op jit(solution)/shard_map/pack/pallas_call | solution.py:64
  30.5 3.3 %collective-permute-start.6 = (bf16[128,1280]{1,0:T(8,128)(2,1)}, bf16[128,1280]{1,0:T(8,128)(2,1)}, u32[]{:S(2)}, u32[]{:S(2)}) collective-permute-start(bf16[128,1280]{1,0:T(8,128)(2,1)} %pack.15), channel_id=1, source_target_pairs={{0,8},{4,12},{8,0},{12,4},{16,24},{20,28},{24,16},{28,20},{1,9},{5... | collective-permute-start | bytes 983048 | tf_op jit(solution)/shard_map/ppermute | solution.py:302
  33.7 1.0 %pack.11 = bf16[128,1280]{1,0:T(8,128)(2,1)} custom-call(bf16[1,128,12288]{2,1,0:T(8,128)(2,1)S(1)} %copy-done, bf16[2,64,4096]{2,1,0:T(8,128)(2,1)S(1)} %bitcast.13, bf16[128,1280]{1,0:T(8,128)(2,1)S(1)} %collective-permute-done.2.refs_0_.refs_1_.refs_5_), custom_call_target="tpu_custom_call" | custom-call | bytes 655360 | tf_op jit(solution)/shard_map/pack/pallas_call | solution.py:64
  34.7 0.1 collective-permute-start.3
  34.8 0.0 collective-permute-done.refs_0_.refs_4_
  34.8 1.0 %pack.9 = bf16[128,1280]{1,0:T(8,128)(2,1)} custom-call(bf16[1,128,12288]{2,1,0:T(8,128)(2,1)S(1)} %copy-done, bf16[2,64,4096]{2,1,0:T(8,128)(2,1)S(1)} %bitcast.14, bf16[128,1280]{1,0:T(8,128)(2,1)S(1)} %collective-permute-done.refs_0_.refs_4_), custom_call_target="tpu_custom_call" | custom-call | bytes 655360 | tf_op jit(solution)/shard_map/pack/pallas_call | solution.py:64
  35.9 0.0 copy-start.8
  35.9 0.0 copy-start.9
  35.9 0.0 copy-start.10
  35.9 6.7 %collective-permute-start.1 = (bf16[128,1280]{1,0:T(8,128)(2,1)}, bf16[128,1280]{1,0:T(8,128)(2,1)}, u32[]{:S(2)}, u32[]{:S(2)}) collective-permute-start(bf16[128,1280]{1,0:T(8,128)(2,1)} %pack.9), channel_id=1, source_target_pairs={{0,16},{4,20},{8,24},{12,28},{16,0},{20,4},{24,8},{28,12},{1,17},{... | collective-permute-start | bytes 983048 | tf_op jit(solution)/shard_map/ppermute | solution.py:302
  42.7 1.2 %copy-done.2 = bf16[2,4096,64]{1,2,0:T(8,128)(2,1)S(1)} copy-done((bf16[2,4096,64]{1,2,0:T(8,128)(2,1)S(1)}, bf16[2,4096,64]{1,2,0:T(8,128)(2,1)}, u32[]{:S(2)}) %copy-start.2) | copy-done | bytes 1048600
  43.9 1.0 %copy-done.4 = bf16[128,1280]{1,0:T(8,128)(2,1)S(1)} copy-done((bf16[128,1280]{1,0:T(8,128)(2,1)S(1)}, bf16[128,1280]{1,0:T(8,128)(2,1)}, u32[]{:S(2)}) %copy-start.4) | copy-done | bytes 327704
  44.9 0.3 pack.13.refs_0_
  45.1 0.0 collective-permute-done.5.refs_1_
  45.2 0.0 collective-permute-done.6.refs_2_
  45.2 0.0 copy-done.8
  45.2 0.6 copy-done.5
  45.8 0.1 copy-done.7
  45.9 5.8 %attend_early.1 = (f32[4,64,768]{2,1,0:T(8,128)S(1)}, f32[2,8,768]{2,1,0:T(8,128)S(1)}, f32[8,128]{1,0:T(8,128)S(1)}, bf16[6,128,1280]{2,1,0:T(8,128)(2,1)S(1)},...) custom-call(s32[4]{0:T(128)S(1)} %copy-done.9, s32[1]{0:T(128)} %bitcast.1.me_ref, ...), custom_call_target="tpu_custom_call" | custom-call | flops 905969664 | bytes 2359296 | tf_op jit(solution)/shard_map/attend_early/pallas_call | solution.py:251
  51.7 9.6 %collective-permute-done.3.refs_1_ = bf16[128,1280]{1,0:T(8,128)(2,1)} collective-permute-done((bf16[128,1280]{1,0:T(8,128)(2,1)}, bf16[128,1280]{1,0:T(8,128)(2,1)}, u32[]{:S(2)}, u32[]{:S(2)}) %collective-permute-start.3) | collective-permute-done | bytes 327712 | tf_op jit(solution)/shard_map/ppermute | solution.py:302
  61.3 6.0 %collective-permute-done.1.refs_0_ = bf16[128,1280]{1,0:T(8,128)(2,1)} collective-permute-done((bf16[128,1280]{1,0:T(8,128)(2,1)}, bf16[128,1280]{1,0:T(8,128)(2,1)}, u32[]{:S(2)}, u32[]{:S(2)}) %collective-permute-start.1) | collective-permute-done | bytes 327712 | tf_op jit(solution)/shard_map/ppermute | solution.py:302
  67.3 3.5 %attend_late.1 = (f32[2,64,128]{2,1,0:T(8,128)S(1)}, bf16[2,64,128]{2,1,0:T(8,128)(2,1)S(1)}, bf16[2,64,128]{2,1,0:T(8,128)(2,1)S(1)}, bf16[2,64,128]{2,1,0:T(8,128)(2,1)S(1)}) custom-call(bf16[128,1280]{1,0:T(8,128)(2,1)} %collective-permute-done.1.refs_0_, bf16[128,1280]{1,0:T(8,128)(2,1)} %collective-permute-done.3.refs_1_, ...), custom_call_target="tpu_custom_call" | custom-call | flops 402653184 | bytes 3145728 | tf_op jit(solution)/shard_map/attend_late/pallas_call | solution.py:282
  70.8 0.1 collective-permute-start.7
  70.8 2.3 %collective-permute-start.8 = (bf16[2,64,128]{2,1,0:T(8,128)(2,1)S(1)}, bf16[2,64,128]{2,1,0:T(8,128)(2,1)S(1)}, u32[]{:S(2)}, u32[]{:S(2)}) collective-permute-start(bf16[2,64,128]{2,1,0:T(8,128)(2,1)S(1)} %get-tuple-element.25), channel_id=1, source_target_pairs={{0,24},{4,28},{8,16},{12,20},{16,8},{20,12},{24,0},{28,4},{1,25},{... | collective-permute-start | bytes 98312 | tf_op jit(solution)/shard_map/ppermute | solution.py:302
  73.1 1.2 %collective-permute-start.9 = (bf16[2,64,128]{2,1,0:T(8,128)(2,1)S(1)}, bf16[2,64,128]{2,1,0:T(8,128)(2,1)S(1)}, u32[]{:S(2)}, u32[]{:S(2)}) collective-permute-start(bf16[2,64,128]{2,1,0:T(8,128)(2,1)S(1)} %get-tuple-element.26), channel_id=1, source_target_pairs={{0,8},{4,12},{8,0},{12,4},{16,24},{20,28},{24,16},{28,20},{1,9},{5... | collective-permute-start | bytes 98312 | tf_op jit(solution)/shard_map/ppermute | solution.py:302
  74.3 1.4 %collective-permute-done.7 = bf16[2,64,128]{2,1,0:T(8,128)(2,1)S(1)} collective-permute-done((bf16[2,64,128]{2,1,0:T(8,128)(2,1)S(1)}, bf16[2,64,128]{2,1,0:T(8,128)(2,1)S(1)}, u32[]{:S(2)}, u32[]{:S(2)}) %collective-permute-start.7) | collective-permute-done | bytes 32800 | tf_op jit(solution)/shard_map/ppermute | solution.py:302
  75.7 0.9 %collective-permute-done.8 = bf16[2,64,128]{2,1,0:T(8,128)(2,1)S(1)} collective-permute-done((bf16[2,64,128]{2,1,0:T(8,128)(2,1)S(1)}, bf16[2,64,128]{2,1,0:T(8,128)(2,1)S(1)}, u32[]{:S(2)}, u32[]{:S(2)}) %collective-permute-start.8) | collective-permute-done | bytes 32800 | tf_op jit(solution)/shard_map/ppermute | solution.py:302
  76.6 0.4 collective-permute-done.9
  77.1 0.6 collective-permute-start.10
  77.7 3.4 %collective-permute-done.10 = f32[1,64,128]{2,1,0:T(8,128)S(1)} collective-permute-done((f32[1,64,128]{2,1,0:T(8,128)S(1)}, f32[1,64,128]{2,1,0:T(8,128)S(1)}, u32[]{:S(2)}, u32[]{:S(2)}) %collective-permute-start.10) | collective-permute-done | bytes 32800 | tf_op jit(solution)/shard_map/ppermute | solution.py:302
  81.1 0.0 collective-permute-start.11
  81.1 1.6 %collective-permute-start.12 = (f32[64,128]{1,0:T(8,128)S(1)}, f32[64,128]{1,0:T(8,128)S(1)}, u32[]{:S(2)}, u32[]{:S(2)}) collective-permute-start(f32[64,128]{1,0:T(8,128)S(1)} %fusion), channel_id=1, source_target_pairs={{0,2},{1,3},{2,0},{3,1},{4,6},{5,7},{6,4},{7,5},{8,10},{9,11},{10,... | collective-permute-start | bytes 98312 | tf_op jit(solution)/shard_map/ppermute | solution.py:302
  82.7 0.3 collective-permute-start.13
  82.9 1.7 %collective-permute-done.11 = f32[64,128]{1,0:T(8,128)S(1)} collective-permute-done((f32[64,128]{1,0:T(8,128)S(1)}, f32[64,128]{1,0:T(8,128)S(1)}, u32[]{:S(2)}, u32[]{:S(2)}) %collective-permute-start.11) | collective-permute-done | bytes 32800 | tf_op jit(solution)/shard_map/ppermute | solution.py:302
  84.7 0.4 collective-permute-done.12
  85.1 0.0 collective-permute-done.13
  85.1 0.6 add_bitcast_fusion
  (16 shorter events, 0.1 us)
Async XLA Ops:
  0.0 8.1 %copy-start = (bf16[1,128,12288]{2,1,0:T(8,128)(2,1)S(1)}, bf16[1,128,12288]{2,1,0:T(8,128)(2,1)}, u32[]{:S(2)}) copy-start(bf16[1,128,12288]{2,1,0:T(8,128)(2,1)} %qkv_ref.15) | copy-start | bytes 9437188
  2.1 14.9 %collective-permute-start.2 = (bf16[128,1280]{1,0:T(8,128)(2,1)}, bf16[128,1280]{1,0:T(8,128)(2,1)S(1)}, u32[]{:S(2)}, u32[]{:S(2)}) collective-permute-start(bf16[128,1280]{1,0:T(8,128)(2,1)} %pack.10), channel_id=1, source_target_pairs={{0,28},{4,24},{8,20},{12,16},{16,12},{20,8},{24,4},{28,0},{1,29},{... | collective-permute-start | bytes 983048 | tf_op jit(solution)/shard_map/ppermute | solution.py:302
  8.1 1.2 %copy-start.1 = (bf16[2,4096,64]{1,2,0:T(8,128)(2,1)S(1)}, bf16[2,4096,64]{1,2,0:T(8,128)(2,1)}, u32[]{:S(2)}) copy-start(bf16[2,4096,64]{1,2,0:T(8,128)(2,1)} %param.6) | copy-start | bytes 3145732
  9.7 18.0 %collective-permute-start.4 = (bf16[128,1280]{1,0:T(8,128)(2,1)S(1)}, bf16[128,1280]{1,0:T(8,128)(2,1)S(1)}, u32[]{:S(2)}, u32[]{:S(2)}) collective-permute-start(bf16[128,1280]{1,0:T(8,128)(2,1)S(1)} %pack.12), channel_id=1, source_target_pairs={{0,12},{4,8},{8,4},{12,0},{16,28},{20,24},{24,20},{28,16},{1,13},{... | collective-permute-start | bytes 983048 | tf_op jit(solution)/shard_map/ppermute | solution.py:302
  10.0 24.8 %collective-permute-start = (bf16[128,1280]{1,0:T(8,128)(2,1)S(1)}, bf16[128,1280]{1,0:T(8,128)(2,1)S(1)}, u32[]{:S(2)}, u32[]{:S(2)}) collective-permute-start(bf16[128,1280]{1,0:T(8,128)(2,1)S(1)} %pack.8), channel_id=1, source_target_pairs={{0,24},{4,28},{8,16},{12,20},{16,8},{20,12},{24,0},{28,4},{1,25},{... | collective-permute-start | bytes 983048 | tf_op jit(solution)/shard_map/ppermute | solution.py:302
  27.6 2.8 %copy-start.3 = (bf16[128,1280]{1,0:T(8,128)(2,1)}, bf16[128,1280]{1,0:T(8,128)(2,1)S(1)}, u32[]{:S(2)}) copy-start(bf16[128,1280]{1,0:T(8,128)(2,1)S(1)} %collective-permute-done.4.refs_0_.refs_1_.refs_3_) | copy-start | bytes 983044
  28.6 16.5 %collective-permute-start.5 = (bf16[128,1280]{1,0:T(8,128)(2,1)}, bf16[128,1280]{1,0:T(8,128)(2,1)}, u32[]{:S(2)}, u32[]{:S(2)}) collective-permute-start(bf16[128,1280]{1,0:T(8,128)(2,1)} %pack.14), channel_id=1, source_target_pairs={{0,4},{4,0},{8,12},{12,8},{16,20},{20,16},{24,28},{28,24},{1,5},{5... | collective-permute-start | bytes 983048 | tf_op jit(solution)/shard_map/ppermute | solution.py:302
  30.5 14.7 %collective-permute-start.6 = (bf16[128,1280]{1,0:T(8,128)(2,1)}, bf16[128,1280]{1,0:T(8,128)(2,1)}, u32[]{:S(2)}, u32[]{:S(2)}) collective-permute-start(bf16[128,1280]{1,0:T(8,128)(2,1)} %pack.15), channel_id=1, source_target_pairs={{0,8},{4,12},{8,0},{12,4},{16,24},{20,28},{24,16},{28,20},{1,9},{5... | collective-permute-start | bytes 983048 | tf_op jit(solution)/shard_map/ppermute | solution.py:302
  34.7 26.5 %collective-permute-start.3 = (bf16[128,1280]{1,0:T(8,128)(2,1)}, bf16[128,1280]{1,0:T(8,128)(2,1)}, u32[]{:S(2)}, u32[]{:S(2)}) collective-permute-start(bf16[128,1280]{1,0:T(8,128)(2,1)} %pack.11), channel_id=1, source_target_pairs={{0,20},{4,16},{8,28},{12,24},{16,4},{20,0},{24,12},{28,8},{1,21},{... | collective-permute-start | bytes 983048 | tf_op jit(solution)/shard_map/ppermute | solution.py:302
  34.8 1.1 %copy-start.6 = (bf16[128,1280]{1,0:T(8,128)(2,1)}, bf16[128,1280]{1,0:T(8,128)(2,1)S(1)}, u32[]{:S(2)}) copy-start(bf16[128,1280]{1,0:T(8,128)(2,1)S(1)} %collective-permute-done.refs_0_.refs_4_) | copy-start | bytes 983044
  35.9 9.3 %copy-start.8 = (f32[1000]{0:T(1024)S(1)}, f32[1000]{0:T(1024)}, u32[]{:S(2)}) copy-start(f32[1000]{0:T(1024)} %step_weight_ref.1) | copy-start | bytes 12004
  35.9 9.3 %copy-start.9 = (s32[4]{0:T(128)S(1)}, s32[4]{0:T(128)}, u32[]{:S(2)}) copy-start(s32[4]{0:T(128)} %frames_ref.1) | copy-start | bytes 52
  35.9 9.3 %copy-start.10 = (s32[2]{0:T(128)S(1)}, s32[2]{0:T(128)}, u32[]{:S(2)}) copy-start(s32[2]{0:T(128)} %timestep_ref.1) | copy-start | bytes 28
  35.9 31.4 %collective-permute-start.1 = (bf16[128,1280]{1,0:T(8,128)(2,1)}, bf16[128,1280]{1,0:T(8,128)(2,1)}, u32[]{:S(2)}, u32[]{:S(2)}) collective-permute-start(bf16[128,1280]{1,0:T(8,128)(2,1)} %pack.9), channel_id=1, source_target_pairs={{0,16},{4,20},{8,24},{12,28},{16,0},{20,4},{24,8},{28,12},{1,17},{... | collective-permute-start | bytes 983048 | tf_op jit(solution)/shard_map/ppermute | solution.py:302
  42.7 1.2 %copy-start.2 = (bf16[2,4096,64]{1,2,0:T(8,128)(2,1)S(1)}, bf16[2,4096,64]{1,2,0:T(8,128)(2,1)}, u32[]{:S(2)}) copy-start(bf16[2,4096,64]{1,2,0:T(8,128)(2,1)} %param.6) | copy-start | bytes 3145732
  43.9 1.0 %copy-start.4 = (bf16[128,1280]{1,0:T(8,128)(2,1)S(1)}, bf16[128,1280]{1,0:T(8,128)(2,1)}, u32[]{:S(2)}) copy-start(bf16[128,1280]{1,0:T(8,128)(2,1)} %copy-done.3) | copy-start | bytes 983044
  44.9 1.0 %copy-start.5 = (bf16[128,1280]{1,0:T(8,128)(2,1)S(1)}, bf16[128,1280]{1,0:T(8,128)(2,1)}, u32[]{:S(2)}) copy-start(bf16[128,1280]{1,0:T(8,128)(2,1)} %copy-done.3) | copy-start | bytes 983044
  44.9 1.1 %copy-start.7 = (bf16[128,1280]{1,0:T(8,128)(2,1)S(1)}, bf16[128,1280]{1,0:T(8,128)(2,1)}, u32[]{:S(2)}) copy-start(bf16[128,1280]{1,0:T(8,128)(2,1)} %copy-done.6) | copy-start | bytes 983044
  70.8 5.0 %collective-permute-start.7 = (bf16[2,64,128]{2,1,0:T(8,128)(2,1)S(1)}, bf16[2,64,128]{2,1,0:T(8,128)(2,1)S(1)}, u32[]{:S(2)}, u32[]{:S(2)}) collective-permute-start(bf16[2,64,128]{2,1,0:T(8,128)(2,1)S(1)} %get-tuple-element.24), channel_id=1, source_target_pairs={{0,16},{4,20},{8,24},{12,28},{16,0},{20,4},{24,8},{28,12},{1,17},{... | collective-permute-start | bytes 98312 | tf_op jit(solution)/shard_map/ppermute | solution.py:302
  70.8 5.8 %collective-permute-start.8 = (bf16[2,64,128]{2,1,0:T(8,128)(2,1)S(1)}, bf16[2,64,128]{2,1,0:T(8,128)(2,1)S(1)}, u32[]{:S(2)}, u32[]{:S(2)}) collective-permute-start(bf16[2,64,128]{2,1,0:T(8,128)(2,1)S(1)} %get-tuple-element.25), channel_id=1, source_target_pairs={{0,24},{4,28},{8,16},{12,20},{16,8},{20,12},{24,0},{28,4},{1,25},{... | collective-permute-start | bytes 98312 | tf_op jit(solution)/shard_map/ppermute | solution.py:302
  73.1 3.9 %collective-permute-start.9 = (bf16[2,64,128]{2,1,0:T(8,128)(2,1)S(1)}, bf16[2,64,128]{2,1,0:T(8,128)(2,1)S(1)}, u32[]{:S(2)}, u32[]{:S(2)}) collective-permute-start(bf16[2,64,128]{2,1,0:T(8,128)(2,1)S(1)} %get-tuple-element.26), channel_id=1, source_target_pairs={{0,8},{4,12},{8,0},{12,4},{16,24},{20,28},{24,16},{28,20},{1,9},{5... | collective-permute-start | bytes 98312 | tf_op jit(solution)/shard_map/ppermute | solution.py:302
  77.1 4.0 %collective-permute-start.10 = (f32[1,64,128]{2,1,0:T(8,128)S(1)}, f32[1,64,128]{2,1,0:T(8,128)S(1)}, u32[]{:S(2)}, u32[]{:S(2)}) collective-permute-start(f32[1,64,128]{2,1,0:T(8,128)S(1)} %slice.9), channel_id=1, source_target_pairs={{0,4},{4,0},{8,12},{12,8},{16,20},{20,16},{24,28},{28,24},{1,5},{5... | collective-permute-start | bytes 98312 | tf_op jit(solution)/shard_map/ppermute | solution.py:302
  81.1 3.6 %collective-permute-start.11 = (f32[64,128]{1,0:T(8,128)S(1)}, f32[64,128]{1,0:T(8,128)S(1)}, u32[]{:S(2)}, u32[]{:S(2)}) collective-permute-start(f32[64,128]{1,0:T(8,128)S(1)} %fusion), channel_id=1, source_target_pairs={{0,3},{1,2},{2,1},{3,0},{4,7},{5,6},{6,5},{7,4},{8,11},{9,10},{10,... | collective-permute-start | bytes 98312 | tf_op jit(solution)/shard_map/ppermute | solution.py:302
  81.1 4.0 %collective-permute-start.12 = (f32[64,128]{1,0:T(8,128)S(1)}, f32[64,128]{1,0:T(8,128)S(1)}, u32[]{:S(2)}, u32[]{:S(2)}) collective-permute-start(f32[64,128]{1,0:T(8,128)S(1)} %fusion), channel_id=1, source_target_pairs={{0,2},{1,3},{2,0},{3,1},{4,6},{5,7},{6,4},{7,5},{8,10},{9,11},{10,... | collective-permute-start | bytes 98312 | tf_op jit(solution)/shard_map/ppermute | solution.py:302
  82.7 2.4 %collective-permute-start.13 = (f32[64,128]{1,0:T(8,128)S(1)}, f32[64,128]{1,0:T(8,128)S(1)}, u32[]{:S(2)}, u32[]{:S(2)}) collective-permute-start(f32[64,128]{1,0:T(8,128)S(1)} %fusion), channel_id=1, source_target_pairs={{0,1},{1,0},{2,3},{3,2},{4,5},{5,4},{6,7},{7,6},{8,9},{9,8},{10,11... | collective-permute-start | bytes 98312 | tf_op jit(solution)/shard_map/ppermute | solution.py:302

commit v28 on v25

--- a/solution.py
+++ b/solution.py
@@ -321,7 +321,7 @@
         k = seq_count - 1 - n
         pieces[k] = swap(pack(me, model, qkv, readout_t, k, count, [pieces[k + 2]] if n > 1 else [], n == 0), "seq", k)
     for k in range(half - 1, 0, -1):
-        after = [] if k == half - 1 else [pieces[k + 1], pieces[seq_count - 1]] if k > 1 else [pieces[half - 1]]
+        after = [] if k == half - 1 else [pieces[k + 1]] if k > 1 else [pieces[seq_count - 1]]
         pieces[k] = swap(pack(me, model, qkv, readout_t, k, count, after), "seq", k)
     pieces[0] = pack(me, model, qkv, readout_t, 0, count, [pieces[half - 1]])
     late = [half, half + 1]

time: 86 us -> 86 us (level)
  waiting for transfers between devices: 41.5 us -> 39.5 us
  starting transfers between devices: 23.9 us -> 25 us
  local copies, waits for them, and re-layouts: 3.22 us -> 4.19 us
    ppermute x14, waiting for transfers between devices: 41.5 us -> 39.5 us  [swap(): return lax.ppermute(array, axis, [(i, i ^ offset) for i in range(size)])]
    ppermute x14, starting transfers between devices: 23.9 us -> 25 us  [swap(): return lax.ppermute(array, axis, [(i, i ^ offset) for i in range(size)])]
    unnamed x20 -> x22, local copies, waits for them, and re-layouts: 3.21 us -> 4.18 us
  transfers between devices with their start and end apart: 14 -> 14, of which waited for: 10 -> 11; matrix products, arithmetic and copies ran while one was open for 0% -> 0% of each run, Pallas kernels for 12% -> 12%
where the time goes in v28:
time: 86 us; the launch traced here: 85.7 us
  waiting for transfers between devices  39.5 us (46%)
  starting transfers between devices  25 us (29%)
  Pallas kernels  16.2 us (19%)
  local copies, waits for them, and re-layouts  4.19 us (5%)
    ppermute x14, waiting for transfers between devices, swap(): return lax.ppermute(array, axis, [(i, i ^ offset) for i in range(size)])  39.5 us
    ppermute x14, starting transfers between devices, swap(): return lax.ppermute(array, axis, [(i, i ^ offset) for i in range(size)])  25 us
    pallas_call x8, Pallas kernels, pack(): pl.pallas_call(functools.partial(pack_kernel, k), in_specs=[SMEM, SMEM] +...  6.91 us
    pallas_call x1, Pallas kernels, attend_early(): pl.pallas_call(functools.partial(early_kernel, offsets, late), in_specs=[...  5.77 us
    unnamed x22, local copies, waits for them, and re-layouts  4.18 us
    pallas_call x1, Pallas kernels, attend_late(): pl.pallas_call(functools.partial(late_kernel, offsets, late), in_specs=[V...  3.47 us
  transfers between devices with their start and end apart: 14, of which 11 were waited for; matrix products, arithmetic and copies ran while one was open for 0% of the time, Pallas kernels for 12%

profile of v28, /device:TPU:0, one launch (start us, length us, event | category | flops | bytes accessed | tf_op | source)
XLA Modules:
  0.0 85.7 jit_solution(14852427705316676936)
XLA Ops:
  0.0 2.1 %pack.10 = bf16[128,1280]{1,0:T(8,128)(2,1)} custom-call(s32[1]{0:T(128)} %bitcast.me_ref, s32[1]{0:T(128)} %bitcast.1.model_ref, bf16[1,128,12288]{2,1,0:T(8,128)(2,1)} %qkv_ref.15, bf16[2,64,4096]{2,1,0:T(8,128)(2,1)} %bitcast.9), custom_call_target="tpu_custom_call" | custom-call | bytes 655360 | tf_op jit(solution)/shard_map/pack/pallas_call | solution.py:63
  2.1 6.0 %collective-permute-start.2 = (bf16[128,1280]{1,0:T(8,128)(2,1)}, bf16[128,1280]{1,0:T(8,128)(2,1)S(1)}, u32[]{:S(2)}, u32[]{:S(2)}) collective-permute-start(bf16[128,1280]{1,0:T(8,128)(2,1)} %pack.10), channel_id=1, source_target_pairs={{0,28},{4,24},{8,20},{12,16},{16,12},{20,8},{24,4},{28,0},{1,29},{... | collective-permute-start | bytes 983048 | tf_op jit(solution)/shard_map/ppermute | solution.py:301
  8.1 1.2 %copy-done.1 = bf16[2,4096,64]{1,2,0:T(8,128)(2,1)S(1)} copy-done((bf16[2,4096,64]{1,2,0:T(8,128)(2,1)S(1)}, bf16[2,4096,64]{1,2,0:T(8,128)(2,1)}, u32[]{:S(2)}) %copy-start.1) | copy-done | bytes 1048600
  9.4 0.3 pack.12
  9.7 0.1 collective-permute-start.4
  9.7 0.3 pack.8
  10.0 0.9 %collective-permute-start = (bf16[128,1280]{1,0:T(8,128)(2,1)S(1)}, bf16[128,1280]{1,0:T(8,128)(2,1)S(1)}, u32[]{:S(2)}, u32[]{:S(2)}) collective-permute-start(bf16[128,1280]{1,0:T(8,128)(2,1)S(1)} %pack.8), channel_id=1, source_target_pairs={{0,24},{4,28},{8,16},{12,20},{16,8},{20,12},{24,0},{28,4},{1,25},{... | collective-permute-start | bytes 983048 | tf_op jit(solution)/shard_map/ppermute | solution.py:301
  10.9 6.0 %collective-permute-done.2.refs_0_.refs_5_ = bf16[128,1280]{1,0:T(8,128)(2,1)S(1)} collective-permute-done((bf16[128,1280]{1,0:T(8,128)(2,1)}, bf16[128,1280]{1,0:T(8,128)(2,1)S(1)}, u32[]{:S(2)}, u32[]{:S(2)}) %collective-permute-start.2) | collective-permute-done | bytes 327712 | tf_op jit(solution)/shard_map/ppermute | solution.py:301
  17.0 1.0 %pack.14 = bf16[128,1280]{1,0:T(8,128)(2,1)} custom-call(s32[1]{0:T(128)} %bitcast.me_ref, s32[1]{0:T(128)} %bitcast.1.model_ref, bf16[1,128,12288]{2,1,0:T(8,128)(2,1)S(1)} %copy-done, bf16[2,64,4096]{2,1,0:T(8,128)(2,1)S(1)} %bitcast.12, bf16[128,1280]{1,0:T(8,128)(2,1)S(1)} %collective-permute-done.2.refs_0_.refs_5_), custom_call_target="tpu_custom_call" | custom-call | bytes 655360 | tf_op jit(solution)/shard_map/pack/pallas_call | solution.py:63
  18.0 1.8 %collective-permute-start.5 = (bf16[128,1280]{1,0:T(8,128)(2,1)}, bf16[128,1280]{1,0:T(8,128)(2,1)}, u32[]{:S(2)}, u32[]{:S(2)}) collective-permute-start(bf16[128,1280]{1,0:T(8,128)(2,1)} %pack.14), channel_id=1, source_target_pairs={{0,4},{4,0},{8,12},{12,8},{16,20},{20,16},{24,28},{28,24},{1,5},{5... | collective-permute-start | bytes 983048 | tf_op jit(solution)/shard_map/ppermute | solution.py:301
  19.7 7.9 %collective-permute-done.4.refs_0_.refs_3_ = bf16[128,1280]{1,0:T(8,128)(2,1)S(1)} collective-permute-done((bf16[128,1280]{1,0:T(8,128)(2,1)S(1)}, bf16[128,1280]{1,0:T(8,128)(2,1)S(1)}, u32[]{:S(2)}, u32[]{:S(2)}) %collective-permute-start.4) | collective-permute-done | bytes 327712 | tf_op jit(solution)/shard_map/ppermute | solution.py:301
  27.6 1.0 %pack.15 = bf16[128,1280]{1,0:T(8,128)(2,1)} custom-call(s32[1]{0:T(128)} %bitcast.me_ref, s32[1]{0:T(128)} %bitcast.1.model_ref, bf16[1,128,12288]{2,1,0:T(8,128)(2,1)S(1)} %copy-done, bf16[2,64,4096]{2,1,0:T(8,128)(2,1)S(1)} %bitcast.13, bf16[128,1280]{1,0:T(8,128)(2,1)S(1)} %collective-permute-done.4.refs_0_.refs_3_), custom_call_target="tpu_custom_call" | custom-call | bytes 655360 | tf_op jit(solution)/shard_map/pack/pallas_call | solution.py:63
  28.7 2.8 %collective-permute-start.6 = (bf16[128,1280]{1,0:T(8,128)(2,1)}, bf16[128,1280]{1,0:T(8,128)(2,1)}, u32[]{:S(2)}, u32[]{:S(2)}) collective-permute-start(bf16[128,1280]{1,0:T(8,128)(2,1)} %pack.15), channel_id=1, source_target_pairs={{0,8},{4,12},{8,0},{12,4},{16,24},{20,28},{24,16},{28,20},{1,9},{5... | collective-permute-start | bytes 983048 | tf_op jit(solution)/shard_map/ppermute | solution.py:301
  31.4 1.0 %pack.11 = bf16[128,1280]{1,0:T(8,128)(2,1)} custom-call(s32[1]{0:T(128)} %bitcast.me_ref, s32[1]{0:T(128)} %bitcast.1.model_ref, bf16[1,128,12288]{2,1,0:T(8,128)(2,1)S(1)} %copy-done, bf16[2,64,4096]{2,1,0:T(8,128)(2,1)S(1)} %bitcast.14, bf16[128,1280]{1,0:T(8,128)(2,1)S(1)} %collective-permute-done.2.refs_0_.refs_5_), custom_call_target="tpu_custom_call" | custom-call | bytes 655360 | tf_op jit(solution)/shard_map/pack/pallas_call | solution.py:63
  32.4 0.6 collective-permute-start.3
  33.0 1.7 %collective-permute-done.refs_0_.refs_4_ = bf16[128,1280]{1,0:T(8,128)(2,1)S(1)} collective-permute-done((bf16[128,1280]{1,0:T(8,128)(2,1)S(1)}, bf16[128,1280]{1,0:T(8,128)(2,1)S(1)}, u32[]{:S(2)}, u32[]{:S(2)}) %collective-permute-start) | collective-permute-done | bytes 327712 | tf_op jit(solution)/shard_map/ppermute | solution.py:301
  34.7 1.0 %pack.9 = bf16[128,1280]{1,0:T(8,128)(2,1)} custom-call(s32[1]{0:T(128)} %bitcast.me_ref, s32[1]{0:T(128)} %bitcast.1.model_ref, bf16[1,128,12288]{2,1,0:T(8,128)(2,1)S(1)} %copy-done, bf16[2,64,4096]{2,1,0:T(8,128)(2,1)S(1)} %bitcast.15, bf16[128,1280]{1,0:T(8,128)(2,1)S(1)} %collective-permute-done.refs_0_.refs_4_), custom_call_target="tpu_custom_call" | custom-call | bytes 655360 | tf_op jit(solution)/shard_map/pack/pallas_call | solution.py:63
  35.7 0.0 copy-start.8
  35.7 0.0 copy-start.9
  35.8 0.0 copy-start.10
  35.8 6.9 %collective-permute-start.1 = (bf16[128,1280]{1,0:T(8,128)(2,1)}, bf16[128,1280]{1,0:T(8,128)(2,1)}, u32[]{:S(2)}, u32[]{:S(2)}) collective-permute-start(bf16[128,1280]{1,0:T(8,128)(2,1)} %pack.9), channel_id=1, source_target_pairs={{0,16},{4,20},{8,24},{12,28},{16,0},{20,4},{24,8},{28,12},{1,17},{... | collective-permute-start | bytes 983048 | tf_op jit(solution)/shard_map/ppermute | solution.py:301
  42.6 1.2 %copy-done.2 = bf16[2,4096,64]{1,2,0:T(8,128)(2,1)S(1)} copy-done((bf16[2,4096,64]{1,2,0:T(8,128)(2,1)S(1)}, bf16[2,4096,64]{1,2,0:T(8,128)(2,1)}, u32[]{:S(2)}) %copy-start.2) | copy-done | bytes 1048600
  43.9 1.0 %copy-done.4 = bf16[128,1280]{1,0:T(8,128)(2,1)S(1)} copy-done((bf16[128,1280]{1,0:T(8,128)(2,1)S(1)}, bf16[128,1280]{1,0:T(8,128)(2,1)}, u32[]{:S(2)}) %copy-start.4) | copy-done | bytes 327704
  44.8 0.3 pack.13.refs_0_
  45.1 0.0 collective-permute-done.5.refs_1_
  45.1 0.0 collective-permute-done.6.refs_2_
  45.1 0.0 copy-done.8
  45.2 0.6 copy-done.5
  45.8 0.1 copy-done.7
  45.9 5.8 %attend_early.1 = (f32[4,64,768]{2,1,0:T(8,128)S(1)}, f32[2,8,768]{2,1,0:T(8,128)S(1)}, f32[8,128]{1,0:T(8,128)S(1)}, bf16[6,128,1280]{2,1,0:T(8,128)(2,1)S(1)},...) custom-call(s32[4]{0:T(128)S(1)} %copy-done.9, s32[1]{0:T(128)} %bitcast.me_ref, ...), custom_call_target="tpu_custom_call" | custom-call | flops 905969664 | bytes 2359296 | tf_op jit(solution)/shard_map/attend_early/pallas_call | solution.py:250
  51.7 9.6 %collective-permute-done.3.refs_1_ = bf16[128,1280]{1,0:T(8,128)(2,1)} collective-permute-done((bf16[128,1280]{1,0:T(8,128)(2,1)}, bf16[128,1280]{1,0:T(8,128)(2,1)}, u32[]{:S(2)}, u32[]{:S(2)}) %collective-permute-start.3) | collective-permute-done | bytes 327712 | tf_op jit(solution)/shard_map/ppermute | solution.py:301
  61.3 6.0 %collective-permute-done.1.refs_0_ = bf16[128,1280]{1,0:T(8,128)(2,1)} collective-permute-done((bf16[128,1280]{1,0:T(8,128)(2,1)}, bf16[128,1280]{1,0:T(8,128)(2,1)}, u32[]{:S(2)}, u32[]{:S(2)}) %collective-permute-start.1) | collective-permute-done | bytes 327712 | tf_op jit(solution)/shard_map/ppermute | solution.py:301
  67.3 3.5 %attend_late.1 = (f32[2,64,128]{2,1,0:T(8,128)S(1)}, bf16[2,64,128]{2,1,0:T(8,128)(2,1)S(1)}, bf16[2,64,128]{2,1,0:T(8,128)(2,1)S(1)}, bf16[2,64,128]{2,1,0:T(8,128)(2,1)S(1)}) custom-call(bf16[128,1280]{1,0:T(8,128)(2,1)} %collective-permute-done.1.refs_0_, bf16[128,1280]{1,0:T(8,128)(2,1)} %collective-permute-done.3.refs_1_, ...), custom_call_target="tpu_custom_call" | custom-call | flops 402653184 | bytes 3145728 | tf_op jit(solution)/shard_map/attend_late/pallas_call | solution.py:281
  70.8 0.1 collective-permute-start.7
  70.8 2.3 %collective-permute-start.8 = (bf16[2,64,128]{2,1,0:T(8,128)(2,1)S(1)}, bf16[2,64,128]{2,1,0:T(8,128)(2,1)S(1)}, u32[]{:S(2)}, u32[]{:S(2)}) collective-permute-start(bf16[2,64,128]{2,1,0:T(8,128)(2,1)S(1)} %get-tuple-element.25), channel_id=1, source_target_pairs={{0,24},{4,28},{8,16},{12,20},{16,8},{20,12},{24,0},{28,4},{1,25},{... | collective-permute-start | bytes 98312 | tf_op jit(solution)/shard_map/ppermute | solution.py:301
  73.1 1.2 %collective-permute-start.9 = (bf16[2,64,128]{2,1,0:T(8,128)(2,1)S(1)}, bf16[2,64,128]{2,1,0:T(8,128)(2,1)S(1)}, u32[]{:S(2)}, u32[]{:S(2)}) collective-permute-start(bf16[2,64,128]{2,1,0:T(8,128)(2,1)S(1)} %get-tuple-element.26), channel_id=1, source_target_pairs={{0,8},{4,12},{8,0},{12,4},{16,24},{20,28},{24,16},{28,20},{1,9},{5... | collective-permute-start | bytes 98312 | tf_op jit(solution)/shard_map/ppermute | solution.py:301
  74.3 1.4 %collective-permute-done.7 = bf16[2,64,128]{2,1,0:T(8,128)(2,1)S(1)} collective-permute-done((bf16[2,64,128]{2,1,0:T(8,128)(2,1)S(1)}, bf16[2,64,128]{2,1,0:T(8,128)(2,1)S(1)}, u32[]{:S(2)}, u32[]{:S(2)}) %collective-permute-start.7) | collective-permute-done | bytes 32800 | tf_op jit(solution)/shard_map/ppermute | solution.py:301
  75.7 0.9 %collective-permute-done.8 = bf16[2,64,128]{2,1,0:T(8,128)(2,1)S(1)} collective-permute-done((bf16[2,64,128]{2,1,0:T(8,128)(2,1)S(1)}, bf16[2,64,128]{2,1,0:T(8,128)(2,1)S(1)}, u32[]{:S(2)}, u32[]{:S(2)}) %collective-permute-start.8) | collective-permute-done | bytes 32800 | tf_op jit(solution)/shard_map/ppermute | solution.py:301
  76.6 0.4 collective-permute-done.9
  77.1 0.6 collective-permute-start.10
  77.7 3.4 %collective-permute-done.10 = f32[1,64,128]{2,1,0:T(8,128)S(1)} collective-permute-done((f32[1,64,128]{2,1,0:T(8,128)S(1)}, f32[1,64,128]{2,1,0:T(8,128)S(1)}, u32[]{:S(2)}, u32[]{:S(2)}) %collective-permute-start.10) | collective-permute-done | bytes 32800 | tf_op jit(solution)/shard_map/ppermute | solution.py:301
  81.1 0.0 collective-permute-start.11
  81.1 1.6 %collective-permute-start.12 = (f32[64,128]{1,0:T(8,128)S(1)}, f32[64,128]{1,0:T(8,128)S(1)}, u32[]{:S(2)}, u32[]{:S(2)}) collective-permute-start(f32[64,128]{1,0:T(8,128)S(1)} %fusion), channel_id=1, source_target_pairs={{0,2},{1,3},{2,0},{3,1},{4,6},{5,7},{6,4},{7,5},{8,10},{9,11},{10,... | collective-permute-start | bytes 98312 | tf_op jit(solution)/shard_map/ppermute | solution.py:301
  82.7 0.3 collective-permute-start.13
  82.9 1.7 %collective-permute-done.11 = f32[64,128]{1,0:T(8,128)S(1)} collective-permute-done((f32[64,128]{1,0:T(8,128)S(1)}, f32[64,128]{1,0:T(8,128)S(1)}, u32[]{:S(2)}, u32[]{:S(2)}) %collective-permute-start.11) | collective-permute-done | bytes 32800 | tf_op jit(solution)/shard_map/ppermute | solution.py:301
  84.7 0.4 collective-permute-done.12
  85.1 0.0 collective-permute-done.13
  85.1 0.6 add_bitcast_fusion
  (16 shorter events, 0.1 us)
Async XLA Ops:
  0.0 8.1 %copy-start = (bf16[1,128,12288]{2,1,0:T(8,128)(2,1)S(1)}, bf16[1,128,12288]{2,1,0:T(8,128)(2,1)}, u32[]{:S(2)}) copy-start(bf16[1,128,12288]{2,1,0:T(8,128)(2,1)} %qkv_ref.15) | copy-start | bytes 9437188
  2.1 14.9 %collective-permute-start.2 = (bf16[128,1280]{1,0:T(8,128)(2,1)}, bf16[128,1280]{1,0:T(8,128)(2,1)S(1)}, u32[]{:S(2)}, u32[]{:S(2)}) collective-permute-start(bf16[128,1280]{1,0:T(8,128)(2,1)} %pack.10), channel_id=1, source_target_pairs={{0,28},{4,24},{8,20},{12,16},{16,12},{20,8},{24,4},{28,0},{1,29},{... | collective-permute-start | bytes 983048 | tf_op jit(solution)/shard_map/ppermute | solution.py:301
  8.1 1.2 %copy-start.1 = (bf16[2,4096,64]{1,2,0:T(8,128)(2,1)S(1)}, bf16[2,4096,64]{1,2,0:T(8,128)(2,1)}, u32[]{:S(2)}) copy-start(bf16[2,4096,64]{1,2,0:T(8,128)(2,1)} %param.6) | copy-start | bytes 3145732
  9.7 18.0 %collective-permute-start.4 = (bf16[128,1280]{1,0:T(8,128)(2,1)S(1)}, bf16[128,1280]{1,0:T(8,128)(2,1)S(1)}, u32[]{:S(2)}, u32[]{:S(2)}) collective-permute-start(bf16[128,1280]{1,0:T(8,128)(2,1)S(1)} %pack.12), channel_id=1, source_target_pairs={{0,12},{4,8},{8,4},{12,0},{16,28},{20,24},{24,20},{28,16},{1,13},{... | collective-permute-start | bytes 983048 | tf_op jit(solution)/shard_map/ppermute | solution.py:301
  10.0 24.7 %collective-permute-start = (bf16[128,1280]{1,0:T(8,128)(2,1)S(1)}, bf16[128,1280]{1,0:T(8,128)(2,1)S(1)}, u32[]{:S(2)}, u32[]{:S(2)}) collective-permute-start(bf16[128,1280]{1,0:T(8,128)(2,1)S(1)} %pack.8), channel_id=1, source_target_pairs={{0,24},{4,28},{8,16},{12,20},{16,8},{20,12},{24,0},{28,4},{1,25},{... | collective-permute-start | bytes 983048 | tf_op jit(solution)/shard_map/ppermute | solution.py:301
  18.0 27.2 %collective-permute-start.5 = (bf16[128,1280]{1,0:T(8,128)(2,1)}, bf16[128,1280]{1,0:T(8,128)(2,1)}, u32[]{:S(2)}, u32[]{:S(2)}) collective-permute-start(bf16[128,1280]{1,0:T(8,128)(2,1)} %pack.14), channel_id=1, source_target_pairs={{0,4},{4,0},{8,12},{12,8},{16,20},{20,16},{24,28},{28,24},{1,5},{5... | collective-permute-start | bytes 983048 | tf_op jit(solution)/shard_map/ppermute | solution.py:301
  27.6 4.8 %copy-start.3 = (bf16[128,1280]{1,0:T(8,128)(2,1)}, bf16[128,1280]{1,0:T(8,128)(2,1)S(1)}, u32[]{:S(2)}) copy-start(bf16[128,1280]{1,0:T(8,128)(2,1)S(1)} %collective-permute-done.4.refs_0_.refs_3_) | copy-start | bytes 983044
  28.7 16.5 %collective-permute-start.6 = (bf16[128,1280]{1,0:T(8,128)(2,1)}, bf16[128,1280]{1,0:T(8,128)(2,1)}, u32[]{:S(2)}, u32[]{:S(2)}) collective-permute-start(bf16[128,1280]{1,0:T(8,128)(2,1)} %pack.15), channel_id=1, source_target_pairs={{0,8},{4,12},{8,0},{12,4},{16,24},{20,28},{24,16},{28,20},{1,9},{5... | collective-permute-start | bytes 983048 | tf_op jit(solution)/shard_map/ppermute | solution.py:301
  32.4 28.8 %collective-permute-start.3 = (bf16[128,1280]{1,0:T(8,128)(2,1)}, bf16[128,1280]{1,0:T(8,128)(2,1)}, u32[]{:S(2)}, u32[]{:S(2)}) collective-permute-start(bf16[128,1280]{1,0:T(8,128)(2,1)} %pack.11), channel_id=1, source_target_pairs={{0,20},{4,16},{8,28},{12,24},{16,4},{20,0},{24,12},{28,8},{1,21},{... | collective-permute-start | bytes 983048 | tf_op jit(solution)/shard_map/ppermute | solution.py:301
  34.7 1.0 %copy-start.6 = (bf16[128,1280]{1,0:T(8,128)(2,1)}, bf16[128,1280]{1,0:T(8,128)(2,1)S(1)}, u32[]{:S(2)}) copy-start(bf16[128,1280]{1,0:T(8,128)(2,1)S(1)} %collective-permute-done.refs_0_.refs_4_) | copy-start | bytes 983044
  35.7 9.4 %copy-start.8 = (f32[1000]{0:T(1024)S(1)}, f32[1000]{0:T(1024)}, u32[]{:S(2)}) copy-start(f32[1000]{0:T(1024)} %step_weight_ref.1) | copy-start | bytes 12004
  35.7 9.4 %copy-start.9 = (s32[4]{0:T(128)S(1)}, s32[4]{0:T(128)}, u32[]{:S(2)}) copy-start(s32[4]{0:T(128)} %frames_ref.1) | copy-start | bytes 52
  35.8 9.4 %copy-start.10 = (s32[2]{0:T(128)S(1)}, s32[2]{0:T(128)}, u32[]{:S(2)}) copy-start(s32[2]{0:T(128)} %timestep_ref.1) | copy-start | bytes 28
  35.8 31.5 %collective-permute-start.1 = (bf16[128,1280]{1,0:T(8,128)(2,1)}, bf16[128,1280]{1,0:T(8,128)(2,1)}, u32[]{:S(2)}, u32[]{:S(2)}) collective-permute-start(bf16[128,1280]{1,0:T(8,128)(2,1)} %pack.9), channel_id=1, source_target_pairs={{0,16},{4,20},{8,24},{12,28},{16,0},{20,4},{24,8},{28,12},{1,17},{... | collective-permute-start | bytes 983048 | tf_op jit(solution)/shard_map/ppermute | solution.py:301
  42.6 1.2 %copy-start.2 = (bf16[2,4096,64]{1,2,0:T(8,128)(2,1)S(1)}, bf16[2,4096,64]{1,2,0:T(8,128)(2,1)}, u32[]{:S(2)}) copy-start(bf16[2,4096,64]{1,2,0:T(8,128)(2,1)} %param.6) | copy-start | bytes 3145732
  43.9 1.0 %copy-start.4 = (bf16[128,1280]{1,0:T(8,128)(2,1)S(1)}, bf16[128,1280]{1,0:T(8,128)(2,1)}, u32[]{:S(2)}) copy-start(bf16[128,1280]{1,0:T(8,128)(2,1)} %copy-done.3) | copy-start | bytes 983044
  44.8 1.0 %copy-start.5 = (bf16[128,1280]{1,0:T(8,128)(2,1)S(1)}, bf16[128,1280]{1,0:T(8,128)(2,1)}, u32[]{:S(2)}) copy-start(bf16[128,1280]{1,0:T(8,128)(2,1)} %copy-done.3) | copy-start | bytes 983044
  44.8 1.1 %copy-start.7 = (bf16[128,1280]{1,0:T(8,128)(2,1)S(1)}, bf16[128,1280]{1,0:T(8,128)(2,1)}, u32[]{:S(2)}) copy-start(bf16[128,1280]{1,0:T(8,128)(2,1)} %copy-done.6) | copy-start | bytes 983044
  70.8 5.0 %collective-permute-start.7 = (bf16[2,64,128]{2,1,0:T(8,128)(2,1)S(1)}, bf16[2,64,128]{2,1,0:T(8,128)(2,1)S(1)}, u32[]{:S(2)}, u32[]{:S(2)}) collective-permute-start(bf16[2,64,128]{2,1,0:T(8,128)(2,1)S(1)} %get-tuple-element.24), channel_id=1, source_target_pairs={{0,16},{4,20},{8,24},{12,28},{16,0},{20,4},{24,8},{28,12},{1,17},{... | collective-permute-start | bytes 98312 | tf_op jit(solution)/shard_map/ppermute | solution.py:301
  70.8 5.8 %collective-permute-start.8 = (bf16[2,64,128]{2,1,0:T(8,128)(2,1)S(1)}, bf16[2,64,128]{2,1,0:T(8,128)(2,1)S(1)}, u32[]{:S(2)}, u32[]{:S(2)}) collective-permute-start(bf16[2,64,128]{2,1,0:T(8,128)(2,1)S(1)} %get-tuple-element.25), channel_id=1, source_target_pairs={{0,24},{4,28},{8,16},{12,20},{16,8},{20,12},{24,0},{28,4},{1,25},{... | collective-permute-start | bytes 98312 | tf_op jit(solution)/shard_map/ppermute | solution.py:301
  73.1 3.9 %collective-permute-start.9 = (bf16[2,64,128]{2,1,0:T(8,128)(2,1)S(1)}, bf16[2,64,128]{2,1,0:T(8,128)(2,1)S(1)}, u32[]{:S(2)}, u32[]{:S(2)}) collective-permute-start(bf16[2,64,128]{2,1,0:T(8,128)(2,1)S(1)} %get-tuple-element.26), channel_id=1, source_target_pairs={{0,8},{4,12},{8,0},{12,4},{16,24},{20,28},{24,16},{28,20},{1,9},{5... | collective-permute-start | bytes 98312 | tf_op jit(solution)/shard_map/ppermute | solution.py:301
  77.1 4.0 %collective-permute-start.10 = (f32[1,64,128]{2,1,0:T(8,128)S(1)}, f32[1,64,128]{2,1,0:T(8,128)S(1)}, u32[]{:S(2)}, u32[]{:S(2)}) collective-permute-start(f32[1,64,128]{2,1,0:T(8,128)S(1)} %slice.9), channel_id=1, source_target_pairs={{0,4},{4,0},{8,12},{12,8},{16,20},{20,16},{24,28},{28,24},{1,5},{5... | collective-permute-start | bytes 98312 | tf_op jit(solution)/shard_map/ppermute | solution.py:301
  81.1 3.6 %collective-permute-start.11 = (f32[64,128]{1,0:T(8,128)S(1)}, f32[64,128]{1,0:T(8,128)S(1)}, u32[]{:S(2)}, u32[]{:S(2)}) collective-permute-start(f32[64,128]{1,0:T(8,128)S(1)} %fusion), channel_id=1, source_target_pairs={{0,3},{1,2},{2,1},{3,0},{4,7},{5,6},{6,5},{7,4},{8,11},{9,10},{10,... | collective-permute-start | bytes 98312 | tf_op jit(solution)/shard_map/ppermute | solution.py:301
  81.1 4.0 %collective-permute-start.12 = (f32[64,128]{1,0:T(8,128)S(1)}, f32[64,128]{1,0:T(8,128)S(1)}, u32[]{:S(2)}, u32[]{:S(2)}) collective-permute-start(f32[64,128]{1,0:T(8,128)S(1)} %fusion), channel_id=1, source_target_pairs={{0,2},{1,3},{2,0},{3,1},{4,6},{5,7},{6,4},{7,5},{8,10},{9,11},{10,... | collective-permute-start | bytes 98312 | tf_op jit(solution)/shard_map/ppermute | solution.py:301
  82.7 2.4 %collective-permute-start.13 = (f32[64,128]{1,0:T(8,128)S(1)}, f32[64,128]{1,0:T(8,128)S(1)}, u32[]{:S(2)}, u32[]{:S(2)}) collective-permute-start(f32[64,128]{1,0:T(8,128)S(1)} %fusion), channel_id=1, source_target_pairs={{0,1},{1,0},{2,3},{3,2},{4,5},{5,4},{6,7},{7,6},{8,9},{9,8},{10,11... | collective-permute-start | bytes 98312 | tf_op jit(solution)/shard_map/ppermute | solution.py:301

commit v29 on v25

--- a/solution.py
+++ b/solution.py
@@ -238,6 +238,13 @@
                 lambda i=i, t=t: folded[i] if t == blocks else early_folded[i, :, t * 2 * rows : (t + 1) * 2 * rows]
                 for t in tiles_in
             ]
+            if start == 0:
+                column = (2 * i + 1) * HD
+                tiles = [
+                    functools.partial(score_tile, lambda n=n, c=column: pieces[n][:, c : c + HD], queries)
+                    for n in (early, early + 1)
+                ]
+                values = [lambda i=i, n=n: folded[i, :, n * rows : (n + 1) * rows] for n in range(2)]
             units.append((tiles, values, shifts, finish))
     run_units(units, lat)
 

time: 86 us -> 86 us (level)
  no operation moved by 1% of the time
where the time goes in v29:
time: 86 us; the launch traced here: 85.7 us
  waiting for transfers between devices  41.5 us (48%)
  starting transfers between devices  23.9 us (28%)
  Pallas kernels  16.2 us (19%)
  local copies, waits for them, and re-layouts  3.22 us (4%)
    ppermute x14, waiting for transfers between devices, swap(): return lax.ppermute(array, axis, [(i, i ^ offset) for i in range(size)])  41.5 us
    ppermute x14, starting transfers between devices, swap(): return lax.ppermute(array, axis, [(i, i ^ offset) for i in range(size)])  23.9 us
    pallas_call x8, Pallas kernels, pack(): pl.pallas_call(functools.partial(pack_kernel, k), in_specs=[SMEM, SMEM] +...  6.94 us
    pallas_call x1, Pallas kernels, attend_early(): pl.pallas_call(functools.partial(early_kernel, offsets, late), in_specs=[...  5.77 us
    pallas_call x1, Pallas kernels, attend_late(): pl.pallas_call(functools.partial(late_kernel, offsets, late), in_specs=[V...  3.49 us
    unnamed x20, local copies, waits for them, and re-layouts  3.21 us
  transfers between devices with their start and end apart: 14, of which 10 were waited for; matrix products, arithmetic and copies ran while one was open for 0% of the time, Pallas kernels for 12%

profile of v29, /device:TPU:0, one launch (start us, length us, event | category | flops | bytes accessed | tf_op | source)
XLA Modules:
  0.0 85.7 jit_solution(5577648004104482297)
XLA Ops:
  0.0 2.1 %pack.10 = bf16[128,1280]{1,0:T(8,128)(2,1)} custom-call(s32[1]{0:T(128)} %bitcast.me_ref, s32[1]{0:T(128)} %bitcast.1.model_ref, bf16[1,128,12288]{2,1,0:T(8,128)(2,1)} %qkv_ref.15, bf16[2,64,4096]{2,1,0:T(8,128)(2,1)} %bitcast.9), custom_call_target="tpu_custom_call" | custom-call | bytes 655360 | tf_op jit(solution)/shard_map/pack/pallas_call | solution.py:63
  2.1 6.0 %collective-permute-start.2 = (bf16[128,1280]{1,0:T(8,128)(2,1)}, bf16[128,1280]{1,0:T(8,128)(2,1)S(1)}, u32[]{:S(2)}, u32[]{:S(2)}) collective-permute-start(bf16[128,1280]{1,0:T(8,128)(2,1)} %pack.10), channel_id=1, source_target_pairs={{0,28},{4,24},{8,20},{12,16},{16,12},{20,8},{24,4},{28,0},{1,29},{... | collective-permute-start | bytes 983048 | tf_op jit(solution)/shard_map/ppermute | solution.py:308
  8.1 0.0 copy-done
  8.1 1.2 %copy-done.1 = bf16[2,4096,64]{1,2,0:T(8,128)(2,1)S(1)} copy-done((bf16[2,4096,64]{1,2,0:T(8,128)(2,1)S(1)}, bf16[2,4096,64]{1,2,0:T(8,128)(2,1)}, u32[]{:S(2)}) %copy-start.1) | copy-done | bytes 1048600
  9.4 0.3 pack.12
  9.6 0.1 collective-permute-start.4
  9.7 0.3 pack.8
  10.0 0.9 %collective-permute-start = (bf16[128,1280]{1,0:T(8,128)(2,1)S(1)}, bf16[128,1280]{1,0:T(8,128)(2,1)S(1)}, u32[]{:S(2)}, u32[]{:S(2)}) collective-permute-start(bf16[128,1280]{1,0:T(8,128)(2,1)S(1)} %pack.8), channel_id=1, source_target_pairs={{0,24},{4,28},{8,16},{12,20},{16,8},{20,12},{24,0},{28,4},{1,25},{... | collective-permute-start | bytes 983048 | tf_op jit(solution)/shard_map/ppermute | solution.py:308
  10.9 6.0 %collective-permute-done.2.refs_0_.refs_1_.refs_5_ = bf16[128,1280]{1,0:T(8,128)(2,1)S(1)} collective-permute-done((bf16[128,1280]{1,0:T(8,128)(2,1)}, bf16[128,1280]{1,0:T(8,128)(2,1)S(1)}, u32[]{:S(2)}, u32[]{:S(2)}) %collective-permute-start.2) | collective-permute-done | bytes 327712 | tf_op jit(solution)/shard_map/ppermute | solution.py:308
  16.9 10.7 %collective-permute-done.4.refs_0_.refs_3_ = bf16[128,1280]{1,0:T(8,128)(2,1)S(1)} collective-permute-done((bf16[128,1280]{1,0:T(8,128)(2,1)S(1)}, bf16[128,1280]{1,0:T(8,128)(2,1)S(1)}, u32[]{:S(2)}, u32[]{:S(2)}) %collective-permute-start.4) | collective-permute-done | bytes 327712 | tf_op jit(solution)/shard_map/ppermute | solution.py:308
  27.6 1.0 %pack.15 = bf16[128,1280]{1,0:T(8,128)(2,1)} custom-call(s32[1]{0:T(128)} %bitcast.me_ref, s32[1]{0:T(128)} %bitcast.1.model_ref, bf16[1,128,12288]{2,1,0:T(8,128)(2,1)S(1)} %copy-done, bf16[2,64,4096]{2,1,0:T(8,128)(2,1)S(1)} %bitcast.12, bf16[128,1280]{1,0:T(8,128)(2,1)S(1)} %collective-permute-done.4.refs_0_.refs_3_, ...), custom_call_target="tpu_custom_call" | custom-call | bytes 655360 | tf_op jit(solution)/shard_map/pack/pallas_call | solution.py:63
  28.6 2.7 %collective-permute-start.6 = (bf16[128,1280]{1,0:T(8,128)(2,1)}, bf16[128,1280]{1,0:T(8,128)(2,1)}, u32[]{:S(2)}, u32[]{:S(2)}) collective-permute-start(bf16[128,1280]{1,0:T(8,128)(2,1)} %pack.15), channel_id=1, source_target_pairs={{0,8},{4,12},{8,0},{12,4},{16,24},{20,28},{24,16},{28,20},{1,9},{5... | collective-permute-start | bytes 983048 | tf_op jit(solution)/shard_map/ppermute | solution.py:308
  31.3 1.0 %pack.14 = bf16[128,1280]{1,0:T(8,128)(2,1)} custom-call(s32[1]{0:T(128)} %bitcast.me_ref, s32[1]{0:T(128)} %bitcast.1.model_ref, bf16[1,128,12288]{2,1,0:T(8,128)(2,1)S(1)} %copy-done, bf16[2,64,4096]{2,1,0:T(8,128)(2,1)S(1)} %bitcast.13, bf16[128,1280]{1,0:T(8,128)(2,1)S(1)} %collective-permute-done.4.refs_0_.refs_3_), custom_call_target="tpu_custom_call" | custom-call | bytes 655360 | tf_op jit(solution)/shard_map/pack/pallas_call | solution.py:63
  32.4 1.4 %collective-permute-start.5 = (bf16[128,1280]{1,0:T(8,128)(2,1)}, bf16[128,1280]{1,0:T(8,128)(2,1)}, u32[]{:S(2)}, u32[]{:S(2)}) collective-permute-start(bf16[128,1280]{1,0:T(8,128)(2,1)} %pack.14), channel_id=1, source_target_pairs={{0,4},{4,0},{8,12},{12,8},{16,20},{20,16},{24,28},{28,24},{1,5},{5... | collective-permute-start | bytes 983048 | tf_op jit(solution)/shard_map/ppermute | solution.py:308
  33.7 0.0 copy-done.3
  33.7 1.0 %pack.11 = bf16[128,1280]{1,0:T(8,128)(2,1)} custom-call(s32[1]{0:T(128)} %bitcast.me_ref, s32[1]{0:T(128)} %bitcast.1.model_ref, bf16[1,128,12288]{2,1,0:T(8,128)(2,1)S(1)} %copy-done, bf16[2,64,4096]{2,1,0:T(8,128)(2,1)S(1)} %bitcast.14, bf16[128,1280]{1,0:T(8,128)(2,1)S(1)} %collective-permute-done.2.refs_0_.refs_1_.refs_5_), custom_call_target="tpu_custom_call" | custom-call | bytes 655360 | tf_op jit(solution)/shard_map/pack/pallas_call | solution.py:63
  34.7 0.1 collective-permute-start.3
  34.8 0.0 collective-permute-done.refs_0_.refs_4_
  34.8 1.0 %pack.9 = bf16[128,1280]{1,0:T(8,128)(2,1)} custom-call(s32[1]{0:T(128)} %bitcast.me_ref, s32[1]{0:T(128)} %bitcast.1.model_ref, bf16[1,128,12288]{2,1,0:T(8,128)(2,1)S(1)} %copy-done, bf16[2,64,4096]{2,1,0:T(8,128)(2,1)S(1)} %bitcast.15, bf16[128,1280]{1,0:T(8,128)(2,1)S(1)} %collective-permute-done.refs_0_.refs_4_), custom_call_target="tpu_custom_call" | custom-call | bytes 655360 | tf_op jit(solution)/shard_map/pack/pallas_call | solution.py:63
  35.9 0.0 copy-start.7
  35.9 0.0 copy-start.8
  35.9 0.0 copy-start.9
  35.9 6.7 %collective-permute-start.1 = (bf16[128,1280]{1,0:T(8,128)(2,1)}, bf16[128,1280]{1,0:T(8,128)(2,1)}, u32[]{:S(2)}, u32[]{:S(2)}) collective-permute-start(bf16[128,1280]{1,0:T(8,128)(2,1)} %pack.9), channel_id=1, source_target_pairs={{0,16},{4,20},{8,24},{12,28},{16,0},{20,4},{24,8},{28,12},{1,17},{... | collective-permute-start | bytes 983048 | tf_op jit(solution)/shard_map/ppermute | solution.py:308
  42.6 1.2 %copy-done.2 = bf16[2,4096,64]{1,2,0:T(8,128)(2,1)S(1)} copy-done((bf16[2,4096,64]{1,2,0:T(8,128)(2,1)S(1)}, bf16[2,4096,64]{1,2,0:T(8,128)(2,1)}, u32[]{:S(2)}) %copy-start.2) | copy-done | bytes 1048600
  43.9 0.3 pack.13.refs_0_
  44.2 0.0 collective-permute-done.6.refs_2_
  44.2 0.0 collective-permute-done.5.refs_1_
  44.2 0.6 copy-done.4
  44.8 0.1 copy-done.6
  44.9 5.8 %attend_early.1 = (f32[4,64,768]{2,1,0:T(8,128)S(1)}, f32[2,8,768]{2,1,0:T(8,128)S(1)}, f32[8,128]{1,0:T(8,128)S(1)}, bf16[6,128,1280]{2,1,0:T(8,128)(2,1)S(1)},...) custom-call(s32[4]{0:T(128)S(1)} %copy-done.8, s32[1]{0:T(128)} %bitcast.me_ref, ...), custom_call_target="tpu_custom_call" | custom-call | flops 905969664 | bytes 2359296 | tf_op jit(solution)/shard_map/attend_early/pallas_call | solution.py:257
  50.7 10.6 %collective-permute-done.3.refs_1_ = bf16[128,1280]{1,0:T(8,128)(2,1)} collective-permute-done((bf16[128,1280]{1,0:T(8,128)(2,1)}, bf16[128,1280]{1,0:T(8,128)(2,1)}, u32[]{:S(2)}, u32[]{:S(2)}) %collective-permute-start.3) | collective-permute-done | bytes 327712 | tf_op jit(solution)/shard_map/ppermute | solution.py:308
  61.4 5.9 %collective-permute-done.1.refs_0_ = bf16[128,1280]{1,0:T(8,128)(2,1)} collective-permute-done((bf16[128,1280]{1,0:T(8,128)(2,1)}, bf16[128,1280]{1,0:T(8,128)(2,1)}, u32[]{:S(2)}, u32[]{:S(2)}) %collective-permute-start.1) | collective-permute-done | bytes 327712 | tf_op jit(solution)/shard_map/ppermute | solution.py:308
  67.3 3.5 %attend_late.1 = (f32[2,64,128]{2,1,0:T(8,128)S(1)}, bf16[2,64,128]{2,1,0:T(8,128)(2,1)S(1)}, bf16[2,64,128]{2,1,0:T(8,128)(2,1)S(1)}, bf16[2,64,128]{2,1,0:T(8,128)(2,1)S(1)}) custom-call(bf16[128,1280]{1,0:T(8,128)(2,1)} %collective-permute-done.1.refs_0_, bf16[128,1280]{1,0:T(8,128)(2,1)} %collective-permute-done.3.refs_1_, ...), custom_call_target="tpu_custom_call" | custom-call | flops 402653184 | bytes 3145728 | tf_op jit(solution)/shard_map/attend_late/pallas_call | solution.py:288
  70.8 0.1 collective-permute-start.7
  70.8 2.3 %collective-permute-start.8 = (bf16[2,64,128]{2,1,0:T(8,128)(2,1)S(1)}, bf16[2,64,128]{2,1,0:T(8,128)(2,1)S(1)}, u32[]{:S(2)}, u32[]{:S(2)}) collective-permute-start(bf16[2,64,128]{2,1,0:T(8,128)(2,1)S(1)} %get-tuple-element.25), channel_id=1, source_target_pairs={{0,24},{4,28},{8,16},{12,20},{16,8},{20,12},{24,0},{28,4},{1,25},{... | collective-permute-start | bytes 98312 | tf_op jit(solution)/shard_map/ppermute | solution.py:308
  73.1 1.2 %collective-permute-start.9 = (bf16[2,64,128]{2,1,0:T(8,128)(2,1)S(1)}, bf16[2,64,128]{2,1,0:T(8,128)(2,1)S(1)}, u32[]{:S(2)}, u32[]{:S(2)}) collective-permute-start(bf16[2,64,128]{2,1,0:T(8,128)(2,1)S(1)} %get-tuple-element.26), channel_id=1, source_target_pairs={{0,8},{4,12},{8,0},{12,4},{16,24},{20,28},{24,16},{28,20},{1,9},{5... | collective-permute-start | bytes 98312 | tf_op jit(solution)/shard_map/ppermute | solution.py:308
  74.3 1.4 %collective-permute-done.7 = bf16[2,64,128]{2,1,0:T(8,128)(2,1)S(1)} collective-permute-done((bf16[2,64,128]{2,1,0:T(8,128)(2,1)S(1)}, bf16[2,64,128]{2,1,0:T(8,128)(2,1)S(1)}, u32[]{:S(2)}, u32[]{:S(2)}) %collective-permute-start.7) | collective-permute-done | bytes 32800 | tf_op jit(solution)/shard_map/ppermute | solution.py:308
  75.7 0.9 %collective-permute-done.8 = bf16[2,64,128]{2,1,0:T(8,128)(2,1)S(1)} collective-permute-done((bf16[2,64,128]{2,1,0:T(8,128)(2,1)S(1)}, bf16[2,64,128]{2,1,0:T(8,128)(2,1)S(1)}, u32[]{:S(2)}, u32[]{:S(2)}) %collective-permute-start.8) | collective-permute-done | bytes 32800 | tf_op jit(solution)/shard_map/ppermute | solution.py:308
  76.6 0.4 collective-permute-done.9
  77.1 0.6 collective-permute-start.10
  77.7 3.4 %collective-permute-done.10 = f32[1,64,128]{2,1,0:T(8,128)S(1)} collective-permute-done((f32[1,64,128]{2,1,0:T(8,128)S(1)}, f32[1,64,128]{2,1,0:T(8,128)S(1)}, u32[]{:S(2)}, u32[]{:S(2)}) %collective-permute-start.10) | collective-permute-done | bytes 32800 | tf_op jit(solution)/shard_map/ppermute | solution.py:308
  81.1 0.0 collective-permute-start.11
  81.1 1.6 %collective-permute-start.12 = (f32[64,128]{1,0:T(8,128)S(1)}, f32[64,128]{1,0:T(8,128)S(1)}, u32[]{:S(2)}, u32[]{:S(2)}) collective-permute-start(f32[64,128]{1,0:T(8,128)S(1)} %fusion), channel_id=1, source_target_pairs={{0,2},{1,3},{2,0},{3,1},{4,6},{5,7},{6,4},{7,5},{8,10},{9,11},{10,... | collective-permute-start | bytes 98312 | tf_op jit(solution)/shard_map/ppermute | solution.py:308
  82.7 0.3 collective-permute-start.13
  82.9 1.7 %collective-permute-done.11 = f32[64,128]{1,0:T(8,128)S(1)} collective-permute-done((f32[64,128]{1,0:T(8,128)S(1)}, f32[64,128]{1,0:T(8,128)S(1)}, u32[]{:S(2)}, u32[]{:S(2)}) %collective-permute-start.11) | collective-permute-done | bytes 32800 | tf_op jit(solution)/shard_map/ppermute | solution.py:308
  84.7 0.4 collective-permute-done.12
  85.1 0.0 collective-permute-done.13
  85.1 0.6 add_bitcast_fusion
  (14 shorter events, 0.0 us)
Async XLA Ops:
  0.0 8.1 %copy-start = (bf16[1,128,12288]{2,1,0:T(8,128)(2,1)S(1)}, bf16[1,128,12288]{2,1,0:T(8,128)(2,1)}, u32[]{:S(2)}) copy-start(bf16[1,128,12288]{2,1,0:T(8,128)(2,1)} %qkv_ref.15) | copy-start | bytes 9437188
  2.1 14.9 %collective-permute-start.2 = (bf16[128,1280]{1,0:T(8,128)(2,1)}, bf16[128,1280]{1,0:T(8,128)(2,1)S(1)}, u32[]{:S(2)}, u32[]{:S(2)}) collective-permute-start(bf16[128,1280]{1,0:T(8,128)(2,1)} %pack.10), channel_id=1, source_target_pairs={{0,28},{4,24},{8,20},{12,16},{16,12},{20,8},{24,4},{28,0},{1,29},{... | collective-permute-start | bytes 983048 | tf_op jit(solution)/shard_map/ppermute | solution.py:308
  8.1 1.2 %copy-start.1 = (bf16[2,4096,64]{1,2,0:T(8,128)(2,1)S(1)}, bf16[2,4096,64]{1,2,0:T(8,128)(2,1)}, u32[]{:S(2)}) copy-start(bf16[2,4096,64]{1,2,0:T(8,128)(2,1)} %param.6) | copy-start | bytes 3145732
  9.6 18.0 %collective-permute-start.4 = (bf16[128,1280]{1,0:T(8,128)(2,1)S(1)}, bf16[128,1280]{1,0:T(8,128)(2,1)S(1)}, u32[]{:S(2)}, u32[]{:S(2)}) collective-permute-start(bf16[128,1280]{1,0:T(8,128)(2,1)S(1)} %pack.12), channel_id=1, source_target_pairs={{0,12},{4,8},{8,4},{12,0},{16,28},{20,24},{24,20},{28,16},{1,13},{... | collective-permute-start | bytes 983048 | tf_op jit(solution)/shard_map/ppermute | solution.py:308
  10.0 24.8 %collective-permute-start = (bf16[128,1280]{1,0:T(8,128)(2,1)S(1)}, bf16[128,1280]{1,0:T(8,128)(2,1)S(1)}, u32[]{:S(2)}, u32[]{:S(2)}) collective-permute-start(bf16[128,1280]{1,0:T(8,128)(2,1)S(1)} %pack.8), channel_id=1, source_target_pairs={{0,24},{4,28},{8,16},{12,20},{16,8},{20,12},{24,0},{28,4},{1,25},{... | collective-permute-start | bytes 983048 | tf_op jit(solution)/shard_map/ppermute | solution.py:308
  16.9 16.8 %copy-start.3 = (bf16[128,1280]{1,0:T(8,128)(2,1)}, bf16[128,1280]{1,0:T(8,128)(2,1)S(1)}, u32[]{:S(2)}) copy-start(bf16[128,1280]{1,0:T(8,128)(2,1)S(1)} %collective-permute-done.2.refs_0_.refs_1_.refs_5_) | copy-start | bytes 983044
  28.6 15.5 %collective-permute-start.6 = (bf16[128,1280]{1,0:T(8,128)(2,1)}, bf16[128,1280]{1,0:T(8,128)(2,1)}, u32[]{:S(2)}, u32[]{:S(2)}) collective-permute-start(bf16[128,1280]{1,0:T(8,128)(2,1)} %pack.15), channel_id=1, source_target_pairs={{0,8},{4,12},{8,0},{12,4},{16,24},{20,28},{24,16},{28,20},{1,9},{5... | collective-permute-start | bytes 983048 | tf_op jit(solution)/shard_map/ppermute | solution.py:308
  32.4 11.8 %collective-permute-start.5 = (bf16[128,1280]{1,0:T(8,128)(2,1)}, bf16[128,1280]{1,0:T(8,128)(2,1)}, u32[]{:S(2)}, u32[]{:S(2)}) collective-permute-start(bf16[128,1280]{1,0:T(8,128)(2,1)} %pack.14), channel_id=1, source_target_pairs={{0,4},{4,0},{8,12},{12,8},{16,20},{20,16},{24,28},{28,24},{1,5},{5... | collective-permute-start | bytes 983048 | tf_op jit(solution)/shard_map/ppermute | solution.py:308
  34.7 26.6 %collective-permute-start.3 = (bf16[128,1280]{1,0:T(8,128)(2,1)}, bf16[128,1280]{1,0:T(8,128)(2,1)}, u32[]{:S(2)}, u32[]{:S(2)}) collective-permute-start(bf16[128,1280]{1,0:T(8,128)(2,1)} %pack.11), channel_id=1, source_target_pairs={{0,20},{4,16},{8,28},{12,24},{16,4},{20,0},{24,12},{28,8},{1,21},{... | collective-permute-start | bytes 983048 | tf_op jit(solution)/shard_map/ppermute | solution.py:308
  34.8 1.1 %copy-start.5 = (bf16[128,1280]{1,0:T(8,128)(2,1)}, bf16[128,1280]{1,0:T(8,128)(2,1)S(1)}, u32[]{:S(2)}) copy-start(bf16[128,1280]{1,0:T(8,128)(2,1)S(1)} %collective-permute-done.refs_0_.refs_4_) | copy-start | bytes 983044
  35.9 8.3 %copy-start.7 = (f32[1000]{0:T(1024)S(1)}, f32[1000]{0:T(1024)}, u32[]{:S(2)}) copy-start(f32[1000]{0:T(1024)} %step_weight_ref.1) | copy-start | bytes 12004
  35.9 8.3 %copy-start.8 = (s32[4]{0:T(128)S(1)}, s32[4]{0:T(128)}, u32[]{:S(2)}) copy-start(s32[4]{0:T(128)} %frames_ref.1) | copy-start | bytes 52
  35.9 8.3 %copy-start.9 = (s32[2]{0:T(128)S(1)}, s32[2]{0:T(128)}, u32[]{:S(2)}) copy-start(s32[2]{0:T(128)} %timestep_ref.1) | copy-start | bytes 28
  35.9 31.4 %collective-permute-start.1 = (bf16[128,1280]{1,0:T(8,128)(2,1)}, bf16[128,1280]{1,0:T(8,128)(2,1)}, u32[]{:S(2)}, u32[]{:S(2)}) collective-permute-start(bf16[128,1280]{1,0:T(8,128)(2,1)} %pack.9), channel_id=1, source_target_pairs={{0,16},{4,20},{8,24},{12,28},{16,0},{20,4},{24,8},{28,12},{1,17},{... | collective-permute-start | bytes 983048 | tf_op jit(solution)/shard_map/ppermute | solution.py:308
  42.6 1.2 %copy-start.2 = (bf16[2,4096,64]{1,2,0:T(8,128)(2,1)S(1)}, bf16[2,4096,64]{1,2,0:T(8,128)(2,1)}, u32[]{:S(2)}) copy-start(bf16[2,4096,64]{1,2,0:T(8,128)(2,1)} %param.6) | copy-start | bytes 3145732
  43.9 1.0 %copy-start.4 = (bf16[128,1280]{1,0:T(8,128)(2,1)S(1)}, bf16[128,1280]{1,0:T(8,128)(2,1)}, u32[]{:S(2)}) copy-start(bf16[128,1280]{1,0:T(8,128)(2,1)} %copy-done.3) | copy-start | bytes 983044
  43.9 1.1 %copy-start.6 = (bf16[128,1280]{1,0:T(8,128)(2,1)S(1)}, bf16[128,1280]{1,0:T(8,128)(2,1)}, u32[]{:S(2)}) copy-start(bf16[128,1280]{1,0:T(8,128)(2,1)} %copy-done.5) | copy-start | bytes 983044
  70.8 5.0 %collective-permute-start.7 = (bf16[2,64,128]{2,1,0:T(8,128)(2,1)S(1)}, bf16[2,64,128]{2,1,0:T(8,128)(2,1)S(1)}, u32[]{:S(2)}, u32[]{:S(2)}) collective-permute-start(bf16[2,64,128]{2,1,0:T(8,128)(2,1)S(1)} %get-tuple-element.24), channel_id=1, source_target_pairs={{0,16},{4,20},{8,24},{12,28},{16,0},{20,4},{24,8},{28,12},{1,17},{... | collective-permute-start | bytes 98312 | tf_op jit(solution)/shard_map/ppermute | solution.py:308
  70.8 5.8 %collective-permute-start.8 = (bf16[2,64,128]{2,1,0:T(8,128)(2,1)S(1)}, bf16[2,64,128]{2,1,0:T(8,128)(2,1)S(1)}, u32[]{:S(2)}, u32[]{:S(2)}) collective-permute-start(bf16[2,64,128]{2,1,0:T(8,128)(2,1)S(1)} %get-tuple-element.25), channel_id=1, source_target_pairs={{0,24},{4,28},{8,16},{12,20},{16,8},{20,12},{24,0},{28,4},{1,25},{... | collective-permute-start | bytes 98312 | tf_op jit(solution)/shard_map/ppermute | solution.py:308
  73.1 3.9 %collective-permute-start.9 = (bf16[2,64,128]{2,1,0:T(8,128)(2,1)S(1)}, bf16[2,64,128]{2,1,0:T(8,128)(2,1)S(1)}, u32[]{:S(2)}, u32[]{:S(2)}) collective-permute-start(bf16[2,64,128]{2,1,0:T(8,128)(2,1)S(1)} %get-tuple-element.26), channel_id=1, source_target_pairs={{0,8},{4,12},{8,0},{12,4},{16,24},{20,28},{24,16},{28,20},{1,9},{5... | collective-permute-start | bytes 98312 | tf_op jit(solution)/shard_map/ppermute | solution.py:308
  77.1 4.0 %collective-permute-start.10 = (f32[1,64,128]{2,1,0:T(8,128)S(1)}, f32[1,64,128]{2,1,0:T(8,128)S(1)}, u32[]{:S(2)}, u32[]{:S(2)}) collective-permute-start(f32[1,64,128]{2,1,0:T(8,128)S(1)} %slice.9), channel_id=1, source_target_pairs={{0,4},{4,0},{8,12},{12,8},{16,20},{20,16},{24,28},{28,24},{1,5},{5... | collective-permute-start | bytes 98312 | tf_op jit(solution)/shard_map/ppermute | solution.py:308
  81.1 3.6 %collective-permute-start.11 = (f32[64,128]{1,0:T(8,128)S(1)}, f32[64,128]{1,0:T(8,128)S(1)}, u32[]{:S(2)}, u32[]{:S(2)}) collective-permute-start(f32[64,128]{1,0:T(8,128)S(1)} %fusion), channel_id=1, source_target_pairs={{0,3},{1,2},{2,1},{3,0},{4,7},{5,6},{6,5},{7,4},{8,11},{9,10},{10,... | collective-permute-start | bytes 98312 | tf_op jit(solution)/shard_map/ppermute | solution.py:308
  81.1 4.0 %collective-permute-start.12 = (f32[64,128]{1,0:T(8,128)S(1)}, f32[64,128]{1,0:T(8,128)S(1)}, u32[]{:S(2)}, u32[]{:S(2)}) collective-permute-start(f32[64,128]{1,0:T(8,128)S(1)} %fusion), channel_id=1, source_target_pairs={{0,2},{1,3},{2,0},{3,1},{4,6},{5,7},{6,4},{7,5},{8,10},{9,11},{10,... | collective-permute-start | bytes 98312 | tf_op jit(solution)/shard_map/ppermute | solution.py:308
  82.7 2.4 %collective-permute-start.13 = (f32[64,128]{1,0:T(8,128)S(1)}, f32[64,128]{1,0:T(8,128)S(1)}, u32[]{:S(2)}, u32[]{:S(2)}) collective-permute-start(f32[64,128]{1,0:T(8,128)S(1)} %fusion), channel_id=1, source_target_pairs={{0,1},{1,0},{2,3},{3,2},{4,5},{5,4},{6,7},{7,6},{8,9},{9,8},{10,11... | collective-permute-start | bytes 98312 | tf_op jit(solution)/shard_map/ppermute | solution.py:308

commit v30 on v29

--- a/solution.py
+++ b/solution.py
@@ -209,7 +209,7 @@
             out_ref[k % size] = (results[start][:, j * rows : (j + 1) * rows] * factor).astype(out_ref.dtype)
 
     units = []
-    for start, number, tiles_in in ((0, early, [blocks]), (early, 2, range(blocks + 1))):
+    for start, number, tiles_in in ((early, 2, range(blocks + 1)), (0, early, [blocks])):
         rows_ref = late_ref if start else wide_ref
         shifts = [rows_ref[n : n + 1] for n in range(rows_ref.shape[0])]
         for i in range(count):

time: 86 us -> 86 us (level)
  no operation moved by 1% of the time
where the time goes in v30:
time: 86 us; the launch traced here: 85.7 us
  waiting for transfers between devices  41.5 us (48%)
  starting transfers between devices  23.9 us (28%)
  Pallas kernels  16.2 us (19%)
  local copies, waits for them, and re-layouts  3.22 us (4%)
    ppermute x14, waiting for transfers between devices, swap(): return lax.ppermute(array, axis, [(i, i ^ offset) for i in range(size)])  41.5 us
    ppermute x14, starting transfers between devices, swap(): return lax.ppermute(array, axis, [(i, i ^ offset) for i in range(size)])  23.9 us
    pallas_call x8, Pallas kernels, pack(): pl.pallas_call(functools.partial(pack_kernel, k), in_specs=[SMEM, SMEM] +...  6.94 us
    pallas_call x1, Pallas kernels, attend_early(): pl.pallas_call(functools.partial(early_kernel, offsets, late), in_specs=[...  5.77 us
    pallas_call x1, Pallas kernels, attend_late(): pl.pallas_call(functools.partial(late_kernel, offsets, late), in_specs=[V...  3.49 us
    unnamed x20, local copies, waits for them, and re-layouts  3.21 us
  transfers between devices with their start and end apart: 14, of which 10 were waited for; matrix products, arithmetic and copies ran while one was open for 0% of the time, Pallas kernels for 12%

profile of v30, /device:TPU:0, one launch (start us, length us, event | category | flops | bytes accessed | tf_op | source)
XLA Modules:
  0.0 85.7 jit_solution(17207154113256128601)
XLA Ops:
  0.0 2.1 %pack.10 = bf16[128,1280]{1,0:T(8,128)(2,1)} custom-call(s32[1]{0:T(128)} %bitcast.me_ref, s32[1]{0:T(128)} %bitcast.1.model_ref, bf16[1,128,12288]{2,1,0:T(8,128)(2,1)} %qkv_ref.15, bf16[2,64,4096]{2,1,0:T(8,128)(2,1)} %bitcast.9), custom_call_target="tpu_custom_call" | custom-call | bytes 655360 | tf_op jit(solution)/shard_map/pack/pallas_call | solution.py:63
  2.1 6.0 %collective-permute-start.2 = (bf16[128,1280]{1,0:T(8,128)(2,1)}, bf16[128,1280]{1,0:T(8,128)(2,1)S(1)}, u32[]{:S(2)}, u32[]{:S(2)}) collective-permute-start(bf16[128,1280]{1,0:T(8,128)(2,1)} %pack.10), channel_id=1, source_target_pairs={{0,28},{4,24},{8,20},{12,16},{16,12},{20,8},{24,4},{28,0},{1,29},{... | collective-permute-start | bytes 983048 | tf_op jit(solution)/shard_map/ppermute | solution.py:308
  8.1 0.0 copy-done
  8.1 1.2 %copy-done.1 = bf16[2,4096,64]{1,2,0:T(8,128)(2,1)S(1)} copy-done((bf16[2,4096,64]{1,2,0:T(8,128)(2,1)S(1)}, bf16[2,4096,64]{1,2,0:T(8,128)(2,1)}, u32[]{:S(2)}) %copy-start.1) | copy-done | bytes 1048600
  9.4 0.3 pack.12
  9.6 0.1 collective-permute-start.4
  9.7 0.3 pack.8
  10.0 0.9 %collective-permute-start = (bf16[128,1280]{1,0:T(8,128)(2,1)S(1)}, bf16[128,1280]{1,0:T(8,128)(2,1)S(1)}, u32[]{:S(2)}, u32[]{:S(2)}) collective-permute-start(bf16[128,1280]{1,0:T(8,128)(2,1)S(1)} %pack.8), channel_id=1, source_target_pairs={{0,24},{4,28},{8,16},{12,20},{16,8},{20,12},{24,0},{28,4},{1,25},{... | collective-permute-start | bytes 983048 | tf_op jit(solution)/shard_map/ppermute | solution.py:308
  10.9 6.0 %collective-permute-done.2.refs_0_.refs_1_.refs_5_ = bf16[128,1280]{1,0:T(8,128)(2,1)S(1)} collective-permute-done((bf16[128,1280]{1,0:T(8,128)(2,1)}, bf16[128,1280]{1,0:T(8,128)(2,1)S(1)}, u32[]{:S(2)}, u32[]{:S(2)}) %collective-permute-start.2) | collective-permute-done | bytes 327712 | tf_op jit(solution)/shard_map/ppermute | solution.py:308
  16.9 10.7 %collective-permute-done.4.refs_0_.refs_3_ = bf16[128,1280]{1,0:T(8,128)(2,1)S(1)} collective-permute-done((bf16[128,1280]{1,0:T(8,128)(2,1)S(1)}, bf16[128,1280]{1,0:T(8,128)(2,1)S(1)}, u32[]{:S(2)}, u32[]{:S(2)}) %collective-permute-start.4) | collective-permute-done | bytes 327712 | tf_op jit(solution)/shard_map/ppermute | solution.py:308
  27.6 1.0 %pack.15 = bf16[128,1280]{1,0:T(8,128)(2,1)} custom-call(s32[1]{0:T(128)} %bitcast.me_ref, s32[1]{0:T(128)} %bitcast.1.model_ref, bf16[1,128,12288]{2,1,0:T(8,128)(2,1)S(1)} %copy-done, bf16[2,64,4096]{2,1,0:T(8,128)(2,1)S(1)} %bitcast.12, bf16[128,1280]{1,0:T(8,128)(2,1)S(1)} %collective-permute-done.4.refs_0_.refs_3_, ...), custom_call_target="tpu_custom_call" | custom-call | bytes 655360 | tf_op jit(solution)/shard_map/pack/pallas_call | solution.py:63
  28.6 2.7 %collective-permute-start.6 = (bf16[128,1280]{1,0:T(8,128)(2,1)}, bf16[128,1280]{1,0:T(8,128)(2,1)}, u32[]{:S(2)}, u32[]{:S(2)}) collective-permute-start(bf16[128,1280]{1,0:T(8,128)(2,1)} %pack.15), channel_id=1, source_target_pairs={{0,8},{4,12},{8,0},{12,4},{16,24},{20,28},{24,16},{28,20},{1,9},{5... | collective-permute-start | bytes 983048 | tf_op jit(solution)/shard_map/ppermute | solution.py:308
  31.3 1.0 %pack.14 = bf16[128,1280]{1,0:T(8,128)(2,1)} custom-call(s32[1]{0:T(128)} %bitcast.me_ref, s32[1]{0:T(128)} %bitcast.1.model_ref, bf16[1,128,12288]{2,1,0:T(8,128)(2,1)S(1)} %copy-done, bf16[2,64,4096]{2,1,0:T(8,128)(2,1)S(1)} %bitcast.13, bf16[128,1280]{1,0:T(8,128)(2,1)S(1)} %collective-permute-done.4.refs_0_.refs_3_), custom_call_target="tpu_custom_call" | custom-call | bytes 655360 | tf_op jit(solution)/shard_map/pack/pallas_call | solution.py:63
  32.4 1.4 %collective-permute-start.5 = (bf16[128,1280]{1,0:T(8,128)(2,1)}, bf16[128,1280]{1,0:T(8,128)(2,1)}, u32[]{:S(2)}, u32[]{:S(2)}) collective-permute-start(bf16[128,1280]{1,0:T(8,128)(2,1)} %pack.14), channel_id=1, source_target_pairs={{0,4},{4,0},{8,12},{12,8},{16,20},{20,16},{24,28},{28,24},{1,5},{5... | collective-permute-start | bytes 983048 | tf_op jit(solution)/shard_map/ppermute | solution.py:308
  33.7 0.0 copy-done.3
  33.7 1.0 %pack.11 = bf16[128,1280]{1,0:T(8,128)(2,1)} custom-call(s32[1]{0:T(128)} %bitcast.me_ref, s32[1]{0:T(128)} %bitcast.1.model_ref, bf16[1,128,12288]{2,1,0:T(8,128)(2,1)S(1)} %copy-done, bf16[2,64,4096]{2,1,0:T(8,128)(2,1)S(1)} %bitcast.14, bf16[128,1280]{1,0:T(8,128)(2,1)S(1)} %collective-permute-done.2.refs_0_.refs_1_.refs_5_), custom_call_target="tpu_custom_call" | custom-call | bytes 655360 | tf_op jit(solution)/shard_map/pack/pallas_call | solution.py:63
  34.7 0.1 collective-permute-start.3
  34.8 0.0 collective-permute-done.refs_0_.refs_4_
  34.8 1.0 %pack.9 = bf16[128,1280]{1,0:T(8,128)(2,1)} custom-call(s32[1]{0:T(128)} %bitcast.me_ref, s32[1]{0:T(128)} %bitcast.1.model_ref, bf16[1,128,12288]{2,1,0:T(8,128)(2,1)S(1)} %copy-done, bf16[2,64,4096]{2,1,0:T(8,128)(2,1)S(1)} %bitcast.15, bf16[128,1280]{1,0:T(8,128)(2,1)S(1)} %collective-permute-done.refs_0_.refs_4_), custom_call_target="tpu_custom_call" | custom-call | bytes 655360 | tf_op jit(solution)/shard_map/pack/pallas_call | solution.py:63
  35.9 0.0 copy-start.7
  35.9 0.0 copy-start.8
  35.9 0.0 copy-start.9
  35.9 6.7 %collective-permute-start.1 = (bf16[128,1280]{1,0:T(8,128)(2,1)}, bf16[128,1280]{1,0:T(8,128)(2,1)}, u32[]{:S(2)}, u32[]{:S(2)}) collective-permute-start(bf16[128,1280]{1,0:T(8,128)(2,1)} %pack.9), channel_id=1, source_target_pairs={{0,16},{4,20},{8,24},{12,28},{16,0},{20,4},{24,8},{28,12},{1,17},{... | collective-permute-start | bytes 983048 | tf_op jit(solution)/shard_map/ppermute | solution.py:308
  42.6 1.2 %copy-done.2 = bf16[2,4096,64]{1,2,0:T(8,128)(2,1)S(1)} copy-done((bf16[2,4096,64]{1,2,0:T(8,128)(2,1)S(1)}, bf16[2,4096,64]{1,2,0:T(8,128)(2,1)}, u32[]{:S(2)}) %copy-start.2) | copy-done | bytes 1048600
  43.9 0.3 pack.13.refs_0_
  44.2 0.0 collective-permute-done.6.refs_2_
  44.2 0.0 collective-permute-done.5.refs_1_
  44.2 0.6 copy-done.4
  44.8 0.1 copy-done.6
  44.9 5.8 %attend_early.1 = (f32[4,64,768]{2,1,0:T(8,128)S(1)}, f32[2,8,768]{2,1,0:T(8,128)S(1)}, f32[8,128]{1,0:T(8,128)S(1)}, bf16[6,128,1280]{2,1,0:T(8,128)(2,1)S(1)},...) custom-call(s32[4]{0:T(128)S(1)} %copy-done.8, s32[1]{0:T(128)} %bitcast.me_ref, ...), custom_call_target="tpu_custom_call" | custom-call | flops 905969664 | bytes 2359296 | tf_op jit(solution)/shard_map/attend_early/pallas_call | solution.py:257
  50.7 10.6 %collective-permute-done.3.refs_1_ = bf16[128,1280]{1,0:T(8,128)(2,1)} collective-permute-done((bf16[128,1280]{1,0:T(8,128)(2,1)}, bf16[128,1280]{1,0:T(8,128)(2,1)}, u32[]{:S(2)}, u32[]{:S(2)}) %collective-permute-start.3) | collective-permute-done | bytes 327712 | tf_op jit(solution)/shard_map/ppermute | solution.py:308
  61.4 5.9 %collective-permute-done.1.refs_0_ = bf16[128,1280]{1,0:T(8,128)(2,1)} collective-permute-done((bf16[128,1280]{1,0:T(8,128)(2,1)}, bf16[128,1280]{1,0:T(8,128)(2,1)}, u32[]{:S(2)}, u32[]{:S(2)}) %collective-permute-start.1) | collective-permute-done | bytes 327712 | tf_op jit(solution)/shard_map/ppermute | solution.py:308
  67.3 3.5 %attend_late.1 = (f32[2,64,128]{2,1,0:T(8,128)S(1)}, bf16[2,64,128]{2,1,0:T(8,128)(2,1)S(1)}, bf16[2,64,128]{2,1,0:T(8,128)(2,1)S(1)}, bf16[2,64,128]{2,1,0:T(8,128)(2,1)S(1)}) custom-call(bf16[128,1280]{1,0:T(8,128)(2,1)} %collective-permute-done.1.refs_0_, bf16[128,1280]{1,0:T(8,128)(2,1)} %collective-permute-done.3.refs_1_, ...), custom_call_target="tpu_custom_call" | custom-call | flops 402653184 | bytes 3145728 | tf_op jit(solution)/shard_map/attend_late/pallas_call | solution.py:288
  70.8 0.1 collective-permute-start.7
  70.8 2.3 %collective-permute-start.8 = (bf16[2,64,128]{2,1,0:T(8,128)(2,1)S(1)}, bf16[2,64,128]{2,1,0:T(8,128)(2,1)S(1)}, u32[]{:S(2)}, u32[]{:S(2)}) collective-permute-start(bf16[2,64,128]{2,1,0:T(8,128)(2,1)S(1)} %get-tuple-element.25), channel_id=1, source_target_pairs={{0,24},{4,28},{8,16},{12,20},{16,8},{20,12},{24,0},{28,4},{1,25},{... | collective-permute-start | bytes 98312 | tf_op jit(solution)/shard_map/ppermute | solution.py:308
  73.1 1.2 %collective-permute-start.9 = (bf16[2,64,128]{2,1,0:T(8,128)(2,1)S(1)}, bf16[2,64,128]{2,1,0:T(8,128)(2,1)S(1)}, u32[]{:S(2)}, u32[]{:S(2)}) collective-permute-start(bf16[2,64,128]{2,1,0:T(8,128)(2,1)S(1)} %get-tuple-element.26), channel_id=1, source_target_pairs={{0,8},{4,12},{8,0},{12,4},{16,24},{20,28},{24,16},{28,20},{1,9},{5... | collective-permute-start | bytes 98312 | tf_op jit(solution)/shard_map/ppermute | solution.py:308
  74.3 1.4 %collective-permute-done.7 = bf16[2,64,128]{2,1,0:T(8,128)(2,1)S(1)} collective-permute-done((bf16[2,64,128]{2,1,0:T(8,128)(2,1)S(1)}, bf16[2,64,128]{2,1,0:T(8,128)(2,1)S(1)}, u32[]{:S(2)}, u32[]{:S(2)}) %collective-permute-start.7) | collective-permute-done | bytes 32800 | tf_op jit(solution)/shard_map/ppermute | solution.py:308
  75.7 0.9 %collective-permute-done.8 = bf16[2,64,128]{2,1,0:T(8,128)(2,1)S(1)} collective-permute-done((bf16[2,64,128]{2,1,0:T(8,128)(2,1)S(1)}, bf16[2,64,128]{2,1,0:T(8,128)(2,1)S(1)}, u32[]{:S(2)}, u32[]{:S(2)}) %collective-permute-start.8) | collective-permute-done | bytes 32800 | tf_op jit(solution)/shard_map/ppermute | solution.py:308
  76.6 0.4 collective-permute-done.9
  77.1 0.6 collective-permute-start.10
  77.7 3.4 %collective-permute-done.10 = f32[1,64,128]{2,1,0:T(8,128)S(1)} collective-permute-done((f32[1,64,128]{2,1,0:T(8,128)S(1)}, f32[1,64,128]{2,1,0:T(8,128)S(1)}, u32[]{:S(2)}, u32[]{:S(2)}) %collective-permute-start.10) | collective-permute-done | bytes 32800 | tf_op jit(solution)/shard_map/ppermute | solution.py:308
  81.1 0.0 collective-permute-start.11
  81.1 1.6 %collective-permute-start.12 = (f32[64,128]{1,0:T(8,128)S(1)}, f32[64,128]{1,0:T(8,128)S(1)}, u32[]{:S(2)}, u32[]{:S(2)}) collective-permute-start(f32[64,128]{1,0:T(8,128)S(1)} %fusion), channel_id=1, source_target_pairs={{0,2},{1,3},{2,0},{3,1},{4,6},{5,7},{6,4},{7,5},{8,10},{9,11},{10,... | collective-permute-start | bytes 98312 | tf_op jit(solution)/shard_map/ppermute | solution.py:308
  82.7 0.3 collective-permute-start.13
  82.9 1.8 %collective-permute-done.11 = f32[64,128]{1,0:T(8,128)S(1)} collective-permute-done((f32[64,128]{1,0:T(8,128)S(1)}, f32[64,128]{1,0:T(8,128)S(1)}, u32[]{:S(2)}, u32[]{:S(2)}) %collective-permute-start.11) | collective-permute-done | bytes 32800 | tf_op jit(solution)/shard_map/ppermute | solution.py:308
  84.7 0.4 collective-permute-done.12
  85.1 0.0 collective-permute-done.13
  85.1 0.6 add_bitcast_fusion
  (14 shorter events, 0.0 us)
Async XLA Ops:
  0.0 8.1 %copy-start = (bf16[1,128,12288]{2,1,0:T(8,128)(2,1)S(1)}, bf16[1,128,12288]{2,1,0:T(8,128)(2,1)}, u32[]{:S(2)}) copy-start(bf16[1,128,12288]{2,1,0:T(8,128)(2,1)} %qkv_ref.15) | copy-start | bytes 9437188
  2.1 14.9 %collective-permute-start.2 = (bf16[128,1280]{1,0:T(8,128)(2,1)}, bf16[128,1280]{1,0:T(8,128)(2,1)S(1)}, u32[]{:S(2)}, u32[]{:S(2)}) collective-permute-start(bf16[128,1280]{1,0:T(8,128)(2,1)} %pack.10), channel_id=1, source_target_pairs={{0,28},{4,24},{8,20},{12,16},{16,12},{20,8},{24,4},{28,0},{1,29},{... | collective-permute-start | bytes 983048 | tf_op jit(solution)/shard_map/ppermute | solution.py:308
  8.1 1.2 %copy-start.1 = (bf16[2,4096,64]{1,2,0:T(8,128)(2,1)S(1)}, bf16[2,4096,64]{1,2,0:T(8,128)(2,1)}, u32[]{:S(2)}) copy-start(bf16[2,4096,64]{1,2,0:T(8,128)(2,1)} %param.6) | copy-start | bytes 3145732
  9.6 18.0 %collective-permute-start.4 = (bf16[128,1280]{1,0:T(8,128)(2,1)S(1)}, bf16[128,1280]{1,0:T(8,128)(2,1)S(1)}, u32[]{:S(2)}, u32[]{:S(2)}) collective-permute-start(bf16[128,1280]{1,0:T(8,128)(2,1)S(1)} %pack.12), channel_id=1, source_target_pairs={{0,12},{4,8},{8,4},{12,0},{16,28},{20,24},{24,20},{28,16},{1,13},{... | collective-permute-start | bytes 983048 | tf_op jit(solution)/shard_map/ppermute | solution.py:308
  10.0 24.8 %collective-permute-start = (bf16[128,1280]{1,0:T(8,128)(2,1)S(1)}, bf16[128,1280]{1,0:T(8,128)(2,1)S(1)}, u32[]{:S(2)}, u32[]{:S(2)}) collective-permute-start(bf16[128,1280]{1,0:T(8,128)(2,1)S(1)} %pack.8), channel_id=1, source_target_pairs={{0,24},{4,28},{8,16},{12,20},{16,8},{20,12},{24,0},{28,4},{1,25},{... | collective-permute-start | bytes 983048 | tf_op jit(solution)/shard_map/ppermute | solution.py:308
  16.9 16.8 %copy-start.3 = (bf16[128,1280]{1,0:T(8,128)(2,1)}, bf16[128,1280]{1,0:T(8,128)(2,1)S(1)}, u32[]{:S(2)}) copy-start(bf16[128,1280]{1,0:T(8,128)(2,1)S(1)} %collective-permute-done.2.refs_0_.refs_1_.refs_5_) | copy-start | bytes 983044
  28.6 15.5 %collective-permute-start.6 = (bf16[128,1280]{1,0:T(8,128)(2,1)}, bf16[128,1280]{1,0:T(8,128)(2,1)}, u32[]{:S(2)}, u32[]{:S(2)}) collective-permute-start(bf16[128,1280]{1,0:T(8,128)(2,1)} %pack.15), channel_id=1, source_target_pairs={{0,8},{4,12},{8,0},{12,4},{16,24},{20,28},{24,16},{28,20},{1,9},{5... | collective-permute-start | bytes 983048 | tf_op jit(solution)/shard_map/ppermute | solution.py:308
  32.4 11.8 %collective-permute-start.5 = (bf16[128,1280]{1,0:T(8,128)(2,1)}, bf16[128,1280]{1,0:T(8,128)(2,1)}, u32[]{:S(2)}, u32[]{:S(2)}) collective-permute-start(bf16[128,1280]{1,0:T(8,128)(2,1)} %pack.14), channel_id=1, source_target_pairs={{0,4},{4,0},{8,12},{12,8},{16,20},{20,16},{24,28},{28,24},{1,5},{5... | collective-permute-start | bytes 983048 | tf_op jit(solution)/shard_map/ppermute | solution.py:308
  34.7 26.6 %collective-permute-start.3 = (bf16[128,1280]{1,0:T(8,128)(2,1)}, bf16[128,1280]{1,0:T(8,128)(2,1)}, u32[]{:S(2)}, u32[]{:S(2)}) collective-permute-start(bf16[128,1280]{1,0:T(8,128)(2,1)} %pack.11), channel_id=1, source_target_pairs={{0,20},{4,16},{8,28},{12,24},{16,4},{20,0},{24,12},{28,8},{1,21},{... | collective-permute-start | bytes 983048 | tf_op jit(solution)/shard_map/ppermute | solution.py:308
  34.8 1.1 %copy-start.5 = (bf16[128,1280]{1,0:T(8,128)(2,1)}, bf16[128,1280]{1,0:T(8,128)(2,1)S(1)}, u32[]{:S(2)}) copy-start(bf16[128,1280]{1,0:T(8,128)(2,1)S(1)} %collective-permute-done.refs_0_.refs_4_) | copy-start | bytes 983044
  35.9 8.3 %copy-start.7 = (f32[1000]{0:T(1024)S(1)}, f32[1000]{0:T(1024)}, u32[]{:S(2)}) copy-start(f32[1000]{0:T(1024)} %step_weight_ref.1) | copy-start | bytes 12004
  35.9 8.3 %copy-start.8 = (s32[4]{0:T(128)S(1)}, s32[4]{0:T(128)}, u32[]{:S(2)}) copy-start(s32[4]{0:T(128)} %frames_ref.1) | copy-start | bytes 52
  35.9 8.3 %copy-start.9 = (s32[2]{0:T(128)S(1)}, s32[2]{0:T(128)}, u32[]{:S(2)}) copy-start(s32[2]{0:T(128)} %timestep_ref.1) | copy-start | bytes 28
  35.9 31.4 %collective-permute-start.1 = (bf16[128,1280]{1,0:T(8,128)(2,1)}, bf16[128,1280]{1,0:T(8,128)(2,1)}, u32[]{:S(2)}, u32[]{:S(2)}) collective-permute-start(bf16[128,1280]{1,0:T(8,128)(2,1)} %pack.9), channel_id=1, source_target_pairs={{0,16},{4,20},{8,24},{12,28},{16,0},{20,4},{24,8},{28,12},{1,17},{... | collective-permute-start | bytes 983048 | tf_op jit(solution)/shard_map/ppermute | solution.py:308
  42.6 1.2 %copy-start.2 = (bf16[2,4096,64]{1,2,0:T(8,128)(2,1)S(1)}, bf16[2,4096,64]{1,2,0:T(8,128)(2,1)}, u32[]{:S(2)}) copy-start(bf16[2,4096,64]{1,2,0:T(8,128)(2,1)} %param.6) | copy-start | bytes 3145732
  43.9 1.0 %copy-start.4 = (bf16[128,1280]{1,0:T(8,128)(2,1)S(1)}, bf16[128,1280]{1,0:T(8,128)(2,1)}, u32[]{:S(2)}) copy-start(bf16[128,1280]{1,0:T(8,128)(2,1)} %copy-done.3) | copy-start | bytes 983044
  43.9 1.1 %copy-start.6 = (bf16[128,1280]{1,0:T(8,128)(2,1)S(1)}, bf16[128,1280]{1,0:T(8,128)(2,1)}, u32[]{:S(2)}) copy-start(bf16[128,1280]{1,0:T(8,128)(2,1)} %copy-done.5) | copy-start | bytes 983044
  70.8 4.9 %collective-permute-start.7 = (bf16[2,64,128]{2,1,0:T(8,128)(2,1)S(1)}, bf16[2,64,128]{2,1,0:T(8,128)(2,1)S(1)}, u32[]{:S(2)}, u32[]{:S(2)}) collective-permute-start(bf16[2,64,128]{2,1,0:T(8,128)(2,1)S(1)} %get-tuple-element.24), channel_id=1, source_target_pairs={{0,16},{4,20},{8,24},{12,28},{16,0},{20,4},{24,8},{28,12},{1,17},{... | collective-permute-start | bytes 98312 | tf_op jit(solution)/shard_map/ppermute | solution.py:308
  70.8 5.8 %collective-permute-start.8 = (bf16[2,64,128]{2,1,0:T(8,128)(2,1)S(1)}, bf16[2,64,128]{2,1,0:T(8,128)(2,1)S(1)}, u32[]{:S(2)}, u32[]{:S(2)}) collective-permute-start(bf16[2,64,128]{2,1,0:T(8,128)(2,1)S(1)} %get-tuple-element.25), channel_id=1, source_target_pairs={{0,24},{4,28},{8,16},{12,20},{16,8},{20,12},{24,0},{28,4},{1,25},{... | collective-permute-start | bytes 98312 | tf_op jit(solution)/shard_map/ppermute | solution.py:308
  73.1 3.9 %collective-permute-start.9 = (bf16[2,64,128]{2,1,0:T(8,128)(2,1)S(1)}, bf16[2,64,128]{2,1,0:T(8,128)(2,1)S(1)}, u32[]{:S(2)}, u32[]{:S(2)}) collective-permute-start(bf16[2,64,128]{2,1,0:T(8,128)(2,1)S(1)} %get-tuple-element.26), channel_id=1, source_target_pairs={{0,8},{4,12},{8,0},{12,4},{16,24},{20,28},{24,16},{28,20},{1,9},{5... | collective-permute-start | bytes 98312 | tf_op jit(solution)/shard_map/ppermute | solution.py:308
  77.1 4.0 %collective-permute-start.10 = (f32[1,64,128]{2,1,0:T(8,128)S(1)}, f32[1,64,128]{2,1,0:T(8,128)S(1)}, u32[]{:S(2)}, u32[]{:S(2)}) collective-permute-start(f32[1,64,128]{2,1,0:T(8,128)S(1)} %slice.9), channel_id=1, source_target_pairs={{0,4},{4,0},{8,12},{12,8},{16,20},{20,16},{24,28},{28,24},{1,5},{5... | collective-permute-start | bytes 98312 | tf_op jit(solution)/shard_map/ppermute | solution.py:308
  81.1 3.6 %collective-permute-start.11 = (f32[64,128]{1,0:T(8,128)S(1)}, f32[64,128]{1,0:T(8,128)S(1)}, u32[]{:S(2)}, u32[]{:S(2)}) collective-permute-start(f32[64,128]{1,0:T(8,128)S(1)} %fusion), channel_id=1, source_target_pairs={{0,3},{1,2},{2,1},{3,0},{4,7},{5,6},{6,5},{7,4},{8,11},{9,10},{10,... | collective-permute-start | bytes 98312 | tf_op jit(solution)/shard_map/ppermute | solution.py:308
  81.1 4.0 %collective-permute-start.12 = (f32[64,128]{1,0:T(8,128)S(1)}, f32[64,128]{1,0:T(8,128)S(1)}, u32[]{:S(2)}, u32[]{:S(2)}) collective-permute-start(f32[64,128]{1,0:T(8,128)S(1)} %fusion), channel_id=1, source_target_pairs={{0,2},{1,3},{2,0},{3,1},{4,6},{5,7},{6,4},{7,5},{8,10},{9,11},{10,... | collective-permute-start | bytes 98312 | tf_op jit(solution)/shard_map/ppermute | solution.py:308
  82.7 2.5 %collective-permute-start.13 = (f32[64,128]{1,0:T(8,128)S(1)}, f32[64,128]{1,0:T(8,128)S(1)}, u32[]{:S(2)}, u32[]{:S(2)}) collective-permute-start(f32[64,128]{1,0:T(8,128)S(1)} %fusion), channel_id=1, source_target_pairs={{0,1},{1,0},{2,3},{3,2},{4,5},{5,4},{6,7},{7,6},{8,9},{9,8},{10,11... | collective-permute-start | bytes 98312 | tf_op jit(solution)/shard_map/ppermute | solution.py:308
